TPU v7x, 32 devices: a whole 2x2x4 slice. The times are simulated.
32 devices in a mesh: dp: 4 (over y, x), ctx: 2 (over core), head: 4 (over z).
Axes of the slice: x: 2, y: 2, z: 4, core: 2. Of those that a mesh axis runs over, the one named last changes fastest.
Arguments:
- enc_query: bfloat16 [2048, 4096], P(('dp', 'ctx'), 'head'), parts along dimension 0, may hold values from -30 to 30
- enc_key: bfloat16 [2048, 4096], P(('dp', 'ctx'), 'head'), parts along dimension 0, may hold values from -6 to 6
- enc_value: bfloat16 [2048, 4096], P(('dp', 'ctx'), 'head'), parts along dimension 0, may hold values from -6 to 6
- doc_ids: int32 [2048], P(('dp', 'ctx')), parts along dimension 0, may hold values from 0 to 5, never falling along the last dimension, each value on 1 to 256 neighbouring positions
- key_map: bfloat16 [4096, 2048], P('ctx', 'head'), may hold values from -0.09375 to 0.09375
- value_map: bfloat16 [4096, 2048], P('ctx', 'head'), may hold values from -0.09375 to 0.09375
- tgt_query: bfloat16 [512, 2048], P(('dp', 'ctx'), 'head'), parts along dimension 0, may hold values from -150 to 150
Outputs:
- cross_out: bfloat16 [512, 2048], P(('dp', 'ctx'), 'head'), parts along dimension 0
There are 4 independent parts, one for each index of `dp`. A program takes and returns all parts, laid end to end along the dimension named above; an argument that names none is the same for every part. Nothing has to cross between parts.
Inputs may be any that keep to these rules, and one draw needn't show every extreme that they name: `doc_ids`: document ids never fall along the pack; each document holds 1 to 256 consecutive positions and one holds exactly 256.
All inputs are finite; a program needn't handle non-finite values.
Results may differ from a plain program's by a relative error of at most 0.011.
Values may be sent and summed in bfloat16 or wider, within the bound.
No kernel may reach another device: no remote copies, remote signals or barrier semaphores. Data moves between devices by JAX's collectives and lax.ppermute only.
A program may use at most 64 MiB of HBM per device.

v0:
```python
import jax
import jax.numpy as jnp
from jax import lax
from jax.sharding import PartitionSpec as P

HEAD_DIM = 256


NEG_FILL = -1e30


def passed_along(value, axis, steps):
    count = lax.axis_size(axis)
    leading, last = (max(0, -steps), min(count, count - steps))
    return lax.ppermute(value, axis, [(source, source + steps) for source in range(leading, last)])


def masked_scores(query, keys, query_mark, key_mark):
    scale = query.shape[2] ** (-0.5)
    raw = jnp.einsum("rhe,khe->hrk", query, keys, preferred_element_type=jnp.float32) * scale
    same = query_mark[:, None] == key_mark[None, :]
    return jnp.where(same[None], raw, NEG_FILL)


def weighted(weights, values):
    return jnp.einsum(
        "hrk,khe->rhe", weights.astype(jnp.bfloat16), values, preferred_element_type=jnp.float32
    )


def normalize(summed, total):
    return summed / jnp.transpose(total)[:, :, None]


def dense_attend(query, keys, values, query_mark, key_mark):
    scores = masked_scores(query, keys, query_mark, key_mark)
    top = jnp.max(scores, axis=2, keepdims=True)
    weights = jnp.exp(scores - top)
    return normalize(weighted(weights, values), jnp.sum(weights, axis=2))


def on_device(enc_query, enc_key, enc_value, doc_ids, key_map, value_map, tgt_query):
    head_dim = HEAD_DIM
    heads_here = enc_query.shape[1] // head_dim
    cross_here = key_map.shape[1] // head_dim
    rows = enc_query.shape[0]
    tgt_rows = tgt_query.shape[0]
    query = enc_query.reshape(rows, heads_here, head_dim)
    own_key = enc_key.reshape(rows, heads_here, head_dim)
    own_value = enc_value.reshape(rows, heads_here, head_dim)
    own_mark = (doc_ids + 1).astype(jnp.bfloat16)
    arrived = {}
    for offset in (1, -1):
        arrived[offset] = passed_along((own_key, own_value, own_mark), "ctx", offset)
    left_key, left_value, left_mark = arrived[1]
    right_key, right_value, right_mark = arrived[-1]
    keys = jnp.concatenate([left_key, own_key, right_key], 0)
    values = jnp.concatenate([left_value, own_value, right_value], 0)
    marks = jnp.concatenate([left_mark, own_mark, right_mark], 0)
    enc_out = dense_attend(query, keys, values, own_mark, marks).astype(jnp.bfloat16)
    enc_flat = enc_out.reshape(rows, heads_here * head_dim)
    enc_full = lax.all_gather(enc_flat, "head", axis=1, tiled=True)
    key_sum = jnp.dot(
        enc_full,
        lax.all_gather(key_map, "ctx", axis=0, tiled=True),
        preferred_element_type=jnp.float32,
    )
    value_sum = jnp.dot(
        enc_full,
        lax.all_gather(value_map, "ctx", axis=0, tiled=True),
        preferred_element_type=jnp.float32,
    )
    memory_key = key_sum.astype(jnp.bfloat16).reshape(rows, cross_here, head_dim)
    memory_value = value_sum.astype(jnp.bfloat16).reshape(rows, cross_here, head_dim)
    target = tgt_query.reshape(tgt_rows, cross_here, head_dim)
    target_mark = own_mark.reshape(tgt_rows, rows // tgt_rows)[:, 0]
    near = {}
    for offset in (1, -1):
        near[offset] = passed_along((memory_key, memory_value, own_mark), "ctx", offset)
    keys = jnp.concatenate([near[1][0], memory_key, near[-1][0]], 0)
    values = jnp.concatenate([near[1][1], memory_value, near[-1][1]], 0)
    marks = jnp.concatenate([near[1][2], own_mark, near[-1][2]], 0)
    cross_out = dense_attend(target, keys, values, target_mark, marks)
    return cross_out.astype(jnp.bfloat16).reshape(tgt_rows, cross_here * head_dim)


def solution(mesh):
    in_specs = (
        P(("dp", "ctx"), "head"),
        P(("dp", "ctx"), "head"),
        P(("dp", "ctx"), "head"),
        P(("dp", "ctx")),
        P("ctx", "head"),
        P("ctx", "head"),
        P(("dp", "ctx"), "head"),
    )
    out_specs = P(("dp", "ctx"), "head")
    return jax.shard_map(
        on_device, mesh=mesh, in_specs=in_specs, out_specs=out_specs, check_vma=False
    )
```

profile of v0, /device:TPU:0, one launch (start us, length us, event | category | flops | bytes accessed | tf_op | source)
XLA Modules:
  0.0 122.0 jit_solution(6046243604585231799)
XLA Ops:
  6.5 1.3 %copy.34 = bf16[256,1024]{0,1:T(8,128)(2,1)S(1)} copy(bf16[256,1024]{1,0:T(8,128)(2,1)} %param.8) | data formatting | bytes 1048576 | tf_op args[1]
  8.1 2.4 %collective-permute-start.4 = (bf16[256,4,256]{2,0,1:T(8,128)(2,1)S(1)}, bf16[256,4,256]{2,0,1:T(8,128)(2,1)S(1)}, u32[]{:S(2)}, u32[]{:S(2)}) collective-permute-start(bf16[256,4,256]{2,0,1:T(8,128)(2,1)S(1)} %copy.35), channel_id=1, source_target_pairs={{0,4},{1,5},{2,6},{3,7},{8,12},{9,13},{10,14},{11,15},{16,20},{17,... | collective-permute-start | bytes 1572872 | tf_op jit(solution)/shard_map/ppermute | solution.py:15
  10.4 1.3 %collective-permute-start.5 = (bf16[256,4,256]{2,0,1:T(8,128)(2,1)S(1)}, bf16[256,4,256]{2,0,1:T(8,128)(2,1)S(1)}, u32[]{:S(2)}, u32[]{:S(2)}) collective-permute-start(bf16[256,4,256]{2,0,1:T(8,128)(2,1)S(1)} %copy.35), channel_id=1, source_target_pairs={{4,0},{5,1},{6,2},{7,3},{12,8},{13,9},{14,10},{15,11},{20,16},{21,... | collective-permute-start | bytes 1572872 | tf_op jit(solution)/shard_map/ppermute | solution.py:15
  11.7 0.7 add_convert_fusion
  12.4 3.0 %collective-permute-start.2 = (bf16[256]{0:T(256)(128)(2,1)S(1)}, bf16[256]{0:T(256)(128)(2,1)S(1)}, u32[]{:S(2)}, u32[]{:S(2)}) collective-permute-start(bf16[256]{0:T(256)(128)(2,1)S(1)} %add_convert_fusion), channel_id=1, source_target_pairs={{0,4},{1,5},{2,6},{3,7},{8,12},{9,13},{10,14},{11,15},{16,20},{17,... | collective-permute-start | bytes 1544 | tf_op jit(solution)/shard_map/ppermute | solution.py:15
  15.5 1.3 %collective-permute-start.3 = (bf16[256]{0:T(256)(128)(2,1)S(1)}, bf16[256]{0:T(256)(128)(2,1)S(1)}, u32[]{:S(2)}, u32[]{:S(2)}) collective-permute-start(bf16[256]{0:T(256)(128)(2,1)S(1)} %add_convert_fusion), channel_id=1, source_target_pairs={{4,0},{5,1},{6,2},{7,3},{12,8},{13,9},{14,10},{15,11},{20,16},{21,... | collective-permute-start | bytes 1544 | tf_op jit(solution)/shard_map/ppermute | solution.py:15
  16.8 1.2 %copy.33 = bf16[256,1024]{0,1:T(8,128)(2,1)S(1)} copy(bf16[256,1024]{1,0:T(8,128)(2,1)} %param.9) | data formatting | bytes 1048576 | tf_op args[2]
  18.0 3.1 %collective-permute-start = (bf16[256,4,256]{0,2,1:T(8,128)(2,1)S(1)}, bf16[256,4,256]{0,2,1:T(8,128)(2,1)S(1)}, u32[]{:S(2)}, u32[]{:S(2)}) collective-permute-start(bf16[256,4,256]{0,2,1:T(8,128)(2,1)S(1)} %bitcast.60), channel_id=1, source_target_pairs={{0,4},{1,5},{2,6},{3,7},{8,12},{9,13},{10,14},{11,15},{16,20},{17,... | collective-permute-start | bytes 1572872 | tf_op jit(solution)/shard_map/ppermute | solution.py:15
  21.1 1.3 %collective-permute-start.1 = (bf16[256,4,256]{0,2,1:T(8,128)(2,1)S(1)}, bf16[256,4,256]{0,2,1:T(8,128)(2,1)S(1)}, u32[]{:S(2)}, u32[]{:S(2)}) collective-permute-start(bf16[256,4,256]{0,2,1:T(8,128)(2,1)S(1)} %bitcast.61), channel_id=1, source_target_pairs={{4,0},{5,1},{6,2},{7,3},{12,8},{13,9},{14,10},{15,11},{20,16},{21,... | collective-permute-start | bytes 1572872 | tf_op jit(solution)/shard_map/ppermute | solution.py:15
  23.4 0.7 fusion
  24.0 0.9 collective-permute-done.1
  24.9 1.9 %divide_convert_fusion = bf16[256,4,256]{0,2,1:T(8,128)(2,1)} fusion(f32[4,768,256]{2,1,0:T(8,128)S(1)} %get-tuple-element.6, f32[4,256]{1,0:T(4,128)S(1)} %get-tuple-element.5, pred[256,768]{0,1:T(8,128)(4,1)S(1)} %broadcast_compare_fusion, bf16[256,4,256]{0,2,1:T(8,128)(2,1)S(1)} %collective-permute-done.1, bf16[256,4,256]{0,2,1:T(8,128)(2,1)S(1)} %bitcast.62, ...), kind=kOutput, calls=%fused_computation.30 | convolution fusion | flops 411041792 | bytes 5447680 | tf_op jit(solution)/shard_map/hrk,khe->rhe/dot_general | solution.py:26
  26.9 0.7 all-gather.8.cloned.1.call-update
  27.6 0.7 all-gather.6.cloned.1.call-update
  28.7 46.4 %all-gather.4.cloned.1.call-done = bf16[256,4096]{0,1:T(8,128)(2,1)} async-done(((bf16[256,1024]{0,1:T(8,128)(2,1)}), bf16[256,4096]{0,1:T(8,128)(2,1)}) %all-gather.4.cloned.1.call-update) | async-done | bytes 2097168 | tf_op jit(solution)/shard_map/all_gather | solution.py:62
  75.0 14.0 %all-gather.8.cloned.1.call-done = bf16[4096,512]{1,0:T(8,128)(2,1)} async-done(((bf16[2048,512]{1,0:T(8,128)(2,1)}), bf16[4096,512]{1,0:T(8,128)(2,1)}) %all-gather.8.cloned.1.call-update) | async-done | bytes 4194320 | tf_op jit(solution)/shard_map/all_gather | solution.py:65
  89.0 4.1 %convolution_convert_fusion = bf16[256,512]{1,0:T(8,128)(2,1)S(1)} fusion(bf16[256,4096]{0,1:T(8,128)(2,1)} %all-gather.4.cloned.1.call-done, bf16[4096,512]{1,0:T(8,128)(2,1)} %all-gather.8.cloned.1.call-done), kind=kOutput, calls=%fused_computation.22 | convolution fusion | flops 1073872896 | bytes 6553600 | tf_op jit(solution)/shard_map/dot_general | solution.py:63
  93.1 2.3 %collective-permute-start.8 = (bf16[256,2,256]{2,0,1:T(8,128)(2,1)S(1)}, bf16[256,2,256]{2,0,1:T(8,128)(2,1)S(1)}, u32[]{:S(2)}, u32[]{:S(2)}) collective-permute-start(bf16[256,2,256]{2,0,1:T(8,128)(2,1)S(1)} %bitcast.64), channel_id=1, source_target_pairs={{0,4},{1,5},{2,6},{3,7},{8,12},{9,13},{10,14},{11,15},{16,20},{17,... | collective-permute-start | bytes 786440 | tf_op jit(solution)/shard_map/ppermute | solution.py:15
  95.4 1.3 %collective-permute-start.9 = (bf16[256,2,256]{2,0,1:T(8,128)(2,1)S(1)}, bf16[256,2,256]{2,0,1:T(8,128)(2,1)S(1)}, u32[]{:S(2)}, u32[]{:S(2)}) collective-permute-start(bf16[256,2,256]{2,0,1:T(8,128)(2,1)S(1)} %bitcast.65), channel_id=1, source_target_pairs={{4,0},{5,1},{6,2},{7,3},{12,8},{13,9},{14,10},{15,11},{20,16},{21,... | collective-permute-start | bytes 786440 | tf_op jit(solution)/shard_map/ppermute | solution.py:15
  96.7 8.7 %all-gather.6.cloned.1.call-done = bf16[4096,512]{1,0:T(8,128)(2,1)} async-done(((bf16[2048,512]{1,0:T(8,128)(2,1)}), bf16[4096,512]{1,0:T(8,128)(2,1)}) %all-gather.6.cloned.1.call-update) | async-done | bytes 4194320 | tf_op jit(solution)/shard_map/all_gather | solution.py:70
  105.4 3.4 %convolution_convert_fusion.1 = bf16[256,512]{1,0:T(8,128)(2,1)S(1)} fusion(bf16[256,4096]{0,1:T(8,128)(2,1)S(1)} %copy-done, bf16[4096,512]{1,0:T(8,128)(2,1)} %all-gather.6.cloned.1.call-done), kind=kOutput, calls=%fused_computation.23 | convolution fusion | flops 1073872896 | bytes 6553600 | tf_op jit(solution)/shard_map/dot_general | solution.py:68
  108.9 2.1 %collective-permute-start.6 = (bf16[256,2,256]{2,0,1:T(8,128)(2,1)S(1)}, bf16[256,2,256]{2,0,1:T(8,128)(2,1)S(1)}, u32[]{:S(2)}, u32[]{:S(2)}) collective-permute-start(bf16[256,2,256]{2,0,1:T(8,128)(2,1)S(1)} %bitcast.67), channel_id=1, source_target_pairs={{0,4},{1,5},{2,6},{3,7},{8,12},{9,13},{10,14},{11,15},{16,20},{17,... | collective-permute-start | bytes 786440 | tf_op jit(solution)/shard_map/ppermute | solution.py:15
  111.0 1.3 %collective-permute-start.7 = (bf16[256,2,256]{2,0,1:T(8,128)(2,1)S(1)}, bf16[256,2,256]{2,0,1:T(8,128)(2,1)S(1)}, u32[]{:S(2)}, u32[]{:S(2)}) collective-permute-start(bf16[256,2,256]{2,0,1:T(8,128)(2,1)S(1)} %bitcast.68), channel_id=1, source_target_pairs={{4,0},{5,1},{6,2},{7,3},{12,8},{13,9},{14,10},{15,11},{20,16},{21,... | collective-permute-start | bytes 786440 | tf_op jit(solution)/shard_map/ppermute | solution.py:15
  113.0 1.4 %collective-permute-done.7 = bf16[256,2,256]{2,0,1:T(8,128)(2,1)S(1)} collective-permute-done((bf16[256,2,256]{2,0,1:T(8,128)(2,1)S(1)}, bf16[256,2,256]{2,0,1:T(8,128)(2,1)S(1)}, u32[]{:S(2)}, u32[]{:S(2)}) %collective-permute-start.7) | collective-permute-done | bytes 262176 | tf_op jit(solution)/shard_map/ppermute | solution.py:15
  (31 shorter events, 3.3 us)
Async XLA Ops:
  6.5 16.1 %copy-start.1 = (bf16[256,1024]{1,0:T(8,128)(2,1)S(1)}, bf16[256,1024]{1,0:T(8,128)(2,1)}, u32[]{:S(2)}) copy-start(bf16[256,1024]{1,0:T(8,128)(2,1)} %param.7) | copy-start | bytes 1572868
  6.5 68.5 %all-gather.4.cloned.1.call-start = ((), (), s32[]{:S(2)}) async-start(), calls=%async_computation | async-start | bytes 2621440 | tf_op jit(solution)/shard_map/all_gather | solution.py:62
  8.1 14.6 %collective-permute-start.4 = (bf16[256,4,256]{2,0,1:T(8,128)(2,1)S(1)}, bf16[256,4,256]{2,0,1:T(8,128)(2,1)S(1)}, u32[]{:S(2)}, u32[]{:S(2)}) collective-permute-start(bf16[256,4,256]{2,0,1:T(8,128)(2,1)S(1)} %copy.35), channel_id=1, source_target_pairs={{0,4},{1,5},{2,6},{3,7},{8,12},{9,13},{10,14},{11,15},{16,20},{17,... | collective-permute-start | bytes 1572872 | tf_op jit(solution)/shard_map/ppermute | solution.py:15
  10.4 12.2 %collective-permute-start.5 = (bf16[256,4,256]{2,0,1:T(8,128)(2,1)S(1)}, bf16[256,4,256]{2,0,1:T(8,128)(2,1)S(1)}, u32[]{:S(2)}, u32[]{:S(2)}) collective-permute-start(bf16[256,4,256]{2,0,1:T(8,128)(2,1)S(1)} %copy.35), channel_id=1, source_target_pairs={{4,0},{5,1},{6,2},{7,3},{12,8},{13,9},{14,10},{15,11},{20,16},{21,... | collective-permute-start | bytes 1572872 | tf_op jit(solution)/shard_map/ppermute | solution.py:15
  12.4 8.7 %collective-permute-start.2 = (bf16[256]{0:T(256)(128)(2,1)S(1)}, bf16[256]{0:T(256)(128)(2,1)S(1)}, u32[]{:S(2)}, u32[]{:S(2)}) collective-permute-start(bf16[256]{0:T(256)(128)(2,1)S(1)} %add_convert_fusion), channel_id=1, source_target_pairs={{0,4},{1,5},{2,6},{3,7},{8,12},{9,13},{10,14},{11,15},{16,20},{17,... | collective-permute-start | bytes 1544 | tf_op jit(solution)/shard_map/ppermute | solution.py:15
  15.5 6.9 %collective-permute-start.3 = (bf16[256]{0:T(256)(128)(2,1)S(1)}, bf16[256]{0:T(256)(128)(2,1)S(1)}, u32[]{:S(2)}, u32[]{:S(2)}) collective-permute-start(bf16[256]{0:T(256)(128)(2,1)S(1)} %add_convert_fusion), channel_id=1, source_target_pairs={{4,0},{5,1},{6,2},{7,3},{12,8},{13,9},{14,10},{15,11},{20,16},{21,... | collective-permute-start | bytes 1544 | tf_op jit(solution)/shard_map/ppermute | solution.py:15
  18.0 6.0 %collective-permute-start = (bf16[256,4,256]{0,2,1:T(8,128)(2,1)S(1)}, bf16[256,4,256]{0,2,1:T(8,128)(2,1)S(1)}, u32[]{:S(2)}, u32[]{:S(2)}) collective-permute-start(bf16[256,4,256]{0,2,1:T(8,128)(2,1)S(1)} %bitcast.60), channel_id=1, source_target_pairs={{0,4},{1,5},{2,6},{3,7},{8,12},{9,13},{10,14},{11,15},{16,20},{17,... | collective-permute-start | bytes 1572872 | tf_op jit(solution)/shard_map/ppermute | solution.py:15
  21.1 3.8 %collective-permute-start.1 = (bf16[256,4,256]{0,2,1:T(8,128)(2,1)S(1)}, bf16[256,4,256]{0,2,1:T(8,128)(2,1)S(1)}, u32[]{:S(2)}, u32[]{:S(2)}) collective-permute-start(bf16[256,4,256]{0,2,1:T(8,128)(2,1)S(1)} %bitcast.61), channel_id=1, source_target_pairs={{4,0},{5,1},{6,2},{7,3},{12,8},{13,9},{14,10},{15,11},{20,16},{21,... | collective-permute-start | bytes 1572872 | tf_op jit(solution)/shard_map/ppermute | solution.py:15
  26.8 62.1 %all-gather.8.cloned.1.call-start = ((), (), s32[]{:S(2)}) async-start(), calls=%async_computation.2 | async-start | bytes 6291456 | tf_op jit(solution)/shard_map/all_gather | solution.py:65
  27.6 77.8 %all-gather.6.cloned.1.call-start = ((), (), s32[]{:S(2)}) async-start(), calls=%async_computation.1 | async-start | bytes 6291456 | tf_op jit(solution)/shard_map/all_gather | solution.py:70
  75.0 30.4 %copy-start = (bf16[256,4096]{0,1:T(8,128)(2,1)S(1)}, bf16[256,4096]{0,1:T(8,128)(2,1)}, u32[]{:S(2)}) copy-start(bf16[256,4096]{0,1:T(8,128)(2,1)} %all-gather.4.cloned.1.call-done) | copy-start | bytes 6291460
  93.1 19.3 %copy-start.2 = (bf16[64,512]{1,0:T(8,128)(2,1)S(1)}, bf16[64,512]{1,0:T(8,128)(2,1)}, u32[]{:S(2)}) copy-start(bf16[64,512]{1,0:T(8,128)(2,1)} %param.13) | copy-start | bytes 196612
  93.1 19.2 %collective-permute-start.8 = (bf16[256,2,256]{2,0,1:T(8,128)(2,1)S(1)}, bf16[256,2,256]{2,0,1:T(8,128)(2,1)S(1)}, u32[]{:S(2)}, u32[]{:S(2)}) collective-permute-start(bf16[256,2,256]{2,0,1:T(8,128)(2,1)S(1)} %bitcast.64), channel_id=1, source_target_pairs={{0,4},{1,5},{2,6},{3,7},{8,12},{9,13},{10,14},{11,15},{16,20},{17,... | collective-permute-start | bytes 786440 | tf_op jit(solution)/shard_map/ppermute | solution.py:15
  95.4 17.0 %collective-permute-start.9 = (bf16[256,2,256]{2,0,1:T(8,128)(2,1)S(1)}, bf16[256,2,256]{2,0,1:T(8,128)(2,1)S(1)}, u32[]{:S(2)}, u32[]{:S(2)}) collective-permute-start(bf16[256,2,256]{2,0,1:T(8,128)(2,1)S(1)} %bitcast.65), channel_id=1, source_target_pairs={{4,0},{5,1},{6,2},{7,3},{12,8},{13,9},{14,10},{15,11},{20,16},{21,... | collective-permute-start | bytes 786440 | tf_op jit(solution)/shard_map/ppermute | solution.py:15
  108.9 4.2 %collective-permute-start.6 = (bf16[256,2,256]{2,0,1:T(8,128)(2,1)S(1)}, bf16[256,2,256]{2,0,1:T(8,128)(2,1)S(1)}, u32[]{:S(2)}, u32[]{:S(2)}) collective-permute-start(bf16[256,2,256]{2,0,1:T(8,128)(2,1)S(1)} %bitcast.67), channel_id=1, source_target_pairs={{0,4},{1,5},{2,6},{3,7},{8,12},{9,13},{10,14},{11,15},{16,20},{17,... | collective-permute-start | bytes 786440 | tf_op jit(solution)/shard_map/ppermute | solution.py:15
  111.0 3.4 %collective-permute-start.7 = (bf16[256,2,256]{2,0,1:T(8,128)(2,1)S(1)}, bf16[256,2,256]{2,0,1:T(8,128)(2,1)S(1)}, u32[]{:S(2)}, u32[]{:S(2)}) collective-permute-start(bf16[256,2,256]{2,0,1:T(8,128)(2,1)S(1)} %bitcast.68), channel_id=1, source_target_pairs={{4,0},{5,1},{6,2},{7,3},{12,8},{13,9},{14,10},{15,11},{20,16},{21,... | collective-permute-start | bytes 786440 | tf_op jit(solution)/shard_map/ppermute | solution.py:15
Sparse Core Ops, SparseCore 0:
  26.9 48.0 all-gather.3
  76.6 12.3 all-gather.7
  90.5 14.8 all-gather.5
where the time goes:
time: 122 us
  waiting for transfers between devices  72.7 us (60%)
  starting transfers between devices  19.4 us (16%)
  between operations  13.4 us (11%)
  matrix products  10.9 us (9%)
  local copies, waits for them, and re-layouts  3.67 us (3%)
  other arithmetic  1.91 us (2%)
    all_gather x1, waiting for transfers between devices, on_device(): enc_full = lax.all_gather(enc_flat, 'head', axis=1, tiled=True)  46.4 us
    ppermute x10, starting transfers between devices, passed_along(): lax.ppermute(value, axis, [(source, source + steps) for source in range(l...  19.3 us
    all_gather x1, waiting for transfers between devices, on_device(): lax.all_gather(key_map, 'ctx', axis=0, tiled=True)  14 us
    all_gather x1, waiting for transfers between devices, on_device(): lax.all_gather(value_map, 'ctx', axis=0, tiled=True)  8.72 us
    dot_general x1, matrix products, on_device(): jnp.dot(enc_full, lax.all_gather(key_map, 'ctx', axis=0, tiled=True), pre...  4.08 us
    dot_general x1, matrix products, on_device(): jnp.dot(enc_full, lax.all_gather(value_map, 'ctx', axis=0, tiled=True), p...  3.45 us
    unnamed x8, local copies, waits for them, and re-layouts  2.56 us
  transfers between devices with their start and end apart: 13, of which 5 were waited for; matrix products, arithmetic and copies ran while one was open for 10% of the time, Pallas kernels for 0%

commit v1 on v0

v1 whole, which is shorter than its diff:
```python
import functools

import jax
import jax.numpy as jnp
from jax import lax
from jax.experimental import pallas as pl
from jax.experimental.pallas import tpu as pltpu
from jax.sharding import PartitionSpec as P

HEAD_DIM = 256
NEG_FILL = -1e30
F32 = jnp.float32
BF16 = jnp.bfloat16
STATS = 128


def ring_order(count):
    return list(range(0, count, 2)) + list(range(1, count, 2))[::-1]


def links_of(count):
    if count == 2:
        return [[(0, 1), (1, 0)]]
    return [[(i, i + 1) for i in range(count - 1)], [(i + 1, i) for i in range(count - 1)]]


def dot_t(a, b):
    return lax.dot_general(a, b, (((1,), (1,)), ((), ())), preferred_element_type=F32)


def attend_kernel(blocks, scale, mask_ref, q_ref, *refs):
    keys, values, out_ref = refs[:blocks], refs[blocks : 2 * blocks], refs[-1]
    scores = jnp.concatenate([dot_t(q_ref[...], k[...]) for k in keys], axis=1) * scale
    scores = jnp.where(mask_ref[...] > 0, scores, NEG_FILL)
    weights = jnp.exp(scores - jnp.max(scores, axis=1, keepdims=True))
    total = jnp.sum(weights, axis=1, keepdims=True)
    rounded = weights.astype(BF16)
    summed = jnp.zeros(out_ref.shape, F32)
    width = keys[0].shape[0]
    for i, v in enumerate(values):
        summed += jnp.dot(rounded[:, i * width : (i + 1) * width], v[...], preferred_element_type=F32)
    out_ref[...] = (summed / total).astype(BF16)


def encoder_attend(query, keys, values, mask, first, heads):
    rows = query.shape[0]
    blocks = len(keys)
    block = pl.BlockSpec((rows, HEAD_DIM), lambda h: (0, first + h))
    return pl.pallas_call(
        functools.partial(attend_kernel, blocks, HEAD_DIM**-0.5),
        grid=(heads,),
        in_specs=[pl.BlockSpec(mask.shape, lambda h: (0, 0))] + [block] * (1 + 2 * blocks),
        out_specs=pl.BlockSpec((rows, HEAD_DIM), lambda h: (0, h)),
        out_shape=jax.ShapeDtypeStruct((rows, heads * HEAD_DIM), BF16),
        name="encoder_attend",
    )(mask, query, *keys, *values)


def project_kernel(parts, has_acc, rows_ref, *refs):
    acc_ref, out_ref = (refs[0], refs[-1])
    refs = refs[1:-1] if has_acc else refs[:-1]
    half = out_ref.shape[1] // 2
    for side in range(2):
        columns = slice(side * half, (side + 1) * half)
        total = acc_ref[:, columns] if has_acc else jnp.zeros((out_ref.shape[0], half), F32)
        for i in range(parts):
            total += jnp.dot(refs[3 * i][...], refs[3 * i + 1 + side][...], preferred_element_type=F32)
        out_ref[:, columns] = total


def project(acc, chunks, places, key_full, value_full):
    rows, depth = chunks[0].shape
    width = key_full.shape[1]
    whole = pl.BlockSpec((rows, 2 * width), lambda i, s: (0, 0))
    specs, operands = [], []
    if acc is not None:
        specs.append(whole)
        operands.append(acc)
    for i, chunk in enumerate(chunks):
        piece = pl.BlockSpec((depth, width), lambda g, s, i=i: (s[i], 0))
        specs += [pl.BlockSpec((rows, depth), lambda g, s: (0, 0)), piece, piece]
        operands += [chunk, key_full, value_full]
    return pl.pallas_call(
        functools.partial(project_kernel, len(chunks), acc is not None),
        grid_spec=pltpu.PrefetchScalarGridSpec(
            num_scalar_prefetch=1, grid=(1,), in_specs=specs, out_specs=whole
        ),
        out_shape=jax.ShapeDtypeStruct((rows, 2 * width), F32),
        compiler_params=pltpu.CompilerParams(vmem_limit_bytes=32 << 20),
        name="project",
    )(jnp.stack(places).astype(jnp.int32), *operands)


def cross_kernel(scale, places_ref, acc_ref, e_ref, kmap_ref, vmap_ref, tgt_ref, mask_ref, out_ref):
    width = kmap_ref.shape[1]
    mem_key = (acc_ref[:, :width] + jnp.dot(e_ref[...], kmap_ref[...], preferred_element_type=F32)).astype(BF16)
    mem_value = (acc_ref[:, width:] + jnp.dot(e_ref[...], vmap_ref[...], preferred_element_type=F32)).astype(BF16)
    heads = width // HEAD_DIM
    lane = lax.broadcasted_iota(jnp.int32, (out_ref.shape[0], STATS), 1)
    stats = jnp.zeros((out_ref.shape[0], STATS), F32)
    for h in range(heads):
        columns = slice(h * HEAD_DIM, (h + 1) * HEAD_DIM)
        scores = dot_t(tgt_ref[:, columns], mem_key[:, columns]) * scale
        scores = jnp.where(mask_ref[...] > 0, scores, NEG_FILL)
        top = jnp.max(scores, axis=1, keepdims=True)
        weights = jnp.exp(scores - top)
        total = jnp.sum(weights, axis=1, keepdims=True)
        out_ref[:, columns] = jnp.dot(weights.astype(BF16), mem_value[:, columns], preferred_element_type=F32)
        stats = jnp.where(lane == h, top, jnp.where(lane == heads + h, total, stats))
    out_ref[:, width:] = stats


def cross_attend(acc, chunk, place, key_full, value_full, targets, mask):
    rows, depth = chunk.shape
    width = key_full.shape[1]
    count = targets.shape[0]
    piece = pl.BlockSpec((depth, width), lambda g, s: (s[0], 0))
    whole = lambda shape: pl.BlockSpec(shape, lambda g, s: (0, 0))
    return pl.pallas_call(
        functools.partial(cross_kernel, HEAD_DIM**-0.5),
        grid_spec=pltpu.PrefetchScalarGridSpec(
            num_scalar_prefetch=1,
            grid=(1,),
            in_specs=[whole(acc.shape), whole(chunk.shape), piece, piece, whole(targets.shape), whole(mask.shape)],
            out_specs=whole((count, width + STATS)),
        ),
        out_shape=jax.ShapeDtypeStruct((count, width + STATS), F32),
        compiler_params=pltpu.CompilerParams(vmem_limit_bytes=32 << 20),
        name="cross_attend",
    )(place.reshape(1).astype(jnp.int32), acc, chunk, key_full, value_full, targets, mask)


def combine_kernel(count, valid_ref, *refs):
    parts, out_ref = refs[:-1], refs[-1]
    width = out_ref.shape[1]
    heads = width // HEAD_DIM
    for h in range(heads):
        columns = slice(h * HEAD_DIM, (h + 1) * HEAD_DIM)
        tops = [r[:, width + h : width + h + 1] for r in parts]
        tops = [tops[0]] + [jnp.where(valid_ref[i] > 0, t, NEG_FILL) for i, t in enumerate(tops[1:])]
        top = functools.reduce(jnp.maximum, tops)
        factors = [jnp.exp(t - top) for t in tops]
        total = sum(f * r[:, width + heads + h : width + heads + h + 1] for f, r in zip(factors, parts))
        summed = sum(f * r[:, columns] for f, r in zip(factors, parts))
        out_ref[:, columns] = (summed / total).astype(BF16)


def combine(own, others, valid):
    count, wide = own.shape
    return pl.pallas_call(
        functools.partial(combine_kernel, 1 + len(others)),
        in_specs=[pl.BlockSpec(memory_space=pltpu.SMEM)] + [pl.BlockSpec(memory_space=pltpu.VMEM)] * (1 + len(others)),
        out_specs=pl.BlockSpec(memory_space=pltpu.VMEM),
        out_shape=jax.ShapeDtypeStruct((count, wide - STATS), BF16),
        name="combine",
    )(valid, own, *others)


def on_device(enc_query, enc_key, enc_value, doc_ids, key_map, value_map, tgt_query):
    rows, features = enc_query.shape
    tgt_rows = tgt_query.shape[0]
    n_ctx, n_head = lax.axis_size("ctx"), lax.axis_size("head")
    ctx, head = lax.axis_index("ctx"), lax.axis_index("head")
    links = links_of(n_ctx)
    bring = lambda x, pairs: lax.ppermute(x, "ctx", pairs)

    marks = doc_ids + 1
    all_marks = [marks] + [bring(marks, pairs) for pairs in links]
    keys = [enc_key] + [bring(enc_key, pairs) for pairs in links]
    values = [enc_value] + [bring(enc_value, pairs) for pairs in links]
    targets = jnp.concatenate([tgt_query] + [bring(tgt_query, pairs) for pairs in links], 0)

    mask = (marks[:, None] == jnp.concatenate(all_marks)[None, :]).astype(F32)
    step = rows // tgt_rows
    tgt_marks = jnp.concatenate([m.reshape(tgt_rows, step)[:, 0] for m in all_marks])
    tgt_mask = (tgt_marks[:, None] == marks[None, :]).astype(F32)

    if n_ctx == 2:
        def whole_map(own):
            other = bring(own, links[0])
            low = jnp.where(ctx == 0, own, other)
            high = jnp.where(ctx == 0, other, own)
            return jnp.concatenate([low, high], 0)
    else:
        def whole_map(own):
            return lax.all_gather(own, "ctx", axis=0, tiled=True)
    key_full, value_full = whole_map(key_map), whole_map(value_map)

    chunks = 2
    heads_chunk = features // HEAD_DIM // chunks
    order = ring_order(n_head)
    pairs = [(order[i], order[(i + 1) % n_head]) for i in range(n_head)]
    before = [0] * n_head
    for source, target in pairs:
        before[target] = source
    before = jnp.array(before, jnp.int32)

    held = [encoder_attend(enc_query, keys, values, mask, j * heads_chunk, heads_chunk) for j in range(chunks)]
    owner, acc = head, None
    for turn in range(n_head - 1):
        later = [lax.ppermute(h, "head", pairs) for h in held]
        acc = project(acc, held, [owner * chunks + j for j in range(chunks)], key_full, value_full)
        held, owner = later, before[owner]
    acc = project(acc, held[:-1], [owner * chunks + j for j in range(chunks - 1)], key_full, value_full)
    partial = cross_attend(acc, held[-1], owner * chunks + chunks - 1, key_full, value_full, targets, tgt_mask)

    others, valid = [], []
    for i, pairs in enumerate(links):
        back = [(target, source) for source, target in pairs]
        piece = partial[(i + 1) * tgt_rows : (i + 2) * tgt_rows]
        others.append(bring(piece, back))
        valid.append(1 if n_ctx == 2 else jnp.where(ctx == (n_ctx - 1 if i == 0 else 0), 0, 1))
    valid = jnp.stack([jnp.asarray(v, jnp.int32) for v in valid])
    return combine(partial[:tgt_rows], others, valid)


def solution(mesh):
    in_specs = (
        P(("dp", "ctx"), "head"),
        P(("dp", "ctx"), "head"),
        P(("dp", "ctx"), "head"),
        P(("dp", "ctx")),
        P("ctx", "head"),
        P("ctx", "head"),
        P(("dp", "ctx"), "head"),
    )
    out_specs = P(("dp", "ctx"), "head")
    return jax.shard_map(
        on_device, mesh=mesh, in_specs=in_specs, out_specs=out_specs, check_vma=False
    )
```

time: 122 us -> 59.9 us (0.49)
  waiting for transfers between devices: 72.7 us -> 8.1 us
  Pallas kernels: 0 us -> 13.5 us
  matrix products: 10.9 us -> 0 us
  between operations: 13.4 us -> 6.07 us
  other arithmetic: 1.91 us -> 5.63 us
  local copies, waits for them, and re-layouts: 3.67 us -> 7.23 us
    all_gather x3 -> x0, waiting for transfers between devices: 69 us -> none  [the longest x1 46.4 us: on_device(): enc_full = lax.all_gather(enc_flat, 'head', axis=1, tiled=True)]
    pallas_call x0 -> x8, Pallas kernels: none -> 13.5 us  [the longest x2 6.74 us: encoder_attend(): pl.pallas_call(functools.partial(attend_kernel, blocks, HEAD_DIM ** (-0.5...]
    dot_general x6 -> x0, matrix products: 10.9 us -> none  [the longest x1 4.08 us: on_device(): jnp.dot(enc_full, lax.all_gather(key_map, 'ctx', axis=0, tiled=True), pre...]
    ppermute x10 -> x13, waiting for transfers between devices: 2.3 us -> 8.1 us  [the longest x6 6.69 us: on_device(): later = [lax.ppermute(h, 'head', pairs) for h in held]]
    select_n x0 -> x1, other arithmetic: none -> 3.11 us  [whole_map(): low = jnp.where(ctx == 0, own, other)]
    dynamic_slice x0 -> x3, local copies, waits for them, and re-layouts: none -> 3.08 us  [on_device(): held, owner = (later, before[owner])]
    unnamed x3 -> x0, waiting for transfers between devices: 1.39 us -> none
    unnamed x8 -> x16, local copies, waits for them, and re-layouts: 2.56 us -> 3.05 us
  transfers between devices with their start and end apart: 13 -> 13, of which waited for: 5 -> 4; matrix products, arithmetic and copies ran while one was open for 10% -> 15% of each run, Pallas kernels for 0% -> 18%
where the time goes in v1:
time: 59.9 us; the launch traced here: 59.6 us
  starting transfers between devices  19.1 us (32%)
  Pallas kernels  13.5 us (23%)
  waiting for transfers between devices  8.1 us (14%)
  local copies, waits for them, and re-layouts  7.23 us (12%)
  between operations  6.07 us (10%)
  other arithmetic  5.63 us (9%)
    ppermute x6, starting transfers between devices, on_device(): later = [lax.ppermute(h, 'head', pairs) for h in held]  17.5 us
    pallas_call x2, Pallas kernels, encoder_attend(): pl.pallas_call(functools.partial(attend_kernel, blocks, HEAD_DIM ** (-0.5...  6.74 us
    ppermute x6, waiting for transfers between devices, on_device(): later = [lax.ppermute(h, 'head', pairs) for h in held]  6.69 us
    pallas_call x4, Pallas kernels, project(): pl.pallas_call(functools.partial(project_kernel, len(chunks), acc is not...  4.19 us
    select_n x1, other arithmetic, whole_map(): low = jnp.where(ctx == 0, own, other)  3.11 us
    dynamic_slice x3, local copies, waits for them, and re-layouts, on_device(): held, owner = (later, before[owner])  3.08 us
    unnamed x16, local copies, waits for them, and re-layouts  3.05 us
    pallas_call x1, Pallas kernels, combine(): pl.pallas_call(functools.partial(combine_kernel, 1 + len(others)), in_spe...  1.82 us
  transfers between devices with their start and end apart: 13, of which 4 were waited for; matrix products, arithmetic and copies ran while one was open for 15% of the time, Pallas kernels for 18%

profile of v1, /device:TPU:0, one launch (start us, length us, event | category | flops | bytes accessed | tf_op | source)
XLA Modules:
  0.0 59.6 jit_solution(16161291018623419785)
XLA Ops:
  2.3 1.2 %dynamic_slice.9 = s32[1]{0:T(128)} dynamic-slice(s32[4]{0:T(128)} %constant.27.clone, s32[]{:T(128)S(6)} %select_n.29), dynamic_slice_sizes={1} | dynamic-slice | bytes 12 | tf_op jit(solution)/shard_map/dynamic_slice | solution.py:203
  6.4 1.2 %dynamic_slice.10 = s32[1]{0:T(128)} dynamic-slice(s32[4]{0:T(128)} %constant.27.clone, s32[]{:T(128)S(6)} %select_n.30), dynamic_slice_sizes={1} | dynamic-slice | bytes 12 | tf_op jit(solution)/shard_map/dynamic_slice | solution.py:203
  8.4 0.9 %compare_convert_fusion.mask_ref = f32[256,512]{1,0:T(8,128)} fusion(s32[512]{0:T(512)S(1)} %pad_add_fusion, s32[256]{0:T(256)S(1)} %broadcast_add_fusion), kind=kLoop, calls=%fused_computation.6 | loop fusion | flops 262144 | bytes 527360 | tf_op jit(solution)/shard_map/convert_element_type | solution.py:173
  9.3 0.8 %copy-done.3 = bf16[256,1024]{1,0:T(8,128)(2,1)} copy-done((bf16[256,1024]{1,0:T(8,128)(2,1)}, bf16[256,1024]{1,0:T(8,128)(2,1)S(1)}, u32[]{:S(2)}) %copy-start.3) | copy-done | bytes 524312
  10.1 0.8 %copy-done.4 = bf16[256,1024]{1,0:T(8,128)(2,1)} copy-done((bf16[256,1024]{1,0:T(8,128)(2,1)}, bf16[256,1024]{1,0:T(8,128)(2,1)S(1)}, u32[]{:S(2)}) %copy-start.4) | copy-done | bytes 524312
  11.0 3.4 %encoder_attend.2.refs_0_ = bf16[256,512]{1,0:T(8,128)(2,1)} custom-call(f32[256,512]{1,0:T(8,128)} %compare_convert_fusion.mask_ref, bf16[256,1024]{1,0:T(8,128)(2,1)} %q_ref.3, bf16[256,1024]{1,0:T(8,128)(2,1)} %refs_0_.3, bf16[256,1024]{1,0:T(8,128)(2,1)} %copy-done.3, bf16[256,1024]{1,0:T(8,128)(2,1)} %refs_2_.3, bf16[256,1024]{1,0:T(8,128)(2,1)} %copy-done.4), custom_call_target="tpu_custom_call" | custom-call | tf_op jit(solution)/shard_map/encoder_attend/pallas_call | solution.py:49
  14.4 4.1 %collective-permute-start.5 = (bf16[256,512]{1,0:T(8,128)(2,1)}, bf16[256,512]{1,0:T(8,128)(2,1)S(1)}, u32[]{:S(2)}, u32[]{:S(2)}) collective-permute-start(bf16[256,512]{1,0:T(8,128)(2,1)} %encoder_attend.2.refs_0_), channel_id=1, source_target_pairs={{0,2},{2,3},{3,1},{1,0},{4,6},{6,7},{7,5},{5,4},{8,10},{10,11},{11... | collective-permute-start | bytes 786440 | tf_op jit(solution)/shard_map/ppermute | solution.py:201
  18.5 3.3 %encoder_attend.3.refs_3_ = bf16[256,512]{1,0:T(8,128)(2,1)} custom-call(f32[256,512]{1,0:T(8,128)} %compare_convert_fusion.mask_ref, bf16[256,1024]{1,0:T(8,128)(2,1)} %q_ref.3, bf16[256,1024]{1,0:T(8,128)(2,1)} %refs_0_.3, bf16[256,1024]{1,0:T(8,128)(2,1)} %copy-done.3, bf16[256,1024]{1,0:T(8,128)(2,1)} %refs_2_.3, bf16[256,1024]{1,0:T(8,128)(2,1)} %copy-done.4), custom_call_target="tpu_custom_call" | custom-call | tf_op jit(solution)/shard_map/encoder_attend/pallas_call | solution.py:49
  21.8 1.6 %collective-permute-start.6 = (bf16[256,512]{1,0:T(8,128)(2,1)}, bf16[256,512]{1,0:T(8,128)(2,1)S(1)}, u32[]{:S(2)}, u32[]{:S(2)}) collective-permute-start(bf16[256,512]{1,0:T(8,128)(2,1)} %encoder_attend.3.refs_3_), channel_id=1, source_target_pairs={{0,2},{2,3},{3,1},{1,0},{4,6},{6,7},{7,5},{5,4},{8,10},{10,11},{11... | collective-permute-start | bytes 786440 | tf_op jit(solution)/shard_map/ppermute | solution.py:201
  27.0 1.8 %collective-permute-start.7 = (bf16[256,512]{1,0:T(8,128)(2,1)S(1)}, bf16[256,512]{1,0:T(8,128)(2,1)S(1)}, u32[]{:S(2)}, u32[]{:S(2)}) collective-permute-start(bf16[256,512]{1,0:T(8,128)(2,1)S(1)} %collective-permute-done.5.refs_1_), channel_id=1, source_target_pairs={{0,2},{2,3},{3,1},{1,0},{4,6},{6,7},{7,5},{5,4},{8,10},{10,11},{11... | collective-permute-start | bytes 786440 | tf_op jit(solution)/shard_map/ppermute | solution.py:201
  28.8 2.3 %collective-permute-done.6.refs_4_ = bf16[256,512]{1,0:T(8,128)(2,1)S(1)} collective-permute-done((bf16[256,512]{1,0:T(8,128)(2,1)}, bf16[256,512]{1,0:T(8,128)(2,1)S(1)}, u32[]{:S(2)}, u32[]{:S(2)}) %collective-permute-start.6) | collective-permute-done | bytes 262176 | tf_op jit(solution)/shard_map/ppermute | solution.py:201
  31.1 3.3 %collective-permute-start.8 = (bf16[256,512]{1,0:T(8,128)(2,1)S(1)}, bf16[256,512]{1,0:T(8,128)(2,1)S(1)}, u32[]{:S(2)}, u32[]{:S(2)}) collective-permute-start(bf16[256,512]{1,0:T(8,128)(2,1)S(1)} %collective-permute-done.6.refs_4_), channel_id=1, source_target_pairs={{0,2},{2,3},{3,1},{1,0},{4,6},{6,7},{7,5},{5,4},{8,10},{10,11},{11... | collective-permute-start | bytes 786440 | tf_op jit(solution)/shard_map/ppermute | solution.py:201
  34.5 2.1 %collective-permute-done.7.refs_1_ = bf16[256,512]{1,0:T(8,128)(2,1)S(1)} collective-permute-done((bf16[256,512]{1,0:T(8,128)(2,1)S(1)}, bf16[256,512]{1,0:T(8,128)(2,1)S(1)}, u32[]{:S(2)}, u32[]{:S(2)}) %collective-permute-start.7) | collective-permute-done | bytes 262176 | tf_op jit(solution)/shard_map/ppermute | solution.py:201
  36.6 3.4 %collective-permute-start.9 = (bf16[256,512]{1,0:T(8,128)(2,1)S(1)}, bf16[256,512]{1,0:T(8,128)(2,1)S(1)}, u32[]{:S(2)}, u32[]{:S(2)}) collective-permute-start(bf16[256,512]{1,0:T(8,128)(2,1)S(1)} %collective-permute-done.7.refs_1_), channel_id=1, source_target_pairs={{0,2},{2,3},{3,1},{1,0},{4,6},{6,7},{7,5},{5,4},{8,10},{10,11},{11... | collective-permute-start | bytes 786440 | tf_op jit(solution)/shard_map/ppermute | solution.py:201
  40.0 2.2 %collective-permute-done.8.refs_4_ = bf16[256,512]{1,0:T(8,128)(2,1)S(1)} collective-permute-done((bf16[256,512]{1,0:T(8,128)(2,1)S(1)}, bf16[256,512]{1,0:T(8,128)(2,1)S(1)}, u32[]{:S(2)}, u32[]{:S(2)}) %collective-permute-start.8) | collective-permute-done | bytes 262176 | tf_op jit(solution)/shard_map/ppermute | solution.py:201
  42.2 3.4 %collective-permute-start.10 = (bf16[256,512]{1,0:T(8,128)(2,1)S(1)}, bf16[256,512]{1,0:T(8,128)(2,1)S(1)}, u32[]{:S(2)}, u32[]{:S(2)}) collective-permute-start(bf16[256,512]{1,0:T(8,128)(2,1)S(1)} %collective-permute-done.8.refs_4_), channel_id=1, source_target_pairs={{0,2},{2,3},{3,1},{1,0},{4,6},{6,7},{7,5},{5,4},{8,10},{10,11},{11... | collective-permute-start | bytes 786440 | tf_op jit(solution)/shard_map/ppermute | solution.py:201
  45.6 3.1 %broadcast_select_fusion.1 = (bf16[2048,512]{1,0:T(8,128)(2,1)S(1)}, bf16[2048,512]{1,0:T(8,128)(2,1)S(1)}, bf16[2048,512]{1,0:T(8,128)(2,1)S(1)}, bf16[2048,512]{1,0:T(8,128)(2,1)S(1)}) fusion(bf16[2048,512]{1,0:T(8,128)(2,1)S(1)} %copy-done.2, bf16[2048,512]{1,0:T(8,128)(2,1)} %collective-permute-done.4, pred[]{:T(512)S(6)} %eq.17, ...), kind=kLoop, calls=%fused_computation.3 | loop fusion | flops 4194304 | bytes 16777216 | tf_op jit(solution)/shard_map/jit(_where)/select_n | solution.py:181
  50.0 1.2 %project.4.refs_0_ = f32[256,1024]{1,0:T(8,128)S(1)} custom-call(s32[2]{0:T(128)S(1)} %pad_add_fusion.3.rows_ref, bf16[256,512]{1,0:T(8,128)(2,1)S(1)} %copy-done, bf16[4096,512]{1,0:T(8,128)(2,1)S(1)} %pad_maximum_fusion.refs_1_.refs_4_.refs_2_.refs_5_.kmap_ref, bf16[4096,512]{1,0:T(8,128)(2,1)S(1)} %pad_maximum_fusion.1.refs_2_.refs_5_.refs_3_.refs_6_.vmap_ref, ...), custom_call_target="tpu_custom_call" | custom-call | tf_op jit(solution)/shard_map/project/pallas_call | solution.py:83
  51.3 1.3 %project.5.refs_0_ = f32[256,1024]{1,0:T(8,128)S(1)} custom-call(s32[2]{0:T(128)S(1)} %pad_add_fusion.2.rows_ref, f32[256,1024]{1,0:T(8,128)S(1)} %project.4.refs_0_, bf16[256,512]{1,0:T(8,128)(2,1)S(1)} %collective-permute-done.5.refs_1_, bf16[4096,512]{1,0:T(8,128)(2,1)S(1)} %pad_maximum_fusion.refs_1_.refs_4_.refs_2_.refs_5_.kmap_ref, ...), custom_call_target="tpu_custom_call" | custom-call | tf_op jit(solution)/shard_map/project/pallas_call | solution.py:83
  52.6 1.3 %project.6.refs_0_ = f32[256,1024]{1,0:T(8,128)S(1)} custom-call(s32[2]{0:T(128)S(1)} %pad_add_fusion.1.rows_ref, f32[256,1024]{1,0:T(8,128)S(1)} %project.5.refs_0_, bf16[256,512]{1,0:T(8,128)(2,1)S(1)} %collective-permute-done.7.refs_1_, bf16[4096,512]{1,0:T(8,128)(2,1)S(1)} %pad_maximum_fusion.refs_1_.refs_4_.refs_2_.refs_5_.kmap_ref, ...), custom_call_target="tpu_custom_call" | custom-call | tf_op jit(solution)/shard_map/project/pallas_call | solution.py:83
  54.3 0.8 %cross_attend.1 = f32[128,640]{1,0:T(8,128)S(1)} custom-call(s32[1]{0:T(128)S(6)} %sub.3.places_ref, f32[256,1024]{1,0:T(8,128)S(1)} %project.7.acc_ref, bf16[256,512]{1,0:T(8,128)(2,1)S(1)} %collective-permute-done.10.e_ref, bf16[4096,512]{1,0:T(8,128)(2,1)S(1)} %pad_maximum_fusion.refs_1_.refs_4_.refs_2_.refs_5_.kmap_ref, ...), custom_call_target="tpu_custom_call" | custom-call | tf_op jit(solution)/shard_map/cross_attend/pallas_call | solution.py:119
  55.0 0.7 %fusion = (f32[64,640]{1,0:T(8,128)S(1)}, f32[64,640]{1,0:T(8,128)}) fusion(f32[128,640]{1,0:T(8,128)S(1)} %cross_attend.1), kind=kLoop, calls=%fused_computation.17 | loop fusion | bytes 655360 | tf_op jit(solution)/shard_map/slice | solution.py:210
  55.7 1.4 %collective-permute-done.12.refs_1_ = f32[64,640]{1,0:T(8,128)S(1)} collective-permute-done((f32[64,640]{1,0:T(8,128)S(1)}, f32[64,640]{1,0:T(8,128)S(1)}, u32[]{:S(2)}, u32[]{:S(2)}) %collective-permute-start.12) | collective-permute-done | bytes 163872 | tf_op jit(solution)/shard_map/ppermute | solution.py:165
  57.8 1.8 %combine.1 = bf16[64,512]{1,0:T(8,128)(2,1)} custom-call(s32[1]{0:T(128)} %constant.8.clone.1.valid_ref, f32[64,640]{1,0:T(8,128)} %get-tuple-element.10.refs_0_, f32[64,640]{1,0:T(8,128)} %copy-done.5), custom_call_target="tpu_custom_call" | custom-call | tf_op jit(solution)/shard_map/combine/pallas_call | solution.py:150
  (46 shorter events, 6.1 us)
Async XLA Ops:
  0.0 45.6 %collective-permute-start.3 = (bf16[2048,512]{1,0:T(8,128)(2,1)}, bf16[2048,512]{1,0:T(8,128)(2,1)}, u32[]{:S(2)}, u32[]{:S(2)}) collective-permute-start(bf16[2048,512]{1,0:T(8,128)(2,1)} %param.12), channel_id=1, source_target_pairs={{0,4},{4,0},{1,5},{5,1},{2,6},{6,2},{3,7},{7,3},{8,12},{12,8},{9,1... | collective-permute-start | bytes 6291464 | tf_op jit(solution)/shard_map/ppermute | solution.py:165
  0.5 45.2 %collective-permute-start.4 = (bf16[2048,512]{1,0:T(8,128)(2,1)}, bf16[2048,512]{1,0:T(8,128)(2,1)}, u32[]{:S(2)}, u32[]{:S(2)}) collective-permute-start(bf16[2048,512]{1,0:T(8,128)(2,1)} %param.13), channel_id=1, source_target_pairs={{0,4},{4,0},{1,5},{5,1},{2,6},{6,2},{3,7},{7,3},{8,12},{12,8},{9,1... | collective-permute-start | bytes 6291464 | tf_op jit(solution)/shard_map/ppermute | solution.py:165
  1.2 7.1 %collective-permute-start = (s32[256]{0:T(256)S(1)}, s32[256]{0:T(256)S(1)}, u32[]{:S(2)}, u32[]{:S(2)}) collective-permute-start(s32[256]{0:T(256)S(1)} %broadcast_add_fusion), channel_id=1, source_target_pairs={{0,4},{4,0},{1,5},{5,1},{2,6},{6,2},{3,7},{7,3},{8,12},{12,8},{9,1... | collective-permute-start | bytes 3080 | tf_op jit(solution)/shard_map/ppermute | solution.py:165
  1.6 7.7 %collective-permute-start.1 = (bf16[256,1024]{1,0:T(8,128)(2,1)}, bf16[256,1024]{1,0:T(8,128)(2,1)S(1)}, u32[]{:S(2)}, u32[]{:S(2)}) collective-permute-start(bf16[256,1024]{1,0:T(8,128)(2,1)} %refs_0_.3), channel_id=1, source_target_pairs={{0,4},{4,0},{1,5},{5,1},{2,6},{6,2},{3,7},{7,3},{8,12},{12,8},{9,1... | collective-permute-start | bytes 1572872 | tf_op jit(solution)/shard_map/ppermute | solution.py:165
  1.7 7.6 %collective-permute-start.2 = (bf16[256,1024]{1,0:T(8,128)(2,1)}, bf16[256,1024]{1,0:T(8,128)(2,1)S(1)}, u32[]{:S(2)}, u32[]{:S(2)}) collective-permute-start(bf16[256,1024]{1,0:T(8,128)(2,1)} %refs_2_.3), channel_id=1, source_target_pairs={{0,4},{4,0},{1,5},{5,1},{2,6},{6,2},{3,7},{7,3},{8,12},{12,8},{9,1... | collective-permute-start | bytes 1572872 | tf_op jit(solution)/shard_map/ppermute | solution.py:165
  8.3 26.2 %collective-permute-start.11 = (bf16[64,512]{1,0:T(8,128)(2,1)}, bf16[64,512]{1,0:T(8,128)(2,1)S(1)}, u32[]{:S(2)}, u32[]{:S(2)}) collective-permute-start(bf16[64,512]{1,0:T(8,128)(2,1)} %param.14), channel_id=1, source_target_pairs={{0,4},{4,0},{1,5},{5,1},{2,6},{6,2},{3,7},{7,3},{8,12},{12,8},{9,1... | collective-permute-start | bytes 196616 | tf_op jit(solution)/shard_map/ppermute | solution.py:165
  9.3 0.8 %copy-start.3 = (bf16[256,1024]{1,0:T(8,128)(2,1)}, bf16[256,1024]{1,0:T(8,128)(2,1)S(1)}, u32[]{:S(2)}) copy-start(bf16[256,1024]{1,0:T(8,128)(2,1)S(1)} %collective-permute-done.1.refs_1_) | copy-start | bytes 1572868
  10.1 0.8 %copy-start.4 = (bf16[256,1024]{1,0:T(8,128)(2,1)}, bf16[256,1024]{1,0:T(8,128)(2,1)S(1)}, u32[]{:S(2)}) copy-start(bf16[256,1024]{1,0:T(8,128)(2,1)S(1)} %collective-permute-done.2.refs_3_) | copy-start | bytes 1572868
  14.4 11.1 %copy-start.7 = (s32[4]{0:T(128)S(1)}, s32[4]{0:T(128)}, u32[]{:S(2)}) copy-start(s32[4]{0:T(128)} %constant.27.clone) | copy-start | bytes 52
  14.4 20.1 %copy-start.6 = (bf16[64,512]{1,0:T(8,128)(2,1)S(1)}, bf16[64,512]{1,0:T(8,128)(2,1)}, u32[]{:S(2)}) copy-start(bf16[64,512]{1,0:T(8,128)(2,1)} %param.14) | copy-start | bytes 196612
  14.4 31.2 %copy-start.2 = (bf16[2048,512]{1,0:T(8,128)(2,1)S(1)}, bf16[2048,512]{1,0:T(8,128)(2,1)}, u32[]{:S(2)}) copy-start(bf16[2048,512]{1,0:T(8,128)(2,1)} %param.13) | copy-start | bytes 6291460
  14.4 12.6 %collective-permute-start.5 = (bf16[256,512]{1,0:T(8,128)(2,1)}, bf16[256,512]{1,0:T(8,128)(2,1)S(1)}, u32[]{:S(2)}, u32[]{:S(2)}) collective-permute-start(bf16[256,512]{1,0:T(8,128)(2,1)} %encoder_attend.2.refs_0_), channel_id=1, source_target_pairs={{0,2},{2,3},{3,1},{1,0},{4,6},{6,7},{7,5},{5,4},{8,10},{10,11},{11... | collective-permute-start | bytes 786440 | tf_op jit(solution)/shard_map/ppermute | solution.py:201
  21.8 9.3 %collective-permute-start.6 = (bf16[256,512]{1,0:T(8,128)(2,1)}, bf16[256,512]{1,0:T(8,128)(2,1)S(1)}, u32[]{:S(2)}, u32[]{:S(2)}) collective-permute-start(bf16[256,512]{1,0:T(8,128)(2,1)} %encoder_attend.3.refs_3_), channel_id=1, source_target_pairs={{0,2},{2,3},{3,1},{1,0},{4,6},{6,7},{7,5},{5,4},{8,10},{10,11},{11... | collective-permute-start | bytes 786440 | tf_op jit(solution)/shard_map/ppermute | solution.py:201
  27.0 9.6 %collective-permute-start.7 = (bf16[256,512]{1,0:T(8,128)(2,1)S(1)}, bf16[256,512]{1,0:T(8,128)(2,1)S(1)}, u32[]{:S(2)}, u32[]{:S(2)}) collective-permute-start(bf16[256,512]{1,0:T(8,128)(2,1)S(1)} %collective-permute-done.5.refs_1_), channel_id=1, source_target_pairs={{0,2},{2,3},{3,1},{1,0},{4,6},{6,7},{7,5},{5,4},{8,10},{10,11},{11... | collective-permute-start | bytes 786440 | tf_op jit(solution)/shard_map/ppermute | solution.py:201
  31.1 11.1 %collective-permute-start.8 = (bf16[256,512]{1,0:T(8,128)(2,1)S(1)}, bf16[256,512]{1,0:T(8,128)(2,1)S(1)}, u32[]{:S(2)}, u32[]{:S(2)}) collective-permute-start(bf16[256,512]{1,0:T(8,128)(2,1)S(1)} %collective-permute-done.6.refs_4_), channel_id=1, source_target_pairs={{0,2},{2,3},{3,1},{1,0},{4,6},{6,7},{7,5},{5,4},{8,10},{10,11},{11... | collective-permute-start | bytes 786440 | tf_op jit(solution)/shard_map/ppermute | solution.py:201
  36.6 17.2 %collective-permute-start.9 = (bf16[256,512]{1,0:T(8,128)(2,1)S(1)}, bf16[256,512]{1,0:T(8,128)(2,1)S(1)}, u32[]{:S(2)}, u32[]{:S(2)}) collective-permute-start(bf16[256,512]{1,0:T(8,128)(2,1)S(1)} %collective-permute-done.7.refs_1_), channel_id=1, source_target_pairs={{0,2},{2,3},{3,1},{1,0},{4,6},{6,7},{7,5},{5,4},{8,10},{10,11},{11... | collective-permute-start | bytes 786440 | tf_op jit(solution)/shard_map/ppermute | solution.py:201
  42.2 12.1 %collective-permute-start.10 = (bf16[256,512]{1,0:T(8,128)(2,1)S(1)}, bf16[256,512]{1,0:T(8,128)(2,1)S(1)}, u32[]{:S(2)}, u32[]{:S(2)}) collective-permute-start(bf16[256,512]{1,0:T(8,128)(2,1)S(1)} %collective-permute-done.8.refs_4_), channel_id=1, source_target_pairs={{0,2},{2,3},{3,1},{1,0},{4,6},{6,7},{7,5},{5,4},{8,10},{10,11},{11... | collective-permute-start | bytes 786440 | tf_op jit(solution)/shard_map/ppermute | solution.py:201
  49.0 1.0 %copy-start = (bf16[256,512]{1,0:T(8,128)(2,1)S(1)}, bf16[256,512]{1,0:T(8,128)(2,1)}, u32[]{:S(2)}) copy-start(bf16[256,512]{1,0:T(8,128)(2,1)} %encoder_attend.2.refs_0_) | copy-start | bytes 786436
  49.0 1.0 %copy-start.1 = (bf16[256,512]{1,0:T(8,128)(2,1)S(1)}, bf16[256,512]{1,0:T(8,128)(2,1)}, u32[]{:S(2)}) copy-start(bf16[256,512]{1,0:T(8,128)(2,1)} %encoder_attend.3.refs_3_) | copy-start | bytes 786436
  55.7 1.4 %collective-permute-start.12 = (f32[64,640]{1,0:T(8,128)S(1)}, f32[64,640]{1,0:T(8,128)S(1)}, u32[]{:S(2)}, u32[]{:S(2)}) collective-permute-start(f32[64,640]{1,0:T(8,128)S(1)} %get-tuple-element.9), channel_id=1, source_target_pairs={{4,0},{0,4},{5,1},{1,5},{6,2},{2,6},{7,3},{3,7},{12,8},{8,12},{13,... | collective-permute-start | bytes 491528 | tf_op jit(solution)/shard_map/ppermute | solution.py:165
  57.1 0.7 %copy-start.5 = (f32[64,640]{1,0:T(8,128)}, f32[64,640]{1,0:T(8,128)S(1)}, u32[]{:S(2)}) copy-start(f32[64,640]{1,0:T(8,128)S(1)} %collective-permute-done.12.refs_1_) | copy-start | bytes 491524

commit v2 on v1

v2 whole, which is shorter than its diff:
```python
import functools

import jax
import jax.numpy as jnp
from jax import lax
from jax.experimental import pallas as pl
from jax.experimental.pallas import tpu as pltpu
from jax.sharding import PartitionSpec as P

HEAD_DIM = 256
NEG_FILL = -1e30
F32 = jnp.float32
BF16 = jnp.bfloat16
STATS = 128
VMEM = pl.BlockSpec(memory_space=pltpu.VMEM)


def links_of(count):
    if count == 2:
        return [[(0, 1), (1, 0)]]
    return [[(i, i + 1) for i in range(count - 1)], [(i + 1, i) for i in range(count - 1)]]


def dot_t(a, b):
    return lax.dot_general(a, b, (((1,), (1,)), ((), ())), preferred_element_type=F32)


def same_mark(row_marks, column_marks):
    down = jnp.transpose(jnp.broadcast_to(row_marks, (STATS, row_marks.shape[1])))
    pieces = [down == column_marks[:, i : i + STATS] for i in range(0, column_marks.shape[1], STATS)]
    return jnp.concatenate(pieces, axis=1)


def attend_kernel(blocks, first, scale, *refs):
    marks, q_ref = refs[:blocks], refs[blocks]
    keys, values = refs[blocks + 1 : 2 * blocks + 1], refs[2 * blocks + 1 : 3 * blocks + 1]
    out_ref = refs[-1]
    own = marks[0][...]
    same = jnp.concatenate([same_mark(own, m[...]) for m in marks], axis=1)
    width = keys[0].shape[0]
    for h in range(out_ref.shape[1] // HEAD_DIM):
        at = slice((first + h) * HEAD_DIM, (first + h + 1) * HEAD_DIM)
        query = q_ref[:, at]
        scores = jnp.concatenate([dot_t(query, k[:, at]) for k in keys], axis=1) * scale
        scores = jnp.where(same, scores, NEG_FILL)
        weights = jnp.exp(scores - jnp.max(scores, axis=1, keepdims=True))
        total = jnp.sum(weights, axis=1, keepdims=True)
        rounded = weights.astype(BF16)
        summed = 0.0
        for i, v in enumerate(values):
            summed += jnp.dot(rounded[:, i * width : (i + 1) * width], v[:, at], preferred_element_type=F32)
        out_ref[:, h * HEAD_DIM : (h + 1) * HEAD_DIM] = (summed / total).astype(BF16)


def encoder_attend(query, keys, values, marks, first, heads):
    rows = query.shape[0]
    operands = [*marks, query, *keys, *values]
    pairs = rows * rows * len(keys) * heads
    return pl.pallas_call(
        functools.partial(attend_kernel, len(keys), first, HEAD_DIM**-0.5),
        in_specs=[VMEM] * len(operands),
        out_specs=VMEM,
        out_shape=jax.ShapeDtypeStruct((rows, heads * HEAD_DIM), BF16),
        compiler_params=pltpu.CompilerParams(vmem_limit_bytes=32 << 20),
        cost_estimate=pl.CostEstimate(
            flops=4 * pairs * HEAD_DIM, bytes_accessed=2 * rows * heads * HEAD_DIM * 6, transcendentals=pairs
        ),
        name="encoder_attend",
    )(*operands)


def project_kernel(parts, has_acc, rows_ref, *refs):
    acc_ref, out_ref = (refs[0], refs[-1])
    refs = refs[1:-1] if has_acc else refs[:-1]
    half = out_ref.shape[1] // 2
    for side in range(2):
        columns = slice(side * half, (side + 1) * half)
        total = acc_ref[:, columns] if has_acc else jnp.zeros((out_ref.shape[0], half), F32)
        for i in range(parts):
            total += jnp.dot(refs[3 * i][...], refs[3 * i + 1 + side][...], preferred_element_type=F32)
        out_ref[:, columns] = total


def project(acc, chunks, places, key_full, value_full):
    rows, depth = chunks[0].shape
    width = key_full.shape[1]
    whole = pl.BlockSpec((rows, 2 * width), lambda i, s: (0, 0))
    specs, operands = [], []
    if acc is not None:
        specs.append(whole)
        operands.append(acc)
    for i, chunk in enumerate(chunks):
        piece = pl.BlockSpec((depth, width), lambda g, s, i=i: (s[i], 0))
        specs += [pl.BlockSpec((rows, depth), lambda g, s: (0, 0)), piece, piece]
        operands += [chunk, key_full, value_full]
    return pl.pallas_call(
        functools.partial(project_kernel, len(chunks), acc is not None),
        grid_spec=pltpu.PrefetchScalarGridSpec(
            num_scalar_prefetch=1, grid=(1,), in_specs=specs, out_specs=whole
        ),
        out_shape=jax.ShapeDtypeStruct((rows, 2 * width), F32),
        compiler_params=pltpu.CompilerParams(vmem_limit_bytes=32 << 20),
        cost_estimate=pl.CostEstimate(
            flops=4 * rows * depth * width * len(chunks),
            bytes_accessed=8 * depth * width * len(chunks),
            transcendentals=0,
        ),
        name="project",
    )(jnp.stack(places).astype(jnp.int32), *operands)


def cross_kernel(scale, places_ref, acc_ref, e_ref, kmap_ref, vmap_ref, *refs):
    parts = len(refs) // 3
    own_ref, targets, marks, outs = refs[0], refs[1 : 1 + parts], refs[1 + parts : 1 + 2 * parts], refs[1 + 2 * parts :]
    width = kmap_ref.shape[1]
    mem_key = (acc_ref[:, :width] + jnp.dot(e_ref[...], kmap_ref[...], preferred_element_type=F32)).astype(BF16)
    mem_value = (acc_ref[:, width:] + jnp.dot(e_ref[...], vmap_ref[...], preferred_element_type=F32)).astype(BF16)
    heads = width // HEAD_DIM
    for tgt_ref, mark_ref, out_ref in zip(targets, marks, outs):
        same = mark_ref[...] == own_ref[...]
        lane = lax.broadcasted_iota(jnp.int32, (out_ref.shape[0], STATS), 1)
        stats = jnp.zeros((out_ref.shape[0], STATS), F32)
        for h in range(heads):
            columns = slice(h * HEAD_DIM, (h + 1) * HEAD_DIM)
            scores = dot_t(tgt_ref[:, columns], mem_key[:, columns]) * scale
            scores = jnp.where(same, scores, NEG_FILL)
            top = jnp.max(scores, axis=1, keepdims=True)
            weights = jnp.exp(scores - top)
            total = jnp.sum(weights, axis=1, keepdims=True)
            out_ref[:, columns] = jnp.dot(weights.astype(BF16), mem_value[:, columns], preferred_element_type=F32)
            stats = jnp.where(lane == h, top, jnp.where(lane == heads + h, total, stats))
        out_ref[:, width:] = stats


def cross_attend(acc, chunk, place, key_full, value_full, own_marks, targets, tgt_marks):
    rows, depth = chunk.shape
    width = key_full.shape[1]
    count = targets[0].shape[0]
    piece = pl.BlockSpec((depth, width), lambda g, s: (s[0], 0))
    whole = lambda x: pl.BlockSpec(x.shape, lambda g, s: (0, 0))
    result = jax.ShapeDtypeStruct((count, width + STATS), F32)
    return pl.pallas_call(
        functools.partial(cross_kernel, HEAD_DIM**-0.5),
        grid_spec=pltpu.PrefetchScalarGridSpec(
            num_scalar_prefetch=1,
            grid=(1,),
            in_specs=[whole(acc), whole(chunk), piece, piece] + [whole(x) for x in [own_marks, *targets, *tgt_marks]],
            out_specs=[whole(result)] * len(targets),
        ),
        out_shape=[result] * len(targets),
        compiler_params=pltpu.CompilerParams(vmem_limit_bytes=32 << 20),
        name="cross_attend",
    )(place.reshape(1).astype(jnp.int32), acc, chunk, key_full, value_full, own_marks, *targets, *tgt_marks)


def combine_kernel(*refs):
    parts, out_ref = refs[:-1], refs[-1]
    width = out_ref.shape[1]
    heads = width // HEAD_DIM
    for h in range(heads):
        columns = slice(h * HEAD_DIM, (h + 1) * HEAD_DIM)
        tops = [r[:, width + h : width + h + 1] for r in parts]
        top = functools.reduce(jnp.maximum, tops)
        factors = [jnp.exp(t - top) for t in tops]
        total = sum(f * r[:, width + heads + h : width + heads + h + 1] for f, r in zip(factors, parts))
        summed = sum(f * r[:, columns] for f, r in zip(factors, parts))
        out_ref[:, columns] = (summed / total).astype(BF16)


def combine(parts):
    count, wide = parts[0].shape
    return pl.pallas_call(
        combine_kernel,
        in_specs=[VMEM] * len(parts),
        out_specs=VMEM,
        out_shape=jax.ShapeDtypeStruct((count, wide - STATS), BF16),
        name="combine",
    )(*parts)


def on_device(enc_query, enc_key, enc_value, doc_ids, key_map, value_map, tgt_query):
    rows, features = enc_query.shape
    tgt_rows = tgt_query.shape[0]
    n_ctx, n_head = lax.axis_size("ctx"), lax.axis_size("head")
    ctx, head = lax.axis_index("ctx"), lax.axis_index("head")
    links = links_of(n_ctx)
    bring = lambda x, pairs: lax.ppermute(x, "ctx", pairs)

    marks = (doc_ids + 1).reshape(1, rows)
    all_marks = [marks] + [bring(marks, pairs) for pairs in links]
    keys = [enc_key] + [bring(enc_key, pairs) for pairs in links]
    values = [enc_value] + [bring(enc_value, pairs) for pairs in links]

    chunks = 2
    heads_chunk = features // HEAD_DIM // chunks
    held = [encoder_attend(enc_query, keys, values, all_marks, j * heads_chunk, heads_chunk) for j in range(chunks)]

    key_map, value_map, tgt_query, _ = lax.optimization_barrier((key_map, value_map, tgt_query, held[-1]))
    targets = [tgt_query] + [bring(tgt_query, pairs) for pairs in links]
    step = rows // tgt_rows
    tgt_marks = [m.reshape(tgt_rows, step)[:, :1] for m in all_marks]
    if n_ctx == 2:
        key_full, value_full = (jnp.concatenate([own, bring(own, links[0])], 0) for own in (key_map, value_map))
    else:
        key_full, value_full = (lax.all_gather(own, "ctx", axis=0, tiled=True) for own in (key_map, value_map))

    def place(owner, chunk):
        block = owner * chunks + chunk
        if n_ctx == 2:
            block = lax.rem(block + ctx * (n_head * chunks // 2), n_head * chunks)
        return block

    ways = [1 if j % 2 == 0 else -1 for j in range(chunks)]
    rings = [[(i, (i + way) % n_head) for i in range(n_head)] for way in ways]
    acc = None
    for turn in range(n_head - 1):
        later = [lax.ppermute(h, "head", ring) for h, ring in zip(held, rings)]
        places = [place(lax.rem(head + n_head - way * turn, n_head), j) for j, way in enumerate(ways)]
        acc = project(acc, held, places, key_full, value_full)
        held = later
    places = [place(lax.rem(head + n_head - way * (n_head - 1), n_head), j) for j, way in enumerate(ways)]
    acc = project(acc, held[:-1], places[:-1], key_full, value_full)
    own, *rest = cross_attend(acc, held[-1], places[-1], key_full, value_full, marks, targets, tgt_marks)

    parts = [own]
    for i, (pairs, piece) in enumerate(zip(links, rest)):
        other = bring(piece, [(target, source) for source, target in pairs])
        if n_ctx > 2:
            last = n_ctx - 1 if i == 0 else 0
            column = lax.broadcasted_iota(jnp.int32, other.shape, 1)
            other = jnp.where((ctx == last) & (column >= tgt_query.shape[1]), NEG_FILL, other)
        parts.append(other)
    return combine(parts)


def solution(mesh):
    in_specs = (
        P(("dp", "ctx"), "head"),
        P(("dp", "ctx"), "head"),
        P(("dp", "ctx"), "head"),
        P(("dp", "ctx")),
        P("ctx", "head"),
        P("ctx", "head"),
        P(("dp", "ctx"), "head"),
    )
    out_specs = P(("dp", "ctx"), "head")
    return jax.shard_map(
        on_device, mesh=mesh, in_specs=in_specs, out_specs=out_specs, check_vma=False
    )
```

time: 59.9 us -> 58.7 us (0.980)
  waiting for transfers between devices: 8.1 us -> 18.5 us
  local copies, waits for them, and re-layouts: 7.23 us -> 14.3 us
  between operations: 6.07 us -> 0.21 us
  starting transfers between devices: 19.1 us -> 14.5 us
  Pallas kernels: 13.5 us -> 9.04 us
  other arithmetic: 5.63 us -> 1.62 us
    ppermute x6, waiting for transfers between devices: 6.69 us -> 15.8 us  [on_device(): later = [lax.ppermute(h, 'head', ring) for h, ring in zip(held, rings)]]
    unnamed x16 -> x19, local copies, waits for them, and re-layouts: 3.05 us -> 10.1 us
    pallas_call x3, Pallas kernels: 8.57 us -> 3.55 us  [the longest x1 1.83 us: combine(): pl.pallas_call(combine_kernel, in_specs=[VMEM] * len(parts), out_specs=VM...]
    ppermute x6, starting transfers between devices: 17.5 us -> 12.9 us  [on_device(): later = [lax.ppermute(h, 'head', ring) for h, ring in zip(held, rings)]]
    concatenate x0 -> x2, local copies, waits for them, and re-layouts: none -> 3.45 us  [on_device(): jnp.concatenate([own, bring(own, links[0])], 0)]
    select_n x1 -> x0, other arithmetic: 3.11 us -> none  [whole_map(): low = jnp.where(ctx == 0, own, other)]
    dynamic_slice x3 -> x0, local copies, waits for them, and re-layouts: 3.08 us -> none  [on_device(): held, owner = (later, before[owner])]
    ppermute x7, waiting for transfers between devices: 1.41 us -> 2.7 us  [on_device(): bring = lambda x, pairs: lax.ppermute(x, 'ctx', pairs)]
  transfers between devices with their start and end apart: 13 -> 13, of which waited for: 4 -> 7; matrix products, arithmetic and copies ran while one was open for 15% -> 14% of each run, Pallas kernels for 18% -> 9%
where the time goes in v2:
time: 58.7 us; the launch traced here: 58.1 us
  waiting for transfers between devices  18.5 us (32%)
  starting transfers between devices  14.5 us (25%)
  local copies, waits for them, and re-layouts  14.3 us (24%)
  Pallas kernels  9.04 us (15%)
  other arithmetic  1.62 us (3%)
    ppermute x6, waiting for transfers between devices, on_device(): later = [lax.ppermute(h, 'head', ring) for h, ring in zip(held, rings)]  15.8 us
    ppermute x6, starting transfers between devices, on_device(): later = [lax.ppermute(h, 'head', ring) for h, ring in zip(held, rings)]  12.9 us
    unnamed x19, local copies, waits for them, and re-layouts  10.1 us
    pallas_call x4, Pallas kernels, project(): pl.pallas_call(functools.partial(project_kernel, len(chunks), acc is not...  4.2 us
    concatenate x2, local copies, waits for them, and re-layouts, on_device(): jnp.concatenate([own, bring(own, links[0])], 0)  3.45 us
    ppermute x7, waiting for transfers between devices, on_device(): bring = lambda x, pairs: lax.ppermute(x, 'ctx', pairs)  2.7 us
    pallas_call x1, Pallas kernels, combine(): pl.pallas_call(combine_kernel, in_specs=[VMEM] * len(parts), out_specs=VM...  1.83 us
    pallas_call x2, Pallas kernels, encoder_attend(): pl.pallas_call(functools.partial(attend_kernel, len(keys), first, HEAD_DI...  1.72 us
  transfers between devices with their start and end apart: 13, of which 7 were waited for; matrix products, arithmetic and copies ran while one was open for 14% of the time, Pallas kernels for 9%

profile of v2, /device:TPU:0, one launch (start us, length us, event | category | flops | bytes accessed | tf_op | source)
XLA Modules:
  0.0 58.1 jit_solution(5956499727097578938)
XLA Ops:
  1.6 1.1 %collective-permute-done.refs_1_ = s32[1,256]{1,0:T(1,128)S(1)} collective-permute-done((s32[1,256]{1,0:T(1,128)S(1)}, s32[1,256]{1,0:T(1,128)S(1)}, u32[]{:S(2)}, u32[]{:S(2)}) %collective-permute-start) | collective-permute-done | bytes 1056 | tf_op jit(solution)/shard_map/ppermute | solution.py:187
  3.0 1.0 %copy-done = bf16[256,1024]{1,0:T(8,128)(2,1)S(1)} copy-done((bf16[256,1024]{1,0:T(8,128)(2,1)S(1)}, bf16[256,1024]{1,0:T(8,128)(2,1)}, u32[]{:S(2)}) %copy-start) | copy-done | bytes 524312
  4.0 1.0 %copy-done.2 = bf16[256,1024]{1,0:T(8,128)(2,1)S(1)} copy-done((bf16[256,1024]{1,0:T(8,128)(2,1)S(1)}, bf16[256,1024]{1,0:T(8,128)(2,1)}, u32[]{:S(2)}) %copy-start.2) | copy-done | bytes 524312
  5.0 1.0 %copy-done.4 = bf16[256,1024]{1,0:T(8,128)(2,1)S(1)} copy-done((bf16[256,1024]{1,0:T(8,128)(2,1)S(1)}, bf16[256,1024]{1,0:T(8,128)(2,1)}, u32[]{:S(2)}) %copy-start.4) | copy-done | bytes 524312
  7.5 5.0 %collective-permute-start.6 = (bf16[256,512]{1,0:T(8,128)(2,1)S(1)}, bf16[256,512]{1,0:T(8,128)(2,1)S(1)}, u32[]{:S(2)}, u32[]{:S(2)}) collective-permute-start(bf16[256,512]{1,0:T(8,128)(2,1)S(1)} %encoder_attend.3.refs_3_), channel_id=1, source_target_pairs={{0,3},{1,0},{2,1},{3,2},{4,7},{5,4},{6,5},{7,6},{8,11},{9,8},{10,9... | collective-permute-start | bytes 786440 | tf_op jit(solution)/shard_map/ppermute | solution.py:217
  12.5 1.0 %copy-done.1 = bf16[256,1024]{1,0:T(8,128)(2,1)S(1)} copy-done((bf16[256,1024]{1,0:T(8,128)(2,1)S(1)}, bf16[256,1024]{1,0:T(8,128)(2,1)}, u32[]{:S(2)}) %copy-start.1) | copy-done | bytes 524312
  13.5 1.0 %copy-done.3 = bf16[256,1024]{1,0:T(8,128)(2,1)S(1)} copy-done((bf16[256,1024]{1,0:T(8,128)(2,1)S(1)}, bf16[256,1024]{1,0:T(8,128)(2,1)}, u32[]{:S(2)}) %copy-start.3) | copy-done | bytes 524312
  14.6 1.0 %copy-done.5 = bf16[256,1024]{1,0:T(8,128)(2,1)S(1)} copy-done((bf16[256,1024]{1,0:T(8,128)(2,1)S(1)}, bf16[256,1024]{1,0:T(8,128)(2,1)}, u32[]{:S(2)}) %copy-start.5) | copy-done | bytes 524312
  18.4 8.0 %collective-permute-done.5.refs_1_ = bf16[256,512]{1,0:T(8,128)(2,1)S(1)} collective-permute-done((bf16[256,512]{1,0:T(8,128)(2,1)S(1)}, bf16[256,512]{1,0:T(8,128)(2,1)S(1)}, u32[]{:S(2)}, u32[]{:S(2)}) %collective-permute-start.5) | collective-permute-done | bytes 262176 | tf_op jit(solution)/shard_map/ppermute | solution.py:217
  26.5 3.7 %collective-permute-start.8 = (bf16[256,512]{1,0:T(8,128)(2,1)S(1)}, bf16[256,512]{1,0:T(8,128)(2,1)S(1)}, u32[]{:S(2)}, u32[]{:S(2)}) collective-permute-start(bf16[256,512]{1,0:T(8,128)(2,1)S(1)} %collective-permute-done.6.refs_4_), channel_id=1, source_target_pairs={{0,3},{1,0},{2,1},{3,2},{4,7},{5,4},{6,5},{7,6},{8,11},{9,8},{10,9... | collective-permute-start | bytes 786440 | tf_op jit(solution)/shard_map/ppermute | solution.py:217
  30.2 2.5 %constant_dynamic-update-slice_fusion.1 = (bf16[4096,512]{1,0:T(8,128)(2,1)S(1)}, bf16[4096,512]{1,0:T(8,128)(2,1)S(1)}) fusion(bf16[2048,512]{1,0:T(8,128)(2,1)} %param.11, bf16[2048,512]{1,0:T(8,128)(2,1)} %param.12), kind=kLoop, calls=%fused_computation.1 | loop fusion | bytes 8388608
  32.7 4.7 %collective-permute-done.7.refs_1_ = bf16[256,512]{1,0:T(8,128)(2,1)S(1)} collective-permute-done((bf16[256,512]{1,0:T(8,128)(2,1)S(1)}, bf16[256,512]{1,0:T(8,128)(2,1)S(1)}, u32[]{:S(2)}, u32[]{:S(2)}) %collective-permute-start.7) | collective-permute-done | bytes 262176 | tf_op jit(solution)/shard_map/ppermute | solution.py:217
  37.4 1.3 %collective-permute-start.9 = (bf16[256,512]{1,0:T(8,128)(2,1)S(1)}, bf16[256,512]{1,0:T(8,128)(2,1)S(1)}, u32[]{:S(2)}, u32[]{:S(2)}) collective-permute-start(bf16[256,512]{1,0:T(8,128)(2,1)S(1)} %collective-permute-done.7.refs_1_), channel_id=1, source_target_pairs={{0,1},{1,2},{2,3},{3,0},{4,5},{5,6},{6,7},{7,4},{8,9},{9,10},{10,1... | collective-permute-start | bytes 786440 | tf_op jit(solution)/shard_map/ppermute | solution.py:217
  38.7 1.8 %collective-permute-done.8.refs_4_ = bf16[256,512]{1,0:T(8,128)(2,1)S(1)} collective-permute-done((bf16[256,512]{1,0:T(8,128)(2,1)S(1)}, bf16[256,512]{1,0:T(8,128)(2,1)S(1)}, u32[]{:S(2)}, u32[]{:S(2)}) %collective-permute-start.8) | collective-permute-done | bytes 262176 | tf_op jit(solution)/shard_map/ppermute | solution.py:217
  40.4 2.8 %collective-permute-start.10 = (bf16[256,512]{1,0:T(8,128)(2,1)S(1)}, bf16[256,512]{1,0:T(8,128)(2,1)S(1)}, u32[]{:S(2)}, u32[]{:S(2)}) collective-permute-start(bf16[256,512]{1,0:T(8,128)(2,1)S(1)} %collective-permute-done.8.refs_4_), channel_id=1, source_target_pairs={{0,3},{1,0},{2,1},{3,2},{4,7},{5,4},{6,5},{7,6},{8,11},{9,8},{10,9... | collective-permute-start | bytes 786440 | tf_op jit(solution)/shard_map/ppermute | solution.py:217
  43.2 1.7 %constant_dynamic-update-slice_fusion.refs_1_.refs_4_.refs_2_.refs_5_.kmap_ref = bf16[4096,512]{1,0:T(8,128)(2,1)S(1)} fusion(bf16[4096,512]{1,0:T(8,128)(2,1)S(1)} %get-tuple-element.15, bf16[2048,512]{1,0:T(8,128)(2,1)} %collective-permute-done.3), kind=kLoop, calls=%fused_computation | loop fusion | bytes 4194304 | tf_op jit(solution)/shard_map/concatenate | solution.py:203
  45.0 1.7 %constant_dynamic-update-slice_fusion.2.refs_2_.refs_5_.refs_3_.refs_6_.vmap_ref = bf16[4096,512]{1,0:T(8,128)(2,1)S(1)} fusion(bf16[4096,512]{1,0:T(8,128)(2,1)S(1)} %get-tuple-element.16, bf16[2048,512]{1,0:T(8,128)(2,1)} %collective-permute-done.4), kind=kLoop, calls=%fused_computation.2 | loop fusion | bytes 4194304 | tf_op jit(solution)/shard_map/concatenate | solution.py:203
  46.7 1.2 %project.4.refs_0_ = f32[256,1024]{1,0:T(8,128)S(1)} custom-call(s32[2]{0:T(128)S(1)} %pad_add_fusion.2.rows_ref, bf16[256,512]{1,0:T(8,128)(2,1)S(1)} %encoder_attend.2.refs_0_, bf16[4096,512]{1,0:T(8,128)(2,1)S(1)} %constant_dynamic-update-slice_fusion.refs_1_.refs_4_.refs_2_.refs_5_.kmap_ref, ...), custom_call_target="tpu_custom_call" | custom-call | flops 536870912 | bytes 4194304 | tf_op jit(solution)/shard_map/project/pallas_call | solution.py:96
  47.9 1.3 %project.5.refs_0_ = f32[256,1024]{1,0:T(8,128)S(1)} custom-call(s32[2]{0:T(128)S(1)} %pad_add_fusion.1.rows_ref, f32[256,1024]{1,0:T(8,128)S(1)} %project.4.refs_0_, bf16[256,512]{1,0:T(8,128)(2,1)S(1)} %collective-permute-done.5.refs_1_, bf16[4096,512]{1,0:T(8,128)(2,1)S(1)} %constant_dynamic-update-slice_fusion.refs_1_.refs_4_.refs_2_.refs_5_.kmap_ref, ...), custom_call_target="tpu_custom_call" | custom-call | flops 536870912 | bytes 4194304 | tf_op jit(solution)/shard_map/project/pallas_call | solution.py:96
  49.2 1.3 %project.6.refs_0_ = f32[256,1024]{1,0:T(8,128)S(1)} custom-call(s32[2]{0:T(128)S(1)} %pad_add_fusion.rows_ref, f32[256,1024]{1,0:T(8,128)S(1)} %project.5.refs_0_, bf16[256,512]{1,0:T(8,128)(2,1)S(1)} %collective-permute-done.7.refs_1_, bf16[4096,512]{1,0:T(8,128)(2,1)S(1)} %constant_dynamic-update-slice_fusion.refs_1_.refs_4_.refs_2_.refs_5_.kmap_ref, ...), custom_call_target="tpu_custom_call" | custom-call | flops 536870912 | bytes 4194304 | tf_op jit(solution)/shard_map/project/pallas_call | solution.py:96
  50.9 1.4 %collective-permute-done.10.e_ref = bf16[256,512]{1,0:T(8,128)(2,1)S(1)} collective-permute-done((bf16[256,512]{1,0:T(8,128)(2,1)S(1)}, bf16[256,512]{1,0:T(8,128)(2,1)S(1)}, u32[]{:S(2)}, u32[]{:S(2)}) %collective-permute-start.10) | collective-permute-done | bytes 262176 | tf_op jit(solution)/shard_map/ppermute | solution.py:217
  52.3 1.3 %cross_attend.1 = (f32[64,640]{1,0:T(8,128)S(1)}, f32[64,640]{1,0:T(8,128)S(1)}) custom-call(s32[1]{0:T(128)} %bitcast.places_ref, f32[256,1024]{1,0:T(8,128)S(1)} %project.7.acc_ref, bf16[256,512]{1,0:T(8,128)(2,1)S(1)} %collective-permute-done.10.e_ref, bf16[4096,512]{1,0:T(8,128)(2,1)S(1)} %constant_dynamic-update-slice_fusion.refs_1_.refs_4_.refs_2_.refs_5_.kmap_ref, ...), custom_call_target="tpu_custom_call" | custom-call | tf_op jit(solution)/shard_map/cross_attend/pallas_call | solution.py:142
  54.3 1.4 %collective-permute-done.12.refs_1_ = f32[64,640]{1,0:T(8,128)S(1)} collective-permute-done((f32[64,640]{1,0:T(8,128)S(1)}, f32[64,640]{1,0:T(8,128)S(1)}, u32[]{:S(2)}, u32[]{:S(2)}) %collective-permute-start.12) | collective-permute-done | bytes 163872 | tf_op jit(solution)/shard_map/ppermute | solution.py:187
  56.3 1.8 %combine.1 = bf16[64,512]{1,0:T(8,128)(2,1)} custom-call(f32[64,640]{1,0:T(8,128)} %copy-done.6, f32[64,640]{1,0:T(8,128)} %copy-done.8), custom_call_target="tpu_custom_call" | custom-call | tf_op jit(solution)/shard_map/combine/pallas_call | solution.py:172
  (39 shorter events, 7.9 us)
Async XLA Ops:
  0.0 2.7 %collective-permute-start.1 = (bf16[256,1024]{1,0:T(8,128)(2,1)}, bf16[256,1024]{1,0:T(8,128)(2,1)S(1)}, u32[]{:S(2)}, u32[]{:S(2)}) collective-permute-start(bf16[256,1024]{1,0:T(8,128)(2,1)} %refs_3_.3), channel_id=1, source_target_pairs={{0,4},{4,0},{1,5},{5,1},{2,6},{6,2},{3,7},{7,3},{8,12},{12,8},{9,1... | collective-permute-start | bytes 1572872 | tf_op jit(solution)/shard_map/ppermute | solution.py:187
  0.5 2.5 %collective-permute-start.2 = (bf16[256,1024]{1,0:T(8,128)(2,1)}, bf16[256,1024]{1,0:T(8,128)(2,1)S(1)}, u32[]{:S(2)}, u32[]{:S(2)}) collective-permute-start(bf16[256,1024]{1,0:T(8,128)(2,1)} %refs_5_.3), channel_id=1, source_target_pairs={{0,4},{4,0},{1,5},{5,1},{2,6},{6,2},{3,7},{7,3},{8,12},{12,8},{9,1... | collective-permute-start | bytes 1572872 | tf_op jit(solution)/shard_map/ppermute | solution.py:187
  1.2 1.5 %collective-permute-start = (s32[1,256]{1,0:T(1,128)S(1)}, s32[1,256]{1,0:T(1,128)S(1)}, u32[]{:S(2)}, u32[]{:S(2)}) collective-permute-start(s32[1,256]{1,0:T(1,128)S(1)} %bitcast.13), channel_id=1, source_target_pairs={{0,4},{4,0},{1,5},{5,1},{2,6},{6,2},{3,7},{7,3},{8,12},{12,8},{9,1... | collective-permute-start | bytes 3080 | tf_op jit(solution)/shard_map/ppermute | solution.py:187
  3.0 1.0 %copy-start = (bf16[256,1024]{1,0:T(8,128)(2,1)S(1)}, bf16[256,1024]{1,0:T(8,128)(2,1)}, u32[]{:S(2)}) copy-start(bf16[256,1024]{1,0:T(8,128)(2,1)} %refs_2_.3) | copy-start | bytes 1572868
  4.0 1.0 %copy-start.2 = (bf16[256,1024]{1,0:T(8,128)(2,1)S(1)}, bf16[256,1024]{1,0:T(8,128)(2,1)}, u32[]{:S(2)}) copy-start(bf16[256,1024]{1,0:T(8,128)(2,1)} %refs_3_.3) | copy-start | bytes 1572868
  5.0 1.0 %copy-start.4 = (bf16[256,1024]{1,0:T(8,128)(2,1)S(1)}, bf16[256,1024]{1,0:T(8,128)(2,1)}, u32[]{:S(2)}) copy-start(bf16[256,1024]{1,0:T(8,128)(2,1)} %refs_5_.3) | copy-start | bytes 1572868
  6.1 12.3 %copy-start.7 = (bf16[64,512]{1,0:T(8,128)(2,1)S(1)}, bf16[64,512]{1,0:T(8,128)(2,1)}, u32[]{:S(2)}) copy-start(bf16[64,512]{1,0:T(8,128)(2,1)} %refs_1_) | copy-start | bytes 196612
  6.9 36.3 %collective-permute-start.3 = (bf16[2048,512]{1,0:T(8,128)(2,1)}, bf16[2048,512]{1,0:T(8,128)(2,1)}, u32[]{:S(2)}, u32[]{:S(2)}) collective-permute-start(bf16[2048,512]{1,0:T(8,128)(2,1)} %param.11), channel_id=1, source_target_pairs={{0,4},{4,0},{1,5},{5,1},{2,6},{6,2},{3,7},{7,3},{8,12},{12,8},{9,1... | collective-permute-start | bytes 6291464 | tf_op jit(solution)/shard_map/ppermute | solution.py:187
  7.4 37.6 %collective-permute-start.4 = (bf16[2048,512]{1,0:T(8,128)(2,1)}, bf16[2048,512]{1,0:T(8,128)(2,1)}, u32[]{:S(2)}, u32[]{:S(2)}) collective-permute-start(bf16[2048,512]{1,0:T(8,128)(2,1)} %param.12), channel_id=1, source_target_pairs={{0,4},{4,0},{1,5},{5,1},{2,6},{6,2},{3,7},{7,3},{8,12},{12,8},{9,1... | collective-permute-start | bytes 6291464 | tf_op jit(solution)/shard_map/ppermute | solution.py:187
  7.5 19.0 %collective-permute-start.6 = (bf16[256,512]{1,0:T(8,128)(2,1)S(1)}, bf16[256,512]{1,0:T(8,128)(2,1)S(1)}, u32[]{:S(2)}, u32[]{:S(2)}) collective-permute-start(bf16[256,512]{1,0:T(8,128)(2,1)S(1)} %encoder_attend.3.refs_3_), channel_id=1, source_target_pairs={{0,3},{1,0},{2,1},{3,2},{4,7},{5,4},{6,5},{7,6},{8,11},{9,8},{10,9... | collective-permute-start | bytes 786440 | tf_op jit(solution)/shard_map/ppermute | solution.py:217
  12.5 1.0 %copy-start.1 = (bf16[256,1024]{1,0:T(8,128)(2,1)S(1)}, bf16[256,1024]{1,0:T(8,128)(2,1)}, u32[]{:S(2)}) copy-start(bf16[256,1024]{1,0:T(8,128)(2,1)} %refs_2_.3) | copy-start | bytes 1572868
  13.5 1.0 %copy-start.3 = (bf16[256,1024]{1,0:T(8,128)(2,1)S(1)}, bf16[256,1024]{1,0:T(8,128)(2,1)}, u32[]{:S(2)}) copy-start(bf16[256,1024]{1,0:T(8,128)(2,1)} %refs_3_.3) | copy-start | bytes 1572868
  14.6 1.0 %copy-start.5 = (bf16[256,1024]{1,0:T(8,128)(2,1)S(1)}, bf16[256,1024]{1,0:T(8,128)(2,1)}, u32[]{:S(2)}) copy-start(bf16[256,1024]{1,0:T(8,128)(2,1)} %refs_5_.3) | copy-start | bytes 1572868
  16.5 9.9 %collective-permute-start.5 = (bf16[256,512]{1,0:T(8,128)(2,1)S(1)}, bf16[256,512]{1,0:T(8,128)(2,1)S(1)}, u32[]{:S(2)}, u32[]{:S(2)}) collective-permute-start(bf16[256,512]{1,0:T(8,128)(2,1)S(1)} %encoder_attend.2.refs_0_), channel_id=1, source_target_pairs={{0,1},{1,2},{2,3},{3,0},{4,5},{5,6},{6,7},{7,4},{8,9},{9,10},{10,1... | collective-permute-start | bytes 786440 | tf_op jit(solution)/shard_map/ppermute | solution.py:217
  18.4 32.6 %collective-permute-start.11 = (bf16[64,512]{1,0:T(8,128)(2,1)S(1)}, bf16[64,512]{1,0:T(8,128)(2,1)S(1)}, u32[]{:S(2)}, u32[]{:S(2)}) collective-permute-start(bf16[64,512]{1,0:T(8,128)(2,1)S(1)} %copy-done.7), channel_id=1, source_target_pairs={{0,4},{4,0},{1,5},{5,1},{2,6},{6,2},{3,7},{7,3},{8,12},{12,8},{9,1... | collective-permute-start | bytes 196616 | tf_op jit(solution)/shard_map/ppermute | solution.py:187
  26.4 11.0 %collective-permute-start.7 = (bf16[256,512]{1,0:T(8,128)(2,1)S(1)}, bf16[256,512]{1,0:T(8,128)(2,1)S(1)}, u32[]{:S(2)}, u32[]{:S(2)}) collective-permute-start(bf16[256,512]{1,0:T(8,128)(2,1)S(1)} %collective-permute-done.5.refs_1_), channel_id=1, source_target_pairs={{0,1},{1,2},{2,3},{3,0},{4,5},{5,6},{6,7},{7,4},{8,9},{9,10},{10,1... | collective-permute-start | bytes 786440 | tf_op jit(solution)/shard_map/ppermute | solution.py:217
  26.5 13.9 %collective-permute-start.8 = (bf16[256,512]{1,0:T(8,128)(2,1)S(1)}, bf16[256,512]{1,0:T(8,128)(2,1)S(1)}, u32[]{:S(2)}, u32[]{:S(2)}) collective-permute-start(bf16[256,512]{1,0:T(8,128)(2,1)S(1)} %collective-permute-done.6.refs_4_), channel_id=1, source_target_pairs={{0,3},{1,0},{2,1},{3,2},{4,7},{5,4},{6,5},{7,6},{8,11},{9,8},{10,9... | collective-permute-start | bytes 786440 | tf_op jit(solution)/shard_map/ppermute | solution.py:217
  37.4 13.0 %collective-permute-start.9 = (bf16[256,512]{1,0:T(8,128)(2,1)S(1)}, bf16[256,512]{1,0:T(8,128)(2,1)S(1)}, u32[]{:S(2)}, u32[]{:S(2)}) collective-permute-start(bf16[256,512]{1,0:T(8,128)(2,1)S(1)} %collective-permute-done.7.refs_1_), channel_id=1, source_target_pairs={{0,1},{1,2},{2,3},{3,0},{4,5},{5,6},{6,7},{7,4},{8,9},{9,10},{10,1... | collective-permute-start | bytes 786440 | tf_op jit(solution)/shard_map/ppermute | solution.py:217
  40.4 11.8 %collective-permute-start.10 = (bf16[256,512]{1,0:T(8,128)(2,1)S(1)}, bf16[256,512]{1,0:T(8,128)(2,1)S(1)}, u32[]{:S(2)}, u32[]{:S(2)}) collective-permute-start(bf16[256,512]{1,0:T(8,128)(2,1)S(1)} %collective-permute-done.8.refs_4_), channel_id=1, source_target_pairs={{0,3},{1,0},{2,1},{3,2},{4,7},{5,4},{6,5},{7,6},{8,11},{9,8},{10,9... | collective-permute-start | bytes 786440 | tf_op jit(solution)/shard_map/ppermute | solution.py:217
  53.6 0.7 %copy-start.6 = (f32[64,640]{1,0:T(8,128)}, f32[64,640]{1,0:T(8,128)S(1)}, u32[]{:S(2)}) copy-start(f32[64,640]{1,0:T(8,128)S(1)} %get-tuple-element.13.refs_0_) | copy-start | bytes 491524
  54.3 1.4 %collective-permute-start.12 = (f32[64,640]{1,0:T(8,128)S(1)}, f32[64,640]{1,0:T(8,128)S(1)}, u32[]{:S(2)}, u32[]{:S(2)}) collective-permute-start(f32[64,640]{1,0:T(8,128)S(1)} %get-tuple-element.14), channel_id=1, source_target_pairs={{4,0},{0,4},{5,1},{1,5},{6,2},{2,6},{7,3},{3,7},{12,8},{8,12},{13,... | collective-permute-start | bytes 491528 | tf_op jit(solution)/shard_map/ppermute | solution.py:187
  55.7 0.7 %copy-start.8 = (f32[64,640]{1,0:T(8,128)}, f32[64,640]{1,0:T(8,128)S(1)}, u32[]{:S(2)}) copy-start(f32[64,640]{1,0:T(8,128)S(1)} %collective-permute-done.12.refs_1_) | copy-start | bytes 491524

commit v3 on v0

v3 whole, which is shorter than its diff:
```python
import functools

import jax
import jax.numpy as jnp
from jax import lax
from jax.experimental import pallas as pl
from jax.experimental.pallas import tpu as pltpu
from jax.sharding import PartitionSpec as P

HEAD_DIM = 256
NEG_FILL = -1e30
F32 = jnp.float32
BF16 = jnp.bfloat16
LANES = 128
SCALE = HEAD_DIM**-0.5
VMEM = pl.BlockSpec(memory_space=pltpu.VMEM)
HBM = pl.BlockSpec(memory_space=pltpu.HBM)


def ring_order(count):
    return list(range(0, count, 2)) + list(range(1, count, 2))[::-1]


def links_of(count):
    if count == 2:
        return [[(0, 1), (1, 0)]]
    return [[(i, i + 1) for i in range(count - 1)], [(i + 1, i) for i in range(count - 1)]]


def dot_t(a, b):
    return lax.dot_general(a, b, (((1,), (1,)), ((), ())), preferred_element_type=F32)


def dot(a, b):
    return jnp.dot(a, b, preferred_element_type=F32)


def head_columns(h):
    return slice(h * HEAD_DIM, (h + 1) * HEAD_DIM)


def down_lanes(row):
    return jnp.transpose(jnp.broadcast_to(row, (LANES, row.shape[1])))


def same_mark(down, row):
    return jnp.concatenate([down == row[:, i : i + LANES] for i in range(0, row.shape[1], LANES)], axis=1)


def softmax_block(scores, same):
    scores = jnp.where(same, scores * SCALE, NEG_FILL)
    top = jnp.max(scores, axis=1, keepdims=True)
    weights = jnp.exp(scores - top)
    return top, weights, jnp.sum(weights, axis=1, keepdims=True)


def call(kernel, name, outs, operands, flops=0, exps=0, specs=None, scratch=(), limit=8 << 20):
    out_shape = [jax.ShapeDtypeStruct(*o) for o in outs]
    moved = sum(x.size * x.dtype.itemsize for x in [*operands, *out_shape])
    return pl.pallas_call(
        kernel,
        in_specs=specs or [VMEM] * len(operands),
        out_specs=[VMEM] * len(outs),
        out_shape=out_shape,
        scratch_shapes=list(scratch),
        compiler_params=pltpu.CompilerParams(vmem_limit_bytes=limit),
        cost_estimate=pl.CostEstimate(flops=flops, bytes_accessed=moved, transcendentals=exps),
        name=name,
    )(*operands)


def attend_own_kernel(marks_ref, q_hbm, k_hbm, v_hbm, q_ref, sum_ref, stat_ref, k_ref, v_ref, sems):
    heads = q_ref.shape[1] // HEAD_DIM
    copies = []
    for h in range(heads):
        at = head_columns(h)
        for i, (source, target) in enumerate(((q_hbm, q_ref), (k_hbm, k_ref), (v_hbm, v_ref))):
            copies.append(pltpu.make_async_copy(source.at[:, at], target.at[:, at], sems.at[3 * h + i]))
    for copy in copies:
        copy.start()
    marks = marks_ref[...]
    same = same_mark(down_lanes(marks), marks)
    lane = lax.broadcasted_iota(jnp.int32, stat_ref.shape, 1)
    stats = jnp.zeros(stat_ref.shape, F32)
    for h in range(heads):
        at = head_columns(h)
        copies[3 * h].wait()
        copies[3 * h + 1].wait()
        top, weights, total = softmax_block(dot_t(q_ref[:, at], k_ref[:, at]), same)
        copies[3 * h + 2].wait()
        sum_ref[:, at] = dot(weights.astype(BF16), v_ref[:, at])
        stats = jnp.where(lane == h, top, jnp.where(lane == heads + h, total, stats))
    stat_ref[...] = stats


def attend_near_kernel(near, *refs):
    marks, (q_ref, sum_ref, stat_ref) = refs[: near + 1], refs[near + 1 : near + 4]
    keys, values = refs[near + 4 : 2 * near + 4], refs[2 * near + 4 : 3 * near + 4]
    outs = refs[3 * near + 4 :]
    heads = q_ref.shape[1] // HEAD_DIM
    down = down_lanes(marks[0][...])
    same = jnp.concatenate([same_mark(down, m[...]) for m in marks[1:]], axis=1)
    rows = q_ref.shape[0]
    each = heads // len(outs)
    for h in range(heads):
        at = head_columns(h)
        scores = jnp.concatenate([dot_t(q_ref[:, at], k[:, at]) for k in keys], axis=1)
        scores = jnp.where(same, scores * SCALE, NEG_FILL)
        own_top, own_total = stat_ref[:, h : h + 1], stat_ref[:, heads + h : heads + h + 1]
        top = jnp.maximum(jnp.max(scores, axis=1, keepdims=True), own_top)
        weights = jnp.exp(scores - top)
        factor = jnp.exp(own_top - top)
        total = factor * own_total + jnp.sum(weights, axis=1, keepdims=True)
        rounded = weights.astype(BF16)
        summed = factor * sum_ref[:, at]
        for i, v in enumerate(values):
            summed += dot(rounded[:, i * rows : (i + 1) * rows], v[:, at])
        outs[h // each][:, head_columns(h % each)] = (summed / total).astype(BF16)


def encoder_attend(query, key, value, marks, keys, values, near_marks, chunks):
    rows, width = query.shape
    heads = width // HEAD_DIM
    pairs = rows * rows * heads
    copied, summed, stats = call(
        attend_own_kernel,
        "attend_own",
        [((rows, width), BF16), ((rows, width), F32), ((rows, LANES), F32)],
        [marks, *(pltpu.with_memory_space_constraint(x, pltpu.HBM) for x in (query, key, value))],
        flops=4 * pairs * HEAD_DIM,
        exps=pairs,
        specs=[VMEM, HBM, HBM, HBM],
        scratch=[pltpu.VMEM((rows, width), BF16)] * 2 + [pltpu.SemaphoreType.DMA((3 * heads,))],
    )
    return call(
        functools.partial(attend_near_kernel, len(keys)),
        "attend_near",
        [((rows, width // chunks), BF16)] * chunks,
        [marks, *near_marks, copied, summed, stats, *keys, *values],
        flops=4 * pairs * HEAD_DIM * len(keys),
        exps=pairs * len(keys),
    )


def target_mask_kernel(step, own_ref, *refs):
    marks, out_ref, down_ref = refs[:-2], refs[-2], refs[-1]
    own = own_ref[...]
    count = out_ref.shape[0] // len(marks)
    for i, mark_ref in enumerate(marks):
        down_ref[...] = down_lanes(mark_ref[...])
        down = down_ref[pl.ds(0, count, stride=step), :]
        out_ref[i * count : (i + 1) * count, :] = same_mark(down, own).astype(F32)


def target_mask(marks, all_marks, tgt_rows):
    rows = marks.shape[1]
    return call(
        functools.partial(target_mask_kernel, rows // tgt_rows),
        "target_mask",
        [((tgt_rows * len(all_marks), rows), F32)],
        [marks, *all_marks],
        scratch=[pltpu.VMEM((rows, LANES), jnp.int32)],
    )[0]


def add_products(acc_of, store, e_ref, place, key_shards, value_shards):
    shard, block = place
    depth = e_ref.shape[1]
    at = pl.ds(pl.multiple_of(block * depth, depth), depth)

    def add(i):
        for side, shards in enumerate((key_shards, value_shards)):
            store(side, acc_of(side) + dot(e_ref[...], shards[i][at, :]))

    if len(key_shards) == 1:
        add(0)
    else:
        for i in range(len(key_shards)):
            pl.when(shard == i)(functools.partial(add, i))


def project_kernel(chunks, shards, has_acc, places, *refs):
    out_ref = refs[-1]
    e_refs, maps = refs[:chunks], refs[chunks : chunks + 2 * shards]
    half = out_ref.shape[1] // 2
    side_of = lambda side: slice(side * half, (side + 1) * half)

    def store(side, value):
        out_ref[:, side_of(side)] = value

    for i, (e_ref, place) in enumerate(zip(e_refs, places())):
        if i:
            acc_of = lambda side: out_ref[:, side_of(side)]
        elif has_acc:
            acc_of = lambda side: refs[-2][:, side_of(side)]
        else:
            acc_of = lambda side: 0.0
        add_products(acc_of, store, e_ref, place, maps[:shards], maps[shards:])


def project(acc, chunks, places, key_shards, value_shards):
    rows, depth = chunks[0].shape
    width = key_shards[0].shape[1]
    operands = [*chunks, *key_shards, *value_shards] + ([] if acc is None else [acc])
    return call(
        functools.partial(project_kernel, len(chunks), len(key_shards), acc is not None, places),
        "project",
        [((rows, 2 * width), F32)],
        operands,
        flops=4 * rows * depth * width * len(chunks),
    )[0]


def cross_kernel(shards, places, e_ref, *refs):
    maps, (acc_ref, tgt_ref, mask_ref) = refs[: 2 * shards], refs[2 * shards : 2 * shards + 3]
    outs, mem_ref = refs[2 * shards + 3 : -1], refs[-1]
    half = mem_ref.shape[1] // 2
    side_of = lambda side: slice(side * half, (side + 1) * half)

    def store(side, value):
        mem_ref[:, side_of(side)] = value.astype(BF16)

    (place,) = places()
    add_products(lambda side: acc_ref[:, side_of(side)], store, e_ref, place, maps[:shards], maps[shards:])
    heads = half // HEAD_DIM
    count = outs[0].shape[0]
    lane = lax.broadcasted_iota(jnp.int32, (tgt_ref.shape[0], LANES), 1)
    stats = jnp.zeros(lane.shape, F32)
    same = mask_ref[...] > 0
    for h in range(heads):
        at = head_columns(h)
        top, weights, total = softmax_block(dot_t(tgt_ref[:, at], mem_ref[:, at]), same)
        summed = dot(weights.astype(BF16), mem_ref[:, head_columns(heads + h)])
        for i, out_ref in enumerate(outs):
            out_ref[:, at] = summed[i * count : (i + 1) * count]
        stats = jnp.where(lane == h, top, jnp.where(lane == heads + h, total, stats))
    for i, out_ref in enumerate(outs):
        out_ref[:, half:] = stats[i * count : (i + 1) * count]


def cross_attend(acc, chunk, places, key_shards, value_shards, targets, mask, parts):
    rows, depth = chunk.shape
    width = key_shards[0].shape[1]
    count = targets.shape[0] // parts
    return call(
        functools.partial(cross_kernel, len(key_shards), places),
        "cross_attend",
        [((count, width + LANES), F32)] * parts,
        [chunk, *key_shards, *value_shards, acc, targets, mask],
        flops=4 * rows * depth * width,
        scratch=[pltpu.VMEM((rows, 2 * width), BF16)],
    )


def combine_kernel(*refs):
    parts, out_ref = refs[:-1], refs[-1]
    width = out_ref.shape[1]
    heads = width // HEAD_DIM
    for h in range(heads):
        at = head_columns(h)
        tops = [r[:, width + h : width + h + 1] for r in parts]
        top = functools.reduce(jnp.maximum, tops)
        factors = [jnp.exp(t - top) for t in tops]
        total = sum(f * r[:, width + heads + h : width + heads + h + 1] for f, r in zip(factors, parts))
        summed = sum(f * r[:, at] for f, r in zip(factors, parts))
        out_ref[:, at] = (summed / total).astype(BF16)


def on_device(enc_query, enc_key, enc_value, doc_ids, key_map, value_map, tgt_query):
    rows, features = enc_query.shape
    tgt_rows, width = tgt_query.shape
    n_ctx, n_head = lax.axis_size("ctx"), lax.axis_size("head")
    links = links_of(n_ctx)
    bring = lambda x: [lax.ppermute(x, "ctx", pairs) for pairs in links]

    marks = (doc_ids if n_ctx == 2 else doc_ids + 1).reshape(1, rows)
    keys, values, near_marks = bring(enc_key), bring(enc_value), bring(marks)
    chunks = 2
    held = encoder_attend(enc_query, enc_key, enc_value, marks, keys, values, near_marks, chunks)

    key_map, value_map, tgt_query, *held = lax.optimization_barrier((key_map, value_map, tgt_query, *held))
    targets = jnp.concatenate([tgt_query, *bring(tgt_query)], 0)
    mask = target_mask(marks, [marks, *near_marks], tgt_rows)
    if n_ctx == 2:
        key_shards, value_shards = [key_map, *bring(key_map)], [value_map, *bring(value_map)]
    else:
        key_shards, value_shards = ([lax.all_gather(x, "ctx", axis=0, tiled=True)] for x in (key_map, value_map))
    shard_blocks = n_head * chunks // len(key_shards)

    order = ring_order(n_head)
    ring = [(order[i], order[(i + 1) % n_head]) for i in range(n_head)]
    before = {target: source for source, target in ring}

    def places(turn, which):
        head, ctx = lax.axis_index("head"), lax.axis_index("ctx")
        owner = 0
        for i in range(n_head):
            source = i
            for _ in range(turn):
                source = before[source]
            owner = owner + jnp.where(head == i, source, 0)
        found = []
        for j in which:
            block = owner * chunks + j
            shard = jnp.where(lax.div(block, shard_blocks) == ctx, 0, 1) if len(key_shards) == 2 else None
            found.append((shard, lax.rem(block, shard_blocks)))
        return found

    acc, every = None, tuple(range(chunks))
    for turn in range(n_head - 1):
        later = [lax.ppermute(h, "head", ring) for h in held]
        acc = project(acc, held, functools.partial(places, turn, every), key_shards, value_shards)
        held = later
    last = n_head - 1
    acc = project(acc, held[:-1], functools.partial(places, last, every[:-1]), key_shards, value_shards)
    parts = cross_attend(
        acc, held[-1], functools.partial(places, last, every[-1:]), key_shards, value_shards, targets, mask, 1 + len(links)
    )

    combined = [parts[0]]
    for i, (pairs, piece) in enumerate(zip(links, parts[1:])):
        other = lax.ppermute(piece, "ctx", [(target, source) for source, target in pairs])
        if n_ctx > 2:
            end = n_ctx - 1 if i == 0 else 0
            column = lax.broadcasted_iota(jnp.int32, other.shape, 1)
            other = jnp.where((lax.axis_index("ctx") == end) & (column >= width), NEG_FILL, other)
        combined.append(other)
    return call(combine_kernel, "combine", [((tgt_rows, width), BF16)], combined, limit=4 << 20)[0]


def solution(mesh):
    in_specs = (
        P(("dp", "ctx"), "head"),
        P(("dp", "ctx"), "head"),
        P(("dp", "ctx"), "head"),
        P(("dp", "ctx")),
        P("ctx", "head"),
        P("ctx", "head"),
        P(("dp", "ctx"), "head"),
    )
    out_specs = P(("dp", "ctx"), "head")
    return jax.shard_map(
        on_device, mesh=mesh, in_specs=in_specs, out_specs=out_specs, check_vma=False
    )
```

time: 122 us -> 50.1 us (0.41)
  waiting for transfers between devices: 72.7 us -> 16.9 us
  between operations: 13.4 us -> 0.14 us
  Pallas kernels: 0 us -> 11.3 us
  matrix products: 10.9 us -> 0 us
  local copies, waits for them, and re-layouts: 3.67 us -> 0.91 us
  other arithmetic: 1.91 us -> 0.01 us
    all_gather x3 -> x0, waiting for transfers between devices: 69 us -> none  [the longest x1 46.4 us: on_device(): enc_full = lax.all_gather(enc_flat, 'head', axis=1, tiled=True)]
    ppermute x10 -> x13, waiting for transfers between devices: 2.3 us -> 16.9 us  [the longest x6 15.5 us: on_device(): later = [lax.ppermute(h, 'head', ring) for h in held]]
    pallas_call x0 -> x9, Pallas kernels: none -> 11.3 us  [call(): pl.pallas_call(kernel, in_specs=specs or [VMEM] * len(operands), out_spec...]
    dot_general x6 -> x0, matrix products: 10.9 us -> none  [the longest x1 4.08 us: on_device(): jnp.dot(enc_full, lax.all_gather(key_map, 'ctx', axis=0, tiled=True), pre...]
    unnamed x8, local copies, waits for them, and re-layouts: 2.56 us -> 0.91 us
    unnamed x3 -> x0, waiting for transfers between devices: 1.39 us -> none
    ppermute x10 -> x13, starting transfers between devices: 19.3 us -> 20.6 us  [the longest x6 19 us: on_device(): later = [lax.ppermute(h, 'head', ring) for h in held]]
  transfers between devices with their start and end apart: 13 -> 13, of which waited for: 5 -> 6; matrix products, arithmetic and copies ran while one was open for 10% -> 0% of each run, Pallas kernels for 0% -> 14%
where the time goes in v3:
time: 50.1 us; the launch traced here: 49.9 us
  starting transfers between devices  20.6 us (41%)
  waiting for transfers between devices  16.9 us (34%)
  Pallas kernels  11.3 us (23%)
  local copies, waits for them, and re-layouts  0.91 us (2%)
    ppermute x6, starting transfers between devices, on_device(): later = [lax.ppermute(h, 'head', ring) for h in held]  19 us
    ppermute x6, waiting for transfers between devices, on_device(): later = [lax.ppermute(h, 'head', ring) for h in held]  15.5 us
    pallas_call x9, Pallas kernels, call(): pl.pallas_call(kernel, in_specs=specs or [VMEM] * len(operands), out_spec...  11.3 us
    ppermute x6, starting transfers between devices, on_device(): bring = lambda x: [lax.ppermute(x, 'ctx', pairs) for pairs in links]  1.54 us
    ppermute x1, waiting for transfers between devices, on_device(): lax.ppermute(piece, 'ctx', [(target, source) for source, target in pairs])  1.38 us
  transfers between devices with their start and end apart: 13, of which 6 were waited for; matrix products, arithmetic and copies ran while one was open for 0% of the time, Pallas kernels for 14%

profile of v3, /device:TPU:0, one launch (start us, length us, event | category | flops | bytes accessed | tf_op | source)
XLA Modules:
  0.0 49.9 jit_solution(6953001325004951276)
XLA Ops:
  0.0 0.5 collective-permute-start.1
  0.5 0.5 collective-permute-start
  1.0 0.9 %copy-done.2 = s32[256]{0:T(256)S(1)} copy-done((s32[256]{0:T(256)S(1)}, s32[256]{0:T(256)}, u32[]{:S(2)}) %copy-start.2) | copy-done | bytes 1048
  1.9 3.6 %attend_own.1 = (bf16[256,1024]{1,0:T(8,128)(2,1)S(1)}, f32[256,1024]{1,0:T(8,128)S(1)}, f32[256,128]{1,0:T(8,128)S(1)}) custom-call(s32[1,256]{1,0:T(1,128)S(1)} %bitcast.2, bf16[256,1024]{1,0:T(8,128)(2,1)} %q_hbm.1, bf16[256,1024]{1,0:T(8,128)(2,1)} %k_hbm.1, bf16[256,1024]{1,0:T(8,128)(2,1)} %v_hbm.1), custom_call_target="tpu_custom_call" | custom-call | flops 268435456 | bytes 3277824 | tf_op jit(solution)/shard_map/attend_own/pallas_call | solution.py:60
  5.5 2.4 %attend_near.1 = (bf16[256,512]{1,0:T(8,128)(2,1)S(1)}, bf16[256,512]{1,0:T(8,128)(2,1)S(1)}) custom-call(s32[1,256]{1,0:T(1,128)S(1)} %bitcast.3, s32[1,256]{1,0:T(1,128)S(1)} %collective-permute-done.refs_1_, bf16[256,1024]{1,0:T(8,128)(2,1)S(1)} %get-tuple-element.17.refs_2_, f32[256,1024]{1,0:T(8,128)S(1)} %get-tuple-element.18.refs_3_, ...), custom_call_target="tpu_custom_call" | custom-call | flops 268435456 | bytes 3278848 | tf_op jit(solution)/shard_map/attend_near/pallas_call | solution.py:60
  8.0 0.4 collective-permute-start.6
  8.5 3.9 %collective-permute-start.8 = (bf16[256,512]{1,0:T(8,128)(2,1)S(1)}, bf16[256,512]{1,0:T(8,128)(2,1)S(1)}, u32[]{:S(2)}, u32[]{:S(2)}) collective-permute-start(bf16[256,512]{1,0:T(8,128)(2,1)S(1)} %get-tuple-element.25.refs_0_), channel_id=1, source_target_pairs={{0,2},{2,3},{3,1},{1,0},{4,6},{6,7},{7,5},{5,4},{8,10},{10,11},{11... | collective-permute-start | bytes 786440 | tf_op jit(solution)/shard_map/ppermute | solution.py:311
  12.4 1.6 %collective-permute-start.3 = (bf16[256,512]{1,0:T(8,128)(2,1)S(1)}, bf16[256,512]{1,0:T(8,128)(2,1)S(1)}, u32[]{:S(2)}, u32[]{:S(2)}) collective-permute-start(bf16[256,512]{1,0:T(8,128)(2,1)S(1)} %get-tuple-element.22.refs_1_), channel_id=1, source_target_pairs={{0,2},{2,3},{3,1},{1,0},{4,6},{6,7},{7,5},{5,4},{8,10},{10,11},{11... | collective-permute-start | bytes 786440 | tf_op jit(solution)/shard_map/ppermute | solution.py:311
  14.0 5.1 %collective-permute-done.8.refs_0_ = bf16[256,512]{1,0:T(8,128)(2,1)S(1)} collective-permute-done((bf16[256,512]{1,0:T(8,128)(2,1)S(1)}, bf16[256,512]{1,0:T(8,128)(2,1)S(1)}, u32[]{:S(2)}, u32[]{:S(2)}) %collective-permute-start.8) | collective-permute-done | bytes 262176 | tf_op jit(solution)/shard_map/ppermute | solution.py:311
  19.1 3.4 %collective-permute-start.9 = (bf16[256,512]{1,0:T(8,128)(2,1)S(1)}, bf16[256,512]{1,0:T(8,128)(2,1)S(1)}, u32[]{:S(2)}, u32[]{:S(2)}) collective-permute-start(bf16[256,512]{1,0:T(8,128)(2,1)S(1)} %collective-permute-done.8.refs_0_), channel_id=1, source_target_pairs={{0,2},{2,3},{3,1},{1,0},{4,6},{6,7},{7,5},{5,4},{8,10},{10,11},{11... | collective-permute-start | bytes 786440 | tf_op jit(solution)/shard_map/ppermute | solution.py:311
  22.5 2.2 %collective-permute-done.3.refs_1_ = bf16[256,512]{1,0:T(8,128)(2,1)S(1)} collective-permute-done((bf16[256,512]{1,0:T(8,128)(2,1)S(1)}, bf16[256,512]{1,0:T(8,128)(2,1)S(1)}, u32[]{:S(2)}, u32[]{:S(2)}) %collective-permute-start.3) | collective-permute-done | bytes 262176 | tf_op jit(solution)/shard_map/ppermute | solution.py:311
  24.7 3.4 %collective-permute-start.4 = (bf16[256,512]{1,0:T(8,128)(2,1)S(1)}, bf16[256,512]{1,0:T(8,128)(2,1)S(1)}, u32[]{:S(2)}, u32[]{:S(2)}) collective-permute-start(bf16[256,512]{1,0:T(8,128)(2,1)S(1)} %collective-permute-done.3.refs_1_), channel_id=1, source_target_pairs={{0,2},{2,3},{3,1},{1,0},{4,6},{6,7},{7,5},{5,4},{8,10},{10,11},{11... | collective-permute-start | bytes 786440 | tf_op jit(solution)/shard_map/ppermute | solution.py:311
  28.2 2.1 %collective-permute-done.9.refs_0_ = bf16[256,512]{1,0:T(8,128)(2,1)S(1)} collective-permute-done((bf16[256,512]{1,0:T(8,128)(2,1)S(1)}, bf16[256,512]{1,0:T(8,128)(2,1)S(1)}, u32[]{:S(2)}, u32[]{:S(2)}) %collective-permute-start.9) | collective-permute-done | bytes 262176 | tf_op jit(solution)/shard_map/ppermute | solution.py:311
  30.3 3.4 %collective-permute-start.10 = (bf16[256,512]{1,0:T(8,128)(2,1)S(1)}, bf16[256,512]{1,0:T(8,128)(2,1)S(1)}, u32[]{:S(2)}, u32[]{:S(2)}) collective-permute-start(bf16[256,512]{1,0:T(8,128)(2,1)S(1)} %collective-permute-done.9.refs_0_), channel_id=1, source_target_pairs={{0,2},{2,3},{3,1},{1,0},{4,6},{6,7},{7,5},{5,4},{8,10},{10,11},{11... | collective-permute-start | bytes 786440 | tf_op jit(solution)/shard_map/ppermute | solution.py:311
  33.7 2.2 %collective-permute-done.4.refs_1_ = bf16[256,512]{1,0:T(8,128)(2,1)S(1)} collective-permute-done((bf16[256,512]{1,0:T(8,128)(2,1)S(1)}, bf16[256,512]{1,0:T(8,128)(2,1)S(1)}, u32[]{:S(2)}, u32[]{:S(2)}) %collective-permute-start.4) | collective-permute-done | bytes 262176 | tf_op jit(solution)/shard_map/ppermute | solution.py:311
  35.9 3.4 %collective-permute-start.5 = (bf16[256,512]{1,0:T(8,128)(2,1)S(1)}, bf16[256,512]{1,0:T(8,128)(2,1)S(1)}, u32[]{:S(2)}, u32[]{:S(2)}) collective-permute-start(bf16[256,512]{1,0:T(8,128)(2,1)S(1)} %collective-permute-done.4.refs_1_), channel_id=1, source_target_pairs={{0,2},{2,3},{3,1},{1,0},{4,6},{6,7},{7,5},{5,4},{8,10},{10,11},{11... | collective-permute-start | bytes 786440 | tf_op jit(solution)/shard_map/ppermute | solution.py:311
  39.4 0.9 %project.4.refs_6_ = f32[256,1024]{1,0:T(8,128)S(1)} custom-call(bf16[256,512]{1,0:T(8,128)(2,1)S(1)} %get-tuple-element.25.refs_0_, bf16[256,512]{1,0:T(8,128)(2,1)S(1)} %get-tuple-element.22.refs_1_, bf16[2048,512]{1,0:T(8,128)(2,1)S(1)} %copy-done, bf16[2048,512]{1,0:T(8,128)(2,1)S(1)} %collective-permute-done.6.refs_3_.refs_2_.refs_1_, ...), custom_call_target="tpu_custom_call" | custom-call | flops 536870912 | bytes 9961472 | tf_op jit(solution)/shard_map/project/pallas_call | solution.py:60
  40.3 0.9 %project.5.refs_6_ = f32[256,1024]{1,0:T(8,128)S(1)} custom-call(bf16[256,512]{1,0:T(8,128)(2,1)S(1)} %collective-permute-done.8.refs_0_, bf16[256,512]{1,0:T(8,128)(2,1)S(1)} %collective-permute-done.3.refs_1_, bf16[2048,512]{1,0:T(8,128)(2,1)S(1)} %copy-done, bf16[2048,512]{1,0:T(8,128)(2,1)S(1)} %collective-permute-done.6.refs_3_.refs_2_.refs_1_, ...), custom_call_target="tpu_custom_call" | custom-call | flops 536870912 | bytes 11010048 | tf_op jit(solution)/shard_map/project/pallas_call | solution.py:60
  41.2 0.9 %project.6.refs_5_ = f32[256,1024]{1,0:T(8,128)S(1)} custom-call(bf16[256,512]{1,0:T(8,128)(2,1)S(1)} %collective-permute-done.9.refs_0_, bf16[256,512]{1,0:T(8,128)(2,1)S(1)} %collective-permute-done.4.refs_1_, bf16[2048,512]{1,0:T(8,128)(2,1)S(1)} %copy-done, bf16[2048,512]{1,0:T(8,128)(2,1)S(1)} %collective-permute-done.6.refs_3_.refs_2_.refs_1_, ...), custom_call_target="tpu_custom_call" | custom-call | flops 536870912 | bytes 11010048 | tf_op jit(solution)/shard_map/project/pallas_call | solution.py:60
  42.1 0.5 project.7.refs_4_
  42.6 3.9 %collective-permute-done.5.e_ref = bf16[256,512]{1,0:T(8,128)(2,1)S(1)} collective-permute-done((bf16[256,512]{1,0:T(8,128)(2,1)S(1)}, bf16[256,512]{1,0:T(8,128)(2,1)S(1)}, u32[]{:S(2)}, u32[]{:S(2)}) %collective-permute-start.5) | collective-permute-done | bytes 262176 | tf_op jit(solution)/shard_map/ppermute | solution.py:311
  46.5 1.1 %cross_attend.1 = (f32[64,640]{1,0:T(8,128)S(1)}, f32[64,640]{1,0:T(8,128)S(1)}) custom-call(bf16[256,512]{1,0:T(8,128)(2,1)S(1)} %collective-permute-done.5.e_ref, bf16[2048,512]{1,0:T(8,128)(2,1)S(1)} %copy-done, bf16[2048,512]{1,0:T(8,128)(2,1)S(1)} %collective-permute-done.6.refs_3_.refs_2_.refs_1_, bf16[2048,512]{1,0:T(8,128)(2,1)S(1)} %copy-done.1, ...), custom_call_target="tpu_custom_call" | custom-call | flops 268435456 | bytes 10289152 | tf_op jit(solution)/shard_map/cross_attend/pallas_call | solution.py:60
  47.7 1.4 %collective-permute-done.12.refs_1_ = f32[64,640]{1,0:T(8,128)S(1)} collective-permute-done((f32[64,640]{1,0:T(8,128)S(1)}, f32[64,640]{1,0:T(8,128)S(1)}, u32[]{:S(2)}, u32[]{:S(2)}) %collective-permute-start.12) | collective-permute-done | bytes 163872 | tf_op jit(solution)/shard_map/ppermute | solution.py:322
  49.1 0.8 %combine.1 = bf16[64,512]{1,0:T(8,128)(2,1)} custom-call(f32[64,640]{1,0:T(8,128)S(1)} %get-tuple-element.27.refs_0_, f32[64,640]{1,0:T(8,128)S(1)} %collective-permute-done.12.refs_1_), custom_call_target="tpu_custom_call" | custom-call | bytes 393216 | tf_op jit(solution)/shard_map/combine/pallas_call | solution.py:60
  (20 shorter events, 0.5 us)
Async XLA Ops:
  0.0 5.5 %collective-permute-start.1 = (bf16[256,1024]{1,0:T(8,128)(2,1)}, bf16[256,1024]{1,0:T(8,128)(2,1)S(1)}, u32[]{:S(2)}, u32[]{:S(2)}) collective-permute-start(bf16[256,1024]{1,0:T(8,128)(2,1)} %k_hbm.1), channel_id=1, source_target_pairs={{0,4},{4,0},{1,5},{5,1},{2,6},{6,2},{3,7},{7,3},{8,12},{12,8},{9,1... | collective-permute-start | bytes 1572872 | tf_op jit(solution)/shard_map/ppermute | solution.py:274
  0.5 5.1 %collective-permute-start.2 = (bf16[256,1024]{1,0:T(8,128)(2,1)}, bf16[256,1024]{1,0:T(8,128)(2,1)S(1)}, u32[]{:S(2)}, u32[]{:S(2)}) collective-permute-start(bf16[256,1024]{1,0:T(8,128)(2,1)} %v_hbm.1), channel_id=1, source_target_pairs={{0,4},{4,0},{1,5},{5,1},{2,6},{6,2},{3,7},{7,3},{8,12},{12,8},{9,1... | collective-permute-start | bytes 1572872 | tf_op jit(solution)/shard_map/ppermute | solution.py:274
  0.5 7.4 %copy-start = (bf16[2048,512]{1,0:T(8,128)(2,1)S(1)}, bf16[2048,512]{1,0:T(8,128)(2,1)}, u32[]{:S(2)}) copy-start(bf16[2048,512]{1,0:T(8,128)(2,1)} %refs_0_) | copy-start | bytes 6291460
  0.5 7.8 %copy-start.1 = (bf16[2048,512]{1,0:T(8,128)(2,1)S(1)}, bf16[2048,512]{1,0:T(8,128)(2,1)}, u32[]{:S(2)}) copy-start(bf16[2048,512]{1,0:T(8,128)(2,1)} %refs_2_.3) | copy-start | bytes 6291460
  0.5 5.0 %collective-permute-start = (s32[1,256]{1,0:T(1,128)}, s32[1,256]{1,0:T(1,128)S(1)}, u32[]{:S(2)}, u32[]{:S(2)}) collective-permute-start(s32[1,256]{1,0:T(1,128)} %bitcast.1), channel_id=1, source_target_pairs={{0,4},{4,0},{1,5},{5,1},{2,6},{6,2},{3,7},{7,3},{8,12},{12,8},{9,1... | collective-permute-start | bytes 3080 | tf_op jit(solution)/shard_map/ppermute | solution.py:274
  1.0 0.9 %copy-start.2 = (s32[256]{0:T(256)S(1)}, s32[256]{0:T(256)}, u32[]{:S(2)}) copy-start(s32[256]{0:T(256)} %param.10) | copy-start | bytes 3076
  1.9 26.2 %copy-start.3 = (bf16[64,512]{1,0:T(8,128)(2,1)S(1)}, bf16[64,512]{1,0:T(8,128)(2,1)}, u32[]{:S(2)}) copy-start(bf16[64,512]{1,0:T(8,128)(2,1)} %param.13) | copy-start | bytes 196612
  8.0 31.4 %collective-permute-start.6 = (bf16[2048,512]{1,0:T(8,128)(2,1)S(1)}, bf16[2048,512]{1,0:T(8,128)(2,1)S(1)}, u32[]{:S(2)}, u32[]{:S(2)}) collective-permute-start(bf16[2048,512]{1,0:T(8,128)(2,1)S(1)} %copy-done), channel_id=1, source_target_pairs={{0,4},{4,0},{1,5},{5,1},{2,6},{6,2},{3,7},{7,3},{8,12},{12,8},{9,1... | collective-permute-start | bytes 6291464 | tf_op jit(solution)/shard_map/ppermute | solution.py:274
  8.4 31.0 %collective-permute-start.7 = (bf16[2048,512]{1,0:T(8,128)(2,1)S(1)}, bf16[2048,512]{1,0:T(8,128)(2,1)S(1)}, u32[]{:S(2)}, u32[]{:S(2)}) collective-permute-start(bf16[2048,512]{1,0:T(8,128)(2,1)S(1)} %copy-done.1), channel_id=1, source_target_pairs={{0,4},{4,0},{1,5},{5,1},{2,6},{6,2},{3,7},{7,3},{8,12},{12,8},{9,1... | collective-permute-start | bytes 6291464 | tf_op jit(solution)/shard_map/ppermute | solution.py:274
  8.5 10.6 %collective-permute-start.8 = (bf16[256,512]{1,0:T(8,128)(2,1)S(1)}, bf16[256,512]{1,0:T(8,128)(2,1)S(1)}, u32[]{:S(2)}, u32[]{:S(2)}) collective-permute-start(bf16[256,512]{1,0:T(8,128)(2,1)S(1)} %get-tuple-element.25.refs_0_), channel_id=1, source_target_pairs={{0,2},{2,3},{3,1},{1,0},{4,6},{6,7},{7,5},{5,4},{8,10},{10,11},{11... | collective-permute-start | bytes 786440 | tf_op jit(solution)/shard_map/ppermute | solution.py:311
  12.4 12.3 %collective-permute-start.3 = (bf16[256,512]{1,0:T(8,128)(2,1)S(1)}, bf16[256,512]{1,0:T(8,128)(2,1)S(1)}, u32[]{:S(2)}, u32[]{:S(2)}) collective-permute-start(bf16[256,512]{1,0:T(8,128)(2,1)S(1)} %get-tuple-element.22.refs_1_), channel_id=1, source_target_pairs={{0,2},{2,3},{3,1},{1,0},{4,6},{6,7},{7,5},{5,4},{8,10},{10,11},{11... | collective-permute-start | bytes 786440 | tf_op jit(solution)/shard_map/ppermute | solution.py:311
  19.1 11.2 %collective-permute-start.9 = (bf16[256,512]{1,0:T(8,128)(2,1)S(1)}, bf16[256,512]{1,0:T(8,128)(2,1)S(1)}, u32[]{:S(2)}, u32[]{:S(2)}) collective-permute-start(bf16[256,512]{1,0:T(8,128)(2,1)S(1)} %collective-permute-done.8.refs_0_), channel_id=1, source_target_pairs={{0,2},{2,3},{3,1},{1,0},{4,6},{6,7},{7,5},{5,4},{8,10},{10,11},{11... | collective-permute-start | bytes 786440 | tf_op jit(solution)/shard_map/ppermute | solution.py:311
  24.7 11.2 %collective-permute-start.4 = (bf16[256,512]{1,0:T(8,128)(2,1)S(1)}, bf16[256,512]{1,0:T(8,128)(2,1)S(1)}, u32[]{:S(2)}, u32[]{:S(2)}) collective-permute-start(bf16[256,512]{1,0:T(8,128)(2,1)S(1)} %collective-permute-done.3.refs_1_), channel_id=1, source_target_pairs={{0,2},{2,3},{3,1},{1,0},{4,6},{6,7},{7,5},{5,4},{8,10},{10,11},{11... | collective-permute-start | bytes 786440 | tf_op jit(solution)/shard_map/ppermute | solution.py:311
  28.1 11.2 %collective-permute-start.11 = (bf16[64,512]{1,0:T(8,128)(2,1)S(1)}, bf16[64,512]{1,0:T(8,128)(2,1)S(1)}, u32[]{:S(2)}, u32[]{:S(2)}) collective-permute-start(bf16[64,512]{1,0:T(8,128)(2,1)S(1)} %copy-done.3), channel_id=1, source_target_pairs={{0,4},{4,0},{1,5},{5,1},{2,6},{6,2},{3,7},{7,3},{8,12},{12,8},{9,1... | collective-permute-start | bytes 196616 | tf_op jit(solution)/shard_map/ppermute | solution.py:274
  30.3 11.8 %collective-permute-start.10 = (bf16[256,512]{1,0:T(8,128)(2,1)S(1)}, bf16[256,512]{1,0:T(8,128)(2,1)S(1)}, u32[]{:S(2)}, u32[]{:S(2)}) collective-permute-start(bf16[256,512]{1,0:T(8,128)(2,1)S(1)} %collective-permute-done.9.refs_0_), channel_id=1, source_target_pairs={{0,2},{2,3},{3,1},{1,0},{4,6},{6,7},{7,5},{5,4},{8,10},{10,11},{11... | collective-permute-start | bytes 786440 | tf_op jit(solution)/shard_map/ppermute | solution.py:311
  35.9 10.5 %collective-permute-start.5 = (bf16[256,512]{1,0:T(8,128)(2,1)S(1)}, bf16[256,512]{1,0:T(8,128)(2,1)S(1)}, u32[]{:S(2)}, u32[]{:S(2)}) collective-permute-start(bf16[256,512]{1,0:T(8,128)(2,1)S(1)} %collective-permute-done.4.refs_1_), channel_id=1, source_target_pairs={{0,2},{2,3},{3,1},{1,0},{4,6},{6,7},{7,5},{5,4},{8,10},{10,11},{11... | collective-permute-start | bytes 786440 | tf_op jit(solution)/shard_map/ppermute | solution.py:311
  47.6 1.5 %collective-permute-start.12 = (f32[64,640]{1,0:T(8,128)S(1)}, f32[64,640]{1,0:T(8,128)S(1)}, u32[]{:S(2)}, u32[]{:S(2)}) collective-permute-start(f32[64,640]{1,0:T(8,128)S(1)} %get-tuple-element.28), channel_id=1, source_target_pairs={{4,0},{0,4},{5,1},{1,5},{6,2},{2,6},{7,3},{3,7},{12,8},{8,12},{13,... | collective-permute-start | bytes 491528 | tf_op jit(solution)/shard_map/ppermute | solution.py:322

commit v4 on v3

v4 whole, which is shorter than its diff:
```python
import functools

import jax
import jax.numpy as jnp
from jax import lax
from jax.experimental import pallas as pl
from jax.experimental.pallas import tpu as pltpu
from jax.sharding import PartitionSpec as P

HEAD_DIM = 256
NEG_FILL = -1e30
F32 = jnp.float32
BF16 = jnp.bfloat16
LANES = 128
SCALE = HEAD_DIM**-0.5
VMEM = pl.BlockSpec(memory_space=pltpu.VMEM)
HBM = pl.BlockSpec(memory_space=pltpu.HBM)


def ring_order(count):
    return list(range(0, count, 2)) + list(range(1, count, 2))[::-1]


def links_of(count):
    if count == 2:
        return [[(0, 1), (1, 0)]]
    return [[(i, i + 1) for i in range(count - 1)], [(i + 1, i) for i in range(count - 1)]]


def dot_t(a, b):
    return lax.dot_general(a, b, (((1,), (1,)), ((), ())), preferred_element_type=F32)


def dot(a, b):
    return jnp.dot(a, b, preferred_element_type=F32)


def head_columns(h):
    return slice(h * HEAD_DIM, (h + 1) * HEAD_DIM)


def down_lanes(row):
    return jnp.transpose(jnp.broadcast_to(row, (LANES, row.shape[1])))


def same_mark(down, row):
    return jnp.concatenate([down == row[:, i : i + LANES] for i in range(0, row.shape[1], LANES)], axis=1)


def softmax_block(scores, same):
    scores = jnp.where(same, scores * SCALE, NEG_FILL)
    top = jnp.max(scores, axis=1, keepdims=True)
    weights = jnp.exp(scores - top)
    return top, weights, jnp.sum(weights, axis=1, keepdims=True)


def call(kernel, name, outs, operands, flops=0, exps=0, specs=None, scratch=(), limit=8 << 20):
    out_shape = [jax.ShapeDtypeStruct(*o) for o in outs]
    moved = sum(x.size * x.dtype.itemsize for x in [*operands, *out_shape])
    return pl.pallas_call(
        kernel,
        in_specs=specs or [VMEM] * len(operands),
        out_specs=[VMEM] * len(outs),
        out_shape=out_shape,
        scratch_shapes=list(scratch),
        compiler_params=pltpu.CompilerParams(vmem_limit_bytes=limit),
        cost_estimate=pl.CostEstimate(flops=flops, bytes_accessed=moved, transcendentals=exps),
        name=name,
    )(*operands)


def fetch_kernel(count, *refs):
    sources, targets, sems = refs[:count], refs[count : 2 * count], refs[-1]
    copies = [pltpu.make_async_copy(s, t, sems.at[i]) for i, (s, t) in enumerate(zip(sources, targets))]
    for copy in copies:
        copy.start()
    for copy in copies:
        copy.wait()


def fetch(*arrays):
    return call(
        functools.partial(fetch_kernel, len(arrays)),
        "fetch",
        [(x.shape, x.dtype) for x in arrays],
        [pltpu.with_memory_space_constraint(x, pltpu.HBM) for x in arrays],
        specs=[HBM] * len(arrays),
        scratch=[pltpu.SemaphoreType.DMA((len(arrays),))],
    )


def attend_kernel(blocks, *refs):
    marks, q_ref = refs[:blocks], refs[blocks]
    keys, values = refs[blocks + 1 : 2 * blocks + 1], refs[2 * blocks + 1 : 3 * blocks + 1]
    outs = refs[3 * blocks + 1 :]
    down = down_lanes(marks[0][...])
    same = jnp.concatenate([same_mark(down, m[...]) for m in marks], axis=1)
    rows = q_ref.shape[0]
    heads = q_ref.shape[1] // HEAD_DIM
    each = heads // len(outs)
    for h in range(heads):
        at = head_columns(h)
        scores = jnp.concatenate([dot_t(q_ref[:, at], k[:, at]) for k in keys], axis=1)
        _, weights, total = softmax_block(scores, same)
        rounded = weights.astype(BF16)
        summed = sum(dot(rounded[:, i * rows : (i + 1) * rows], v[:, at]) for i, v in enumerate(values))
        outs[h // each][:, head_columns(h % each)] = (summed / total).astype(BF16)


def encoder_attend(query, keys, values, marks, chunks):
    rows, width = query.shape
    pairs = rows * rows * len(keys) * (width // HEAD_DIM)
    return list(
        call(
            functools.partial(attend_kernel, len(keys)),
            "encoder_attend",
            [((rows, width // chunks), BF16)] * chunks,
            [*marks, query, *keys, *values],
            flops=4 * pairs * HEAD_DIM,
            exps=pairs,
        )
    )


def target_mask_kernel(step, own_ref, *refs):
    marks, out_ref, down_ref = refs[:-2], refs[-2], refs[-1]
    own = own_ref[...]
    count = out_ref.shape[0] // len(marks)
    for i, mark_ref in enumerate(marks):
        down_ref[...] = down_lanes(mark_ref[...])
        down = down_ref[pl.ds(0, count, stride=step), :]
        out_ref[i * count : (i + 1) * count, :] = same_mark(down, own).astype(F32)


def target_mask(marks, all_marks, tgt_rows):
    rows = marks.shape[1]
    return call(
        functools.partial(target_mask_kernel, rows // tgt_rows),
        "target_mask",
        [((tgt_rows * len(all_marks), rows), F32)],
        [marks, *all_marks],
        scratch=[pltpu.VMEM((rows, LANES), jnp.int32)],
    )[0]


def add_products(acc_of, store, e_refs, place, key_shards, value_shards):
    shard, row = place
    depth = e_refs[0].shape[1]
    at = pl.ds(pl.multiple_of(row, depth), depth * len(e_refs))
    chunks = jnp.concatenate([r[...] for r in e_refs], axis=1)

    def add(i):
        for side, shards in enumerate((key_shards, value_shards)):
            store(side, acc_of(side) + dot(chunks, shards[i][at, :]))

    if len(key_shards) == 1:
        add(0)
    else:
        for i in range(len(key_shards)):
            pl.when(shard == i)(functools.partial(add, i))


def project_kernel(chunks, shards, has_acc, place, *refs):
    out_ref = refs[-1]
    e_refs, maps = refs[:chunks], refs[chunks : chunks + 2 * shards]
    half = out_ref.shape[1] // 2
    side_of = lambda side: slice(side * half, (side + 1) * half)

    def store(side, value):
        out_ref[:, side_of(side)] = value

    acc_of = lambda side: refs[-2][:, side_of(side)] if has_acc else 0.0
    add_products(acc_of, store, e_refs, place(), maps[:shards], maps[shards:])


def project(acc, chunks, place, key_shards, value_shards):
    rows, depth = chunks[0].shape
    width = key_shards[0].shape[1]
    operands = [*chunks, *key_shards, *value_shards] + ([] if acc is None else [acc])
    return call(
        functools.partial(project_kernel, len(chunks), len(key_shards), acc is not None, place),
        "project",
        [((rows, 2 * width), F32)],
        operands,
        flops=4 * rows * depth * width * len(chunks),
    )[0]


def cross_kernel(shards, place, e_ref, *refs):
    maps, (acc_ref, tgt_ref, mask_ref) = refs[: 2 * shards], refs[2 * shards : 2 * shards + 3]
    outs, mem_ref = refs[2 * shards + 3 : -1], refs[-1]
    half = mem_ref.shape[1] // 2
    side_of = lambda side: slice(side * half, (side + 1) * half)

    def store(side, value):
        mem_ref[:, side_of(side)] = value.astype(BF16)

    add_products(lambda side: acc_ref[:, side_of(side)], store, [e_ref], place(), maps[:shards], maps[shards:])
    heads = half // HEAD_DIM
    count = outs[0].shape[0]
    lane = lax.broadcasted_iota(jnp.int32, (tgt_ref.shape[0], LANES), 1)
    stats = jnp.zeros(lane.shape, F32)
    same = mask_ref[...] > 0
    for h in range(heads):
        at = head_columns(h)
        top, weights, total = softmax_block(dot_t(tgt_ref[:, at], mem_ref[:, at]), same)
        summed = dot(weights.astype(BF16), mem_ref[:, head_columns(heads + h)])
        for i, out_ref in enumerate(outs):
            out_ref[:, at] = summed[i * count : (i + 1) * count]
        stats = jnp.where(lane == h, top, jnp.where(lane == heads + h, total, stats))
    for i, out_ref in enumerate(outs):
        out_ref[:, half:] = stats[i * count : (i + 1) * count]


def cross_attend(acc, chunk, place, key_shards, value_shards, targets, mask, parts):
    rows, depth = chunk.shape
    width = key_shards[0].shape[1]
    count = targets.shape[0] // parts
    return call(
        functools.partial(cross_kernel, len(key_shards), place),
        "cross_attend",
        [((count, width + LANES), F32)] * parts,
        [chunk, *key_shards, *value_shards, acc, targets, mask],
        flops=4 * rows * depth * width,
        scratch=[pltpu.VMEM((rows, 2 * width), BF16)],
    )


def combine_kernel(*refs):
    parts, out_ref = refs[:-1], refs[-1]
    width = out_ref.shape[1]
    heads = width // HEAD_DIM
    for h in range(heads):
        at = head_columns(h)
        tops = [r[:, width + h : width + h + 1] for r in parts]
        top = functools.reduce(jnp.maximum, tops)
        factors = [jnp.exp(t - top) for t in tops]
        total = sum(f * r[:, width + heads + h : width + heads + h + 1] for f, r in zip(factors, parts))
        summed = sum(f * r[:, at] for f, r in zip(factors, parts))
        out_ref[:, at] = (summed / total).astype(BF16)


def on_device(enc_query, enc_key, enc_value, doc_ids, key_map, value_map, tgt_query):
    rows, features = enc_query.shape
    tgt_rows, width = tgt_query.shape
    n_ctx, n_head = lax.axis_size("ctx"), lax.axis_size("head")
    links = links_of(n_ctx)
    bring = lambda x: [lax.ppermute(x, "ctx", pairs) for pairs in links]

    marks = (doc_ids if n_ctx == 2 else doc_ids + 1).reshape(1, rows)
    keys, values, near_marks = bring(enc_key), bring(enc_value), bring(marks)
    query, own_key, own_value, marks = fetch(enc_query, enc_key, enc_value, marks)
    chunks = 2
    held = encoder_attend(query, [own_key, *keys], [own_value, *values], [marks, *near_marks], chunks)

    key_map, value_map, tgt_query, *_ = lax.optimization_barrier(
        (key_map, value_map, tgt_query, *keys, *values, *near_marks, query)
    )
    near_targets = bring(tgt_query)
    if n_ctx == 2:
        key_shards, value_shards = [key_map, *bring(key_map)], [value_map, *bring(value_map)]
    else:
        key_shards, value_shards = ([lax.all_gather(x, "ctx", axis=0, tiled=True)] for x in (key_map, value_map))
    targets = jnp.concatenate([tgt_query, *near_targets], 0)
    mask = target_mask(marks, [marks, *near_marks], tgt_rows)

    order = ring_order(n_head)
    ring = [(order[i], order[(i + 1) % n_head]) for i in range(n_head)]
    before = {target: source for source, target in ring}

    def place(turn, first):
        head, ctx = lax.axis_index("head"), lax.axis_index("ctx")
        owner = 0
        for i in range(n_head):
            source = i
            for _ in range(turn):
                source = before[source]
            owner = owner + jnp.where(head == i, source, 0)
        row = owner * features + first
        if len(key_shards) == 1:
            return None, row
        shard_rows = n_head * features // 2
        return jnp.where(lax.div(row, shard_rows) == ctx, 0, 1), lax.rem(row, shard_rows)

    acc, last = None, n_head - 1
    for turn in range(last):
        if turn == last - 1:
            pieces = [p for h in held for p in jnp.split(h, 2, axis=1)]
        else:
            pieces = held
        later = [lax.ppermute(p, "head", ring) for p in pieces]
        acc = project(acc, held, functools.partial(place, turn, 0), key_shards, value_shards)
        held = later
    acc = project(acc, held[:-1], functools.partial(place, last, 0), key_shards, value_shards)
    first = features - held[-1].shape[1]
    parts = cross_attend(
        acc, held[-1], functools.partial(place, last, first), key_shards, value_shards, targets, mask, 1 + len(links)
    )

    combined = [parts[0]]
    for i, (pairs, piece) in enumerate(zip(links, parts[1:])):
        other = lax.ppermute(piece, "ctx", [(target, source) for source, target in pairs])
        if n_ctx > 2:
            end = n_ctx - 1 if i == 0 else 0
            column = lax.broadcasted_iota(jnp.int32, other.shape, 1)
            other = jnp.where((lax.axis_index("ctx") == end) & (column >= width), NEG_FILL, other)
        combined.append(other)
    return call(combine_kernel, "combine", [((tgt_rows, width), BF16)], combined, limit=4 << 20)[0]


def solution(mesh):
    in_specs = (
        P(("dp", "ctx"), "head"),
        P(("dp", "ctx"), "head"),
        P(("dp", "ctx"), "head"),
        P(("dp", "ctx")),
        P("ctx", "head"),
        P("ctx", "head"),
        P(("dp", "ctx"), "head"),
    )
    out_specs = P(("dp", "ctx"), "head")
    return jax.shard_map(
        on_device, mesh=mesh, in_specs=in_specs, out_specs=out_specs, check_vma=False
    )
```

time: 50.1 us -> 46.1 us (0.920)
  Pallas kernels: 11.3 us -> 7.6 us
  starting transfers between devices: 20.6 us -> 22.1 us
  local copies, waits for them, and re-layouts: 0.91 us -> 0.05 us
  waiting for transfers between devices: 16.9 us -> 16.1 us
    pallas_call x9, Pallas kernels: 11.3 us -> 7.6 us  [call(): pl.pallas_call(kernel, in_specs=specs or [VMEM] * len(operands), out_spec...]
    ppermute x6 -> x8, starting transfers between devices: 19 us -> 20.6 us  [on_device(): later = [lax.ppermute(p, 'head', ring) for p in pieces]]
    ppermute x6 -> x8, waiting for transfers between devices: 15.5 us -> 14.3 us  [on_device(): later = [lax.ppermute(p, 'head', ring) for p in pieces]]
    unnamed x8 -> x6, local copies, waits for them, and re-layouts: 0.91 us -> 0.01 us
  transfers between devices with their start and end apart: 13 -> 15, of which waited for: 6 -> 8; matrix products, arithmetic and copies ran while one was open for 0% -> 0% of each run, Pallas kernels for 14% -> 13%
where the time goes in v4:
time: 46.1 us; the launch traced here: 46 us
  starting transfers between devices  22.1 us (48%)
  waiting for transfers between devices  16.1 us (35%)
  Pallas kernels  7.6 us (16%)
    ppermute x8, starting transfers between devices, on_device(): later = [lax.ppermute(p, 'head', ring) for p in pieces]  20.6 us
    ppermute x8, waiting for transfers between devices, on_device(): later = [lax.ppermute(p, 'head', ring) for p in pieces]  14.3 us
    pallas_call x9, Pallas kernels, call(): pl.pallas_call(kernel, in_specs=specs or [VMEM] * len(operands), out_spec...  7.6 us
    ppermute x6, starting transfers between devices, on_device(): bring = lambda x: [lax.ppermute(x, 'ctx', pairs) for pairs in links]  1.48 us
    ppermute x1, waiting for transfers between devices, on_device(): lax.ppermute(piece, 'ctx', [(target, source) for source, target in pairs])  1.38 us
  transfers between devices with their start and end apart: 15, of which 8 were waited for; matrix products, arithmetic and copies ran while one was open for 0% of the time, Pallas kernels for 13%

profile of v4, /device:TPU:0, one launch (start us, length us, event | category | flops | bytes accessed | tf_op | source)
XLA Modules:
  0.0 46.0 jit_solution(2325403183961653337)
XLA Ops:
  0.0 0.5 collective-permute-start.1
  1.0 1.5 %fetch.1 = (bf16[256,1024]{1,0:T(8,128)(2,1)S(1)}, bf16[256,1024]{1,0:T(8,128)(2,1)S(1)}, bf16[256,1024]{1,0:T(8,128)(2,1)S(1)}, s32[1,256]{1,0:T(1,128)S(1)}) custom-call(bf16[256,1024]{1,0:T(8,128)(2,1)} %refs_0_.1, bf16[256,1024]{1,0:T(8,128)(2,1)} %refs_1_.1, bf16[256,1024]{1,0:T(8,128)(2,1)} %refs_2_.1, s32[1,256]{1,0:T(1,128)} %bitcast.2), custom_call_target="tpu_custom_call" | custom-call | bytes 3147776 | tf_op jit(solution)/shard_map/fetch/pallas_call | solution.py:60
  3.5 1.3 %encoder_attend.1 = (bf16[256,512]{1,0:T(8,128)(2,1)S(1)}, bf16[256,512]{1,0:T(8,128)(2,1)S(1)}) custom-call(s32[1,256]{1,0:T(1,128)S(1)} %get-tuple-element.16.refs_0_.own_ref, s32[1,256]{1,0:T(1,128)S(1)} %collective-permute-done.refs_1_, bf16[256,1024]{1,0:T(8,128)(2,1)S(1)} %get-tuple-element.17.refs_2_, ...), custom_call_target="tpu_custom_call" | custom-call | flops 536870912 | bytes 3147776 | tf_op jit(solution)/shard_map/encoder_attend/pallas_call | solution.py:60
  4.7 4.0 %collective-permute-start.8 = (bf16[256,512]{1,0:T(8,128)(2,1)S(1)}, bf16[256,512]{1,0:T(8,128)(2,1)S(1)}, u32[]{:S(2)}, u32[]{:S(2)}) collective-permute-start(bf16[256,512]{1,0:T(8,128)(2,1)S(1)} %get-tuple-element.23.refs_0_), channel_id=1, source_target_pairs={{0,2},{2,3},{3,1},{1,0},{4,6},{6,7},{7,5},{5,4},{8,10},{10,11},{11... | collective-permute-start | bytes 786440 | tf_op jit(solution)/shard_map/ppermute | solution.py:291
  8.7 1.6 %collective-permute-start.3 = (bf16[256,512]{1,0:T(8,128)(2,1)S(1)}, bf16[256,512]{1,0:T(8,128)(2,1)S(1)}, u32[]{:S(2)}, u32[]{:S(2)}) collective-permute-start(bf16[256,512]{1,0:T(8,128)(2,1)S(1)} %get-tuple-element.20.refs_1_), channel_id=1, source_target_pairs={{0,2},{2,3},{3,1},{1,0},{4,6},{6,7},{7,5},{5,4},{8,10},{10,11},{11... | collective-permute-start | bytes 786440 | tf_op jit(solution)/shard_map/ppermute | solution.py:291
  10.3 5.1 %collective-permute-done.8.refs_0_ = bf16[256,512]{1,0:T(8,128)(2,1)S(1)} collective-permute-done((bf16[256,512]{1,0:T(8,128)(2,1)S(1)}, bf16[256,512]{1,0:T(8,128)(2,1)S(1)}, u32[]{:S(2)}, u32[]{:S(2)}) %collective-permute-start.8) | collective-permute-done | bytes 262176 | tf_op jit(solution)/shard_map/ppermute | solution.py:291
  15.4 3.4 %collective-permute-start.9 = (bf16[256,512]{1,0:T(8,128)(2,1)S(1)}, bf16[256,512]{1,0:T(8,128)(2,1)S(1)}, u32[]{:S(2)}, u32[]{:S(2)}) collective-permute-start(bf16[256,512]{1,0:T(8,128)(2,1)S(1)} %collective-permute-done.8.refs_0_), channel_id=1, source_target_pairs={{0,2},{2,3},{3,1},{1,0},{4,6},{6,7},{7,5},{5,4},{8,10},{10,11},{11... | collective-permute-start | bytes 786440 | tf_op jit(solution)/shard_map/ppermute | solution.py:291
  18.9 2.1 %collective-permute-done.3.refs_1_ = bf16[256,512]{1,0:T(8,128)(2,1)S(1)} collective-permute-done((bf16[256,512]{1,0:T(8,128)(2,1)S(1)}, bf16[256,512]{1,0:T(8,128)(2,1)S(1)}, u32[]{:S(2)}, u32[]{:S(2)}) %collective-permute-start.3) | collective-permute-done | bytes 262176 | tf_op jit(solution)/shard_map/ppermute | solution.py:291
  21.0 3.4 %collective-permute-start.4 = (bf16[256,512]{1,0:T(8,128)(2,1)S(1)}, bf16[256,512]{1,0:T(8,128)(2,1)S(1)}, u32[]{:S(2)}, u32[]{:S(2)}) collective-permute-start(bf16[256,512]{1,0:T(8,128)(2,1)S(1)} %collective-permute-done.3.refs_1_), channel_id=1, source_target_pairs={{0,2},{2,3},{3,1},{1,0},{4,6},{6,7},{7,5},{5,4},{8,10},{10,11},{11... | collective-permute-start | bytes 786440 | tf_op jit(solution)/shard_map/ppermute | solution.py:291
  24.4 2.2 %collective-permute-done.9.refs_0_ = bf16[256,512]{1,0:T(8,128)(2,1)S(1)} collective-permute-done((bf16[256,512]{1,0:T(8,128)(2,1)S(1)}, bf16[256,512]{1,0:T(8,128)(2,1)S(1)}, u32[]{:S(2)}, u32[]{:S(2)}) %collective-permute-start.9) | collective-permute-done | bytes 262176 | tf_op jit(solution)/shard_map/ppermute | solution.py:291
  26.7 3.4 %collective-permute-start.10 = (bf16[256,256]{1,0:T(8,128)(2,1)S(1)}, bf16[256,256]{1,0:T(8,128)(2,1)S(1)}, u32[]{:S(2)}, u32[]{:S(2)}) collective-permute-start(bf16[256,256]{1,0:T(8,128)(2,1)S(1)} %get-tuple-element.30), channel_id=1, source_target_pairs={{0,2},{2,3},{3,1},{1,0},{4,6},{6,7},{7,5},{5,4},{8,10},{10,11},{11... | collective-permute-start | bytes 393224 | tf_op jit(solution)/shard_map/ppermute | solution.py:291
  30.1 0.7 %collective-permute-start.11 = (bf16[256,256]{1,0:T(8,128)(2,1)S(1)}, bf16[256,256]{1,0:T(8,128)(2,1)S(1)}, u32[]{:S(2)}, u32[]{:S(2)}) collective-permute-start(bf16[256,256]{1,0:T(8,128)(2,1)S(1)} %get-tuple-element.29), channel_id=1, source_target_pairs={{0,2},{2,3},{3,1},{1,0},{4,6},{6,7},{7,5},{5,4},{8,10},{10,11},{11... | collective-permute-start | bytes 393224 | tf_op jit(solution)/shard_map/ppermute | solution.py:291
  30.8 1.5 %collective-permute-done.4.refs_1_ = bf16[256,512]{1,0:T(8,128)(2,1)S(1)} collective-permute-done((bf16[256,512]{1,0:T(8,128)(2,1)S(1)}, bf16[256,512]{1,0:T(8,128)(2,1)S(1)}, u32[]{:S(2)}, u32[]{:S(2)}) %collective-permute-start.4) | collective-permute-done | bytes 262176 | tf_op jit(solution)/shard_map/ppermute | solution.py:291
  32.3 3.4 %collective-permute-start.12 = (bf16[256,256]{1,0:T(8,128)(2,1)S(1)}, bf16[256,256]{1,0:T(8,128)(2,1)S(1)}, u32[]{:S(2)}, u32[]{:S(2)}) collective-permute-start(bf16[256,256]{1,0:T(8,128)(2,1)S(1)} %get-tuple-element.27), channel_id=1, source_target_pairs={{0,2},{2,3},{3,1},{1,0},{4,6},{6,7},{7,5},{5,4},{8,10},{10,11},{11... | collective-permute-start | bytes 393224 | tf_op jit(solution)/shard_map/ppermute | solution.py:291
  35.7 0.7 %collective-permute-start.5 = (bf16[256,256]{1,0:T(8,128)(2,1)S(1)}, bf16[256,256]{1,0:T(8,128)(2,1)S(1)}, u32[]{:S(2)}, u32[]{:S(2)}) collective-permute-start(bf16[256,256]{1,0:T(8,128)(2,1)S(1)} %get-tuple-element.28), channel_id=1, source_target_pairs={{0,2},{2,3},{3,1},{1,0},{4,6},{6,7},{7,5},{5,4},{8,10},{10,11},{11... | collective-permute-start | bytes 393224 | tf_op jit(solution)/shard_map/ppermute | solution.py:291
  36.4 0.7 %project.4.refs_6_ = f32[256,1024]{1,0:T(8,128)S(1)} custom-call(bf16[256,512]{1,0:T(8,128)(2,1)S(1)} %get-tuple-element.23.refs_0_, bf16[256,512]{1,0:T(8,128)(2,1)S(1)} %get-tuple-element.20.refs_1_, bf16[2048,512]{1,0:T(8,128)(2,1)S(1)} %copy-done, bf16[2048,512]{1,0:T(8,128)(2,1)S(1)} %collective-permute-done.6.refs_3_.refs_4_.refs_1_, ...), custom_call_target="tpu_custom_call" | custom-call | flops 536870912 | bytes 9961472 | tf_op jit(solution)/shard_map/project/pallas_call | solution.py:60
  37.2 0.7 %project.5.refs_6_ = f32[256,1024]{1,0:T(8,128)S(1)} custom-call(bf16[256,512]{1,0:T(8,128)(2,1)S(1)} %collective-permute-done.8.refs_0_, bf16[256,512]{1,0:T(8,128)(2,1)S(1)} %collective-permute-done.3.refs_1_, bf16[2048,512]{1,0:T(8,128)(2,1)S(1)} %copy-done, bf16[2048,512]{1,0:T(8,128)(2,1)S(1)} %collective-permute-done.6.refs_3_.refs_4_.refs_1_, ...), custom_call_target="tpu_custom_call" | custom-call | flops 536870912 | bytes 11010048 | tf_op jit(solution)/shard_map/project/pallas_call | solution.py:60
  37.9 0.7 %project.6.refs_7_ = f32[256,1024]{1,0:T(8,128)S(1)} custom-call(bf16[256,512]{1,0:T(8,128)(2,1)S(1)} %collective-permute-done.9.refs_0_, bf16[256,512]{1,0:T(8,128)(2,1)S(1)} %collective-permute-done.4.refs_1_, bf16[2048,512]{1,0:T(8,128)(2,1)S(1)} %copy-done, bf16[2048,512]{1,0:T(8,128)(2,1)S(1)} %collective-permute-done.6.refs_3_.refs_4_.refs_1_, ...), custom_call_target="tpu_custom_call" | custom-call | flops 536870912 | bytes 11010048 | tf_op jit(solution)/shard_map/project/pallas_call | solution.py:60
  38.7 2.0 %collective-permute-done.12.refs_2_ = bf16[256,256]{1,0:T(8,128)(2,1)S(1)} collective-permute-done((bf16[256,256]{1,0:T(8,128)(2,1)S(1)}, bf16[256,256]{1,0:T(8,128)(2,1)S(1)}, u32[]{:S(2)}, u32[]{:S(2)}) %collective-permute-start.12) | collective-permute-done | bytes 131104 | tf_op jit(solution)/shard_map/ppermute | solution.py:291
  40.7 0.6 %project.7.refs_4_ = f32[256,1024]{1,0:T(8,128)S(1)} custom-call(bf16[256,256]{1,0:T(8,128)(2,1)S(1)} %collective-permute-done.10.refs_0_, bf16[256,256]{1,0:T(8,128)(2,1)S(1)} %collective-permute-done.11.refs_1_, bf16[256,256]{1,0:T(8,128)(2,1)S(1)} %collective-permute-done.12.refs_2_, bf16[2048,512]{1,0:T(8,128)(2,1)S(1)} %copy-done, ...), custom_call_target="tpu_custom_call" | custom-call | flops 402653184 | bytes 10878976 | tf_op jit(solution)/shard_map/project/pallas_call | solution.py:60
  41.3 1.4 %collective-permute-done.5.e_ref = bf16[256,256]{1,0:T(8,128)(2,1)S(1)} collective-permute-done((bf16[256,256]{1,0:T(8,128)(2,1)S(1)}, bf16[256,256]{1,0:T(8,128)(2,1)S(1)}, u32[]{:S(2)}, u32[]{:S(2)}) %collective-permute-start.5) | collective-permute-done | bytes 131104 | tf_op jit(solution)/shard_map/ppermute | solution.py:291
  42.7 1.0 %cross_attend.1 = (f32[64,640]{1,0:T(8,128)S(1)}, f32[64,640]{1,0:T(8,128)S(1)}) custom-call(bf16[256,256]{1,0:T(8,128)(2,1)S(1)} %collective-permute-done.5.e_ref, bf16[2048,512]{1,0:T(8,128)(2,1)S(1)} %copy-done, bf16[2048,512]{1,0:T(8,128)(2,1)S(1)} %collective-permute-done.6.refs_3_.refs_4_.refs_1_, bf16[2048,512]{1,0:T(8,128)(2,1)S(1)} %copy-done.1, ...), custom_call_target="tpu_custom_call" | custom-call | flops 134217728 | bytes 10158080 | tf_op jit(solution)/shard_map/cross_attend/pallas_call | solution.py:60
  43.8 1.4 %collective-permute-done.14.refs_1_ = f32[64,640]{1,0:T(8,128)S(1)} collective-permute-done((f32[64,640]{1,0:T(8,128)S(1)}, f32[64,640]{1,0:T(8,128)S(1)}, u32[]{:S(2)}, u32[]{:S(2)}) %collective-permute-start.14) | collective-permute-done | bytes 163872 | tf_op jit(solution)/shard_map/ppermute | solution.py:302
  45.2 0.8 %combine.1 = bf16[64,512]{1,0:T(8,128)(2,1)} custom-call(f32[64,640]{1,0:T(8,128)S(1)} %get-tuple-element.25.refs_0_, f32[64,640]{1,0:T(8,128)S(1)} %collective-permute-done.14.refs_1_), custom_call_target="tpu_custom_call" | custom-call | bytes 393216 | tf_op jit(solution)/shard_map/combine/pallas_call | solution.py:60
  (24 shorter events, 1.7 us)
Async XLA Ops:
  0.0 3.0 %collective-permute-start.1 = (bf16[256,1024]{1,0:T(8,128)(2,1)}, bf16[256,1024]{1,0:T(8,128)(2,1)S(1)}, u32[]{:S(2)}, u32[]{:S(2)}) collective-permute-start(bf16[256,1024]{1,0:T(8,128)(2,1)} %refs_1_.1), channel_id=1, source_target_pairs={{0,4},{4,0},{1,5},{5,1},{2,6},{6,2},{3,7},{7,3},{8,12},{12,8},{9,1... | collective-permute-start | bytes 1572872 | tf_op jit(solution)/shard_map/ppermute | solution.py:248
  0.5 2.5 %collective-permute-start.2 = (bf16[256,1024]{1,0:T(8,128)(2,1)}, bf16[256,1024]{1,0:T(8,128)(2,1)S(1)}, u32[]{:S(2)}, u32[]{:S(2)}) collective-permute-start(bf16[256,1024]{1,0:T(8,128)(2,1)} %refs_2_.1), channel_id=1, source_target_pairs={{0,4},{4,0},{1,5},{5,1},{2,6},{6,2},{3,7},{7,3},{8,12},{12,8},{9,1... | collective-permute-start | bytes 1572872 | tf_op jit(solution)/shard_map/ppermute | solution.py:248
  0.5 18.3 %copy-start.2 = (bf16[64,512]{1,0:T(8,128)(2,1)S(1)}, bf16[64,512]{1,0:T(8,128)(2,1)}, u32[]{:S(2)}) copy-start(bf16[64,512]{1,0:T(8,128)(2,1)} %param.13) | copy-start | bytes 196612
  0.5 2.4 %collective-permute-start = (s32[1,256]{1,0:T(1,128)}, s32[1,256]{1,0:T(1,128)S(1)}, u32[]{:S(2)}, u32[]{:S(2)}) collective-permute-start(s32[1,256]{1,0:T(1,128)} %bitcast.1), channel_id=1, source_target_pairs={{0,4},{4,0},{1,5},{5,1},{2,6},{6,2},{3,7},{7,3},{8,12},{12,8},{9,1... | collective-permute-start | bytes 3080 | tf_op jit(solution)/shard_map/ppermute | solution.py:248
  1.0 35.4 %copy-start.1 = (bf16[2048,512]{1,0:T(8,128)(2,1)S(1)}, bf16[2048,512]{1,0:T(8,128)(2,1)}, u32[]{:S(2)}) copy-start(bf16[2048,512]{1,0:T(8,128)(2,1)} %refs_2_.5) | copy-start | bytes 6291460
  2.5 33.9 %copy-start = (bf16[2048,512]{1,0:T(8,128)(2,1)S(1)}, bf16[2048,512]{1,0:T(8,128)(2,1)}, u32[]{:S(2)}) copy-start(bf16[2048,512]{1,0:T(8,128)(2,1)} %refs_0_.2) | copy-start | bytes 6291460
  3.0 32.8 %collective-permute-start.6 = (bf16[2048,512]{1,0:T(8,128)(2,1)}, bf16[2048,512]{1,0:T(8,128)(2,1)S(1)}, u32[]{:S(2)}, u32[]{:S(2)}) collective-permute-start(bf16[2048,512]{1,0:T(8,128)(2,1)} %refs_0_.2), channel_id=1, source_target_pairs={{0,4},{4,0},{1,5},{5,1},{2,6},{6,2},{3,7},{7,3},{8,12},{12,8},{9,1... | collective-permute-start | bytes 6291464 | tf_op jit(solution)/shard_map/ppermute | solution.py:248
  3.3 33.1 %collective-permute-start.7 = (bf16[2048,512]{1,0:T(8,128)(2,1)}, bf16[2048,512]{1,0:T(8,128)(2,1)S(1)}, u32[]{:S(2)}, u32[]{:S(2)}) collective-permute-start(bf16[2048,512]{1,0:T(8,128)(2,1)} %refs_2_.5), channel_id=1, source_target_pairs={{0,4},{4,0},{1,5},{5,1},{2,6},{6,2},{3,7},{7,3},{8,12},{12,8},{9,1... | collective-permute-start | bytes 6291464 | tf_op jit(solution)/shard_map/ppermute | solution.py:248
  4.7 10.7 %collective-permute-start.8 = (bf16[256,512]{1,0:T(8,128)(2,1)S(1)}, bf16[256,512]{1,0:T(8,128)(2,1)S(1)}, u32[]{:S(2)}, u32[]{:S(2)}) collective-permute-start(bf16[256,512]{1,0:T(8,128)(2,1)S(1)} %get-tuple-element.23.refs_0_), channel_id=1, source_target_pairs={{0,2},{2,3},{3,1},{1,0},{4,6},{6,7},{7,5},{5,4},{8,10},{10,11},{11... | collective-permute-start | bytes 786440 | tf_op jit(solution)/shard_map/ppermute | solution.py:291
  8.7 12.3 %collective-permute-start.3 = (bf16[256,512]{1,0:T(8,128)(2,1)S(1)}, bf16[256,512]{1,0:T(8,128)(2,1)S(1)}, u32[]{:S(2)}, u32[]{:S(2)}) collective-permute-start(bf16[256,512]{1,0:T(8,128)(2,1)S(1)} %get-tuple-element.20.refs_1_), channel_id=1, source_target_pairs={{0,2},{2,3},{3,1},{1,0},{4,6},{6,7},{7,5},{5,4},{8,10},{10,11},{11... | collective-permute-start | bytes 786440 | tf_op jit(solution)/shard_map/ppermute | solution.py:291
  15.4 11.2 %collective-permute-start.9 = (bf16[256,512]{1,0:T(8,128)(2,1)S(1)}, bf16[256,512]{1,0:T(8,128)(2,1)S(1)}, u32[]{:S(2)}, u32[]{:S(2)}) collective-permute-start(bf16[256,512]{1,0:T(8,128)(2,1)S(1)} %collective-permute-done.8.refs_0_), channel_id=1, source_target_pairs={{0,2},{2,3},{3,1},{1,0},{4,6},{6,7},{7,5},{5,4},{8,10},{10,11},{11... | collective-permute-start | bytes 786440 | tf_op jit(solution)/shard_map/ppermute | solution.py:291
  18.8 5.6 %collective-permute-start.13 = (bf16[64,512]{1,0:T(8,128)(2,1)S(1)}, bf16[64,512]{1,0:T(8,128)(2,1)S(1)}, u32[]{:S(2)}, u32[]{:S(2)}) collective-permute-start(bf16[64,512]{1,0:T(8,128)(2,1)S(1)} %copy-done.2), channel_id=1, source_target_pairs={{0,4},{4,0},{1,5},{5,1},{2,6},{6,2},{3,7},{7,3},{8,12},{12,8},{9,1... | collective-permute-start | bytes 196616 | tf_op jit(solution)/shard_map/ppermute | solution.py:248
  21.0 11.2 %collective-permute-start.4 = (bf16[256,512]{1,0:T(8,128)(2,1)S(1)}, bf16[256,512]{1,0:T(8,128)(2,1)S(1)}, u32[]{:S(2)}, u32[]{:S(2)}) collective-permute-start(bf16[256,512]{1,0:T(8,128)(2,1)S(1)} %collective-permute-done.3.refs_1_), channel_id=1, source_target_pairs={{0,2},{2,3},{3,1},{1,0},{4,6},{6,7},{7,5},{5,4},{8,10},{10,11},{11... | collective-permute-start | bytes 786440 | tf_op jit(solution)/shard_map/ppermute | solution.py:291
  26.7 12.0 %collective-permute-start.10 = (bf16[256,256]{1,0:T(8,128)(2,1)S(1)}, bf16[256,256]{1,0:T(8,128)(2,1)S(1)}, u32[]{:S(2)}, u32[]{:S(2)}) collective-permute-start(bf16[256,256]{1,0:T(8,128)(2,1)S(1)} %get-tuple-element.30), channel_id=1, source_target_pairs={{0,2},{2,3},{3,1},{1,0},{4,6},{6,7},{7,5},{5,4},{8,10},{10,11},{11... | collective-permute-start | bytes 393224 | tf_op jit(solution)/shard_map/ppermute | solution.py:291
  30.1 8.6 %collective-permute-start.11 = (bf16[256,256]{1,0:T(8,128)(2,1)S(1)}, bf16[256,256]{1,0:T(8,128)(2,1)S(1)}, u32[]{:S(2)}, u32[]{:S(2)}) collective-permute-start(bf16[256,256]{1,0:T(8,128)(2,1)S(1)} %get-tuple-element.29), channel_id=1, source_target_pairs={{0,2},{2,3},{3,1},{1,0},{4,6},{6,7},{7,5},{5,4},{8,10},{10,11},{11... | collective-permute-start | bytes 393224 | tf_op jit(solution)/shard_map/ppermute | solution.py:291
  32.3 8.4 %collective-permute-start.12 = (bf16[256,256]{1,0:T(8,128)(2,1)S(1)}, bf16[256,256]{1,0:T(8,128)(2,1)S(1)}, u32[]{:S(2)}, u32[]{:S(2)}) collective-permute-start(bf16[256,256]{1,0:T(8,128)(2,1)S(1)} %get-tuple-element.27), channel_id=1, source_target_pairs={{0,2},{2,3},{3,1},{1,0},{4,6},{6,7},{7,5},{5,4},{8,10},{10,11},{11... | collective-permute-start | bytes 393224 | tf_op jit(solution)/shard_map/ppermute | solution.py:291
  35.7 7.0 %collective-permute-start.5 = (bf16[256,256]{1,0:T(8,128)(2,1)S(1)}, bf16[256,256]{1,0:T(8,128)(2,1)S(1)}, u32[]{:S(2)}, u32[]{:S(2)}) collective-permute-start(bf16[256,256]{1,0:T(8,128)(2,1)S(1)} %get-tuple-element.28), channel_id=1, source_target_pairs={{0,2},{2,3},{3,1},{1,0},{4,6},{6,7},{7,5},{5,4},{8,10},{10,11},{11... | collective-permute-start | bytes 393224 | tf_op jit(solution)/shard_map/ppermute | solution.py:291
  43.7 1.5 %collective-permute-start.14 = (f32[64,640]{1,0:T(8,128)S(1)}, f32[64,640]{1,0:T(8,128)S(1)}, u32[]{:S(2)}, u32[]{:S(2)}) collective-permute-start(f32[64,640]{1,0:T(8,128)S(1)} %get-tuple-element.26), channel_id=1, source_target_pairs={{4,0},{0,4},{5,1},{1,5},{6,2},{2,6},{7,3},{3,7},{12,8},{8,12},{13,... | collective-permute-start | bytes 491528 | tf_op jit(solution)/shard_map/ppermute | solution.py:302

commit v5 on v4

--- a/solution.py
+++ b/solution.py
@@ -89,37 +89,33 @@
     )
 
 
-def attend_kernel(blocks, *refs):
+def attend_kernel(blocks, first, *refs):
     marks, q_ref = refs[:blocks], refs[blocks]
     keys, values = refs[blocks + 1 : 2 * blocks + 1], refs[2 * blocks + 1 : 3 * blocks + 1]
-    outs = refs[3 * blocks + 1 :]
+    out_ref = refs[-1]
     down = down_lanes(marks[0][...])
     same = jnp.concatenate([same_mark(down, m[...]) for m in marks], axis=1)
     rows = q_ref.shape[0]
-    heads = q_ref.shape[1] // HEAD_DIM
-    each = heads // len(outs)
-    for h in range(heads):
-        at = head_columns(h)
+    for h in range(out_ref.shape[1] // HEAD_DIM):
+        at = head_columns(first + h)
         scores = jnp.concatenate([dot_t(q_ref[:, at], k[:, at]) for k in keys], axis=1)
         _, weights, total = softmax_block(scores, same)
         rounded = weights.astype(BF16)
         summed = sum(dot(rounded[:, i * rows : (i + 1) * rows], v[:, at]) for i, v in enumerate(values))
-        outs[h // each][:, head_columns(h % each)] = (summed / total).astype(BF16)
-
-
-def encoder_attend(query, keys, values, marks, chunks):
-    rows, width = query.shape
-    pairs = rows * rows * len(keys) * (width // HEAD_DIM)
-    return list(
-        call(
-            functools.partial(attend_kernel, len(keys)),
-            "encoder_attend",
-            [((rows, width // chunks), BF16)] * chunks,
-            [*marks, query, *keys, *values],
-            flops=4 * pairs * HEAD_DIM,
-            exps=pairs,
-        )
-    )
+        out_ref[:, head_columns(h)] = (summed / total).astype(BF16)
+
+
+def encoder_attend(query, keys, values, marks, first, heads):
+    rows = query.shape[0]
+    pairs = rows * rows * len(keys) * heads
+    return call(
+        functools.partial(attend_kernel, len(keys), first),
+        "encoder_attend",
+        [((rows, heads * HEAD_DIM), BF16)],
+        [*marks, query, *keys, *values],
+        flops=4 * pairs * HEAD_DIM,
+        exps=pairs,
+    )[0]
 
 
 def target_mask_kernel(step, own_ref, *refs):
@@ -186,25 +182,50 @@
     )[0]
 
 
-def cross_kernel(shards, place, e_ref, *refs):
-    maps, (acc_ref, tgt_ref, mask_ref) = refs[: 2 * shards], refs[2 * shards : 2 * shards + 3]
-    outs, mem_ref = refs[2 * shards + 3 : -1], refs[-1]
-    half = mem_ref.shape[1] // 2
-    side_of = lambda side: slice(side * half, (side + 1) * half)
-
-    def store(side, value):
-        mem_ref[:, side_of(side)] = value.astype(BF16)
-
-    add_products(lambda side: acc_ref[:, side_of(side)], store, [e_ref], place(), maps[:shards], maps[shards:])
+def pick_kernel(shards, place, *refs):
+    maps, out_ref = refs[:-1], refs[-1]
+    shard, row = place()
+    depth, width = out_ref.shape[0], out_ref.shape[1] // 2
+    at = pl.ds(pl.multiple_of(row, depth), depth)
+
+    def copy(i):
+        out_ref[:, :width] = maps[i][at, :]
+        out_ref[:, width:] = maps[shards + i][at, :]
+
+    if shards == 1:
+        copy(0)
+    else:
+        for i in range(shards):
+            pl.when(shard == i)(functools.partial(copy, i))
+
+
+def pick(place, depth, key_shards, value_shards):
+    return call(
+        functools.partial(pick_kernel, len(key_shards), place),
+        "pick",
+        [((depth, 2 * key_shards[0].shape[1]), BF16)],
+        [*key_shards, *value_shards],
+    )[0]
+
+
+def cross_kernel(acc_ref, e_ref, map_ref, tgt_ref, mask_ref, *outs):
+    half = map_ref.shape[1] // 2
     heads = half // HEAD_DIM
     count = outs[0].shape[0]
+    chunk = e_ref[...]
+
+    def memory(at):
+        return (acc_ref[:, at] + dot(chunk, map_ref[:, at])).astype(BF16)
+
     lane = lax.broadcasted_iota(jnp.int32, (tgt_ref.shape[0], LANES), 1)
     stats = jnp.zeros(lane.shape, F32)
     same = mask_ref[...] > 0
+    keys = [memory(head_columns(h)) for h in range(heads)]
+    values = [memory(head_columns(heads + h)) for h in range(heads)]
     for h in range(heads):
         at = head_columns(h)
-        top, weights, total = softmax_block(dot_t(tgt_ref[:, at], mem_ref[:, at]), same)
-        summed = dot(weights.astype(BF16), mem_ref[:, head_columns(heads + h)])
+        top, weights, total = softmax_block(dot_t(tgt_ref[:, at], keys[h]), same)
+        summed = dot(weights.astype(BF16), values[h])
         for i, out_ref in enumerate(outs):
             out_ref[:, at] = summed[i * count : (i + 1) * count]
         stats = jnp.where(lane == h, top, jnp.where(lane == heads + h, total, stats))
@@ -212,17 +233,15 @@
         out_ref[:, half:] = stats[i * count : (i + 1) * count]
 
 
-def cross_attend(acc, chunk, place, key_shards, value_shards, targets, mask, parts):
-    rows, depth = chunk.shape
-    width = key_shards[0].shape[1]
+def cross_attend(acc, chunk, maps, targets, mask, parts):
+    width = targets.shape[1]
     count = targets.shape[0] // parts
     return call(
-        functools.partial(cross_kernel, len(key_shards), place),
+        cross_kernel,
         "cross_attend",
         [((count, width + LANES), F32)] * parts,
-        [chunk, *key_shards, *value_shards, acc, targets, mask],
-        flops=4 * rows * depth * width,
-        scratch=[pltpu.VMEM((rows, 2 * width), BF16)],
+        [acc, chunk, maps, targets, mask],
+        flops=2 * chunk.size * 2 * width,
     )
 
 
@@ -250,9 +269,6 @@
     marks = (doc_ids if n_ctx == 2 else doc_ids + 1).reshape(1, rows)
     keys, values, near_marks = bring(enc_key), bring(enc_value), bring(marks)
     query, own_key, own_value, marks = fetch(enc_query, enc_key, enc_value, marks)
-    chunks = 2
-    held = encoder_attend(query, [own_key, *keys], [own_value, *values], [marks, *near_marks], chunks)
-
     key_map, value_map, tgt_query, *_ = lax.optimization_barrier(
         (key_map, value_map, tgt_query, *keys, *values, *near_marks, query)
     )
@@ -263,6 +279,13 @@
         key_shards, value_shards = ([lax.all_gather(x, "ctx", axis=0, tiled=True)] for x in (key_map, value_map))
     targets = jnp.concatenate([tgt_query, *near_targets], 0)
     mask = target_mask(marks, [marks, *near_marks], tgt_rows)
+
+    chunks = 2
+    heads = features // HEAD_DIM // chunks
+    held = [
+        encoder_attend(query, [own_key, *keys], [own_value, *values], [marks, *near_marks], j * heads, heads)
+        for j in range(chunks)
+    ]
 
     order = ring_order(n_head)
     ring = [(order[i], order[(i + 1) % n_head]) for i in range(n_head)]
@@ -292,10 +315,9 @@
         acc = project(acc, held, functools.partial(place, turn, 0), key_shards, value_shards)
         held = later
     acc = project(acc, held[:-1], functools.partial(place, last, 0), key_shards, value_shards)
-    first = features - held[-1].shape[1]
-    parts = cross_attend(
-        acc, held[-1], functools.partial(place, last, first), key_shards, value_shards, targets, mask, 1 + len(links)
-    )
+    depth = held[-1].shape[1]
+    last_maps = pick(functools.partial(place, last, features - depth), depth, key_shards, value_shards)
+    parts = cross_attend(acc, held[-1], last_maps, targets, mask, 1 + len(links))
 
     combined = [parts[0]]
     for i, (pairs, piece) in enumerate(zip(links, parts[1:])):

time: 46.1 us -> 46 us (level)
  waiting for transfers between devices: 16.1 us -> 15.3 us
  starting transfers between devices: 22.1 us -> 22.7 us
    ppermute x8, waiting for transfers between devices: 14.3 us -> 13.3 us  [on_device(): later = [lax.ppermute(p, 'head', ring) for p in pieces]]
    ppermute x8, starting transfers between devices: 20.6 us -> 21.2 us  [on_device(): later = [lax.ppermute(p, 'head', ring) for p in pieces]]
    pallas_call x9 -> x11, Pallas kernels: 7.6 us -> 7.64 us  [call(): pl.pallas_call(kernel, in_specs=specs or [VMEM] * len(operands), out_spec...]
where the time goes in v5:
time: 46 us; the launch traced here: 45.9 us
  starting transfers between devices  22.7 us (49%)
  waiting for transfers between devices  15.3 us (33%)
  Pallas kernels  7.64 us (17%)
    ppermute x8, starting transfers between devices, on_device(): later = [lax.ppermute(p, 'head', ring) for p in pieces]  21.2 us
    ppermute x8, waiting for transfers between devices, on_device(): later = [lax.ppermute(p, 'head', ring) for p in pieces]  13.3 us
    pallas_call x11, Pallas kernels, call(): pl.pallas_call(kernel, in_specs=specs or [VMEM] * len(operands), out_spec...  7.64 us
    ppermute x6, starting transfers between devices, on_device(): bring = lambda x: [lax.ppermute(x, 'ctx', pairs) for pairs in links]  1.48 us
    ppermute x1, waiting for transfers between devices, on_device(): lax.ppermute(piece, 'ctx', [(target, source) for source, target in pairs])  1.38 us
  transfers between devices with their start and end apart: 15, of which 8 were waited for; matrix products, arithmetic and copies ran while one was open for 0% of the time, Pallas kernels for 13%

profile of v5, /device:TPU:0, one launch (start us, length us, event | category | flops | bytes accessed | tf_op | source)
XLA Modules:
  0.0 45.9 jit_solution(1755692173263372521)
XLA Ops:
  1.0 1.4 %fetch.1 = (bf16[256,1024]{1,0:T(8,128)(2,1)S(1)}, bf16[256,1024]{1,0:T(8,128)(2,1)S(1)}, bf16[256,1024]{1,0:T(8,128)(2,1)S(1)}, s32[1,256]{1,0:T(1,128)S(1)}) custom-call(bf16[256,1024]{1,0:T(8,128)(2,1)} %refs_0_.1, bf16[256,1024]{1,0:T(8,128)(2,1)} %refs_1_.1, bf16[256,1024]{1,0:T(8,128)(2,1)} %refs_2_.1, s32[1,256]{1,0:T(1,128)} %bitcast.2), custom_call_target="tpu_custom_call" | custom-call | bytes 3147776 | tf_op jit(solution)/shard_map/fetch/pallas_call | solution.py:60
  3.5 0.9 %encoder_attend.3.refs_1_ = bf16[256,512]{1,0:T(8,128)(2,1)S(1)} custom-call(s32[1,256]{1,0:T(1,128)S(1)} %get-tuple-element.14.refs_0_.own_ref, s32[1,256]{1,0:T(1,128)S(1)} %collective-permute-done.refs_1_, bf16[256,1024]{1,0:T(8,128)(2,1)S(1)} %get-tuple-element.15.refs_2_, bf16[256,1024]{1,0:T(8,128)(2,1)S(1)} %get-tuple-element.16.refs_3_, ...), custom_call_target="tpu_custom_call" | custom-call | flops 268435456 | bytes 2885632 | tf_op jit(solution)/shard_map/encoder_attend/pallas_call | solution.py:60
  4.4 4.0 %collective-permute-start.7 = (bf16[256,512]{1,0:T(8,128)(2,1)S(1)}, bf16[256,512]{1,0:T(8,128)(2,1)S(1)}, u32[]{:S(2)}, u32[]{:S(2)}) collective-permute-start(bf16[256,512]{1,0:T(8,128)(2,1)S(1)} %encoder_attend.3.refs_1_), channel_id=1, source_target_pairs={{0,2},{2,3},{3,1},{1,0},{4,6},{6,7},{7,5},{5,4},{8,10},{10,11},{11... | collective-permute-start | bytes 786440 | tf_op jit(solution)/shard_map/ppermute | solution.py:314
  8.4 0.9 %encoder_attend.2.refs_0_ = bf16[256,512]{1,0:T(8,128)(2,1)S(1)} custom-call(s32[1,256]{1,0:T(1,128)S(1)} %get-tuple-element.14.refs_0_.own_ref, s32[1,256]{1,0:T(1,128)S(1)} %collective-permute-done.refs_1_, bf16[256,1024]{1,0:T(8,128)(2,1)S(1)} %get-tuple-element.15.refs_2_, bf16[256,1024]{1,0:T(8,128)(2,1)S(1)} %get-tuple-element.16.refs_3_, ...), custom_call_target="tpu_custom_call" | custom-call | flops 268435456 | bytes 2885632 | tf_op jit(solution)/shard_map/encoder_attend/pallas_call | solution.py:60
  9.2 1.6 %collective-permute-start.3 = (bf16[256,512]{1,0:T(8,128)(2,1)S(1)}, bf16[256,512]{1,0:T(8,128)(2,1)S(1)}, u32[]{:S(2)}, u32[]{:S(2)}) collective-permute-start(bf16[256,512]{1,0:T(8,128)(2,1)S(1)} %encoder_attend.2.refs_0_), channel_id=1, source_target_pairs={{0,2},{2,3},{3,1},{1,0},{4,6},{6,7},{7,5},{5,4},{8,10},{10,11},{11... | collective-permute-start | bytes 786440 | tf_op jit(solution)/shard_map/ppermute | solution.py:314
  10.9 4.2 %collective-permute-done.7.refs_1_ = bf16[256,512]{1,0:T(8,128)(2,1)S(1)} collective-permute-done((bf16[256,512]{1,0:T(8,128)(2,1)S(1)}, bf16[256,512]{1,0:T(8,128)(2,1)S(1)}, u32[]{:S(2)}, u32[]{:S(2)}) %collective-permute-start.7) | collective-permute-done | bytes 262176 | tf_op jit(solution)/shard_map/ppermute | solution.py:314
  15.0 3.4 %collective-permute-start.8 = (bf16[256,512]{1,0:T(8,128)(2,1)S(1)}, bf16[256,512]{1,0:T(8,128)(2,1)S(1)}, u32[]{:S(2)}, u32[]{:S(2)}) collective-permute-start(bf16[256,512]{1,0:T(8,128)(2,1)S(1)} %collective-permute-done.7.refs_1_), channel_id=1, source_target_pairs={{0,2},{2,3},{3,1},{1,0},{4,6},{6,7},{7,5},{5,4},{8,10},{10,11},{11... | collective-permute-start | bytes 786440 | tf_op jit(solution)/shard_map/ppermute | solution.py:314
  18.6 2.1 %collective-permute-done.3.refs_0_ = bf16[256,512]{1,0:T(8,128)(2,1)S(1)} collective-permute-done((bf16[256,512]{1,0:T(8,128)(2,1)S(1)}, bf16[256,512]{1,0:T(8,128)(2,1)S(1)}, u32[]{:S(2)}, u32[]{:S(2)}) %collective-permute-start.3) | collective-permute-done | bytes 262176 | tf_op jit(solution)/shard_map/ppermute | solution.py:314
  20.7 3.4 %collective-permute-start.4 = (bf16[256,512]{1,0:T(8,128)(2,1)S(1)}, bf16[256,512]{1,0:T(8,128)(2,1)S(1)}, u32[]{:S(2)}, u32[]{:S(2)}) collective-permute-start(bf16[256,512]{1,0:T(8,128)(2,1)S(1)} %collective-permute-done.3.refs_0_), channel_id=1, source_target_pairs={{0,2},{2,3},{3,1},{1,0},{4,6},{6,7},{7,5},{5,4},{8,10},{10,11},{11... | collective-permute-start | bytes 786440 | tf_op jit(solution)/shard_map/ppermute | solution.py:314
  24.1 2.2 %collective-permute-done.8.refs_1_ = bf16[256,512]{1,0:T(8,128)(2,1)S(1)} collective-permute-done((bf16[256,512]{1,0:T(8,128)(2,1)S(1)}, bf16[256,512]{1,0:T(8,128)(2,1)S(1)}, u32[]{:S(2)}, u32[]{:S(2)}) %collective-permute-start.8) | collective-permute-done | bytes 262176 | tf_op jit(solution)/shard_map/ppermute | solution.py:314
  26.3 3.4 %collective-permute-start.9 = (bf16[256,256]{1,0:T(8,128)(2,1)S(1)}, bf16[256,256]{1,0:T(8,128)(2,1)S(1)}, u32[]{:S(2)}, u32[]{:S(2)}) collective-permute-start(bf16[256,256]{1,0:T(8,128)(2,1)S(1)} %get-tuple-element.24), channel_id=1, source_target_pairs={{0,2},{2,3},{3,1},{1,0},{4,6},{6,7},{7,5},{5,4},{8,10},{10,11},{11... | collective-permute-start | bytes 393224 | tf_op jit(solution)/shard_map/ppermute | solution.py:314
  29.7 2.2 %collective-permute-done.4.refs_0_ = bf16[256,512]{1,0:T(8,128)(2,1)S(1)} collective-permute-done((bf16[256,512]{1,0:T(8,128)(2,1)S(1)}, bf16[256,512]{1,0:T(8,128)(2,1)S(1)}, u32[]{:S(2)}, u32[]{:S(2)}) %collective-permute-start.4) | collective-permute-done | bytes 262176 | tf_op jit(solution)/shard_map/ppermute | solution.py:314
  31.9 3.4 %collective-permute-start.5 = (bf16[256,256]{1,0:T(8,128)(2,1)S(1)}, bf16[256,256]{1,0:T(8,128)(2,1)S(1)}, u32[]{:S(2)}, u32[]{:S(2)}) collective-permute-start(bf16[256,256]{1,0:T(8,128)(2,1)S(1)} %get-tuple-element.26), channel_id=1, source_target_pairs={{0,2},{2,3},{3,1},{1,0},{4,6},{6,7},{7,5},{5,4},{8,10},{10,11},{11... | collective-permute-start | bytes 393224 | tf_op jit(solution)/shard_map/ppermute | solution.py:314
  35.3 0.7 %collective-permute-start.6 = (bf16[256,256]{1,0:T(8,128)(2,1)S(1)}, bf16[256,256]{1,0:T(8,128)(2,1)S(1)}, u32[]{:S(2)}, u32[]{:S(2)}) collective-permute-start(bf16[256,256]{1,0:T(8,128)(2,1)S(1)} %get-tuple-element.25), channel_id=1, source_target_pairs={{0,2},{2,3},{3,1},{1,0},{4,6},{6,7},{7,5},{5,4},{8,10},{10,11},{11... | collective-permute-start | bytes 393224 | tf_op jit(solution)/shard_map/ppermute | solution.py:314
  36.0 1.2 %collective-permute-start.12 = (bf16[256,256]{1,0:T(8,128)(2,1)S(1)}, bf16[256,256]{1,0:T(8,128)(2,1)S(1)}, u32[]{:S(2)}, u32[]{:S(2)}) collective-permute-start(bf16[256,256]{1,0:T(8,128)(2,1)S(1)} %get-tuple-element.23), channel_id=1, source_target_pairs={{0,2},{2,3},{3,1},{1,0},{4,6},{6,7},{7,5},{5,4},{8,10},{10,11},{11... | collective-permute-start | bytes 393224 | tf_op jit(solution)/shard_map/ppermute | solution.py:314
  37.3 0.7 %project.4.refs_6_ = f32[256,1024]{1,0:T(8,128)S(1)} custom-call(bf16[256,512]{1,0:T(8,128)(2,1)S(1)} %encoder_attend.2.refs_0_, bf16[256,512]{1,0:T(8,128)(2,1)S(1)} %encoder_attend.3.refs_1_, bf16[2048,512]{1,0:T(8,128)(2,1)S(1)} %copy-done, bf16[2048,512]{1,0:T(8,128)(2,1)S(1)} %collective-permute-done.10.refs_3_.refs_4_.refs_1_, ...), custom_call_target="tpu_custom_call" | custom-call | flops 536870912 | bytes 9961472 | tf_op jit(solution)/shard_map/project/pallas_call | solution.py:60
  38.1 0.7 %project.5.refs_6_ = f32[256,1024]{1,0:T(8,128)S(1)} custom-call(bf16[256,512]{1,0:T(8,128)(2,1)S(1)} %collective-permute-done.3.refs_0_, bf16[256,512]{1,0:T(8,128)(2,1)S(1)} %collective-permute-done.7.refs_1_, bf16[2048,512]{1,0:T(8,128)(2,1)S(1)} %copy-done, bf16[2048,512]{1,0:T(8,128)(2,1)S(1)} %collective-permute-done.10.refs_3_.refs_4_.refs_1_, ...), custom_call_target="tpu_custom_call" | custom-call | flops 536870912 | bytes 11010048 | tf_op jit(solution)/shard_map/project/pallas_call | solution.py:60
  38.8 0.7 %project.6.refs_7_ = f32[256,1024]{1,0:T(8,128)S(1)} custom-call(bf16[256,512]{1,0:T(8,128)(2,1)S(1)} %collective-permute-done.4.refs_0_, bf16[256,512]{1,0:T(8,128)(2,1)S(1)} %collective-permute-done.8.refs_1_, bf16[2048,512]{1,0:T(8,128)(2,1)S(1)} %copy-done, bf16[2048,512]{1,0:T(8,128)(2,1)S(1)} %collective-permute-done.10.refs_3_.refs_4_.refs_1_, ...), custom_call_target="tpu_custom_call" | custom-call | flops 536870912 | bytes 11010048 | tf_op jit(solution)/shard_map/project/pallas_call | solution.py:60
  39.6 1.9 %collective-permute-done.6.refs_1_ = bf16[256,256]{1,0:T(8,128)(2,1)S(1)} collective-permute-done((bf16[256,256]{1,0:T(8,128)(2,1)S(1)}, bf16[256,256]{1,0:T(8,128)(2,1)S(1)}, u32[]{:S(2)}, u32[]{:S(2)}) %collective-permute-start.6) | collective-permute-done | bytes 131104 | tf_op jit(solution)/shard_map/ppermute | solution.py:314
  41.5 0.6 %project.7.acc_ref = f32[256,1024]{1,0:T(8,128)S(1)} custom-call(bf16[256,256]{1,0:T(8,128)(2,1)S(1)} %collective-permute-done.5.refs_0_, bf16[256,256]{1,0:T(8,128)(2,1)S(1)} %collective-permute-done.6.refs_1_, bf16[256,256]{1,0:T(8,128)(2,1)S(1)} %collective-permute-done.9.refs_2_, bf16[2048,512]{1,0:T(8,128)(2,1)S(1)} %copy-done, ...), custom_call_target="tpu_custom_call" | custom-call | flops 402653184 | bytes 10878976 | tf_op jit(solution)/shard_map/project/pallas_call | solution.py:60
  42.1 0.8 %collective-permute-done.12.e_ref = bf16[256,256]{1,0:T(8,128)(2,1)S(1)} collective-permute-done((bf16[256,256]{1,0:T(8,128)(2,1)S(1)}, bf16[256,256]{1,0:T(8,128)(2,1)S(1)}, u32[]{:S(2)}, u32[]{:S(2)}) %collective-permute-start.12) | collective-permute-done | bytes 131104 | tf_op jit(solution)/shard_map/ppermute | solution.py:314
  42.9 0.7 %cross_attend.1 = (f32[64,640]{1,0:T(8,128)S(1)}, f32[64,640]{1,0:T(8,128)S(1)}) custom-call(f32[256,1024]{1,0:T(8,128)S(1)} %project.7.acc_ref, bf16[256,256]{1,0:T(8,128)(2,1)S(1)} %collective-permute-done.12.e_ref, bf16[256,1024]{1,0:T(8,128)(2,1)S(1)} %pick.1.map_ref, bf16[128,512]{1,0:T(8,128)(2,1)S(1)} %pad_maximum_fusion.tgt_ref, ...), custom_call_target="tpu_custom_call" | custom-call | flops 134217728 | bytes 2293760 | tf_op jit(solution)/shard_map/cross_attend/pallas_call | solution.py:60
  43.6 1.4 %collective-permute-done.14.refs_1_ = f32[64,640]{1,0:T(8,128)S(1)} collective-permute-done((f32[64,640]{1,0:T(8,128)S(1)}, f32[64,640]{1,0:T(8,128)S(1)}, u32[]{:S(2)}, u32[]{:S(2)}) %collective-permute-start.14) | collective-permute-done | bytes 163872 | tf_op jit(solution)/shard_map/ppermute | solution.py:324
  45.0 0.8 %combine.1 = bf16[64,512]{1,0:T(8,128)(2,1)} custom-call(f32[64,640]{1,0:T(8,128)S(1)} %get-tuple-element.21.refs_0_, f32[64,640]{1,0:T(8,128)S(1)} %collective-permute-done.14.refs_1_), custom_call_target="tpu_custom_call" | custom-call | bytes 393216 | tf_op jit(solution)/shard_map/combine/pallas_call | solution.py:60
  (26 shorter events, 2.4 us)
Async XLA Ops:
  0.0 3.0 %collective-permute-start.1 = (bf16[256,1024]{1,0:T(8,128)(2,1)}, bf16[256,1024]{1,0:T(8,128)(2,1)S(1)}, u32[]{:S(2)}, u32[]{:S(2)}) collective-permute-start(bf16[256,1024]{1,0:T(8,128)(2,1)} %refs_1_.1), channel_id=1, source_target_pairs={{0,4},{4,0},{1,5},{5,1},{2,6},{6,2},{3,7},{7,3},{8,12},{12,8},{9,1... | collective-permute-start | bytes 1572872 | tf_op jit(solution)/shard_map/ppermute | solution.py:267
  0.5 2.5 %collective-permute-start.2 = (bf16[256,1024]{1,0:T(8,128)(2,1)}, bf16[256,1024]{1,0:T(8,128)(2,1)S(1)}, u32[]{:S(2)}, u32[]{:S(2)}) collective-permute-start(bf16[256,1024]{1,0:T(8,128)(2,1)} %refs_2_.1), channel_id=1, source_target_pairs={{0,4},{4,0},{1,5},{5,1},{2,6},{6,2},{3,7},{7,3},{8,12},{12,8},{9,1... | collective-permute-start | bytes 1572872 | tf_op jit(solution)/shard_map/ppermute | solution.py:267
  0.5 2.4 %collective-permute-start = (s32[1,256]{1,0:T(1,128)}, s32[1,256]{1,0:T(1,128)S(1)}, u32[]{:S(2)}, u32[]{:S(2)}) collective-permute-start(s32[1,256]{1,0:T(1,128)} %bitcast.1), channel_id=1, source_target_pairs={{0,4},{4,0},{1,5},{5,1},{2,6},{6,2},{3,7},{7,3},{8,12},{12,8},{9,1... | collective-permute-start | bytes 3080 | tf_op jit(solution)/shard_map/ppermute | solution.py:267
  3.0 33.1 %collective-permute-start.10 = (bf16[2048,512]{1,0:T(8,128)(2,1)}, bf16[2048,512]{1,0:T(8,128)(2,1)S(1)}, u32[]{:S(2)}, u32[]{:S(2)}) collective-permute-start(bf16[2048,512]{1,0:T(8,128)(2,1)} %refs_0_.2), channel_id=1, source_target_pairs={{0,4},{4,0},{1,5},{5,1},{2,6},{6,2},{3,7},{7,3},{8,12},{12,8},{9,1... | collective-permute-start | bytes 6291464 | tf_op jit(solution)/shard_map/ppermute | solution.py:267
  3.3 33.9 %collective-permute-start.11 = (bf16[2048,512]{1,0:T(8,128)(2,1)}, bf16[2048,512]{1,0:T(8,128)(2,1)S(1)}, u32[]{:S(2)}, u32[]{:S(2)}) collective-permute-start(bf16[2048,512]{1,0:T(8,128)(2,1)} %refs_2_.5), channel_id=1, source_target_pairs={{0,4},{4,0},{1,5},{5,1},{2,6},{6,2},{3,7},{7,3},{8,12},{12,8},{9,1... | collective-permute-start | bytes 6291464 | tf_op jit(solution)/shard_map/ppermute | solution.py:267
  3.5 14.9 %copy-start.2 = (bf16[64,512]{1,0:T(8,128)(2,1)S(1)}, bf16[64,512]{1,0:T(8,128)(2,1)}, u32[]{:S(2)}) copy-start(bf16[64,512]{1,0:T(8,128)(2,1)} %param.13) | copy-start | bytes 196612
  4.3 32.9 %copy-start = (bf16[2048,512]{1,0:T(8,128)(2,1)S(1)}, bf16[2048,512]{1,0:T(8,128)(2,1)}, u32[]{:S(2)}) copy-start(bf16[2048,512]{1,0:T(8,128)(2,1)} %refs_0_.2) | copy-start | bytes 6291460
  4.3 32.9 %copy-start.1 = (bf16[2048,512]{1,0:T(8,128)(2,1)S(1)}, bf16[2048,512]{1,0:T(8,128)(2,1)}, u32[]{:S(2)}) copy-start(bf16[2048,512]{1,0:T(8,128)(2,1)} %refs_2_.5) | copy-start | bytes 6291460
  4.4 10.7 %collective-permute-start.7 = (bf16[256,512]{1,0:T(8,128)(2,1)S(1)}, bf16[256,512]{1,0:T(8,128)(2,1)S(1)}, u32[]{:S(2)}, u32[]{:S(2)}) collective-permute-start(bf16[256,512]{1,0:T(8,128)(2,1)S(1)} %encoder_attend.3.refs_1_), channel_id=1, source_target_pairs={{0,2},{2,3},{3,1},{1,0},{4,6},{6,7},{7,5},{5,4},{8,10},{10,11},{11... | collective-permute-start | bytes 786440 | tf_op jit(solution)/shard_map/ppermute | solution.py:314
  9.2 11.4 %collective-permute-start.3 = (bf16[256,512]{1,0:T(8,128)(2,1)S(1)}, bf16[256,512]{1,0:T(8,128)(2,1)S(1)}, u32[]{:S(2)}, u32[]{:S(2)}) collective-permute-start(bf16[256,512]{1,0:T(8,128)(2,1)S(1)} %encoder_attend.2.refs_0_), channel_id=1, source_target_pairs={{0,2},{2,3},{3,1},{1,0},{4,6},{6,7},{7,5},{5,4},{8,10},{10,11},{11... | collective-permute-start | bytes 786440 | tf_op jit(solution)/shard_map/ppermute | solution.py:314
  15.0 11.2 %collective-permute-start.8 = (bf16[256,512]{1,0:T(8,128)(2,1)S(1)}, bf16[256,512]{1,0:T(8,128)(2,1)S(1)}, u32[]{:S(2)}, u32[]{:S(2)}) collective-permute-start(bf16[256,512]{1,0:T(8,128)(2,1)S(1)} %collective-permute-done.7.refs_1_), channel_id=1, source_target_pairs={{0,2},{2,3},{3,1},{1,0},{4,6},{6,7},{7,5},{5,4},{8,10},{10,11},{11... | collective-permute-start | bytes 786440 | tf_op jit(solution)/shard_map/ppermute | solution.py:314
  18.4 5.6 %collective-permute-start.13 = (bf16[64,512]{1,0:T(8,128)(2,1)S(1)}, bf16[64,512]{1,0:T(8,128)(2,1)S(1)}, u32[]{:S(2)}, u32[]{:S(2)}) collective-permute-start(bf16[64,512]{1,0:T(8,128)(2,1)S(1)} %copy-done.2), channel_id=1, source_target_pairs={{0,4},{4,0},{1,5},{5,1},{2,6},{6,2},{3,7},{7,3},{8,12},{12,8},{9,1... | collective-permute-start | bytes 196616 | tf_op jit(solution)/shard_map/ppermute | solution.py:267
  20.7 11.2 %collective-permute-start.4 = (bf16[256,512]{1,0:T(8,128)(2,1)S(1)}, bf16[256,512]{1,0:T(8,128)(2,1)S(1)}, u32[]{:S(2)}, u32[]{:S(2)}) collective-permute-start(bf16[256,512]{1,0:T(8,128)(2,1)S(1)} %collective-permute-done.3.refs_0_), channel_id=1, source_target_pairs={{0,2},{2,3},{3,1},{1,0},{4,6},{6,7},{7,5},{5,4},{8,10},{10,11},{11... | collective-permute-start | bytes 786440 | tf_op jit(solution)/shard_map/ppermute | solution.py:314
  26.3 13.3 %collective-permute-start.9 = (bf16[256,256]{1,0:T(8,128)(2,1)S(1)}, bf16[256,256]{1,0:T(8,128)(2,1)S(1)}, u32[]{:S(2)}, u32[]{:S(2)}) collective-permute-start(bf16[256,256]{1,0:T(8,128)(2,1)S(1)} %get-tuple-element.24), channel_id=1, source_target_pairs={{0,2},{2,3},{3,1},{1,0},{4,6},{6,7},{7,5},{5,4},{8,10},{10,11},{11... | collective-permute-start | bytes 393224 | tf_op jit(solution)/shard_map/ppermute | solution.py:314
  31.9 7.7 %collective-permute-start.5 = (bf16[256,256]{1,0:T(8,128)(2,1)S(1)}, bf16[256,256]{1,0:T(8,128)(2,1)S(1)}, u32[]{:S(2)}, u32[]{:S(2)}) collective-permute-start(bf16[256,256]{1,0:T(8,128)(2,1)S(1)} %get-tuple-element.26), channel_id=1, source_target_pairs={{0,2},{2,3},{3,1},{1,0},{4,6},{6,7},{7,5},{5,4},{8,10},{10,11},{11... | collective-permute-start | bytes 393224 | tf_op jit(solution)/shard_map/ppermute | solution.py:314
  35.3 6.1 %collective-permute-start.6 = (bf16[256,256]{1,0:T(8,128)(2,1)S(1)}, bf16[256,256]{1,0:T(8,128)(2,1)S(1)}, u32[]{:S(2)}, u32[]{:S(2)}) collective-permute-start(bf16[256,256]{1,0:T(8,128)(2,1)S(1)} %get-tuple-element.25), channel_id=1, source_target_pairs={{0,2},{2,3},{3,1},{1,0},{4,6},{6,7},{7,5},{5,4},{8,10},{10,11},{11... | collective-permute-start | bytes 393224 | tf_op jit(solution)/shard_map/ppermute | solution.py:314
  36.0 6.9 %collective-permute-start.12 = (bf16[256,256]{1,0:T(8,128)(2,1)S(1)}, bf16[256,256]{1,0:T(8,128)(2,1)S(1)}, u32[]{:S(2)}, u32[]{:S(2)}) collective-permute-start(bf16[256,256]{1,0:T(8,128)(2,1)S(1)} %get-tuple-element.23), channel_id=1, source_target_pairs={{0,2},{2,3},{3,1},{1,0},{4,6},{6,7},{7,5},{5,4},{8,10},{10,11},{11... | collective-permute-start | bytes 393224 | tf_op jit(solution)/shard_map/ppermute | solution.py:314
  43.6 1.5 %collective-permute-start.14 = (f32[64,640]{1,0:T(8,128)S(1)}, f32[64,640]{1,0:T(8,128)S(1)}, u32[]{:S(2)}, u32[]{:S(2)}) collective-permute-start(f32[64,640]{1,0:T(8,128)S(1)} %get-tuple-element.22), channel_id=1, source_target_pairs={{4,0},{0,4},{5,1},{1,5},{6,2},{2,6},{7,3},{3,7},{12,8},{8,12},{13,... | collective-permute-start | bytes 491528 | tf_op jit(solution)/shard_map/ppermute | solution.py:324

commit v6 on v5

--- a/solution.py
+++ b/solution.py
@@ -156,6 +156,17 @@
             pl.when(shard == i)(functools.partial(add, i))
 
 
+def halve_kernel(source, *outs):
+    width = outs[0].shape[1]
+    for i, out in enumerate(outs):
+        out[...] = source[:, i * width : (i + 1) * width]
+
+
+def halve(chunk):
+    rows, width = chunk.shape
+    return call(halve_kernel, "halve", [((rows, width // 2), chunk.dtype)] * 2, [chunk], flops=10**10)
+
+
 def project_kernel(chunks, shards, has_acc, place, *refs):
     out_ref = refs[-1]
     e_refs, maps = refs[:chunks], refs[chunks : chunks + 2 * shards]
@@ -269,9 +280,6 @@
     marks = (doc_ids if n_ctx == 2 else doc_ids + 1).reshape(1, rows)
     keys, values, near_marks = bring(enc_key), bring(enc_value), bring(marks)
     query, own_key, own_value, marks = fetch(enc_query, enc_key, enc_value, marks)
-    key_map, value_map, tgt_query, *_ = lax.optimization_barrier(
-        (key_map, value_map, tgt_query, *keys, *values, *near_marks, query)
-    )
     near_targets = bring(tgt_query)
     if n_ctx == 2:
         key_shards, value_shards = [key_map, *bring(key_map)], [value_map, *bring(value_map)]
@@ -308,7 +316,7 @@
     acc, last = None, n_head - 1
     for turn in range(last):
         if turn == last - 1:
-            pieces = [p for h in held for p in jnp.split(h, 2, axis=1)]
+            pieces = [p for h in held for p in halve(h)]
         else:
             pieces = held
         later = [lax.ppermute(p, "head", ring) for p in pieces]

time: 46 us -> 47.9 us (1.041)
  waiting for transfers between devices: 15.3 us -> 23.3 us
  starting transfers between devices: 22.7 us -> 16.7 us
    ppermute x6, waiting for transfers between devices: 0.6 us -> 7.12 us  [on_device(): bring = lambda x: [lax.ppermute(x, 'ctx', pairs) for pairs in links]]
    ppermute x8, starting transfers between devices: 21.2 us -> 15 us  [on_device(): later = [lax.ppermute(p, 'head', ring) for p in pieces]]
    ppermute x8, waiting for transfers between devices: 13.3 us -> 14.8 us  [on_device(): later = [lax.ppermute(p, 'head', ring) for p in pieces]]
    pallas_call x11 -> x13, Pallas kernels: 7.64 us -> 7.68 us  [call(): pl.pallas_call(kernel, in_specs=specs or [VMEM] * len(operands), out_spec...]
  transfers between devices with their start and end apart: 15 -> 15, of which waited for: 8 -> 8; matrix products, arithmetic and copies ran while one was open for 0% -> 0% of each run, Pallas kernels for 13% -> 11%
where the time goes in v6:
time: 47.9 us; the launch traced here: 47.8 us
  waiting for transfers between devices  23.3 us (49%)
  starting transfers between devices  16.7 us (35%)
  Pallas kernels  7.68 us (16%)
    ppermute x8, starting transfers between devices, on_device(): later = [lax.ppermute(p, 'head', ring) for p in pieces]  15 us
    ppermute x8, waiting for transfers between devices, on_device(): later = [lax.ppermute(p, 'head', ring) for p in pieces]  14.8 us
    pallas_call x13, Pallas kernels, call(): pl.pallas_call(kernel, in_specs=specs or [VMEM] * len(operands), out_spec...  7.68 us
    ppermute x6, waiting for transfers between devices, on_device(): bring = lambda x: [lax.ppermute(x, 'ctx', pairs) for pairs in links]  7.12 us
    ppermute x6, starting transfers between devices, on_device(): bring = lambda x: [lax.ppermute(x, 'ctx', pairs) for pairs in links]  1.54 us
    ppermute x1, waiting for transfers between devices, on_device(): lax.ppermute(piece, 'ctx', [(target, source) for source, target in pairs])  1.38 us
  transfers between devices with their start and end apart: 15, of which 8 were waited for; matrix products, arithmetic and copies ran while one was open for 0% of the time, Pallas kernels for 11%

profile of v6, /device:TPU:0, one launch (start us, length us, event | category | flops | bytes accessed | tf_op | source)
XLA Modules:
  0.0 47.8 jit_solution(16247632865376712121)
XLA Ops:
  1.0 1.4 %fetch.1 = (bf16[256,1024]{1,0:T(8,128)(2,1)S(1)}, bf16[256,1024]{1,0:T(8,128)(2,1)S(1)}, bf16[256,1024]{1,0:T(8,128)(2,1)S(1)}, s32[1,256]{1,0:T(1,128)S(1)}) custom-call(bf16[256,1024]{1,0:T(8,128)(2,1)} %refs_0_.2, bf16[256,1024]{1,0:T(8,128)(2,1)} %refs_1_.1, bf16[256,1024]{1,0:T(8,128)(2,1)} %refs_2_.5, s32[1,256]{1,0:T(1,128)} %bitcast.2), custom_call_target="tpu_custom_call" | custom-call | bytes 3147776 | tf_op jit(solution)/shard_map/fetch/pallas_call | solution.py:60
  2.4 0.6 %collective-permute-done.refs_1_ = s32[1,256]{1,0:T(1,128)S(1)} collective-permute-done((s32[1,256]{1,0:T(1,128)}, s32[1,256]{1,0:T(1,128)S(1)}, u32[]{:S(2)}, u32[]{:S(2)}) %collective-permute-start) | collective-permute-done | bytes 1056 | tf_op jit(solution)/shard_map/ppermute | solution.py:278
  3.0 0.9 %encoder_attend.3.refs_1_ = bf16[256,512]{1,0:T(8,128)(2,1)S(1)} custom-call(s32[1,256]{1,0:T(1,128)S(1)} %get-tuple-element.15.refs_0_.own_ref, s32[1,256]{1,0:T(1,128)S(1)} %collective-permute-done.refs_1_, bf16[256,1024]{1,0:T(8,128)(2,1)S(1)} %get-tuple-element.16.refs_2_, bf16[256,1024]{1,0:T(8,128)(2,1)S(1)} %get-tuple-element.17.refs_3_, ...), custom_call_target="tpu_custom_call" | custom-call | flops 268435456 | bytes 2885632 | tf_op jit(solution)/shard_map/encoder_attend/pallas_call | solution.py:60
  3.8 4.0 %collective-permute-start.7 = (bf16[256,512]{1,0:T(8,128)(2,1)S(1)}, bf16[256,512]{1,0:T(8,128)(2,1)S(1)}, u32[]{:S(2)}, u32[]{:S(2)}) collective-permute-start(bf16[256,512]{1,0:T(8,128)(2,1)S(1)} %encoder_attend.3.refs_1_), channel_id=1, source_target_pairs={{0,2},{2,3},{3,1},{1,0},{4,6},{6,7},{7,5},{5,4},{8,10},{10,11},{11... | collective-permute-start | bytes 786440 | tf_op jit(solution)/shard_map/ppermute | solution.py:322
  7.9 0.9 %encoder_attend.2.refs_0_ = bf16[256,512]{1,0:T(8,128)(2,1)S(1)} custom-call(s32[1,256]{1,0:T(1,128)S(1)} %get-tuple-element.15.refs_0_.own_ref, s32[1,256]{1,0:T(1,128)S(1)} %collective-permute-done.refs_1_, bf16[256,1024]{1,0:T(8,128)(2,1)S(1)} %get-tuple-element.16.refs_2_, bf16[256,1024]{1,0:T(8,128)(2,1)S(1)} %get-tuple-element.17.refs_3_, ...), custom_call_target="tpu_custom_call" | custom-call | flops 268435456 | bytes 2885632 | tf_op jit(solution)/shard_map/encoder_attend/pallas_call | solution.py:60
  8.7 1.6 %collective-permute-start.3 = (bf16[256,512]{1,0:T(8,128)(2,1)S(1)}, bf16[256,512]{1,0:T(8,128)(2,1)S(1)}, u32[]{:S(2)}, u32[]{:S(2)}) collective-permute-start(bf16[256,512]{1,0:T(8,128)(2,1)S(1)} %encoder_attend.2.refs_0_), channel_id=1, source_target_pairs={{0,2},{2,3},{3,1},{1,0},{4,6},{6,7},{7,5},{5,4},{8,10},{10,11},{11... | collective-permute-start | bytes 786440 | tf_op jit(solution)/shard_map/ppermute | solution.py:322
  10.3 4.2 %collective-permute-done.7.refs_1_ = bf16[256,512]{1,0:T(8,128)(2,1)S(1)} collective-permute-done((bf16[256,512]{1,0:T(8,128)(2,1)S(1)}, bf16[256,512]{1,0:T(8,128)(2,1)S(1)}, u32[]{:S(2)}, u32[]{:S(2)}) %collective-permute-start.7) | collective-permute-done | bytes 262176 | tf_op jit(solution)/shard_map/ppermute | solution.py:322
  14.5 3.4 %collective-permute-start.8 = (bf16[256,512]{1,0:T(8,128)(2,1)S(1)}, bf16[256,512]{1,0:T(8,128)(2,1)S(1)}, u32[]{:S(2)}, u32[]{:S(2)}) collective-permute-start(bf16[256,512]{1,0:T(8,128)(2,1)S(1)} %collective-permute-done.7.refs_1_), channel_id=1, source_target_pairs={{0,2},{2,3},{3,1},{1,0},{4,6},{6,7},{7,5},{5,4},{8,10},{10,11},{11... | collective-permute-start | bytes 786440 | tf_op jit(solution)/shard_map/ppermute | solution.py:322
  18.6 6.5 %collective-permute-done.13 = bf16[64,512]{1,0:T(8,128)(2,1)S(1)} collective-permute-done((bf16[64,512]{1,0:T(8,128)(2,1)S(1)}, bf16[64,512]{1,0:T(8,128)(2,1)S(1)}, u32[]{:S(2)}, u32[]{:S(2)}) %collective-permute-start.13) | collective-permute-done | bytes 65568 | tf_op jit(solution)/shard_map/ppermute | solution.py:278
  25.2 0.7 %collective-permute-start.4 = (bf16[256,512]{1,0:T(8,128)(2,1)S(1)}, bf16[256,512]{1,0:T(8,128)(2,1)S(1)}, u32[]{:S(2)}, u32[]{:S(2)}) collective-permute-start(bf16[256,512]{1,0:T(8,128)(2,1)S(1)} %collective-permute-done.3.refs_0_), channel_id=1, source_target_pairs={{0,2},{2,3},{3,1},{1,0},{4,6},{6,7},{7,5},{5,4},{8,10},{10,11},{11... | collective-permute-start | bytes 786440 | tf_op jit(solution)/shard_map/ppermute | solution.py:322
  25.9 2.5 %collective-permute-start.9 = (bf16[256,256]{1,0:T(8,128)(2,1)S(1)}, bf16[256,256]{1,0:T(8,128)(2,1)S(1)}, u32[]{:S(2)}, u32[]{:S(2)}) collective-permute-start(bf16[256,256]{1,0:T(8,128)(2,1)S(1)} %get-tuple-element.21), channel_id=1, source_target_pairs={{0,2},{2,3},{3,1},{1,0},{4,6},{6,7},{7,5},{5,4},{8,10},{10,11},{11... | collective-permute-start | bytes 393224 | tf_op jit(solution)/shard_map/ppermute | solution.py:322
  28.4 6.0 %collective-permute-done.4.source.refs_0_ = bf16[256,512]{1,0:T(8,128)(2,1)S(1)} collective-permute-done((bf16[256,512]{1,0:T(8,128)(2,1)S(1)}, bf16[256,512]{1,0:T(8,128)(2,1)S(1)}, u32[]{:S(2)}, u32[]{:S(2)}) %collective-permute-start.4) | collective-permute-done | bytes 262176 | tf_op jit(solution)/shard_map/ppermute | solution.py:322
  34.4 1.6 %collective-permute-start.5 = (bf16[256,256]{1,0:T(8,128)(2,1)S(1)}, bf16[256,256]{1,0:T(8,128)(2,1)S(1)}, u32[]{:S(2)}, u32[]{:S(2)}) collective-permute-start(bf16[256,256]{1,0:T(8,128)(2,1)S(1)} %get-tuple-element.19), channel_id=1, source_target_pairs={{0,2},{2,3},{3,1},{1,0},{4,6},{6,7},{7,5},{5,4},{8,10},{10,11},{11... | collective-permute-start | bytes 393224 | tf_op jit(solution)/shard_map/ppermute | solution.py:322
  36.4 0.9 %collective-permute-start.12 = (bf16[256,256]{1,0:T(8,128)(2,1)S(1)}, bf16[256,256]{1,0:T(8,128)(2,1)S(1)}, u32[]{:S(2)}, u32[]{:S(2)}) collective-permute-start(bf16[256,256]{1,0:T(8,128)(2,1)S(1)} %get-tuple-element.22), channel_id=1, source_target_pairs={{0,2},{2,3},{3,1},{1,0},{4,6},{6,7},{7,5},{5,4},{8,10},{10,11},{11... | collective-permute-start | bytes 393224 | tf_op jit(solution)/shard_map/ppermute | solution.py:322
  37.3 0.7 %project.4.refs_6_ = f32[256,1024]{1,0:T(8,128)S(1)} custom-call(bf16[256,512]{1,0:T(8,128)(2,1)S(1)} %encoder_attend.2.refs_0_, bf16[256,512]{1,0:T(8,128)(2,1)S(1)} %encoder_attend.3.refs_1_, bf16[2048,512]{1,0:T(8,128)(2,1)S(1)} %copy-done, bf16[2048,512]{1,0:T(8,128)(2,1)S(1)} %collective-permute-done.10.refs_3_.refs_4_.refs_1_, ...), custom_call_target="tpu_custom_call" | custom-call | flops 536870912 | bytes 9961472 | tf_op jit(solution)/shard_map/project/pallas_call | solution.py:60
  38.0 0.7 %project.5.refs_6_ = f32[256,1024]{1,0:T(8,128)S(1)} custom-call(bf16[256,512]{1,0:T(8,128)(2,1)S(1)} %collective-permute-done.3.refs_0_, bf16[256,512]{1,0:T(8,128)(2,1)S(1)} %collective-permute-done.7.refs_1_, bf16[2048,512]{1,0:T(8,128)(2,1)S(1)} %copy-done, bf16[2048,512]{1,0:T(8,128)(2,1)S(1)} %collective-permute-done.10.refs_3_.refs_4_.refs_1_, ...), custom_call_target="tpu_custom_call" | custom-call | flops 536870912 | bytes 11010048 | tf_op jit(solution)/shard_map/project/pallas_call | solution.py:60
  38.8 0.8 %project.6.refs_7_ = f32[256,1024]{1,0:T(8,128)S(1)} custom-call(bf16[256,512]{1,0:T(8,128)(2,1)S(1)} %collective-permute-done.4.source.refs_0_, bf16[256,512]{1,0:T(8,128)(2,1)S(1)} %collective-permute-done.8.source.refs_1_, bf16[2048,512]{1,0:T(8,128)(2,1)S(1)} %copy-done, bf16[2048,512]{1,0:T(8,128)(2,1)S(1)} %collective-permute-done.10.refs_3_.refs_4_.refs_1_, ...), custom_call_target="tpu_custom_call" | custom-call | flops 536870912 | bytes 11010048 | tf_op jit(solution)/shard_map/project/pallas_call | solution.py:60
  39.6 1.3 %collective-permute-done.5.refs_0_ = bf16[256,256]{1,0:T(8,128)(2,1)S(1)} collective-permute-done((bf16[256,256]{1,0:T(8,128)(2,1)S(1)}, bf16[256,256]{1,0:T(8,128)(2,1)S(1)}, u32[]{:S(2)}, u32[]{:S(2)}) %collective-permute-start.5) | collective-permute-done | bytes 131104 | tf_op jit(solution)/shard_map/ppermute | solution.py:322
  40.9 2.5 %collective-permute-done.6.refs_1_ = bf16[256,256]{1,0:T(8,128)(2,1)S(1)} collective-permute-done((bf16[256,256]{1,0:T(8,128)(2,1)S(1)}, bf16[256,256]{1,0:T(8,128)(2,1)S(1)}, u32[]{:S(2)}, u32[]{:S(2)}) %collective-permute-start.6) | collective-permute-done | bytes 131104 | tf_op jit(solution)/shard_map/ppermute | solution.py:322
  43.4 0.6 %project.7.acc_ref = f32[256,1024]{1,0:T(8,128)S(1)} custom-call(bf16[256,256]{1,0:T(8,128)(2,1)S(1)} %collective-permute-done.5.refs_0_, bf16[256,256]{1,0:T(8,128)(2,1)S(1)} %collective-permute-done.6.refs_1_, bf16[256,256]{1,0:T(8,128)(2,1)S(1)} %collective-permute-done.9.refs_2_, bf16[2048,512]{1,0:T(8,128)(2,1)S(1)} %copy-done, ...), custom_call_target="tpu_custom_call" | custom-call | flops 402653184 | bytes 10878976 | tf_op jit(solution)/shard_map/project/pallas_call | solution.py:60
  44.0 0.8 %collective-permute-done.12.e_ref = bf16[256,256]{1,0:T(8,128)(2,1)S(1)} collective-permute-done((bf16[256,256]{1,0:T(8,128)(2,1)S(1)}, bf16[256,256]{1,0:T(8,128)(2,1)S(1)}, u32[]{:S(2)}, u32[]{:S(2)}) %collective-permute-start.12) | collective-permute-done | bytes 131104 | tf_op jit(solution)/shard_map/ppermute | solution.py:322
  44.8 0.7 %cross_attend.1 = (f32[64,640]{1,0:T(8,128)S(1)}, f32[64,640]{1,0:T(8,128)S(1)}) custom-call(f32[256,1024]{1,0:T(8,128)S(1)} %project.7.acc_ref, bf16[256,256]{1,0:T(8,128)(2,1)S(1)} %collective-permute-done.12.e_ref, bf16[256,1024]{1,0:T(8,128)(2,1)S(1)} %pick.1.map_ref, bf16[128,512]{1,0:T(8,128)(2,1)S(1)} %pad_maximum_fusion.tgt_ref, ...), custom_call_target="tpu_custom_call" | custom-call | flops 134217728 | bytes 2293760 | tf_op jit(solution)/shard_map/cross_attend/pallas_call | solution.py:60
  45.6 1.4 %collective-permute-done.14.refs_1_ = f32[64,640]{1,0:T(8,128)S(1)} collective-permute-done((f32[64,640]{1,0:T(8,128)S(1)}, f32[64,640]{1,0:T(8,128)S(1)}, u32[]{:S(2)}, u32[]{:S(2)}) %collective-permute-start.14) | collective-permute-done | bytes 163872 | tf_op jit(solution)/shard_map/ppermute | solution.py:332
  47.0 0.8 %combine.1 = bf16[64,512]{1,0:T(8,128)(2,1)} custom-call(f32[64,640]{1,0:T(8,128)S(1)} %get-tuple-element.23.refs_0_, f32[64,640]{1,0:T(8,128)S(1)} %collective-permute-done.14.refs_1_), custom_call_target="tpu_custom_call" | custom-call | bytes 393216 | tf_op jit(solution)/shard_map/combine/pallas_call | solution.py:60
  (26 shorter events, 2.2 us)
Async XLA Ops:
  0.0 3.0 %collective-permute-start.1 = (bf16[256,1024]{1,0:T(8,128)(2,1)}, bf16[256,1024]{1,0:T(8,128)(2,1)S(1)}, u32[]{:S(2)}, u32[]{:S(2)}) collective-permute-start(bf16[256,1024]{1,0:T(8,128)(2,1)} %refs_1_.1), channel_id=1, source_target_pairs={{0,4},{4,0},{1,5},{5,1},{2,6},{6,2},{3,7},{7,3},{8,12},{12,8},{9,1... | collective-permute-start | bytes 1572872 | tf_op jit(solution)/shard_map/ppermute | solution.py:278
  0.5 2.5 %collective-permute-start.2 = (bf16[256,1024]{1,0:T(8,128)(2,1)}, bf16[256,1024]{1,0:T(8,128)(2,1)S(1)}, u32[]{:S(2)}, u32[]{:S(2)}) collective-permute-start(bf16[256,1024]{1,0:T(8,128)(2,1)} %refs_2_.5), channel_id=1, source_target_pairs={{0,4},{4,0},{1,5},{5,1},{2,6},{6,2},{3,7},{7,3},{8,12},{12,8},{9,1... | collective-permute-start | bytes 1572872 | tf_op jit(solution)/shard_map/ppermute | solution.py:278
  0.5 2.4 %collective-permute-start = (s32[1,256]{1,0:T(1,128)}, s32[1,256]{1,0:T(1,128)S(1)}, u32[]{:S(2)}, u32[]{:S(2)}) collective-permute-start(s32[1,256]{1,0:T(1,128)} %bitcast.1), channel_id=1, source_target_pairs={{0,4},{4,0},{1,5},{5,1},{2,6},{6,2},{3,7},{7,3},{8,12},{12,8},{9,1... | collective-permute-start | bytes 3080 | tf_op jit(solution)/shard_map/ppermute | solution.py:278
  3.0 15.0 %copy-start.1 = (bf16[2048,512]{1,0:T(8,128)(2,1)S(1)}, bf16[2048,512]{1,0:T(8,128)(2,1)}, u32[]{:S(2)}) copy-start(bf16[2048,512]{1,0:T(8,128)(2,1)} %refs_2_.9) | copy-start | bytes 6291460
  3.8 14.1 %copy-start = (bf16[2048,512]{1,0:T(8,128)(2,1)S(1)}, bf16[2048,512]{1,0:T(8,128)(2,1)}, u32[]{:S(2)}) copy-start(bf16[2048,512]{1,0:T(8,128)(2,1)} %refs_0_.3) | copy-start | bytes 6291460
  3.8 14.6 %copy-start.2 = (bf16[64,512]{1,0:T(8,128)(2,1)S(1)}, bf16[64,512]{1,0:T(8,128)(2,1)}, u32[]{:S(2)}) copy-start(bf16[64,512]{1,0:T(8,128)(2,1)} %param.13) | copy-start | bytes 196612
  3.8 10.7 %collective-permute-start.7 = (bf16[256,512]{1,0:T(8,128)(2,1)S(1)}, bf16[256,512]{1,0:T(8,128)(2,1)S(1)}, u32[]{:S(2)}, u32[]{:S(2)}) collective-permute-start(bf16[256,512]{1,0:T(8,128)(2,1)S(1)} %encoder_attend.3.refs_1_), channel_id=1, source_target_pairs={{0,2},{2,3},{3,1},{1,0},{4,6},{6,7},{7,5},{5,4},{8,10},{10,11},{11... | collective-permute-start | bytes 786440 | tf_op jit(solution)/shard_map/ppermute | solution.py:322
  8.7 16.5 %collective-permute-start.3 = (bf16[256,512]{1,0:T(8,128)(2,1)S(1)}, bf16[256,512]{1,0:T(8,128)(2,1)S(1)}, u32[]{:S(2)}, u32[]{:S(2)}) collective-permute-start(bf16[256,512]{1,0:T(8,128)(2,1)S(1)} %encoder_attend.2.refs_0_), channel_id=1, source_target_pairs={{0,2},{2,3},{3,1},{1,0},{4,6},{6,7},{7,5},{5,4},{8,10},{10,11},{11... | collective-permute-start | bytes 786440 | tf_op jit(solution)/shard_map/ppermute | solution.py:322
  14.5 11.4 %collective-permute-start.8 = (bf16[256,512]{1,0:T(8,128)(2,1)S(1)}, bf16[256,512]{1,0:T(8,128)(2,1)S(1)}, u32[]{:S(2)}, u32[]{:S(2)}) collective-permute-start(bf16[256,512]{1,0:T(8,128)(2,1)S(1)} %collective-permute-done.7.refs_1_), channel_id=1, source_target_pairs={{0,2},{2,3},{3,1},{1,0},{4,6},{6,7},{7,5},{5,4},{8,10},{10,11},{11... | collective-permute-start | bytes 786440 | tf_op jit(solution)/shard_map/ppermute | solution.py:322
  17.9 18.5 %collective-permute-start.10 = (bf16[2048,512]{1,0:T(8,128)(2,1)S(1)}, bf16[2048,512]{1,0:T(8,128)(2,1)S(1)}, u32[]{:S(2)}, u32[]{:S(2)}) collective-permute-start(bf16[2048,512]{1,0:T(8,128)(2,1)S(1)} %copy-done), channel_id=1, source_target_pairs={{0,4},{4,0},{1,5},{5,1},{2,6},{6,2},{3,7},{7,3},{8,12},{12,8},{9,1... | collective-permute-start | bytes 6291464 | tf_op jit(solution)/shard_map/ppermute | solution.py:278
  17.9 19.3 %collective-permute-start.11 = (bf16[2048,512]{1,0:T(8,128)(2,1)S(1)}, bf16[2048,512]{1,0:T(8,128)(2,1)S(1)}, u32[]{:S(2)}, u32[]{:S(2)}) collective-permute-start(bf16[2048,512]{1,0:T(8,128)(2,1)S(1)} %copy-done.1), channel_id=1, source_target_pairs={{0,4},{4,0},{1,5},{5,1},{2,6},{6,2},{3,7},{7,3},{8,12},{12,8},{9,1... | collective-permute-start | bytes 6291464 | tf_op jit(solution)/shard_map/ppermute | solution.py:278
  18.4 6.7 %collective-permute-start.13 = (bf16[64,512]{1,0:T(8,128)(2,1)S(1)}, bf16[64,512]{1,0:T(8,128)(2,1)S(1)}, u32[]{:S(2)}, u32[]{:S(2)}) collective-permute-start(bf16[64,512]{1,0:T(8,128)(2,1)S(1)} %copy-done.2), channel_id=1, source_target_pairs={{0,4},{4,0},{1,5},{5,1},{2,6},{6,2},{3,7},{7,3},{8,12},{12,8},{9,1... | collective-permute-start | bytes 196616 | tf_op jit(solution)/shard_map/ppermute | solution.py:278
  25.2 9.2 %collective-permute-start.4 = (bf16[256,512]{1,0:T(8,128)(2,1)S(1)}, bf16[256,512]{1,0:T(8,128)(2,1)S(1)}, u32[]{:S(2)}, u32[]{:S(2)}) collective-permute-start(bf16[256,512]{1,0:T(8,128)(2,1)S(1)} %collective-permute-done.3.refs_0_), channel_id=1, source_target_pairs={{0,2},{2,3},{3,1},{1,0},{4,6},{6,7},{7,5},{5,4},{8,10},{10,11},{11... | collective-permute-start | bytes 786440 | tf_op jit(solution)/shard_map/ppermute | solution.py:322
  25.9 13.6 %collective-permute-start.9 = (bf16[256,256]{1,0:T(8,128)(2,1)S(1)}, bf16[256,256]{1,0:T(8,128)(2,1)S(1)}, u32[]{:S(2)}, u32[]{:S(2)}) collective-permute-start(bf16[256,256]{1,0:T(8,128)(2,1)S(1)} %get-tuple-element.21), channel_id=1, source_target_pairs={{0,2},{2,3},{3,1},{1,0},{4,6},{6,7},{7,5},{5,4},{8,10},{10,11},{11... | collective-permute-start | bytes 393224 | tf_op jit(solution)/shard_map/ppermute | solution.py:322
  34.4 6.5 %collective-permute-start.5 = (bf16[256,256]{1,0:T(8,128)(2,1)S(1)}, bf16[256,256]{1,0:T(8,128)(2,1)S(1)}, u32[]{:S(2)}, u32[]{:S(2)}) collective-permute-start(bf16[256,256]{1,0:T(8,128)(2,1)S(1)} %get-tuple-element.19), channel_id=1, source_target_pairs={{0,2},{2,3},{3,1},{1,0},{4,6},{6,7},{7,5},{5,4},{8,10},{10,11},{11... | collective-permute-start | bytes 393224 | tf_op jit(solution)/shard_map/ppermute | solution.py:322
  36.0 7.4 %collective-permute-start.6 = (bf16[256,256]{1,0:T(8,128)(2,1)S(1)}, bf16[256,256]{1,0:T(8,128)(2,1)S(1)}, u32[]{:S(2)}, u32[]{:S(2)}) collective-permute-start(bf16[256,256]{1,0:T(8,128)(2,1)S(1)} %get-tuple-element.20), channel_id=1, source_target_pairs={{0,2},{2,3},{3,1},{1,0},{4,6},{6,7},{7,5},{5,4},{8,10},{10,11},{11... | collective-permute-start | bytes 393224 | tf_op jit(solution)/shard_map/ppermute | solution.py:322
  36.4 8.4 %collective-permute-start.12 = (bf16[256,256]{1,0:T(8,128)(2,1)S(1)}, bf16[256,256]{1,0:T(8,128)(2,1)S(1)}, u32[]{:S(2)}, u32[]{:S(2)}) collective-permute-start(bf16[256,256]{1,0:T(8,128)(2,1)S(1)} %get-tuple-element.22), channel_id=1, source_target_pairs={{0,2},{2,3},{3,1},{1,0},{4,6},{6,7},{7,5},{5,4},{8,10},{10,11},{11... | collective-permute-start | bytes 393224 | tf_op jit(solution)/shard_map/ppermute | solution.py:322
  45.5 1.5 %collective-permute-start.14 = (f32[64,640]{1,0:T(8,128)S(1)}, f32[64,640]{1,0:T(8,128)S(1)}, u32[]{:S(2)}, u32[]{:S(2)}) collective-permute-start(f32[64,640]{1,0:T(8,128)S(1)} %get-tuple-element.24), channel_id=1, source_target_pairs={{4,0},{0,4},{5,1},{1,5},{6,2},{2,6},{7,3},{3,7},{12,8},{8,12},{13,... | collective-permute-start | bytes 491528 | tf_op jit(solution)/shard_map/ppermute | solution.py:332

commit v7 on v6

--- a/solution.py
+++ b/solution.py
@@ -118,27 +118,6 @@
     )[0]
 
 
-def target_mask_kernel(step, own_ref, *refs):
-    marks, out_ref, down_ref = refs[:-2], refs[-2], refs[-1]
-    own = own_ref[...]
-    count = out_ref.shape[0] // len(marks)
-    for i, mark_ref in enumerate(marks):
-        down_ref[...] = down_lanes(mark_ref[...])
-        down = down_ref[pl.ds(0, count, stride=step), :]
-        out_ref[i * count : (i + 1) * count, :] = same_mark(down, own).astype(F32)
-
-
-def target_mask(marks, all_marks, tgt_rows):
-    rows = marks.shape[1]
-    return call(
-        functools.partial(target_mask_kernel, rows // tgt_rows),
-        "target_mask",
-        [((tgt_rows * len(all_marks), rows), F32)],
-        [marks, *all_marks],
-        scratch=[pltpu.VMEM((rows, LANES), jnp.int32)],
-    )[0]
-
-
 def add_products(acc_of, store, e_refs, place, key_shards, value_shards):
     shard, row = place
     depth = e_refs[0].shape[1]
@@ -193,30 +172,42 @@
     )[0]
 
 
-def pick_kernel(shards, place, *refs):
-    maps, out_ref = refs[:-1], refs[-1]
+def prepare_kernel(shards, parts, step, place, *refs):
+    maps, targets, marks = refs[: 2 * shards], refs[2 * shards : 2 * shards + parts], refs[2 * shards + parts : -4]
+    map_ref, tgt_ref, mask_ref, down_ref = refs[-4:]
     shard, row = place()
-    depth, width = out_ref.shape[0], out_ref.shape[1] // 2
+    depth, width = map_ref.shape[0], map_ref.shape[1] // 2
     at = pl.ds(pl.multiple_of(row, depth), depth)
 
     def copy(i):
-        out_ref[:, :width] = maps[i][at, :]
-        out_ref[:, width:] = maps[shards + i][at, :]
+        map_ref[:, :width] = maps[i][at, :]
+        map_ref[:, width:] = maps[shards + i][at, :]
 
     if shards == 1:
         copy(0)
     else:
         for i in range(shards):
             pl.when(shard == i)(functools.partial(copy, i))
-
-
-def pick(place, depth, key_shards, value_shards):
-    return call(
-        functools.partial(pick_kernel, len(key_shards), place),
-        "pick",
-        [((depth, 2 * key_shards[0].shape[1]), BF16)],
-        [*key_shards, *value_shards],
-    )[0]
+    own = marks[0][...]
+    count = targets[0].shape[0]
+    for i, (target_ref, mark_ref) in enumerate(zip(targets, marks)):
+        part = slice(i * count, (i + 1) * count)
+        tgt_ref[part, :] = target_ref[...]
+        down_ref[...] = down_lanes(mark_ref[...])
+        down = down_ref[pl.ds(0, count, stride=step), :]
+        mask_ref[part, :] = same_mark(down, own).astype(F32)
+
+
+def prepare(place, depth, key_shards, value_shards, targets, marks):
+    rows, count, width = marks[0].shape[1], targets[0].shape[0], targets[0].shape[1]
+    total = count * len(targets)
+    return call(
+        functools.partial(prepare_kernel, len(key_shards), len(targets), rows // count, place),
+        "prepare",
+        [((depth, 2 * width), BF16), ((total, width), BF16), ((total, rows), F32)],
+        [*key_shards, *value_shards, *targets, *marks],
+        scratch=[pltpu.VMEM((rows, LANES), jnp.int32)],
+    )
 
 
 def cross_kernel(acc_ref, e_ref, map_ref, tgt_ref, mask_ref, *outs):
@@ -285,8 +276,6 @@
         key_shards, value_shards = [key_map, *bring(key_map)], [value_map, *bring(value_map)]
     else:
         key_shards, value_shards = ([lax.all_gather(x, "ctx", axis=0, tiled=True)] for x in (key_map, value_map))
-    targets = jnp.concatenate([tgt_query, *near_targets], 0)
-    mask = target_mask(marks, [marks, *near_marks], tgt_rows)
 
     chunks = 2
     heads = features // HEAD_DIM // chunks
@@ -324,7 +313,14 @@
         held = later
     acc = project(acc, held[:-1], functools.partial(place, last, 0), key_shards, value_shards)
     depth = held[-1].shape[1]
-    last_maps = pick(functools.partial(place, last, features - depth), depth, key_shards, value_shards)
+    last_maps, targets, mask = prepare(
+        functools.partial(place, last, features - depth),
+        depth,
+        key_shards,
+        value_shards,
+        [tgt_query, *near_targets],
+        [marks, *near_marks],
+    )
     parts = cross_attend(acc, held[-1], last_maps, targets, mask, 1 + len(links))
 
     combined = [parts[0]]

time: 47.9 us -> 45.5 us (0.950)
  waiting for transfers between devices: 23.3 us -> 14.8 us
  starting transfers between devices: 16.7 us -> 22.8 us
    ppermute x6, waiting for transfers between devices: 7.12 us -> 0.6 us  [on_device(): bring = lambda x: [lax.ppermute(x, 'ctx', pairs) for pairs in links]]
    ppermute x8, starting transfers between devices: 15 us -> 21.2 us  [on_device(): later = [lax.ppermute(p, 'head', ring) for p in pieces]]
    ppermute x8, waiting for transfers between devices: 14.8 us -> 12.8 us  [on_device(): later = [lax.ppermute(p, 'head', ring) for p in pieces]]
    pallas_call x13 -> x12, Pallas kernels: 7.68 us -> 7.66 us  [call(): pl.pallas_call(kernel, in_specs=specs or [VMEM] * len(operands), out_spec...]
  transfers between devices with their start and end apart: 15 -> 15, of which waited for: 8 -> 8; matrix products, arithmetic and copies ran while one was open for 0% -> 0% of each run, Pallas kernels for 11% -> 12%
where the time goes in v7:
time: 45.5 us; the launch traced here: 45.4 us
  starting transfers between devices  22.8 us (50%)
  waiting for transfers between devices  14.8 us (33%)
  Pallas kernels  7.66 us (17%)
    ppermute x8, starting transfers between devices, on_device(): later = [lax.ppermute(p, 'head', ring) for p in pieces]  21.2 us
    ppermute x8, waiting for transfers between devices, on_device(): later = [lax.ppermute(p, 'head', ring) for p in pieces]  12.8 us
    pallas_call x12, Pallas kernels, call(): pl.pallas_call(kernel, in_specs=specs or [VMEM] * len(operands), out_spec...  7.66 us
    ppermute x6, starting transfers between devices, on_device(): bring = lambda x: [lax.ppermute(x, 'ctx', pairs) for pairs in links]  1.54 us
    ppermute x1, waiting for transfers between devices, on_device(): lax.ppermute(piece, 'ctx', [(target, source) for source, target in pairs])  1.38 us
  transfers between devices with their start and end apart: 15, of which 8 were waited for; matrix products, arithmetic and copies ran while one was open for 0% of the time, Pallas kernels for 12%

profile of v7, /device:TPU:0, one launch (start us, length us, event | category | flops | bytes accessed | tf_op | source)
XLA Modules:
  0.0 45.4 jit_solution(8770628728890543575)
XLA Ops:
  1.0 1.4 %fetch.1 = (bf16[256,1024]{1,0:T(8,128)(2,1)S(1)}, bf16[256,1024]{1,0:T(8,128)(2,1)S(1)}, bf16[256,1024]{1,0:T(8,128)(2,1)S(1)}, s32[1,256]{1,0:T(1,128)S(1)}) custom-call(bf16[256,1024]{1,0:T(8,128)(2,1)} %refs_0_.2, bf16[256,1024]{1,0:T(8,128)(2,1)} %refs_1_.1, bf16[256,1024]{1,0:T(8,128)(2,1)} %refs_2_.5, s32[1,256]{1,0:T(1,128)} %bitcast.2), custom_call_target="tpu_custom_call" | custom-call | bytes 3147776 | tf_op jit(solution)/shard_map/fetch/pallas_call | solution.py:60
  3.0 0.9 %encoder_attend.3.refs_1_ = bf16[256,512]{1,0:T(8,128)(2,1)S(1)} custom-call(s32[1,256]{1,0:T(1,128)S(1)} %get-tuple-element.18.refs_0_.refs_6_, s32[1,256]{1,0:T(1,128)S(1)} %collective-permute-done.refs_1_.refs_7_, bf16[256,1024]{1,0:T(8,128)(2,1)S(1)} %get-tuple-element.19.refs_2_, bf16[256,1024]{1,0:T(8,128)(2,1)S(1)} %get-tuple-element.20.refs_3_, ...), custom_call_target="tpu_custom_call" | custom-call | flops 268435456 | bytes 2885632 | tf_op jit(solution)/shard_map/encoder_attend/pallas_call | solution.py:60
  3.8 4.0 %collective-permute-start.7 = (bf16[256,512]{1,0:T(8,128)(2,1)S(1)}, bf16[256,512]{1,0:T(8,128)(2,1)S(1)}, u32[]{:S(2)}, u32[]{:S(2)}) collective-permute-start(bf16[256,512]{1,0:T(8,128)(2,1)S(1)} %encoder_attend.3.refs_1_), channel_id=1, source_target_pairs={{0,2},{2,3},{3,1},{1,0},{4,6},{6,7},{7,5},{5,4},{8,10},{10,11},{11... | collective-permute-start | bytes 786440 | tf_op jit(solution)/shard_map/ppermute | solution.py:311
  7.9 0.9 %encoder_attend.2.refs_0_ = bf16[256,512]{1,0:T(8,128)(2,1)S(1)} custom-call(s32[1,256]{1,0:T(1,128)S(1)} %get-tuple-element.18.refs_0_.refs_6_, s32[1,256]{1,0:T(1,128)S(1)} %collective-permute-done.refs_1_.refs_7_, bf16[256,1024]{1,0:T(8,128)(2,1)S(1)} %get-tuple-element.19.refs_2_, bf16[256,1024]{1,0:T(8,128)(2,1)S(1)} %get-tuple-element.20.refs_3_, ...), custom_call_target="tpu_custom_call" | custom-call | flops 268435456 | bytes 2885632 | tf_op jit(solution)/shard_map/encoder_attend/pallas_call | solution.py:60
  8.7 1.6 %collective-permute-start.3 = (bf16[256,512]{1,0:T(8,128)(2,1)S(1)}, bf16[256,512]{1,0:T(8,128)(2,1)S(1)}, u32[]{:S(2)}, u32[]{:S(2)}) collective-permute-start(bf16[256,512]{1,0:T(8,128)(2,1)S(1)} %encoder_attend.2.refs_0_), channel_id=1, source_target_pairs={{0,2},{2,3},{3,1},{1,0},{4,6},{6,7},{7,5},{5,4},{8,10},{10,11},{11... | collective-permute-start | bytes 786440 | tf_op jit(solution)/shard_map/ppermute | solution.py:311
  10.3 4.2 %collective-permute-done.7.refs_1_ = bf16[256,512]{1,0:T(8,128)(2,1)S(1)} collective-permute-done((bf16[256,512]{1,0:T(8,128)(2,1)S(1)}, bf16[256,512]{1,0:T(8,128)(2,1)S(1)}, u32[]{:S(2)}, u32[]{:S(2)}) %collective-permute-start.7) | collective-permute-done | bytes 262176 | tf_op jit(solution)/shard_map/ppermute | solution.py:311
  14.5 3.4 %collective-permute-start.8 = (bf16[256,512]{1,0:T(8,128)(2,1)S(1)}, bf16[256,512]{1,0:T(8,128)(2,1)S(1)}, u32[]{:S(2)}, u32[]{:S(2)}) collective-permute-start(bf16[256,512]{1,0:T(8,128)(2,1)S(1)} %collective-permute-done.7.refs_1_), channel_id=1, source_target_pairs={{0,2},{2,3},{3,1},{1,0},{4,6},{6,7},{7,5},{5,4},{8,10},{10,11},{11... | collective-permute-start | bytes 786440 | tf_op jit(solution)/shard_map/ppermute | solution.py:311
  18.5 1.6 %collective-permute-done.3.refs_0_ = bf16[256,512]{1,0:T(8,128)(2,1)S(1)} collective-permute-done((bf16[256,512]{1,0:T(8,128)(2,1)S(1)}, bf16[256,512]{1,0:T(8,128)(2,1)S(1)}, u32[]{:S(2)}, u32[]{:S(2)}) %collective-permute-start.3) | collective-permute-done | bytes 262176 | tf_op jit(solution)/shard_map/ppermute | solution.py:311
  20.1 3.4 %collective-permute-start.4 = (bf16[256,512]{1,0:T(8,128)(2,1)S(1)}, bf16[256,512]{1,0:T(8,128)(2,1)S(1)}, u32[]{:S(2)}, u32[]{:S(2)}) collective-permute-start(bf16[256,512]{1,0:T(8,128)(2,1)S(1)} %collective-permute-done.3.refs_0_), channel_id=1, source_target_pairs={{0,2},{2,3},{3,1},{1,0},{4,6},{6,7},{7,5},{5,4},{8,10},{10,11},{11... | collective-permute-start | bytes 786440 | tf_op jit(solution)/shard_map/ppermute | solution.py:311
  23.5 2.2 %collective-permute-done.8.source.refs_1_ = bf16[256,512]{1,0:T(8,128)(2,1)S(1)} collective-permute-done((bf16[256,512]{1,0:T(8,128)(2,1)S(1)}, bf16[256,512]{1,0:T(8,128)(2,1)S(1)}, u32[]{:S(2)}, u32[]{:S(2)}) %collective-permute-start.8) | collective-permute-done | bytes 262176 | tf_op jit(solution)/shard_map/ppermute | solution.py:311
  25.8 3.4 %collective-permute-start.9 = (bf16[256,256]{1,0:T(8,128)(2,1)S(1)}, bf16[256,256]{1,0:T(8,128)(2,1)S(1)}, u32[]{:S(2)}, u32[]{:S(2)}) collective-permute-start(bf16[256,256]{1,0:T(8,128)(2,1)S(1)} %get-tuple-element.24), channel_id=1, source_target_pairs={{0,2},{2,3},{3,1},{1,0},{4,6},{6,7},{7,5},{5,4},{8,10},{10,11},{11... | collective-permute-start | bytes 393224 | tf_op jit(solution)/shard_map/ppermute | solution.py:311
  29.2 2.2 %collective-permute-done.4.source.refs_0_ = bf16[256,512]{1,0:T(8,128)(2,1)S(1)} collective-permute-done((bf16[256,512]{1,0:T(8,128)(2,1)S(1)}, bf16[256,512]{1,0:T(8,128)(2,1)S(1)}, u32[]{:S(2)}, u32[]{:S(2)}) %collective-permute-start.4) | collective-permute-done | bytes 262176 | tf_op jit(solution)/shard_map/ppermute | solution.py:311
  31.4 3.4 %collective-permute-start.5 = (bf16[256,256]{1,0:T(8,128)(2,1)S(1)}, bf16[256,256]{1,0:T(8,128)(2,1)S(1)}, u32[]{:S(2)}, u32[]{:S(2)}) collective-permute-start(bf16[256,256]{1,0:T(8,128)(2,1)S(1)} %get-tuple-element.22), channel_id=1, source_target_pairs={{0,2},{2,3},{3,1},{1,0},{4,6},{6,7},{7,5},{5,4},{8,10},{10,11},{11... | collective-permute-start | bytes 393224 | tf_op jit(solution)/shard_map/ppermute | solution.py:311
  34.8 0.7 %collective-permute-start.6 = (bf16[256,256]{1,0:T(8,128)(2,1)S(1)}, bf16[256,256]{1,0:T(8,128)(2,1)S(1)}, u32[]{:S(2)}, u32[]{:S(2)}) collective-permute-start(bf16[256,256]{1,0:T(8,128)(2,1)S(1)} %get-tuple-element.23), channel_id=1, source_target_pairs={{0,2},{2,3},{3,1},{1,0},{4,6},{6,7},{7,5},{5,4},{8,10},{10,11},{11... | collective-permute-start | bytes 393224 | tf_op jit(solution)/shard_map/ppermute | solution.py:311
  35.5 1.2 %collective-permute-start.12 = (bf16[256,256]{1,0:T(8,128)(2,1)S(1)}, bf16[256,256]{1,0:T(8,128)(2,1)S(1)}, u32[]{:S(2)}, u32[]{:S(2)}) collective-permute-start(bf16[256,256]{1,0:T(8,128)(2,1)S(1)} %get-tuple-element.25), channel_id=1, source_target_pairs={{0,2},{2,3},{3,1},{1,0},{4,6},{6,7},{7,5},{5,4},{8,10},{10,11},{11... | collective-permute-start | bytes 393224 | tf_op jit(solution)/shard_map/ppermute | solution.py:311
  36.9 0.7 %project.4.refs_6_ = f32[256,1024]{1,0:T(8,128)S(1)} custom-call(bf16[256,512]{1,0:T(8,128)(2,1)S(1)} %encoder_attend.2.refs_0_, bf16[256,512]{1,0:T(8,128)(2,1)S(1)} %encoder_attend.3.refs_1_, bf16[2048,512]{1,0:T(8,128)(2,1)S(1)} %copy-done, bf16[2048,512]{1,0:T(8,128)(2,1)S(1)} %collective-permute-done.10.refs_3_.refs_4_.refs_1_, ...), custom_call_target="tpu_custom_call" | custom-call | flops 536870912 | bytes 9961472 | tf_op jit(solution)/shard_map/project/pallas_call | solution.py:60
  37.7 0.7 %project.5.refs_6_ = f32[256,1024]{1,0:T(8,128)S(1)} custom-call(bf16[256,512]{1,0:T(8,128)(2,1)S(1)} %collective-permute-done.3.refs_0_, bf16[256,512]{1,0:T(8,128)(2,1)S(1)} %collective-permute-done.7.refs_1_, bf16[2048,512]{1,0:T(8,128)(2,1)S(1)} %copy-done, bf16[2048,512]{1,0:T(8,128)(2,1)S(1)} %collective-permute-done.10.refs_3_.refs_4_.refs_1_, ...), custom_call_target="tpu_custom_call" | custom-call | flops 536870912 | bytes 11010048 | tf_op jit(solution)/shard_map/project/pallas_call | solution.py:60
  38.5 0.7 %project.6.refs_7_ = f32[256,1024]{1,0:T(8,128)S(1)} custom-call(bf16[256,512]{1,0:T(8,128)(2,1)S(1)} %collective-permute-done.4.source.refs_0_, bf16[256,512]{1,0:T(8,128)(2,1)S(1)} %collective-permute-done.8.source.refs_1_, bf16[2048,512]{1,0:T(8,128)(2,1)S(1)} %copy-done, bf16[2048,512]{1,0:T(8,128)(2,1)S(1)} %collective-permute-done.10.refs_3_.refs_4_.refs_1_, ...), custom_call_target="tpu_custom_call" | custom-call | flops 536870912 | bytes 11010048 | tf_op jit(solution)/shard_map/project/pallas_call | solution.py:60
  39.2 1.8 %collective-permute-done.6.refs_1_ = bf16[256,256]{1,0:T(8,128)(2,1)S(1)} collective-permute-done((bf16[256,256]{1,0:T(8,128)(2,1)S(1)}, bf16[256,256]{1,0:T(8,128)(2,1)S(1)}, u32[]{:S(2)}, u32[]{:S(2)}) %collective-permute-start.6) | collective-permute-done | bytes 131104 | tf_op jit(solution)/shard_map/ppermute | solution.py:311
  41.0 0.6 %project.7.acc_ref = f32[256,1024]{1,0:T(8,128)S(1)} custom-call(bf16[256,256]{1,0:T(8,128)(2,1)S(1)} %collective-permute-done.5.refs_0_, bf16[256,256]{1,0:T(8,128)(2,1)S(1)} %collective-permute-done.6.refs_1_, bf16[256,256]{1,0:T(8,128)(2,1)S(1)} %collective-permute-done.9.refs_2_, bf16[2048,512]{1,0:T(8,128)(2,1)S(1)} %copy-done, ...), custom_call_target="tpu_custom_call" | custom-call | flops 402653184 | bytes 10878976 | tf_op jit(solution)/shard_map/project/pallas_call | solution.py:60
  41.6 0.8 %collective-permute-done.12.e_ref = bf16[256,256]{1,0:T(8,128)(2,1)S(1)} collective-permute-done((bf16[256,256]{1,0:T(8,128)(2,1)S(1)}, bf16[256,256]{1,0:T(8,128)(2,1)S(1)}, u32[]{:S(2)}, u32[]{:S(2)}) %collective-permute-start.12) | collective-permute-done | bytes 131104 | tf_op jit(solution)/shard_map/ppermute | solution.py:311
  42.4 0.7 %cross_attend.1 = (f32[64,640]{1,0:T(8,128)S(1)}, f32[64,640]{1,0:T(8,128)S(1)}) custom-call(f32[256,1024]{1,0:T(8,128)S(1)} %project.7.acc_ref, bf16[256,256]{1,0:T(8,128)(2,1)S(1)} %collective-permute-done.12.e_ref, bf16[256,1024]{1,0:T(8,128)(2,1)S(1)} %get-tuple-element.26.map_ref, bf16[128,512]{1,0:T(8,128)(2,1)S(1)} %get-tuple-element.27.tgt_ref, ...), custom_call_target="tpu_custom_call" | custom-call | flops 134217728 | bytes 2293760 | tf_op jit(solution)/shard_map/cross_attend/pallas_call | solution.py:60
  43.1 1.4 %collective-permute-done.14.refs_1_ = f32[64,640]{1,0:T(8,128)S(1)} collective-permute-done((f32[64,640]{1,0:T(8,128)S(1)}, f32[64,640]{1,0:T(8,128)S(1)}, u32[]{:S(2)}, u32[]{:S(2)}) %collective-permute-start.14) | collective-permute-done | bytes 163872 | tf_op jit(solution)/shard_map/ppermute | solution.py:328
  44.5 0.8 %combine.1 = bf16[64,512]{1,0:T(8,128)(2,1)} custom-call(f32[64,640]{1,0:T(8,128)S(1)} %get-tuple-element.29.refs_0_, f32[64,640]{1,0:T(8,128)S(1)} %collective-permute-done.14.refs_1_), custom_call_target="tpu_custom_call" | custom-call | bytes 393216 | tf_op jit(solution)/shard_map/combine/pallas_call | solution.py:60
  (24 shorter events, 2.4 us)
Async XLA Ops:
  0.0 3.0 %collective-permute-start.1 = (bf16[256,1024]{1,0:T(8,128)(2,1)}, bf16[256,1024]{1,0:T(8,128)(2,1)S(1)}, u32[]{:S(2)}, u32[]{:S(2)}) collective-permute-start(bf16[256,1024]{1,0:T(8,128)(2,1)} %refs_1_.1), channel_id=1, source_target_pairs={{0,4},{4,0},{1,5},{5,1},{2,6},{6,2},{3,7},{7,3},{8,12},{12,8},{9,1... | collective-permute-start | bytes 1572872 | tf_op jit(solution)/shard_map/ppermute | solution.py:269
  0.5 2.5 %collective-permute-start.2 = (bf16[256,1024]{1,0:T(8,128)(2,1)}, bf16[256,1024]{1,0:T(8,128)(2,1)S(1)}, u32[]{:S(2)}, u32[]{:S(2)}) collective-permute-start(bf16[256,1024]{1,0:T(8,128)(2,1)} %refs_2_.5), channel_id=1, source_target_pairs={{0,4},{4,0},{1,5},{5,1},{2,6},{6,2},{3,7},{7,3},{8,12},{12,8},{9,1... | collective-permute-start | bytes 1572872 | tf_op jit(solution)/shard_map/ppermute | solution.py:269
  0.5 2.4 %collective-permute-start = (s32[1,256]{1,0:T(1,128)}, s32[1,256]{1,0:T(1,128)S(1)}, u32[]{:S(2)}, u32[]{:S(2)}) collective-permute-start(s32[1,256]{1,0:T(1,128)} %bitcast.1), channel_id=1, source_target_pairs={{0,4},{4,0},{1,5},{5,1},{2,6},{6,2},{3,7},{7,3},{8,12},{12,8},{9,1... | collective-permute-start | bytes 3080 | tf_op jit(solution)/shard_map/ppermute | solution.py:269
  3.0 15.0 %copy-start.1 = (bf16[2048,512]{1,0:T(8,128)(2,1)S(1)}, bf16[2048,512]{1,0:T(8,128)(2,1)}, u32[]{:S(2)}) copy-start(bf16[2048,512]{1,0:T(8,128)(2,1)} %refs_2_.9) | copy-start | bytes 6291460
  3.8 14.1 %copy-start = (bf16[2048,512]{1,0:T(8,128)(2,1)S(1)}, bf16[2048,512]{1,0:T(8,128)(2,1)}, u32[]{:S(2)}) copy-start(bf16[2048,512]{1,0:T(8,128)(2,1)} %refs_0_.3) | copy-start | bytes 6291460
  3.8 14.6 %copy-start.2 = (bf16[64,512]{1,0:T(8,128)(2,1)S(1)}, bf16[64,512]{1,0:T(8,128)(2,1)}, u32[]{:S(2)}) copy-start(bf16[64,512]{1,0:T(8,128)(2,1)} %refs_4_.7) | copy-start | bytes 196612
  3.8 10.7 %collective-permute-start.7 = (bf16[256,512]{1,0:T(8,128)(2,1)S(1)}, bf16[256,512]{1,0:T(8,128)(2,1)S(1)}, u32[]{:S(2)}, u32[]{:S(2)}) collective-permute-start(bf16[256,512]{1,0:T(8,128)(2,1)S(1)} %encoder_attend.3.refs_1_), channel_id=1, source_target_pairs={{0,2},{2,3},{3,1},{1,0},{4,6},{6,7},{7,5},{5,4},{8,10},{10,11},{11... | collective-permute-start | bytes 786440 | tf_op jit(solution)/shard_map/ppermute | solution.py:311
  8.7 11.4 %collective-permute-start.3 = (bf16[256,512]{1,0:T(8,128)(2,1)S(1)}, bf16[256,512]{1,0:T(8,128)(2,1)S(1)}, u32[]{:S(2)}, u32[]{:S(2)}) collective-permute-start(bf16[256,512]{1,0:T(8,128)(2,1)S(1)} %encoder_attend.2.refs_0_), channel_id=1, source_target_pairs={{0,2},{2,3},{3,1},{1,0},{4,6},{6,7},{7,5},{5,4},{8,10},{10,11},{11... | collective-permute-start | bytes 786440 | tf_op jit(solution)/shard_map/ppermute | solution.py:311
  14.5 11.2 %collective-permute-start.8 = (bf16[256,512]{1,0:T(8,128)(2,1)S(1)}, bf16[256,512]{1,0:T(8,128)(2,1)S(1)}, u32[]{:S(2)}, u32[]{:S(2)}) collective-permute-start(bf16[256,512]{1,0:T(8,128)(2,1)S(1)} %collective-permute-done.7.refs_1_), channel_id=1, source_target_pairs={{0,2},{2,3},{3,1},{1,0},{4,6},{6,7},{7,5},{5,4},{8,10},{10,11},{11... | collective-permute-start | bytes 786440 | tf_op jit(solution)/shard_map/ppermute | solution.py:311
  17.9 17.6 %collective-permute-start.10 = (bf16[2048,512]{1,0:T(8,128)(2,1)S(1)}, bf16[2048,512]{1,0:T(8,128)(2,1)S(1)}, u32[]{:S(2)}, u32[]{:S(2)}) collective-permute-start(bf16[2048,512]{1,0:T(8,128)(2,1)S(1)} %copy-done), channel_id=1, source_target_pairs={{0,4},{4,0},{1,5},{5,1},{2,6},{6,2},{3,7},{7,3},{8,12},{12,8},{9,1... | collective-permute-start | bytes 6291464 | tf_op jit(solution)/shard_map/ppermute | solution.py:269
  17.9 18.8 %collective-permute-start.11 = (bf16[2048,512]{1,0:T(8,128)(2,1)S(1)}, bf16[2048,512]{1,0:T(8,128)(2,1)S(1)}, u32[]{:S(2)}, u32[]{:S(2)}) collective-permute-start(bf16[2048,512]{1,0:T(8,128)(2,1)S(1)} %copy-done.1), channel_id=1, source_target_pairs={{0,4},{4,0},{1,5},{5,1},{2,6},{6,2},{3,7},{7,3},{8,12},{12,8},{9,1... | collective-permute-start | bytes 6291464 | tf_op jit(solution)/shard_map/ppermute | solution.py:269
  18.4 16.4 %collective-permute-start.13 = (bf16[64,512]{1,0:T(8,128)(2,1)S(1)}, bf16[64,512]{1,0:T(8,128)(2,1)S(1)}, u32[]{:S(2)}, u32[]{:S(2)}) collective-permute-start(bf16[64,512]{1,0:T(8,128)(2,1)S(1)} %copy-done.2), channel_id=1, source_target_pairs={{0,4},{4,0},{1,5},{5,1},{2,6},{6,2},{3,7},{7,3},{8,12},{12,8},{9,1... | collective-permute-start | bytes 196616 | tf_op jit(solution)/shard_map/ppermute | solution.py:269
  20.1 11.2 %collective-permute-start.4 = (bf16[256,512]{1,0:T(8,128)(2,1)S(1)}, bf16[256,512]{1,0:T(8,128)(2,1)S(1)}, u32[]{:S(2)}, u32[]{:S(2)}) collective-permute-start(bf16[256,512]{1,0:T(8,128)(2,1)S(1)} %collective-permute-done.3.refs_0_), channel_id=1, source_target_pairs={{0,2},{2,3},{3,1},{1,0},{4,6},{6,7},{7,5},{5,4},{8,10},{10,11},{11... | collective-permute-start | bytes 786440 | tf_op jit(solution)/shard_map/ppermute | solution.py:311
  25.8 13.4 %collective-permute-start.9 = (bf16[256,256]{1,0:T(8,128)(2,1)S(1)}, bf16[256,256]{1,0:T(8,128)(2,1)S(1)}, u32[]{:S(2)}, u32[]{:S(2)}) collective-permute-start(bf16[256,256]{1,0:T(8,128)(2,1)S(1)} %get-tuple-element.24), channel_id=1, source_target_pairs={{0,2},{2,3},{3,1},{1,0},{4,6},{6,7},{7,5},{5,4},{8,10},{10,11},{11... | collective-permute-start | bytes 393224 | tf_op jit(solution)/shard_map/ppermute | solution.py:311
  31.4 7.8 %collective-permute-start.5 = (bf16[256,256]{1,0:T(8,128)(2,1)S(1)}, bf16[256,256]{1,0:T(8,128)(2,1)S(1)}, u32[]{:S(2)}, u32[]{:S(2)}) collective-permute-start(bf16[256,256]{1,0:T(8,128)(2,1)S(1)} %get-tuple-element.22), channel_id=1, source_target_pairs={{0,2},{2,3},{3,1},{1,0},{4,6},{6,7},{7,5},{5,4},{8,10},{10,11},{11... | collective-permute-start | bytes 393224 | tf_op jit(solution)/shard_map/ppermute | solution.py:311
  34.8 6.1 %collective-permute-start.6 = (bf16[256,256]{1,0:T(8,128)(2,1)S(1)}, bf16[256,256]{1,0:T(8,128)(2,1)S(1)}, u32[]{:S(2)}, u32[]{:S(2)}) collective-permute-start(bf16[256,256]{1,0:T(8,128)(2,1)S(1)} %get-tuple-element.23), channel_id=1, source_target_pairs={{0,2},{2,3},{3,1},{1,0},{4,6},{6,7},{7,5},{5,4},{8,10},{10,11},{11... | collective-permute-start | bytes 393224 | tf_op jit(solution)/shard_map/ppermute | solution.py:311
  35.5 6.9 %collective-permute-start.12 = (bf16[256,256]{1,0:T(8,128)(2,1)S(1)}, bf16[256,256]{1,0:T(8,128)(2,1)S(1)}, u32[]{:S(2)}, u32[]{:S(2)}) collective-permute-start(bf16[256,256]{1,0:T(8,128)(2,1)S(1)} %get-tuple-element.25), channel_id=1, source_target_pairs={{0,2},{2,3},{3,1},{1,0},{4,6},{6,7},{7,5},{5,4},{8,10},{10,11},{11... | collective-permute-start | bytes 393224 | tf_op jit(solution)/shard_map/ppermute | solution.py:311
  43.1 1.5 %collective-permute-start.14 = (f32[64,640]{1,0:T(8,128)S(1)}, f32[64,640]{1,0:T(8,128)S(1)}, u32[]{:S(2)}, u32[]{:S(2)}) collective-permute-start(f32[64,640]{1,0:T(8,128)S(1)} %get-tuple-element.30), channel_id=1, source_target_pairs={{4,0},{0,4},{5,1},{1,5},{6,2},{2,6},{7,3},{3,7},{12,8},{8,12},{13,... | collective-permute-start | bytes 491528 | tf_op jit(solution)/shard_map/ppermute | solution.py:328

commit v8 on v7

--- a/solution.py
+++ b/solution.py
@@ -120,8 +120,8 @@
 
 def add_products(acc_of, store, e_refs, place, key_shards, value_shards):
     shard, row = place
-    depth = e_refs[0].shape[1]
-    at = pl.ds(pl.multiple_of(row, depth), depth * len(e_refs))
+    widths = [r.shape[1] for r in e_refs]
+    at = pl.ds(pl.multiple_of(row, min(widths)), sum(widths))
     chunks = jnp.concatenate([r[...] for r in e_refs], axis=1)
 
     def add(i):
@@ -135,15 +135,16 @@
             pl.when(shard == i)(functools.partial(add, i))
 
 
-def halve_kernel(source, *outs):
+def split_kernel(source, *outs):
     width = outs[0].shape[1]
     for i, out in enumerate(outs):
         out[...] = source[:, i * width : (i + 1) * width]
 
 
-def halve(chunk):
+def split(chunk, parts, weight):
     rows, width = chunk.shape
-    return call(halve_kernel, "halve", [((rows, width // 2), chunk.dtype)] * 2, [chunk], flops=10**10)
+    outs = [((rows, width // parts), chunk.dtype)] * parts
+    return call(split_kernel, "split", outs, [chunk], flops=weight * 10**10)
 
 
 def project_kernel(chunks, shards, has_acc, place, *refs):
@@ -160,15 +161,14 @@
 
 
 def project(acc, chunks, place, key_shards, value_shards):
-    rows, depth = chunks[0].shape
-    width = key_shards[0].shape[1]
+    rows, width = chunks[0].shape[0], key_shards[0].shape[1]
     operands = [*chunks, *key_shards, *value_shards] + ([] if acc is None else [acc])
     return call(
         functools.partial(project_kernel, len(chunks), len(key_shards), acc is not None, place),
         "project",
         [((rows, 2 * width), F32)],
         operands,
-        flops=4 * rows * depth * width * len(chunks),
+        flops=4 * width * sum(x.size for x in chunks),
     )[0]
 
 
@@ -277,11 +277,10 @@
     else:
         key_shards, value_shards = ([lax.all_gather(x, "ctx", axis=0, tiled=True)] for x in (key_map, value_map))
 
-    chunks = 2
-    heads = features // HEAD_DIM // chunks
+    heads = features // HEAD_DIM
     held = [
-        encoder_attend(query, [own_key, *keys], [own_value, *values], [marks, *near_marks], j * heads, heads)
-        for j in range(chunks)
+        encoder_attend(query, [own_key, *keys], [own_value, *values], [marks, *near_marks], first, count)
+        for first, count in ((0, 1), (1, heads - 1))
     ]
 
     order = ring_order(n_head)
@@ -305,9 +304,9 @@
     acc, last = None, n_head - 1
     for turn in range(last):
         if turn == last - 1:
-            pieces = [p for h in held for p in halve(h)]
+            pieces = [*split(held[0], 2, 2), *split(held[1], heads - 1, 1)]
         else:
-            pieces = held
+            pieces = held if turn == 0 else [*split(held[0], 1, 1), *held[1:]]
         later = [lax.ppermute(p, "head", ring) for p in pieces]
         acc = project(acc, held, functools.partial(place, turn, 0), key_shards, value_shards)
         held = later

time: 45.5 us -> 46.1 us (1.013)
  waiting for transfers between devices: 14.8 us -> 17.7 us
  starting transfers between devices: 22.8 us -> 20.3 us
    ppermute x8 -> x9, waiting for transfers between devices: 12.8 us -> 15.8 us  [on_device(): later = [lax.ppermute(p, 'head', ring) for p in pieces]]
    ppermute x8 -> x9, starting transfers between devices: 21.2 us -> 18.7 us  [on_device(): later = [lax.ppermute(p, 'head', ring) for p in pieces]]
    pallas_call x12 -> x13, Pallas kernels: 7.66 us -> 7.72 us  [call(): pl.pallas_call(kernel, in_specs=specs or [VMEM] * len(operands), out_spec...]
  transfers between devices with their start and end apart: 15 -> 16, of which waited for: 8 -> 8; matrix products, arithmetic and copies ran while one was open for 0% -> 0% of each run, Pallas kernels for 12% -> 12%
where the time goes in v8:
time: 46.1 us; the launch traced here: 45.9 us
  starting transfers between devices  20.3 us (44%)
  waiting for transfers between devices  17.7 us (38%)
  Pallas kernels  7.72 us (17%)
    ppermute x9, starting transfers between devices, on_device(): later = [lax.ppermute(p, 'head', ring) for p in pieces]  18.7 us
    ppermute x9, waiting for transfers between devices, on_device(): later = [lax.ppermute(p, 'head', ring) for p in pieces]  15.8 us
    pallas_call x13, Pallas kernels, call(): pl.pallas_call(kernel, in_specs=specs or [VMEM] * len(operands), out_spec...  7.72 us
    ppermute x6, starting transfers between devices, on_device(): bring = lambda x: [lax.ppermute(x, 'ctx', pairs) for pairs in links]  1.54 us
    ppermute x1, waiting for transfers between devices, on_device(): lax.ppermute(piece, 'ctx', [(target, source) for source, target in pairs])  1.38 us
  transfers between devices with their start and end apart: 16, of which 8 were waited for; matrix products, arithmetic and copies ran while one was open for 0% of the time, Pallas kernels for 12%

profile of v8, /device:TPU:0, one launch (start us, length us, event | category | flops | bytes accessed | tf_op | source)
XLA Modules:
  0.0 45.9 jit_solution(4422722550938252049)
XLA Ops:
  1.0 1.4 %fetch.1 = (bf16[256,1024]{1,0:T(8,128)(2,1)S(1)}, bf16[256,1024]{1,0:T(8,128)(2,1)S(1)}, bf16[256,1024]{1,0:T(8,128)(2,1)S(1)}, s32[1,256]{1,0:T(1,128)S(1)}) custom-call(bf16[256,1024]{1,0:T(8,128)(2,1)} %refs_0_.2, bf16[256,1024]{1,0:T(8,128)(2,1)} %refs_1_.1, bf16[256,1024]{1,0:T(8,128)(2,1)} %refs_2_.5, s32[1,256]{1,0:T(1,128)} %bitcast.2), custom_call_target="tpu_custom_call" | custom-call | bytes 3147776 | tf_op jit(solution)/shard_map/fetch/pallas_call | solution.py:60
  3.0 0.7 %encoder_attend.2.refs_0_ = bf16[256,256]{1,0:T(8,128)(2,1)S(1)} custom-call(s32[1,256]{1,0:T(1,128)S(1)} %get-tuple-element.19.refs_0_.refs_6_, s32[1,256]{1,0:T(1,128)S(1)} %collective-permute-done.refs_1_.refs_7_, bf16[256,1024]{1,0:T(8,128)(2,1)S(1)} %get-tuple-element.20.refs_2_, bf16[256,1024]{1,0:T(8,128)(2,1)S(1)} %get-tuple-element.21.refs_3_, ...), custom_call_target="tpu_custom_call" | custom-call | flops 134217728 | bytes 2754560 | tf_op jit(solution)/shard_map/encoder_attend/pallas_call | solution.py:60
  3.6 4.0 %collective-permute-start.3 = (bf16[256,256]{1,0:T(8,128)(2,1)S(1)}, bf16[256,256]{1,0:T(8,128)(2,1)S(1)}, u32[]{:S(2)}, u32[]{:S(2)}) collective-permute-start(bf16[256,256]{1,0:T(8,128)(2,1)S(1)} %encoder_attend.2.refs_0_), channel_id=1, source_target_pairs={{0,2},{2,3},{3,1},{1,0},{4,6},{6,7},{7,5},{5,4},{8,10},{10,11},{11... | collective-permute-start | bytes 393224 | tf_op jit(solution)/shard_map/ppermute | solution.py:310
  7.7 1.1 %encoder_attend.3.refs_1_ = bf16[256,768]{1,0:T(8,128)(2,1)S(1)} custom-call(s32[1,256]{1,0:T(1,128)S(1)} %get-tuple-element.19.refs_0_.refs_6_, s32[1,256]{1,0:T(1,128)S(1)} %collective-permute-done.refs_1_.refs_7_, bf16[256,1024]{1,0:T(8,128)(2,1)S(1)} %get-tuple-element.20.refs_2_, bf16[256,1024]{1,0:T(8,128)(2,1)S(1)} %get-tuple-element.21.refs_3_, ...), custom_call_target="tpu_custom_call" | custom-call | flops 402653184 | bytes 3016704 | tf_op jit(solution)/shard_map/encoder_attend/pallas_call | solution.py:60
  8.8 1.6 %collective-permute-start.7 = (bf16[256,768]{1,0:T(8,128)(2,1)S(1)}, bf16[256,768]{1,0:T(8,128)(2,1)S(1)}, u32[]{:S(2)}, u32[]{:S(2)}) collective-permute-start(bf16[256,768]{1,0:T(8,128)(2,1)S(1)} %encoder_attend.3.refs_1_), channel_id=1, source_target_pairs={{0,2},{2,3},{3,1},{1,0},{4,6},{6,7},{7,5},{5,4},{8,10},{10,11},{11... | collective-permute-start | bytes 1179656 | tf_op jit(solution)/shard_map/ppermute | solution.py:310
  10.4 0.6 %collective-permute-done.3.source.refs_0_ = bf16[256,256]{1,0:T(8,128)(2,1)S(1)} collective-permute-done((bf16[256,256]{1,0:T(8,128)(2,1)S(1)}, bf16[256,256]{1,0:T(8,128)(2,1)S(1)}, u32[]{:S(2)}, u32[]{:S(2)}) %collective-permute-start.3) | collective-permute-done | bytes 131104 | tf_op jit(solution)/shard_map/ppermute | solution.py:310
  11.0 3.4 %collective-permute-start.4 = (bf16[256,256]{1,0:T(8,128)(2,1)S(1)}, bf16[256,256]{1,0:T(8,128)(2,1)S(1)}, u32[]{:S(2)}, u32[]{:S(2)}) collective-permute-start(bf16[256,256]{1,0:T(8,128)(2,1)S(1)} %split.3), channel_id=1, source_target_pairs={{0,2},{2,3},{3,1},{1,0},{4,6},{6,7},{7,5},{5,4},{8,10},{10,11},{11... | collective-permute-start | bytes 393224 | tf_op jit(solution)/shard_map/ppermute | solution.py:310
  15.0 5.8 %collective-permute-done.7.refs_1_ = bf16[256,768]{1,0:T(8,128)(2,1)S(1)} collective-permute-done((bf16[256,768]{1,0:T(8,128)(2,1)S(1)}, bf16[256,768]{1,0:T(8,128)(2,1)S(1)}, u32[]{:S(2)}, u32[]{:S(2)}) %collective-permute-start.7) | collective-permute-done | bytes 393248 | tf_op jit(solution)/shard_map/ppermute | solution.py:310
  20.8 2.5 %collective-permute-start.8 = (bf16[256,768]{1,0:T(8,128)(2,1)S(1)}, bf16[256,768]{1,0:T(8,128)(2,1)S(1)}, u32[]{:S(2)}, u32[]{:S(2)}) collective-permute-start(bf16[256,768]{1,0:T(8,128)(2,1)S(1)} %collective-permute-done.7.refs_1_), channel_id=1, source_target_pairs={{0,2},{2,3},{3,1},{1,0},{4,6},{6,7},{7,5},{5,4},{8,10},{10,11},{11... | collective-permute-start | bytes 1179656 | tf_op jit(solution)/shard_map/ppermute | solution.py:310
  23.3 2.1 %collective-permute-start.5 = (bf16[256,128]{1,0:T(8,128)(2,1)S(1)}, bf16[256,128]{1,0:T(8,128)(2,1)S(1)}, u32[]{:S(2)}, u32[]{:S(2)}) collective-permute-start(bf16[256,128]{1,0:T(8,128)(2,1)S(1)} %get-tuple-element.23), channel_id=1, source_target_pairs={{0,2},{2,3},{3,1},{1,0},{4,6},{6,7},{7,5},{5,4},{8,10},{10,11},{11... | collective-permute-start | bytes 196616 | tf_op jit(solution)/shard_map/ppermute | solution.py:310
  25.4 6.2 %collective-permute-done.8.source.refs_1_ = bf16[256,768]{1,0:T(8,128)(2,1)S(1)} collective-permute-done((bf16[256,768]{1,0:T(8,128)(2,1)S(1)}, bf16[256,768]{1,0:T(8,128)(2,1)S(1)}, u32[]{:S(2)}, u32[]{:S(2)}) %collective-permute-start.8) | collective-permute-done | bytes 393248 | tf_op jit(solution)/shard_map/ppermute | solution.py:310
  31.6 2.9 %collective-permute-start.6 = (bf16[256,128]{1,0:T(8,128)(2,1)S(1)}, bf16[256,128]{1,0:T(8,128)(2,1)S(1)}, u32[]{:S(2)}, u32[]{:S(2)}) collective-permute-start(bf16[256,128]{1,0:T(8,128)(2,1)S(1)} %get-tuple-element.24), channel_id=1, source_target_pairs={{0,2},{2,3},{3,1},{1,0},{4,6},{6,7},{7,5},{5,4},{8,10},{10,11},{11... | collective-permute-start | bytes 196616 | tf_op jit(solution)/shard_map/ppermute | solution.py:310
  34.5 0.7 %collective-permute-start.10 = (bf16[256,256]{1,0:T(8,128)(2,1)S(1)}, bf16[256,256]{1,0:T(8,128)(2,1)S(1)}, u32[]{:S(2)}, u32[]{:S(2)}) collective-permute-start(bf16[256,256]{1,0:T(8,128)(2,1)S(1)} %get-tuple-element.26), channel_id=1, source_target_pairs={{0,2},{2,3},{3,1},{1,0},{4,6},{6,7},{7,5},{5,4},{8,10},{10,11},{11... | collective-permute-start | bytes 393224 | tf_op jit(solution)/shard_map/ppermute | solution.py:310
  35.2 1.2 %collective-permute-start.9 = (bf16[256,256]{1,0:T(8,128)(2,1)S(1)}, bf16[256,256]{1,0:T(8,128)(2,1)S(1)}, u32[]{:S(2)}, u32[]{:S(2)}) collective-permute-start(bf16[256,256]{1,0:T(8,128)(2,1)S(1)} %get-tuple-element.25), channel_id=1, source_target_pairs={{0,2},{2,3},{3,1},{1,0},{4,6},{6,7},{7,5},{5,4},{8,10},{10,11},{11... | collective-permute-start | bytes 393224 | tf_op jit(solution)/shard_map/ppermute | solution.py:310
  36.5 0.7 %project.4.refs_6_ = f32[256,1024]{1,0:T(8,128)S(1)} custom-call(bf16[256,256]{1,0:T(8,128)(2,1)S(1)} %encoder_attend.2.refs_0_, bf16[256,768]{1,0:T(8,128)(2,1)S(1)} %encoder_attend.3.refs_1_, bf16[2048,512]{1,0:T(8,128)(2,1)S(1)} %copy-done, bf16[2048,512]{1,0:T(8,128)(2,1)S(1)} %collective-permute-done.11.refs_3_.refs_5_.refs_1_, ...), custom_call_target="tpu_custom_call" | custom-call | flops 536870912 | bytes 9961472 | tf_op jit(solution)/shard_map/project/pallas_call | solution.py:60
  37.5 0.7 %project.5.refs_6_ = f32[256,1024]{1,0:T(8,128)S(1)} custom-call(bf16[256,256]{1,0:T(8,128)(2,1)S(1)} %collective-permute-done.3.source.refs_0_, bf16[256,768]{1,0:T(8,128)(2,1)S(1)} %collective-permute-done.7.refs_1_, bf16[2048,512]{1,0:T(8,128)(2,1)S(1)} %copy-done, bf16[2048,512]{1,0:T(8,128)(2,1)S(1)} %collective-permute-done.11.refs_3_.refs_5_.refs_1_, ...), custom_call_target="tpu_custom_call" | custom-call | flops 536870912 | bytes 11010048 | tf_op jit(solution)/shard_map/project/pallas_call | solution.py:60
  38.4 0.7 %project.6.refs_8_ = f32[256,1024]{1,0:T(8,128)S(1)} custom-call(bf16[256,256]{1,0:T(8,128)(2,1)S(1)} %collective-permute-done.4.source.refs_0_, bf16[256,768]{1,0:T(8,128)(2,1)S(1)} %collective-permute-done.8.source.refs_1_, bf16[2048,512]{1,0:T(8,128)(2,1)S(1)} %copy-done, bf16[2048,512]{1,0:T(8,128)(2,1)S(1)} %collective-permute-done.11.refs_3_.refs_5_.refs_1_, ...), custom_call_target="tpu_custom_call" | custom-call | flops 536870912 | bytes 11010048 | tf_op jit(solution)/shard_map/project/pallas_call | solution.py:60
  39.2 1.0 %collective-permute-done.10.refs_3_ = bf16[256,256]{1,0:T(8,128)(2,1)S(1)} collective-permute-done((bf16[256,256]{1,0:T(8,128)(2,1)S(1)}, bf16[256,256]{1,0:T(8,128)(2,1)S(1)}, u32[]{:S(2)}, u32[]{:S(2)}) %collective-permute-start.10) | collective-permute-done | bytes 131104 | tf_op jit(solution)/shard_map/ppermute | solution.py:310
  40.2 1.4 %collective-permute-done.9.refs_2_ = bf16[256,256]{1,0:T(8,128)(2,1)S(1)} collective-permute-done((bf16[256,256]{1,0:T(8,128)(2,1)S(1)}, bf16[256,256]{1,0:T(8,128)(2,1)S(1)}, u32[]{:S(2)}, u32[]{:S(2)}) %collective-permute-start.9) | collective-permute-done | bytes 131104 | tf_op jit(solution)/shard_map/ppermute | solution.py:310
  41.6 0.6 %project.7.acc_ref = f32[256,1024]{1,0:T(8,128)S(1)} custom-call(bf16[256,128]{1,0:T(8,128)(2,1)S(1)} %collective-permute-done.5.refs_0_, bf16[256,128]{1,0:T(8,128)(2,1)S(1)} %collective-permute-done.6.refs_1_, bf16[256,256]{1,0:T(8,128)(2,1)S(1)} %collective-permute-done.9.refs_2_, bf16[256,256]{1,0:T(8,128)(2,1)S(1)} %collective-permute-done.10.refs_3_, ...), custom_call_target="tpu_custom_call" | custom-call | flops 402653184 | bytes 10878976 | tf_op jit(solution)/shard_map/project/pallas_call | solution.py:60
  42.2 0.8 %collective-permute-done.13.e_ref = bf16[256,256]{1,0:T(8,128)(2,1)S(1)} collective-permute-done((bf16[256,256]{1,0:T(8,128)(2,1)S(1)}, bf16[256,256]{1,0:T(8,128)(2,1)S(1)}, u32[]{:S(2)}, u32[]{:S(2)}) %collective-permute-start.13) | collective-permute-done | bytes 131104 | tf_op jit(solution)/shard_map/ppermute | solution.py:310
  43.0 0.7 %cross_attend.1 = (f32[64,640]{1,0:T(8,128)S(1)}, f32[64,640]{1,0:T(8,128)S(1)}) custom-call(f32[256,1024]{1,0:T(8,128)S(1)} %project.7.acc_ref, bf16[256,256]{1,0:T(8,128)(2,1)S(1)} %collective-permute-done.13.e_ref, bf16[256,1024]{1,0:T(8,128)(2,1)S(1)} %get-tuple-element.28.map_ref, bf16[128,512]{1,0:T(8,128)(2,1)S(1)} %get-tuple-element.29.tgt_ref, ...), custom_call_target="tpu_custom_call" | custom-call | flops 134217728 | bytes 2293760 | tf_op jit(solution)/shard_map/cross_attend/pallas_call | solution.py:60
  43.7 1.4 %collective-permute-done.15.refs_1_ = f32[64,640]{1,0:T(8,128)S(1)} collective-permute-done((f32[64,640]{1,0:T(8,128)S(1)}, f32[64,640]{1,0:T(8,128)S(1)}, u32[]{:S(2)}, u32[]{:S(2)}) %collective-permute-start.15) | collective-permute-done | bytes 163872 | tf_op jit(solution)/shard_map/ppermute | solution.py:327
  45.1 0.8 %combine.1 = bf16[64,512]{1,0:T(8,128)(2,1)} custom-call(f32[64,640]{1,0:T(8,128)S(1)} %get-tuple-element.31.refs_0_, f32[64,640]{1,0:T(8,128)S(1)} %collective-permute-done.15.refs_1_), custom_call_target="tpu_custom_call" | custom-call | bytes 393216 | tf_op jit(solution)/shard_map/combine/pallas_call | solution.py:60
  (27 shorter events, 2.8 us)
Async XLA Ops:
  0.0 3.0 %collective-permute-start.1 = (bf16[256,1024]{1,0:T(8,128)(2,1)}, bf16[256,1024]{1,0:T(8,128)(2,1)S(1)}, u32[]{:S(2)}, u32[]{:S(2)}) collective-permute-start(bf16[256,1024]{1,0:T(8,128)(2,1)} %refs_1_.1), channel_id=1, source_target_pairs={{0,4},{4,0},{1,5},{5,1},{2,6},{6,2},{3,7},{7,3},{8,12},{12,8},{9,1... | collective-permute-start | bytes 1572872 | tf_op jit(solution)/shard_map/ppermute | solution.py:269
  0.5 2.5 %collective-permute-start.2 = (bf16[256,1024]{1,0:T(8,128)(2,1)}, bf16[256,1024]{1,0:T(8,128)(2,1)S(1)}, u32[]{:S(2)}, u32[]{:S(2)}) collective-permute-start(bf16[256,1024]{1,0:T(8,128)(2,1)} %refs_2_.5), channel_id=1, source_target_pairs={{0,4},{4,0},{1,5},{5,1},{2,6},{6,2},{3,7},{7,3},{8,12},{12,8},{9,1... | collective-permute-start | bytes 1572872 | tf_op jit(solution)/shard_map/ppermute | solution.py:269
  0.5 2.4 %collective-permute-start = (s32[1,256]{1,0:T(1,128)}, s32[1,256]{1,0:T(1,128)S(1)}, u32[]{:S(2)}, u32[]{:S(2)}) collective-permute-start(s32[1,256]{1,0:T(1,128)} %bitcast.1), channel_id=1, source_target_pairs={{0,4},{4,0},{1,5},{5,1},{2,6},{6,2},{3,7},{7,3},{8,12},{12,8},{9,1... | collective-permute-start | bytes 3080 | tf_op jit(solution)/shard_map/ppermute | solution.py:269
  3.6 7.4 %collective-permute-start.3 = (bf16[256,256]{1,0:T(8,128)(2,1)S(1)}, bf16[256,256]{1,0:T(8,128)(2,1)S(1)}, u32[]{:S(2)}, u32[]{:S(2)}) collective-permute-start(bf16[256,256]{1,0:T(8,128)(2,1)S(1)} %encoder_attend.2.refs_0_), channel_id=1, source_target_pairs={{0,2},{2,3},{3,1},{1,0},{4,6},{6,7},{7,5},{5,4},{8,10},{10,11},{11... | collective-permute-start | bytes 393224 | tf_op jit(solution)/shard_map/ppermute | solution.py:310
  8.7 5.7 %copy-start = (bf16[2048,512]{1,0:T(8,128)(2,1)S(1)}, bf16[2048,512]{1,0:T(8,128)(2,1)}, u32[]{:S(2)}) copy-start(bf16[2048,512]{1,0:T(8,128)(2,1)} %refs_0_.3) | copy-start | bytes 6291460
  8.7 5.7 %copy-start.1 = (bf16[2048,512]{1,0:T(8,128)(2,1)S(1)}, bf16[2048,512]{1,0:T(8,128)(2,1)}, u32[]{:S(2)}) copy-start(bf16[2048,512]{1,0:T(8,128)(2,1)} %refs_2_.9) | copy-start | bytes 6291460
  8.7 6.2 %copy-start.2 = (bf16[64,512]{1,0:T(8,128)(2,1)S(1)}, bf16[64,512]{1,0:T(8,128)(2,1)}, u32[]{:S(2)}) copy-start(bf16[64,512]{1,0:T(8,128)(2,1)} %refs_4_.9) | copy-start | bytes 196612
  8.8 12.0 %collective-permute-start.7 = (bf16[256,768]{1,0:T(8,128)(2,1)S(1)}, bf16[256,768]{1,0:T(8,128)(2,1)S(1)}, u32[]{:S(2)}, u32[]{:S(2)}) collective-permute-start(bf16[256,768]{1,0:T(8,128)(2,1)S(1)} %encoder_attend.3.refs_1_), channel_id=1, source_target_pairs={{0,2},{2,3},{3,1},{1,0},{4,6},{6,7},{7,5},{5,4},{8,10},{10,11},{11... | collective-permute-start | bytes 1179656 | tf_op jit(solution)/shard_map/ppermute | solution.py:310
  11.0 12.3 %collective-permute-start.4 = (bf16[256,256]{1,0:T(8,128)(2,1)S(1)}, bf16[256,256]{1,0:T(8,128)(2,1)S(1)}, u32[]{:S(2)}, u32[]{:S(2)}) collective-permute-start(bf16[256,256]{1,0:T(8,128)(2,1)S(1)} %split.3), channel_id=1, source_target_pairs={{0,2},{2,3},{3,1},{1,0},{4,6},{6,7},{7,5},{5,4},{8,10},{10,11},{11... | collective-permute-start | bytes 393224 | tf_op jit(solution)/shard_map/ppermute | solution.py:310
  14.4 20.1 %collective-permute-start.11 = (bf16[2048,512]{1,0:T(8,128)(2,1)S(1)}, bf16[2048,512]{1,0:T(8,128)(2,1)S(1)}, u32[]{:S(2)}, u32[]{:S(2)}) collective-permute-start(bf16[2048,512]{1,0:T(8,128)(2,1)S(1)} %copy-done), channel_id=1, source_target_pairs={{0,4},{4,0},{1,5},{5,1},{2,6},{6,2},{3,7},{7,3},{8,12},{12,8},{9,1... | collective-permute-start | bytes 6291464 | tf_op jit(solution)/shard_map/ppermute | solution.py:269
  14.5 20.8 %collective-permute-start.12 = (bf16[2048,512]{1,0:T(8,128)(2,1)S(1)}, bf16[2048,512]{1,0:T(8,128)(2,1)S(1)}, u32[]{:S(2)}, u32[]{:S(2)}) collective-permute-start(bf16[2048,512]{1,0:T(8,128)(2,1)S(1)} %copy-done.1), channel_id=1, source_target_pairs={{0,4},{4,0},{1,5},{5,1},{2,6},{6,2},{3,7},{7,3},{8,12},{12,8},{9,1... | collective-permute-start | bytes 6291464 | tf_op jit(solution)/shard_map/ppermute | solution.py:269
  15.0 22.2 %collective-permute-start.14 = (bf16[64,512]{1,0:T(8,128)(2,1)S(1)}, bf16[64,512]{1,0:T(8,128)(2,1)S(1)}, u32[]{:S(2)}, u32[]{:S(2)}) collective-permute-start(bf16[64,512]{1,0:T(8,128)(2,1)S(1)} %copy-done.2), channel_id=1, source_target_pairs={{0,4},{4,0},{1,5},{5,1},{2,6},{6,2},{3,7},{7,3},{8,12},{12,8},{9,1... | collective-permute-start | bytes 196616 | tf_op jit(solution)/shard_map/ppermute | solution.py:269
  20.8 10.8 %collective-permute-start.8 = (bf16[256,768]{1,0:T(8,128)(2,1)S(1)}, bf16[256,768]{1,0:T(8,128)(2,1)S(1)}, u32[]{:S(2)}, u32[]{:S(2)}) collective-permute-start(bf16[256,768]{1,0:T(8,128)(2,1)S(1)} %collective-permute-done.7.refs_1_), channel_id=1, source_target_pairs={{0,2},{2,3},{3,1},{1,0},{4,6},{6,7},{7,5},{5,4},{8,10},{10,11},{11... | collective-permute-start | bytes 1179656 | tf_op jit(solution)/shard_map/ppermute | solution.py:310
  23.3 15.9 %collective-permute-start.5 = (bf16[256,128]{1,0:T(8,128)(2,1)S(1)}, bf16[256,128]{1,0:T(8,128)(2,1)S(1)}, u32[]{:S(2)}, u32[]{:S(2)}) collective-permute-start(bf16[256,128]{1,0:T(8,128)(2,1)S(1)} %get-tuple-element.23), channel_id=1, source_target_pairs={{0,2},{2,3},{3,1},{1,0},{4,6},{6,7},{7,5},{5,4},{8,10},{10,11},{11... | collective-permute-start | bytes 196616 | tf_op jit(solution)/shard_map/ppermute | solution.py:310
  31.6 7.6 %collective-permute-start.6 = (bf16[256,128]{1,0:T(8,128)(2,1)S(1)}, bf16[256,128]{1,0:T(8,128)(2,1)S(1)}, u32[]{:S(2)}, u32[]{:S(2)}) collective-permute-start(bf16[256,128]{1,0:T(8,128)(2,1)S(1)} %get-tuple-element.24), channel_id=1, source_target_pairs={{0,2},{2,3},{3,1},{1,0},{4,6},{6,7},{7,5},{5,4},{8,10},{10,11},{11... | collective-permute-start | bytes 196616 | tf_op jit(solution)/shard_map/ppermute | solution.py:310
  34.5 5.6 %collective-permute-start.10 = (bf16[256,256]{1,0:T(8,128)(2,1)S(1)}, bf16[256,256]{1,0:T(8,128)(2,1)S(1)}, u32[]{:S(2)}, u32[]{:S(2)}) collective-permute-start(bf16[256,256]{1,0:T(8,128)(2,1)S(1)} %get-tuple-element.26), channel_id=1, source_target_pairs={{0,2},{2,3},{3,1},{1,0},{4,6},{6,7},{7,5},{5,4},{8,10},{10,11},{11... | collective-permute-start | bytes 393224 | tf_op jit(solution)/shard_map/ppermute | solution.py:310
  35.2 6.4 %collective-permute-start.9 = (bf16[256,256]{1,0:T(8,128)(2,1)S(1)}, bf16[256,256]{1,0:T(8,128)(2,1)S(1)}, u32[]{:S(2)}, u32[]{:S(2)}) collective-permute-start(bf16[256,256]{1,0:T(8,128)(2,1)S(1)} %get-tuple-element.25), channel_id=1, source_target_pairs={{0,2},{2,3},{3,1},{1,0},{4,6},{6,7},{7,5},{5,4},{8,10},{10,11},{11... | collective-permute-start | bytes 393224 | tf_op jit(solution)/shard_map/ppermute | solution.py:310
  37.2 5.8 %collective-permute-start.13 = (bf16[256,256]{1,0:T(8,128)(2,1)S(1)}, bf16[256,256]{1,0:T(8,128)(2,1)S(1)}, u32[]{:S(2)}, u32[]{:S(2)}) collective-permute-start(bf16[256,256]{1,0:T(8,128)(2,1)S(1)} %get-tuple-element.27), channel_id=1, source_target_pairs={{0,2},{2,3},{3,1},{1,0},{4,6},{6,7},{7,5},{5,4},{8,10},{10,11},{11... | collective-permute-start | bytes 393224 | tf_op jit(solution)/shard_map/ppermute | solution.py:310
  43.7 1.5 %collective-permute-start.15 = (f32[64,640]{1,0:T(8,128)S(1)}, f32[64,640]{1,0:T(8,128)S(1)}, u32[]{:S(2)}, u32[]{:S(2)}) collective-permute-start(f32[64,640]{1,0:T(8,128)S(1)} %get-tuple-element.32), channel_id=1, source_target_pairs={{4,0},{0,4},{5,1},{1,5},{6,2},{2,6},{7,3},{3,7},{12,8},{8,12},{13,... | collective-permute-start | bytes 491528 | tf_op jit(solution)/shard_map/ppermute | solution.py:327

commit v9 on v7

--- a/solution.py
+++ b/solution.py
@@ -87,6 +87,31 @@
         specs=[HBM] * len(arrays),
         scratch=[pltpu.SemaphoreType.DMA((len(arrays),))],
     )
+
+
+def pack_kernel(*refs):
+    sources, out_ref, sems = refs[:-2], refs[-2], refs[-1]
+    copies, row = [], 0
+    for i, source in enumerate(sources):
+        rows = source.shape[0]
+        copies.append(pltpu.make_async_copy(source, out_ref.at[pl.ds(row, rows), :], sems.at[i]))
+        row += rows
+    for copy in copies:
+        copy.start()
+    for copy in copies:
+        copy.wait()
+
+
+def pack(*arrays):
+    rows = sum(x.shape[0] for x in arrays)
+    return call(
+        pack_kernel,
+        "pack",
+        [((rows, arrays[0].shape[1]), arrays[0].dtype)],
+        [pltpu.with_memory_space_constraint(x, pltpu.HBM) for x in arrays],
+        specs=[HBM] * len(arrays),
+        scratch=[pltpu.SemaphoreType.DMA((len(arrays),))],
+    )[0]
 
 
 def attend_kernel(blocks, first, *refs):
@@ -118,21 +143,12 @@
     )[0]
 
 
-def add_products(acc_of, store, e_refs, place, key_shards, value_shards):
-    shard, row = place
-    depth = e_refs[0].shape[1]
-    at = pl.ds(pl.multiple_of(row, depth), depth * len(e_refs))
-    chunks = jnp.concatenate([r[...] for r in e_refs], axis=1)
-
-    def add(i):
-        for side, shards in enumerate((key_shards, value_shards)):
-            store(side, acc_of(side) + dot(chunks, shards[i][at, :]))
-
-    if len(key_shards) == 1:
-        add(0)
+def in_shard(shards, shard, act):
+    if len(shards) == 1:
+        act(shards[0])
     else:
-        for i in range(len(key_shards)):
-            pl.when(shard == i)(functools.partial(add, i))
+        for i, maps in enumerate(shards):
+            pl.when(shard == i)(functools.partial(act, maps))
 
 
 def halve_kernel(source, *outs):
@@ -143,28 +159,32 @@
 
 def halve(chunk):
     rows, width = chunk.shape
-    return call(halve_kernel, "halve", [((rows, width // 2), chunk.dtype)] * 2, [chunk], flops=10**10)
-
-
-def project_kernel(chunks, shards, has_acc, place, *refs):
-    out_ref = refs[-1]
-    e_refs, maps = refs[:chunks], refs[chunks : chunks + 2 * shards]
+    return call(halve_kernel, "halve", [((rows, width // 2), chunk.dtype)] * 2, [chunk], flops=3 * 10**10)
+
+
+def project_kernel(chunks, shards, map_rows, has_acc, place, *refs):
+    e_refs, maps, out_ref = refs[:chunks], refs[chunks : chunks + shards], refs[-1]
     half = out_ref.shape[1] // 2
-    side_of = lambda side: slice(side * half, (side + 1) * half)
-
-    def store(side, value):
-        out_ref[:, side_of(side)] = value
-
-    acc_of = lambda side: refs[-2][:, side_of(side)] if has_acc else 0.0
-    add_products(acc_of, store, e_refs, place(), maps[:shards], maps[shards:])
-
-
-def project(acc, chunks, place, key_shards, value_shards):
+    depth = e_refs[0].shape[1]
+    shard, row = place()
+    row = pl.multiple_of(row, depth)
+    chunk = jnp.concatenate([r[...] for r in e_refs], axis=1)
+
+    def add(map_ref):
+        for side in range(2):
+            columns = slice(side * half, (side + 1) * half)
+            product = dot(chunk, map_ref[pl.ds(side * map_rows + row, depth * chunks), :])
+            out_ref[:, columns] = refs[-2][:, columns] + product if has_acc else product
+
+    in_shard(maps, shard, add)
+
+
+def project(acc, chunks, place, shards, map_rows):
     rows, depth = chunks[0].shape
-    width = key_shards[0].shape[1]
-    operands = [*chunks, *key_shards, *value_shards] + ([] if acc is None else [acc])
-    return call(
-        functools.partial(project_kernel, len(chunks), len(key_shards), acc is not None, place),
+    width = shards[0].shape[1]
+    operands = [*chunks, *shards] + ([] if acc is None else [acc])
+    return call(
+        functools.partial(project_kernel, len(chunks), len(shards), map_rows, acc is not None, place),
         "project",
         [((rows, 2 * width), F32)],
         operands,
@@ -172,40 +192,38 @@
     )[0]
 
 
-def prepare_kernel(shards, parts, step, place, *refs):
-    maps, targets, marks = refs[: 2 * shards], refs[2 * shards : 2 * shards + parts], refs[2 * shards + parts : -4]
+def prepare_kernel(shards, parts, map_rows, step, place, *refs):
+    maps, marks, near = refs[:shards], refs[shards : shards + parts], refs[shards + parts : -4]
     map_ref, tgt_ref, mask_ref, down_ref = refs[-4:]
     shard, row = place()
     depth, width = map_ref.shape[0], map_ref.shape[1] // 2
-    at = pl.ds(pl.multiple_of(row, depth), depth)
-
-    def copy(i):
-        map_ref[:, :width] = maps[i][at, :]
-        map_ref[:, width:] = maps[shards + i][at, :]
-
-    if shards == 1:
-        copy(0)
-    else:
-        for i in range(shards):
-            pl.when(shard == i)(functools.partial(copy, i))
+    row = pl.multiple_of(row, depth)
+
+    def copy(source):
+        for side in range(2):
+            map_ref[:, side * width : (side + 1) * width] = source[pl.ds(side * map_rows + row, depth), :]
+
+    in_shard(maps, shard, copy)
     own = marks[0][...]
-    count = targets[0].shape[0]
-    for i, (target_ref, mark_ref) in enumerate(zip(targets, marks)):
+    count = tgt_ref.shape[0] // parts
+    below = slice(2 * map_rows, 2 * map_rows + count)
+    targets = [maps[0][below, :]] + ([r[...] for r in near] if near else [m[below, :] for m in maps[1:]])
+    for i, (target, mark_ref) in enumerate(zip(targets, marks)):
         part = slice(i * count, (i + 1) * count)
-        tgt_ref[part, :] = target_ref[...]
+        tgt_ref[part, :] = target
         down_ref[...] = down_lanes(mark_ref[...])
         down = down_ref[pl.ds(0, count, stride=step), :]
         mask_ref[part, :] = same_mark(down, own).astype(F32)
 
 
-def prepare(place, depth, key_shards, value_shards, targets, marks):
-    rows, count, width = marks[0].shape[1], targets[0].shape[0], targets[0].shape[1]
-    total = count * len(targets)
-    return call(
-        functools.partial(prepare_kernel, len(key_shards), len(targets), rows // count, place),
+def prepare(place, depth, shards, map_rows, count, near_targets, marks):
+    rows, width = marks[0].shape[1], shards[0].shape[1]
+    total = count * len(marks)
+    return call(
+        functools.partial(prepare_kernel, len(shards), len(marks), map_rows, rows // count, place),
         "prepare",
         [((depth, 2 * width), BF16), ((total, width), BF16), ((total, rows), F32)],
-        [*key_shards, *value_shards, *targets, *marks],
+        [*shards, *marks, *near_targets],
         scratch=[pltpu.VMEM((rows, LANES), jnp.int32)],
     )
 
@@ -271,11 +289,14 @@
     marks = (doc_ids if n_ctx == 2 else doc_ids + 1).reshape(1, rows)
     keys, values, near_marks = bring(enc_key), bring(enc_value), bring(marks)
     query, own_key, own_value, marks = fetch(enc_query, enc_key, enc_value, marks)
-    near_targets = bring(tgt_query)
+    near_targets = []
     if n_ctx == 2:
-        key_shards, value_shards = [key_map, *bring(key_map)], [value_map, *bring(value_map)]
+        own_maps = pack(key_map, value_map, tgt_query)
+        shards = [own_maps, *bring(own_maps)]
     else:
-        key_shards, value_shards = ([lax.all_gather(x, "ctx", axis=0, tiled=True)] for x in (key_map, value_map))
+        whole = [lax.all_gather(x, "ctx", axis=0, tiled=True) for x in (key_map, value_map)]
+        shards, near_targets = [pack(*whole, tgt_query)], bring(tgt_query)
+    map_rows = (shards[0].shape[0] - tgt_rows) // 2
 
     chunks = 2
     heads = features // HEAD_DIM // chunks
@@ -297,10 +318,9 @@
                 source = before[source]
             owner = owner + jnp.where(head == i, source, 0)
         row = owner * features + first
-        if len(key_shards) == 1:
+        if len(shards) == 1:
             return None, row
-        shard_rows = n_head * features // 2
-        return jnp.where(lax.div(row, shard_rows) == ctx, 0, 1), lax.rem(row, shard_rows)
+        return jnp.where(lax.div(row, map_rows) == ctx, 0, 1), lax.rem(row, map_rows)
 
     acc, last = None, n_head - 1
     for turn in range(last):
@@ -309,16 +329,17 @@
         else:
             pieces = held
         later = [lax.ppermute(p, "head", ring) for p in pieces]
-        acc = project(acc, held, functools.partial(place, turn, 0), key_shards, value_shards)
+        acc = project(acc, held, functools.partial(place, turn, 0), shards, map_rows)
         held = later
-    acc = project(acc, held[:-1], functools.partial(place, last, 0), key_shards, value_shards)
+    acc = project(acc, held[:-1], functools.partial(place, last, 0), shards, map_rows)
     depth = held[-1].shape[1]
     last_maps, targets, mask = prepare(
         functools.partial(place, last, features - depth),
         depth,
-        key_shards,
-        value_shards,
-        [tgt_query, *near_targets],
+        shards,
+        map_rows,
+        tgt_rows,
+        near_targets,
         [marks, *near_marks],
     )
     parts = cross_attend(acc, held[-1], last_maps, targets, mask, 1 + len(links))

time: 45.5 us -> 45.5 us (level)
  Pallas kernels: 7.66 us -> 9.91 us
  waiting for transfers between devices: 14.8 us -> 13.1 us
  starting transfers between devices: 22.8 us -> 22.2 us
    pallas_call x12 -> x13, Pallas kernels: 7.66 us -> 9.91 us  [call(): pl.pallas_call(kernel, in_specs=specs or [VMEM] * len(operands), out_spec...]
    ppermute x8, waiting for transfers between devices: 12.8 us -> 11.1 us  [on_device(): later = [lax.ppermute(p, 'head', ring) for p in pieces]]
    ppermute x6 -> x4, starting transfers between devices: 1.54 us -> 1.03 us  [on_device(): bring = lambda x: [lax.ppermute(x, 'ctx', pairs) for pairs in links]]
  transfers between devices with their start and end apart: 15 -> 13, of which waited for: 8 -> 7; matrix products, arithmetic and copies ran while one was open for 0% -> 0% of each run, Pallas kernels for 12% -> 17%
where the time goes in v9:
time: 45.5 us; the launch traced here: 45.3 us
  starting transfers between devices  22.2 us (49%)
  waiting for transfers between devices  13.1 us (29%)
  Pallas kernels  9.91 us (22%)
    ppermute x8, starting transfers between devices, on_device(): later = [lax.ppermute(p, 'head', ring) for p in pieces]  21.1 us
    ppermute x8, waiting for transfers between devices, on_device(): later = [lax.ppermute(p, 'head', ring) for p in pieces]  11.1 us
    pallas_call x13, Pallas kernels, call(): pl.pallas_call(kernel, in_specs=specs or [VMEM] * len(operands), out_spec...  9.91 us
    ppermute x1, waiting for transfers between devices, on_device(): lax.ppermute(piece, 'ctx', [(target, source) for source, target in pairs])  1.38 us
    ppermute x4, starting transfers between devices, on_device(): bring = lambda x: [lax.ppermute(x, 'ctx', pairs) for pairs in links]  1.03 us
  transfers between devices with their start and end apart: 13, of which 7 were waited for; matrix products, arithmetic and copies ran while one was open for 0% of the time, Pallas kernels for 17%

profile of v9, /device:TPU:0, one launch (start us, length us, event | category | flops | bytes accessed | tf_op | source)
XLA Modules:
  0.0 45.3 jit_solution(4810618205438372772)
XLA Ops:
  1.0 1.4 %fetch.1 = (bf16[256,1024]{1,0:T(8,128)(2,1)S(1)}, bf16[256,1024]{1,0:T(8,128)(2,1)S(1)}, bf16[256,1024]{1,0:T(8,128)(2,1)S(1)}, s32[1,256]{1,0:T(1,128)S(1)}) custom-call(bf16[256,1024]{1,0:T(8,128)(2,1)} %refs_0_.2, bf16[256,1024]{1,0:T(8,128)(2,1)} %refs_1_.2, bf16[256,1024]{1,0:T(8,128)(2,1)} %refs_2_.2, s32[1,256]{1,0:T(1,128)} %bitcast.2), custom_call_target="tpu_custom_call" | custom-call | bytes 3147776 | tf_op jit(solution)/shard_map/fetch/pallas_call | solution.py:60
  3.0 0.9 %encoder_attend.3.refs_1_ = bf16[256,512]{1,0:T(8,128)(2,1)S(1)} custom-call(s32[1,256]{1,0:T(1,128)S(1)} %get-tuple-element.18.refs_0_.refs_2_, s32[1,256]{1,0:T(1,128)S(1)} %collective-permute-done.refs_1_.refs_3_, bf16[256,1024]{1,0:T(8,128)(2,1)S(1)} %get-tuple-element.19.refs_2_, bf16[256,1024]{1,0:T(8,128)(2,1)S(1)} %get-tuple-element.20.refs_3_, ...), custom_call_target="tpu_custom_call" | custom-call | flops 268435456 | bytes 2885632 | tf_op jit(solution)/shard_map/encoder_attend/pallas_call | solution.py:60
  3.8 4.0 %collective-permute-start.7 = (bf16[256,512]{1,0:T(8,128)(2,1)S(1)}, bf16[256,512]{1,0:T(8,128)(2,1)S(1)}, u32[]{:S(2)}, u32[]{:S(2)}) collective-permute-start(bf16[256,512]{1,0:T(8,128)(2,1)S(1)} %encoder_attend.3.refs_1_), channel_id=1, source_target_pairs={{0,2},{2,3},{3,1},{1,0},{4,6},{6,7},{7,5},{5,4},{8,10},{10,11},{11... | collective-permute-start | bytes 786440 | tf_op jit(solution)/shard_map/ppermute | solution.py:331
  7.8 0.9 %encoder_attend.2.refs_0_ = bf16[256,512]{1,0:T(8,128)(2,1)S(1)} custom-call(s32[1,256]{1,0:T(1,128)S(1)} %get-tuple-element.18.refs_0_.refs_2_, s32[1,256]{1,0:T(1,128)S(1)} %collective-permute-done.refs_1_.refs_3_, bf16[256,1024]{1,0:T(8,128)(2,1)S(1)} %get-tuple-element.19.refs_2_, bf16[256,1024]{1,0:T(8,128)(2,1)S(1)} %get-tuple-element.20.refs_3_, ...), custom_call_target="tpu_custom_call" | custom-call | flops 268435456 | bytes 2885632 | tf_op jit(solution)/shard_map/encoder_attend/pallas_call | solution.py:60
  8.7 1.6 %collective-permute-start.3 = (bf16[256,512]{1,0:T(8,128)(2,1)S(1)}, bf16[256,512]{1,0:T(8,128)(2,1)S(1)}, u32[]{:S(2)}, u32[]{:S(2)}) collective-permute-start(bf16[256,512]{1,0:T(8,128)(2,1)S(1)} %encoder_attend.2.refs_0_), channel_id=1, source_target_pairs={{0,2},{2,3},{3,1},{1,0},{4,6},{6,7},{7,5},{5,4},{8,10},{10,11},{11... | collective-permute-start | bytes 786440 | tf_op jit(solution)/shard_map/ppermute | solution.py:331
  10.3 4.2 %collective-permute-done.7.refs_1_ = bf16[256,512]{1,0:T(8,128)(2,1)S(1)} collective-permute-done((bf16[256,512]{1,0:T(8,128)(2,1)S(1)}, bf16[256,512]{1,0:T(8,128)(2,1)S(1)}, u32[]{:S(2)}, u32[]{:S(2)}) %collective-permute-start.7) | collective-permute-done | bytes 262176 | tf_op jit(solution)/shard_map/ppermute | solution.py:331
  14.5 3.4 %collective-permute-start.8 = (bf16[256,512]{1,0:T(8,128)(2,1)S(1)}, bf16[256,512]{1,0:T(8,128)(2,1)S(1)}, u32[]{:S(2)}, u32[]{:S(2)}) collective-permute-start(bf16[256,512]{1,0:T(8,128)(2,1)S(1)} %collective-permute-done.7.refs_1_), channel_id=1, source_target_pairs={{0,2},{2,3},{3,1},{1,0},{4,6},{6,7},{7,5},{5,4},{8,10},{10,11},{11... | collective-permute-start | bytes 786440 | tf_op jit(solution)/shard_map/ppermute | solution.py:331
  17.9 2.2 %pack.1.refs_2_.refs_3_.refs_0_ = bf16[4160,512]{1,0:T(8,128)(2,1)S(1)} custom-call(bf16[2048,512]{1,0:T(8,128)(2,1)} %refs_0_.3, bf16[2048,512]{1,0:T(8,128)(2,1)} %refs_1_.3, bf16[64,512]{1,0:T(8,128)(2,1)} %refs_2_.3), custom_call_target="tpu_custom_call" | custom-call | bytes 8519680 | tf_op jit(solution)/shard_map/pack/pallas_call | solution.py:60
  20.2 3.3 %collective-permute-start.4 = (bf16[256,512]{1,0:T(8,128)(2,1)S(1)}, bf16[256,512]{1,0:T(8,128)(2,1)S(1)}, u32[]{:S(2)}, u32[]{:S(2)}) collective-permute-start(bf16[256,512]{1,0:T(8,128)(2,1)S(1)} %collective-permute-done.3.refs_0_), channel_id=1, source_target_pairs={{0,2},{2,3},{3,1},{1,0},{4,6},{6,7},{7,5},{5,4},{8,10},{10,11},{11... | collective-permute-start | bytes 786440 | tf_op jit(solution)/shard_map/ppermute | solution.py:331
  23.5 2.2 %collective-permute-done.8.source.refs_1_ = bf16[256,512]{1,0:T(8,128)(2,1)S(1)} collective-permute-done((bf16[256,512]{1,0:T(8,128)(2,1)S(1)}, bf16[256,512]{1,0:T(8,128)(2,1)S(1)}, u32[]{:S(2)}, u32[]{:S(2)}) %collective-permute-start.8) | collective-permute-done | bytes 262176 | tf_op jit(solution)/shard_map/ppermute | solution.py:331
  25.8 3.4 %collective-permute-start.9 = (bf16[256,256]{1,0:T(8,128)(2,1)S(1)}, bf16[256,256]{1,0:T(8,128)(2,1)S(1)}, u32[]{:S(2)}, u32[]{:S(2)}) collective-permute-start(bf16[256,256]{1,0:T(8,128)(2,1)S(1)} %get-tuple-element.24), channel_id=1, source_target_pairs={{0,2},{2,3},{3,1},{1,0},{4,6},{6,7},{7,5},{5,4},{8,10},{10,11},{11... | collective-permute-start | bytes 393224 | tf_op jit(solution)/shard_map/ppermute | solution.py:331
  29.2 2.2 %collective-permute-done.4.source.refs_0_ = bf16[256,512]{1,0:T(8,128)(2,1)S(1)} collective-permute-done((bf16[256,512]{1,0:T(8,128)(2,1)S(1)}, bf16[256,512]{1,0:T(8,128)(2,1)S(1)}, u32[]{:S(2)}, u32[]{:S(2)}) %collective-permute-start.4) | collective-permute-done | bytes 262176 | tf_op jit(solution)/shard_map/ppermute | solution.py:331
  31.4 3.4 %collective-permute-start.5 = (bf16[256,256]{1,0:T(8,128)(2,1)S(1)}, bf16[256,256]{1,0:T(8,128)(2,1)S(1)}, u32[]{:S(2)}, u32[]{:S(2)}) collective-permute-start(bf16[256,256]{1,0:T(8,128)(2,1)S(1)} %get-tuple-element.22), channel_id=1, source_target_pairs={{0,2},{2,3},{3,1},{1,0},{4,6},{6,7},{7,5},{5,4},{8,10},{10,11},{11... | collective-permute-start | bytes 393224 | tf_op jit(solution)/shard_map/ppermute | solution.py:331
  34.8 0.7 %collective-permute-start.6 = (bf16[256,256]{1,0:T(8,128)(2,1)S(1)}, bf16[256,256]{1,0:T(8,128)(2,1)S(1)}, u32[]{:S(2)}, u32[]{:S(2)}) collective-permute-start(bf16[256,256]{1,0:T(8,128)(2,1)S(1)} %get-tuple-element.23), channel_id=1, source_target_pairs={{0,2},{2,3},{3,1},{1,0},{4,6},{6,7},{7,5},{5,4},{8,10},{10,11},{11... | collective-permute-start | bytes 393224 | tf_op jit(solution)/shard_map/ppermute | solution.py:331
  35.5 1.2 %collective-permute-start.11 = (bf16[256,256]{1,0:T(8,128)(2,1)S(1)}, bf16[256,256]{1,0:T(8,128)(2,1)S(1)}, u32[]{:S(2)}, u32[]{:S(2)}) collective-permute-start(bf16[256,256]{1,0:T(8,128)(2,1)S(1)} %get-tuple-element.25), channel_id=1, source_target_pairs={{0,2},{2,3},{3,1},{1,0},{4,6},{6,7},{7,5},{5,4},{8,10},{10,11},{11... | collective-permute-start | bytes 393224 | tf_op jit(solution)/shard_map/ppermute | solution.py:331
  36.9 0.7 %project.4.refs_4_ = f32[256,1024]{1,0:T(8,128)S(1)} custom-call(bf16[256,512]{1,0:T(8,128)(2,1)S(1)} %encoder_attend.2.refs_0_, bf16[256,512]{1,0:T(8,128)(2,1)S(1)} %encoder_attend.3.refs_1_, bf16[4160,512]{1,0:T(8,128)(2,1)S(1)} %pack.1.refs_2_.refs_3_.refs_0_, bf16[4160,512]{1,0:T(8,128)(2,1)S(1)} %collective-permute-done.10.refs_3_.refs_4_.refs_1_), custom_call_target="tpu_custom_call" | custom-call | flops 536870912 | bytes 10092544 | tf_op jit(solution)/shard_map/project/pallas_call | solution.py:60
  37.7 0.7 %project.5.refs_4_ = f32[256,1024]{1,0:T(8,128)S(1)} custom-call(bf16[256,512]{1,0:T(8,128)(2,1)S(1)} %collective-permute-done.3.refs_0_, bf16[256,512]{1,0:T(8,128)(2,1)S(1)} %collective-permute-done.7.refs_1_, bf16[4160,512]{1,0:T(8,128)(2,1)S(1)} %pack.1.refs_2_.refs_3_.refs_0_, bf16[4160,512]{1,0:T(8,128)(2,1)S(1)} %collective-permute-done.10.refs_3_.refs_4_.refs_1_, ...), custom_call_target="tpu_custom_call" | custom-call | flops 536870912 | bytes 11141120 | tf_op jit(solution)/shard_map/project/pallas_call | solution.py:60
  38.4 0.7 %project.6.refs_5_ = f32[256,1024]{1,0:T(8,128)S(1)} custom-call(bf16[256,512]{1,0:T(8,128)(2,1)S(1)} %collective-permute-done.4.source.refs_0_, bf16[256,512]{1,0:T(8,128)(2,1)S(1)} %collective-permute-done.8.source.refs_1_, bf16[4160,512]{1,0:T(8,128)(2,1)S(1)} %pack.1.refs_2_.refs_3_.refs_0_, ...), custom_call_target="tpu_custom_call" | custom-call | flops 536870912 | bytes 11141120 | tf_op jit(solution)/shard_map/project/pallas_call | solution.py:60
  39.2 1.8 %collective-permute-done.6.refs_1_ = bf16[256,256]{1,0:T(8,128)(2,1)S(1)} collective-permute-done((bf16[256,256]{1,0:T(8,128)(2,1)S(1)}, bf16[256,256]{1,0:T(8,128)(2,1)S(1)}, u32[]{:S(2)}, u32[]{:S(2)}) %collective-permute-start.6) | collective-permute-done | bytes 131104 | tf_op jit(solution)/shard_map/ppermute | solution.py:331
  41.0 0.6 %project.7.acc_ref = f32[256,1024]{1,0:T(8,128)S(1)} custom-call(bf16[256,256]{1,0:T(8,128)(2,1)S(1)} %collective-permute-done.5.refs_0_, bf16[256,256]{1,0:T(8,128)(2,1)S(1)} %collective-permute-done.6.refs_1_, bf16[256,256]{1,0:T(8,128)(2,1)S(1)} %collective-permute-done.9.refs_2_, bf16[4160,512]{1,0:T(8,128)(2,1)S(1)} %pack.1.refs_2_.refs_3_.refs_0_, ...), custom_call_target="tpu_custom_call" | custom-call | flops 402653184 | bytes 11010048 | tf_op jit(solution)/shard_map/project/pallas_call | solution.py:60
  41.6 0.8 %collective-permute-done.11.e_ref = bf16[256,256]{1,0:T(8,128)(2,1)S(1)} collective-permute-done((bf16[256,256]{1,0:T(8,128)(2,1)S(1)}, bf16[256,256]{1,0:T(8,128)(2,1)S(1)}, u32[]{:S(2)}, u32[]{:S(2)}) %collective-permute-start.11) | collective-permute-done | bytes 131104 | tf_op jit(solution)/shard_map/ppermute | solution.py:331
  42.4 0.7 %cross_attend.1 = (f32[64,640]{1,0:T(8,128)S(1)}, f32[64,640]{1,0:T(8,128)S(1)}) custom-call(f32[256,1024]{1,0:T(8,128)S(1)} %project.7.acc_ref, bf16[256,256]{1,0:T(8,128)(2,1)S(1)} %collective-permute-done.11.e_ref, bf16[256,1024]{1,0:T(8,128)(2,1)S(1)} %get-tuple-element.26.map_ref, bf16[128,512]{1,0:T(8,128)(2,1)S(1)} %get-tuple-element.27.tgt_ref, ...), custom_call_target="tpu_custom_call" | custom-call | flops 134217728 | bytes 2293760 | tf_op jit(solution)/shard_map/cross_attend/pallas_call | solution.py:60
  43.1 1.4 %collective-permute-done.12.refs_1_ = f32[64,640]{1,0:T(8,128)S(1)} collective-permute-done((f32[64,640]{1,0:T(8,128)S(1)}, f32[64,640]{1,0:T(8,128)S(1)}, u32[]{:S(2)}, u32[]{:S(2)}) %collective-permute-start.12) | collective-permute-done | bytes 163872 | tf_op jit(solution)/shard_map/ppermute | solution.py:349
  44.5 0.8 %combine.1 = bf16[64,512]{1,0:T(8,128)(2,1)} custom-call(f32[64,640]{1,0:T(8,128)S(1)} %get-tuple-element.29.refs_0_, f32[64,640]{1,0:T(8,128)S(1)} %collective-permute-done.12.refs_1_), custom_call_target="tpu_custom_call" | custom-call | bytes 393216 | tf_op jit(solution)/shard_map/combine/pallas_call | solution.py:60
  (15 shorter events, 1.9 us)
Async XLA Ops:
  0.0 3.0 %collective-permute-start.1 = (bf16[256,1024]{1,0:T(8,128)(2,1)}, bf16[256,1024]{1,0:T(8,128)(2,1)S(1)}, u32[]{:S(2)}, u32[]{:S(2)}) collective-permute-start(bf16[256,1024]{1,0:T(8,128)(2,1)} %refs_1_.2), channel_id=1, source_target_pairs={{0,4},{4,0},{1,5},{5,1},{2,6},{6,2},{3,7},{7,3},{8,12},{12,8},{9,1... | collective-permute-start | bytes 1572872 | tf_op jit(solution)/shard_map/ppermute | solution.py:287
  0.5 2.5 %collective-permute-start.2 = (bf16[256,1024]{1,0:T(8,128)(2,1)}, bf16[256,1024]{1,0:T(8,128)(2,1)S(1)}, u32[]{:S(2)}, u32[]{:S(2)}) collective-permute-start(bf16[256,1024]{1,0:T(8,128)(2,1)} %refs_2_.2), channel_id=1, source_target_pairs={{0,4},{4,0},{1,5},{5,1},{2,6},{6,2},{3,7},{7,3},{8,12},{12,8},{9,1... | collective-permute-start | bytes 1572872 | tf_op jit(solution)/shard_map/ppermute | solution.py:287
  0.5 2.4 %collective-permute-start = (s32[1,256]{1,0:T(1,128)}, s32[1,256]{1,0:T(1,128)S(1)}, u32[]{:S(2)}, u32[]{:S(2)}) collective-permute-start(s32[1,256]{1,0:T(1,128)} %bitcast.1), channel_id=1, source_target_pairs={{0,4},{4,0},{1,5},{5,1},{2,6},{6,2},{3,7},{7,3},{8,12},{12,8},{9,1... | collective-permute-start | bytes 3080 | tf_op jit(solution)/shard_map/ppermute | solution.py:287
  3.8 10.7 %collective-permute-start.7 = (bf16[256,512]{1,0:T(8,128)(2,1)S(1)}, bf16[256,512]{1,0:T(8,128)(2,1)S(1)}, u32[]{:S(2)}, u32[]{:S(2)}) collective-permute-start(bf16[256,512]{1,0:T(8,128)(2,1)S(1)} %encoder_attend.3.refs_1_), channel_id=1, source_target_pairs={{0,2},{2,3},{3,1},{1,0},{4,6},{6,7},{7,5},{5,4},{8,10},{10,11},{11... | collective-permute-start | bytes 786440 | tf_op jit(solution)/shard_map/ppermute | solution.py:331
  8.7 11.5 %collective-permute-start.3 = (bf16[256,512]{1,0:T(8,128)(2,1)S(1)}, bf16[256,512]{1,0:T(8,128)(2,1)S(1)}, u32[]{:S(2)}, u32[]{:S(2)}) collective-permute-start(bf16[256,512]{1,0:T(8,128)(2,1)S(1)} %encoder_attend.2.refs_0_), channel_id=1, source_target_pairs={{0,2},{2,3},{3,1},{1,0},{4,6},{6,7},{7,5},{5,4},{8,10},{10,11},{11... | collective-permute-start | bytes 786440 | tf_op jit(solution)/shard_map/ppermute | solution.py:331
  14.5 11.2 %collective-permute-start.8 = (bf16[256,512]{1,0:T(8,128)(2,1)S(1)}, bf16[256,512]{1,0:T(8,128)(2,1)S(1)}, u32[]{:S(2)}, u32[]{:S(2)}) collective-permute-start(bf16[256,512]{1,0:T(8,128)(2,1)S(1)} %collective-permute-done.7.refs_1_), channel_id=1, source_target_pairs={{0,2},{2,3},{3,1},{1,0},{4,6},{6,7},{7,5},{5,4},{8,10},{10,11},{11... | collective-permute-start | bytes 786440 | tf_op jit(solution)/shard_map/ppermute | solution.py:331
  20.1 16.6 %collective-permute-start.10 = (bf16[4160,512]{1,0:T(8,128)(2,1)S(1)}, bf16[4160,512]{1,0:T(8,128)(2,1)S(1)}, u32[]{:S(2)}, u32[]{:S(2)}) collective-permute-start(bf16[4160,512]{1,0:T(8,128)(2,1)S(1)} %pack.1.refs_2_.refs_3_.refs_0_), channel_id=1, source_target_pairs={{0,4},{4,0},{1,5},{5,1},{2,6},{6,2},{3,7},{7,3},{8,12},{12,8},{9,1... | collective-permute-start | bytes 12779528 | tf_op jit(solution)/shard_map/ppermute | solution.py:287
  20.2 11.1 %collective-permute-start.4 = (bf16[256,512]{1,0:T(8,128)(2,1)S(1)}, bf16[256,512]{1,0:T(8,128)(2,1)S(1)}, u32[]{:S(2)}, u32[]{:S(2)}) collective-permute-start(bf16[256,512]{1,0:T(8,128)(2,1)S(1)} %collective-permute-done.3.refs_0_), channel_id=1, source_target_pairs={{0,2},{2,3},{3,1},{1,0},{4,6},{6,7},{7,5},{5,4},{8,10},{10,11},{11... | collective-permute-start | bytes 786440 | tf_op jit(solution)/shard_map/ppermute | solution.py:331
  25.8 13.4 %collective-permute-start.9 = (bf16[256,256]{1,0:T(8,128)(2,1)S(1)}, bf16[256,256]{1,0:T(8,128)(2,1)S(1)}, u32[]{:S(2)}, u32[]{:S(2)}) collective-permute-start(bf16[256,256]{1,0:T(8,128)(2,1)S(1)} %get-tuple-element.24), channel_id=1, source_target_pairs={{0,2},{2,3},{3,1},{1,0},{4,6},{6,7},{7,5},{5,4},{8,10},{10,11},{11... | collective-permute-start | bytes 393224 | tf_op jit(solution)/shard_map/ppermute | solution.py:331
  31.4 7.8 %collective-permute-start.5 = (bf16[256,256]{1,0:T(8,128)(2,1)S(1)}, bf16[256,256]{1,0:T(8,128)(2,1)S(1)}, u32[]{:S(2)}, u32[]{:S(2)}) collective-permute-start(bf16[256,256]{1,0:T(8,128)(2,1)S(1)} %get-tuple-element.22), channel_id=1, source_target_pairs={{0,2},{2,3},{3,1},{1,0},{4,6},{6,7},{7,5},{5,4},{8,10},{10,11},{11... | collective-permute-start | bytes 393224 | tf_op jit(solution)/shard_map/ppermute | solution.py:331
  34.8 6.1 %collective-permute-start.6 = (bf16[256,256]{1,0:T(8,128)(2,1)S(1)}, bf16[256,256]{1,0:T(8,128)(2,1)S(1)}, u32[]{:S(2)}, u32[]{:S(2)}) collective-permute-start(bf16[256,256]{1,0:T(8,128)(2,1)S(1)} %get-tuple-element.23), channel_id=1, source_target_pairs={{0,2},{2,3},{3,1},{1,0},{4,6},{6,7},{7,5},{5,4},{8,10},{10,11},{11... | collective-permute-start | bytes 393224 | tf_op jit(solution)/shard_map/ppermute | solution.py:331
  35.5 6.9 %collective-permute-start.11 = (bf16[256,256]{1,0:T(8,128)(2,1)S(1)}, bf16[256,256]{1,0:T(8,128)(2,1)S(1)}, u32[]{:S(2)}, u32[]{:S(2)}) collective-permute-start(bf16[256,256]{1,0:T(8,128)(2,1)S(1)} %get-tuple-element.25), channel_id=1, source_target_pairs={{0,2},{2,3},{3,1},{1,0},{4,6},{6,7},{7,5},{5,4},{8,10},{10,11},{11... | collective-permute-start | bytes 393224 | tf_op jit(solution)/shard_map/ppermute | solution.py:331
  43.0 1.5 %collective-permute-start.12 = (f32[64,640]{1,0:T(8,128)S(1)}, f32[64,640]{1,0:T(8,128)S(1)}, u32[]{:S(2)}, u32[]{:S(2)}) collective-permute-start(f32[64,640]{1,0:T(8,128)S(1)} %get-tuple-element.30), channel_id=1, source_target_pairs={{4,0},{0,4},{5,1},{1,5},{6,2},{2,6},{7,3},{3,7},{12,8},{8,12},{13,... | collective-permute-start | bytes 491528 | tf_op jit(solution)/shard_map/ppermute | solution.py:349

commit v10 on v9

--- a/solution.py
+++ b/solution.py
@@ -13,6 +13,7 @@
 BF16 = jnp.bfloat16
 LANES = 128
 SCALE = HEAD_DIM**-0.5
+WEIGH_FLOPS = 6 * 10**9
 VMEM = pl.BlockSpec(memory_space=pltpu.VMEM)
 HBM = pl.BlockSpec(memory_space=pltpu.HBM)
 
@@ -114,32 +115,71 @@
     )[0]
 
 
-def attend_kernel(blocks, first, *refs):
-    marks, q_ref = refs[:blocks], refs[blocks]
-    keys, values = refs[blocks + 1 : 2 * blocks + 1], refs[2 * blocks + 1 : 3 * blocks + 1]
-    out_ref = refs[-1]
+def weigh_kernel(blocks, first, heads, fetches, *refs):
+    marks, q_ref, keys = refs[:blocks], refs[blocks], refs[blocks + 1 : 2 * blocks + 1]
+    rest = refs[2 * blocks + 1 :]
+    weight_ref, total_ref = rest[fetches : fetches + 2]
+    if fetches:
+        copy = pltpu.make_async_copy(rest[0], rest[-2], rest[-1])
+        copy.start()
     down = down_lanes(marks[0][...])
     same = jnp.concatenate([same_mark(down, m[...]) for m in marks], axis=1)
-    rows = q_ref.shape[0]
-    for h in range(out_ref.shape[1] // HEAD_DIM):
+    span = same.shape[1]
+    lane = lax.broadcasted_iota(jnp.int32, total_ref.shape, 1)
+    totals = jnp.zeros(total_ref.shape, F32)
+    for h in range(heads):
         at = head_columns(first + h)
         scores = jnp.concatenate([dot_t(q_ref[:, at], k[:, at]) for k in keys], axis=1)
         _, weights, total = softmax_block(scores, same)
-        rounded = weights.astype(BF16)
-        summed = sum(dot(rounded[:, i * rows : (i + 1) * rows], v[:, at]) for i, v in enumerate(values))
-        out_ref[:, head_columns(h)] = (summed / total).astype(BF16)
-
-
-def encoder_attend(query, keys, values, marks, first, heads):
-    rows = query.shape[0]
-    pairs = rows * rows * len(keys) * heads
-    return call(
-        functools.partial(attend_kernel, len(keys), first),
-        "encoder_attend",
+        weight_ref[:, h * span : (h + 1) * span] = weights.astype(BF16)
+        totals = jnp.where(lane == h, total, totals)
+    total_ref[...] = totals
+    if fetches:
+        copy.wait()
+
+
+def weigh(query, keys, marks, first, heads, fetched=None):
+    rows, span = query.shape[0], query.shape[0] * len(keys)
+    outs = [((rows, heads * span), BF16), ((rows, LANES), F32)]
+    operands = [*marks, query, *keys]
+    specs, scratch = [VMEM] * len(operands), []
+    if fetched is not None:
+        operands.append(pltpu.with_memory_space_constraint(fetched, pltpu.HBM))
+        specs.append(HBM)
+        outs.append((fetched.shape, fetched.dtype))
+        scratch.append(pltpu.SemaphoreType.DMA)
+    return call(
+        functools.partial(weigh_kernel, len(keys), first, heads, len(scratch)),
+        "weigh",
+        outs,
+        operands,
+        flops=WEIGH_FLOPS,
+        exps=rows * span * heads,
+        specs=specs,
+        scratch=scratch,
+    )
+
+
+def mix_kernel(first, heads, weight_ref, total_ref, *refs):
+    values, out_ref = refs[:-1], refs[-1]
+    rows = total_ref.shape[0]
+    for h in range(heads):
+        start = h * rows * len(values)
+        summed = sum(
+            dot(weight_ref[:, start + i * rows : start + (i + 1) * rows], v[:, head_columns(first + h)])
+            for i, v in enumerate(values)
+        )
+        out_ref[:, head_columns(h)] = (summed / total_ref[:, h : h + 1]).astype(BF16)
+
+
+def mix(weights, totals, values, first, heads):
+    rows = totals.shape[0]
+    return call(
+        functools.partial(mix_kernel, first, heads),
+        "mix",
         [((rows, heads * HEAD_DIM), BF16)],
-        [*marks, query, *keys, *values],
-        flops=4 * pairs * HEAD_DIM,
-        exps=pairs,
+        [weights, totals, *values],
+        flops=2 * weights.size * HEAD_DIM,
     )[0]
 
 
@@ -228,41 +268,60 @@
     )
 
 
-def cross_kernel(acc_ref, e_ref, map_ref, tgt_ref, mask_ref, *outs):
-    half = map_ref.shape[1] // 2
-    heads = half // HEAD_DIM
-    count = outs[0].shape[0]
-    chunk = e_ref[...]
-
-    def memory(at):
-        return (acc_ref[:, at] + dot(chunk, map_ref[:, at])).astype(BF16)
-
-    lane = lax.broadcasted_iota(jnp.int32, (tgt_ref.shape[0], LANES), 1)
+def cross_part(queries, keys, values, same, out_ref):
+    heads = len(keys)
+    lane = lax.broadcasted_iota(jnp.int32, (out_ref.shape[0], LANES), 1)
     stats = jnp.zeros(lane.shape, F32)
-    same = mask_ref[...] > 0
-    keys = [memory(head_columns(h)) for h in range(heads)]
-    values = [memory(head_columns(heads + h)) for h in range(heads)]
     for h in range(heads):
         at = head_columns(h)
-        top, weights, total = softmax_block(dot_t(tgt_ref[:, at], keys[h]), same)
-        summed = dot(weights.astype(BF16), values[h])
-        for i, out_ref in enumerate(outs):
-            out_ref[:, at] = summed[i * count : (i + 1) * count]
+        top, weights, total = softmax_block(dot_t(queries[:, at], keys[h]), same)
+        out_ref[:, at] = dot(weights.astype(BF16), values[h])
         stats = jnp.where(lane == h, top, jnp.where(lane == heads + h, total, stats))
+    out_ref[:, heads * HEAD_DIM :] = stats
+
+
+def cross_near_kernel(acc_ref, e_ref, map_ref, tgt_ref, mask_ref, mem_ref, *outs):
+    heads = map_ref.shape[1] // 2 // HEAD_DIM
+    chunk = e_ref[...]
+    memory = []
+    for h in range(2 * heads):
+        at = head_columns(h)
+        memory.append((acc_ref[:, at] + dot(chunk, map_ref[:, at])).astype(BF16))
+    count = outs[0].shape[0]
     for i, out_ref in enumerate(outs):
-        out_ref[:, half:] = stats[i * count : (i + 1) * count]
-
-
-def cross_attend(acc, chunk, maps, targets, mask, parts):
-    width = targets.shape[1]
-    count = targets.shape[0] // parts
-    return call(
-        cross_kernel,
-        "cross_attend",
-        [((count, width + LANES), F32)] * parts,
+        part = slice((i + 1) * count, (i + 2) * count)
+        cross_part(tgt_ref[part, :], memory[:heads], memory[heads:], mask_ref[part, :] > 0, out_ref)
+    for h in range(2 * heads):
+        mem_ref[:, head_columns(h)] = memory[h]
+
+
+def cross_near(acc, chunk, maps, targets, mask, parts):
+    rows, width = acc.shape[0], targets.shape[1]
+    return call(
+        cross_near_kernel,
+        "cross_near",
+        [((rows, 2 * width), BF16)] + [((targets.shape[0] // parts, width + LANES), F32)] * (parts - 1),
         [acc, chunk, maps, targets, mask],
         flops=2 * chunk.size * 2 * width,
     )
+
+
+def cross_own_kernel(mem_ref, tgt_ref, mask_ref, out_ref):
+    heads = mem_ref.shape[1] // 2 // HEAD_DIM
+    memory = [mem_ref[:, head_columns(h)] for h in range(2 * heads)]
+    part = slice(0, out_ref.shape[0])
+    cross_part(tgt_ref[part, :], memory[:heads], memory[heads:], mask_ref[part, :] > 0, out_ref)
+
+
+def cross_own(memory, targets, mask, parts):
+    width = targets.shape[1]
+    return call(
+        cross_own_kernel,
+        "cross_own",
+        [((targets.shape[0] // parts, width + LANES), F32)],
+        [memory, targets, mask],
+        flops=4 * targets.size * memory.shape[0] // parts,
+    )[0]
 
 
 def combine_kernel(*refs):
@@ -287,8 +346,8 @@
     bring = lambda x: [lax.ppermute(x, "ctx", pairs) for pairs in links]
 
     marks = (doc_ids if n_ctx == 2 else doc_ids + 1).reshape(1, rows)
-    keys, values, near_marks = bring(enc_key), bring(enc_value), bring(marks)
-    query, own_key, own_value, marks = fetch(enc_query, enc_key, enc_value, marks)
+    keys, near_marks, values = bring(enc_key), bring(marks), bring(enc_value)
+    query, own_key, marks = fetch(enc_query, enc_key, marks)
     near_targets = []
     if n_ctx == 2:
         own_maps = pack(key_map, value_map, tgt_query)
@@ -300,10 +359,19 @@
 
     chunks = 2
     heads = features // HEAD_DIM // chunks
-    held = [
-        encoder_attend(query, [own_key, *keys], [own_value, *values], [marks, *near_marks], j * heads, heads)
-        for j in range(chunks)
-    ]
+    held = [None] * chunks
+    own_value = None
+    for j in reversed(range(chunks)):
+        weights, totals, *fetched = weigh(
+            query,
+            [own_key, *keys],
+            [marks, *near_marks],
+            j * heads,
+            heads,
+            enc_value if own_value is None else None,
+        )
+        own_value = fetched[0] if fetched else own_value
+        held[j] = mix(weights, totals, [own_value, *values], j * heads, heads)
 
     order = ring_order(n_head)
     ring = [(order[i], order[(i + 1) % n_head]) for i in range(n_head)]
@@ -342,10 +410,10 @@
         near_targets,
         [marks, *near_marks],
     )
-    parts = cross_attend(acc, held[-1], last_maps, targets, mask, 1 + len(links))
-
-    combined = [parts[0]]
-    for i, (pairs, piece) in enumerate(zip(links, parts[1:])):
+    parts = 1 + len(links)
+    memory, *shares = cross_near(acc, held[-1], last_maps, targets, mask, parts)
+    combined = [cross_own(memory, targets, mask, parts)]
+    for i, (pairs, piece) in enumerate(zip(links, shares)):
         other = lax.ppermute(piece, "ctx", [(target, source) for source, target in pairs])
         if n_ctx > 2:
             end = n_ctx - 1 if i == 0 else 0

time: 45.5 us -> 45.3 us (level)
  waiting for transfers between devices: 13.1 us -> 11.9 us
  Pallas kernels: 9.91 us -> 10.9 us
    pallas_call x13 -> x16, Pallas kernels: 9.91 us -> 10.9 us  [call(): pl.pallas_call(kernel, in_specs=specs or [VMEM] * len(operands), out_spec...]
    ppermute x1, waiting for transfers between devices: 1.38 us -> 0.71 us  [on_device(): lax.ppermute(piece, 'ctx', [(target, source) for source, target in pairs])]
    ppermute x4, waiting for transfers between devices: 0.6 us -> 0.01 us  [on_device(): bring = lambda x: [lax.ppermute(x, 'ctx', pairs) for pairs in links]]
  transfers between devices with their start and end apart: 13 -> 13, of which waited for: 7 -> 6; matrix products, arithmetic and copies ran while one was open for 0% -> 0% of each run, Pallas kernels for 17% -> 20%
where the time goes in v10:
time: 45.3 us; the launch traced here: 45.1 us
  starting transfers between devices  22.2 us (49%)
  waiting for transfers between devices  11.9 us (26%)
  Pallas kernels  10.9 us (24%)
    ppermute x8, starting transfers between devices, on_device(): later = [lax.ppermute(p, 'head', ring) for p in pieces]  21 us
    ppermute x8, waiting for transfers between devices, on_device(): later = [lax.ppermute(p, 'head', ring) for p in pieces]  11.1 us
    pallas_call x16, Pallas kernels, call(): pl.pallas_call(kernel, in_specs=specs or [VMEM] * len(operands), out_spec...  10.9 us
    ppermute x4, starting transfers between devices, on_device(): bring = lambda x: [lax.ppermute(x, 'ctx', pairs) for pairs in links]  1.03 us
  transfers between devices with their start and end apart: 13, of which 6 were waited for; matrix products, arithmetic and copies ran while one was open for 0% of the time, Pallas kernels for 20%

profile of v10, /device:TPU:0, one launch (start us, length us, event | category | flops | bytes accessed | tf_op | source)
XLA Modules:
  0.0 45.1 jit_solution(14559061978010091649)
XLA Ops:
  1.0 1.2 %fetch.1 = (bf16[256,1024]{1,0:T(8,128)(2,1)S(1)}, bf16[256,1024]{1,0:T(8,128)(2,1)S(1)}, s32[1,256]{1,0:T(1,128)S(1)}) custom-call(bf16[256,1024]{1,0:T(8,128)(2,1)} %refs_0_.2, bf16[256,1024]{1,0:T(8,128)(2,1)} %refs_1_.2, s32[1,256]{1,0:T(1,128)} %bitcast.2), custom_call_target="tpu_custom_call" | custom-call | bytes 2099200 | tf_op jit(solution)/shard_map/fetch/pallas_call | solution.py:61
  2.2 1.1 %weigh.3 = (bf16[256,1024]{1,0:T(8,128)(2,1)S(1)}, f32[256,128]{1,0:T(8,128)S(1)}, bf16[256,1024]{1,0:T(8,128)(2,1)S(1)}) custom-call(s32[1,256]{1,0:T(1,128)S(1)} %get-tuple-element.22.refs_0_.refs_2_, s32[1,256]{1,0:T(1,128)S(1)} %collective-permute-done.refs_1_.refs_3_, bf16[256,1024]{1,0:T(8,128)(2,1)S(1)} %get-tuple-element.23.refs_2_, ...), custom_call_target="tpu_custom_call" | custom-call | flops 6000000000 | bytes 3278848 | tf_op jit(solution)/shard_map/weigh/pallas_call | solution.py:61
  3.6 4.0 %collective-permute-start.7 = (bf16[256,512]{1,0:T(8,128)(2,1)S(1)}, bf16[256,512]{1,0:T(8,128)(2,1)S(1)}, u32[]{:S(2)}, u32[]{:S(2)}) collective-permute-start(bf16[256,512]{1,0:T(8,128)(2,1)S(1)} %mix.3.refs_1_), channel_id=1, source_target_pairs={{0,2},{2,3},{3,1},{1,0},{4,6},{6,7},{7,5},{5,4},{8,10},{10,11},{11... | collective-permute-start | bytes 786440 | tf_op jit(solution)/shard_map/ppermute | solution.py:399
  8.5 1.6 %collective-permute-start.3 = (bf16[256,512]{1,0:T(8,128)(2,1)S(1)}, bf16[256,512]{1,0:T(8,128)(2,1)S(1)}, u32[]{:S(2)}, u32[]{:S(2)}) collective-permute-start(bf16[256,512]{1,0:T(8,128)(2,1)S(1)} %mix.2.refs_0_), channel_id=1, source_target_pairs={{0,2},{2,3},{3,1},{1,0},{4,6},{6,7},{7,5},{5,4},{8,10},{10,11},{11... | collective-permute-start | bytes 786440 | tf_op jit(solution)/shard_map/ppermute | solution.py:399
  10.1 4.2 %collective-permute-done.7.refs_1_ = bf16[256,512]{1,0:T(8,128)(2,1)S(1)} collective-permute-done((bf16[256,512]{1,0:T(8,128)(2,1)S(1)}, bf16[256,512]{1,0:T(8,128)(2,1)S(1)}, u32[]{:S(2)}, u32[]{:S(2)}) %collective-permute-start.7) | collective-permute-done | bytes 262176 | tf_op jit(solution)/shard_map/ppermute | solution.py:399
  14.3 3.4 %collective-permute-start.8 = (bf16[256,512]{1,0:T(8,128)(2,1)S(1)}, bf16[256,512]{1,0:T(8,128)(2,1)S(1)}, u32[]{:S(2)}, u32[]{:S(2)}) collective-permute-start(bf16[256,512]{1,0:T(8,128)(2,1)S(1)} %collective-permute-done.7.refs_1_), channel_id=1, source_target_pairs={{0,2},{2,3},{3,1},{1,0},{4,6},{6,7},{7,5},{5,4},{8,10},{10,11},{11... | collective-permute-start | bytes 786440 | tf_op jit(solution)/shard_map/ppermute | solution.py:399
  17.7 2.2 %pack.1.refs_2_.refs_3_.refs_0_ = bf16[4160,512]{1,0:T(8,128)(2,1)S(1)} custom-call(bf16[2048,512]{1,0:T(8,128)(2,1)} %refs_0_.3, bf16[2048,512]{1,0:T(8,128)(2,1)} %refs_1_.3, bf16[64,512]{1,0:T(8,128)(2,1)} %refs_2_.1), custom_call_target="tpu_custom_call" | custom-call | bytes 8519680 | tf_op jit(solution)/shard_map/pack/pallas_call | solution.py:61
  20.0 3.3 %collective-permute-start.4 = (bf16[256,512]{1,0:T(8,128)(2,1)S(1)}, bf16[256,512]{1,0:T(8,128)(2,1)S(1)}, u32[]{:S(2)}, u32[]{:S(2)}) collective-permute-start(bf16[256,512]{1,0:T(8,128)(2,1)S(1)} %collective-permute-done.3.refs_0_), channel_id=1, source_target_pairs={{0,2},{2,3},{3,1},{1,0},{4,6},{6,7},{7,5},{5,4},{8,10},{10,11},{11... | collective-permute-start | bytes 786440 | tf_op jit(solution)/shard_map/ppermute | solution.py:399
  23.3 2.2 %collective-permute-done.8.source.refs_1_ = bf16[256,512]{1,0:T(8,128)(2,1)S(1)} collective-permute-done((bf16[256,512]{1,0:T(8,128)(2,1)S(1)}, bf16[256,512]{1,0:T(8,128)(2,1)S(1)}, u32[]{:S(2)}, u32[]{:S(2)}) %collective-permute-start.8) | collective-permute-done | bytes 262176 | tf_op jit(solution)/shard_map/ppermute | solution.py:399
  25.5 3.4 %collective-permute-start.9 = (bf16[256,256]{1,0:T(8,128)(2,1)S(1)}, bf16[256,256]{1,0:T(8,128)(2,1)S(1)}, u32[]{:S(2)}, u32[]{:S(2)}) collective-permute-start(bf16[256,256]{1,0:T(8,128)(2,1)S(1)} %get-tuple-element.32), channel_id=1, source_target_pairs={{0,2},{2,3},{3,1},{1,0},{4,6},{6,7},{7,5},{5,4},{8,10},{10,11},{11... | collective-permute-start | bytes 393224 | tf_op jit(solution)/shard_map/ppermute | solution.py:399
  29.0 2.2 %collective-permute-done.4.source.refs_0_ = bf16[256,512]{1,0:T(8,128)(2,1)S(1)} collective-permute-done((bf16[256,512]{1,0:T(8,128)(2,1)S(1)}, bf16[256,512]{1,0:T(8,128)(2,1)S(1)}, u32[]{:S(2)}, u32[]{:S(2)}) %collective-permute-start.4) | collective-permute-done | bytes 262176 | tf_op jit(solution)/shard_map/ppermute | solution.py:399
  31.2 3.4 %collective-permute-start.5 = (bf16[256,256]{1,0:T(8,128)(2,1)S(1)}, bf16[256,256]{1,0:T(8,128)(2,1)S(1)}, u32[]{:S(2)}, u32[]{:S(2)}) collective-permute-start(bf16[256,256]{1,0:T(8,128)(2,1)S(1)} %get-tuple-element.28), channel_id=1, source_target_pairs={{0,2},{2,3},{3,1},{1,0},{4,6},{6,7},{7,5},{5,4},{8,10},{10,11},{11... | collective-permute-start | bytes 393224 | tf_op jit(solution)/shard_map/ppermute | solution.py:399
  34.6 0.7 %collective-permute-start.6 = (bf16[256,256]{1,0:T(8,128)(2,1)S(1)}, bf16[256,256]{1,0:T(8,128)(2,1)S(1)}, u32[]{:S(2)}, u32[]{:S(2)}) collective-permute-start(bf16[256,256]{1,0:T(8,128)(2,1)S(1)} %get-tuple-element.29), channel_id=1, source_target_pairs={{0,2},{2,3},{3,1},{1,0},{4,6},{6,7},{7,5},{5,4},{8,10},{10,11},{11... | collective-permute-start | bytes 393224 | tf_op jit(solution)/shard_map/ppermute | solution.py:399
  35.3 1.2 %collective-permute-start.11 = (bf16[256,256]{1,0:T(8,128)(2,1)S(1)}, bf16[256,256]{1,0:T(8,128)(2,1)S(1)}, u32[]{:S(2)}, u32[]{:S(2)}) collective-permute-start(bf16[256,256]{1,0:T(8,128)(2,1)S(1)} %get-tuple-element.33), channel_id=1, source_target_pairs={{0,2},{2,3},{3,1},{1,0},{4,6},{6,7},{7,5},{5,4},{8,10},{10,11},{11... | collective-permute-start | bytes 393224 | tf_op jit(solution)/shard_map/ppermute | solution.py:399
  36.7 0.7 %project.4.refs_4_ = f32[256,1024]{1,0:T(8,128)S(1)} custom-call(bf16[256,512]{1,0:T(8,128)(2,1)S(1)} %mix.2.refs_0_, bf16[256,512]{1,0:T(8,128)(2,1)S(1)} %mix.3.refs_1_, bf16[4160,512]{1,0:T(8,128)(2,1)S(1)} %pack.1.refs_2_.refs_3_.refs_0_, bf16[4160,512]{1,0:T(8,128)(2,1)S(1)} %collective-permute-done.10.refs_3_.refs_4_.refs_1_), custom_call_target="tpu_custom_call" | custom-call | flops 536870912 | bytes 10092544 | tf_op jit(solution)/shard_map/project/pallas_call | solution.py:61
  37.4 0.7 %project.5.refs_4_ = f32[256,1024]{1,0:T(8,128)S(1)} custom-call(bf16[256,512]{1,0:T(8,128)(2,1)S(1)} %collective-permute-done.3.refs_0_, bf16[256,512]{1,0:T(8,128)(2,1)S(1)} %collective-permute-done.7.refs_1_, bf16[4160,512]{1,0:T(8,128)(2,1)S(1)} %pack.1.refs_2_.refs_3_.refs_0_, bf16[4160,512]{1,0:T(8,128)(2,1)S(1)} %collective-permute-done.10.refs_3_.refs_4_.refs_1_, ...), custom_call_target="tpu_custom_call" | custom-call | flops 536870912 | bytes 11141120 | tf_op jit(solution)/shard_map/project/pallas_call | solution.py:61
  38.2 0.7 %project.6.refs_5_ = f32[256,1024]{1,0:T(8,128)S(1)} custom-call(bf16[256,512]{1,0:T(8,128)(2,1)S(1)} %collective-permute-done.4.source.refs_0_, bf16[256,512]{1,0:T(8,128)(2,1)S(1)} %collective-permute-done.8.source.refs_1_, bf16[4160,512]{1,0:T(8,128)(2,1)S(1)} %pack.1.refs_2_.refs_3_.refs_0_, ...), custom_call_target="tpu_custom_call" | custom-call | flops 536870912 | bytes 11141120 | tf_op jit(solution)/shard_map/project/pallas_call | solution.py:61
  39.0 1.8 %collective-permute-done.6.refs_1_ = bf16[256,256]{1,0:T(8,128)(2,1)S(1)} collective-permute-done((bf16[256,256]{1,0:T(8,128)(2,1)S(1)}, bf16[256,256]{1,0:T(8,128)(2,1)S(1)}, u32[]{:S(2)}, u32[]{:S(2)}) %collective-permute-start.6) | collective-permute-done | bytes 131104 | tf_op jit(solution)/shard_map/ppermute | solution.py:399
  40.7 0.6 %project.7.acc_ref = f32[256,1024]{1,0:T(8,128)S(1)} custom-call(bf16[256,256]{1,0:T(8,128)(2,1)S(1)} %collective-permute-done.5.refs_0_, bf16[256,256]{1,0:T(8,128)(2,1)S(1)} %collective-permute-done.6.refs_1_, bf16[256,256]{1,0:T(8,128)(2,1)S(1)} %collective-permute-done.9.refs_2_, bf16[4160,512]{1,0:T(8,128)(2,1)S(1)} %pack.1.refs_2_.refs_3_.refs_0_, ...), custom_call_target="tpu_custom_call" | custom-call | flops 402653184 | bytes 11010048 | tf_op jit(solution)/shard_map/project/pallas_call | solution.py:61
  41.3 0.8 %collective-permute-done.11.e_ref = bf16[256,256]{1,0:T(8,128)(2,1)S(1)} collective-permute-done((bf16[256,256]{1,0:T(8,128)(2,1)S(1)}, bf16[256,256]{1,0:T(8,128)(2,1)S(1)}, u32[]{:S(2)}, u32[]{:S(2)}) %collective-permute-start.11) | collective-permute-done | bytes 131104 | tf_op jit(solution)/shard_map/ppermute | solution.py:399
  42.1 0.7 %cross_near.1 = (bf16[256,1024]{1,0:T(8,128)(2,1)S(1)}, f32[64,640]{1,0:T(8,128)S(1)}) custom-call(f32[256,1024]{1,0:T(8,128)S(1)} %project.7.acc_ref, bf16[256,256]{1,0:T(8,128)(2,1)S(1)} %collective-permute-done.11.e_ref, bf16[256,1024]{1,0:T(8,128)(2,1)S(1)} %get-tuple-element.34.map_ref, bf16[128,512]{1,0:T(8,128)(2,1)S(1)} %get-tuple-element.35.tgt_ref, ...), custom_call_target="tpu_custom_call" | custom-call | flops 134217728 | bytes 2654208 | tf_op jit(solution)/shard_map/cross_near/pallas_call | solution.py:61
  42.9 0.7 %cross_own.1.refs_0_ = f32[64,640]{1,0:T(8,128)S(1)} custom-call(bf16[256,1024]{1,0:T(8,128)(2,1)S(1)} %get-tuple-element.37.mem_ref, bf16[128,512]{1,0:T(8,128)(2,1)S(1)} %get-tuple-element.35.tgt_ref, f32[128,256]{1,0:T(8,128)S(1)} %get-tuple-element.36.mask_ref), custom_call_target="tpu_custom_call" | custom-call | flops 33554432 | bytes 950272 | tf_op jit(solution)/shard_map/cross_own/pallas_call | solution.py:61
  43.5 0.7 %collective-permute-done.12.refs_1_ = f32[64,640]{1,0:T(8,128)S(1)} collective-permute-done((f32[64,640]{1,0:T(8,128)S(1)}, f32[64,640]{1,0:T(8,128)S(1)}, u32[]{:S(2)}, u32[]{:S(2)}) %collective-permute-start.12) | collective-permute-done | bytes 163872 | tf_op jit(solution)/shard_map/ppermute | solution.py:417
  44.2 0.8 %combine.1 = bf16[64,512]{1,0:T(8,128)(2,1)} custom-call(f32[64,640]{1,0:T(8,128)S(1)} %cross_own.1.refs_0_, f32[64,640]{1,0:T(8,128)S(1)} %collective-permute-done.12.refs_1_), custom_call_target="tpu_custom_call" | custom-call | bytes 393216 | tf_op jit(solution)/shard_map/combine/pallas_call | solution.py:61
  (18 shorter events, 2.5 us)
Async XLA Ops:
  0.0 2.2 %collective-permute-start.1 = (bf16[256,1024]{1,0:T(8,128)(2,1)}, bf16[256,1024]{1,0:T(8,128)(2,1)S(1)}, u32[]{:S(2)}, u32[]{:S(2)}) collective-permute-start(bf16[256,1024]{1,0:T(8,128)(2,1)} %refs_1_.2), channel_id=1, source_target_pairs={{0,4},{4,0},{1,5},{5,1},{2,6},{6,2},{3,7},{7,3},{8,12},{12,8},{9,1... | collective-permute-start | bytes 1572872 | tf_op jit(solution)/shard_map/ppermute | solution.py:346
  0.5 1.7 %collective-permute-start = (s32[1,256]{1,0:T(1,128)}, s32[1,256]{1,0:T(1,128)S(1)}, u32[]{:S(2)}, u32[]{:S(2)}) collective-permute-start(s32[1,256]{1,0:T(1,128)} %bitcast.1), channel_id=1, source_target_pairs={{0,4},{4,0},{1,5},{5,1},{2,6},{6,2},{3,7},{7,3},{8,12},{12,8},{9,1... | collective-permute-start | bytes 3080 | tf_op jit(solution)/shard_map/ppermute | solution.py:346
  0.5 2.8 %collective-permute-start.2 = (bf16[256,1024]{1,0:T(8,128)(2,1)}, bf16[256,1024]{1,0:T(8,128)(2,1)S(1)}, u32[]{:S(2)}, u32[]{:S(2)}) collective-permute-start(bf16[256,1024]{1,0:T(8,128)(2,1)} %refs_5_.1), channel_id=1, source_target_pairs={{0,4},{4,0},{1,5},{5,1},{2,6},{6,2},{3,7},{7,3},{8,12},{12,8},{9,1... | collective-permute-start | bytes 1572872 | tf_op jit(solution)/shard_map/ppermute | solution.py:346
  3.6 10.7 %collective-permute-start.7 = (bf16[256,512]{1,0:T(8,128)(2,1)S(1)}, bf16[256,512]{1,0:T(8,128)(2,1)S(1)}, u32[]{:S(2)}, u32[]{:S(2)}) collective-permute-start(bf16[256,512]{1,0:T(8,128)(2,1)S(1)} %mix.3.refs_1_), channel_id=1, source_target_pairs={{0,2},{2,3},{3,1},{1,0},{4,6},{6,7},{7,5},{5,4},{8,10},{10,11},{11... | collective-permute-start | bytes 786440 | tf_op jit(solution)/shard_map/ppermute | solution.py:399
  8.5 11.5 %collective-permute-start.3 = (bf16[256,512]{1,0:T(8,128)(2,1)S(1)}, bf16[256,512]{1,0:T(8,128)(2,1)S(1)}, u32[]{:S(2)}, u32[]{:S(2)}) collective-permute-start(bf16[256,512]{1,0:T(8,128)(2,1)S(1)} %mix.2.refs_0_), channel_id=1, source_target_pairs={{0,2},{2,3},{3,1},{1,0},{4,6},{6,7},{7,5},{5,4},{8,10},{10,11},{11... | collective-permute-start | bytes 786440 | tf_op jit(solution)/shard_map/ppermute | solution.py:399
  14.3 11.2 %collective-permute-start.8 = (bf16[256,512]{1,0:T(8,128)(2,1)S(1)}, bf16[256,512]{1,0:T(8,128)(2,1)S(1)}, u32[]{:S(2)}, u32[]{:S(2)}) collective-permute-start(bf16[256,512]{1,0:T(8,128)(2,1)S(1)} %collective-permute-done.7.refs_1_), channel_id=1, source_target_pairs={{0,2},{2,3},{3,1},{1,0},{4,6},{6,7},{7,5},{5,4},{8,10},{10,11},{11... | collective-permute-start | bytes 786440 | tf_op jit(solution)/shard_map/ppermute | solution.py:399
  19.9 16.6 %collective-permute-start.10 = (bf16[4160,512]{1,0:T(8,128)(2,1)S(1)}, bf16[4160,512]{1,0:T(8,128)(2,1)S(1)}, u32[]{:S(2)}, u32[]{:S(2)}) collective-permute-start(bf16[4160,512]{1,0:T(8,128)(2,1)S(1)} %pack.1.refs_2_.refs_3_.refs_0_), channel_id=1, source_target_pairs={{0,4},{4,0},{1,5},{5,1},{2,6},{6,2},{3,7},{7,3},{8,12},{12,8},{9,1... | collective-permute-start | bytes 12779528 | tf_op jit(solution)/shard_map/ppermute | solution.py:346
  20.0 11.1 %collective-permute-start.4 = (bf16[256,512]{1,0:T(8,128)(2,1)S(1)}, bf16[256,512]{1,0:T(8,128)(2,1)S(1)}, u32[]{:S(2)}, u32[]{:S(2)}) collective-permute-start(bf16[256,512]{1,0:T(8,128)(2,1)S(1)} %collective-permute-done.3.refs_0_), channel_id=1, source_target_pairs={{0,2},{2,3},{3,1},{1,0},{4,6},{6,7},{7,5},{5,4},{8,10},{10,11},{11... | collective-permute-start | bytes 786440 | tf_op jit(solution)/shard_map/ppermute | solution.py:399
  25.5 13.4 %collective-permute-start.9 = (bf16[256,256]{1,0:T(8,128)(2,1)S(1)}, bf16[256,256]{1,0:T(8,128)(2,1)S(1)}, u32[]{:S(2)}, u32[]{:S(2)}) collective-permute-start(bf16[256,256]{1,0:T(8,128)(2,1)S(1)} %get-tuple-element.32), channel_id=1, source_target_pairs={{0,2},{2,3},{3,1},{1,0},{4,6},{6,7},{7,5},{5,4},{8,10},{10,11},{11... | collective-permute-start | bytes 393224 | tf_op jit(solution)/shard_map/ppermute | solution.py:399
  31.2 7.8 %collective-permute-start.5 = (bf16[256,256]{1,0:T(8,128)(2,1)S(1)}, bf16[256,256]{1,0:T(8,128)(2,1)S(1)}, u32[]{:S(2)}, u32[]{:S(2)}) collective-permute-start(bf16[256,256]{1,0:T(8,128)(2,1)S(1)} %get-tuple-element.28), channel_id=1, source_target_pairs={{0,2},{2,3},{3,1},{1,0},{4,6},{6,7},{7,5},{5,4},{8,10},{10,11},{11... | collective-permute-start | bytes 393224 | tf_op jit(solution)/shard_map/ppermute | solution.py:399
  34.6 6.1 %collective-permute-start.6 = (bf16[256,256]{1,0:T(8,128)(2,1)S(1)}, bf16[256,256]{1,0:T(8,128)(2,1)S(1)}, u32[]{:S(2)}, u32[]{:S(2)}) collective-permute-start(bf16[256,256]{1,0:T(8,128)(2,1)S(1)} %get-tuple-element.29), channel_id=1, source_target_pairs={{0,2},{2,3},{3,1},{1,0},{4,6},{6,7},{7,5},{5,4},{8,10},{10,11},{11... | collective-permute-start | bytes 393224 | tf_op jit(solution)/shard_map/ppermute | solution.py:399
  35.3 6.9 %collective-permute-start.11 = (bf16[256,256]{1,0:T(8,128)(2,1)S(1)}, bf16[256,256]{1,0:T(8,128)(2,1)S(1)}, u32[]{:S(2)}, u32[]{:S(2)}) collective-permute-start(bf16[256,256]{1,0:T(8,128)(2,1)S(1)} %get-tuple-element.33), channel_id=1, source_target_pairs={{0,2},{2,3},{3,1},{1,0},{4,6},{6,7},{7,5},{5,4},{8,10},{10,11},{11... | collective-permute-start | bytes 393224 | tf_op jit(solution)/shard_map/ppermute | solution.py:399
  42.8 1.5 %collective-permute-start.12 = (f32[64,640]{1,0:T(8,128)S(1)}, f32[64,640]{1,0:T(8,128)S(1)}, u32[]{:S(2)}, u32[]{:S(2)}) collective-permute-start(f32[64,640]{1,0:T(8,128)S(1)} %get-tuple-element.38), channel_id=1, source_target_pairs={{4,0},{0,4},{5,1},{1,5},{6,2},{2,6},{7,3},{3,7},{12,8},{8,12},{13,... | collective-permute-start | bytes 491528 | tf_op jit(solution)/shard_map/ppermute | solution.py:417

commit v11 on v10

--- a/solution.py
+++ b/solution.py
@@ -70,13 +70,30 @@
     )(*operands)
 
 
-def fetch_kernel(count, *refs):
-    sources, targets, sems = refs[:count], refs[count : 2 * count], refs[-1]
-    copies = [pltpu.make_async_copy(s, t, sems.at[i]) for i, (s, t) in enumerate(zip(sources, targets))]
+def copies_of(source, target, sems, first, parts=4):
+    rows = source.shape[0]
+    parts = parts if rows % (16 * parts) == 0 else 1
+    step = rows // parts
+    made = []
+    for i in range(parts):
+        at = pl.ds(i * step, step)
+        made.append(pltpu.make_async_copy(source.at[at, :], target.at[at, :], sems.at[first + i]))
+    return made
+
+
+def run_all(copies):
     for copy in copies:
         copy.start()
     for copy in copies:
         copy.wait()
+
+
+def fetch_kernel(count, *refs):
+    sources, targets, sems = refs[:count], refs[count : 2 * count], refs[-1]
+    copies = []
+    for source, target in zip(sources, targets):
+        copies += copies_of(source, target, sems, len(copies))
+    run_all(copies)
 
 
 def fetch(*arrays):
@@ -86,21 +103,18 @@
         [(x.shape, x.dtype) for x in arrays],
         [pltpu.with_memory_space_constraint(x, pltpu.HBM) for x in arrays],
         specs=[HBM] * len(arrays),
-        scratch=[pltpu.SemaphoreType.DMA((len(arrays),))],
+        scratch=[pltpu.SemaphoreType.DMA((4 * len(arrays),))],
     )
 
 
 def pack_kernel(*refs):
     sources, out_ref, sems = refs[:-2], refs[-2], refs[-1]
     copies, row = [], 0
-    for i, source in enumerate(sources):
+    for source in sources:
         rows = source.shape[0]
-        copies.append(pltpu.make_async_copy(source, out_ref.at[pl.ds(row, rows), :], sems.at[i]))
+        copies += copies_of(source, out_ref.at[pl.ds(row, rows), :], sems, len(copies))
         row += rows
-    for copy in copies:
-        copy.start()
-    for copy in copies:
-        copy.wait()
+    run_all(copies)
 
 
 def pack(*arrays):
@@ -111,7 +125,7 @@
         [((rows, arrays[0].shape[1]), arrays[0].dtype)],
         [pltpu.with_memory_space_constraint(x, pltpu.HBM) for x in arrays],
         specs=[HBM] * len(arrays),
-        scratch=[pltpu.SemaphoreType.DMA((len(arrays),))],
+        scratch=[pltpu.SemaphoreType.DMA((4 * len(arrays),))],
     )[0]
 
 
@@ -120,8 +134,9 @@
     rest = refs[2 * blocks + 1 :]
     weight_ref, total_ref = rest[fetches : fetches + 2]
     if fetches:
-        copy = pltpu.make_async_copy(rest[0], rest[-2], rest[-1])
-        copy.start()
+        copies = copies_of(rest[0], rest[-2], rest[-1], 0)
+        for copy in copies:
+            copy.start()
     down = down_lanes(marks[0][...])
     same = jnp.concatenate([same_mark(down, m[...]) for m in marks], axis=1)
     span = same.shape[1]
@@ -135,7 +150,8 @@
         totals = jnp.where(lane == h, total, totals)
     total_ref[...] = totals
     if fetches:
-        copy.wait()
+        for copy in copies:
+            copy.wait()
 
 
 def weigh(query, keys, marks, first, heads, fetched=None):
@@ -147,7 +163,7 @@
         operands.append(pltpu.with_memory_space_constraint(fetched, pltpu.HBM))
         specs.append(HBM)
         outs.append((fetched.shape, fetched.dtype))
-        scratch.append(pltpu.SemaphoreType.DMA)
+        scratch.append(pltpu.SemaphoreType.DMA((4,)))
     return call(
         functools.partial(weigh_kernel, len(keys), first, heads, len(scratch)),
         "weigh",
@@ -268,60 +284,39 @@
     )
 
 
-def cross_part(queries, keys, values, same, out_ref):
-    heads = len(keys)
-    lane = lax.broadcasted_iota(jnp.int32, (out_ref.shape[0], LANES), 1)
-    stats = jnp.zeros(lane.shape, F32)
-    for h in range(heads):
-        at = head_columns(h)
-        top, weights, total = softmax_block(dot_t(queries[:, at], keys[h]), same)
-        out_ref[:, at] = dot(weights.astype(BF16), values[h])
-        stats = jnp.where(lane == h, top, jnp.where(lane == heads + h, total, stats))
-    out_ref[:, heads * HEAD_DIM :] = stats
-
-
-def cross_near_kernel(acc_ref, e_ref, map_ref, tgt_ref, mask_ref, mem_ref, *outs):
+def cross_kernel(acc_ref, e_ref, map_ref, tgt_ref, mask_ref, *outs):
     heads = map_ref.shape[1] // 2 // HEAD_DIM
     chunk = e_ref[...]
     memory = []
     for h in range(2 * heads):
         at = head_columns(h)
         memory.append((acc_ref[:, at] + dot(chunk, map_ref[:, at])).astype(BF16))
+    keys, values = memory[:heads], memory[heads:]
     count = outs[0].shape[0]
+    same = mask_ref[...] > 0
+    lane = lax.broadcasted_iota(jnp.int32, (same.shape[0], LANES), 1)
+    stats = jnp.zeros(lane.shape, F32)
+    for h in range(heads):
+        at = head_columns(h)
+        top, weights, total = softmax_block(dot_t(tgt_ref[:, at], keys[h]), same)
+        summed = dot(weights.astype(BF16), values[h])
+        for i, out_ref in enumerate(outs):
+            out_ref[:, at] = summed[i * count : (i + 1) * count]
+        stats = jnp.where(lane == h, top, jnp.where(lane == heads + h, total, stats))
     for i, out_ref in enumerate(outs):
-        part = slice((i + 1) * count, (i + 2) * count)
-        cross_part(tgt_ref[part, :], memory[:heads], memory[heads:], mask_ref[part, :] > 0, out_ref)
-    for h in range(2 * heads):
-        mem_ref[:, head_columns(h)] = memory[h]
-
-
-def cross_near(acc, chunk, maps, targets, mask, parts):
-    rows, width = acc.shape[0], targets.shape[1]
-    return call(
-        cross_near_kernel,
-        "cross_near",
-        [((rows, 2 * width), BF16)] + [((targets.shape[0] // parts, width + LANES), F32)] * (parts - 1),
+        out_ref[:, heads * HEAD_DIM :] = stats[i * count : (i + 1) * count]
+
+
+def cross_attend(acc, chunk, maps, targets, mask, parts):
+    width = targets.shape[1]
+    count = targets.shape[0] // parts
+    return call(
+        cross_kernel,
+        "cross_attend",
+        [((count, width + LANES), F32)] * parts,
         [acc, chunk, maps, targets, mask],
         flops=2 * chunk.size * 2 * width,
     )
-
-
-def cross_own_kernel(mem_ref, tgt_ref, mask_ref, out_ref):
-    heads = mem_ref.shape[1] // 2 // HEAD_DIM
-    memory = [mem_ref[:, head_columns(h)] for h in range(2 * heads)]
-    part = slice(0, out_ref.shape[0])
-    cross_part(tgt_ref[part, :], memory[:heads], memory[heads:], mask_ref[part, :] > 0, out_ref)
-
-
-def cross_own(memory, targets, mask, parts):
-    width = targets.shape[1]
-    return call(
-        cross_own_kernel,
-        "cross_own",
-        [((targets.shape[0] // parts, width + LANES), F32)],
-        [memory, targets, mask],
-        flops=4 * targets.size * memory.shape[0] // parts,
-    )[0]
 
 
 def combine_kernel(*refs):
@@ -410,9 +405,8 @@
         near_targets,
         [marks, *near_marks],
     )
-    parts = 1 + len(links)
-    memory, *shares = cross_near(acc, held[-1], last_maps, targets, mask, parts)
-    combined = [cross_own(memory, targets, mask, parts)]
+    own, *shares = cross_attend(acc, held[-1], last_maps, targets, mask, 1 + len(links))
+    combined = [own]
     for i, (pairs, piece) in enumerate(zip(links, shares)):
         other = lax.ppermute(piece, "ctx", [(target, source) for source, target in pairs])
         if n_ctx > 2:

time: 45.3 us -> 45.7 us (level)
  waiting for transfers between devices: 11.9 us -> 12.5 us
    ppermute x1, waiting for transfers between devices: 0.71 us -> 1.38 us  [on_device(): lax.ppermute(piece, 'ctx', [(target, source) for source, target in pairs])]
    pallas_call x16 -> x15, Pallas kernels: 10.9 us -> 10.8 us  [call(): pl.pallas_call(kernel, in_specs=specs or [VMEM] * len(operands), out_spec...]
where the time goes in v11:
time: 45.7 us; the launch traced here: 45.5 us
  starting transfers between devices  22 us (48%)
  waiting for transfers between devices  12.5 us (27%)
  Pallas kernels  10.8 us (24%)
    ppermute x8, starting transfers between devices, on_device(): later = [lax.ppermute(p, 'head', ring) for p in pieces]  20.9 us
    ppermute x8, waiting for transfers between devices, on_device(): later = [lax.ppermute(p, 'head', ring) for p in pieces]  11.1 us
    pallas_call x15, Pallas kernels, call(): pl.pallas_call(kernel, in_specs=specs or [VMEM] * len(operands), out_spec...  10.8 us
    ppermute x1, waiting for transfers between devices, on_device(): lax.ppermute(piece, 'ctx', [(target, source) for source, target in pairs])  1.38 us
    ppermute x4, starting transfers between devices, on_device(): bring = lambda x: [lax.ppermute(x, 'ctx', pairs) for pairs in links]  1.03 us
  transfers between devices with their start and end apart: 13, of which 6 were waited for; matrix products, arithmetic and copies ran while one was open for 0% of the time, Pallas kernels for 20%

profile of v11, /device:TPU:0, one launch (start us, length us, event | category | flops | bytes accessed | tf_op | source)
XLA Modules:
  0.0 45.5 jit_solution(3603712882787694575)
XLA Ops:
  1.0 1.4 %fetch.1 = (bf16[256,1024]{1,0:T(8,128)(2,1)S(1)}, bf16[256,1024]{1,0:T(8,128)(2,1)S(1)}, s32[1,256]{1,0:T(1,128)S(1)}) custom-call(bf16[256,1024]{1,0:T(8,128)(2,1)} %refs_0_.2, bf16[256,1024]{1,0:T(8,128)(2,1)} %refs_1_.2, s32[1,256]{1,0:T(1,128)} %bitcast.2), custom_call_target="tpu_custom_call" | custom-call | bytes 2099200 | tf_op jit(solution)/shard_map/fetch/pallas_call | solution.py:61
  2.4 1.5 %weigh.3 = (bf16[256,1024]{1,0:T(8,128)(2,1)S(1)}, f32[256,128]{1,0:T(8,128)S(1)}, bf16[256,1024]{1,0:T(8,128)(2,1)S(1)}) custom-call(s32[1,256]{1,0:T(1,128)S(1)} %get-tuple-element.22.refs_0_.refs_2_, s32[1,256]{1,0:T(1,128)S(1)} %collective-permute-done.refs_1_.refs_3_, bf16[256,1024]{1,0:T(8,128)(2,1)S(1)} %get-tuple-element.23.refs_2_, ...), custom_call_target="tpu_custom_call" | custom-call | flops 6000000000 | bytes 3278848 | tf_op jit(solution)/shard_map/weigh/pallas_call | solution.py:61
  4.2 3.8 %collective-permute-start.7 = (bf16[256,512]{1,0:T(8,128)(2,1)S(1)}, bf16[256,512]{1,0:T(8,128)(2,1)S(1)}, u32[]{:S(2)}, u32[]{:S(2)}) collective-permute-start(bf16[256,512]{1,0:T(8,128)(2,1)S(1)} %mix.3.refs_1_), channel_id=1, source_target_pairs={{0,2},{2,3},{3,1},{1,0},{4,6},{6,7},{7,5},{5,4},{8,10},{10,11},{11... | collective-permute-start | bytes 786440 | tf_op jit(solution)/shard_map/ppermute | solution.py:394
  8.0 0.5 %weigh.2 = (bf16[256,1024]{1,0:T(8,128)(2,1)S(1)}, f32[256,128]{1,0:T(8,128)S(1)}) custom-call(s32[1,256]{1,0:T(1,128)S(1)} %get-tuple-element.22.refs_0_.refs_2_, s32[1,256]{1,0:T(1,128)S(1)} %collective-permute-done.refs_1_.refs_3_, bf16[256,1024]{1,0:T(8,128)(2,1)S(1)} %get-tuple-element.23.refs_2_, bf16[256,1024]{1,0:T(8,128)(2,1)S(1)} %get-tuple-element.24.refs_3_, ...), custom_call_target="tpu_custom_call" | custom-call | flops 6000000000 | bytes 2230272 | tf_op jit(solution)/shard_map/weigh/pallas_call | solution.py:61
  8.9 1.6 %collective-permute-start.3 = (bf16[256,512]{1,0:T(8,128)(2,1)S(1)}, bf16[256,512]{1,0:T(8,128)(2,1)S(1)}, u32[]{:S(2)}, u32[]{:S(2)}) collective-permute-start(bf16[256,512]{1,0:T(8,128)(2,1)S(1)} %mix.2.refs_0_), channel_id=1, source_target_pairs={{0,2},{2,3},{3,1},{1,0},{4,6},{6,7},{7,5},{5,4},{8,10},{10,11},{11... | collective-permute-start | bytes 786440 | tf_op jit(solution)/shard_map/ppermute | solution.py:394
  10.5 4.1 %collective-permute-done.7.refs_1_ = bf16[256,512]{1,0:T(8,128)(2,1)S(1)} collective-permute-done((bf16[256,512]{1,0:T(8,128)(2,1)S(1)}, bf16[256,512]{1,0:T(8,128)(2,1)S(1)}, u32[]{:S(2)}, u32[]{:S(2)}) %collective-permute-start.7) | collective-permute-done | bytes 262176 | tf_op jit(solution)/shard_map/ppermute | solution.py:394
  14.7 3.4 %collective-permute-start.8 = (bf16[256,512]{1,0:T(8,128)(2,1)S(1)}, bf16[256,512]{1,0:T(8,128)(2,1)S(1)}, u32[]{:S(2)}, u32[]{:S(2)}) collective-permute-start(bf16[256,512]{1,0:T(8,128)(2,1)S(1)} %collective-permute-done.7.refs_1_), channel_id=1, source_target_pairs={{0,2},{2,3},{3,1},{1,0},{4,6},{6,7},{7,5},{5,4},{8,10},{10,11},{11... | collective-permute-start | bytes 786440 | tf_op jit(solution)/shard_map/ppermute | solution.py:394
  18.0 2.3 %pack.1.refs_2_.refs_3_.refs_0_ = bf16[4160,512]{1,0:T(8,128)(2,1)S(1)} custom-call(bf16[2048,512]{1,0:T(8,128)(2,1)} %refs_0_.3, bf16[2048,512]{1,0:T(8,128)(2,1)} %refs_1_.3, bf16[64,512]{1,0:T(8,128)(2,1)} %refs_2_.1), custom_call_target="tpu_custom_call" | custom-call | bytes 8519680 | tf_op jit(solution)/shard_map/pack/pallas_call | solution.py:61
  20.4 3.3 %collective-permute-start.4 = (bf16[256,512]{1,0:T(8,128)(2,1)S(1)}, bf16[256,512]{1,0:T(8,128)(2,1)S(1)}, u32[]{:S(2)}, u32[]{:S(2)}) collective-permute-start(bf16[256,512]{1,0:T(8,128)(2,1)S(1)} %collective-permute-done.3.refs_0_), channel_id=1, source_target_pairs={{0,2},{2,3},{3,1},{1,0},{4,6},{6,7},{7,5},{5,4},{8,10},{10,11},{11... | collective-permute-start | bytes 786440 | tf_op jit(solution)/shard_map/ppermute | solution.py:394
  23.7 2.2 %collective-permute-done.8.source.refs_1_ = bf16[256,512]{1,0:T(8,128)(2,1)S(1)} collective-permute-done((bf16[256,512]{1,0:T(8,128)(2,1)S(1)}, bf16[256,512]{1,0:T(8,128)(2,1)S(1)}, u32[]{:S(2)}, u32[]{:S(2)}) %collective-permute-start.8) | collective-permute-done | bytes 262176 | tf_op jit(solution)/shard_map/ppermute | solution.py:394
  25.9 3.4 %collective-permute-start.9 = (bf16[256,256]{1,0:T(8,128)(2,1)S(1)}, bf16[256,256]{1,0:T(8,128)(2,1)S(1)}, u32[]{:S(2)}, u32[]{:S(2)}) collective-permute-start(bf16[256,256]{1,0:T(8,128)(2,1)S(1)} %get-tuple-element.32), channel_id=1, source_target_pairs={{0,2},{2,3},{3,1},{1,0},{4,6},{6,7},{7,5},{5,4},{8,10},{10,11},{11... | collective-permute-start | bytes 393224 | tf_op jit(solution)/shard_map/ppermute | solution.py:394
  29.4 2.2 %collective-permute-done.4.source.refs_0_ = bf16[256,512]{1,0:T(8,128)(2,1)S(1)} collective-permute-done((bf16[256,512]{1,0:T(8,128)(2,1)S(1)}, bf16[256,512]{1,0:T(8,128)(2,1)S(1)}, u32[]{:S(2)}, u32[]{:S(2)}) %collective-permute-start.4) | collective-permute-done | bytes 262176 | tf_op jit(solution)/shard_map/ppermute | solution.py:394
  31.5 3.4 %collective-permute-start.5 = (bf16[256,256]{1,0:T(8,128)(2,1)S(1)}, bf16[256,256]{1,0:T(8,128)(2,1)S(1)}, u32[]{:S(2)}, u32[]{:S(2)}) collective-permute-start(bf16[256,256]{1,0:T(8,128)(2,1)S(1)} %get-tuple-element.28), channel_id=1, source_target_pairs={{0,2},{2,3},{3,1},{1,0},{4,6},{6,7},{7,5},{5,4},{8,10},{10,11},{11... | collective-permute-start | bytes 393224 | tf_op jit(solution)/shard_map/ppermute | solution.py:394
  35.0 0.7 %collective-permute-start.6 = (bf16[256,256]{1,0:T(8,128)(2,1)S(1)}, bf16[256,256]{1,0:T(8,128)(2,1)S(1)}, u32[]{:S(2)}, u32[]{:S(2)}) collective-permute-start(bf16[256,256]{1,0:T(8,128)(2,1)S(1)} %get-tuple-element.29), channel_id=1, source_target_pairs={{0,2},{2,3},{3,1},{1,0},{4,6},{6,7},{7,5},{5,4},{8,10},{10,11},{11... | collective-permute-start | bytes 393224 | tf_op jit(solution)/shard_map/ppermute | solution.py:394
  35.7 1.2 %collective-permute-start.11 = (bf16[256,256]{1,0:T(8,128)(2,1)S(1)}, bf16[256,256]{1,0:T(8,128)(2,1)S(1)}, u32[]{:S(2)}, u32[]{:S(2)}) collective-permute-start(bf16[256,256]{1,0:T(8,128)(2,1)S(1)} %get-tuple-element.33), channel_id=1, source_target_pairs={{0,2},{2,3},{3,1},{1,0},{4,6},{6,7},{7,5},{5,4},{8,10},{10,11},{11... | collective-permute-start | bytes 393224 | tf_op jit(solution)/shard_map/ppermute | solution.py:394
  37.1 0.7 %project.4.refs_4_ = f32[256,1024]{1,0:T(8,128)S(1)} custom-call(bf16[256,512]{1,0:T(8,128)(2,1)S(1)} %mix.2.refs_0_, bf16[256,512]{1,0:T(8,128)(2,1)S(1)} %mix.3.refs_1_, bf16[4160,512]{1,0:T(8,128)(2,1)S(1)} %pack.1.refs_2_.refs_3_.refs_0_, bf16[4160,512]{1,0:T(8,128)(2,1)S(1)} %collective-permute-done.10.refs_3_.refs_4_.refs_1_), custom_call_target="tpu_custom_call" | custom-call | flops 536870912 | bytes 10092544 | tf_op jit(solution)/shard_map/project/pallas_call | solution.py:61
  37.8 0.7 %project.5.refs_4_ = f32[256,1024]{1,0:T(8,128)S(1)} custom-call(bf16[256,512]{1,0:T(8,128)(2,1)S(1)} %collective-permute-done.3.refs_0_, bf16[256,512]{1,0:T(8,128)(2,1)S(1)} %collective-permute-done.7.refs_1_, bf16[4160,512]{1,0:T(8,128)(2,1)S(1)} %pack.1.refs_2_.refs_3_.refs_0_, bf16[4160,512]{1,0:T(8,128)(2,1)S(1)} %collective-permute-done.10.refs_3_.refs_4_.refs_1_, ...), custom_call_target="tpu_custom_call" | custom-call | flops 536870912 | bytes 11141120 | tf_op jit(solution)/shard_map/project/pallas_call | solution.py:61
  38.6 0.7 %project.6.refs_5_ = f32[256,1024]{1,0:T(8,128)S(1)} custom-call(bf16[256,512]{1,0:T(8,128)(2,1)S(1)} %collective-permute-done.4.source.refs_0_, bf16[256,512]{1,0:T(8,128)(2,1)S(1)} %collective-permute-done.8.source.refs_1_, bf16[4160,512]{1,0:T(8,128)(2,1)S(1)} %pack.1.refs_2_.refs_3_.refs_0_, ...), custom_call_target="tpu_custom_call" | custom-call | flops 536870912 | bytes 11141120 | tf_op jit(solution)/shard_map/project/pallas_call | solution.py:61
  39.4 1.8 %collective-permute-done.6.refs_1_ = bf16[256,256]{1,0:T(8,128)(2,1)S(1)} collective-permute-done((bf16[256,256]{1,0:T(8,128)(2,1)S(1)}, bf16[256,256]{1,0:T(8,128)(2,1)S(1)}, u32[]{:S(2)}, u32[]{:S(2)}) %collective-permute-start.6) | collective-permute-done | bytes 131104 | tf_op jit(solution)/shard_map/ppermute | solution.py:394
  41.1 0.6 %project.7.acc_ref = f32[256,1024]{1,0:T(8,128)S(1)} custom-call(bf16[256,256]{1,0:T(8,128)(2,1)S(1)} %collective-permute-done.5.refs_0_, bf16[256,256]{1,0:T(8,128)(2,1)S(1)} %collective-permute-done.6.refs_1_, bf16[256,256]{1,0:T(8,128)(2,1)S(1)} %collective-permute-done.9.refs_2_, bf16[4160,512]{1,0:T(8,128)(2,1)S(1)} %pack.1.refs_2_.refs_3_.refs_0_, ...), custom_call_target="tpu_custom_call" | custom-call | flops 402653184 | bytes 11010048 | tf_op jit(solution)/shard_map/project/pallas_call | solution.py:61
  41.7 0.8 %collective-permute-done.11.e_ref = bf16[256,256]{1,0:T(8,128)(2,1)S(1)} collective-permute-done((bf16[256,256]{1,0:T(8,128)(2,1)S(1)}, bf16[256,256]{1,0:T(8,128)(2,1)S(1)}, u32[]{:S(2)}, u32[]{:S(2)}) %collective-permute-start.11) | collective-permute-done | bytes 131104 | tf_op jit(solution)/shard_map/ppermute | solution.py:394
  42.5 0.7 %cross_attend.1 = (f32[64,640]{1,0:T(8,128)S(1)}, f32[64,640]{1,0:T(8,128)S(1)}) custom-call(f32[256,1024]{1,0:T(8,128)S(1)} %project.7.acc_ref, bf16[256,256]{1,0:T(8,128)(2,1)S(1)} %collective-permute-done.11.e_ref, bf16[256,1024]{1,0:T(8,128)(2,1)S(1)} %get-tuple-element.34.map_ref, bf16[128,512]{1,0:T(8,128)(2,1)S(1)} %get-tuple-element.35.tgt_ref, ...), custom_call_target="tpu_custom_call" | custom-call | flops 134217728 | bytes 2293760 | tf_op jit(solution)/shard_map/cross_attend/pallas_call | solution.py:61
  43.3 1.4 %collective-permute-done.12.refs_1_ = f32[64,640]{1,0:T(8,128)S(1)} collective-permute-done((f32[64,640]{1,0:T(8,128)S(1)}, f32[64,640]{1,0:T(8,128)S(1)}, u32[]{:S(2)}, u32[]{:S(2)}) %collective-permute-start.12) | collective-permute-done | bytes 163872 | tf_op jit(solution)/shard_map/ppermute | solution.py:411
  44.7 0.8 %combine.1 = bf16[64,512]{1,0:T(8,128)(2,1)} custom-call(f32[64,640]{1,0:T(8,128)S(1)} %get-tuple-element.37.refs_0_, f32[64,640]{1,0:T(8,128)S(1)} %collective-permute-done.12.refs_1_), custom_call_target="tpu_custom_call" | custom-call | bytes 393216 | tf_op jit(solution)/shard_map/combine/pallas_call | solution.py:61
  (17 shorter events, 2.0 us)
Async XLA Ops:
  0.0 2.4 %collective-permute-start.1 = (bf16[256,1024]{1,0:T(8,128)(2,1)}, bf16[256,1024]{1,0:T(8,128)(2,1)S(1)}, u32[]{:S(2)}, u32[]{:S(2)}) collective-permute-start(bf16[256,1024]{1,0:T(8,128)(2,1)} %refs_1_.2), channel_id=1, source_target_pairs={{0,4},{4,0},{1,5},{5,1},{2,6},{6,2},{3,7},{7,3},{8,12},{12,8},{9,1... | collective-permute-start | bytes 1572872 | tf_op jit(solution)/shard_map/ppermute | solution.py:341
  0.5 1.9 %collective-permute-start = (s32[1,256]{1,0:T(1,128)}, s32[1,256]{1,0:T(1,128)S(1)}, u32[]{:S(2)}, u32[]{:S(2)}) collective-permute-start(s32[1,256]{1,0:T(1,128)} %bitcast.1), channel_id=1, source_target_pairs={{0,4},{4,0},{1,5},{5,1},{2,6},{6,2},{3,7},{7,3},{8,12},{12,8},{9,1... | collective-permute-start | bytes 3080 | tf_op jit(solution)/shard_map/ppermute | solution.py:341
  0.5 3.3 %collective-permute-start.2 = (bf16[256,1024]{1,0:T(8,128)(2,1)}, bf16[256,1024]{1,0:T(8,128)(2,1)S(1)}, u32[]{:S(2)}, u32[]{:S(2)}) collective-permute-start(bf16[256,1024]{1,0:T(8,128)(2,1)} %refs_5_.1), channel_id=1, source_target_pairs={{0,4},{4,0},{1,5},{5,1},{2,6},{6,2},{3,7},{7,3},{8,12},{12,8},{9,1... | collective-permute-start | bytes 1572872 | tf_op jit(solution)/shard_map/ppermute | solution.py:341
  4.2 10.5 %collective-permute-start.7 = (bf16[256,512]{1,0:T(8,128)(2,1)S(1)}, bf16[256,512]{1,0:T(8,128)(2,1)S(1)}, u32[]{:S(2)}, u32[]{:S(2)}) collective-permute-start(bf16[256,512]{1,0:T(8,128)(2,1)S(1)} %mix.3.refs_1_), channel_id=1, source_target_pairs={{0,2},{2,3},{3,1},{1,0},{4,6},{6,7},{7,5},{5,4},{8,10},{10,11},{11... | collective-permute-start | bytes 786440 | tf_op jit(solution)/shard_map/ppermute | solution.py:394
  8.9 11.5 %collective-permute-start.3 = (bf16[256,512]{1,0:T(8,128)(2,1)S(1)}, bf16[256,512]{1,0:T(8,128)(2,1)S(1)}, u32[]{:S(2)}, u32[]{:S(2)}) collective-permute-start(bf16[256,512]{1,0:T(8,128)(2,1)S(1)} %mix.2.refs_0_), channel_id=1, source_target_pairs={{0,2},{2,3},{3,1},{1,0},{4,6},{6,7},{7,5},{5,4},{8,10},{10,11},{11... | collective-permute-start | bytes 786440 | tf_op jit(solution)/shard_map/ppermute | solution.py:394
  14.7 11.2 %collective-permute-start.8 = (bf16[256,512]{1,0:T(8,128)(2,1)S(1)}, bf16[256,512]{1,0:T(8,128)(2,1)S(1)}, u32[]{:S(2)}, u32[]{:S(2)}) collective-permute-start(bf16[256,512]{1,0:T(8,128)(2,1)S(1)} %collective-permute-done.7.refs_1_), channel_id=1, source_target_pairs={{0,2},{2,3},{3,1},{1,0},{4,6},{6,7},{7,5},{5,4},{8,10},{10,11},{11... | collective-permute-start | bytes 786440 | tf_op jit(solution)/shard_map/ppermute | solution.py:394
  20.3 16.6 %collective-permute-start.10 = (bf16[4160,512]{1,0:T(8,128)(2,1)S(1)}, bf16[4160,512]{1,0:T(8,128)(2,1)S(1)}, u32[]{:S(2)}, u32[]{:S(2)}) collective-permute-start(bf16[4160,512]{1,0:T(8,128)(2,1)S(1)} %pack.1.refs_2_.refs_3_.refs_0_), channel_id=1, source_target_pairs={{0,4},{4,0},{1,5},{5,1},{2,6},{6,2},{3,7},{7,3},{8,12},{12,8},{9,1... | collective-permute-start | bytes 12779528 | tf_op jit(solution)/shard_map/ppermute | solution.py:341
  20.4 11.1 %collective-permute-start.4 = (bf16[256,512]{1,0:T(8,128)(2,1)S(1)}, bf16[256,512]{1,0:T(8,128)(2,1)S(1)}, u32[]{:S(2)}, u32[]{:S(2)}) collective-permute-start(bf16[256,512]{1,0:T(8,128)(2,1)S(1)} %collective-permute-done.3.refs_0_), channel_id=1, source_target_pairs={{0,2},{2,3},{3,1},{1,0},{4,6},{6,7},{7,5},{5,4},{8,10},{10,11},{11... | collective-permute-start | bytes 786440 | tf_op jit(solution)/shard_map/ppermute | solution.py:394
  25.9 13.4 %collective-permute-start.9 = (bf16[256,256]{1,0:T(8,128)(2,1)S(1)}, bf16[256,256]{1,0:T(8,128)(2,1)S(1)}, u32[]{:S(2)}, u32[]{:S(2)}) collective-permute-start(bf16[256,256]{1,0:T(8,128)(2,1)S(1)} %get-tuple-element.32), channel_id=1, source_target_pairs={{0,2},{2,3},{3,1},{1,0},{4,6},{6,7},{7,5},{5,4},{8,10},{10,11},{11... | collective-permute-start | bytes 393224 | tf_op jit(solution)/shard_map/ppermute | solution.py:394
  31.5 7.8 %collective-permute-start.5 = (bf16[256,256]{1,0:T(8,128)(2,1)S(1)}, bf16[256,256]{1,0:T(8,128)(2,1)S(1)}, u32[]{:S(2)}, u32[]{:S(2)}) collective-permute-start(bf16[256,256]{1,0:T(8,128)(2,1)S(1)} %get-tuple-element.28), channel_id=1, source_target_pairs={{0,2},{2,3},{3,1},{1,0},{4,6},{6,7},{7,5},{5,4},{8,10},{10,11},{11... | collective-permute-start | bytes 393224 | tf_op jit(solution)/shard_map/ppermute | solution.py:394
  35.0 6.2 %collective-permute-start.6 = (bf16[256,256]{1,0:T(8,128)(2,1)S(1)}, bf16[256,256]{1,0:T(8,128)(2,1)S(1)}, u32[]{:S(2)}, u32[]{:S(2)}) collective-permute-start(bf16[256,256]{1,0:T(8,128)(2,1)S(1)} %get-tuple-element.29), channel_id=1, source_target_pairs={{0,2},{2,3},{3,1},{1,0},{4,6},{6,7},{7,5},{5,4},{8,10},{10,11},{11... | collective-permute-start | bytes 393224 | tf_op jit(solution)/shard_map/ppermute | solution.py:394
  35.7 6.9 %collective-permute-start.11 = (bf16[256,256]{1,0:T(8,128)(2,1)S(1)}, bf16[256,256]{1,0:T(8,128)(2,1)S(1)}, u32[]{:S(2)}, u32[]{:S(2)}) collective-permute-start(bf16[256,256]{1,0:T(8,128)(2,1)S(1)} %get-tuple-element.33), channel_id=1, source_target_pairs={{0,2},{2,3},{3,1},{1,0},{4,6},{6,7},{7,5},{5,4},{8,10},{10,11},{11... | collective-permute-start | bytes 393224 | tf_op jit(solution)/shard_map/ppermute | solution.py:394
  43.2 1.5 %collective-permute-start.12 = (f32[64,640]{1,0:T(8,128)S(1)}, f32[64,640]{1,0:T(8,128)S(1)}, u32[]{:S(2)}, u32[]{:S(2)}) collective-permute-start(f32[64,640]{1,0:T(8,128)S(1)} %get-tuple-element.38), channel_id=1, source_target_pairs={{4,0},{0,4},{5,1},{1,5},{6,2},{2,6},{7,3},{3,7},{12,8},{8,12},{13,... | collective-permute-start | bytes 491528 | tf_op jit(solution)/shard_map/ppermute | solution.py:411

commit v12 on v11

--- a/solution.py
+++ b/solution.py
@@ -70,17 +70,6 @@
     )(*operands)
 
 
-def copies_of(source, target, sems, first, parts=4):
-    rows = source.shape[0]
-    parts = parts if rows % (16 * parts) == 0 else 1
-    step = rows // parts
-    made = []
-    for i in range(parts):
-        at = pl.ds(i * step, step)
-        made.append(pltpu.make_async_copy(source.at[at, :], target.at[at, :], sems.at[first + i]))
-    return made
-
-
 def run_all(copies):
     for copy in copies:
         copy.start()
@@ -90,10 +79,7 @@
 
 def fetch_kernel(count, *refs):
     sources, targets, sems = refs[:count], refs[count : 2 * count], refs[-1]
-    copies = []
-    for source, target in zip(sources, targets):
-        copies += copies_of(source, target, sems, len(copies))
-    run_all(copies)
+    run_all([pltpu.make_async_copy(s, t, sems.at[i]) for i, (s, t) in enumerate(zip(sources, targets))])
 
 
 def fetch(*arrays):
@@ -103,16 +89,16 @@
         [(x.shape, x.dtype) for x in arrays],
         [pltpu.with_memory_space_constraint(x, pltpu.HBM) for x in arrays],
         specs=[HBM] * len(arrays),
-        scratch=[pltpu.SemaphoreType.DMA((4 * len(arrays),))],
+        scratch=[pltpu.SemaphoreType.DMA((len(arrays),))],
     )
 
 
 def pack_kernel(*refs):
     sources, out_ref, sems = refs[:-2], refs[-2], refs[-1]
     copies, row = [], 0
-    for source in sources:
+    for i, source in enumerate(sources):
         rows = source.shape[0]
-        copies += copies_of(source, out_ref.at[pl.ds(row, rows), :], sems, len(copies))
+        copies.append(pltpu.make_async_copy(source, out_ref.at[pl.ds(row, rows), :], sems.at[i]))
         row += rows
     run_all(copies)
 
@@ -125,18 +111,13 @@
         [((rows, arrays[0].shape[1]), arrays[0].dtype)],
         [pltpu.with_memory_space_constraint(x, pltpu.HBM) for x in arrays],
         specs=[HBM] * len(arrays),
-        scratch=[pltpu.SemaphoreType.DMA((4 * len(arrays),))],
+        scratch=[pltpu.SemaphoreType.DMA((len(arrays),))],
     )[0]
 
 
-def weigh_kernel(blocks, first, heads, fetches, *refs):
+def weigh_kernel(blocks, first, heads, *refs):
     marks, q_ref, keys = refs[:blocks], refs[blocks], refs[blocks + 1 : 2 * blocks + 1]
-    rest = refs[2 * blocks + 1 :]
-    weight_ref, total_ref = rest[fetches : fetches + 2]
-    if fetches:
-        copies = copies_of(rest[0], rest[-2], rest[-1], 0)
-        for copy in copies:
-            copy.start()
+    weight_ref, total_ref = refs[2 * blocks + 1 :]
     down = down_lanes(marks[0][...])
     same = jnp.concatenate([same_mark(down, m[...]) for m in marks], axis=1)
     span = same.shape[1]
@@ -149,30 +130,17 @@
         weight_ref[:, h * span : (h + 1) * span] = weights.astype(BF16)
         totals = jnp.where(lane == h, total, totals)
     total_ref[...] = totals
-    if fetches:
-        for copy in copies:
-            copy.wait()
-
-
-def weigh(query, keys, marks, first, heads, fetched=None):
+
+
+def weigh(query, keys, marks, first, heads):
     rows, span = query.shape[0], query.shape[0] * len(keys)
-    outs = [((rows, heads * span), BF16), ((rows, LANES), F32)]
-    operands = [*marks, query, *keys]
-    specs, scratch = [VMEM] * len(operands), []
-    if fetched is not None:
-        operands.append(pltpu.with_memory_space_constraint(fetched, pltpu.HBM))
-        specs.append(HBM)
-        outs.append((fetched.shape, fetched.dtype))
-        scratch.append(pltpu.SemaphoreType.DMA((4,)))
-    return call(
-        functools.partial(weigh_kernel, len(keys), first, heads, len(scratch)),
+    return call(
+        functools.partial(weigh_kernel, len(keys), first, heads),
         "weigh",
-        outs,
-        operands,
+        [((rows, heads * span), BF16), ((rows, LANES), F32)],
+        [*marks, query, *keys],
         flops=WEIGH_FLOPS,
         exps=rows * span * heads,
-        specs=specs,
-        scratch=scratch,
     )
 
 
@@ -342,7 +310,7 @@
 
     marks = (doc_ids if n_ctx == 2 else doc_ids + 1).reshape(1, rows)
     keys, near_marks, values = bring(enc_key), bring(marks), bring(enc_value)
-    query, own_key, marks = fetch(enc_query, enc_key, marks)
+    query, own_key, own_value, marks = fetch(enc_query, enc_key, enc_value, marks)
     near_targets = []
     if n_ctx == 2:
         own_maps = pack(key_map, value_map, tgt_query)
@@ -355,17 +323,8 @@
     chunks = 2
     heads = features // HEAD_DIM // chunks
     held = [None] * chunks
-    own_value = None
     for j in reversed(range(chunks)):
-        weights, totals, *fetched = weigh(
-            query,
-            [own_key, *keys],
-            [marks, *near_marks],
-            j * heads,
-            heads,
-            enc_value if own_value is None else None,
-        )
-        own_value = fetched[0] if fetched else own_value
+        weights, totals = weigh(query, [own_key, *keys], [marks, *near_marks], j * heads, heads)
         held[j] = mix(weights, totals, [own_value, *values], j * heads, heads)
 
     order = ring_order(n_head)

time: 45.7 us -> 44.9 us (0.982)
  Pallas kernels: 10.8 us -> 9.92 us
    pallas_call x15, Pallas kernels: 10.8 us -> 9.92 us  [call(): pl.pallas_call(kernel, in_specs=specs or [VMEM] * len(operands), out_spec...]
  transfers between devices with their start and end apart: 13 -> 13, of which waited for: 6 -> 6; matrix products, arithmetic and copies ran while one was open for 0% -> 0% of each run, Pallas kernels for 20% -> 18%
where the time goes in v12:
time: 44.9 us; the launch traced here: 44.8 us
  starting transfers between devices  22.2 us (49%)
  waiting for transfers between devices  12.5 us (28%)
  Pallas kernels  9.92 us (22%)
    ppermute x8, starting transfers between devices, on_device(): later = [lax.ppermute(p, 'head', ring) for p in pieces]  21.1 us
    ppermute x8, waiting for transfers between devices, on_device(): later = [lax.ppermute(p, 'head', ring) for p in pieces]  11.1 us
    pallas_call x15, Pallas kernels, call(): pl.pallas_call(kernel, in_specs=specs or [VMEM] * len(operands), out_spec...  9.92 us
    ppermute x1, waiting for transfers between devices, on_device(): lax.ppermute(piece, 'ctx', [(target, source) for source, target in pairs])  1.38 us
    ppermute x4, starting transfers between devices, on_device(): bring = lambda x: [lax.ppermute(x, 'ctx', pairs) for pairs in links]  1.03 us
  transfers between devices with their start and end apart: 13, of which 6 were waited for; matrix products, arithmetic and copies ran while one was open for 0% of the time, Pallas kernels for 18%

profile of v12, /device:TPU:0, one launch (start us, length us, event | category | flops | bytes accessed | tf_op | source)
XLA Modules:
  0.0 44.8 jit_solution(6083498514434284256)
XLA Ops:
  1.0 1.4 %fetch.1 = (bf16[256,1024]{1,0:T(8,128)(2,1)S(1)}, bf16[256,1024]{1,0:T(8,128)(2,1)S(1)}, bf16[256,1024]{1,0:T(8,128)(2,1)S(1)}, s32[1,256]{1,0:T(1,128)S(1)}) custom-call(bf16[256,1024]{1,0:T(8,128)(2,1)} %refs_0_.2, bf16[256,1024]{1,0:T(8,128)(2,1)} %refs_1_.2, bf16[256,1024]{1,0:T(8,128)(2,1)} %refs_2_.2, s32[1,256]{1,0:T(1,128)} %bitcast.2), custom_call_target="tpu_custom_call" | custom-call | bytes 3147776 | tf_op jit(solution)/shard_map/fetch/pallas_call | solution.py:61
  2.4 0.6 %weigh.3 = (bf16[256,1024]{1,0:T(8,128)(2,1)S(1)}, f32[256,128]{1,0:T(8,128)S(1)}) custom-call(s32[1,256]{1,0:T(1,128)S(1)} %get-tuple-element.22.refs_0_.refs_2_, s32[1,256]{1,0:T(1,128)S(1)} %collective-permute-done.refs_1_.refs_3_, bf16[256,1024]{1,0:T(8,128)(2,1)S(1)} %get-tuple-element.23.refs_2_, bf16[256,1024]{1,0:T(8,128)(2,1)S(1)} %get-tuple-element.24.refs_3_, ...), custom_call_target="tpu_custom_call" | custom-call | flops 6000000000 | bytes 2230272 | tf_op jit(solution)/shard_map/weigh/pallas_call | solution.py:61
  3.3 4.0 %collective-permute-start.7 = (bf16[256,512]{1,0:T(8,128)(2,1)S(1)}, bf16[256,512]{1,0:T(8,128)(2,1)S(1)}, u32[]{:S(2)}, u32[]{:S(2)}) collective-permute-start(bf16[256,512]{1,0:T(8,128)(2,1)S(1)} %mix.3.refs_1_), channel_id=1, source_target_pairs={{0,2},{2,3},{3,1},{1,0},{4,6},{6,7},{7,5},{5,4},{8,10},{10,11},{11... | collective-permute-start | bytes 786440 | tf_op jit(solution)/shard_map/ppermute | solution.py:353
  7.3 0.5 %weigh.2 = (bf16[256,1024]{1,0:T(8,128)(2,1)S(1)}, f32[256,128]{1,0:T(8,128)S(1)}) custom-call(s32[1,256]{1,0:T(1,128)S(1)} %get-tuple-element.22.refs_0_.refs_2_, s32[1,256]{1,0:T(1,128)S(1)} %collective-permute-done.refs_1_.refs_3_, bf16[256,1024]{1,0:T(8,128)(2,1)S(1)} %get-tuple-element.23.refs_2_, bf16[256,1024]{1,0:T(8,128)(2,1)S(1)} %get-tuple-element.24.refs_3_, ...), custom_call_target="tpu_custom_call" | custom-call | flops 6000000000 | bytes 2230272 | tf_op jit(solution)/shard_map/weigh/pallas_call | solution.py:61
  8.2 1.6 %collective-permute-start.3 = (bf16[256,512]{1,0:T(8,128)(2,1)S(1)}, bf16[256,512]{1,0:T(8,128)(2,1)S(1)}, u32[]{:S(2)}, u32[]{:S(2)}) collective-permute-start(bf16[256,512]{1,0:T(8,128)(2,1)S(1)} %mix.2.refs_0_), channel_id=1, source_target_pairs={{0,2},{2,3},{3,1},{1,0},{4,6},{6,7},{7,5},{5,4},{8,10},{10,11},{11... | collective-permute-start | bytes 786440 | tf_op jit(solution)/shard_map/ppermute | solution.py:353
  9.8 4.2 %collective-permute-done.7.refs_1_ = bf16[256,512]{1,0:T(8,128)(2,1)S(1)} collective-permute-done((bf16[256,512]{1,0:T(8,128)(2,1)S(1)}, bf16[256,512]{1,0:T(8,128)(2,1)S(1)}, u32[]{:S(2)}, u32[]{:S(2)}) %collective-permute-start.7) | collective-permute-done | bytes 262176 | tf_op jit(solution)/shard_map/ppermute | solution.py:353
  14.0 3.4 %collective-permute-start.8 = (bf16[256,512]{1,0:T(8,128)(2,1)S(1)}, bf16[256,512]{1,0:T(8,128)(2,1)S(1)}, u32[]{:S(2)}, u32[]{:S(2)}) collective-permute-start(bf16[256,512]{1,0:T(8,128)(2,1)S(1)} %collective-permute-done.7.refs_1_), channel_id=1, source_target_pairs={{0,2},{2,3},{3,1},{1,0},{4,6},{6,7},{7,5},{5,4},{8,10},{10,11},{11... | collective-permute-start | bytes 786440 | tf_op jit(solution)/shard_map/ppermute | solution.py:353
  17.3 2.2 %pack.1.refs_2_.refs_3_.refs_0_ = bf16[4160,512]{1,0:T(8,128)(2,1)S(1)} custom-call(bf16[2048,512]{1,0:T(8,128)(2,1)} %refs_0_.3, bf16[2048,512]{1,0:T(8,128)(2,1)} %refs_1_.3, bf16[64,512]{1,0:T(8,128)(2,1)} %refs_2_.3), custom_call_target="tpu_custom_call" | custom-call | bytes 8519680 | tf_op jit(solution)/shard_map/pack/pallas_call | solution.py:61
  19.7 3.3 %collective-permute-start.4 = (bf16[256,512]{1,0:T(8,128)(2,1)S(1)}, bf16[256,512]{1,0:T(8,128)(2,1)S(1)}, u32[]{:S(2)}, u32[]{:S(2)}) collective-permute-start(bf16[256,512]{1,0:T(8,128)(2,1)S(1)} %collective-permute-done.3.refs_0_), channel_id=1, source_target_pairs={{0,2},{2,3},{3,1},{1,0},{4,6},{6,7},{7,5},{5,4},{8,10},{10,11},{11... | collective-permute-start | bytes 786440 | tf_op jit(solution)/shard_map/ppermute | solution.py:353
  23.0 2.2 %collective-permute-done.8.source.refs_1_ = bf16[256,512]{1,0:T(8,128)(2,1)S(1)} collective-permute-done((bf16[256,512]{1,0:T(8,128)(2,1)S(1)}, bf16[256,512]{1,0:T(8,128)(2,1)S(1)}, u32[]{:S(2)}, u32[]{:S(2)}) %collective-permute-start.8) | collective-permute-done | bytes 262176 | tf_op jit(solution)/shard_map/ppermute | solution.py:353
  25.2 3.4 %collective-permute-start.9 = (bf16[256,256]{1,0:T(8,128)(2,1)S(1)}, bf16[256,256]{1,0:T(8,128)(2,1)S(1)}, u32[]{:S(2)}, u32[]{:S(2)}) collective-permute-start(bf16[256,256]{1,0:T(8,128)(2,1)S(1)} %get-tuple-element.32), channel_id=1, source_target_pairs={{0,2},{2,3},{3,1},{1,0},{4,6},{6,7},{7,5},{5,4},{8,10},{10,11},{11... | collective-permute-start | bytes 393224 | tf_op jit(solution)/shard_map/ppermute | solution.py:353
  28.6 2.2 %collective-permute-done.4.source.refs_0_ = bf16[256,512]{1,0:T(8,128)(2,1)S(1)} collective-permute-done((bf16[256,512]{1,0:T(8,128)(2,1)S(1)}, bf16[256,512]{1,0:T(8,128)(2,1)S(1)}, u32[]{:S(2)}, u32[]{:S(2)}) %collective-permute-start.4) | collective-permute-done | bytes 262176 | tf_op jit(solution)/shard_map/ppermute | solution.py:353
  30.8 3.4 %collective-permute-start.5 = (bf16[256,256]{1,0:T(8,128)(2,1)S(1)}, bf16[256,256]{1,0:T(8,128)(2,1)S(1)}, u32[]{:S(2)}, u32[]{:S(2)}) collective-permute-start(bf16[256,256]{1,0:T(8,128)(2,1)S(1)} %get-tuple-element.28), channel_id=1, source_target_pairs={{0,2},{2,3},{3,1},{1,0},{4,6},{6,7},{7,5},{5,4},{8,10},{10,11},{11... | collective-permute-start | bytes 393224 | tf_op jit(solution)/shard_map/ppermute | solution.py:353
  34.3 0.7 %collective-permute-start.6 = (bf16[256,256]{1,0:T(8,128)(2,1)S(1)}, bf16[256,256]{1,0:T(8,128)(2,1)S(1)}, u32[]{:S(2)}, u32[]{:S(2)}) collective-permute-start(bf16[256,256]{1,0:T(8,128)(2,1)S(1)} %get-tuple-element.29), channel_id=1, source_target_pairs={{0,2},{2,3},{3,1},{1,0},{4,6},{6,7},{7,5},{5,4},{8,10},{10,11},{11... | collective-permute-start | bytes 393224 | tf_op jit(solution)/shard_map/ppermute | solution.py:353
  34.9 1.2 %collective-permute-start.11 = (bf16[256,256]{1,0:T(8,128)(2,1)S(1)}, bf16[256,256]{1,0:T(8,128)(2,1)S(1)}, u32[]{:S(2)}, u32[]{:S(2)}) collective-permute-start(bf16[256,256]{1,0:T(8,128)(2,1)S(1)} %get-tuple-element.33), channel_id=1, source_target_pairs={{0,2},{2,3},{3,1},{1,0},{4,6},{6,7},{7,5},{5,4},{8,10},{10,11},{11... | collective-permute-start | bytes 393224 | tf_op jit(solution)/shard_map/ppermute | solution.py:353
  36.4 0.7 %project.4.refs_4_ = f32[256,1024]{1,0:T(8,128)S(1)} custom-call(bf16[256,512]{1,0:T(8,128)(2,1)S(1)} %mix.2.refs_0_, bf16[256,512]{1,0:T(8,128)(2,1)S(1)} %mix.3.refs_1_, bf16[4160,512]{1,0:T(8,128)(2,1)S(1)} %pack.1.refs_2_.refs_3_.refs_0_, bf16[4160,512]{1,0:T(8,128)(2,1)S(1)} %collective-permute-done.10.refs_3_.refs_4_.refs_1_), custom_call_target="tpu_custom_call" | custom-call | flops 536870912 | bytes 10092544 | tf_op jit(solution)/shard_map/project/pallas_call | solution.py:61
  37.1 0.7 %project.5.refs_4_ = f32[256,1024]{1,0:T(8,128)S(1)} custom-call(bf16[256,512]{1,0:T(8,128)(2,1)S(1)} %collective-permute-done.3.refs_0_, bf16[256,512]{1,0:T(8,128)(2,1)S(1)} %collective-permute-done.7.refs_1_, bf16[4160,512]{1,0:T(8,128)(2,1)S(1)} %pack.1.refs_2_.refs_3_.refs_0_, bf16[4160,512]{1,0:T(8,128)(2,1)S(1)} %collective-permute-done.10.refs_3_.refs_4_.refs_1_, ...), custom_call_target="tpu_custom_call" | custom-call | flops 536870912 | bytes 11141120 | tf_op jit(solution)/shard_map/project/pallas_call | solution.py:61
  37.9 0.7 %project.6.refs_5_ = f32[256,1024]{1,0:T(8,128)S(1)} custom-call(bf16[256,512]{1,0:T(8,128)(2,1)S(1)} %collective-permute-done.4.source.refs_0_, bf16[256,512]{1,0:T(8,128)(2,1)S(1)} %collective-permute-done.8.source.refs_1_, bf16[4160,512]{1,0:T(8,128)(2,1)S(1)} %pack.1.refs_2_.refs_3_.refs_0_, ...), custom_call_target="tpu_custom_call" | custom-call | flops 536870912 | bytes 11141120 | tf_op jit(solution)/shard_map/project/pallas_call | solution.py:61
  38.6 1.8 %collective-permute-done.6.refs_1_ = bf16[256,256]{1,0:T(8,128)(2,1)S(1)} collective-permute-done((bf16[256,256]{1,0:T(8,128)(2,1)S(1)}, bf16[256,256]{1,0:T(8,128)(2,1)S(1)}, u32[]{:S(2)}, u32[]{:S(2)}) %collective-permute-start.6) | collective-permute-done | bytes 131104 | tf_op jit(solution)/shard_map/ppermute | solution.py:353
  40.4 0.6 %project.7.acc_ref = f32[256,1024]{1,0:T(8,128)S(1)} custom-call(bf16[256,256]{1,0:T(8,128)(2,1)S(1)} %collective-permute-done.5.refs_0_, bf16[256,256]{1,0:T(8,128)(2,1)S(1)} %collective-permute-done.6.refs_1_, bf16[256,256]{1,0:T(8,128)(2,1)S(1)} %collective-permute-done.9.refs_2_, bf16[4160,512]{1,0:T(8,128)(2,1)S(1)} %pack.1.refs_2_.refs_3_.refs_0_, ...), custom_call_target="tpu_custom_call" | custom-call | flops 402653184 | bytes 11010048 | tf_op jit(solution)/shard_map/project/pallas_call | solution.py:61
  41.0 0.8 %collective-permute-done.11.e_ref = bf16[256,256]{1,0:T(8,128)(2,1)S(1)} collective-permute-done((bf16[256,256]{1,0:T(8,128)(2,1)S(1)}, bf16[256,256]{1,0:T(8,128)(2,1)S(1)}, u32[]{:S(2)}, u32[]{:S(2)}) %collective-permute-start.11) | collective-permute-done | bytes 131104 | tf_op jit(solution)/shard_map/ppermute | solution.py:353
  41.8 0.7 %cross_attend.1 = (f32[64,640]{1,0:T(8,128)S(1)}, f32[64,640]{1,0:T(8,128)S(1)}) custom-call(f32[256,1024]{1,0:T(8,128)S(1)} %project.7.acc_ref, bf16[256,256]{1,0:T(8,128)(2,1)S(1)} %collective-permute-done.11.e_ref, bf16[256,1024]{1,0:T(8,128)(2,1)S(1)} %get-tuple-element.34.map_ref, bf16[128,512]{1,0:T(8,128)(2,1)S(1)} %get-tuple-element.35.tgt_ref, ...), custom_call_target="tpu_custom_call" | custom-call | flops 134217728 | bytes 2293760 | tf_op jit(solution)/shard_map/cross_attend/pallas_call | solution.py:61
  42.6 1.4 %collective-permute-done.12.refs_1_ = f32[64,640]{1,0:T(8,128)S(1)} collective-permute-done((f32[64,640]{1,0:T(8,128)S(1)}, f32[64,640]{1,0:T(8,128)S(1)}, u32[]{:S(2)}, u32[]{:S(2)}) %collective-permute-start.12) | collective-permute-done | bytes 163872 | tf_op jit(solution)/shard_map/ppermute | solution.py:370
  43.9 0.8 %combine.1 = bf16[64,512]{1,0:T(8,128)(2,1)} custom-call(f32[64,640]{1,0:T(8,128)S(1)} %get-tuple-element.37.refs_0_, f32[64,640]{1,0:T(8,128)S(1)} %collective-permute-done.12.refs_1_), custom_call_target="tpu_custom_call" | custom-call | bytes 393216 | tf_op jit(solution)/shard_map/combine/pallas_call | solution.py:61
  (17 shorter events, 2.0 us)
Async XLA Ops:
  0.0 2.4 %collective-permute-start.1 = (bf16[256,1024]{1,0:T(8,128)(2,1)}, bf16[256,1024]{1,0:T(8,128)(2,1)S(1)}, u32[]{:S(2)}, u32[]{:S(2)}) collective-permute-start(bf16[256,1024]{1,0:T(8,128)(2,1)} %refs_1_.2), channel_id=1, source_target_pairs={{0,4},{4,0},{1,5},{5,1},{2,6},{6,2},{3,7},{7,3},{8,12},{12,8},{9,1... | collective-permute-start | bytes 1572872 | tf_op jit(solution)/shard_map/ppermute | solution.py:309
  0.5 1.9 %collective-permute-start = (s32[1,256]{1,0:T(1,128)}, s32[1,256]{1,0:T(1,128)S(1)}, u32[]{:S(2)}, u32[]{:S(2)}) collective-permute-start(s32[1,256]{1,0:T(1,128)} %bitcast.1), channel_id=1, source_target_pairs={{0,4},{4,0},{1,5},{5,1},{2,6},{6,2},{3,7},{7,3},{8,12},{12,8},{9,1... | collective-permute-start | bytes 3080 | tf_op jit(solution)/shard_map/ppermute | solution.py:309
  0.5 2.4 %collective-permute-start.2 = (bf16[256,1024]{1,0:T(8,128)(2,1)}, bf16[256,1024]{1,0:T(8,128)(2,1)S(1)}, u32[]{:S(2)}, u32[]{:S(2)}) collective-permute-start(bf16[256,1024]{1,0:T(8,128)(2,1)} %refs_2_.2), channel_id=1, source_target_pairs={{0,4},{4,0},{1,5},{5,1},{2,6},{6,2},{3,7},{7,3},{8,12},{12,8},{9,1... | collective-permute-start | bytes 1572872 | tf_op jit(solution)/shard_map/ppermute | solution.py:309
  3.3 10.7 %collective-permute-start.7 = (bf16[256,512]{1,0:T(8,128)(2,1)S(1)}, bf16[256,512]{1,0:T(8,128)(2,1)S(1)}, u32[]{:S(2)}, u32[]{:S(2)}) collective-permute-start(bf16[256,512]{1,0:T(8,128)(2,1)S(1)} %mix.3.refs_1_), channel_id=1, source_target_pairs={{0,2},{2,3},{3,1},{1,0},{4,6},{6,7},{7,5},{5,4},{8,10},{10,11},{11... | collective-permute-start | bytes 786440 | tf_op jit(solution)/shard_map/ppermute | solution.py:353
  8.2 11.5 %collective-permute-start.3 = (bf16[256,512]{1,0:T(8,128)(2,1)S(1)}, bf16[256,512]{1,0:T(8,128)(2,1)S(1)}, u32[]{:S(2)}, u32[]{:S(2)}) collective-permute-start(bf16[256,512]{1,0:T(8,128)(2,1)S(1)} %mix.2.refs_0_), channel_id=1, source_target_pairs={{0,2},{2,3},{3,1},{1,0},{4,6},{6,7},{7,5},{5,4},{8,10},{10,11},{11... | collective-permute-start | bytes 786440 | tf_op jit(solution)/shard_map/ppermute | solution.py:353
  14.0 11.2 %collective-permute-start.8 = (bf16[256,512]{1,0:T(8,128)(2,1)S(1)}, bf16[256,512]{1,0:T(8,128)(2,1)S(1)}, u32[]{:S(2)}, u32[]{:S(2)}) collective-permute-start(bf16[256,512]{1,0:T(8,128)(2,1)S(1)} %collective-permute-done.7.refs_1_), channel_id=1, source_target_pairs={{0,2},{2,3},{3,1},{1,0},{4,6},{6,7},{7,5},{5,4},{8,10},{10,11},{11... | collective-permute-start | bytes 786440 | tf_op jit(solution)/shard_map/ppermute | solution.py:353
  19.6 16.6 %collective-permute-start.10 = (bf16[4160,512]{1,0:T(8,128)(2,1)S(1)}, bf16[4160,512]{1,0:T(8,128)(2,1)S(1)}, u32[]{:S(2)}, u32[]{:S(2)}) collective-permute-start(bf16[4160,512]{1,0:T(8,128)(2,1)S(1)} %pack.1.refs_2_.refs_3_.refs_0_), channel_id=1, source_target_pairs={{0,4},{4,0},{1,5},{5,1},{2,6},{6,2},{3,7},{7,3},{8,12},{12,8},{9,1... | collective-permute-start | bytes 12779528 | tf_op jit(solution)/shard_map/ppermute | solution.py:309
  19.7 11.1 %collective-permute-start.4 = (bf16[256,512]{1,0:T(8,128)(2,1)S(1)}, bf16[256,512]{1,0:T(8,128)(2,1)S(1)}, u32[]{:S(2)}, u32[]{:S(2)}) collective-permute-start(bf16[256,512]{1,0:T(8,128)(2,1)S(1)} %collective-permute-done.3.refs_0_), channel_id=1, source_target_pairs={{0,2},{2,3},{3,1},{1,0},{4,6},{6,7},{7,5},{5,4},{8,10},{10,11},{11... | collective-permute-start | bytes 786440 | tf_op jit(solution)/shard_map/ppermute | solution.py:353
  25.2 13.4 %collective-permute-start.9 = (bf16[256,256]{1,0:T(8,128)(2,1)S(1)}, bf16[256,256]{1,0:T(8,128)(2,1)S(1)}, u32[]{:S(2)}, u32[]{:S(2)}) collective-permute-start(bf16[256,256]{1,0:T(8,128)(2,1)S(1)} %get-tuple-element.32), channel_id=1, source_target_pairs={{0,2},{2,3},{3,1},{1,0},{4,6},{6,7},{7,5},{5,4},{8,10},{10,11},{11... | collective-permute-start | bytes 393224 | tf_op jit(solution)/shard_map/ppermute | solution.py:353
  30.8 7.8 %collective-permute-start.5 = (bf16[256,256]{1,0:T(8,128)(2,1)S(1)}, bf16[256,256]{1,0:T(8,128)(2,1)S(1)}, u32[]{:S(2)}, u32[]{:S(2)}) collective-permute-start(bf16[256,256]{1,0:T(8,128)(2,1)S(1)} %get-tuple-element.28), channel_id=1, source_target_pairs={{0,2},{2,3},{3,1},{1,0},{4,6},{6,7},{7,5},{5,4},{8,10},{10,11},{11... | collective-permute-start | bytes 393224 | tf_op jit(solution)/shard_map/ppermute | solution.py:353
  34.3 6.1 %collective-permute-start.6 = (bf16[256,256]{1,0:T(8,128)(2,1)S(1)}, bf16[256,256]{1,0:T(8,128)(2,1)S(1)}, u32[]{:S(2)}, u32[]{:S(2)}) collective-permute-start(bf16[256,256]{1,0:T(8,128)(2,1)S(1)} %get-tuple-element.29), channel_id=1, source_target_pairs={{0,2},{2,3},{3,1},{1,0},{4,6},{6,7},{7,5},{5,4},{8,10},{10,11},{11... | collective-permute-start | bytes 393224 | tf_op jit(solution)/shard_map/ppermute | solution.py:353
  34.9 6.9 %collective-permute-start.11 = (bf16[256,256]{1,0:T(8,128)(2,1)S(1)}, bf16[256,256]{1,0:T(8,128)(2,1)S(1)}, u32[]{:S(2)}, u32[]{:S(2)}) collective-permute-start(bf16[256,256]{1,0:T(8,128)(2,1)S(1)} %get-tuple-element.33), channel_id=1, source_target_pairs={{0,2},{2,3},{3,1},{1,0},{4,6},{6,7},{7,5},{5,4},{8,10},{10,11},{11... | collective-permute-start | bytes 393224 | tf_op jit(solution)/shard_map/ppermute | solution.py:353
  42.5 1.5 %collective-permute-start.12 = (f32[64,640]{1,0:T(8,128)S(1)}, f32[64,640]{1,0:T(8,128)S(1)}, u32[]{:S(2)}, u32[]{:S(2)}) collective-permute-start(f32[64,640]{1,0:T(8,128)S(1)} %get-tuple-element.38), channel_id=1, source_target_pairs={{4,0},{0,4},{5,1},{1,5},{6,2},{2,6},{7,3},{3,7},{12,8},{8,12},{13,... | collective-permute-start | bytes 491528 | tf_op jit(solution)/shard_map/ppermute | solution.py:370

commit v13 on v12

--- a/solution.py
+++ b/solution.py
@@ -14,12 +14,51 @@
 LANES = 128
 SCALE = HEAD_DIM**-0.5
 WEIGH_FLOPS = 6 * 10**9
+SPLIT_FLOPS = 30 * 10**9
 VMEM = pl.BlockSpec(memory_space=pltpu.VMEM)
 HBM = pl.BlockSpec(memory_space=pltpu.HBM)
 
 
 def ring_order(count):
     return list(range(0, count, 2)) + list(range(1, count, 2))[::-1]
+
+
+def ring_owners(count):
+    order = ring_order(count)
+    before = {order[(i + 1) % count]: order[i] for i in range(count)}
+    owners = [list(range(count))]
+    for _ in range(count - 1):
+        owners.append([owners[-1][before[i]] for i in range(count)])
+    return owners
+
+
+def ring_rounds(held, count):
+    order = ring_order(count)
+    ring = [(order[i], order[(i + 1) % count]) for i in range(count)]
+    rounds = [held]
+    for turn in range(count - 1):
+        pieces = [p for h in rounds[-1] for p in split(h, 2)] if turn == count - 2 else rounds[-1]
+        rounds.append([lax.ppermute(p, "head", ring) for p in pieces])
+    return rounds
+
+
+def line_owners():
+    return [[0, 1, 2, 3], [1, 0, 3, 2], [2, 2, 1, 1], [3, 3, 0, 0]]
+
+
+def line_rounds(held, beside):
+    ends, middle, out = [(0, 1), (1, 0), (2, 3), (3, 2)], [(1, 2), (2, 1)], [(1, 0), (2, 3)]
+    send = lambda chunk, pairs: lax.ppermute(chunk, "head", pairs)
+    near, over, third, fourth = [], [], [], []
+    for chunk in held:
+        near.append(send(chunk, ends))
+        over.append(send(chunk, middle))
+    near[0], beside = lax.optimization_barrier((near[0], beside))
+    for i in range(len(held)):
+        far = send(near[i], middle)
+        third.append((over[i], send(over[i], out)))
+        fourth += [(piece, send(piece, out)) for piece in split(far, 1 if i < len(held) - 1 else 2)]
+    return [held, near, third, fourth], beside
 
 
 def links_of(count):
@@ -175,40 +214,53 @@
             pl.when(shard == i)(functools.partial(act, maps))
 
 
-def halve_kernel(source, *outs):
+def split_kernel(source, *outs):
     width = outs[0].shape[1]
     for i, out in enumerate(outs):
         out[...] = source[:, i * width : (i + 1) * width]
 
 
-def halve(chunk):
+def split(chunk, parts):
     rows, width = chunk.shape
-    return call(halve_kernel, "halve", [((rows, width // 2), chunk.dtype)] * 2, [chunk], flops=3 * 10**10)
-
-
-def project_kernel(chunks, shards, map_rows, has_acc, place, *refs):
+    return call(split_kernel, "split", [((rows, width // parts), chunk.dtype)] * parts, [chunk], flops=SPLIT_FLOPS)
+
+
+def flat(chunks):
+    pairs = isinstance(chunks[0], tuple)
+    return ([x for pair in chunks for x in pair] if pairs else list(chunks)), pairs
+
+
+def joined(refs, pairs):
+    chunks = [r[...] for r in refs]
+    if pairs:
+        chunks = [a + b for a, b in zip(chunks[::2], chunks[1::2])]
+    return jnp.concatenate(chunks, axis=1)
+
+
+def project_kernel(chunks, pairs, shards, map_rows, has_acc, place, *refs):
     e_refs, maps, out_ref = refs[:chunks], refs[chunks : chunks + shards], refs[-1]
     half = out_ref.shape[1] // 2
     depth = e_refs[0].shape[1]
     shard, row = place()
     row = pl.multiple_of(row, depth)
-    chunk = jnp.concatenate([r[...] for r in e_refs], axis=1)
+    chunk = joined(e_refs, pairs)
 
     def add(map_ref):
         for side in range(2):
             columns = slice(side * half, (side + 1) * half)
-            product = dot(chunk, map_ref[pl.ds(side * map_rows + row, depth * chunks), :])
+            product = dot(chunk, map_ref[pl.ds(side * map_rows + row, chunk.shape[1]), :])
             out_ref[:, columns] = refs[-2][:, columns] + product if has_acc else product
 
     in_shard(maps, shard, add)
 
 
 def project(acc, chunks, place, shards, map_rows):
+    chunks, pairs = flat(chunks)
     rows, depth = chunks[0].shape
     width = shards[0].shape[1]
     operands = [*chunks, *shards] + ([] if acc is None else [acc])
     return call(
-        functools.partial(project_kernel, len(chunks), len(shards), map_rows, acc is not None, place),
+        functools.partial(project_kernel, len(chunks), pairs, len(shards), map_rows, acc is not None, place),
         "project",
         [((rows, 2 * width), F32)],
         operands,
@@ -252,9 +304,10 @@
     )
 
 
-def cross_kernel(acc_ref, e_ref, map_ref, tgt_ref, mask_ref, *outs):
+def cross_kernel(pieces, pairs, *refs):
+    chunk = joined(refs[:pieces], pairs)
+    acc_ref, map_ref, tgt_ref, mask_ref, *outs = refs[pieces:]
     heads = map_ref.shape[1] // 2 // HEAD_DIM
-    chunk = e_ref[...]
     memory = []
     for h in range(2 * heads):
         at = head_columns(h)
@@ -278,12 +331,13 @@
 def cross_attend(acc, chunk, maps, targets, mask, parts):
     width = targets.shape[1]
     count = targets.shape[0] // parts
-    return call(
-        cross_kernel,
+    pieces, pairs = flat([chunk])
+    return call(
+        functools.partial(cross_kernel, len(pieces), pairs),
         "cross_attend",
         [((count, width + LANES), F32)] * parts,
-        [acc, chunk, maps, targets, mask],
-        flops=2 * chunk.size * 2 * width,
+        [*pieces, acc, maps, targets, mask],
+        flops=2 * maps.size * acc.shape[0],
     )
 
 
@@ -311,15 +365,6 @@
     marks = (doc_ids if n_ctx == 2 else doc_ids + 1).reshape(1, rows)
     keys, near_marks, values = bring(enc_key), bring(marks), bring(enc_value)
     query, own_key, own_value, marks = fetch(enc_query, enc_key, enc_value, marks)
-    near_targets = []
-    if n_ctx == 2:
-        own_maps = pack(key_map, value_map, tgt_query)
-        shards = [own_maps, *bring(own_maps)]
-    else:
-        whole = [lax.all_gather(x, "ctx", axis=0, tiled=True) for x in (key_map, value_map)]
-        shards, near_targets = [pack(*whole, tgt_query)], bring(tgt_query)
-    map_rows = (shards[0].shape[0] - tgt_rows) // 2
-
     chunks = 2
     heads = features // HEAD_DIM // chunks
     held = [None] * chunks
@@ -327,18 +372,23 @@
         weights, totals = weigh(query, [own_key, *keys], [marks, *near_marks], j * heads, heads)
         held[j] = mix(weights, totals, [own_value, *values], j * heads, heads)
 
-    order = ring_order(n_head)
-    ring = [(order[i], order[(i + 1) % n_head]) for i in range(n_head)]
-    before = {target: source for source, target in ring}
+    key_map, value_map, tgt_query, held[0] = lax.optimization_barrier((key_map, value_map, tgt_query, held[0]))
+    if n_ctx == 2:
+        own_maps, near_targets = pack(key_map, value_map, tgt_query), []
+    else:
+        whole = [lax.all_gather(x, "ctx", axis=0, tiled=True) for x in (key_map, value_map)]
+        own_maps, near_targets = pack(*whole, tgt_query), bring(tgt_query)
+    map_rows = (own_maps.shape[0] - tgt_rows) // 2
+
+    if n_head == 4:
+        owners, (rounds, own_maps) = line_owners(), line_rounds(held, own_maps)
+    else:
+        owners, rounds = ring_owners(n_head), ring_rounds(held, n_head)
+    shards = [own_maps, *bring(own_maps)] if n_ctx == 2 else [own_maps]
 
     def place(turn, first):
         head, ctx = lax.axis_index("head"), lax.axis_index("ctx")
-        owner = 0
-        for i in range(n_head):
-            source = i
-            for _ in range(turn):
-                source = before[source]
-            owner = owner + jnp.where(head == i, source, 0)
+        owner = sum(jnp.where(head == i, source, 0) for i, source in enumerate(owners[turn]))
         row = owner * features + first
         if len(shards) == 1:
             return None, row
@@ -346,15 +396,10 @@
 
     acc, last = None, n_head - 1
     for turn in range(last):
-        if turn == last - 1:
-            pieces = [p for h in held for p in halve(h)]
-        else:
-            pieces = held
-        later = [lax.ppermute(p, "head", ring) for p in pieces]
-        acc = project(acc, held, functools.partial(place, turn, 0), shards, map_rows)
-        held = later
+        acc = project(acc, rounds[turn], functools.partial(place, turn, 0), shards, map_rows)
+    held = rounds[last]
     acc = project(acc, held[:-1], functools.partial(place, last, 0), shards, map_rows)
-    depth = held[-1].shape[1]
+    depth = flat(held[-1:])[0][0].shape[1]
     last_maps, targets, mask = prepare(
         functools.partial(place, last, features - depth),
         depth,

time: 44.9 us -> 48.9 us (1.089)
  waiting for transfers between devices: 12.5 us -> 20.6 us
  starting transfers between devices: 22.2 us -> 17.7 us
    ppermute x8 -> x11, waiting for transfers between devices: 11.1 us -> 18 us  [line_rounds(): send = lambda chunk, pairs: lax.ppermute(chunk, 'head', pairs)]
    ppermute x8 -> x11, starting transfers between devices: 21.1 us -> 16.6 us  [line_rounds(): send = lambda chunk, pairs: lax.ppermute(chunk, 'head', pairs)]
    ppermute x4, waiting for transfers between devices: 0.01 us -> 1.26 us  [on_device(): bring = lambda x: [lax.ppermute(x, 'ctx', pairs) for pairs in links]]
  transfers between devices with their start and end apart: 13 -> 16, of which waited for: 6 -> 6; matrix products, arithmetic and copies ran while one was open for 0% -> 0% of each run, Pallas kernels for 18% -> 17%
where the time goes in v13:
time: 48.9 us; the launch traced here: 48.6 us
  waiting for transfers between devices  20.6 us (42%)
  starting transfers between devices  17.7 us (36%)
  Pallas kernels  10 us (20%)
    ppermute x11, waiting for transfers between devices, line_rounds(): send = lambda chunk, pairs: lax.ppermute(chunk, 'head', pairs)  18 us
    ppermute x11, starting transfers between devices, line_rounds(): send = lambda chunk, pairs: lax.ppermute(chunk, 'head', pairs)  16.6 us
    pallas_call x15, Pallas kernels, call(): pl.pallas_call(kernel, in_specs=specs or [VMEM] * len(operands), out_spec...  10 us
    ppermute x1, waiting for transfers between devices, on_device(): lax.ppermute(piece, 'ctx', [(target, source) for source, target in pairs])  1.38 us
    ppermute x4, waiting for transfers between devices, on_device(): bring = lambda x: [lax.ppermute(x, 'ctx', pairs) for pairs in links]  1.26 us
    ppermute x4, starting transfers between devices, on_device(): bring = lambda x: [lax.ppermute(x, 'ctx', pairs) for pairs in links]  1.03 us
  transfers between devices with their start and end apart: 16, of which 6 were waited for; matrix products, arithmetic and copies ran while one was open for 0% of the time, Pallas kernels for 17%

profile of v13, /device:TPU:0, one launch (start us, length us, event | category | flops | bytes accessed | tf_op | source)
XLA Modules:
  0.0 48.6 jit_solution(8414664238023530307)
XLA Ops:
  1.0 1.4 %fetch.1 = (bf16[256,1024]{1,0:T(8,128)(2,1)S(1)}, bf16[256,1024]{1,0:T(8,128)(2,1)S(1)}, bf16[256,1024]{1,0:T(8,128)(2,1)S(1)}, s32[1,256]{1,0:T(1,128)S(1)}) custom-call(bf16[256,1024]{1,0:T(8,128)(2,1)} %refs_0_.1, bf16[256,1024]{1,0:T(8,128)(2,1)} %refs_1_.1, bf16[256,1024]{1,0:T(8,128)(2,1)} %refs_2_.1, s32[1,256]{1,0:T(1,128)} %bitcast.2), custom_call_target="tpu_custom_call" | custom-call | bytes 3147776 | tf_op jit(solution)/shard_map/fetch/pallas_call | solution.py:100
  3.3 3.0 %collective-permute-start.6 = (bf16[256,512]{1,0:T(8,128)(2,1)S(1)}, bf16[256,512]{1,0:T(8,128)(2,1)S(1)}, u32[]{:S(2)}, u32[]{:S(2)}) collective-permute-start(bf16[256,512]{1,0:T(8,128)(2,1)S(1)} %mix.3.refs_0_), channel_id=1, source_target_pairs={{0,1},{1,0},{2,3},{3,2},{4,5},{5,4},{6,7},{7,6},{8,9},{9,8},{10,11... | collective-permute-start | bytes 786440 | tf_op jit(solution)/shard_map/ppermute | solution.py:51
  6.3 0.7 %collective-permute-start.11 = (bf16[256,512]{1,0:T(8,128)(2,1)S(1)}, bf16[256,512]{1,0:T(8,128)(2,1)S(1)}, u32[]{:S(2)}, u32[]{:S(2)}) collective-permute-start(bf16[256,512]{1,0:T(8,128)(2,1)S(1)} %mix.3.refs_0_), channel_id=1, source_target_pairs={{1,2},{2,1},{5,6},{6,5},{9,10},{10,9},{13,14},{14,13},{17,18},{18,... | collective-permute-start | bytes 786440 | tf_op jit(solution)/shard_map/ppermute | solution.py:51
  7.8 4.4 %collective-permute-start.3 = (bf16[256,512]{1,0:T(8,128)(2,1)S(1)}, bf16[256,512]{1,0:T(8,128)(2,1)S(1)}, u32[]{:S(2)}, u32[]{:S(2)}) collective-permute-start(bf16[256,512]{1,0:T(8,128)(2,1)S(1)} %mix.2.refs_1_), channel_id=1, source_target_pairs={{0,1},{1,0},{2,3},{3,2},{4,5},{5,4},{6,7},{7,6},{8,9},{9,8},{10,11... | collective-permute-start | bytes 786440 | tf_op jit(solution)/shard_map/ppermute | solution.py:51
  12.3 0.7 %collective-permute-start.13 = (bf16[256,512]{1,0:T(8,128)(2,1)S(1)}, bf16[256,512]{1,0:T(8,128)(2,1)S(1)}, u32[]{:S(2)}, u32[]{:S(2)}) collective-permute-start(bf16[256,512]{1,0:T(8,128)(2,1)S(1)} %mix.2.refs_1_), channel_id=1, source_target_pairs={{1,2},{2,1},{5,6},{6,5},{9,10},{10,9},{13,14},{14,13},{17,18},{18,... | collective-permute-start | bytes 786440 | tf_op jit(solution)/shard_map/ppermute | solution.py:51
  13.0 2.3 %pack.1.refs_2_.refs_4_.refs_0_ = bf16[4160,512]{1,0:T(8,128)(2,1)S(1)} custom-call(bf16[2048,512]{1,0:T(8,128)(2,1)} %refs_0_.2, bf16[2048,512]{1,0:T(8,128)(2,1)} %refs_1_.2, bf16[64,512]{1,0:T(8,128)(2,1)} %refs_2_.2), custom_call_target="tpu_custom_call" | custom-call | bytes 8519680 | tf_op jit(solution)/shard_map/pack/pallas_call | solution.py:100
  15.2 0.7 %collective-permute-start.7 = (bf16[256,512]{1,0:T(8,128)(2,1)S(1)}, bf16[256,512]{1,0:T(8,128)(2,1)S(1)}, u32[]{:S(2)}, u32[]{:S(2)}) collective-permute-start(bf16[256,512]{1,0:T(8,128)(2,1)S(1)} %collective-permute-done.6.refs_0_), channel_id=1, source_target_pairs={{1,2},{2,1},{5,6},{6,5},{9,10},{10,9},{13,14},{14,13},{17,18},{18,... | collective-permute-start | bytes 786440 | tf_op jit(solution)/shard_map/ppermute | solution.py:51
  16.0 1.3 %collective-permute-start.12 = (bf16[256,512]{1,0:T(8,128)(2,1)S(1)}, bf16[256,512]{1,0:T(8,128)(2,1)S(1)}, u32[]{:S(2)}, u32[]{:S(2)}) collective-permute-start(bf16[256,512]{1,0:T(8,128)(2,1)S(1)} %collective-permute-done.11.refs_0_), channel_id=1, source_target_pairs={{1,0},{2,3},{5,4},{6,7},{9,8},{10,11},{13,12},{14,15},{17,16},{18,... | collective-permute-start | bytes 786440 | tf_op jit(solution)/shard_map/ppermute | solution.py:51
  17.3 1.3 %collective-permute-start.14 = (bf16[256,512]{1,0:T(8,128)(2,1)S(1)}, bf16[256,512]{1,0:T(8,128)(2,1)S(1)}, u32[]{:S(2)}, u32[]{:S(2)}) collective-permute-start(bf16[256,512]{1,0:T(8,128)(2,1)S(1)} %collective-permute-done.13.refs_2_), channel_id=1, source_target_pairs={{1,0},{2,3},{5,4},{6,7},{9,8},{10,11},{13,12},{14,15},{17,16},{18,... | collective-permute-start | bytes 786440 | tf_op jit(solution)/shard_map/ppermute | solution.py:51
  18.6 0.7 %collective-permute-start.4 = (bf16[256,512]{1,0:T(8,128)(2,1)S(1)}, bf16[256,512]{1,0:T(8,128)(2,1)S(1)}, u32[]{:S(2)}, u32[]{:S(2)}) collective-permute-start(bf16[256,512]{1,0:T(8,128)(2,1)S(1)} %collective-permute-done.3.refs_1_), channel_id=1, source_target_pairs={{1,2},{2,1},{5,6},{6,5},{9,10},{10,9},{13,14},{14,13},{17,18},{18,... | collective-permute-start | bytes 786440 | tf_op jit(solution)/shard_map/ppermute | solution.py:51
  19.3 1.3 %collective-permute-start.8 = (bf16[256,512]{1,0:T(8,128)(2,1)S(1)}, bf16[256,512]{1,0:T(8,128)(2,1)S(1)}, u32[]{:S(2)}, u32[]{:S(2)}) collective-permute-start(bf16[256,512]{1,0:T(8,128)(2,1)S(1)} %split.3.refs_0_), channel_id=1, source_target_pairs={{1,0},{2,3},{5,4},{6,7},{9,8},{10,11},{13,12},{14,15},{17,16},{18,... | collective-permute-start | bytes 786440 | tf_op jit(solution)/shard_map/ppermute | solution.py:51
  20.7 1.3 %collective-permute-start.9 = (bf16[256,256]{1,0:T(8,128)(2,1)S(1)}, bf16[256,256]{1,0:T(8,128)(2,1)S(1)}, u32[]{:S(2)}, u32[]{:S(2)}) collective-permute-start(bf16[256,256]{1,0:T(8,128)(2,1)S(1)} %get-tuple-element.40.refs_2_), channel_id=1, source_target_pairs={{1,0},{2,3},{5,4},{6,7},{9,8},{10,11},{13,12},{14,15},{17,16},{18,... | collective-permute-start | bytes 393224 | tf_op jit(solution)/shard_map/ppermute | solution.py:51
  22.0 1.2 %collective-permute-done.10.refs_3_.refs_5_.refs_1_ = bf16[4160,512]{1,0:T(8,128)(2,1)S(1)} collective-permute-done((bf16[4160,512]{1,0:T(8,128)(2,1)S(1)}, bf16[4160,512]{1,0:T(8,128)(2,1)S(1)}, u32[]{:S(2)}, u32[]{:S(2)}) %collective-permute-start.10) | collective-permute-done | bytes 4259872 | tf_op jit(solution)/shard_map/ppermute | solution.py:363
  23.2 1.3 %collective-permute-start.5 = (bf16[256,256]{1,0:T(8,128)(2,1)S(1)}, bf16[256,256]{1,0:T(8,128)(2,1)S(1)}, u32[]{:S(2)}, u32[]{:S(2)}) collective-permute-start(bf16[256,256]{1,0:T(8,128)(2,1)S(1)} %get-tuple-element.32.refs_0_), channel_id=1, source_target_pairs={{1,0},{2,3},{5,4},{6,7},{9,8},{10,11},{13,12},{14,15},{17,16},{18,... | collective-permute-start | bytes 393224 | tf_op jit(solution)/shard_map/ppermute | solution.py:51
  24.5 0.7 %project.4.refs_4_ = f32[256,1024]{1,0:T(8,128)S(1)} custom-call(bf16[256,512]{1,0:T(8,128)(2,1)S(1)} %mix.3.refs_0_, bf16[256,512]{1,0:T(8,128)(2,1)S(1)} %mix.2.refs_1_, bf16[4160,512]{1,0:T(8,128)(2,1)S(1)} %pack.1.refs_2_.refs_4_.refs_0_, bf16[4160,512]{1,0:T(8,128)(2,1)S(1)} %collective-permute-done.10.refs_3_.refs_5_.refs_1_), custom_call_target="tpu_custom_call" | custom-call | flops 536870912 | bytes 10092544 | tf_op jit(solution)/shard_map/project/pallas_call | solution.py:100
  25.3 0.7 %project.5.refs_6_ = f32[256,1024]{1,0:T(8,128)S(1)} custom-call(bf16[256,512]{1,0:T(8,128)(2,1)S(1)} %collective-permute-done.6.refs_0_, bf16[256,512]{1,0:T(8,128)(2,1)S(1)} %collective-permute-done.3.refs_1_, bf16[4160,512]{1,0:T(8,128)(2,1)S(1)} %pack.1.refs_2_.refs_4_.refs_0_, bf16[4160,512]{1,0:T(8,128)(2,1)S(1)} %collective-permute-done.10.refs_3_.refs_5_.refs_1_, ...), custom_call_target="tpu_custom_call" | custom-call | flops 536870912 | bytes 11141120 | tf_op jit(solution)/shard_map/project/pallas_call | solution.py:100
  26.0 2.9 %collective-permute-done.12.refs_1_ = bf16[256,512]{1,0:T(8,128)(2,1)S(1)} collective-permute-done((bf16[256,512]{1,0:T(8,128)(2,1)S(1)}, bf16[256,512]{1,0:T(8,128)(2,1)S(1)}, u32[]{:S(2)}, u32[]{:S(2)}) %collective-permute-start.12) | collective-permute-done | bytes 262176 | tf_op jit(solution)/shard_map/ppermute | solution.py:51
  28.9 5.6 %collective-permute-done.14.refs_3_ = bf16[256,512]{1,0:T(8,128)(2,1)S(1)} collective-permute-done((bf16[256,512]{1,0:T(8,128)(2,1)S(1)}, bf16[256,512]{1,0:T(8,128)(2,1)S(1)}, u32[]{:S(2)}, u32[]{:S(2)}) %collective-permute-start.14) | collective-permute-done | bytes 262176 | tf_op jit(solution)/shard_map/ppermute | solution.py:51
  34.6 0.8 %project.6.refs_6_ = f32[256,1024]{1,0:T(8,128)S(1)} custom-call(bf16[256,512]{1,0:T(8,128)(2,1)S(1)} %collective-permute-done.11.refs_0_, bf16[256,512]{1,0:T(8,128)(2,1)S(1)} %collective-permute-done.12.refs_1_, bf16[256,512]{1,0:T(8,128)(2,1)S(1)} %collective-permute-done.13.refs_2_, bf16[256,512]{1,0:T(8,128)(2,1)S(1)} %collective-permute-done.14.refs_3_, ...), custom_call_target="tpu_custom_call" | custom-call | flops 1073741824 | bytes 11665408 | tf_op jit(solution)/shard_map/project/pallas_call | solution.py:100
  35.5 7.4 %collective-permute-done.9.refs_3_ = bf16[256,256]{1,0:T(8,128)(2,1)S(1)} collective-permute-done((bf16[256,256]{1,0:T(8,128)(2,1)S(1)}, bf16[256,256]{1,0:T(8,128)(2,1)S(1)}, u32[]{:S(2)}, u32[]{:S(2)}) %collective-permute-start.9) | collective-permute-done | bytes 131104 | tf_op jit(solution)/shard_map/ppermute | solution.py:51
  43.6 2.0 %collective-permute-done.5.refs_1_ = bf16[256,256]{1,0:T(8,128)(2,1)S(1)} collective-permute-done((bf16[256,256]{1,0:T(8,128)(2,1)S(1)}, bf16[256,256]{1,0:T(8,128)(2,1)S(1)}, u32[]{:S(2)}, u32[]{:S(2)}) %collective-permute-start.5) | collective-permute-done | bytes 131104 | tf_op jit(solution)/shard_map/ppermute | solution.py:51
  45.6 0.7 %cross_attend.1 = (f32[64,640]{1,0:T(8,128)S(1)}, f32[64,640]{1,0:T(8,128)S(1)}) custom-call(bf16[256,256]{1,0:T(8,128)(2,1)S(1)} %get-tuple-element.32.refs_0_, bf16[256,256]{1,0:T(8,128)(2,1)S(1)} %collective-permute-done.5.refs_1_, f32[256,1024]{1,0:T(8,128)S(1)} %project.7.refs_2_, bf16[256,1024]{1,0:T(8,128)(2,1)S(1)} %get-tuple-element.42.refs_3_, ...), custom_call_target="tpu_custom_call" | custom-call | flops 134217728 | bytes 2424832 | tf_op jit(solution)/shard_map/cross_attend/pallas_call | solution.py:100
  46.3 1.4 %collective-permute-done.15.refs_1_ = f32[64,640]{1,0:T(8,128)S(1)} collective-permute-done((f32[64,640]{1,0:T(8,128)S(1)}, f32[64,640]{1,0:T(8,128)S(1)}, u32[]{:S(2)}, u32[]{:S(2)}) %collective-permute-start.15) | collective-permute-done | bytes 163872 | tf_op jit(solution)/shard_map/ppermute | solution.py:415
  47.7 0.8 %combine.1 = bf16[64,512]{1,0:T(8,128)(2,1)} custom-call(f32[64,640]{1,0:T(8,128)S(1)} %get-tuple-element.45.refs_0_, f32[64,640]{1,0:T(8,128)S(1)} %collective-permute-done.15.refs_1_), custom_call_target="tpu_custom_call" | custom-call | bytes 393216 | tf_op jit(solution)/shard_map/combine/pallas_call | solution.py:100
  (23 shorter events, 3.7 us)
Async XLA Ops:
  0.0 2.4 %collective-permute-start.1 = (bf16[256,1024]{1,0:T(8,128)(2,1)}, bf16[256,1024]{1,0:T(8,128)(2,1)S(1)}, u32[]{:S(2)}, u32[]{:S(2)}) collective-permute-start(bf16[256,1024]{1,0:T(8,128)(2,1)} %refs_1_.1), channel_id=1, source_target_pairs={{0,4},{4,0},{1,5},{5,1},{2,6},{6,2},{3,7},{7,3},{8,12},{12,8},{9,1... | collective-permute-start | bytes 1572872 | tf_op jit(solution)/shard_map/ppermute | solution.py:363
  0.5 1.9 %collective-permute-start = (s32[1,256]{1,0:T(1,128)}, s32[1,256]{1,0:T(1,128)S(1)}, u32[]{:S(2)}, u32[]{:S(2)}) collective-permute-start(s32[1,256]{1,0:T(1,128)} %bitcast.1), channel_id=1, source_target_pairs={{0,4},{4,0},{1,5},{5,1},{2,6},{6,2},{3,7},{7,3},{8,12},{12,8},{9,1... | collective-permute-start | bytes 3080 | tf_op jit(solution)/shard_map/ppermute | solution.py:363
  0.5 2.4 %collective-permute-start.2 = (bf16[256,1024]{1,0:T(8,128)(2,1)}, bf16[256,1024]{1,0:T(8,128)(2,1)S(1)}, u32[]{:S(2)}, u32[]{:S(2)}) collective-permute-start(bf16[256,1024]{1,0:T(8,128)(2,1)} %refs_2_.1), channel_id=1, source_target_pairs={{0,4},{4,0},{1,5},{5,1},{2,6},{6,2},{3,7},{7,3},{8,12},{12,8},{9,1... | collective-permute-start | bytes 1572872 | tf_op jit(solution)/shard_map/ppermute | solution.py:363
  3.3 11.9 %collective-permute-start.6 = (bf16[256,512]{1,0:T(8,128)(2,1)S(1)}, bf16[256,512]{1,0:T(8,128)(2,1)S(1)}, u32[]{:S(2)}, u32[]{:S(2)}) collective-permute-start(bf16[256,512]{1,0:T(8,128)(2,1)S(1)} %mix.3.refs_0_), channel_id=1, source_target_pairs={{0,1},{1,0},{2,3},{3,2},{4,5},{5,4},{6,7},{7,6},{8,9},{9,8},{10,11... | collective-permute-start | bytes 786440 | tf_op jit(solution)/shard_map/ppermute | solution.py:51
  6.3 9.7 %collective-permute-start.11 = (bf16[256,512]{1,0:T(8,128)(2,1)S(1)}, bf16[256,512]{1,0:T(8,128)(2,1)S(1)}, u32[]{:S(2)}, u32[]{:S(2)}) collective-permute-start(bf16[256,512]{1,0:T(8,128)(2,1)S(1)} %mix.3.refs_0_), channel_id=1, source_target_pairs={{1,2},{2,1},{5,6},{6,5},{9,10},{10,9},{13,14},{14,13},{17,18},{18,... | collective-permute-start | bytes 786440 | tf_op jit(solution)/shard_map/ppermute | solution.py:51
  7.8 10.8 %collective-permute-start.3 = (bf16[256,512]{1,0:T(8,128)(2,1)S(1)}, bf16[256,512]{1,0:T(8,128)(2,1)S(1)}, u32[]{:S(2)}, u32[]{:S(2)}) collective-permute-start(bf16[256,512]{1,0:T(8,128)(2,1)S(1)} %mix.2.refs_1_), channel_id=1, source_target_pairs={{0,1},{1,0},{2,3},{3,2},{4,5},{5,4},{6,7},{7,6},{8,9},{9,8},{10,11... | collective-permute-start | bytes 786440 | tf_op jit(solution)/shard_map/ppermute | solution.py:51
  12.3 5.0 %collective-permute-start.13 = (bf16[256,512]{1,0:T(8,128)(2,1)S(1)}, bf16[256,512]{1,0:T(8,128)(2,1)S(1)}, u32[]{:S(2)}, u32[]{:S(2)}) collective-permute-start(bf16[256,512]{1,0:T(8,128)(2,1)S(1)} %mix.2.refs_1_), channel_id=1, source_target_pairs={{1,2},{2,1},{5,6},{6,5},{9,10},{10,9},{13,14},{14,13},{17,18},{18,... | collective-permute-start | bytes 786440 | tf_op jit(solution)/shard_map/ppermute | solution.py:51
  15.2 4.1 %collective-permute-start.7 = (bf16[256,512]{1,0:T(8,128)(2,1)S(1)}, bf16[256,512]{1,0:T(8,128)(2,1)S(1)}, u32[]{:S(2)}, u32[]{:S(2)}) collective-permute-start(bf16[256,512]{1,0:T(8,128)(2,1)S(1)} %collective-permute-done.6.refs_0_), channel_id=1, source_target_pairs={{1,2},{2,1},{5,6},{6,5},{9,10},{10,9},{13,14},{14,13},{17,18},{18,... | collective-permute-start | bytes 786440 | tf_op jit(solution)/shard_map/ppermute | solution.py:51
  15.9 7.3 %collective-permute-start.10 = (bf16[4160,512]{1,0:T(8,128)(2,1)S(1)}, bf16[4160,512]{1,0:T(8,128)(2,1)S(1)}, u32[]{:S(2)}, u32[]{:S(2)}) collective-permute-start(bf16[4160,512]{1,0:T(8,128)(2,1)S(1)} %pack.1.refs_2_.refs_4_.refs_0_), channel_id=1, source_target_pairs={{0,4},{4,0},{1,5},{5,1},{2,6},{6,2},{3,7},{7,3},{8,12},{12,8},{9,1... | collective-permute-start | bytes 12779528 | tf_op jit(solution)/shard_map/ppermute | solution.py:363
  16.0 12.9 %collective-permute-start.12 = (bf16[256,512]{1,0:T(8,128)(2,1)S(1)}, bf16[256,512]{1,0:T(8,128)(2,1)S(1)}, u32[]{:S(2)}, u32[]{:S(2)}) collective-permute-start(bf16[256,512]{1,0:T(8,128)(2,1)S(1)} %collective-permute-done.11.refs_0_), channel_id=1, source_target_pairs={{1,0},{2,3},{5,4},{6,7},{9,8},{10,11},{13,12},{14,15},{17,16},{18,... | collective-permute-start | bytes 786440 | tf_op jit(solution)/shard_map/ppermute | solution.py:51
  17.3 17.3 %collective-permute-start.14 = (bf16[256,512]{1,0:T(8,128)(2,1)S(1)}, bf16[256,512]{1,0:T(8,128)(2,1)S(1)}, u32[]{:S(2)}, u32[]{:S(2)}) collective-permute-start(bf16[256,512]{1,0:T(8,128)(2,1)S(1)} %collective-permute-done.13.refs_2_), channel_id=1, source_target_pairs={{1,0},{2,3},{5,4},{6,7},{9,8},{10,11},{13,12},{14,15},{17,16},{18,... | collective-permute-start | bytes 786440 | tf_op jit(solution)/shard_map/ppermute | solution.py:51
  18.6 2.0 %collective-permute-start.4 = (bf16[256,512]{1,0:T(8,128)(2,1)S(1)}, bf16[256,512]{1,0:T(8,128)(2,1)S(1)}, u32[]{:S(2)}, u32[]{:S(2)}) collective-permute-start(bf16[256,512]{1,0:T(8,128)(2,1)S(1)} %collective-permute-done.3.refs_1_), channel_id=1, source_target_pairs={{1,2},{2,1},{5,6},{6,5},{9,10},{10,9},{13,14},{14,13},{17,18},{18,... | collective-permute-start | bytes 786440 | tf_op jit(solution)/shard_map/ppermute | solution.py:51
  19.3 23.6 %collective-permute-start.8 = (bf16[256,512]{1,0:T(8,128)(2,1)S(1)}, bf16[256,512]{1,0:T(8,128)(2,1)S(1)}, u32[]{:S(2)}, u32[]{:S(2)}) collective-permute-start(bf16[256,512]{1,0:T(8,128)(2,1)S(1)} %split.3.refs_0_), channel_id=1, source_target_pairs={{1,0},{2,3},{5,4},{6,7},{9,8},{10,11},{13,12},{14,15},{17,16},{18,... | collective-permute-start | bytes 786440 | tf_op jit(solution)/shard_map/ppermute | solution.py:51
  20.7 22.3 %collective-permute-start.9 = (bf16[256,256]{1,0:T(8,128)(2,1)S(1)}, bf16[256,256]{1,0:T(8,128)(2,1)S(1)}, u32[]{:S(2)}, u32[]{:S(2)}) collective-permute-start(bf16[256,256]{1,0:T(8,128)(2,1)S(1)} %get-tuple-element.40.refs_2_), channel_id=1, source_target_pairs={{1,0},{2,3},{5,4},{6,7},{9,8},{10,11},{13,12},{14,15},{17,16},{18,... | collective-permute-start | bytes 393224 | tf_op jit(solution)/shard_map/ppermute | solution.py:51
  23.2 22.4 %collective-permute-start.5 = (bf16[256,256]{1,0:T(8,128)(2,1)S(1)}, bf16[256,256]{1,0:T(8,128)(2,1)S(1)}, u32[]{:S(2)}, u32[]{:S(2)}) collective-permute-start(bf16[256,256]{1,0:T(8,128)(2,1)S(1)} %get-tuple-element.32.refs_0_), channel_id=1, source_target_pairs={{1,0},{2,3},{5,4},{6,7},{9,8},{10,11},{13,12},{14,15},{17,16},{18,... | collective-permute-start | bytes 393224 | tf_op jit(solution)/shard_map/ppermute | solution.py:51
  46.3 1.5 %collective-permute-start.15 = (f32[64,640]{1,0:T(8,128)S(1)}, f32[64,640]{1,0:T(8,128)S(1)}, u32[]{:S(2)}, u32[]{:S(2)}) collective-permute-start(f32[64,640]{1,0:T(8,128)S(1)} %get-tuple-element.46), channel_id=1, source_target_pairs={{4,0},{0,4},{5,1},{1,5},{6,2},{2,6},{7,3},{3,7},{12,8},{8,12},{13,... | collective-permute-start | bytes 491528 | tf_op jit(solution)/shard_map/ppermute | solution.py:415

commit v14 on v12

--- a/solution.py
+++ b/solution.py
@@ -252,7 +252,7 @@
     )
 
 
-def cross_kernel(acc_ref, e_ref, map_ref, tgt_ref, mask_ref, *outs):
+def cross_kernel(e_ref, acc_ref, map_ref, tgt_ref, mask_ref, *outs):
     heads = map_ref.shape[1] // 2 // HEAD_DIM
     chunk = e_ref[...]
     memory = []
@@ -282,7 +282,7 @@
         cross_kernel,
         "cross_attend",
         [((count, width + LANES), F32)] * parts,
-        [acc, chunk, maps, targets, mask],
+        [chunk, acc, maps, targets, mask],
         flops=2 * chunk.size * 2 * width,
     )
 
@@ -323,7 +323,7 @@
     chunks = 2
     heads = features // HEAD_DIM // chunks
     held = [None] * chunks
-    for j in reversed(range(chunks)):
+    for j in range(chunks):
         weights, totals = weigh(query, [own_key, *keys], [marks, *near_marks], j * heads, heads)
         held[j] = mix(weights, totals, [own_value, *values], j * heads, heads)
 

time: 44.9 us -> 44.3 us (0.987)
  starting transfers between devices: 22.2 us -> 21.6 us
    ppermute x8, starting transfers between devices: 21.1 us -> 20.5 us  [on_device(): later = [lax.ppermute(p, 'head', ring) for p in pieces]]
where the time goes in v14:
time: 44.3 us; the launch traced here: 44.2 us
  starting transfers between devices  21.6 us (49%)
  waiting for transfers between devices  12.5 us (28%)
  Pallas kernels  9.91 us (22%)
    ppermute x8, starting transfers between devices, on_device(): later = [lax.ppermute(p, 'head', ring) for p in pieces]  20.5 us
    ppermute x8, waiting for transfers between devices, on_device(): later = [lax.ppermute(p, 'head', ring) for p in pieces]  11.1 us
    pallas_call x15, Pallas kernels, call(): pl.pallas_call(kernel, in_specs=specs or [VMEM] * len(operands), out_spec...  9.91 us
    ppermute x1, waiting for transfers between devices, on_device(): lax.ppermute(piece, 'ctx', [(target, source) for source, target in pairs])  1.38 us
    ppermute x4, starting transfers between devices, on_device(): bring = lambda x: [lax.ppermute(x, 'ctx', pairs) for pairs in links]  1.03 us
  transfers between devices with their start and end apart: 13, of which 6 were waited for; matrix products, arithmetic and copies ran while one was open for 0% of the time, Pallas kernels for 18%

profile of v14, /device:TPU:0, one launch (start us, length us, event | category | flops | bytes accessed | tf_op | source)
XLA Modules:
  0.0 44.2 jit_solution(16189367986200226641)
XLA Ops:
  1.0 1.4 %fetch.1 = (bf16[256,1024]{1,0:T(8,128)(2,1)S(1)}, bf16[256,1024]{1,0:T(8,128)(2,1)S(1)}, bf16[256,1024]{1,0:T(8,128)(2,1)S(1)}, s32[1,256]{1,0:T(1,128)S(1)}) custom-call(bf16[256,1024]{1,0:T(8,128)(2,1)} %refs_0_.2, bf16[256,1024]{1,0:T(8,128)(2,1)} %refs_1_.2, bf16[256,1024]{1,0:T(8,128)(2,1)} %refs_2_.2, s32[1,256]{1,0:T(1,128)} %bitcast.2), custom_call_target="tpu_custom_call" | custom-call | bytes 3147776 | tf_op jit(solution)/shard_map/fetch/pallas_call | solution.py:61
  2.4 0.6 %weigh.3 = (bf16[256,1024]{1,0:T(8,128)(2,1)S(1)}, f32[256,128]{1,0:T(8,128)S(1)}) custom-call(s32[1,256]{1,0:T(1,128)S(1)} %get-tuple-element.22.refs_0_.refs_2_, s32[1,256]{1,0:T(1,128)S(1)} %collective-permute-done.refs_1_.refs_3_, bf16[256,1024]{1,0:T(8,128)(2,1)S(1)} %get-tuple-element.23.refs_2_, bf16[256,1024]{1,0:T(8,128)(2,1)S(1)} %get-tuple-element.24.refs_3_, ...), custom_call_target="tpu_custom_call" | custom-call | flops 6000000000 | bytes 2230272 | tf_op jit(solution)/shard_map/weigh/pallas_call | solution.py:61
  3.3 4.0 %collective-permute-start.6 = (bf16[256,512]{1,0:T(8,128)(2,1)S(1)}, bf16[256,512]{1,0:T(8,128)(2,1)S(1)}, u32[]{:S(2)}, u32[]{:S(2)}) collective-permute-start(bf16[256,512]{1,0:T(8,128)(2,1)S(1)} %mix.3.refs_0_), channel_id=1, source_target_pairs={{0,2},{2,3},{3,1},{1,0},{4,6},{6,7},{7,5},{5,4},{8,10},{10,11},{11... | collective-permute-start | bytes 786440 | tf_op jit(solution)/shard_map/ppermute | solution.py:353
  7.3 0.5 %weigh.2 = (bf16[256,1024]{1,0:T(8,128)(2,1)S(1)}, f32[256,128]{1,0:T(8,128)S(1)}) custom-call(s32[1,256]{1,0:T(1,128)S(1)} %get-tuple-element.22.refs_0_.refs_2_, s32[1,256]{1,0:T(1,128)S(1)} %collective-permute-done.refs_1_.refs_3_, bf16[256,1024]{1,0:T(8,128)(2,1)S(1)} %get-tuple-element.23.refs_2_, bf16[256,1024]{1,0:T(8,128)(2,1)S(1)} %get-tuple-element.24.refs_3_, ...), custom_call_target="tpu_custom_call" | custom-call | flops 6000000000 | bytes 2230272 | tf_op jit(solution)/shard_map/weigh/pallas_call | solution.py:61
  8.2 1.6 %collective-permute-start.3 = (bf16[256,512]{1,0:T(8,128)(2,1)S(1)}, bf16[256,512]{1,0:T(8,128)(2,1)S(1)}, u32[]{:S(2)}, u32[]{:S(2)}) collective-permute-start(bf16[256,512]{1,0:T(8,128)(2,1)S(1)} %mix.2.refs_1_), channel_id=1, source_target_pairs={{0,2},{2,3},{3,1},{1,0},{4,6},{6,7},{7,5},{5,4},{8,10},{10,11},{11... | collective-permute-start | bytes 786440 | tf_op jit(solution)/shard_map/ppermute | solution.py:353
  9.8 4.2 %collective-permute-done.6.refs_0_ = bf16[256,512]{1,0:T(8,128)(2,1)S(1)} collective-permute-done((bf16[256,512]{1,0:T(8,128)(2,1)S(1)}, bf16[256,512]{1,0:T(8,128)(2,1)S(1)}, u32[]{:S(2)}, u32[]{:S(2)}) %collective-permute-start.6) | collective-permute-done | bytes 262176 | tf_op jit(solution)/shard_map/ppermute | solution.py:353
  14.0 3.4 %collective-permute-start.7 = (bf16[256,512]{1,0:T(8,128)(2,1)S(1)}, bf16[256,512]{1,0:T(8,128)(2,1)S(1)}, u32[]{:S(2)}, u32[]{:S(2)}) collective-permute-start(bf16[256,512]{1,0:T(8,128)(2,1)S(1)} %collective-permute-done.6.refs_0_), channel_id=1, source_target_pairs={{0,2},{2,3},{3,1},{1,0},{4,6},{6,7},{7,5},{5,4},{8,10},{10,11},{11... | collective-permute-start | bytes 786440 | tf_op jit(solution)/shard_map/ppermute | solution.py:353
  17.3 2.2 %pack.1.refs_2_.refs_3_.refs_0_ = bf16[4160,512]{1,0:T(8,128)(2,1)S(1)} custom-call(bf16[2048,512]{1,0:T(8,128)(2,1)} %refs_0_.3, bf16[2048,512]{1,0:T(8,128)(2,1)} %refs_1_.3, bf16[64,512]{1,0:T(8,128)(2,1)} %refs_2_.3), custom_call_target="tpu_custom_call" | custom-call | bytes 8519680 | tf_op jit(solution)/shard_map/pack/pallas_call | solution.py:61
  19.7 3.3 %collective-permute-start.4 = (bf16[256,512]{1,0:T(8,128)(2,1)S(1)}, bf16[256,512]{1,0:T(8,128)(2,1)S(1)}, u32[]{:S(2)}, u32[]{:S(2)}) collective-permute-start(bf16[256,512]{1,0:T(8,128)(2,1)S(1)} %collective-permute-done.3.refs_1_), channel_id=1, source_target_pairs={{0,2},{2,3},{3,1},{1,0},{4,6},{6,7},{7,5},{5,4},{8,10},{10,11},{11... | collective-permute-start | bytes 786440 | tf_op jit(solution)/shard_map/ppermute | solution.py:353
  23.0 2.2 %collective-permute-done.7.source.refs_0_ = bf16[256,512]{1,0:T(8,128)(2,1)S(1)} collective-permute-done((bf16[256,512]{1,0:T(8,128)(2,1)S(1)}, bf16[256,512]{1,0:T(8,128)(2,1)S(1)}, u32[]{:S(2)}, u32[]{:S(2)}) %collective-permute-start.7) | collective-permute-done | bytes 262176 | tf_op jit(solution)/shard_map/ppermute | solution.py:353
  25.2 3.4 %collective-permute-start.8 = (bf16[256,256]{1,0:T(8,128)(2,1)S(1)}, bf16[256,256]{1,0:T(8,128)(2,1)S(1)}, u32[]{:S(2)}, u32[]{:S(2)}) collective-permute-start(bf16[256,256]{1,0:T(8,128)(2,1)S(1)} %get-tuple-element.31), channel_id=1, source_target_pairs={{0,2},{2,3},{3,1},{1,0},{4,6},{6,7},{7,5},{5,4},{8,10},{10,11},{11... | collective-permute-start | bytes 393224 | tf_op jit(solution)/shard_map/ppermute | solution.py:353
  28.6 0.7 %collective-permute-start.9 = (bf16[256,256]{1,0:T(8,128)(2,1)S(1)}, bf16[256,256]{1,0:T(8,128)(2,1)S(1)}, u32[]{:S(2)}, u32[]{:S(2)}) collective-permute-start(bf16[256,256]{1,0:T(8,128)(2,1)S(1)} %get-tuple-element.32), channel_id=1, source_target_pairs={{0,2},{2,3},{3,1},{1,0},{4,6},{6,7},{7,5},{5,4},{8,10},{10,11},{11... | collective-permute-start | bytes 393224 | tf_op jit(solution)/shard_map/ppermute | solution.py:353
  29.3 1.5 %collective-permute-done.4.source.refs_1_ = bf16[256,512]{1,0:T(8,128)(2,1)S(1)} collective-permute-done((bf16[256,512]{1,0:T(8,128)(2,1)S(1)}, bf16[256,512]{1,0:T(8,128)(2,1)S(1)}, u32[]{:S(2)}, u32[]{:S(2)}) %collective-permute-start.4) | collective-permute-done | bytes 262176 | tf_op jit(solution)/shard_map/ppermute | solution.py:353
  30.8 3.4 %collective-permute-start.10 = (bf16[256,256]{1,0:T(8,128)(2,1)S(1)}, bf16[256,256]{1,0:T(8,128)(2,1)S(1)}, u32[]{:S(2)}, u32[]{:S(2)}) collective-permute-start(bf16[256,256]{1,0:T(8,128)(2,1)S(1)} %get-tuple-element.33), channel_id=1, source_target_pairs={{0,2},{2,3},{3,1},{1,0},{4,6},{6,7},{7,5},{5,4},{8,10},{10,11},{11... | collective-permute-start | bytes 393224 | tf_op jit(solution)/shard_map/ppermute | solution.py:353
  34.3 0.7 %collective-permute-start.5 = (bf16[256,256]{1,0:T(8,128)(2,1)S(1)}, bf16[256,256]{1,0:T(8,128)(2,1)S(1)}, u32[]{:S(2)}, u32[]{:S(2)}) collective-permute-start(bf16[256,256]{1,0:T(8,128)(2,1)S(1)} %get-tuple-element.28), channel_id=1, source_target_pairs={{0,2},{2,3},{3,1},{1,0},{4,6},{6,7},{7,5},{5,4},{8,10},{10,11},{11... | collective-permute-start | bytes 393224 | tf_op jit(solution)/shard_map/ppermute | solution.py:353
  35.1 0.7 %project.4.refs_4_ = f32[256,1024]{1,0:T(8,128)S(1)} custom-call(bf16[256,512]{1,0:T(8,128)(2,1)S(1)} %mix.3.refs_0_, bf16[256,512]{1,0:T(8,128)(2,1)S(1)} %mix.2.refs_1_, bf16[4160,512]{1,0:T(8,128)(2,1)S(1)} %pack.1.refs_2_.refs_3_.refs_0_, bf16[4160,512]{1,0:T(8,128)(2,1)S(1)} %collective-permute-done.11.refs_3_.refs_4_.refs_1_), custom_call_target="tpu_custom_call" | custom-call | flops 536870912 | bytes 10092544 | tf_op jit(solution)/shard_map/project/pallas_call | solution.py:61
  35.9 0.7 %project.5.refs_4_ = f32[256,1024]{1,0:T(8,128)S(1)} custom-call(bf16[256,512]{1,0:T(8,128)(2,1)S(1)} %collective-permute-done.6.refs_0_, bf16[256,512]{1,0:T(8,128)(2,1)S(1)} %collective-permute-done.3.refs_1_, bf16[4160,512]{1,0:T(8,128)(2,1)S(1)} %pack.1.refs_2_.refs_3_.refs_0_, bf16[4160,512]{1,0:T(8,128)(2,1)S(1)} %collective-permute-done.11.refs_3_.refs_4_.refs_1_, ...), custom_call_target="tpu_custom_call" | custom-call | flops 536870912 | bytes 11141120 | tf_op jit(solution)/shard_map/project/pallas_call | solution.py:61
  36.6 0.7 %project.6.refs_5_ = f32[256,1024]{1,0:T(8,128)S(1)} custom-call(bf16[256,512]{1,0:T(8,128)(2,1)S(1)} %collective-permute-done.7.source.refs_0_, bf16[256,512]{1,0:T(8,128)(2,1)S(1)} %collective-permute-done.4.source.refs_1_, bf16[4160,512]{1,0:T(8,128)(2,1)S(1)} %pack.1.refs_2_.refs_3_.refs_0_, ...), custom_call_target="tpu_custom_call" | custom-call | flops 536870912 | bytes 11141120 | tf_op jit(solution)/shard_map/project/pallas_call | solution.py:61
  37.4 1.8 %collective-permute-done.10.refs_2_ = bf16[256,256]{1,0:T(8,128)(2,1)S(1)} collective-permute-done((bf16[256,256]{1,0:T(8,128)(2,1)S(1)}, bf16[256,256]{1,0:T(8,128)(2,1)S(1)}, u32[]{:S(2)}, u32[]{:S(2)}) %collective-permute-start.10) | collective-permute-done | bytes 131104 | tf_op jit(solution)/shard_map/ppermute | solution.py:353
  39.2 0.6 %project.7.acc_ref = f32[256,1024]{1,0:T(8,128)S(1)} custom-call(bf16[256,256]{1,0:T(8,128)(2,1)S(1)} %collective-permute-done.8.refs_0_, bf16[256,256]{1,0:T(8,128)(2,1)S(1)} %collective-permute-done.9.refs_1_, bf16[256,256]{1,0:T(8,128)(2,1)S(1)} %collective-permute-done.10.refs_2_, bf16[4160,512]{1,0:T(8,128)(2,1)S(1)} %pack.1.refs_2_.refs_3_.refs_0_, ...), custom_call_target="tpu_custom_call" | custom-call | flops 402653184 | bytes 11010048 | tf_op jit(solution)/shard_map/project/pallas_call | solution.py:61
  39.8 1.4 %collective-permute-done.5.e_ref = bf16[256,256]{1,0:T(8,128)(2,1)S(1)} collective-permute-done((bf16[256,256]{1,0:T(8,128)(2,1)S(1)}, bf16[256,256]{1,0:T(8,128)(2,1)S(1)}, u32[]{:S(2)}, u32[]{:S(2)}) %collective-permute-start.5) | collective-permute-done | bytes 131104 | tf_op jit(solution)/shard_map/ppermute | solution.py:353
  41.2 0.7 %cross_attend.1 = (f32[64,640]{1,0:T(8,128)S(1)}, f32[64,640]{1,0:T(8,128)S(1)}) custom-call(bf16[256,256]{1,0:T(8,128)(2,1)S(1)} %collective-permute-done.5.e_ref, f32[256,1024]{1,0:T(8,128)S(1)} %project.7.acc_ref, bf16[256,1024]{1,0:T(8,128)(2,1)S(1)} %get-tuple-element.34.map_ref, bf16[128,512]{1,0:T(8,128)(2,1)S(1)} %get-tuple-element.35.tgt_ref, ...), custom_call_target="tpu_custom_call" | custom-call | flops 134217728 | bytes 2293760 | tf_op jit(solution)/shard_map/cross_attend/pallas_call | solution.py:61
  42.0 1.4 %collective-permute-done.12.refs_1_ = f32[64,640]{1,0:T(8,128)S(1)} collective-permute-done((f32[64,640]{1,0:T(8,128)S(1)}, f32[64,640]{1,0:T(8,128)S(1)}, u32[]{:S(2)}, u32[]{:S(2)}) %collective-permute-start.12) | collective-permute-done | bytes 163872 | tf_op jit(solution)/shard_map/ppermute | solution.py:370
  43.4 0.8 %combine.1 = bf16[64,512]{1,0:T(8,128)(2,1)} custom-call(f32[64,640]{1,0:T(8,128)S(1)} %get-tuple-element.37.refs_0_, f32[64,640]{1,0:T(8,128)S(1)} %collective-permute-done.12.refs_1_), custom_call_target="tpu_custom_call" | custom-call | bytes 393216 | tf_op jit(solution)/shard_map/combine/pallas_call | solution.py:61
  (17 shorter events, 2.0 us)
Async XLA Ops:
  0.0 2.4 %collective-permute-start.1 = (bf16[256,1024]{1,0:T(8,128)(2,1)}, bf16[256,1024]{1,0:T(8,128)(2,1)S(1)}, u32[]{:S(2)}, u32[]{:S(2)}) collective-permute-start(bf16[256,1024]{1,0:T(8,128)(2,1)} %refs_1_.2), channel_id=1, source_target_pairs={{0,4},{4,0},{1,5},{5,1},{2,6},{6,2},{3,7},{7,3},{8,12},{12,8},{9,1... | collective-permute-start | bytes 1572872 | tf_op jit(solution)/shard_map/ppermute | solution.py:309
  0.5 1.9 %collective-permute-start = (s32[1,256]{1,0:T(1,128)}, s32[1,256]{1,0:T(1,128)S(1)}, u32[]{:S(2)}, u32[]{:S(2)}) collective-permute-start(s32[1,256]{1,0:T(1,128)} %bitcast.1), channel_id=1, source_target_pairs={{0,4},{4,0},{1,5},{5,1},{2,6},{6,2},{3,7},{7,3},{8,12},{12,8},{9,1... | collective-permute-start | bytes 3080 | tf_op jit(solution)/shard_map/ppermute | solution.py:309
  0.5 2.4 %collective-permute-start.2 = (bf16[256,1024]{1,0:T(8,128)(2,1)}, bf16[256,1024]{1,0:T(8,128)(2,1)S(1)}, u32[]{:S(2)}, u32[]{:S(2)}) collective-permute-start(bf16[256,1024]{1,0:T(8,128)(2,1)} %refs_2_.2), channel_id=1, source_target_pairs={{0,4},{4,0},{1,5},{5,1},{2,6},{6,2},{3,7},{7,3},{8,12},{12,8},{9,1... | collective-permute-start | bytes 1572872 | tf_op jit(solution)/shard_map/ppermute | solution.py:309
  3.3 10.7 %collective-permute-start.6 = (bf16[256,512]{1,0:T(8,128)(2,1)S(1)}, bf16[256,512]{1,0:T(8,128)(2,1)S(1)}, u32[]{:S(2)}, u32[]{:S(2)}) collective-permute-start(bf16[256,512]{1,0:T(8,128)(2,1)S(1)} %mix.3.refs_0_), channel_id=1, source_target_pairs={{0,2},{2,3},{3,1},{1,0},{4,6},{6,7},{7,5},{5,4},{8,10},{10,11},{11... | collective-permute-start | bytes 786440 | tf_op jit(solution)/shard_map/ppermute | solution.py:353
  8.2 11.5 %collective-permute-start.3 = (bf16[256,512]{1,0:T(8,128)(2,1)S(1)}, bf16[256,512]{1,0:T(8,128)(2,1)S(1)}, u32[]{:S(2)}, u32[]{:S(2)}) collective-permute-start(bf16[256,512]{1,0:T(8,128)(2,1)S(1)} %mix.2.refs_1_), channel_id=1, source_target_pairs={{0,2},{2,3},{3,1},{1,0},{4,6},{6,7},{7,5},{5,4},{8,10},{10,11},{11... | collective-permute-start | bytes 786440 | tf_op jit(solution)/shard_map/ppermute | solution.py:353
  14.0 11.2 %collective-permute-start.7 = (bf16[256,512]{1,0:T(8,128)(2,1)S(1)}, bf16[256,512]{1,0:T(8,128)(2,1)S(1)}, u32[]{:S(2)}, u32[]{:S(2)}) collective-permute-start(bf16[256,512]{1,0:T(8,128)(2,1)S(1)} %collective-permute-done.6.refs_0_), channel_id=1, source_target_pairs={{0,2},{2,3},{3,1},{1,0},{4,6},{6,7},{7,5},{5,4},{8,10},{10,11},{11... | collective-permute-start | bytes 786440 | tf_op jit(solution)/shard_map/ppermute | solution.py:353
  19.6 15.4 %collective-permute-start.11 = (bf16[4160,512]{1,0:T(8,128)(2,1)S(1)}, bf16[4160,512]{1,0:T(8,128)(2,1)S(1)}, u32[]{:S(2)}, u32[]{:S(2)}) collective-permute-start(bf16[4160,512]{1,0:T(8,128)(2,1)S(1)} %pack.1.refs_2_.refs_3_.refs_0_), channel_id=1, source_target_pairs={{0,4},{4,0},{1,5},{5,1},{2,6},{6,2},{3,7},{7,3},{8,12},{12,8},{9,1... | collective-permute-start | bytes 12779528 | tf_op jit(solution)/shard_map/ppermute | solution.py:309
  19.7 11.1 %collective-permute-start.4 = (bf16[256,512]{1,0:T(8,128)(2,1)S(1)}, bf16[256,512]{1,0:T(8,128)(2,1)S(1)}, u32[]{:S(2)}, u32[]{:S(2)}) collective-permute-start(bf16[256,512]{1,0:T(8,128)(2,1)S(1)} %collective-permute-done.3.refs_1_), channel_id=1, source_target_pairs={{0,2},{2,3},{3,1},{1,0},{4,6},{6,7},{7,5},{5,4},{8,10},{10,11},{11... | collective-permute-start | bytes 786440 | tf_op jit(solution)/shard_map/ppermute | solution.py:353
  25.2 12.2 %collective-permute-start.8 = (bf16[256,256]{1,0:T(8,128)(2,1)S(1)}, bf16[256,256]{1,0:T(8,128)(2,1)S(1)}, u32[]{:S(2)}, u32[]{:S(2)}) collective-permute-start(bf16[256,256]{1,0:T(8,128)(2,1)S(1)} %get-tuple-element.31), channel_id=1, source_target_pairs={{0,2},{2,3},{3,1},{1,0},{4,6},{6,7},{7,5},{5,4},{8,10},{10,11},{11... | collective-permute-start | bytes 393224 | tf_op jit(solution)/shard_map/ppermute | solution.py:353
  28.6 8.8 %collective-permute-start.9 = (bf16[256,256]{1,0:T(8,128)(2,1)S(1)}, bf16[256,256]{1,0:T(8,128)(2,1)S(1)}, u32[]{:S(2)}, u32[]{:S(2)}) collective-permute-start(bf16[256,256]{1,0:T(8,128)(2,1)S(1)} %get-tuple-element.32), channel_id=1, source_target_pairs={{0,2},{2,3},{3,1},{1,0},{4,6},{6,7},{7,5},{5,4},{8,10},{10,11},{11... | collective-permute-start | bytes 393224 | tf_op jit(solution)/shard_map/ppermute | solution.py:353
  30.8 8.4 %collective-permute-start.10 = (bf16[256,256]{1,0:T(8,128)(2,1)S(1)}, bf16[256,256]{1,0:T(8,128)(2,1)S(1)}, u32[]{:S(2)}, u32[]{:S(2)}) collective-permute-start(bf16[256,256]{1,0:T(8,128)(2,1)S(1)} %get-tuple-element.33), channel_id=1, source_target_pairs={{0,2},{2,3},{3,1},{1,0},{4,6},{6,7},{7,5},{5,4},{8,10},{10,11},{11... | collective-permute-start | bytes 393224 | tf_op jit(solution)/shard_map/ppermute | solution.py:353
  34.3 7.0 %collective-permute-start.5 = (bf16[256,256]{1,0:T(8,128)(2,1)S(1)}, bf16[256,256]{1,0:T(8,128)(2,1)S(1)}, u32[]{:S(2)}, u32[]{:S(2)}) collective-permute-start(bf16[256,256]{1,0:T(8,128)(2,1)S(1)} %get-tuple-element.28), channel_id=1, source_target_pairs={{0,2},{2,3},{3,1},{1,0},{4,6},{6,7},{7,5},{5,4},{8,10},{10,11},{11... | collective-permute-start | bytes 393224 | tf_op jit(solution)/shard_map/ppermute | solution.py:353
  41.9 1.5 %collective-permute-start.12 = (f32[64,640]{1,0:T(8,128)S(1)}, f32[64,640]{1,0:T(8,128)S(1)}, u32[]{:S(2)}, u32[]{:S(2)}) collective-permute-start(f32[64,640]{1,0:T(8,128)S(1)} %get-tuple-element.38), channel_id=1, source_target_pairs={{4,0},{0,4},{5,1},{1,5},{6,2},{2,6},{7,3},{3,7},{12,8},{8,12},{13,... | collective-permute-start | bytes 491528 | tf_op jit(solution)/shard_map/ppermute | solution.py:370

commit v15 on v12

--- a/solution.py
+++ b/solution.py
@@ -14,6 +14,7 @@
 LANES = 128
 SCALE = HEAD_DIM**-0.5
 WEIGH_FLOPS = 6 * 10**9
+SPLIT_FLOPS = 15 * 10**9
 VMEM = pl.BlockSpec(memory_space=pltpu.VMEM)
 HBM = pl.BlockSpec(memory_space=pltpu.HBM)
 
@@ -175,15 +176,15 @@
             pl.when(shard == i)(functools.partial(act, maps))
 
 
-def halve_kernel(source, *outs):
+def split_kernel(source, *outs):
     width = outs[0].shape[1]
     for i, out in enumerate(outs):
         out[...] = source[:, i * width : (i + 1) * width]
 
 
-def halve(chunk):
+def split(chunk, parts):
     rows, width = chunk.shape
-    return call(halve_kernel, "halve", [((rows, width // 2), chunk.dtype)] * 2, [chunk], flops=3 * 10**10)
+    return call(split_kernel, "split", [((rows, width // parts), chunk.dtype)] * parts, [chunk], flops=SPLIT_FLOPS)
 
 
 def project_kernel(chunks, shards, map_rows, has_acc, place, *refs):
@@ -311,6 +312,14 @@
     marks = (doc_ids if n_ctx == 2 else doc_ids + 1).reshape(1, rows)
     keys, near_marks, values = bring(enc_key), bring(marks), bring(enc_value)
     query, own_key, own_value, marks = fetch(enc_query, enc_key, enc_value, marks)
+    chunks = 2
+    heads = features // HEAD_DIM // chunks
+    held = [None] * chunks
+    for j in range(chunks):
+        weights, totals = weigh(query, [own_key, *keys], [marks, *near_marks], j * heads, heads)
+        held[j] = mix(weights, totals, [own_value, *values], j * heads, heads)
+
+    key_map, value_map, tgt_query, held[1] = lax.optimization_barrier((key_map, value_map, tgt_query, held[1]))
     near_targets = []
     if n_ctx == 2:
         own_maps = pack(key_map, value_map, tgt_query)
@@ -319,13 +328,6 @@
         whole = [lax.all_gather(x, "ctx", axis=0, tiled=True) for x in (key_map, value_map)]
         shards, near_targets = [pack(*whole, tgt_query)], bring(tgt_query)
     map_rows = (shards[0].shape[0] - tgt_rows) // 2
-
-    chunks = 2
-    heads = features // HEAD_DIM // chunks
-    held = [None] * chunks
-    for j in reversed(range(chunks)):
-        weights, totals = weigh(query, [own_key, *keys], [marks, *near_marks], j * heads, heads)
-        held[j] = mix(weights, totals, [own_value, *values], j * heads, heads)
 
     order = ring_order(n_head)
     ring = [(order[i], order[(i + 1) % n_head]) for i in range(n_head)]
@@ -346,10 +348,7 @@
 
     acc, last = None, n_head - 1
     for turn in range(last):
-        if turn == last - 1:
-            pieces = [p for h in held for p in halve(h)]
-        else:
-            pieces = held
+        pieces = [p for h in held for p in split(h, 2 if turn == 1 else 1)] if turn else held
         later = [lax.ppermute(p, "head", ring) for p in pieces]
         acc = project(acc, held, functools.partial(place, turn, 0), shards, map_rows)
         held = later

time: 44.9 us -> 44.3 us (0.987)
  waiting for transfers between devices: 12.5 us -> 8.63 us
  starting transfers between devices: 22.2 us -> 25.4 us
    ppermute x8 -> x10, waiting for transfers between devices: 11.1 us -> 7.24 us  [on_device(): later = [lax.ppermute(p, 'head', ring) for p in pieces]]
    ppermute x8 -> x10, starting transfers between devices: 21.1 us -> 24.3 us  [on_device(): later = [lax.ppermute(p, 'head', ring) for p in pieces]]
    pallas_call x15 -> x19, Pallas kernels: 9.92 us -> 9.95 us  [call(): pl.pallas_call(kernel, in_specs=specs or [VMEM] * len(operands), out_spec...]
  transfers between devices with their start and end apart: 13 -> 15, of which waited for: 6 -> 5; matrix products, arithmetic and copies ran while one was open for 0% -> 0% of each run, Pallas kernels for 18% -> 18%
where the time goes in v15:
time: 44.3 us; the launch traced here: 44.2 us
  starting transfers between devices  25.4 us (57%)
  Pallas kernels  9.95 us (22%)
  waiting for transfers between devices  8.63 us (19%)
    ppermute x10, starting transfers between devices, on_device(): later = [lax.ppermute(p, 'head', ring) for p in pieces]  24.3 us
    pallas_call x19, Pallas kernels, call(): pl.pallas_call(kernel, in_specs=specs or [VMEM] * len(operands), out_spec...  9.95 us
    ppermute x10, waiting for transfers between devices, on_device(): later = [lax.ppermute(p, 'head', ring) for p in pieces]  7.24 us
    ppermute x1, waiting for transfers between devices, on_device(): lax.ppermute(piece, 'ctx', [(target, source) for source, target in pairs])  1.38 us
    ppermute x4, starting transfers between devices, on_device(): bring = lambda x: [lax.ppermute(x, 'ctx', pairs) for pairs in links]  1.03 us
  transfers between devices with their start and end apart: 15, of which 5 were waited for; matrix products, arithmetic and copies ran while one was open for 0% of the time, Pallas kernels for 18%

profile of v15, /device:TPU:0, one launch (start us, length us, event | category | flops | bytes accessed | tf_op | source)
XLA Modules:
  0.0 44.2 jit_solution(11414152161510044587)
XLA Ops:
  1.0 1.4 %fetch.1 = (bf16[256,1024]{1,0:T(8,128)(2,1)S(1)}, bf16[256,1024]{1,0:T(8,128)(2,1)S(1)}, bf16[256,1024]{1,0:T(8,128)(2,1)S(1)}, s32[1,256]{1,0:T(1,128)S(1)}) custom-call(bf16[256,1024]{1,0:T(8,128)(2,1)} %refs_0_.1, bf16[256,1024]{1,0:T(8,128)(2,1)} %refs_1_.1, bf16[256,1024]{1,0:T(8,128)(2,1)} %refs_2_.1, s32[1,256]{1,0:T(1,128)} %bitcast.2), custom_call_target="tpu_custom_call" | custom-call | bytes 3147776 | tf_op jit(solution)/shard_map/fetch/pallas_call | solution.py:62
  2.4 0.6 %weigh.2 = (bf16[256,1024]{1,0:T(8,128)(2,1)S(1)}, f32[256,128]{1,0:T(8,128)S(1)}) custom-call(s32[1,256]{1,0:T(1,128)S(1)} %get-tuple-element.26.refs_0_.refs_2_, s32[1,256]{1,0:T(1,128)S(1)} %collective-permute-done.refs_1_.refs_3_, bf16[256,1024]{1,0:T(8,128)(2,1)S(1)} %get-tuple-element.27.refs_2_, bf16[256,1024]{1,0:T(8,128)(2,1)S(1)} %get-tuple-element.28.refs_3_, ...), custom_call_target="tpu_custom_call" | custom-call | flops 6000000000 | bytes 2230272 | tf_op jit(solution)/shard_map/weigh/pallas_call | solution.py:62
  3.3 4.0 %collective-permute-start.3 = (bf16[256,512]{1,0:T(8,128)(2,1)S(1)}, bf16[256,512]{1,0:T(8,128)(2,1)S(1)}, u32[]{:S(2)}, u32[]{:S(2)}) collective-permute-start(bf16[256,512]{1,0:T(8,128)(2,1)S(1)} %mix.2.refs_0_), channel_id=1, source_target_pairs={{0,2},{2,3},{3,1},{1,0},{4,6},{6,7},{7,5},{5,4},{8,10},{10,11},{11... | collective-permute-start | bytes 786440 | tf_op jit(solution)/shard_map/ppermute | solution.py:352
  8.2 1.6 %collective-permute-start.8 = (bf16[256,512]{1,0:T(8,128)(2,1)S(1)}, bf16[256,512]{1,0:T(8,128)(2,1)S(1)}, u32[]{:S(2)}, u32[]{:S(2)}) collective-permute-start(bf16[256,512]{1,0:T(8,128)(2,1)S(1)} %mix.3.refs_1_), channel_id=1, source_target_pairs={{0,2},{2,3},{3,1},{1,0},{4,6},{6,7},{7,5},{5,4},{8,10},{10,11},{11... | collective-permute-start | bytes 786440 | tf_op jit(solution)/shard_map/ppermute | solution.py:352
  9.8 2.2 %pack.1.refs_2_.refs_4_.refs_3_.refs_0_ = bf16[4160,512]{1,0:T(8,128)(2,1)S(1)} custom-call(bf16[2048,512]{1,0:T(8,128)(2,1)} %refs_0_.2, bf16[2048,512]{1,0:T(8,128)(2,1)} %refs_1_.2, bf16[64,512]{1,0:T(8,128)(2,1)} %refs_2_.2), custom_call_target="tpu_custom_call" | custom-call | bytes 8519680 | tf_op jit(solution)/shard_map/pack/pallas_call | solution.py:62
  12.1 1.8 %collective-permute-done.3.source.refs_0_ = bf16[256,512]{1,0:T(8,128)(2,1)S(1)} collective-permute-done((bf16[256,512]{1,0:T(8,128)(2,1)S(1)}, bf16[256,512]{1,0:T(8,128)(2,1)S(1)}, u32[]{:S(2)}, u32[]{:S(2)}) %collective-permute-start.3) | collective-permute-done | bytes 262176 | tf_op jit(solution)/shard_map/ppermute | solution.py:352
  14.0 3.4 %collective-permute-start.4 = (bf16[256,256]{1,0:T(8,128)(2,1)S(1)}, bf16[256,256]{1,0:T(8,128)(2,1)S(1)}, u32[]{:S(2)}, u32[]{:S(2)}) collective-permute-start(bf16[256,256]{1,0:T(8,128)(2,1)S(1)} %get-tuple-element.32), channel_id=1, source_target_pairs={{0,2},{2,3},{3,1},{1,0},{4,6},{6,7},{7,5},{5,4},{8,10},{10,11},{11... | collective-permute-start | bytes 393224 | tf_op jit(solution)/shard_map/ppermute | solution.py:352
  17.4 0.7 %collective-permute-start.6 = (bf16[256,256]{1,0:T(8,128)(2,1)S(1)}, bf16[256,256]{1,0:T(8,128)(2,1)S(1)}, u32[]{:S(2)}, u32[]{:S(2)}) collective-permute-start(bf16[256,256]{1,0:T(8,128)(2,1)S(1)} %get-tuple-element.33), channel_id=1, source_target_pairs={{0,2},{2,3},{3,1},{1,0},{4,6},{6,7},{7,5},{5,4},{8,10},{10,11},{11... | collective-permute-start | bytes 393224 | tf_op jit(solution)/shard_map/ppermute | solution.py:352
  18.1 1.5 %collective-permute-done.8.source.refs_1_ = bf16[256,512]{1,0:T(8,128)(2,1)S(1)} collective-permute-done((bf16[256,512]{1,0:T(8,128)(2,1)S(1)}, bf16[256,512]{1,0:T(8,128)(2,1)S(1)}, u32[]{:S(2)}, u32[]{:S(2)}) %collective-permute-start.8) | collective-permute-done | bytes 262176 | tf_op jit(solution)/shard_map/ppermute | solution.py:352
  19.6 3.4 %collective-permute-start.9 = (bf16[256,256]{1,0:T(8,128)(2,1)S(1)}, bf16[256,256]{1,0:T(8,128)(2,1)S(1)}, u32[]{:S(2)}, u32[]{:S(2)}) collective-permute-start(bf16[256,256]{1,0:T(8,128)(2,1)S(1)} %get-tuple-element.37), channel_id=1, source_target_pairs={{0,2},{2,3},{3,1},{1,0},{4,6},{6,7},{7,5},{5,4},{8,10},{10,11},{11... | collective-permute-start | bytes 393224 | tf_op jit(solution)/shard_map/ppermute | solution.py:352
  23.0 0.7 %collective-permute-start.12 = (bf16[256,256]{1,0:T(8,128)(2,1)S(1)}, bf16[256,256]{1,0:T(8,128)(2,1)S(1)}, u32[]{:S(2)}, u32[]{:S(2)}) collective-permute-start(bf16[256,256]{1,0:T(8,128)(2,1)S(1)} %get-tuple-element.41), channel_id=1, source_target_pairs={{0,2},{2,3},{3,1},{1,0},{4,6},{6,7},{7,5},{5,4},{8,10},{10,11},{11... | collective-permute-start | bytes 393224 | tf_op jit(solution)/shard_map/ppermute | solution.py:352
  23.7 2.1 %collective-permute-start.5 = (bf16[256,256]{1,0:T(8,128)(2,1)S(1)}, bf16[256,256]{1,0:T(8,128)(2,1)S(1)}, u32[]{:S(2)}, u32[]{:S(2)}) collective-permute-start(bf16[256,256]{1,0:T(8,128)(2,1)S(1)} %split.7), channel_id=1, source_target_pairs={{0,2},{2,3},{3,1},{1,0},{4,6},{6,7},{7,5},{5,4},{8,10},{10,11},{11... | collective-permute-start | bytes 393224 | tf_op jit(solution)/shard_map/ppermute | solution.py:352
  25.8 2.8 %collective-permute-start.7 = (bf16[256,256]{1,0:T(8,128)(2,1)S(1)}, bf16[256,256]{1,0:T(8,128)(2,1)S(1)}, u32[]{:S(2)}, u32[]{:S(2)}) collective-permute-start(bf16[256,256]{1,0:T(8,128)(2,1)S(1)} %split.8), channel_id=1, source_target_pairs={{0,2},{2,3},{3,1},{1,0},{4,6},{6,7},{7,5},{5,4},{8,10},{10,11},{11... | collective-permute-start | bytes 393224 | tf_op jit(solution)/shard_map/ppermute | solution.py:352
  28.7 2.8 %collective-permute-start.10 = (bf16[256,256]{1,0:T(8,128)(2,1)S(1)}, bf16[256,256]{1,0:T(8,128)(2,1)S(1)}, u32[]{:S(2)}, u32[]{:S(2)}) collective-permute-start(bf16[256,256]{1,0:T(8,128)(2,1)S(1)} %split.10), channel_id=1, source_target_pairs={{0,2},{2,3},{3,1},{1,0},{4,6},{6,7},{7,5},{5,4},{8,10},{10,11},{11... | collective-permute-start | bytes 393224 | tf_op jit(solution)/shard_map/ppermute | solution.py:352
  31.5 2.8 %collective-permute-start.13 = (bf16[256,256]{1,0:T(8,128)(2,1)S(1)}, bf16[256,256]{1,0:T(8,128)(2,1)S(1)}, u32[]{:S(2)}, u32[]{:S(2)}) collective-permute-start(bf16[256,256]{1,0:T(8,128)(2,1)S(1)} %split.11), channel_id=1, source_target_pairs={{0,2},{2,3},{3,1},{1,0},{4,6},{6,7},{7,5},{5,4},{8,10},{10,11},{11... | collective-permute-start | bytes 393224 | tf_op jit(solution)/shard_map/ppermute | solution.py:352
  34.4 0.7 %project.4.refs_4_ = f32[256,1024]{1,0:T(8,128)S(1)} custom-call(bf16[256,512]{1,0:T(8,128)(2,1)S(1)} %mix.2.refs_0_, bf16[256,512]{1,0:T(8,128)(2,1)S(1)} %mix.3.refs_1_, bf16[4160,512]{1,0:T(8,128)(2,1)S(1)} %pack.1.refs_2_.refs_4_.refs_3_.refs_0_, bf16[4160,512]{1,0:T(8,128)(2,1)S(1)} %collective-permute-done.11.refs_3_.refs_5_.refs_4_.refs_1_), custom_call_target="tpu_custom_call" | custom-call | flops 536870912 | bytes 10092544 | tf_op jit(solution)/shard_map/project/pallas_call | solution.py:62
  35.2 0.7 %project.5.refs_6_ = f32[256,1024]{1,0:T(8,128)S(1)} custom-call(bf16[256,512]{1,0:T(8,128)(2,1)S(1)} %collective-permute-done.3.source.refs_0_, bf16[256,512]{1,0:T(8,128)(2,1)S(1)} %collective-permute-done.8.source.refs_1_, bf16[4160,512]{1,0:T(8,128)(2,1)S(1)} %pack.1.refs_2_.refs_4_.refs_3_.refs_0_, ...), custom_call_target="tpu_custom_call" | custom-call | flops 536870912 | bytes 11141120 | tf_op jit(solution)/shard_map/project/pallas_call | solution.py:62
  35.9 0.7 %project.6.refs_5_ = f32[256,1024]{1,0:T(8,128)S(1)} custom-call(bf16[256,256]{1,0:T(8,128)(2,1)S(1)} %collective-permute-done.4.source.refs_0_, bf16[256,256]{1,0:T(8,128)(2,1)S(1)} %collective-permute-done.6.source.refs_1_, bf16[256,256]{1,0:T(8,128)(2,1)S(1)} %collective-permute-done.9.source.refs_2_, ...), custom_call_target="tpu_custom_call" | custom-call | flops 536870912 | bytes 11141120 | tf_op jit(solution)/shard_map/project/pallas_call | solution.py:62
  36.7 2.5 %collective-permute-done.10.refs_2_ = bf16[256,256]{1,0:T(8,128)(2,1)S(1)} collective-permute-done((bf16[256,256]{1,0:T(8,128)(2,1)S(1)}, bf16[256,256]{1,0:T(8,128)(2,1)S(1)}, u32[]{:S(2)}, u32[]{:S(2)}) %collective-permute-start.10) | collective-permute-done | bytes 131104 | tf_op jit(solution)/shard_map/ppermute | solution.py:352
  39.2 0.6 %project.7.acc_ref = f32[256,1024]{1,0:T(8,128)S(1)} custom-call(bf16[256,256]{1,0:T(8,128)(2,1)S(1)} %collective-permute-done.5.refs_0_, bf16[256,256]{1,0:T(8,128)(2,1)S(1)} %collective-permute-done.7.refs_1_, bf16[256,256]{1,0:T(8,128)(2,1)S(1)} %collective-permute-done.10.refs_2_, bf16[4160,512]{1,0:T(8,128)(2,1)S(1)} %pack.1.refs_2_.refs_4_.refs_3_.refs_0_, ...), custom_call_target="tpu_custom_call" | custom-call | flops 402653184 | bytes 11010048 | tf_op jit(solution)/shard_map/project/pallas_call | solution.py:62
  39.8 1.4 %collective-permute-done.13.e_ref = bf16[256,256]{1,0:T(8,128)(2,1)S(1)} collective-permute-done((bf16[256,256]{1,0:T(8,128)(2,1)S(1)}, bf16[256,256]{1,0:T(8,128)(2,1)S(1)}, u32[]{:S(2)}, u32[]{:S(2)}) %collective-permute-start.13) | collective-permute-done | bytes 131104 | tf_op jit(solution)/shard_map/ppermute | solution.py:352
  41.2 0.7 %cross_attend.1 = (f32[64,640]{1,0:T(8,128)S(1)}, f32[64,640]{1,0:T(8,128)S(1)}) custom-call(f32[256,1024]{1,0:T(8,128)S(1)} %project.7.acc_ref, bf16[256,256]{1,0:T(8,128)(2,1)S(1)} %collective-permute-done.13.e_ref, bf16[256,1024]{1,0:T(8,128)(2,1)S(1)} %get-tuple-element.42.map_ref, bf16[128,512]{1,0:T(8,128)(2,1)S(1)} %get-tuple-element.43.tgt_ref, ...), custom_call_target="tpu_custom_call" | custom-call | flops 134217728 | bytes 2293760 | tf_op jit(solution)/shard_map/cross_attend/pallas_call | solution.py:62
  42.0 1.4 %collective-permute-done.14.refs_1_ = f32[64,640]{1,0:T(8,128)S(1)} collective-permute-done((f32[64,640]{1,0:T(8,128)S(1)}, f32[64,640]{1,0:T(8,128)S(1)}, u32[]{:S(2)}, u32[]{:S(2)}) %collective-permute-start.14) | collective-permute-done | bytes 163872 | tf_op jit(solution)/shard_map/ppermute | solution.py:369
  43.4 0.8 %combine.1 = bf16[64,512]{1,0:T(8,128)(2,1)} custom-call(f32[64,640]{1,0:T(8,128)S(1)} %get-tuple-element.45.refs_0_, f32[64,640]{1,0:T(8,128)S(1)} %collective-permute-done.14.refs_1_), custom_call_target="tpu_custom_call" | custom-call | bytes 393216 | tf_op jit(solution)/shard_map/combine/pallas_call | solution.py:62
  (25 shorter events, 2.6 us)
Async XLA Ops:
  0.0 2.4 %collective-permute-start.1 = (bf16[256,1024]{1,0:T(8,128)(2,1)}, bf16[256,1024]{1,0:T(8,128)(2,1)S(1)}, u32[]{:S(2)}, u32[]{:S(2)}) collective-permute-start(bf16[256,1024]{1,0:T(8,128)(2,1)} %refs_1_.1), channel_id=1, source_target_pairs={{0,4},{4,0},{1,5},{5,1},{2,6},{6,2},{3,7},{7,3},{8,12},{12,8},{9,1... | collective-permute-start | bytes 1572872 | tf_op jit(solution)/shard_map/ppermute | solution.py:310
  0.5 1.9 %collective-permute-start = (s32[1,256]{1,0:T(1,128)}, s32[1,256]{1,0:T(1,128)S(1)}, u32[]{:S(2)}, u32[]{:S(2)}) collective-permute-start(s32[1,256]{1,0:T(1,128)} %bitcast.1), channel_id=1, source_target_pairs={{0,4},{4,0},{1,5},{5,1},{2,6},{6,2},{3,7},{7,3},{8,12},{12,8},{9,1... | collective-permute-start | bytes 3080 | tf_op jit(solution)/shard_map/ppermute | solution.py:310
  0.5 2.4 %collective-permute-start.2 = (bf16[256,1024]{1,0:T(8,128)(2,1)}, bf16[256,1024]{1,0:T(8,128)(2,1)S(1)}, u32[]{:S(2)}, u32[]{:S(2)}) collective-permute-start(bf16[256,1024]{1,0:T(8,128)(2,1)} %refs_2_.1), channel_id=1, source_target_pairs={{0,4},{4,0},{1,5},{5,1},{2,6},{6,2},{3,7},{7,3},{8,12},{12,8},{9,1... | collective-permute-start | bytes 1572872 | tf_op jit(solution)/shard_map/ppermute | solution.py:310
  3.3 10.7 %collective-permute-start.3 = (bf16[256,512]{1,0:T(8,128)(2,1)S(1)}, bf16[256,512]{1,0:T(8,128)(2,1)S(1)}, u32[]{:S(2)}, u32[]{:S(2)}) collective-permute-start(bf16[256,512]{1,0:T(8,128)(2,1)S(1)} %mix.2.refs_0_), channel_id=1, source_target_pairs={{0,2},{2,3},{3,1},{1,0},{4,6},{6,7},{7,5},{5,4},{8,10},{10,11},{11... | collective-permute-start | bytes 786440 | tf_op jit(solution)/shard_map/ppermute | solution.py:352
  8.2 11.4 %collective-permute-start.8 = (bf16[256,512]{1,0:T(8,128)(2,1)S(1)}, bf16[256,512]{1,0:T(8,128)(2,1)S(1)}, u32[]{:S(2)}, u32[]{:S(2)}) collective-permute-start(bf16[256,512]{1,0:T(8,128)(2,1)S(1)} %mix.3.refs_1_), channel_id=1, source_target_pairs={{0,2},{2,3},{3,1},{1,0},{4,6},{6,7},{7,5},{5,4},{8,10},{10,11},{11... | collective-permute-start | bytes 786440 | tf_op jit(solution)/shard_map/ppermute | solution.py:352
  12.0 22.2 %collective-permute-start.11 = (bf16[4160,512]{1,0:T(8,128)(2,1)S(1)}, bf16[4160,512]{1,0:T(8,128)(2,1)S(1)}, u32[]{:S(2)}, u32[]{:S(2)}) collective-permute-start(bf16[4160,512]{1,0:T(8,128)(2,1)S(1)} %pack.1.refs_2_.refs_4_.refs_3_.refs_0_), channel_id=1, source_target_pairs={{0,4},{4,0},{1,5},{5,1},{2,6},{6,2},{3,7},{7,3},{8,12},{12,8},{9,1... | collective-permute-start | bytes 12779528 | tf_op jit(solution)/shard_map/ppermute | solution.py:310
  14.0 9.7 %collective-permute-start.4 = (bf16[256,256]{1,0:T(8,128)(2,1)S(1)}, bf16[256,256]{1,0:T(8,128)(2,1)S(1)}, u32[]{:S(2)}, u32[]{:S(2)}) collective-permute-start(bf16[256,256]{1,0:T(8,128)(2,1)S(1)} %get-tuple-element.32), channel_id=1, source_target_pairs={{0,2},{2,3},{3,1},{1,0},{4,6},{6,7},{7,5},{5,4},{8,10},{10,11},{11... | collective-permute-start | bytes 393224 | tf_op jit(solution)/shard_map/ppermute | solution.py:352
  17.4 8.4 %collective-permute-start.6 = (bf16[256,256]{1,0:T(8,128)(2,1)S(1)}, bf16[256,256]{1,0:T(8,128)(2,1)S(1)}, u32[]{:S(2)}, u32[]{:S(2)}) collective-permute-start(bf16[256,256]{1,0:T(8,128)(2,1)S(1)} %get-tuple-element.33), channel_id=1, source_target_pairs={{0,2},{2,3},{3,1},{1,0},{4,6},{6,7},{7,5},{5,4},{8,10},{10,11},{11... | collective-permute-start | bytes 393224 | tf_op jit(solution)/shard_map/ppermute | solution.py:352
  19.6 9.0 %collective-permute-start.9 = (bf16[256,256]{1,0:T(8,128)(2,1)S(1)}, bf16[256,256]{1,0:T(8,128)(2,1)S(1)}, u32[]{:S(2)}, u32[]{:S(2)}) collective-permute-start(bf16[256,256]{1,0:T(8,128)(2,1)S(1)} %get-tuple-element.37), channel_id=1, source_target_pairs={{0,2},{2,3},{3,1},{1,0},{4,6},{6,7},{7,5},{5,4},{8,10},{10,11},{11... | collective-permute-start | bytes 393224 | tf_op jit(solution)/shard_map/ppermute | solution.py:352
  23.0 8.4 %collective-permute-start.12 = (bf16[256,256]{1,0:T(8,128)(2,1)S(1)}, bf16[256,256]{1,0:T(8,128)(2,1)S(1)}, u32[]{:S(2)}, u32[]{:S(2)}) collective-permute-start(bf16[256,256]{1,0:T(8,128)(2,1)S(1)} %get-tuple-element.41), channel_id=1, source_target_pairs={{0,2},{2,3},{3,1},{1,0},{4,6},{6,7},{7,5},{5,4},{8,10},{10,11},{11... | collective-permute-start | bytes 393224 | tf_op jit(solution)/shard_map/ppermute | solution.py:352
  23.7 13.0 %collective-permute-start.5 = (bf16[256,256]{1,0:T(8,128)(2,1)S(1)}, bf16[256,256]{1,0:T(8,128)(2,1)S(1)}, u32[]{:S(2)}, u32[]{:S(2)}) collective-permute-start(bf16[256,256]{1,0:T(8,128)(2,1)S(1)} %split.7), channel_id=1, source_target_pairs={{0,2},{2,3},{3,1},{1,0},{4,6},{6,7},{7,5},{5,4},{8,10},{10,11},{11... | collective-permute-start | bytes 393224 | tf_op jit(solution)/shard_map/ppermute | solution.py:352
  25.8 10.9 %collective-permute-start.7 = (bf16[256,256]{1,0:T(8,128)(2,1)S(1)}, bf16[256,256]{1,0:T(8,128)(2,1)S(1)}, u32[]{:S(2)}, u32[]{:S(2)}) collective-permute-start(bf16[256,256]{1,0:T(8,128)(2,1)S(1)} %split.8), channel_id=1, source_target_pairs={{0,2},{2,3},{3,1},{1,0},{4,6},{6,7},{7,5},{5,4},{8,10},{10,11},{11... | collective-permute-start | bytes 393224 | tf_op jit(solution)/shard_map/ppermute | solution.py:352
  28.7 10.6 %collective-permute-start.10 = (bf16[256,256]{1,0:T(8,128)(2,1)S(1)}, bf16[256,256]{1,0:T(8,128)(2,1)S(1)}, u32[]{:S(2)}, u32[]{:S(2)}) collective-permute-start(bf16[256,256]{1,0:T(8,128)(2,1)S(1)} %split.10), channel_id=1, source_target_pairs={{0,2},{2,3},{3,1},{1,0},{4,6},{6,7},{7,5},{5,4},{8,10},{10,11},{11... | collective-permute-start | bytes 393224 | tf_op jit(solution)/shard_map/ppermute | solution.py:352
  31.5 9.8 %collective-permute-start.13 = (bf16[256,256]{1,0:T(8,128)(2,1)S(1)}, bf16[256,256]{1,0:T(8,128)(2,1)S(1)}, u32[]{:S(2)}, u32[]{:S(2)}) collective-permute-start(bf16[256,256]{1,0:T(8,128)(2,1)S(1)} %split.11), channel_id=1, source_target_pairs={{0,2},{2,3},{3,1},{1,0},{4,6},{6,7},{7,5},{5,4},{8,10},{10,11},{11... | collective-permute-start | bytes 393224 | tf_op jit(solution)/shard_map/ppermute | solution.py:352
  41.9 1.5 %collective-permute-start.14 = (f32[64,640]{1,0:T(8,128)S(1)}, f32[64,640]{1,0:T(8,128)S(1)}, u32[]{:S(2)}, u32[]{:S(2)}) collective-permute-start(f32[64,640]{1,0:T(8,128)S(1)} %get-tuple-element.46), channel_id=1, source_target_pairs={{4,0},{0,4},{5,1},{1,5},{6,2},{2,6},{7,3},{3,7},{12,8},{8,12},{13,... | collective-permute-start | bytes 491528 | tf_op jit(solution)/shard_map/ppermute | solution.py:369

commit v16 on v15

--- a/solution.py
+++ b/solution.py
@@ -124,12 +124,15 @@
     span = same.shape[1]
     lane = lax.broadcasted_iota(jnp.int32, total_ref.shape, 1)
     totals = jnp.zeros(total_ref.shape, F32)
+    results = []
     for h in range(heads):
         at = head_columns(first + h)
         scores = jnp.concatenate([dot_t(q_ref[:, at], k[:, at]) for k in keys], axis=1)
         _, weights, total = softmax_block(scores, same)
-        weight_ref[:, h * span : (h + 1) * span] = weights.astype(BF16)
+        results.append(weights.astype(BF16))
         totals = jnp.where(lane == h, total, totals)
+    for h in range(heads):
+        weight_ref[:, h * span : (h + 1) * span] = results[h]
     total_ref[...] = totals
 
 
@@ -148,13 +151,16 @@
 def mix_kernel(first, heads, weight_ref, total_ref, *refs):
     values, out_ref = refs[:-1], refs[-1]
     rows = total_ref.shape[0]
+    results = []
     for h in range(heads):
         start = h * rows * len(values)
         summed = sum(
             dot(weight_ref[:, start + i * rows : start + (i + 1) * rows], v[:, head_columns(first + h)])
             for i, v in enumerate(values)
         )
-        out_ref[:, head_columns(h)] = (summed / total_ref[:, h : h + 1]).astype(BF16)
+        results.append((summed / total_ref[:, h : h + 1]).astype(BF16))
+    for h in range(heads):
+        out_ref[:, head_columns(h)] = results[h]
 
 
 def mix(weights, totals, values, first, heads):
@@ -256,6 +262,7 @@
 def cross_kernel(acc_ref, e_ref, map_ref, tgt_ref, mask_ref, *outs):
     heads = map_ref.shape[1] // 2 // HEAD_DIM
     chunk = e_ref[...]
+    queries = [tgt_ref[:, head_columns(h)] for h in range(heads)]
     memory = []
     for h in range(2 * heads):
         at = head_columns(h)
@@ -263,17 +270,18 @@
     keys, values = memory[:heads], memory[heads:]
     count = outs[0].shape[0]
     same = mask_ref[...] > 0
+    scores = [dot_t(queries[h], keys[h]) for h in range(heads)]
+    tops, weights, totals = zip(*[softmax_block(x, same) for x in scores])
+    summed = [dot(w.astype(BF16), v) for w, v in zip(weights, values)]
     lane = lax.broadcasted_iota(jnp.int32, (same.shape[0], LANES), 1)
     stats = jnp.zeros(lane.shape, F32)
     for h in range(heads):
-        at = head_columns(h)
-        top, weights, total = softmax_block(dot_t(tgt_ref[:, at], keys[h]), same)
-        summed = dot(weights.astype(BF16), values[h])
-        for i, out_ref in enumerate(outs):
-            out_ref[:, at] = summed[i * count : (i + 1) * count]
-        stats = jnp.where(lane == h, top, jnp.where(lane == heads + h, total, stats))
+        stats = jnp.where(lane == h, tops[h], jnp.where(lane == heads + h, totals[h], stats))
     for i, out_ref in enumerate(outs):
-        out_ref[:, heads * HEAD_DIM :] = stats[i * count : (i + 1) * count]
+        part = slice(i * count, (i + 1) * count)
+        for h in range(heads):
+            out_ref[:, head_columns(h)] = summed[h][part]
+        out_ref[:, heads * HEAD_DIM :] = stats[part]
 
 
 def cross_attend(acc, chunk, maps, targets, mask, parts):
@@ -289,17 +297,19 @@
 
 
 def combine_kernel(*refs):
-    parts, out_ref = refs[:-1], refs[-1]
+    parts, out_ref = [r[...] for r in refs[:-1]], refs[-1]
     width = out_ref.shape[1]
     heads = width // HEAD_DIM
-    for h in range(heads):
-        at = head_columns(h)
-        tops = [r[:, width + h : width + h + 1] for r in parts]
+    results = []
+    for h in range(heads):
+        tops = [x[:, width + h : width + h + 1] for x in parts]
+        totals = [x[:, width + heads + h : width + heads + h + 1] for x in parts]
         top = functools.reduce(jnp.maximum, tops)
         factors = [jnp.exp(t - top) for t in tops]
-        total = sum(f * r[:, width + heads + h : width + heads + h + 1] for f, r in zip(factors, parts))
-        summed = sum(f * r[:, at] for f, r in zip(factors, parts))
-        out_ref[:, at] = (summed / total).astype(BF16)
+        share = 1.0 / sum(f * t for f, t in zip(factors, totals))
+        results.append(sum((f * share) * x[:, head_columns(h)] for f, x in zip(factors, parts)))
+    for h in range(heads):
+        out_ref[:, head_columns(h)] = results[h].astype(BF16)
 
 
 def on_device(enc_query, enc_key, enc_value, doc_ids, key_map, value_map, tgt_query):

time: 44.3 us -> 44.3 us (level)
  no operation moved by 1% of the time
where the time goes in v16:
time: 44.3 us; the launch traced here: 44.1 us
  starting transfers between devices  25.4 us (57%)
  Pallas kernels  9.88 us (22%)
  waiting for transfers between devices  8.63 us (19%)
    ppermute x10, starting transfers between devices, on_device(): later = [lax.ppermute(p, 'head', ring) for p in pieces]  24.3 us
    pallas_call x19, Pallas kernels, call(): pl.pallas_call(kernel, in_specs=specs or [VMEM] * len(operands), out_spec...  9.88 us
    ppermute x10, waiting for transfers between devices, on_device(): later = [lax.ppermute(p, 'head', ring) for p in pieces]  7.24 us
    ppermute x1, waiting for transfers between devices, on_device(): lax.ppermute(piece, 'ctx', [(target, source) for source, target in pairs])  1.38 us
    ppermute x4, starting transfers between devices, on_device(): bring = lambda x: [lax.ppermute(x, 'ctx', pairs) for pairs in links]  1.03 us
  transfers between devices with their start and end apart: 15, of which 5 were waited for; matrix products, arithmetic and copies ran while one was open for 0% of the time, Pallas kernels for 18%

profile of v16, /device:TPU:0, one launch (start us, length us, event | category | flops | bytes accessed | tf_op | source)
XLA Modules:
  0.0 44.1 jit_solution(4559689469138609010)
XLA Ops:
  1.0 1.4 %fetch.1 = (bf16[256,1024]{1,0:T(8,128)(2,1)S(1)}, bf16[256,1024]{1,0:T(8,128)(2,1)S(1)}, bf16[256,1024]{1,0:T(8,128)(2,1)S(1)}, s32[1,256]{1,0:T(1,128)S(1)}) custom-call(bf16[256,1024]{1,0:T(8,128)(2,1)} %refs_0_.1, bf16[256,1024]{1,0:T(8,128)(2,1)} %refs_1_.1, bf16[256,1024]{1,0:T(8,128)(2,1)} %refs_2_.1, s32[1,256]{1,0:T(1,128)} %bitcast.2), custom_call_target="tpu_custom_call" | custom-call | bytes 3147776 | tf_op jit(solution)/shard_map/fetch/pallas_call | solution.py:62
  2.4 0.6 %weigh.2 = (bf16[256,1024]{1,0:T(8,128)(2,1)S(1)}, f32[256,128]{1,0:T(8,128)S(1)}) custom-call(s32[1,256]{1,0:T(1,128)S(1)} %get-tuple-element.26.refs_0_.refs_2_, s32[1,256]{1,0:T(1,128)S(1)} %collective-permute-done.refs_1_.refs_3_, bf16[256,1024]{1,0:T(8,128)(2,1)S(1)} %get-tuple-element.27.refs_2_, bf16[256,1024]{1,0:T(8,128)(2,1)S(1)} %get-tuple-element.28.refs_3_, ...), custom_call_target="tpu_custom_call" | custom-call | flops 6000000000 | bytes 2230272 | tf_op jit(solution)/shard_map/weigh/pallas_call | solution.py:62
  3.3 4.0 %collective-permute-start.3 = (bf16[256,512]{1,0:T(8,128)(2,1)S(1)}, bf16[256,512]{1,0:T(8,128)(2,1)S(1)}, u32[]{:S(2)}, u32[]{:S(2)}) collective-permute-start(bf16[256,512]{1,0:T(8,128)(2,1)S(1)} %mix.2.refs_0_), channel_id=1, source_target_pairs={{0,2},{2,3},{3,1},{1,0},{4,6},{6,7},{7,5},{5,4},{8,10},{10,11},{11... | collective-permute-start | bytes 786440 | tf_op jit(solution)/shard_map/ppermute | solution.py:362
  8.2 1.6 %collective-permute-start.8 = (bf16[256,512]{1,0:T(8,128)(2,1)S(1)}, bf16[256,512]{1,0:T(8,128)(2,1)S(1)}, u32[]{:S(2)}, u32[]{:S(2)}) collective-permute-start(bf16[256,512]{1,0:T(8,128)(2,1)S(1)} %mix.3.refs_1_), channel_id=1, source_target_pairs={{0,2},{2,3},{3,1},{1,0},{4,6},{6,7},{7,5},{5,4},{8,10},{10,11},{11... | collective-permute-start | bytes 786440 | tf_op jit(solution)/shard_map/ppermute | solution.py:362
  9.8 2.2 %pack.1.refs_2_.refs_4_.refs_3_.refs_0_ = bf16[4160,512]{1,0:T(8,128)(2,1)S(1)} custom-call(bf16[2048,512]{1,0:T(8,128)(2,1)} %refs_0_.2, bf16[2048,512]{1,0:T(8,128)(2,1)} %refs_1_.2, bf16[64,512]{1,0:T(8,128)(2,1)} %refs_2_.2), custom_call_target="tpu_custom_call" | custom-call | bytes 8519680 | tf_op jit(solution)/shard_map/pack/pallas_call | solution.py:62
  12.1 1.8 %collective-permute-done.3.source.refs_0_ = bf16[256,512]{1,0:T(8,128)(2,1)S(1)} collective-permute-done((bf16[256,512]{1,0:T(8,128)(2,1)S(1)}, bf16[256,512]{1,0:T(8,128)(2,1)S(1)}, u32[]{:S(2)}, u32[]{:S(2)}) %collective-permute-start.3) | collective-permute-done | bytes 262176 | tf_op jit(solution)/shard_map/ppermute | solution.py:362
  14.0 3.4 %collective-permute-start.4 = (bf16[256,256]{1,0:T(8,128)(2,1)S(1)}, bf16[256,256]{1,0:T(8,128)(2,1)S(1)}, u32[]{:S(2)}, u32[]{:S(2)}) collective-permute-start(bf16[256,256]{1,0:T(8,128)(2,1)S(1)} %get-tuple-element.32), channel_id=1, source_target_pairs={{0,2},{2,3},{3,1},{1,0},{4,6},{6,7},{7,5},{5,4},{8,10},{10,11},{11... | collective-permute-start | bytes 393224 | tf_op jit(solution)/shard_map/ppermute | solution.py:362
  17.4 0.7 %collective-permute-start.6 = (bf16[256,256]{1,0:T(8,128)(2,1)S(1)}, bf16[256,256]{1,0:T(8,128)(2,1)S(1)}, u32[]{:S(2)}, u32[]{:S(2)}) collective-permute-start(bf16[256,256]{1,0:T(8,128)(2,1)S(1)} %get-tuple-element.33), channel_id=1, source_target_pairs={{0,2},{2,3},{3,1},{1,0},{4,6},{6,7},{7,5},{5,4},{8,10},{10,11},{11... | collective-permute-start | bytes 393224 | tf_op jit(solution)/shard_map/ppermute | solution.py:362
  18.1 1.5 %collective-permute-done.8.source.refs_1_ = bf16[256,512]{1,0:T(8,128)(2,1)S(1)} collective-permute-done((bf16[256,512]{1,0:T(8,128)(2,1)S(1)}, bf16[256,512]{1,0:T(8,128)(2,1)S(1)}, u32[]{:S(2)}, u32[]{:S(2)}) %collective-permute-start.8) | collective-permute-done | bytes 262176 | tf_op jit(solution)/shard_map/ppermute | solution.py:362
  19.6 3.4 %collective-permute-start.9 = (bf16[256,256]{1,0:T(8,128)(2,1)S(1)}, bf16[256,256]{1,0:T(8,128)(2,1)S(1)}, u32[]{:S(2)}, u32[]{:S(2)}) collective-permute-start(bf16[256,256]{1,0:T(8,128)(2,1)S(1)} %get-tuple-element.37), channel_id=1, source_target_pairs={{0,2},{2,3},{3,1},{1,0},{4,6},{6,7},{7,5},{5,4},{8,10},{10,11},{11... | collective-permute-start | bytes 393224 | tf_op jit(solution)/shard_map/ppermute | solution.py:362
  23.0 0.7 %collective-permute-start.12 = (bf16[256,256]{1,0:T(8,128)(2,1)S(1)}, bf16[256,256]{1,0:T(8,128)(2,1)S(1)}, u32[]{:S(2)}, u32[]{:S(2)}) collective-permute-start(bf16[256,256]{1,0:T(8,128)(2,1)S(1)} %get-tuple-element.41), channel_id=1, source_target_pairs={{0,2},{2,3},{3,1},{1,0},{4,6},{6,7},{7,5},{5,4},{8,10},{10,11},{11... | collective-permute-start | bytes 393224 | tf_op jit(solution)/shard_map/ppermute | solution.py:362
  23.7 2.1 %collective-permute-start.5 = (bf16[256,256]{1,0:T(8,128)(2,1)S(1)}, bf16[256,256]{1,0:T(8,128)(2,1)S(1)}, u32[]{:S(2)}, u32[]{:S(2)}) collective-permute-start(bf16[256,256]{1,0:T(8,128)(2,1)S(1)} %split.7), channel_id=1, source_target_pairs={{0,2},{2,3},{3,1},{1,0},{4,6},{6,7},{7,5},{5,4},{8,10},{10,11},{11... | collective-permute-start | bytes 393224 | tf_op jit(solution)/shard_map/ppermute | solution.py:362
  25.8 2.8 %collective-permute-start.7 = (bf16[256,256]{1,0:T(8,128)(2,1)S(1)}, bf16[256,256]{1,0:T(8,128)(2,1)S(1)}, u32[]{:S(2)}, u32[]{:S(2)}) collective-permute-start(bf16[256,256]{1,0:T(8,128)(2,1)S(1)} %split.8), channel_id=1, source_target_pairs={{0,2},{2,3},{3,1},{1,0},{4,6},{6,7},{7,5},{5,4},{8,10},{10,11},{11... | collective-permute-start | bytes 393224 | tf_op jit(solution)/shard_map/ppermute | solution.py:362
  28.7 2.8 %collective-permute-start.10 = (bf16[256,256]{1,0:T(8,128)(2,1)S(1)}, bf16[256,256]{1,0:T(8,128)(2,1)S(1)}, u32[]{:S(2)}, u32[]{:S(2)}) collective-permute-start(bf16[256,256]{1,0:T(8,128)(2,1)S(1)} %split.10), channel_id=1, source_target_pairs={{0,2},{2,3},{3,1},{1,0},{4,6},{6,7},{7,5},{5,4},{8,10},{10,11},{11... | collective-permute-start | bytes 393224 | tf_op jit(solution)/shard_map/ppermute | solution.py:362
  31.5 2.8 %collective-permute-start.13 = (bf16[256,256]{1,0:T(8,128)(2,1)S(1)}, bf16[256,256]{1,0:T(8,128)(2,1)S(1)}, u32[]{:S(2)}, u32[]{:S(2)}) collective-permute-start(bf16[256,256]{1,0:T(8,128)(2,1)S(1)} %split.11), channel_id=1, source_target_pairs={{0,2},{2,3},{3,1},{1,0},{4,6},{6,7},{7,5},{5,4},{8,10},{10,11},{11... | collective-permute-start | bytes 393224 | tf_op jit(solution)/shard_map/ppermute | solution.py:362
  34.4 0.7 %project.4.refs_4_ = f32[256,1024]{1,0:T(8,128)S(1)} custom-call(bf16[256,512]{1,0:T(8,128)(2,1)S(1)} %mix.2.refs_0_, bf16[256,512]{1,0:T(8,128)(2,1)S(1)} %mix.3.refs_1_, bf16[4160,512]{1,0:T(8,128)(2,1)S(1)} %pack.1.refs_2_.refs_4_.refs_3_.refs_0_, bf16[4160,512]{1,0:T(8,128)(2,1)S(1)} %collective-permute-done.11.refs_3_.refs_5_.refs_4_.refs_1_), custom_call_target="tpu_custom_call" | custom-call | flops 536870912 | bytes 10092544 | tf_op jit(solution)/shard_map/project/pallas_call | solution.py:62
  35.2 0.7 %project.5.refs_6_ = f32[256,1024]{1,0:T(8,128)S(1)} custom-call(bf16[256,512]{1,0:T(8,128)(2,1)S(1)} %collective-permute-done.3.source.refs_0_, bf16[256,512]{1,0:T(8,128)(2,1)S(1)} %collective-permute-done.8.source.refs_1_, bf16[4160,512]{1,0:T(8,128)(2,1)S(1)} %pack.1.refs_2_.refs_4_.refs_3_.refs_0_, ...), custom_call_target="tpu_custom_call" | custom-call | flops 536870912 | bytes 11141120 | tf_op jit(solution)/shard_map/project/pallas_call | solution.py:62
  35.9 0.7 %project.6.refs_5_ = f32[256,1024]{1,0:T(8,128)S(1)} custom-call(bf16[256,256]{1,0:T(8,128)(2,1)S(1)} %collective-permute-done.4.source.refs_0_, bf16[256,256]{1,0:T(8,128)(2,1)S(1)} %collective-permute-done.6.source.refs_1_, bf16[256,256]{1,0:T(8,128)(2,1)S(1)} %collective-permute-done.9.source.refs_2_, ...), custom_call_target="tpu_custom_call" | custom-call | flops 536870912 | bytes 11141120 | tf_op jit(solution)/shard_map/project/pallas_call | solution.py:62
  36.7 2.5 %collective-permute-done.10.refs_2_ = bf16[256,256]{1,0:T(8,128)(2,1)S(1)} collective-permute-done((bf16[256,256]{1,0:T(8,128)(2,1)S(1)}, bf16[256,256]{1,0:T(8,128)(2,1)S(1)}, u32[]{:S(2)}, u32[]{:S(2)}) %collective-permute-start.10) | collective-permute-done | bytes 131104 | tf_op jit(solution)/shard_map/ppermute | solution.py:362
  39.2 0.6 %project.7.acc_ref = f32[256,1024]{1,0:T(8,128)S(1)} custom-call(bf16[256,256]{1,0:T(8,128)(2,1)S(1)} %collective-permute-done.5.refs_0_, bf16[256,256]{1,0:T(8,128)(2,1)S(1)} %collective-permute-done.7.refs_1_, bf16[256,256]{1,0:T(8,128)(2,1)S(1)} %collective-permute-done.10.refs_2_, bf16[4160,512]{1,0:T(8,128)(2,1)S(1)} %pack.1.refs_2_.refs_4_.refs_3_.refs_0_, ...), custom_call_target="tpu_custom_call" | custom-call | flops 402653184 | bytes 11010048 | tf_op jit(solution)/shard_map/project/pallas_call | solution.py:62
  39.8 1.4 %collective-permute-done.13.e_ref = bf16[256,256]{1,0:T(8,128)(2,1)S(1)} collective-permute-done((bf16[256,256]{1,0:T(8,128)(2,1)S(1)}, bf16[256,256]{1,0:T(8,128)(2,1)S(1)}, u32[]{:S(2)}, u32[]{:S(2)}) %collective-permute-start.13) | collective-permute-done | bytes 131104 | tf_op jit(solution)/shard_map/ppermute | solution.py:362
  41.2 0.6 %cross_attend.1 = (f32[64,640]{1,0:T(8,128)S(1)}, f32[64,640]{1,0:T(8,128)S(1)}) custom-call(f32[256,1024]{1,0:T(8,128)S(1)} %project.7.acc_ref, bf16[256,256]{1,0:T(8,128)(2,1)S(1)} %collective-permute-done.13.e_ref, bf16[256,1024]{1,0:T(8,128)(2,1)S(1)} %get-tuple-element.42.map_ref, bf16[128,512]{1,0:T(8,128)(2,1)S(1)} %get-tuple-element.43.tgt_ref, ...), custom_call_target="tpu_custom_call" | custom-call | flops 134217728 | bytes 2293760 | tf_op jit(solution)/shard_map/cross_attend/pallas_call | solution.py:62
  41.9 1.4 %collective-permute-done.14.refs_1_ = f32[64,640]{1,0:T(8,128)S(1)} collective-permute-done((f32[64,640]{1,0:T(8,128)S(1)}, f32[64,640]{1,0:T(8,128)S(1)}, u32[]{:S(2)}, u32[]{:S(2)}) %collective-permute-start.14) | collective-permute-done | bytes 163872 | tf_op jit(solution)/shard_map/ppermute | solution.py:379
  43.3 0.8 %combine.1 = bf16[64,512]{1,0:T(8,128)(2,1)} custom-call(f32[64,640]{1,0:T(8,128)S(1)} %get-tuple-element.45.refs_0_, f32[64,640]{1,0:T(8,128)S(1)} %collective-permute-done.14.refs_1_), custom_call_target="tpu_custom_call" | custom-call | bytes 393216 | tf_op jit(solution)/shard_map/combine/pallas_call | solution.py:62
  (25 shorter events, 2.6 us)
Async XLA Ops:
  0.0 2.4 %collective-permute-start.1 = (bf16[256,1024]{1,0:T(8,128)(2,1)}, bf16[256,1024]{1,0:T(8,128)(2,1)S(1)}, u32[]{:S(2)}, u32[]{:S(2)}) collective-permute-start(bf16[256,1024]{1,0:T(8,128)(2,1)} %refs_1_.1), channel_id=1, source_target_pairs={{0,4},{4,0},{1,5},{5,1},{2,6},{6,2},{3,7},{7,3},{8,12},{12,8},{9,1... | collective-permute-start | bytes 1572872 | tf_op jit(solution)/shard_map/ppermute | solution.py:320
  0.5 1.9 %collective-permute-start = (s32[1,256]{1,0:T(1,128)}, s32[1,256]{1,0:T(1,128)S(1)}, u32[]{:S(2)}, u32[]{:S(2)}) collective-permute-start(s32[1,256]{1,0:T(1,128)} %bitcast.1), channel_id=1, source_target_pairs={{0,4},{4,0},{1,5},{5,1},{2,6},{6,2},{3,7},{7,3},{8,12},{12,8},{9,1... | collective-permute-start | bytes 3080 | tf_op jit(solution)/shard_map/ppermute | solution.py:320
  0.5 2.4 %collective-permute-start.2 = (bf16[256,1024]{1,0:T(8,128)(2,1)}, bf16[256,1024]{1,0:T(8,128)(2,1)S(1)}, u32[]{:S(2)}, u32[]{:S(2)}) collective-permute-start(bf16[256,1024]{1,0:T(8,128)(2,1)} %refs_2_.1), channel_id=1, source_target_pairs={{0,4},{4,0},{1,5},{5,1},{2,6},{6,2},{3,7},{7,3},{8,12},{12,8},{9,1... | collective-permute-start | bytes 1572872 | tf_op jit(solution)/shard_map/ppermute | solution.py:320
  3.3 10.7 %collective-permute-start.3 = (bf16[256,512]{1,0:T(8,128)(2,1)S(1)}, bf16[256,512]{1,0:T(8,128)(2,1)S(1)}, u32[]{:S(2)}, u32[]{:S(2)}) collective-permute-start(bf16[256,512]{1,0:T(8,128)(2,1)S(1)} %mix.2.refs_0_), channel_id=1, source_target_pairs={{0,2},{2,3},{3,1},{1,0},{4,6},{6,7},{7,5},{5,4},{8,10},{10,11},{11... | collective-permute-start | bytes 786440 | tf_op jit(solution)/shard_map/ppermute | solution.py:362
  8.2 11.4 %collective-permute-start.8 = (bf16[256,512]{1,0:T(8,128)(2,1)S(1)}, bf16[256,512]{1,0:T(8,128)(2,1)S(1)}, u32[]{:S(2)}, u32[]{:S(2)}) collective-permute-start(bf16[256,512]{1,0:T(8,128)(2,1)S(1)} %mix.3.refs_1_), channel_id=1, source_target_pairs={{0,2},{2,3},{3,1},{1,0},{4,6},{6,7},{7,5},{5,4},{8,10},{10,11},{11... | collective-permute-start | bytes 786440 | tf_op jit(solution)/shard_map/ppermute | solution.py:362
  12.0 22.2 %collective-permute-start.11 = (bf16[4160,512]{1,0:T(8,128)(2,1)S(1)}, bf16[4160,512]{1,0:T(8,128)(2,1)S(1)}, u32[]{:S(2)}, u32[]{:S(2)}) collective-permute-start(bf16[4160,512]{1,0:T(8,128)(2,1)S(1)} %pack.1.refs_2_.refs_4_.refs_3_.refs_0_), channel_id=1, source_target_pairs={{0,4},{4,0},{1,5},{5,1},{2,6},{6,2},{3,7},{7,3},{8,12},{12,8},{9,1... | collective-permute-start | bytes 12779528 | tf_op jit(solution)/shard_map/ppermute | solution.py:320
  14.0 9.7 %collective-permute-start.4 = (bf16[256,256]{1,0:T(8,128)(2,1)S(1)}, bf16[256,256]{1,0:T(8,128)(2,1)S(1)}, u32[]{:S(2)}, u32[]{:S(2)}) collective-permute-start(bf16[256,256]{1,0:T(8,128)(2,1)S(1)} %get-tuple-element.32), channel_id=1, source_target_pairs={{0,2},{2,3},{3,1},{1,0},{4,6},{6,7},{7,5},{5,4},{8,10},{10,11},{11... | collective-permute-start | bytes 393224 | tf_op jit(solution)/shard_map/ppermute | solution.py:362
  17.4 8.4 %collective-permute-start.6 = (bf16[256,256]{1,0:T(8,128)(2,1)S(1)}, bf16[256,256]{1,0:T(8,128)(2,1)S(1)}, u32[]{:S(2)}, u32[]{:S(2)}) collective-permute-start(bf16[256,256]{1,0:T(8,128)(2,1)S(1)} %get-tuple-element.33), channel_id=1, source_target_pairs={{0,2},{2,3},{3,1},{1,0},{4,6},{6,7},{7,5},{5,4},{8,10},{10,11},{11... | collective-permute-start | bytes 393224 | tf_op jit(solution)/shard_map/ppermute | solution.py:362
  19.6 9.0 %collective-permute-start.9 = (bf16[256,256]{1,0:T(8,128)(2,1)S(1)}, bf16[256,256]{1,0:T(8,128)(2,1)S(1)}, u32[]{:S(2)}, u32[]{:S(2)}) collective-permute-start(bf16[256,256]{1,0:T(8,128)(2,1)S(1)} %get-tuple-element.37), channel_id=1, source_target_pairs={{0,2},{2,3},{3,1},{1,0},{4,6},{6,7},{7,5},{5,4},{8,10},{10,11},{11... | collective-permute-start | bytes 393224 | tf_op jit(solution)/shard_map/ppermute | solution.py:362
  23.0 8.4 %collective-permute-start.12 = (bf16[256,256]{1,0:T(8,128)(2,1)S(1)}, bf16[256,256]{1,0:T(8,128)(2,1)S(1)}, u32[]{:S(2)}, u32[]{:S(2)}) collective-permute-start(bf16[256,256]{1,0:T(8,128)(2,1)S(1)} %get-tuple-element.41), channel_id=1, source_target_pairs={{0,2},{2,3},{3,1},{1,0},{4,6},{6,7},{7,5},{5,4},{8,10},{10,11},{11... | collective-permute-start | bytes 393224 | tf_op jit(solution)/shard_map/ppermute | solution.py:362
  23.7 13.0 %collective-permute-start.5 = (bf16[256,256]{1,0:T(8,128)(2,1)S(1)}, bf16[256,256]{1,0:T(8,128)(2,1)S(1)}, u32[]{:S(2)}, u32[]{:S(2)}) collective-permute-start(bf16[256,256]{1,0:T(8,128)(2,1)S(1)} %split.7), channel_id=1, source_target_pairs={{0,2},{2,3},{3,1},{1,0},{4,6},{6,7},{7,5},{5,4},{8,10},{10,11},{11... | collective-permute-start | bytes 393224 | tf_op jit(solution)/shard_map/ppermute | solution.py:362
  25.8 10.9 %collective-permute-start.7 = (bf16[256,256]{1,0:T(8,128)(2,1)S(1)}, bf16[256,256]{1,0:T(8,128)(2,1)S(1)}, u32[]{:S(2)}, u32[]{:S(2)}) collective-permute-start(bf16[256,256]{1,0:T(8,128)(2,1)S(1)} %split.8), channel_id=1, source_target_pairs={{0,2},{2,3},{3,1},{1,0},{4,6},{6,7},{7,5},{5,4},{8,10},{10,11},{11... | collective-permute-start | bytes 393224 | tf_op jit(solution)/shard_map/ppermute | solution.py:362
  28.7 10.6 %collective-permute-start.10 = (bf16[256,256]{1,0:T(8,128)(2,1)S(1)}, bf16[256,256]{1,0:T(8,128)(2,1)S(1)}, u32[]{:S(2)}, u32[]{:S(2)}) collective-permute-start(bf16[256,256]{1,0:T(8,128)(2,1)S(1)} %split.10), channel_id=1, source_target_pairs={{0,2},{2,3},{3,1},{1,0},{4,6},{6,7},{7,5},{5,4},{8,10},{10,11},{11... | collective-permute-start | bytes 393224 | tf_op jit(solution)/shard_map/ppermute | solution.py:362
  31.5 9.8 %collective-permute-start.13 = (bf16[256,256]{1,0:T(8,128)(2,1)S(1)}, bf16[256,256]{1,0:T(8,128)(2,1)S(1)}, u32[]{:S(2)}, u32[]{:S(2)}) collective-permute-start(bf16[256,256]{1,0:T(8,128)(2,1)S(1)} %split.11), channel_id=1, source_target_pairs={{0,2},{2,3},{3,1},{1,0},{4,6},{6,7},{7,5},{5,4},{8,10},{10,11},{11... | collective-permute-start | bytes 393224 | tf_op jit(solution)/shard_map/ppermute | solution.py:362
  41.9 1.5 %collective-permute-start.14 = (f32[64,640]{1,0:T(8,128)S(1)}, f32[64,640]{1,0:T(8,128)S(1)}, u32[]{:S(2)}, u32[]{:S(2)}) collective-permute-start(f32[64,640]{1,0:T(8,128)S(1)} %get-tuple-element.46), channel_id=1, source_target_pairs={{4,0},{0,4},{5,1},{1,5},{6,2},{2,6},{7,3},{3,7},{12,8},{8,12},{13,... | collective-permute-start | bytes 491528 | tf_op jit(solution)/shard_map/ppermute | solution.py:379

commit v17 on v16

--- a/solution.py
+++ b/solution.py
@@ -95,7 +95,7 @@
 
 
 def pack_kernel(*refs):
-    sources, out_ref, sems = refs[:-2], refs[-2], refs[-1]
+    sources, out_ref, sems = refs[:-3], refs[-2], refs[-1]
     copies, row = [], 0
     for i, source in enumerate(sources):
         rows = source.shape[0]
@@ -104,14 +104,14 @@
     run_all(copies)
 
 
-def pack(*arrays):
+def pack(*arrays, after):
     rows = sum(x.shape[0] for x in arrays)
     return call(
         pack_kernel,
         "pack",
         [((rows, arrays[0].shape[1]), arrays[0].dtype)],
-        [pltpu.with_memory_space_constraint(x, pltpu.HBM) for x in arrays],
-        specs=[HBM] * len(arrays),
+        [pltpu.with_memory_space_constraint(x, pltpu.HBM) for x in arrays] + [after],
+        specs=[HBM] * len(arrays) + [VMEM],
         scratch=[pltpu.SemaphoreType.DMA((len(arrays),))],
     )[0]
 
@@ -321,6 +321,7 @@
 
     marks = (doc_ids if n_ctx == 2 else doc_ids + 1).reshape(1, rows)
     keys, near_marks, values = bring(enc_key), bring(marks), bring(enc_value)
+    opened = lax.ppermute(marks, "head", [(i + 1, i) for i in range(n_head - 1)])
     query, own_key, own_value, marks = fetch(enc_query, enc_key, enc_value, marks)
     chunks = 2
     heads = features // HEAD_DIM // chunks
@@ -332,11 +333,11 @@
     key_map, value_map, tgt_query, held[1] = lax.optimization_barrier((key_map, value_map, tgt_query, held[1]))
     near_targets = []
     if n_ctx == 2:
-        own_maps = pack(key_map, value_map, tgt_query)
+        own_maps = pack(key_map, value_map, tgt_query, after=opened)
         shards = [own_maps, *bring(own_maps)]
     else:
         whole = [lax.all_gather(x, "ctx", axis=0, tiled=True) for x in (key_map, value_map)]
-        shards, near_targets = [pack(*whole, tgt_query)], bring(tgt_query)
+        shards, near_targets = [pack(*whole, tgt_query, after=opened)], bring(tgt_query)
     map_rows = (shards[0].shape[0] - tgt_rows) // 2
 
     order = ring_order(n_head)

time: 44.3 us -> 46.7 us (1.054)
  starting transfers between devices: 25.4 us -> 27.6 us
    ppermute x0 -> x1, starting transfers between devices: none -> 1.28 us  [on_device(): lax.ppermute(marks, 'head', [(i + 1, i) for i in range(n_head - 1)])]
    ppermute x10, starting transfers between devices: 24.3 us -> 25.2 us  [on_device(): later = [lax.ppermute(p, 'head', ring) for p in pieces]]
  transfers between devices with their start and end apart: 15 -> 16, of which waited for: 5 -> 5; matrix products, arithmetic and copies ran while one was open for 0% -> 0% of each run, Pallas kernels for 18% -> 18%
where the time goes in v17:
time: 46.7 us; the launch traced here: 46.6 us
  starting transfers between devices  27.6 us (59%)
  Pallas kernels  9.89 us (21%)
  waiting for transfers between devices  8.86 us (19%)
    ppermute x10, starting transfers between devices, on_device(): later = [lax.ppermute(p, 'head', ring) for p in pieces]  25.2 us
    pallas_call x19, Pallas kernels, call(): pl.pallas_call(kernel, in_specs=specs or [VMEM] * len(operands), out_spec...  9.89 us
    ppermute x10, waiting for transfers between devices, on_device(): later = [lax.ppermute(p, 'head', ring) for p in pieces]  7.47 us
    ppermute x1, waiting for transfers between devices, on_device(): lax.ppermute(piece, 'ctx', [(target, source) for source, target in pairs])  1.38 us
    ppermute x1, starting transfers between devices, on_device(): lax.ppermute(marks, 'head', [(i + 1, i) for i in range(n_head - 1)])  1.28 us
    ppermute x4, starting transfers between devices, on_device(): bring = lambda x: [lax.ppermute(x, 'ctx', pairs) for pairs in links]  1.1 us
  transfers between devices with their start and end apart: 16, of which 5 were waited for; matrix products, arithmetic and copies ran while one was open for 0% of the time, Pallas kernels for 18%

profile of v17, /device:TPU:0, one launch (start us, length us, event | category | flops | bytes accessed | tf_op | source)
XLA Modules:
  0.0 46.6 jit_solution(2939332466391801676)
XLA Ops:
  0.5 1.3 %collective-permute-start.11 = (s32[1,256]{1,0:T(1,128)}, s32[1,256]{1,0:T(1,128)S(1)}, u32[]{:S(2)}, u32[]{:S(2)}) collective-permute-start(s32[1,256]{1,0:T(1,128)} %bitcast.2), channel_id=1, source_target_pairs={{1,0},{2,1},{3,2},{5,4},{6,5},{7,6},{9,8},{10,9},{11,10},{13,12},{... | collective-permute-start | bytes 3080 | tf_op jit(solution)/shard_map/ppermute | solution.py:324
  2.3 1.4 %fetch.1 = (bf16[256,1024]{1,0:T(8,128)(2,1)S(1)}, bf16[256,1024]{1,0:T(8,128)(2,1)S(1)}, bf16[256,1024]{1,0:T(8,128)(2,1)S(1)}, s32[1,256]{1,0:T(1,128)S(1)}) custom-call(bf16[256,1024]{1,0:T(8,128)(2,1)} %refs_0_.1, bf16[256,1024]{1,0:T(8,128)(2,1)} %refs_1_.1, bf16[256,1024]{1,0:T(8,128)(2,1)} %refs_2_.1, s32[1,256]{1,0:T(1,128)} %bitcast.3), custom_call_target="tpu_custom_call" | custom-call | bytes 3147776 | tf_op jit(solution)/shard_map/fetch/pallas_call | solution.py:62
  4.6 4.8 %collective-permute-start.3 = (bf16[256,512]{1,0:T(8,128)(2,1)S(1)}, bf16[256,512]{1,0:T(8,128)(2,1)S(1)}, u32[]{:S(2)}, u32[]{:S(2)}) collective-permute-start(bf16[256,512]{1,0:T(8,128)(2,1)S(1)} %mix.2.refs_0_), channel_id=1, source_target_pairs={{0,2},{2,3},{3,1},{1,0},{4,6},{6,7},{7,5},{5,4},{8,10},{10,11},{11... | collective-permute-start | bytes 786440 | tf_op jit(solution)/shard_map/ppermute | solution.py:363
  10.4 1.6 %collective-permute-start.8 = (bf16[256,512]{1,0:T(8,128)(2,1)S(1)}, bf16[256,512]{1,0:T(8,128)(2,1)S(1)}, u32[]{:S(2)}, u32[]{:S(2)}) collective-permute-start(bf16[256,512]{1,0:T(8,128)(2,1)S(1)} %mix.3.refs_1_), channel_id=1, source_target_pairs={{0,2},{2,3},{3,1},{1,0},{4,6},{6,7},{7,5},{5,4},{8,10},{10,11},{11... | collective-permute-start | bytes 786440 | tf_op jit(solution)/shard_map/ppermute | solution.py:363
  12.0 2.2 %pack.1.refs_2_.refs_4_.refs_3_.refs_0_ = bf16[4160,512]{1,0:T(8,128)(2,1)S(1)} custom-call(bf16[2048,512]{1,0:T(8,128)(2,1)} %refs_0_.2, bf16[2048,512]{1,0:T(8,128)(2,1)} %refs_1_.2, bf16[64,512]{1,0:T(8,128)(2,1)} %refs_2_.2, s32[1,256]{1,0:T(1,128)S(1)} %collective-permute-done.11.refs_3_), custom_call_target="tpu_custom_call" | custom-call | bytes 8520704 | tf_op jit(solution)/shard_map/pack/pallas_call | solution.py:62
  14.3 1.8 %collective-permute-done.3.source.refs_0_ = bf16[256,512]{1,0:T(8,128)(2,1)S(1)} collective-permute-done((bf16[256,512]{1,0:T(8,128)(2,1)S(1)}, bf16[256,512]{1,0:T(8,128)(2,1)S(1)}, u32[]{:S(2)}, u32[]{:S(2)}) %collective-permute-start.3) | collective-permute-done | bytes 262176 | tf_op jit(solution)/shard_map/ppermute | solution.py:363
  16.1 3.4 %collective-permute-start.4 = (bf16[256,256]{1,0:T(8,128)(2,1)S(1)}, bf16[256,256]{1,0:T(8,128)(2,1)S(1)}, u32[]{:S(2)}, u32[]{:S(2)}) collective-permute-start(bf16[256,256]{1,0:T(8,128)(2,1)S(1)} %get-tuple-element.32), channel_id=1, source_target_pairs={{0,2},{2,3},{3,1},{1,0},{4,6},{6,7},{7,5},{5,4},{8,10},{10,11},{11... | collective-permute-start | bytes 393224 | tf_op jit(solution)/shard_map/ppermute | solution.py:363
  19.6 0.7 %collective-permute-start.6 = (bf16[256,256]{1,0:T(8,128)(2,1)S(1)}, bf16[256,256]{1,0:T(8,128)(2,1)S(1)}, u32[]{:S(2)}, u32[]{:S(2)}) collective-permute-start(bf16[256,256]{1,0:T(8,128)(2,1)S(1)} %get-tuple-element.33), channel_id=1, source_target_pairs={{0,2},{2,3},{3,1},{1,0},{4,6},{6,7},{7,5},{5,4},{8,10},{10,11},{11... | collective-permute-start | bytes 393224 | tf_op jit(solution)/shard_map/ppermute | solution.py:363
  20.2 1.5 %collective-permute-done.8.source.refs_1_ = bf16[256,512]{1,0:T(8,128)(2,1)S(1)} collective-permute-done((bf16[256,512]{1,0:T(8,128)(2,1)S(1)}, bf16[256,512]{1,0:T(8,128)(2,1)S(1)}, u32[]{:S(2)}, u32[]{:S(2)}) %collective-permute-start.8) | collective-permute-done | bytes 262176 | tf_op jit(solution)/shard_map/ppermute | solution.py:363
  21.8 3.4 %collective-permute-start.9 = (bf16[256,256]{1,0:T(8,128)(2,1)S(1)}, bf16[256,256]{1,0:T(8,128)(2,1)S(1)}, u32[]{:S(2)}, u32[]{:S(2)}) collective-permute-start(bf16[256,256]{1,0:T(8,128)(2,1)S(1)} %get-tuple-element.37), channel_id=1, source_target_pairs={{0,2},{2,3},{3,1},{1,0},{4,6},{6,7},{7,5},{5,4},{8,10},{10,11},{11... | collective-permute-start | bytes 393224 | tf_op jit(solution)/shard_map/ppermute | solution.py:363
  25.2 0.7 %collective-permute-start.13 = (bf16[256,256]{1,0:T(8,128)(2,1)S(1)}, bf16[256,256]{1,0:T(8,128)(2,1)S(1)}, u32[]{:S(2)}, u32[]{:S(2)}) collective-permute-start(bf16[256,256]{1,0:T(8,128)(2,1)S(1)} %get-tuple-element.41), channel_id=1, source_target_pairs={{0,2},{2,3},{3,1},{1,0},{4,6},{6,7},{7,5},{5,4},{8,10},{10,11},{11... | collective-permute-start | bytes 393224 | tf_op jit(solution)/shard_map/ppermute | solution.py:363
  25.9 2.1 %collective-permute-start.5 = (bf16[256,256]{1,0:T(8,128)(2,1)S(1)}, bf16[256,256]{1,0:T(8,128)(2,1)S(1)}, u32[]{:S(2)}, u32[]{:S(2)}) collective-permute-start(bf16[256,256]{1,0:T(8,128)(2,1)S(1)} %split.7), channel_id=1, source_target_pairs={{0,2},{2,3},{3,1},{1,0},{4,6},{6,7},{7,5},{5,4},{8,10},{10,11},{11... | collective-permute-start | bytes 393224 | tf_op jit(solution)/shard_map/ppermute | solution.py:363
  28.0 2.8 %collective-permute-start.7 = (bf16[256,256]{1,0:T(8,128)(2,1)S(1)}, bf16[256,256]{1,0:T(8,128)(2,1)S(1)}, u32[]{:S(2)}, u32[]{:S(2)}) collective-permute-start(bf16[256,256]{1,0:T(8,128)(2,1)S(1)} %split.8), channel_id=1, source_target_pairs={{0,2},{2,3},{3,1},{1,0},{4,6},{6,7},{7,5},{5,4},{8,10},{10,11},{11... | collective-permute-start | bytes 393224 | tf_op jit(solution)/shard_map/ppermute | solution.py:363
  30.8 2.8 %collective-permute-start.10 = (bf16[256,256]{1,0:T(8,128)(2,1)S(1)}, bf16[256,256]{1,0:T(8,128)(2,1)S(1)}, u32[]{:S(2)}, u32[]{:S(2)}) collective-permute-start(bf16[256,256]{1,0:T(8,128)(2,1)S(1)} %split.10), channel_id=1, source_target_pairs={{0,2},{2,3},{3,1},{1,0},{4,6},{6,7},{7,5},{5,4},{8,10},{10,11},{11... | collective-permute-start | bytes 393224 | tf_op jit(solution)/shard_map/ppermute | solution.py:363
  33.6 2.8 %collective-permute-start.14 = (bf16[256,256]{1,0:T(8,128)(2,1)S(1)}, bf16[256,256]{1,0:T(8,128)(2,1)S(1)}, u32[]{:S(2)}, u32[]{:S(2)}) collective-permute-start(bf16[256,256]{1,0:T(8,128)(2,1)S(1)} %split.11), channel_id=1, source_target_pairs={{0,2},{2,3},{3,1},{1,0},{4,6},{6,7},{7,5},{5,4},{8,10},{10,11},{11... | collective-permute-start | bytes 393224 | tf_op jit(solution)/shard_map/ppermute | solution.py:363
  36.6 0.7 %project.4.refs_4_ = f32[256,1024]{1,0:T(8,128)S(1)} custom-call(bf16[256,512]{1,0:T(8,128)(2,1)S(1)} %mix.2.refs_0_, bf16[256,512]{1,0:T(8,128)(2,1)S(1)} %mix.3.refs_1_, bf16[4160,512]{1,0:T(8,128)(2,1)S(1)} %pack.1.refs_2_.refs_4_.refs_3_.refs_0_, bf16[4160,512]{1,0:T(8,128)(2,1)S(1)} %collective-permute-done.12.refs_3_.refs_5_.refs_4_.refs_1_), custom_call_target="tpu_custom_call" | custom-call | flops 536870912 | bytes 10092544 | tf_op jit(solution)/shard_map/project/pallas_call | solution.py:62
  37.4 0.7 %project.5.refs_6_ = f32[256,1024]{1,0:T(8,128)S(1)} custom-call(bf16[256,512]{1,0:T(8,128)(2,1)S(1)} %collective-permute-done.3.source.refs_0_, bf16[256,512]{1,0:T(8,128)(2,1)S(1)} %collective-permute-done.8.source.refs_1_, bf16[4160,512]{1,0:T(8,128)(2,1)S(1)} %pack.1.refs_2_.refs_4_.refs_3_.refs_0_, ...), custom_call_target="tpu_custom_call" | custom-call | flops 536870912 | bytes 11141120 | tf_op jit(solution)/shard_map/project/pallas_call | solution.py:62
  38.1 0.7 %project.6.refs_5_ = f32[256,1024]{1,0:T(8,128)S(1)} custom-call(bf16[256,256]{1,0:T(8,128)(2,1)S(1)} %collective-permute-done.4.source.refs_0_, bf16[256,256]{1,0:T(8,128)(2,1)S(1)} %collective-permute-done.6.source.refs_1_, bf16[256,256]{1,0:T(8,128)(2,1)S(1)} %collective-permute-done.9.source.refs_2_, ...), custom_call_target="tpu_custom_call" | custom-call | flops 536870912 | bytes 11141120 | tf_op jit(solution)/shard_map/project/pallas_call | solution.py:62
  38.9 2.5 %collective-permute-done.10.refs_2_ = bf16[256,256]{1,0:T(8,128)(2,1)S(1)} collective-permute-done((bf16[256,256]{1,0:T(8,128)(2,1)S(1)}, bf16[256,256]{1,0:T(8,128)(2,1)S(1)}, u32[]{:S(2)}, u32[]{:S(2)}) %collective-permute-start.10) | collective-permute-done | bytes 131104 | tf_op jit(solution)/shard_map/ppermute | solution.py:363
  41.4 0.6 %project.7.acc_ref = f32[256,1024]{1,0:T(8,128)S(1)} custom-call(bf16[256,256]{1,0:T(8,128)(2,1)S(1)} %collective-permute-done.5.refs_0_, bf16[256,256]{1,0:T(8,128)(2,1)S(1)} %collective-permute-done.7.refs_1_, bf16[256,256]{1,0:T(8,128)(2,1)S(1)} %collective-permute-done.10.refs_2_, bf16[4160,512]{1,0:T(8,128)(2,1)S(1)} %pack.1.refs_2_.refs_4_.refs_3_.refs_0_, ...), custom_call_target="tpu_custom_call" | custom-call | flops 402653184 | bytes 11010048 | tf_op jit(solution)/shard_map/project/pallas_call | solution.py:62
  42.0 1.7 %collective-permute-done.14.e_ref = bf16[256,256]{1,0:T(8,128)(2,1)S(1)} collective-permute-done((bf16[256,256]{1,0:T(8,128)(2,1)S(1)}, bf16[256,256]{1,0:T(8,128)(2,1)S(1)}, u32[]{:S(2)}, u32[]{:S(2)}) %collective-permute-start.14) | collective-permute-done | bytes 131104 | tf_op jit(solution)/shard_map/ppermute | solution.py:363
  43.7 0.6 %cross_attend.1 = (f32[64,640]{1,0:T(8,128)S(1)}, f32[64,640]{1,0:T(8,128)S(1)}) custom-call(f32[256,1024]{1,0:T(8,128)S(1)} %project.7.acc_ref, bf16[256,256]{1,0:T(8,128)(2,1)S(1)} %collective-permute-done.14.e_ref, bf16[256,1024]{1,0:T(8,128)(2,1)S(1)} %get-tuple-element.42.map_ref, bf16[128,512]{1,0:T(8,128)(2,1)S(1)} %get-tuple-element.43.tgt_ref, ...), custom_call_target="tpu_custom_call" | custom-call | flops 134217728 | bytes 2293760 | tf_op jit(solution)/shard_map/cross_attend/pallas_call | solution.py:62
  44.3 1.4 %collective-permute-done.15.refs_1_ = f32[64,640]{1,0:T(8,128)S(1)} collective-permute-done((f32[64,640]{1,0:T(8,128)S(1)}, f32[64,640]{1,0:T(8,128)S(1)}, u32[]{:S(2)}, u32[]{:S(2)}) %collective-permute-start.15) | collective-permute-done | bytes 163872 | tf_op jit(solution)/shard_map/ppermute | solution.py:380
  45.7 0.8 %combine.1 = bf16[64,512]{1,0:T(8,128)(2,1)} custom-call(f32[64,640]{1,0:T(8,128)S(1)} %get-tuple-element.45.refs_0_, f32[64,640]{1,0:T(8,128)S(1)} %collective-permute-done.15.refs_1_), custom_call_target="tpu_custom_call" | custom-call | bytes 393216 | tf_op jit(solution)/shard_map/combine/pallas_call | solution.py:62
  (27 shorter events, 3.2 us)
Async XLA Ops:
  0.0 3.7 %collective-permute-start.1 = (bf16[256,1024]{1,0:T(8,128)(2,1)}, bf16[256,1024]{1,0:T(8,128)(2,1)S(1)}, u32[]{:S(2)}, u32[]{:S(2)}) collective-permute-start(bf16[256,1024]{1,0:T(8,128)(2,1)} %refs_1_.1), channel_id=1, source_target_pairs={{0,4},{4,0},{1,5},{5,1},{2,6},{6,2},{3,7},{7,3},{8,12},{12,8},{9,1... | collective-permute-start | bytes 1572872 | tf_op jit(solution)/shard_map/ppermute | solution.py:320
  0.5 3.3 %collective-permute-start = (s32[1,256]{1,0:T(1,128)}, s32[1,256]{1,0:T(1,128)S(1)}, u32[]{:S(2)}, u32[]{:S(2)}) collective-permute-start(s32[1,256]{1,0:T(1,128)} %bitcast.1), channel_id=1, source_target_pairs={{0,4},{4,0},{1,5},{5,1},{2,6},{6,2},{3,7},{7,3},{8,12},{12,8},{9,1... | collective-permute-start | bytes 3080 | tf_op jit(solution)/shard_map/ppermute | solution.py:320
  0.5 11.5 %collective-permute-start.11 = (s32[1,256]{1,0:T(1,128)}, s32[1,256]{1,0:T(1,128)S(1)}, u32[]{:S(2)}, u32[]{:S(2)}) collective-permute-start(s32[1,256]{1,0:T(1,128)} %bitcast.2), channel_id=1, source_target_pairs={{1,0},{2,1},{3,2},{5,4},{6,5},{7,6},{9,8},{10,9},{11,10},{13,12},{... | collective-permute-start | bytes 3080 | tf_op jit(solution)/shard_map/ppermute | solution.py:324
  1.8 2.5 %collective-permute-start.2 = (bf16[256,1024]{1,0:T(8,128)(2,1)}, bf16[256,1024]{1,0:T(8,128)(2,1)S(1)}, u32[]{:S(2)}, u32[]{:S(2)}) collective-permute-start(bf16[256,1024]{1,0:T(8,128)(2,1)} %refs_2_.1), channel_id=1, source_target_pairs={{0,4},{4,0},{1,5},{5,1},{2,6},{6,2},{3,7},{7,3},{8,12},{12,8},{9,1... | collective-permute-start | bytes 1572872 | tf_op jit(solution)/shard_map/ppermute | solution.py:320
  4.6 11.5 %collective-permute-start.3 = (bf16[256,512]{1,0:T(8,128)(2,1)S(1)}, bf16[256,512]{1,0:T(8,128)(2,1)S(1)}, u32[]{:S(2)}, u32[]{:S(2)}) collective-permute-start(bf16[256,512]{1,0:T(8,128)(2,1)S(1)} %mix.2.refs_0_), channel_id=1, source_target_pairs={{0,2},{2,3},{3,1},{1,0},{4,6},{6,7},{7,5},{5,4},{8,10},{10,11},{11... | collective-permute-start | bytes 786440 | tf_op jit(solution)/shard_map/ppermute | solution.py:363
  10.4 11.4 %collective-permute-start.8 = (bf16[256,512]{1,0:T(8,128)(2,1)S(1)}, bf16[256,512]{1,0:T(8,128)(2,1)S(1)}, u32[]{:S(2)}, u32[]{:S(2)}) collective-permute-start(bf16[256,512]{1,0:T(8,128)(2,1)S(1)} %mix.3.refs_1_), channel_id=1, source_target_pairs={{0,2},{2,3},{3,1},{1,0},{4,6},{6,7},{7,5},{5,4},{8,10},{10,11},{11... | collective-permute-start | bytes 786440 | tf_op jit(solution)/shard_map/ppermute | solution.py:363
  14.2 22.2 %collective-permute-start.12 = (bf16[4160,512]{1,0:T(8,128)(2,1)S(1)}, bf16[4160,512]{1,0:T(8,128)(2,1)S(1)}, u32[]{:S(2)}, u32[]{:S(2)}) collective-permute-start(bf16[4160,512]{1,0:T(8,128)(2,1)S(1)} %pack.1.refs_2_.refs_4_.refs_3_.refs_0_), channel_id=1, source_target_pairs={{0,4},{4,0},{1,5},{5,1},{2,6},{6,2},{3,7},{7,3},{8,12},{12,8},{9,1... | collective-permute-start | bytes 12779528 | tf_op jit(solution)/shard_map/ppermute | solution.py:320
  16.1 9.7 %collective-permute-start.4 = (bf16[256,256]{1,0:T(8,128)(2,1)S(1)}, bf16[256,256]{1,0:T(8,128)(2,1)S(1)}, u32[]{:S(2)}, u32[]{:S(2)}) collective-permute-start(bf16[256,256]{1,0:T(8,128)(2,1)S(1)} %get-tuple-element.32), channel_id=1, source_target_pairs={{0,2},{2,3},{3,1},{1,0},{4,6},{6,7},{7,5},{5,4},{8,10},{10,11},{11... | collective-permute-start | bytes 393224 | tf_op jit(solution)/shard_map/ppermute | solution.py:363
  19.6 8.4 %collective-permute-start.6 = (bf16[256,256]{1,0:T(8,128)(2,1)S(1)}, bf16[256,256]{1,0:T(8,128)(2,1)S(1)}, u32[]{:S(2)}, u32[]{:S(2)}) collective-permute-start(bf16[256,256]{1,0:T(8,128)(2,1)S(1)} %get-tuple-element.33), channel_id=1, source_target_pairs={{0,2},{2,3},{3,1},{1,0},{4,6},{6,7},{7,5},{5,4},{8,10},{10,11},{11... | collective-permute-start | bytes 393224 | tf_op jit(solution)/shard_map/ppermute | solution.py:363
  21.8 9.0 %collective-permute-start.9 = (bf16[256,256]{1,0:T(8,128)(2,1)S(1)}, bf16[256,256]{1,0:T(8,128)(2,1)S(1)}, u32[]{:S(2)}, u32[]{:S(2)}) collective-permute-start(bf16[256,256]{1,0:T(8,128)(2,1)S(1)} %get-tuple-element.37), channel_id=1, source_target_pairs={{0,2},{2,3},{3,1},{1,0},{4,6},{6,7},{7,5},{5,4},{8,10},{10,11},{11... | collective-permute-start | bytes 393224 | tf_op jit(solution)/shard_map/ppermute | solution.py:363
  25.2 8.4 %collective-permute-start.13 = (bf16[256,256]{1,0:T(8,128)(2,1)S(1)}, bf16[256,256]{1,0:T(8,128)(2,1)S(1)}, u32[]{:S(2)}, u32[]{:S(2)}) collective-permute-start(bf16[256,256]{1,0:T(8,128)(2,1)S(1)} %get-tuple-element.41), channel_id=1, source_target_pairs={{0,2},{2,3},{3,1},{1,0},{4,6},{6,7},{7,5},{5,4},{8,10},{10,11},{11... | collective-permute-start | bytes 393224 | tf_op jit(solution)/shard_map/ppermute | solution.py:363
  25.9 13.0 %collective-permute-start.5 = (bf16[256,256]{1,0:T(8,128)(2,1)S(1)}, bf16[256,256]{1,0:T(8,128)(2,1)S(1)}, u32[]{:S(2)}, u32[]{:S(2)}) collective-permute-start(bf16[256,256]{1,0:T(8,128)(2,1)S(1)} %split.7), channel_id=1, source_target_pairs={{0,2},{2,3},{3,1},{1,0},{4,6},{6,7},{7,5},{5,4},{8,10},{10,11},{11... | collective-permute-start | bytes 393224 | tf_op jit(solution)/shard_map/ppermute | solution.py:363
  28.0 10.9 %collective-permute-start.7 = (bf16[256,256]{1,0:T(8,128)(2,1)S(1)}, bf16[256,256]{1,0:T(8,128)(2,1)S(1)}, u32[]{:S(2)}, u32[]{:S(2)}) collective-permute-start(bf16[256,256]{1,0:T(8,128)(2,1)S(1)} %split.8), channel_id=1, source_target_pairs={{0,2},{2,3},{3,1},{1,0},{4,6},{6,7},{7,5},{5,4},{8,10},{10,11},{11... | collective-permute-start | bytes 393224 | tf_op jit(solution)/shard_map/ppermute | solution.py:363
  30.8 10.6 %collective-permute-start.10 = (bf16[256,256]{1,0:T(8,128)(2,1)S(1)}, bf16[256,256]{1,0:T(8,128)(2,1)S(1)}, u32[]{:S(2)}, u32[]{:S(2)}) collective-permute-start(bf16[256,256]{1,0:T(8,128)(2,1)S(1)} %split.10), channel_id=1, source_target_pairs={{0,2},{2,3},{3,1},{1,0},{4,6},{6,7},{7,5},{5,4},{8,10},{10,11},{11... | collective-permute-start | bytes 393224 | tf_op jit(solution)/shard_map/ppermute | solution.py:363
  33.6 10.0 %collective-permute-start.14 = (bf16[256,256]{1,0:T(8,128)(2,1)S(1)}, bf16[256,256]{1,0:T(8,128)(2,1)S(1)}, u32[]{:S(2)}, u32[]{:S(2)}) collective-permute-start(bf16[256,256]{1,0:T(8,128)(2,1)S(1)} %split.11), channel_id=1, source_target_pairs={{0,2},{2,3},{3,1},{1,0},{4,6},{6,7},{7,5},{5,4},{8,10},{10,11},{11... | collective-permute-start | bytes 393224 | tf_op jit(solution)/shard_map/ppermute | solution.py:363
  44.3 1.5 %collective-permute-start.15 = (f32[64,640]{1,0:T(8,128)S(1)}, f32[64,640]{1,0:T(8,128)S(1)}, u32[]{:S(2)}, u32[]{:S(2)}) collective-permute-start(f32[64,640]{1,0:T(8,128)S(1)} %get-tuple-element.46), channel_id=1, source_target_pairs={{4,0},{0,4},{5,1},{1,5},{6,2},{2,6},{7,3},{3,7},{12,8},{8,12},{13,... | collective-permute-start | bytes 491528 | tf_op jit(solution)/shard_map/ppermute | solution.py:380

commit v18 on v16

--- a/solution.py
+++ b/solution.py
@@ -130,7 +130,7 @@
         scores = jnp.concatenate([dot_t(q_ref[:, at], k[:, at]) for k in keys], axis=1)
         _, weights, total = softmax_block(scores, same)
         results.append(weights.astype(BF16))
-        totals = jnp.where(lane == h, total, totals)
+        totals = jnp.where(lane == h, 1.0 / total, totals)
     for h in range(heads):
         weight_ref[:, h * span : (h + 1) * span] = results[h]
     total_ref[...] = totals
@@ -148,29 +148,29 @@
     )
 
 
-def mix_kernel(first, heads, weight_ref, total_ref, *refs):
+def mix_kernel(skip, first, heads, weight_ref, total_ref, *refs):
     values, out_ref = refs[:-1], refs[-1]
     rows = total_ref.shape[0]
     results = []
     for h in range(heads):
-        start = h * rows * len(values)
+        start = (skip + h) * rows * len(values)
         summed = sum(
             dot(weight_ref[:, start + i * rows : start + (i + 1) * rows], v[:, head_columns(first + h)])
             for i, v in enumerate(values)
         )
-        results.append((summed / total_ref[:, h : h + 1]).astype(BF16))
+        results.append((summed * total_ref[:, skip + h : skip + h + 1]).astype(BF16))
     for h in range(heads):
         out_ref[:, head_columns(h)] = results[h]
 
 
-def mix(weights, totals, values, first, heads):
+def mix(weights, totals, values, skip, first, heads):
     rows = totals.shape[0]
     return call(
-        functools.partial(mix_kernel, first, heads),
+        functools.partial(mix_kernel, skip, first, heads),
         "mix",
         [((rows, heads * HEAD_DIM), BF16)],
         [weights, totals, *values],
-        flops=2 * weights.size * HEAD_DIM,
+        flops=2 * rows * rows * len(values) * heads * HEAD_DIM,
     )[0]
 
 
@@ -204,22 +204,21 @@
     def add(map_ref):
         for side in range(2):
             columns = slice(side * half, (side + 1) * half)
-            product = dot(chunk, map_ref[pl.ds(side * map_rows + row, depth * chunks), :])
+            product = dot(chunk, map_ref[pl.ds(side * map_rows + row, chunk.shape[1]), :])
             out_ref[:, columns] = refs[-2][:, columns] + product if has_acc else product
 
     in_shard(maps, shard, add)
 
 
 def project(acc, chunks, place, shards, map_rows):
-    rows, depth = chunks[0].shape
-    width = shards[0].shape[1]
+    rows, width = chunks[0].shape[0], shards[0].shape[1]
     operands = [*chunks, *shards] + ([] if acc is None else [acc])
     return call(
         functools.partial(project_kernel, len(chunks), len(shards), map_rows, acc is not None, place),
         "project",
         [((rows, 2 * width), F32)],
         operands,
-        flops=4 * rows * depth * width * len(chunks),
+        flops=4 * width * sum(x.size for x in chunks),
     )[0]
 
 
@@ -324,12 +323,14 @@
     query, own_key, own_value, marks = fetch(enc_query, enc_key, enc_value, marks)
     chunks = 2
     heads = features // HEAD_DIM // chunks
-    held = [None] * chunks
+    held = []
     for j in range(chunks):
         weights, totals = weigh(query, [own_key, *keys], [marks, *near_marks], j * heads, heads)
-        held[j] = mix(weights, totals, [own_value, *values], j * heads, heads)
-
-    key_map, value_map, tgt_query, held[1] = lax.optimization_barrier((key_map, value_map, tgt_query, held[1]))
+        size = heads if j else 1
+        for skip in range(0, heads, size):
+            held.append(mix(weights, totals, [own_value, *values], skip, j * heads + skip, size))
+
+    key_map, value_map, tgt_query, held[-1] = lax.optimization_barrier((key_map, value_map, tgt_query, held[-1]))
     near_targets = []
     if n_ctx == 2:
         own_maps = pack(key_map, value_map, tgt_query)
@@ -358,7 +359,7 @@
 
     acc, last = None, n_head - 1
     for turn in range(last):
-        pieces = [p for h in held for p in split(h, 2 if turn == 1 else 1)] if turn else held
+        pieces = [p for h in held for p in split(h, h.shape[1] // HEAD_DIM)] if turn else held
         later = [lax.ppermute(p, "head", ring) for p in pieces]
         acc = project(acc, held, functools.partial(place, turn, 0), shards, map_rows)
         held = later

time: 44.3 us -> 44.2 us (level)
  waiting for transfers between devices: 8.63 us -> 7.51 us
  starting transfers between devices: 25.4 us -> 26.3 us
    ppermute x10 -> x11, waiting for transfers between devices: 7.24 us -> 6.11 us  [on_device(): later = [lax.ppermute(p, 'head', ring) for p in pieces]]
    ppermute x10 -> x11, starting transfers between devices: 24.3 us -> 25.2 us  [on_device(): later = [lax.ppermute(p, 'head', ring) for p in pieces]]
    pallas_call x19 -> x21, Pallas kernels: 9.88 us -> 10.1 us  [call(): pl.pallas_call(kernel, in_specs=specs or [VMEM] * len(operands), out_spec...]
  transfers between devices with their start and end apart: 15 -> 16, of which waited for: 5 -> 4; matrix products, arithmetic and copies ran while one was open for 0% -> 0% of each run, Pallas kernels for 18% -> 19%
where the time goes in v18:
time: 44.2 us; the launch traced here: 44.1 us
  starting transfers between devices  26.3 us (60%)
  Pallas kernels  10.1 us (23%)
  waiting for transfers between devices  7.51 us (17%)
    ppermute x11, starting transfers between devices, on_device(): later = [lax.ppermute(p, 'head', ring) for p in pieces]  25.2 us
    pallas_call x21, Pallas kernels, call(): pl.pallas_call(kernel, in_specs=specs or [VMEM] * len(operands), out_spec...  10.1 us
    ppermute x11, waiting for transfers between devices, on_device(): later = [lax.ppermute(p, 'head', ring) for p in pieces]  6.11 us
    ppermute x1, waiting for transfers between devices, on_device(): lax.ppermute(piece, 'ctx', [(target, source) for source, target in pairs])  1.38 us
    ppermute x4, starting transfers between devices, on_device(): bring = lambda x: [lax.ppermute(x, 'ctx', pairs) for pairs in links]  1.03 us
  transfers between devices with their start and end apart: 16, of which 4 were waited for; matrix products, arithmetic and copies ran while one was open for 0% of the time, Pallas kernels for 19%

profile of v18, /device:TPU:0, one launch (start us, length us, event | category | flops | bytes accessed | tf_op | source)
XLA Modules:
  0.0 44.1 jit_solution(273339011970540634)
XLA Ops:
  1.0 1.4 %fetch.1 = (bf16[256,1024]{1,0:T(8,128)(2,1)S(1)}, bf16[256,1024]{1,0:T(8,128)(2,1)S(1)}, bf16[256,1024]{1,0:T(8,128)(2,1)S(1)}, s32[1,256]{1,0:T(1,128)S(1)}) custom-call(bf16[256,1024]{1,0:T(8,128)(2,1)} %refs_0_.1, bf16[256,1024]{1,0:T(8,128)(2,1)} %refs_1_.1, bf16[256,1024]{1,0:T(8,128)(2,1)} %refs_2_.1, s32[1,256]{1,0:T(1,128)} %bitcast.2), custom_call_target="tpu_custom_call" | custom-call | bytes 3147776 | tf_op jit(solution)/shard_map/fetch/pallas_call | solution.py:62
  2.4 0.6 %weigh.2 = (bf16[256,1024]{1,0:T(8,128)(2,1)S(1)}, f32[256,128]{1,0:T(8,128)S(1)}) custom-call(s32[1,256]{1,0:T(1,128)S(1)} %get-tuple-element.24.refs_0_.refs_2_, s32[1,256]{1,0:T(1,128)S(1)} %collective-permute-done.refs_1_.refs_3_, bf16[256,1024]{1,0:T(8,128)(2,1)S(1)} %get-tuple-element.25.refs_2_, bf16[256,1024]{1,0:T(8,128)(2,1)S(1)} %get-tuple-element.26.refs_3_, ...), custom_call_target="tpu_custom_call" | custom-call | flops 6000000000 | bytes 2230272 | tf_op jit(solution)/shard_map/weigh/pallas_call | solution.py:62
  3.2 4.0 %collective-permute-start.3 = (bf16[256,256]{1,0:T(8,128)(2,1)S(1)}, bf16[256,256]{1,0:T(8,128)(2,1)S(1)}, u32[]{:S(2)}, u32[]{:S(2)}) collective-permute-start(bf16[256,256]{1,0:T(8,128)(2,1)S(1)} %mix.3.refs_0_), channel_id=1, source_target_pairs={{0,2},{2,3},{3,1},{1,0},{4,6},{6,7},{7,5},{5,4},{8,10},{10,11},{11... | collective-permute-start | bytes 393224 | tf_op jit(solution)/shard_map/ppermute | solution.py:363
  7.4 1.6 %collective-permute-start.6 = (bf16[256,256]{1,0:T(8,128)(2,1)S(1)}, bf16[256,256]{1,0:T(8,128)(2,1)S(1)}, u32[]{:S(2)}, u32[]{:S(2)}) collective-permute-start(bf16[256,256]{1,0:T(8,128)(2,1)S(1)} %mix.4.refs_1_), channel_id=1, source_target_pairs={{0,2},{2,3},{3,1},{1,0},{4,6},{6,7},{7,5},{5,4},{8,10},{10,11},{11... | collective-permute-start | bytes 393224 | tf_op jit(solution)/shard_map/ppermute | solution.py:363
  9.1 0.6 %weigh.3 = (bf16[256,1024]{1,0:T(8,128)(2,1)S(1)}, f32[256,128]{1,0:T(8,128)S(1)}) custom-call(s32[1,256]{1,0:T(1,128)S(1)} %get-tuple-element.24.refs_0_.refs_2_, s32[1,256]{1,0:T(1,128)S(1)} %collective-permute-done.refs_1_.refs_3_, bf16[256,1024]{1,0:T(8,128)(2,1)S(1)} %get-tuple-element.25.refs_2_, bf16[256,1024]{1,0:T(8,128)(2,1)S(1)} %get-tuple-element.26.refs_3_, ...), custom_call_target="tpu_custom_call" | custom-call | flops 6000000000 | bytes 2230272 | tf_op jit(solution)/shard_map/weigh/pallas_call | solution.py:62
  10.4 2.2 %pack.1.refs_3_.refs_4_.refs_0_ = bf16[4160,512]{1,0:T(8,128)(2,1)S(1)} custom-call(bf16[2048,512]{1,0:T(8,128)(2,1)} %refs_0_.2, bf16[2048,512]{1,0:T(8,128)(2,1)} %refs_1_.2, bf16[64,512]{1,0:T(8,128)(2,1)} %refs_2_.2), custom_call_target="tpu_custom_call" | custom-call | bytes 8519680 | tf_op jit(solution)/shard_map/pack/pallas_call | solution.py:62
  12.7 1.8 %collective-permute-start.4 = (bf16[256,256]{1,0:T(8,128)(2,1)S(1)}, bf16[256,256]{1,0:T(8,128)(2,1)S(1)}, u32[]{:S(2)}, u32[]{:S(2)}) collective-permute-start(bf16[256,256]{1,0:T(8,128)(2,1)S(1)} %split.7), channel_id=1, source_target_pairs={{0,2},{2,3},{3,1},{1,0},{4,6},{6,7},{7,5},{5,4},{8,10},{10,11},{11... | collective-permute-start | bytes 393224 | tf_op jit(solution)/shard_map/ppermute | solution.py:363
  14.5 2.8 %collective-permute-start.7 = (bf16[256,256]{1,0:T(8,128)(2,1)S(1)}, bf16[256,256]{1,0:T(8,128)(2,1)S(1)}, u32[]{:S(2)}, u32[]{:S(2)}) collective-permute-start(bf16[256,256]{1,0:T(8,128)(2,1)S(1)} %split.9), channel_id=1, source_target_pairs={{0,2},{2,3},{3,1},{1,0},{4,6},{6,7},{7,5},{5,4},{8,10},{10,11},{11... | collective-permute-start | bytes 393224 | tf_op jit(solution)/shard_map/ppermute | solution.py:363
  17.3 2.2 %collective-permute-done.9.source.refs_2_ = bf16[256,512]{1,0:T(8,128)(2,1)S(1)} collective-permute-done((bf16[256,512]{1,0:T(8,128)(2,1)S(1)}, bf16[256,512]{1,0:T(8,128)(2,1)S(1)}, u32[]{:S(2)}, u32[]{:S(2)}) %collective-permute-start.9) | collective-permute-done | bytes 262176 | tf_op jit(solution)/shard_map/ppermute | solution.py:363
  19.5 3.4 %collective-permute-start.10 = (bf16[256,256]{1,0:T(8,128)(2,1)S(1)}, bf16[256,256]{1,0:T(8,128)(2,1)S(1)}, u32[]{:S(2)}, u32[]{:S(2)}) collective-permute-start(bf16[256,256]{1,0:T(8,128)(2,1)S(1)} %get-tuple-element.33), channel_id=1, source_target_pairs={{0,2},{2,3},{3,1},{1,0},{4,6},{6,7},{7,5},{5,4},{8,10},{10,11},{11... | collective-permute-start | bytes 393224 | tf_op jit(solution)/shard_map/ppermute | solution.py:363
  23.0 0.7 %collective-permute-start.13 = (bf16[256,256]{1,0:T(8,128)(2,1)S(1)}, bf16[256,256]{1,0:T(8,128)(2,1)S(1)}, u32[]{:S(2)}, u32[]{:S(2)}) collective-permute-start(bf16[256,256]{1,0:T(8,128)(2,1)S(1)} %get-tuple-element.37), channel_id=1, source_target_pairs={{0,2},{2,3},{3,1},{1,0},{4,6},{6,7},{7,5},{5,4},{8,10},{10,11},{11... | collective-permute-start | bytes 393224 | tf_op jit(solution)/shard_map/ppermute | solution.py:363
  23.6 2.1 %collective-permute-start.5 = (bf16[256,256]{1,0:T(8,128)(2,1)S(1)}, bf16[256,256]{1,0:T(8,128)(2,1)S(1)}, u32[]{:S(2)}, u32[]{:S(2)}) collective-permute-start(bf16[256,256]{1,0:T(8,128)(2,1)S(1)} %split.8), channel_id=1, source_target_pairs={{0,2},{2,3},{3,1},{1,0},{4,6},{6,7},{7,5},{5,4},{8,10},{10,11},{11... | collective-permute-start | bytes 393224 | tf_op jit(solution)/shard_map/ppermute | solution.py:363
  25.8 2.8 %collective-permute-start.8 = (bf16[256,256]{1,0:T(8,128)(2,1)S(1)}, bf16[256,256]{1,0:T(8,128)(2,1)S(1)}, u32[]{:S(2)}, u32[]{:S(2)}) collective-permute-start(bf16[256,256]{1,0:T(8,128)(2,1)S(1)} %split.10), channel_id=1, source_target_pairs={{0,2},{2,3},{3,1},{1,0},{4,6},{6,7},{7,5},{5,4},{8,10},{10,11},{11... | collective-permute-start | bytes 393224 | tf_op jit(solution)/shard_map/ppermute | solution.py:363
  28.6 2.8 %collective-permute-start.11 = (bf16[256,256]{1,0:T(8,128)(2,1)S(1)}, bf16[256,256]{1,0:T(8,128)(2,1)S(1)}, u32[]{:S(2)}, u32[]{:S(2)}) collective-permute-start(bf16[256,256]{1,0:T(8,128)(2,1)S(1)} %split.12), channel_id=1, source_target_pairs={{0,2},{2,3},{3,1},{1,0},{4,6},{6,7},{7,5},{5,4},{8,10},{10,11},{11... | collective-permute-start | bytes 393224 | tf_op jit(solution)/shard_map/ppermute | solution.py:363
  31.4 2.8 %collective-permute-start.14 = (bf16[256,256]{1,0:T(8,128)(2,1)S(1)}, bf16[256,256]{1,0:T(8,128)(2,1)S(1)}, u32[]{:S(2)}, u32[]{:S(2)}) collective-permute-start(bf16[256,256]{1,0:T(8,128)(2,1)S(1)} %split.13), channel_id=1, source_target_pairs={{0,2},{2,3},{3,1},{1,0},{4,6},{6,7},{7,5},{5,4},{8,10},{10,11},{11... | collective-permute-start | bytes 393224 | tf_op jit(solution)/shard_map/ppermute | solution.py:363
  34.4 0.7 %project.4.refs_5_ = f32[256,1024]{1,0:T(8,128)S(1)} custom-call(bf16[256,256]{1,0:T(8,128)(2,1)S(1)} %mix.3.refs_0_, bf16[256,256]{1,0:T(8,128)(2,1)S(1)} %mix.4.refs_1_, bf16[256,512]{1,0:T(8,128)(2,1)S(1)} %mix.5.refs_2_, bf16[4160,512]{1,0:T(8,128)(2,1)S(1)} %pack.1.refs_3_.refs_4_.refs_0_, ...), custom_call_target="tpu_custom_call" | custom-call | flops 536870912 | bytes 10092544 | tf_op jit(solution)/shard_map/project/pallas_call | solution.py:62
  35.1 0.7 %project.5.refs_6_ = f32[256,1024]{1,0:T(8,128)S(1)} custom-call(bf16[256,256]{1,0:T(8,128)(2,1)S(1)} %collective-permute-done.3.source.refs_0_, bf16[256,256]{1,0:T(8,128)(2,1)S(1)} %collective-permute-done.6.source.refs_1_, bf16[256,512]{1,0:T(8,128)(2,1)S(1)} %collective-permute-done.9.source.refs_2_, bf16[4160,512]{1,0:T(8,128)(2,1)S(1)} %pack.1.refs_3_.refs_4_.refs_0_, ...), custom_call_target="tpu_custom_call" | custom-call | flops 536870912 | bytes 11141120 | tf_op jit(solution)/shard_map/project/pallas_call | solution.py:62
  35.9 0.7 %project.6.refs_5_ = f32[256,1024]{1,0:T(8,128)S(1)} custom-call(bf16[256,256]{1,0:T(8,128)(2,1)S(1)} %collective-permute-done.4.source.refs_0_, bf16[256,256]{1,0:T(8,128)(2,1)S(1)} %collective-permute-done.7.source.refs_1_, bf16[256,256]{1,0:T(8,128)(2,1)S(1)} %collective-permute-done.10.source.refs_2_, ...), custom_call_target="tpu_custom_call" | custom-call | flops 536870912 | bytes 11141120 | tf_op jit(solution)/shard_map/project/pallas_call | solution.py:62
  36.7 2.5 %collective-permute-done.11.refs_2_ = bf16[256,256]{1,0:T(8,128)(2,1)S(1)} collective-permute-done((bf16[256,256]{1,0:T(8,128)(2,1)S(1)}, bf16[256,256]{1,0:T(8,128)(2,1)S(1)}, u32[]{:S(2)}, u32[]{:S(2)}) %collective-permute-start.11) | collective-permute-done | bytes 131104 | tf_op jit(solution)/shard_map/ppermute | solution.py:363
  39.2 0.6 %project.7.acc_ref = f32[256,1024]{1,0:T(8,128)S(1)} custom-call(bf16[256,256]{1,0:T(8,128)(2,1)S(1)} %collective-permute-done.5.refs_0_, bf16[256,256]{1,0:T(8,128)(2,1)S(1)} %collective-permute-done.8.refs_1_, bf16[256,256]{1,0:T(8,128)(2,1)S(1)} %collective-permute-done.11.refs_2_, bf16[4160,512]{1,0:T(8,128)(2,1)S(1)} %pack.1.refs_3_.refs_4_.refs_0_, ...), custom_call_target="tpu_custom_call" | custom-call | flops 402653184 | bytes 11010048 | tf_op jit(solution)/shard_map/project/pallas_call | solution.py:62
  39.8 1.4 %collective-permute-done.14.e_ref = bf16[256,256]{1,0:T(8,128)(2,1)S(1)} collective-permute-done((bf16[256,256]{1,0:T(8,128)(2,1)S(1)}, bf16[256,256]{1,0:T(8,128)(2,1)S(1)}, u32[]{:S(2)}, u32[]{:S(2)}) %collective-permute-start.14) | collective-permute-done | bytes 131104 | tf_op jit(solution)/shard_map/ppermute | solution.py:363
  41.2 0.6 %cross_attend.1 = (f32[64,640]{1,0:T(8,128)S(1)}, f32[64,640]{1,0:T(8,128)S(1)}) custom-call(f32[256,1024]{1,0:T(8,128)S(1)} %project.7.acc_ref, bf16[256,256]{1,0:T(8,128)(2,1)S(1)} %collective-permute-done.14.e_ref, bf16[256,1024]{1,0:T(8,128)(2,1)S(1)} %get-tuple-element.38.map_ref, bf16[128,512]{1,0:T(8,128)(2,1)S(1)} %get-tuple-element.39.tgt_ref, ...), custom_call_target="tpu_custom_call" | custom-call | flops 134217728 | bytes 2293760 | tf_op jit(solution)/shard_map/cross_attend/pallas_call | solution.py:62
  41.9 1.4 %collective-permute-done.15.refs_1_ = f32[64,640]{1,0:T(8,128)S(1)} collective-permute-done((f32[64,640]{1,0:T(8,128)S(1)}, f32[64,640]{1,0:T(8,128)S(1)}, u32[]{:S(2)}, u32[]{:S(2)}) %collective-permute-start.15) | collective-permute-done | bytes 163872 | tf_op jit(solution)/shard_map/ppermute | solution.py:380
  43.3 0.8 %combine.1 = bf16[64,512]{1,0:T(8,128)(2,1)} custom-call(f32[64,640]{1,0:T(8,128)S(1)} %get-tuple-element.41.refs_0_, f32[64,640]{1,0:T(8,128)S(1)} %collective-permute-done.15.refs_1_), custom_call_target="tpu_custom_call" | custom-call | bytes 393216 | tf_op jit(solution)/shard_map/combine/pallas_call | solution.py:62
  (29 shorter events, 2.6 us)
Async XLA Ops:
  0.0 2.4 %collective-permute-start.1 = (bf16[256,1024]{1,0:T(8,128)(2,1)}, bf16[256,1024]{1,0:T(8,128)(2,1)S(1)}, u32[]{:S(2)}, u32[]{:S(2)}) collective-permute-start(bf16[256,1024]{1,0:T(8,128)(2,1)} %refs_1_.1), channel_id=1, source_target_pairs={{0,4},{4,0},{1,5},{5,1},{2,6},{6,2},{3,7},{7,3},{8,12},{12,8},{9,1... | collective-permute-start | bytes 1572872 | tf_op jit(solution)/shard_map/ppermute | solution.py:319
  0.5 1.9 %collective-permute-start = (s32[1,256]{1,0:T(1,128)}, s32[1,256]{1,0:T(1,128)S(1)}, u32[]{:S(2)}, u32[]{:S(2)}) collective-permute-start(s32[1,256]{1,0:T(1,128)} %bitcast.1), channel_id=1, source_target_pairs={{0,4},{4,0},{1,5},{5,1},{2,6},{6,2},{3,7},{7,3},{8,12},{12,8},{9,1... | collective-permute-start | bytes 3080 | tf_op jit(solution)/shard_map/ppermute | solution.py:319
  0.5 2.4 %collective-permute-start.2 = (bf16[256,1024]{1,0:T(8,128)(2,1)}, bf16[256,1024]{1,0:T(8,128)(2,1)S(1)}, u32[]{:S(2)}, u32[]{:S(2)}) collective-permute-start(bf16[256,1024]{1,0:T(8,128)(2,1)} %refs_2_.1), channel_id=1, source_target_pairs={{0,4},{4,0},{1,5},{5,1},{2,6},{6,2},{3,7},{7,3},{8,12},{12,8},{9,1... | collective-permute-start | bytes 1572872 | tf_op jit(solution)/shard_map/ppermute | solution.py:319
  3.2 9.5 %collective-permute-start.3 = (bf16[256,256]{1,0:T(8,128)(2,1)S(1)}, bf16[256,256]{1,0:T(8,128)(2,1)S(1)}, u32[]{:S(2)}, u32[]{:S(2)}) collective-permute-start(bf16[256,256]{1,0:T(8,128)(2,1)S(1)} %mix.3.refs_0_), channel_id=1, source_target_pairs={{0,2},{2,3},{3,1},{1,0},{4,6},{6,7},{7,5},{5,4},{8,10},{10,11},{11... | collective-permute-start | bytes 393224 | tf_op jit(solution)/shard_map/ppermute | solution.py:363
  7.4 7.1 %collective-permute-start.6 = (bf16[256,256]{1,0:T(8,128)(2,1)S(1)}, bf16[256,256]{1,0:T(8,128)(2,1)S(1)}, u32[]{:S(2)}, u32[]{:S(2)}) collective-permute-start(bf16[256,256]{1,0:T(8,128)(2,1)S(1)} %mix.4.refs_1_), channel_id=1, source_target_pairs={{0,2},{2,3},{3,1},{1,0},{4,6},{6,7},{7,5},{5,4},{8,10},{10,11},{11... | collective-permute-start | bytes 393224 | tf_op jit(solution)/shard_map/ppermute | solution.py:363
  10.0 9.5 %collective-permute-start.9 = (bf16[256,512]{1,0:T(8,128)(2,1)S(1)}, bf16[256,512]{1,0:T(8,128)(2,1)S(1)}, u32[]{:S(2)}, u32[]{:S(2)}) collective-permute-start(bf16[256,512]{1,0:T(8,128)(2,1)S(1)} %mix.5.refs_2_), channel_id=1, source_target_pairs={{0,2},{2,3},{3,1},{1,0},{4,6},{6,7},{7,5},{5,4},{8,10},{10,11},{11... | collective-permute-start | bytes 786440 | tf_op jit(solution)/shard_map/ppermute | solution.py:363
  12.6 21.6 %collective-permute-start.12 = (bf16[4160,512]{1,0:T(8,128)(2,1)S(1)}, bf16[4160,512]{1,0:T(8,128)(2,1)S(1)}, u32[]{:S(2)}, u32[]{:S(2)}) collective-permute-start(bf16[4160,512]{1,0:T(8,128)(2,1)S(1)} %pack.1.refs_3_.refs_4_.refs_0_), channel_id=1, source_target_pairs={{0,4},{4,0},{1,5},{5,1},{2,6},{6,2},{3,7},{7,3},{8,12},{12,8},{9,1... | collective-permute-start | bytes 12779528 | tf_op jit(solution)/shard_map/ppermute | solution.py:319
  12.7 10.9 %collective-permute-start.4 = (bf16[256,256]{1,0:T(8,128)(2,1)S(1)}, bf16[256,256]{1,0:T(8,128)(2,1)S(1)}, u32[]{:S(2)}, u32[]{:S(2)}) collective-permute-start(bf16[256,256]{1,0:T(8,128)(2,1)S(1)} %split.7), channel_id=1, source_target_pairs={{0,2},{2,3},{3,1},{1,0},{4,6},{6,7},{7,5},{5,4},{8,10},{10,11},{11... | collective-permute-start | bytes 393224 | tf_op jit(solution)/shard_map/ppermute | solution.py:363
  14.5 11.2 %collective-permute-start.7 = (bf16[256,256]{1,0:T(8,128)(2,1)S(1)}, bf16[256,256]{1,0:T(8,128)(2,1)S(1)}, u32[]{:S(2)}, u32[]{:S(2)}) collective-permute-start(bf16[256,256]{1,0:T(8,128)(2,1)S(1)} %split.9), channel_id=1, source_target_pairs={{0,2},{2,3},{3,1},{1,0},{4,6},{6,7},{7,5},{5,4},{8,10},{10,11},{11... | collective-permute-start | bytes 393224 | tf_op jit(solution)/shard_map/ppermute | solution.py:363
  19.5 9.0 %collective-permute-start.10 = (bf16[256,256]{1,0:T(8,128)(2,1)S(1)}, bf16[256,256]{1,0:T(8,128)(2,1)S(1)}, u32[]{:S(2)}, u32[]{:S(2)}) collective-permute-start(bf16[256,256]{1,0:T(8,128)(2,1)S(1)} %get-tuple-element.33), channel_id=1, source_target_pairs={{0,2},{2,3},{3,1},{1,0},{4,6},{6,7},{7,5},{5,4},{8,10},{10,11},{11... | collective-permute-start | bytes 393224 | tf_op jit(solution)/shard_map/ppermute | solution.py:363
  23.0 8.4 %collective-permute-start.13 = (bf16[256,256]{1,0:T(8,128)(2,1)S(1)}, bf16[256,256]{1,0:T(8,128)(2,1)S(1)}, u32[]{:S(2)}, u32[]{:S(2)}) collective-permute-start(bf16[256,256]{1,0:T(8,128)(2,1)S(1)} %get-tuple-element.37), channel_id=1, source_target_pairs={{0,2},{2,3},{3,1},{1,0},{4,6},{6,7},{7,5},{5,4},{8,10},{10,11},{11... | collective-permute-start | bytes 393224 | tf_op jit(solution)/shard_map/ppermute | solution.py:363
  23.6 13.0 %collective-permute-start.5 = (bf16[256,256]{1,0:T(8,128)(2,1)S(1)}, bf16[256,256]{1,0:T(8,128)(2,1)S(1)}, u32[]{:S(2)}, u32[]{:S(2)}) collective-permute-start(bf16[256,256]{1,0:T(8,128)(2,1)S(1)} %split.8), channel_id=1, source_target_pairs={{0,2},{2,3},{3,1},{1,0},{4,6},{6,7},{7,5},{5,4},{8,10},{10,11},{11... | collective-permute-start | bytes 393224 | tf_op jit(solution)/shard_map/ppermute | solution.py:363
  25.8 10.9 %collective-permute-start.8 = (bf16[256,256]{1,0:T(8,128)(2,1)S(1)}, bf16[256,256]{1,0:T(8,128)(2,1)S(1)}, u32[]{:S(2)}, u32[]{:S(2)}) collective-permute-start(bf16[256,256]{1,0:T(8,128)(2,1)S(1)} %split.10), channel_id=1, source_target_pairs={{0,2},{2,3},{3,1},{1,0},{4,6},{6,7},{7,5},{5,4},{8,10},{10,11},{11... | collective-permute-start | bytes 393224 | tf_op jit(solution)/shard_map/ppermute | solution.py:363
  28.6 10.6 %collective-permute-start.11 = (bf16[256,256]{1,0:T(8,128)(2,1)S(1)}, bf16[256,256]{1,0:T(8,128)(2,1)S(1)}, u32[]{:S(2)}, u32[]{:S(2)}) collective-permute-start(bf16[256,256]{1,0:T(8,128)(2,1)S(1)} %split.12), channel_id=1, source_target_pairs={{0,2},{2,3},{3,1},{1,0},{4,6},{6,7},{7,5},{5,4},{8,10},{10,11},{11... | collective-permute-start | bytes 393224 | tf_op jit(solution)/shard_map/ppermute | solution.py:363
  31.4 9.8 %collective-permute-start.14 = (bf16[256,256]{1,0:T(8,128)(2,1)S(1)}, bf16[256,256]{1,0:T(8,128)(2,1)S(1)}, u32[]{:S(2)}, u32[]{:S(2)}) collective-permute-start(bf16[256,256]{1,0:T(8,128)(2,1)S(1)} %split.13), channel_id=1, source_target_pairs={{0,2},{2,3},{3,1},{1,0},{4,6},{6,7},{7,5},{5,4},{8,10},{10,11},{11... | collective-permute-start | bytes 393224 | tf_op jit(solution)/shard_map/ppermute | solution.py:363
  41.8 1.5 %collective-permute-start.15 = (f32[64,640]{1,0:T(8,128)S(1)}, f32[64,640]{1,0:T(8,128)S(1)}, u32[]{:S(2)}, u32[]{:S(2)}) collective-permute-start(f32[64,640]{1,0:T(8,128)S(1)} %get-tuple-element.42), channel_id=1, source_target_pairs={{4,0},{0,4},{5,1},{1,5},{6,2},{2,6},{7,3},{3,7},{12,8},{8,12},{13,... | collective-permute-start | bytes 491528 | tf_op jit(solution)/shard_map/ppermute | solution.py:380

commit v19 on v18

--- a/solution.py
+++ b/solution.py
@@ -56,13 +56,13 @@
     return top, weights, jnp.sum(weights, axis=1, keepdims=True)
 
 
-def call(kernel, name, outs, operands, flops=0, exps=0, specs=None, scratch=(), limit=8 << 20):
+def call(kernel, name, outs, operands, flops=0, exps=0, specs=None, scratch=(), limit=8 << 20, out_specs=None):
     out_shape = [jax.ShapeDtypeStruct(*o) for o in outs]
     moved = sum(x.size * x.dtype.itemsize for x in [*operands, *out_shape])
     return pl.pallas_call(
         kernel,
         in_specs=specs or [VMEM] * len(operands),
-        out_specs=[VMEM] * len(outs),
+        out_specs=out_specs or [VMEM] * len(outs),
         out_shape=out_shape,
         scratch_shapes=list(scratch),
         compiler_params=pltpu.CompilerParams(vmem_limit_bytes=limit),
@@ -296,19 +296,35 @@
 
 
 def combine_kernel(*refs):
-    parts, out_ref = [r[...] for r in refs[:-1]], refs[-1]
+    parts, (out_hbm, out_ref, sems) = [r[...] for r in refs[:-3]], refs[-3:]
     width = out_ref.shape[1]
     heads = width // HEAD_DIM
-    results = []
-    for h in range(heads):
+    copies = []
+    for h in range(heads):
+        at = head_columns(h)
         tops = [x[:, width + h : width + h + 1] for x in parts]
         totals = [x[:, width + heads + h : width + heads + h + 1] for x in parts]
         top = functools.reduce(jnp.maximum, tops)
         factors = [jnp.exp(t - top) for t in tops]
         share = 1.0 / sum(f * t for f, t in zip(factors, totals))
-        results.append(sum((f * share) * x[:, head_columns(h)] for f, x in zip(factors, parts)))
-    for h in range(heads):
-        out_ref[:, head_columns(h)] = results[h].astype(BF16)
+        out_ref[:, at] = sum((f * share) * x[:, at] for f, x in zip(factors, parts)).astype(BF16)
+        copies.append(pltpu.make_async_copy(out_ref.at[:, at], out_hbm.at[:, at], sems.at[h]))
+        copies[-1].start()
+    for copy in copies:
+        copy.wait()
+
+
+def combine(parts, width):
+    count = parts[0].shape[0]
+    return call(
+        combine_kernel,
+        "combine",
+        [((count, width), BF16)],
+        parts,
+        scratch=[pltpu.VMEM((count, width), BF16), pltpu.SemaphoreType.DMA((width // HEAD_DIM,))],
+        limit=4 << 20,
+        out_specs=[HBM],
+    )[0]
 
 
 def on_device(enc_query, enc_key, enc_value, doc_ids, key_map, value_map, tgt_query):
@@ -383,7 +399,7 @@
             column = lax.broadcasted_iota(jnp.int32, other.shape, 1)
             other = jnp.where((lax.axis_index("ctx") == end) & (column >= width), NEG_FILL, other)
         combined.append(other)
-    return call(combine_kernel, "combine", [((tgt_rows, width), BF16)], combined, limit=4 << 20)[0]
+    return combine(combined, width)
 
 
 def solution(mesh):

time: 44.2 us -> 44.2 us (level)
  no operation moved by 1% of the time
where the time goes in v19:
time: 44.2 us; the launch traced here: 44.1 us
  starting transfers between devices  26.3 us (60%)
  Pallas kernels  10.1 us (23%)
  waiting for transfers between devices  7.51 us (17%)
    ppermute x11, starting transfers between devices, on_device(): later = [lax.ppermute(p, 'head', ring) for p in pieces]  25.2 us
    pallas_call x21, Pallas kernels, call(): pl.pallas_call(kernel, in_specs=specs or [VMEM] * len(operands), out_spec...  10.1 us
    ppermute x11, waiting for transfers between devices, on_device(): later = [lax.ppermute(p, 'head', ring) for p in pieces]  6.11 us
    ppermute x1, waiting for transfers between devices, on_device(): lax.ppermute(piece, 'ctx', [(target, source) for source, target in pairs])  1.38 us
    ppermute x4, starting transfers between devices, on_device(): bring = lambda x: [lax.ppermute(x, 'ctx', pairs) for pairs in links]  1.03 us
  transfers between devices with their start and end apart: 16, of which 4 were waited for; matrix products, arithmetic and copies ran while one was open for 0% of the time, Pallas kernels for 19%

profile of v19, /device:TPU:0, one launch (start us, length us, event | category | flops | bytes accessed | tf_op | source)
XLA Modules:
  0.0 44.1 jit_solution(6137748885163538495)
XLA Ops:
  1.0 1.4 %fetch.1 = (bf16[256,1024]{1,0:T(8,128)(2,1)S(1)}, bf16[256,1024]{1,0:T(8,128)(2,1)S(1)}, bf16[256,1024]{1,0:T(8,128)(2,1)S(1)}, s32[1,256]{1,0:T(1,128)S(1)}) custom-call(bf16[256,1024]{1,0:T(8,128)(2,1)} %refs_0_.1, bf16[256,1024]{1,0:T(8,128)(2,1)} %refs_1_.1, bf16[256,1024]{1,0:T(8,128)(2,1)} %refs_2_.1, s32[1,256]{1,0:T(1,128)} %bitcast.2), custom_call_target="tpu_custom_call" | custom-call | bytes 3147776 | tf_op jit(solution)/shard_map/fetch/pallas_call | solution.py:62
  2.4 0.6 %weigh.2 = (bf16[256,1024]{1,0:T(8,128)(2,1)S(1)}, f32[256,128]{1,0:T(8,128)S(1)}) custom-call(s32[1,256]{1,0:T(1,128)S(1)} %get-tuple-element.24.refs_0_.refs_2_, s32[1,256]{1,0:T(1,128)S(1)} %collective-permute-done.refs_1_.refs_3_, bf16[256,1024]{1,0:T(8,128)(2,1)S(1)} %get-tuple-element.25.refs_2_, bf16[256,1024]{1,0:T(8,128)(2,1)S(1)} %get-tuple-element.26.refs_3_, ...), custom_call_target="tpu_custom_call" | custom-call | flops 6000000000 | bytes 2230272 | tf_op jit(solution)/shard_map/weigh/pallas_call | solution.py:62
  3.2 4.0 %collective-permute-start.3 = (bf16[256,256]{1,0:T(8,128)(2,1)S(1)}, bf16[256,256]{1,0:T(8,128)(2,1)S(1)}, u32[]{:S(2)}, u32[]{:S(2)}) collective-permute-start(bf16[256,256]{1,0:T(8,128)(2,1)S(1)} %mix.3.refs_0_), channel_id=1, source_target_pairs={{0,2},{2,3},{3,1},{1,0},{4,6},{6,7},{7,5},{5,4},{8,10},{10,11},{11... | collective-permute-start | bytes 393224 | tf_op jit(solution)/shard_map/ppermute | solution.py:379
  7.4 1.6 %collective-permute-start.6 = (bf16[256,256]{1,0:T(8,128)(2,1)S(1)}, bf16[256,256]{1,0:T(8,128)(2,1)S(1)}, u32[]{:S(2)}, u32[]{:S(2)}) collective-permute-start(bf16[256,256]{1,0:T(8,128)(2,1)S(1)} %mix.4.refs_1_), channel_id=1, source_target_pairs={{0,2},{2,3},{3,1},{1,0},{4,6},{6,7},{7,5},{5,4},{8,10},{10,11},{11... | collective-permute-start | bytes 393224 | tf_op jit(solution)/shard_map/ppermute | solution.py:379
  9.1 0.6 %weigh.3 = (bf16[256,1024]{1,0:T(8,128)(2,1)S(1)}, f32[256,128]{1,0:T(8,128)S(1)}) custom-call(s32[1,256]{1,0:T(1,128)S(1)} %get-tuple-element.24.refs_0_.refs_2_, s32[1,256]{1,0:T(1,128)S(1)} %collective-permute-done.refs_1_.refs_3_, bf16[256,1024]{1,0:T(8,128)(2,1)S(1)} %get-tuple-element.25.refs_2_, bf16[256,1024]{1,0:T(8,128)(2,1)S(1)} %get-tuple-element.26.refs_3_, ...), custom_call_target="tpu_custom_call" | custom-call | flops 6000000000 | bytes 2230272 | tf_op jit(solution)/shard_map/weigh/pallas_call | solution.py:62
  10.4 2.2 %pack.1.refs_3_.refs_4_.refs_0_ = bf16[4160,512]{1,0:T(8,128)(2,1)S(1)} custom-call(bf16[2048,512]{1,0:T(8,128)(2,1)} %refs_0_.2, bf16[2048,512]{1,0:T(8,128)(2,1)} %refs_1_.2, bf16[64,512]{1,0:T(8,128)(2,1)} %refs_2_.2), custom_call_target="tpu_custom_call" | custom-call | bytes 8519680 | tf_op jit(solution)/shard_map/pack/pallas_call | solution.py:62
  12.7 1.8 %collective-permute-start.4 = (bf16[256,256]{1,0:T(8,128)(2,1)S(1)}, bf16[256,256]{1,0:T(8,128)(2,1)S(1)}, u32[]{:S(2)}, u32[]{:S(2)}) collective-permute-start(bf16[256,256]{1,0:T(8,128)(2,1)S(1)} %split.7), channel_id=1, source_target_pairs={{0,2},{2,3},{3,1},{1,0},{4,6},{6,7},{7,5},{5,4},{8,10},{10,11},{11... | collective-permute-start | bytes 393224 | tf_op jit(solution)/shard_map/ppermute | solution.py:379
  14.5 2.8 %collective-permute-start.7 = (bf16[256,256]{1,0:T(8,128)(2,1)S(1)}, bf16[256,256]{1,0:T(8,128)(2,1)S(1)}, u32[]{:S(2)}, u32[]{:S(2)}) collective-permute-start(bf16[256,256]{1,0:T(8,128)(2,1)S(1)} %split.9), channel_id=1, source_target_pairs={{0,2},{2,3},{3,1},{1,0},{4,6},{6,7},{7,5},{5,4},{8,10},{10,11},{11... | collective-permute-start | bytes 393224 | tf_op jit(solution)/shard_map/ppermute | solution.py:379
  17.3 2.2 %collective-permute-done.9.source.refs_2_ = bf16[256,512]{1,0:T(8,128)(2,1)S(1)} collective-permute-done((bf16[256,512]{1,0:T(8,128)(2,1)S(1)}, bf16[256,512]{1,0:T(8,128)(2,1)S(1)}, u32[]{:S(2)}, u32[]{:S(2)}) %collective-permute-start.9) | collective-permute-done | bytes 262176 | tf_op jit(solution)/shard_map/ppermute | solution.py:379
  19.5 3.4 %collective-permute-start.10 = (bf16[256,256]{1,0:T(8,128)(2,1)S(1)}, bf16[256,256]{1,0:T(8,128)(2,1)S(1)}, u32[]{:S(2)}, u32[]{:S(2)}) collective-permute-start(bf16[256,256]{1,0:T(8,128)(2,1)S(1)} %get-tuple-element.33), channel_id=1, source_target_pairs={{0,2},{2,3},{3,1},{1,0},{4,6},{6,7},{7,5},{5,4},{8,10},{10,11},{11... | collective-permute-start | bytes 393224 | tf_op jit(solution)/shard_map/ppermute | solution.py:379
  23.0 0.7 %collective-permute-start.13 = (bf16[256,256]{1,0:T(8,128)(2,1)S(1)}, bf16[256,256]{1,0:T(8,128)(2,1)S(1)}, u32[]{:S(2)}, u32[]{:S(2)}) collective-permute-start(bf16[256,256]{1,0:T(8,128)(2,1)S(1)} %get-tuple-element.37), channel_id=1, source_target_pairs={{0,2},{2,3},{3,1},{1,0},{4,6},{6,7},{7,5},{5,4},{8,10},{10,11},{11... | collective-permute-start | bytes 393224 | tf_op jit(solution)/shard_map/ppermute | solution.py:379
  23.6 2.1 %collective-permute-start.5 = (bf16[256,256]{1,0:T(8,128)(2,1)S(1)}, bf16[256,256]{1,0:T(8,128)(2,1)S(1)}, u32[]{:S(2)}, u32[]{:S(2)}) collective-permute-start(bf16[256,256]{1,0:T(8,128)(2,1)S(1)} %split.8), channel_id=1, source_target_pairs={{0,2},{2,3},{3,1},{1,0},{4,6},{6,7},{7,5},{5,4},{8,10},{10,11},{11... | collective-permute-start | bytes 393224 | tf_op jit(solution)/shard_map/ppermute | solution.py:379
  25.8 2.8 %collective-permute-start.8 = (bf16[256,256]{1,0:T(8,128)(2,1)S(1)}, bf16[256,256]{1,0:T(8,128)(2,1)S(1)}, u32[]{:S(2)}, u32[]{:S(2)}) collective-permute-start(bf16[256,256]{1,0:T(8,128)(2,1)S(1)} %split.10), channel_id=1, source_target_pairs={{0,2},{2,3},{3,1},{1,0},{4,6},{6,7},{7,5},{5,4},{8,10},{10,11},{11... | collective-permute-start | bytes 393224 | tf_op jit(solution)/shard_map/ppermute | solution.py:379
  28.6 2.8 %collective-permute-start.11 = (bf16[256,256]{1,0:T(8,128)(2,1)S(1)}, bf16[256,256]{1,0:T(8,128)(2,1)S(1)}, u32[]{:S(2)}, u32[]{:S(2)}) collective-permute-start(bf16[256,256]{1,0:T(8,128)(2,1)S(1)} %split.12), channel_id=1, source_target_pairs={{0,2},{2,3},{3,1},{1,0},{4,6},{6,7},{7,5},{5,4},{8,10},{10,11},{11... | collective-permute-start | bytes 393224 | tf_op jit(solution)/shard_map/ppermute | solution.py:379
  31.4 2.8 %collective-permute-start.14 = (bf16[256,256]{1,0:T(8,128)(2,1)S(1)}, bf16[256,256]{1,0:T(8,128)(2,1)S(1)}, u32[]{:S(2)}, u32[]{:S(2)}) collective-permute-start(bf16[256,256]{1,0:T(8,128)(2,1)S(1)} %split.13), channel_id=1, source_target_pairs={{0,2},{2,3},{3,1},{1,0},{4,6},{6,7},{7,5},{5,4},{8,10},{10,11},{11... | collective-permute-start | bytes 393224 | tf_op jit(solution)/shard_map/ppermute | solution.py:379
  34.4 0.7 %project.4.refs_5_ = f32[256,1024]{1,0:T(8,128)S(1)} custom-call(bf16[256,256]{1,0:T(8,128)(2,1)S(1)} %mix.3.refs_0_, bf16[256,256]{1,0:T(8,128)(2,1)S(1)} %mix.4.refs_1_, bf16[256,512]{1,0:T(8,128)(2,1)S(1)} %mix.5.refs_2_, bf16[4160,512]{1,0:T(8,128)(2,1)S(1)} %pack.1.refs_3_.refs_4_.refs_0_, ...), custom_call_target="tpu_custom_call" | custom-call | flops 536870912 | bytes 10092544 | tf_op jit(solution)/shard_map/project/pallas_call | solution.py:62
  35.1 0.7 %project.5.refs_6_ = f32[256,1024]{1,0:T(8,128)S(1)} custom-call(bf16[256,256]{1,0:T(8,128)(2,1)S(1)} %collective-permute-done.3.source.refs_0_, bf16[256,256]{1,0:T(8,128)(2,1)S(1)} %collective-permute-done.6.source.refs_1_, bf16[256,512]{1,0:T(8,128)(2,1)S(1)} %collective-permute-done.9.source.refs_2_, bf16[4160,512]{1,0:T(8,128)(2,1)S(1)} %pack.1.refs_3_.refs_4_.refs_0_, ...), custom_call_target="tpu_custom_call" | custom-call | flops 536870912 | bytes 11141120 | tf_op jit(solution)/shard_map/project/pallas_call | solution.py:62
  35.9 0.7 %project.6.refs_5_ = f32[256,1024]{1,0:T(8,128)S(1)} custom-call(bf16[256,256]{1,0:T(8,128)(2,1)S(1)} %collective-permute-done.4.source.refs_0_, bf16[256,256]{1,0:T(8,128)(2,1)S(1)} %collective-permute-done.7.source.refs_1_, bf16[256,256]{1,0:T(8,128)(2,1)S(1)} %collective-permute-done.10.source.refs_2_, ...), custom_call_target="tpu_custom_call" | custom-call | flops 536870912 | bytes 11141120 | tf_op jit(solution)/shard_map/project/pallas_call | solution.py:62
  36.7 2.5 %collective-permute-done.11.refs_2_ = bf16[256,256]{1,0:T(8,128)(2,1)S(1)} collective-permute-done((bf16[256,256]{1,0:T(8,128)(2,1)S(1)}, bf16[256,256]{1,0:T(8,128)(2,1)S(1)}, u32[]{:S(2)}, u32[]{:S(2)}) %collective-permute-start.11) | collective-permute-done | bytes 131104 | tf_op jit(solution)/shard_map/ppermute | solution.py:379
  39.2 0.6 %project.7.acc_ref = f32[256,1024]{1,0:T(8,128)S(1)} custom-call(bf16[256,256]{1,0:T(8,128)(2,1)S(1)} %collective-permute-done.5.refs_0_, bf16[256,256]{1,0:T(8,128)(2,1)S(1)} %collective-permute-done.8.refs_1_, bf16[256,256]{1,0:T(8,128)(2,1)S(1)} %collective-permute-done.11.refs_2_, bf16[4160,512]{1,0:T(8,128)(2,1)S(1)} %pack.1.refs_3_.refs_4_.refs_0_, ...), custom_call_target="tpu_custom_call" | custom-call | flops 402653184 | bytes 11010048 | tf_op jit(solution)/shard_map/project/pallas_call | solution.py:62
  39.8 1.4 %collective-permute-done.14.e_ref = bf16[256,256]{1,0:T(8,128)(2,1)S(1)} collective-permute-done((bf16[256,256]{1,0:T(8,128)(2,1)S(1)}, bf16[256,256]{1,0:T(8,128)(2,1)S(1)}, u32[]{:S(2)}, u32[]{:S(2)}) %collective-permute-start.14) | collective-permute-done | bytes 131104 | tf_op jit(solution)/shard_map/ppermute | solution.py:379
  41.2 0.6 %cross_attend.1 = (f32[64,640]{1,0:T(8,128)S(1)}, f32[64,640]{1,0:T(8,128)S(1)}) custom-call(f32[256,1024]{1,0:T(8,128)S(1)} %project.7.acc_ref, bf16[256,256]{1,0:T(8,128)(2,1)S(1)} %collective-permute-done.14.e_ref, bf16[256,1024]{1,0:T(8,128)(2,1)S(1)} %get-tuple-element.38.map_ref, bf16[128,512]{1,0:T(8,128)(2,1)S(1)} %get-tuple-element.39.tgt_ref, ...), custom_call_target="tpu_custom_call" | custom-call | flops 134217728 | bytes 2293760 | tf_op jit(solution)/shard_map/cross_attend/pallas_call | solution.py:62
  41.9 1.4 %collective-permute-done.15.refs_1_ = f32[64,640]{1,0:T(8,128)S(1)} collective-permute-done((f32[64,640]{1,0:T(8,128)S(1)}, f32[64,640]{1,0:T(8,128)S(1)}, u32[]{:S(2)}, u32[]{:S(2)}) %collective-permute-start.15) | collective-permute-done | bytes 163872 | tf_op jit(solution)/shard_map/ppermute | solution.py:396
  43.3 0.8 %combine.1 = bf16[64,512]{1,0:T(8,128)(2,1)} custom-call(f32[64,640]{1,0:T(8,128)S(1)} %get-tuple-element.41.refs_0_, f32[64,640]{1,0:T(8,128)S(1)} %collective-permute-done.15.refs_1_), custom_call_target="tpu_custom_call" | custom-call | bytes 393216 | tf_op jit(solution)/shard_map/combine/pallas_call | solution.py:62
  (29 shorter events, 2.6 us)
Async XLA Ops:
  0.0 2.4 %collective-permute-start.1 = (bf16[256,1024]{1,0:T(8,128)(2,1)}, bf16[256,1024]{1,0:T(8,128)(2,1)S(1)}, u32[]{:S(2)}, u32[]{:S(2)}) collective-permute-start(bf16[256,1024]{1,0:T(8,128)(2,1)} %refs_1_.1), channel_id=1, source_target_pairs={{0,4},{4,0},{1,5},{5,1},{2,6},{6,2},{3,7},{7,3},{8,12},{12,8},{9,1... | collective-permute-start | bytes 1572872 | tf_op jit(solution)/shard_map/ppermute | solution.py:335
  0.5 1.9 %collective-permute-start = (s32[1,256]{1,0:T(1,128)}, s32[1,256]{1,0:T(1,128)S(1)}, u32[]{:S(2)}, u32[]{:S(2)}) collective-permute-start(s32[1,256]{1,0:T(1,128)} %bitcast.1), channel_id=1, source_target_pairs={{0,4},{4,0},{1,5},{5,1},{2,6},{6,2},{3,7},{7,3},{8,12},{12,8},{9,1... | collective-permute-start | bytes 3080 | tf_op jit(solution)/shard_map/ppermute | solution.py:335
  0.5 2.4 %collective-permute-start.2 = (bf16[256,1024]{1,0:T(8,128)(2,1)}, bf16[256,1024]{1,0:T(8,128)(2,1)S(1)}, u32[]{:S(2)}, u32[]{:S(2)}) collective-permute-start(bf16[256,1024]{1,0:T(8,128)(2,1)} %refs_2_.1), channel_id=1, source_target_pairs={{0,4},{4,0},{1,5},{5,1},{2,6},{6,2},{3,7},{7,3},{8,12},{12,8},{9,1... | collective-permute-start | bytes 1572872 | tf_op jit(solution)/shard_map/ppermute | solution.py:335
  3.2 9.5 %collective-permute-start.3 = (bf16[256,256]{1,0:T(8,128)(2,1)S(1)}, bf16[256,256]{1,0:T(8,128)(2,1)S(1)}, u32[]{:S(2)}, u32[]{:S(2)}) collective-permute-start(bf16[256,256]{1,0:T(8,128)(2,1)S(1)} %mix.3.refs_0_), channel_id=1, source_target_pairs={{0,2},{2,3},{3,1},{1,0},{4,6},{6,7},{7,5},{5,4},{8,10},{10,11},{11... | collective-permute-start | bytes 393224 | tf_op jit(solution)/shard_map/ppermute | solution.py:379
  7.4 7.1 %collective-permute-start.6 = (bf16[256,256]{1,0:T(8,128)(2,1)S(1)}, bf16[256,256]{1,0:T(8,128)(2,1)S(1)}, u32[]{:S(2)}, u32[]{:S(2)}) collective-permute-start(bf16[256,256]{1,0:T(8,128)(2,1)S(1)} %mix.4.refs_1_), channel_id=1, source_target_pairs={{0,2},{2,3},{3,1},{1,0},{4,6},{6,7},{7,5},{5,4},{8,10},{10,11},{11... | collective-permute-start | bytes 393224 | tf_op jit(solution)/shard_map/ppermute | solution.py:379
  10.0 9.5 %collective-permute-start.9 = (bf16[256,512]{1,0:T(8,128)(2,1)S(1)}, bf16[256,512]{1,0:T(8,128)(2,1)S(1)}, u32[]{:S(2)}, u32[]{:S(2)}) collective-permute-start(bf16[256,512]{1,0:T(8,128)(2,1)S(1)} %mix.5.refs_2_), channel_id=1, source_target_pairs={{0,2},{2,3},{3,1},{1,0},{4,6},{6,7},{7,5},{5,4},{8,10},{10,11},{11... | collective-permute-start | bytes 786440 | tf_op jit(solution)/shard_map/ppermute | solution.py:379
  12.6 21.6 %collective-permute-start.12 = (bf16[4160,512]{1,0:T(8,128)(2,1)S(1)}, bf16[4160,512]{1,0:T(8,128)(2,1)S(1)}, u32[]{:S(2)}, u32[]{:S(2)}) collective-permute-start(bf16[4160,512]{1,0:T(8,128)(2,1)S(1)} %pack.1.refs_3_.refs_4_.refs_0_), channel_id=1, source_target_pairs={{0,4},{4,0},{1,5},{5,1},{2,6},{6,2},{3,7},{7,3},{8,12},{12,8},{9,1... | collective-permute-start | bytes 12779528 | tf_op jit(solution)/shard_map/ppermute | solution.py:335
  12.7 10.9 %collective-permute-start.4 = (bf16[256,256]{1,0:T(8,128)(2,1)S(1)}, bf16[256,256]{1,0:T(8,128)(2,1)S(1)}, u32[]{:S(2)}, u32[]{:S(2)}) collective-permute-start(bf16[256,256]{1,0:T(8,128)(2,1)S(1)} %split.7), channel_id=1, source_target_pairs={{0,2},{2,3},{3,1},{1,0},{4,6},{6,7},{7,5},{5,4},{8,10},{10,11},{11... | collective-permute-start | bytes 393224 | tf_op jit(solution)/shard_map/ppermute | solution.py:379
  14.5 11.2 %collective-permute-start.7 = (bf16[256,256]{1,0:T(8,128)(2,1)S(1)}, bf16[256,256]{1,0:T(8,128)(2,1)S(1)}, u32[]{:S(2)}, u32[]{:S(2)}) collective-permute-start(bf16[256,256]{1,0:T(8,128)(2,1)S(1)} %split.9), channel_id=1, source_target_pairs={{0,2},{2,3},{3,1},{1,0},{4,6},{6,7},{7,5},{5,4},{8,10},{10,11},{11... | collective-permute-start | bytes 393224 | tf_op jit(solution)/shard_map/ppermute | solution.py:379
  19.5 9.0 %collective-permute-start.10 = (bf16[256,256]{1,0:T(8,128)(2,1)S(1)}, bf16[256,256]{1,0:T(8,128)(2,1)S(1)}, u32[]{:S(2)}, u32[]{:S(2)}) collective-permute-start(bf16[256,256]{1,0:T(8,128)(2,1)S(1)} %get-tuple-element.33), channel_id=1, source_target_pairs={{0,2},{2,3},{3,1},{1,0},{4,6},{6,7},{7,5},{5,4},{8,10},{10,11},{11... | collective-permute-start | bytes 393224 | tf_op jit(solution)/shard_map/ppermute | solution.py:379
  23.0 8.4 %collective-permute-start.13 = (bf16[256,256]{1,0:T(8,128)(2,1)S(1)}, bf16[256,256]{1,0:T(8,128)(2,1)S(1)}, u32[]{:S(2)}, u32[]{:S(2)}) collective-permute-start(bf16[256,256]{1,0:T(8,128)(2,1)S(1)} %get-tuple-element.37), channel_id=1, source_target_pairs={{0,2},{2,3},{3,1},{1,0},{4,6},{6,7},{7,5},{5,4},{8,10},{10,11},{11... | collective-permute-start | bytes 393224 | tf_op jit(solution)/shard_map/ppermute | solution.py:379
  23.6 13.0 %collective-permute-start.5 = (bf16[256,256]{1,0:T(8,128)(2,1)S(1)}, bf16[256,256]{1,0:T(8,128)(2,1)S(1)}, u32[]{:S(2)}, u32[]{:S(2)}) collective-permute-start(bf16[256,256]{1,0:T(8,128)(2,1)S(1)} %split.8), channel_id=1, source_target_pairs={{0,2},{2,3},{3,1},{1,0},{4,6},{6,7},{7,5},{5,4},{8,10},{10,11},{11... | collective-permute-start | bytes 393224 | tf_op jit(solution)/shard_map/ppermute | solution.py:379
  25.8 10.9 %collective-permute-start.8 = (bf16[256,256]{1,0:T(8,128)(2,1)S(1)}, bf16[256,256]{1,0:T(8,128)(2,1)S(1)}, u32[]{:S(2)}, u32[]{:S(2)}) collective-permute-start(bf16[256,256]{1,0:T(8,128)(2,1)S(1)} %split.10), channel_id=1, source_target_pairs={{0,2},{2,3},{3,1},{1,0},{4,6},{6,7},{7,5},{5,4},{8,10},{10,11},{11... | collective-permute-start | bytes 393224 | tf_op jit(solution)/shard_map/ppermute | solution.py:379
  28.6 10.6 %collective-permute-start.11 = (bf16[256,256]{1,0:T(8,128)(2,1)S(1)}, bf16[256,256]{1,0:T(8,128)(2,1)S(1)}, u32[]{:S(2)}, u32[]{:S(2)}) collective-permute-start(bf16[256,256]{1,0:T(8,128)(2,1)S(1)} %split.12), channel_id=1, source_target_pairs={{0,2},{2,3},{3,1},{1,0},{4,6},{6,7},{7,5},{5,4},{8,10},{10,11},{11... | collective-permute-start | bytes 393224 | tf_op jit(solution)/shard_map/ppermute | solution.py:379
  31.4 9.8 %collective-permute-start.14 = (bf16[256,256]{1,0:T(8,128)(2,1)S(1)}, bf16[256,256]{1,0:T(8,128)(2,1)S(1)}, u32[]{:S(2)}, u32[]{:S(2)}) collective-permute-start(bf16[256,256]{1,0:T(8,128)(2,1)S(1)} %split.13), channel_id=1, source_target_pairs={{0,2},{2,3},{3,1},{1,0},{4,6},{6,7},{7,5},{5,4},{8,10},{10,11},{11... | collective-permute-start | bytes 393224 | tf_op jit(solution)/shard_map/ppermute | solution.py:379
  41.8 1.5 %collective-permute-start.15 = (f32[64,640]{1,0:T(8,128)S(1)}, f32[64,640]{1,0:T(8,128)S(1)}, u32[]{:S(2)}, u32[]{:S(2)}) collective-permute-start(f32[64,640]{1,0:T(8,128)S(1)} %get-tuple-element.42), channel_id=1, source_target_pairs={{4,0},{0,4},{5,1},{1,5},{6,2},{2,6},{7,3},{3,7},{12,8},{8,12},{13,... | collective-permute-start | bytes 491528 | tf_op jit(solution)/shard_map/ppermute | solution.py:396

commit v20 on v18

--- a/solution.py
+++ b/solution.py
@@ -340,7 +340,7 @@
         shards, near_targets = [pack(*whole, tgt_query)], bring(tgt_query)
     map_rows = (shards[0].shape[0] - tgt_rows) // 2
 
-    order = ring_order(n_head)
+    order = ring_order(n_head)[::-1]
     ring = [(order[i], order[(i + 1) % n_head]) for i in range(n_head)]
     before = {target: source for source, target in ring}
 

time: 44.2 us -> 45 us (1.018)
  waiting for transfers between devices: 7.51 us -> 16.1 us
  starting transfers between devices: 26.3 us -> 18.4 us
    ppermute x11, waiting for transfers between devices: 6.11 us -> 14.7 us  [on_device(): later = [lax.ppermute(p, 'head', ring) for p in pieces]]
    ppermute x11, starting transfers between devices: 25.2 us -> 17.3 us  [on_device(): later = [lax.ppermute(p, 'head', ring) for p in pieces]]
  transfers between devices with their start and end apart: 16 -> 16, of which waited for: 4 -> 9; matrix products, arithmetic and copies ran while one was open for 0% -> 0% of each run, Pallas kernels for 19% -> 19%
where the time goes in v20:
time: 45 us; the launch traced here: 44.8 us
  starting transfers between devices  18.4 us (41%)
  waiting for transfers between devices  16.1 us (36%)
  Pallas kernels  10.1 us (22%)
    ppermute x11, starting transfers between devices, on_device(): later = [lax.ppermute(p, 'head', ring) for p in pieces]  17.3 us
    ppermute x11, waiting for transfers between devices, on_device(): later = [lax.ppermute(p, 'head', ring) for p in pieces]  14.7 us
    pallas_call x21, Pallas kernels, call(): pl.pallas_call(kernel, in_specs=specs or [VMEM] * len(operands), out_spec...  10.1 us
    ppermute x1, waiting for transfers between devices, on_device(): lax.ppermute(piece, 'ctx', [(target, source) for source, target in pairs])  1.38 us
    ppermute x4, starting transfers between devices, on_device(): bring = lambda x: [lax.ppermute(x, 'ctx', pairs) for pairs in links]  1.03 us
  transfers between devices with their start and end apart: 16, of which 9 were waited for; matrix products, arithmetic and copies ran while one was open for 0% of the time, Pallas kernels for 19%

profile of v20, /device:TPU:0, one launch (start us, length us, event | category | flops | bytes accessed | tf_op | source)
XLA Modules:
  0.0 44.8 jit_solution(14661907551171186549)
XLA Ops:
  1.0 1.4 %fetch.1 = (bf16[256,1024]{1,0:T(8,128)(2,1)S(1)}, bf16[256,1024]{1,0:T(8,128)(2,1)S(1)}, bf16[256,1024]{1,0:T(8,128)(2,1)S(1)}, s32[1,256]{1,0:T(1,128)S(1)}) custom-call(bf16[256,1024]{1,0:T(8,128)(2,1)} %refs_0_.1, bf16[256,1024]{1,0:T(8,128)(2,1)} %refs_1_.1, bf16[256,1024]{1,0:T(8,128)(2,1)} %refs_2_.1, s32[1,256]{1,0:T(1,128)} %bitcast.2), custom_call_target="tpu_custom_call" | custom-call | bytes 3147776 | tf_op jit(solution)/shard_map/fetch/pallas_call | solution.py:62
  3.2 3.0 %collective-permute-start.3 = (bf16[256,256]{1,0:T(8,128)(2,1)S(1)}, bf16[256,256]{1,0:T(8,128)(2,1)S(1)}, u32[]{:S(2)}, u32[]{:S(2)}) collective-permute-start(bf16[256,256]{1,0:T(8,128)(2,1)S(1)} %mix.3.refs_0_), channel_id=1, source_target_pairs={{1,3},{3,2},{2,0},{0,1},{5,7},{7,6},{6,4},{4,5},{9,11},{11,10},{10... | collective-permute-start | bytes 393224 | tf_op jit(solution)/shard_map/ppermute | solution.py:363
  6.4 2.6 %collective-permute-start.6 = (bf16[256,256]{1,0:T(8,128)(2,1)S(1)}, bf16[256,256]{1,0:T(8,128)(2,1)S(1)}, u32[]{:S(2)}, u32[]{:S(2)}) collective-permute-start(bf16[256,256]{1,0:T(8,128)(2,1)S(1)} %mix.4.refs_1_), channel_id=1, source_target_pairs={{1,3},{3,2},{2,0},{0,1},{5,7},{7,6},{6,4},{4,5},{9,11},{11,10},{10... | collective-permute-start | bytes 393224 | tf_op jit(solution)/shard_map/ppermute | solution.py:363
  10.5 2.2 %pack.1.refs_3_.refs_4_.refs_0_ = bf16[4160,512]{1,0:T(8,128)(2,1)S(1)} custom-call(bf16[2048,512]{1,0:T(8,128)(2,1)} %refs_0_.2, bf16[2048,512]{1,0:T(8,128)(2,1)} %refs_1_.2, bf16[64,512]{1,0:T(8,128)(2,1)} %refs_2_.2), custom_call_target="tpu_custom_call" | custom-call | bytes 8519680 | tf_op jit(solution)/shard_map/pack/pallas_call | solution.py:62
  12.9 1.4 %collective-permute-done.6.source.refs_1_ = bf16[256,256]{1,0:T(8,128)(2,1)S(1)} collective-permute-done((bf16[256,256]{1,0:T(8,128)(2,1)S(1)}, bf16[256,256]{1,0:T(8,128)(2,1)S(1)}, u32[]{:S(2)}, u32[]{:S(2)}) %collective-permute-start.6) | collective-permute-done | bytes 131104 | tf_op jit(solution)/shard_map/ppermute | solution.py:363
  14.3 1.8 %collective-permute-start.7 = (bf16[256,256]{1,0:T(8,128)(2,1)S(1)}, bf16[256,256]{1,0:T(8,128)(2,1)S(1)}, u32[]{:S(2)}, u32[]{:S(2)}) collective-permute-start(bf16[256,256]{1,0:T(8,128)(2,1)S(1)} %split.9), channel_id=1, source_target_pairs={{1,3},{3,2},{2,0},{0,1},{5,7},{7,6},{6,4},{4,5},{9,11},{11,10},{10... | collective-permute-start | bytes 393224 | tf_op jit(solution)/shard_map/ppermute | solution.py:363
  16.2 4.0 %collective-permute-done.9.source.refs_2_ = bf16[256,512]{1,0:T(8,128)(2,1)S(1)} collective-permute-done((bf16[256,512]{1,0:T(8,128)(2,1)S(1)}, bf16[256,512]{1,0:T(8,128)(2,1)S(1)}, u32[]{:S(2)}, u32[]{:S(2)}) %collective-permute-start.9) | collective-permute-done | bytes 262176 | tf_op jit(solution)/shard_map/ppermute | solution.py:363
  20.2 1.0 %collective-permute-start.10 = (bf16[256,256]{1,0:T(8,128)(2,1)S(1)}, bf16[256,256]{1,0:T(8,128)(2,1)S(1)}, u32[]{:S(2)}, u32[]{:S(2)}) collective-permute-start(bf16[256,256]{1,0:T(8,128)(2,1)S(1)} %get-tuple-element.33), channel_id=1, source_target_pairs={{1,3},{3,2},{2,0},{0,1},{5,7},{7,6},{6,4},{4,5},{9,11},{11,10},{10... | collective-permute-start | bytes 393224 | tf_op jit(solution)/shard_map/ppermute | solution.py:363
  21.2 3.4 %collective-permute-start.13 = (bf16[256,256]{1,0:T(8,128)(2,1)S(1)}, bf16[256,256]{1,0:T(8,128)(2,1)S(1)}, u32[]{:S(2)}, u32[]{:S(2)}) collective-permute-start(bf16[256,256]{1,0:T(8,128)(2,1)S(1)} %get-tuple-element.37), channel_id=1, source_target_pairs={{1,3},{3,2},{2,0},{0,1},{5,7},{7,6},{6,4},{4,5},{9,11},{11,10},{10... | collective-permute-start | bytes 393224 | tf_op jit(solution)/shard_map/ppermute | solution.py:363
  24.7 1.1 %collective-permute-done.7.source.refs_1_ = bf16[256,256]{1,0:T(8,128)(2,1)S(1)} collective-permute-done((bf16[256,256]{1,0:T(8,128)(2,1)S(1)}, bf16[256,256]{1,0:T(8,128)(2,1)S(1)}, u32[]{:S(2)}, u32[]{:S(2)}) %collective-permute-start.7) | collective-permute-done | bytes 131104 | tf_op jit(solution)/shard_map/ppermute | solution.py:363
  25.8 1.6 %collective-permute-start.8 = (bf16[256,256]{1,0:T(8,128)(2,1)S(1)}, bf16[256,256]{1,0:T(8,128)(2,1)S(1)}, u32[]{:S(2)}, u32[]{:S(2)}) collective-permute-start(bf16[256,256]{1,0:T(8,128)(2,1)S(1)} %split.10), channel_id=1, source_target_pairs={{1,3},{3,2},{2,0},{0,1},{5,7},{7,6},{6,4},{4,5},{9,11},{11,10},{10... | collective-permute-start | bytes 393224 | tf_op jit(solution)/shard_map/ppermute | solution.py:363
  27.4 1.2 %collective-permute-done.10.source.refs_2_ = bf16[256,256]{1,0:T(8,128)(2,1)S(1)} collective-permute-done((bf16[256,256]{1,0:T(8,128)(2,1)S(1)}, bf16[256,256]{1,0:T(8,128)(2,1)S(1)}, u32[]{:S(2)}, u32[]{:S(2)}) %collective-permute-start.10) | collective-permute-done | bytes 131104 | tf_op jit(solution)/shard_map/ppermute | solution.py:363
  28.6 1.6 %collective-permute-start.11 = (bf16[256,256]{1,0:T(8,128)(2,1)S(1)}, bf16[256,256]{1,0:T(8,128)(2,1)S(1)}, u32[]{:S(2)}, u32[]{:S(2)}) collective-permute-start(bf16[256,256]{1,0:T(8,128)(2,1)S(1)} %split.12), channel_id=1, source_target_pairs={{1,3},{3,2},{2,0},{0,1},{5,7},{7,6},{6,4},{4,5},{9,11},{11,10},{10... | collective-permute-start | bytes 393224 | tf_op jit(solution)/shard_map/ppermute | solution.py:363
  30.2 1.2 %collective-permute-done.13.refs_3_.source = bf16[256,256]{1,0:T(8,128)(2,1)S(1)} collective-permute-done((bf16[256,256]{1,0:T(8,128)(2,1)S(1)}, bf16[256,256]{1,0:T(8,128)(2,1)S(1)}, u32[]{:S(2)}, u32[]{:S(2)}) %collective-permute-start.13) | collective-permute-done | bytes 131104 | tf_op jit(solution)/shard_map/ppermute | solution.py:363
  31.4 1.6 %collective-permute-start.14 = (bf16[256,256]{1,0:T(8,128)(2,1)S(1)}, bf16[256,256]{1,0:T(8,128)(2,1)S(1)}, u32[]{:S(2)}, u32[]{:S(2)}) collective-permute-start(bf16[256,256]{1,0:T(8,128)(2,1)S(1)} %split.13), channel_id=1, source_target_pairs={{1,3},{3,2},{2,0},{0,1},{5,7},{7,6},{6,4},{4,5},{9,11},{11,10},{10... | collective-permute-start | bytes 393224 | tf_op jit(solution)/shard_map/ppermute | solution.py:363
  33.2 0.7 %project.4.refs_5_ = f32[256,1024]{1,0:T(8,128)S(1)} custom-call(bf16[256,256]{1,0:T(8,128)(2,1)S(1)} %mix.3.refs_0_, bf16[256,256]{1,0:T(8,128)(2,1)S(1)} %mix.4.refs_1_, bf16[256,512]{1,0:T(8,128)(2,1)S(1)} %mix.5.refs_2_, bf16[4160,512]{1,0:T(8,128)(2,1)S(1)} %pack.1.refs_3_.refs_4_.refs_0_, ...), custom_call_target="tpu_custom_call" | custom-call | flops 536870912 | bytes 10092544 | tf_op jit(solution)/shard_map/project/pallas_call | solution.py:62
  34.0 0.7 %project.5.refs_6_ = f32[256,1024]{1,0:T(8,128)S(1)} custom-call(bf16[256,256]{1,0:T(8,128)(2,1)S(1)} %collective-permute-done.3.source.refs_0_, bf16[256,256]{1,0:T(8,128)(2,1)S(1)} %collective-permute-done.6.source.refs_1_, bf16[256,512]{1,0:T(8,128)(2,1)S(1)} %collective-permute-done.9.source.refs_2_, bf16[4160,512]{1,0:T(8,128)(2,1)S(1)} %pack.1.refs_3_.refs_4_.refs_0_, ...), custom_call_target="tpu_custom_call" | custom-call | flops 536870912 | bytes 11141120 | tf_op jit(solution)/shard_map/project/pallas_call | solution.py:62
  34.7 0.7 %project.6.refs_5_ = f32[256,1024]{1,0:T(8,128)S(1)} custom-call(bf16[256,256]{1,0:T(8,128)(2,1)S(1)} %collective-permute-done.4.source.refs_0_, bf16[256,256]{1,0:T(8,128)(2,1)S(1)} %collective-permute-done.7.source.refs_1_, bf16[256,256]{1,0:T(8,128)(2,1)S(1)} %collective-permute-done.10.source.refs_2_, ...), custom_call_target="tpu_custom_call" | custom-call | flops 536870912 | bytes 11141120 | tf_op jit(solution)/shard_map/project/pallas_call | solution.py:62
  35.5 1.5 %collective-permute-done.8.refs_1_ = bf16[256,256]{1,0:T(8,128)(2,1)S(1)} collective-permute-done((bf16[256,256]{1,0:T(8,128)(2,1)S(1)}, bf16[256,256]{1,0:T(8,128)(2,1)S(1)}, u32[]{:S(2)}, u32[]{:S(2)}) %collective-permute-start.8) | collective-permute-done | bytes 131104 | tf_op jit(solution)/shard_map/ppermute | solution.py:363
  37.0 2.8 %collective-permute-done.11.refs_2_ = bf16[256,256]{1,0:T(8,128)(2,1)S(1)} collective-permute-done((bf16[256,256]{1,0:T(8,128)(2,1)S(1)}, bf16[256,256]{1,0:T(8,128)(2,1)S(1)}, u32[]{:S(2)}, u32[]{:S(2)}) %collective-permute-start.11) | collective-permute-done | bytes 131104 | tf_op jit(solution)/shard_map/ppermute | solution.py:363
  40.4 1.5 %collective-permute-done.14.e_ref = bf16[256,256]{1,0:T(8,128)(2,1)S(1)} collective-permute-done((bf16[256,256]{1,0:T(8,128)(2,1)S(1)}, bf16[256,256]{1,0:T(8,128)(2,1)S(1)}, u32[]{:S(2)}, u32[]{:S(2)}) %collective-permute-start.14) | collective-permute-done | bytes 131104 | tf_op jit(solution)/shard_map/ppermute | solution.py:363
  41.9 0.6 %cross_attend.1 = (f32[64,640]{1,0:T(8,128)S(1)}, f32[64,640]{1,0:T(8,128)S(1)}) custom-call(f32[256,1024]{1,0:T(8,128)S(1)} %project.7.acc_ref, bf16[256,256]{1,0:T(8,128)(2,1)S(1)} %collective-permute-done.14.e_ref, bf16[256,1024]{1,0:T(8,128)(2,1)S(1)} %get-tuple-element.38.map_ref, bf16[128,512]{1,0:T(8,128)(2,1)S(1)} %get-tuple-element.39.tgt_ref, ...), custom_call_target="tpu_custom_call" | custom-call | flops 134217728 | bytes 2293760 | tf_op jit(solution)/shard_map/cross_attend/pallas_call | solution.py:62
  42.6 1.4 %collective-permute-done.15.refs_1_ = f32[64,640]{1,0:T(8,128)S(1)} collective-permute-done((f32[64,640]{1,0:T(8,128)S(1)}, f32[64,640]{1,0:T(8,128)S(1)}, u32[]{:S(2)}, u32[]{:S(2)}) %collective-permute-start.15) | collective-permute-done | bytes 163872 | tf_op jit(solution)/shard_map/ppermute | solution.py:380
  44.0 0.8 %combine.1 = bf16[64,512]{1,0:T(8,128)(2,1)} custom-call(f32[64,640]{1,0:T(8,128)S(1)} %get-tuple-element.41.refs_0_, f32[64,640]{1,0:T(8,128)S(1)} %collective-permute-done.15.refs_1_), custom_call_target="tpu_custom_call" | custom-call | bytes 393216 | tf_op jit(solution)/shard_map/combine/pallas_call | solution.py:62
  (29 shorter events, 4.6 us)
Async XLA Ops:
  0.0 2.4 %collective-permute-start.1 = (bf16[256,1024]{1,0:T(8,128)(2,1)}, bf16[256,1024]{1,0:T(8,128)(2,1)S(1)}, u32[]{:S(2)}, u32[]{:S(2)}) collective-permute-start(bf16[256,1024]{1,0:T(8,128)(2,1)} %refs_1_.1), channel_id=1, source_target_pairs={{0,4},{4,0},{1,5},{5,1},{2,6},{6,2},{3,7},{7,3},{8,12},{12,8},{9,1... | collective-permute-start | bytes 1572872 | tf_op jit(solution)/shard_map/ppermute | solution.py:319
  0.5 1.9 %collective-permute-start = (s32[1,256]{1,0:T(1,128)}, s32[1,256]{1,0:T(1,128)S(1)}, u32[]{:S(2)}, u32[]{:S(2)}) collective-permute-start(s32[1,256]{1,0:T(1,128)} %bitcast.1), channel_id=1, source_target_pairs={{0,4},{4,0},{1,5},{5,1},{2,6},{6,2},{3,7},{7,3},{8,12},{12,8},{9,1... | collective-permute-start | bytes 3080 | tf_op jit(solution)/shard_map/ppermute | solution.py:319
  0.5 2.4 %collective-permute-start.2 = (bf16[256,1024]{1,0:T(8,128)(2,1)}, bf16[256,1024]{1,0:T(8,128)(2,1)S(1)}, u32[]{:S(2)}, u32[]{:S(2)}) collective-permute-start(bf16[256,1024]{1,0:T(8,128)(2,1)} %refs_2_.1), channel_id=1, source_target_pairs={{0,4},{4,0},{1,5},{5,1},{2,6},{6,2},{3,7},{7,3},{8,12},{12,8},{9,1... | collective-permute-start | bytes 1572872 | tf_op jit(solution)/shard_map/ppermute | solution.py:319
  3.2 9.6 %collective-permute-start.3 = (bf16[256,256]{1,0:T(8,128)(2,1)S(1)}, bf16[256,256]{1,0:T(8,128)(2,1)S(1)}, u32[]{:S(2)}, u32[]{:S(2)}) collective-permute-start(bf16[256,256]{1,0:T(8,128)(2,1)S(1)} %mix.3.refs_0_), channel_id=1, source_target_pairs={{1,3},{3,2},{2,0},{0,1},{5,7},{7,6},{6,4},{4,5},{9,11},{11,10},{10... | collective-permute-start | bytes 393224 | tf_op jit(solution)/shard_map/ppermute | solution.py:363
  6.4 7.9 %collective-permute-start.6 = (bf16[256,256]{1,0:T(8,128)(2,1)S(1)}, bf16[256,256]{1,0:T(8,128)(2,1)S(1)}, u32[]{:S(2)}, u32[]{:S(2)}) collective-permute-start(bf16[256,256]{1,0:T(8,128)(2,1)S(1)} %mix.4.refs_1_), channel_id=1, source_target_pairs={{1,3},{3,2},{2,0},{0,1},{5,7},{7,6},{6,4},{4,5},{9,11},{11,10},{10... | collective-permute-start | bytes 393224 | tf_op jit(solution)/shard_map/ppermute | solution.py:363
  10.0 10.2 %collective-permute-start.9 = (bf16[256,512]{1,0:T(8,128)(2,1)S(1)}, bf16[256,512]{1,0:T(8,128)(2,1)S(1)}, u32[]{:S(2)}, u32[]{:S(2)}) collective-permute-start(bf16[256,512]{1,0:T(8,128)(2,1)S(1)} %mix.5.refs_2_), channel_id=1, source_target_pairs={{1,3},{3,2},{2,0},{0,1},{5,7},{7,6},{6,4},{4,5},{9,11},{11,10},{10... | collective-permute-start | bytes 786440 | tf_op jit(solution)/shard_map/ppermute | solution.py:363
  12.7 20.3 %collective-permute-start.12 = (bf16[4160,512]{1,0:T(8,128)(2,1)S(1)}, bf16[4160,512]{1,0:T(8,128)(2,1)S(1)}, u32[]{:S(2)}, u32[]{:S(2)}) collective-permute-start(bf16[4160,512]{1,0:T(8,128)(2,1)S(1)} %pack.1.refs_3_.refs_4_.refs_0_), channel_id=1, source_target_pairs={{0,4},{4,0},{1,5},{5,1},{2,6},{6,2},{3,7},{7,3},{8,12},{12,8},{9,1... | collective-permute-start | bytes 12779528 | tf_op jit(solution)/shard_map/ppermute | solution.py:319
  12.8 11.7 %collective-permute-start.4 = (bf16[256,256]{1,0:T(8,128)(2,1)S(1)}, bf16[256,256]{1,0:T(8,128)(2,1)S(1)}, u32[]{:S(2)}, u32[]{:S(2)}) collective-permute-start(bf16[256,256]{1,0:T(8,128)(2,1)S(1)} %split.7), channel_id=1, source_target_pairs={{1,3},{3,2},{2,0},{0,1},{5,7},{7,6},{6,4},{4,5},{9,11},{11,10},{10... | collective-permute-start | bytes 393224 | tf_op jit(solution)/shard_map/ppermute | solution.py:363
  14.3 11.5 %collective-permute-start.7 = (bf16[256,256]{1,0:T(8,128)(2,1)S(1)}, bf16[256,256]{1,0:T(8,128)(2,1)S(1)}, u32[]{:S(2)}, u32[]{:S(2)}) collective-permute-start(bf16[256,256]{1,0:T(8,128)(2,1)S(1)} %split.9), channel_id=1, source_target_pairs={{1,3},{3,2},{2,0},{0,1},{5,7},{7,6},{6,4},{4,5},{9,11},{11,10},{10... | collective-permute-start | bytes 393224 | tf_op jit(solution)/shard_map/ppermute | solution.py:363
  20.2 8.4 %collective-permute-start.10 = (bf16[256,256]{1,0:T(8,128)(2,1)S(1)}, bf16[256,256]{1,0:T(8,128)(2,1)S(1)}, u32[]{:S(2)}, u32[]{:S(2)}) collective-permute-start(bf16[256,256]{1,0:T(8,128)(2,1)S(1)} %get-tuple-element.33), channel_id=1, source_target_pairs={{1,3},{3,2},{2,0},{0,1},{5,7},{7,6},{6,4},{4,5},{9,11},{11,10},{10... | collective-permute-start | bytes 393224 | tf_op jit(solution)/shard_map/ppermute | solution.py:363
  21.2 10.2 %collective-permute-start.13 = (bf16[256,256]{1,0:T(8,128)(2,1)S(1)}, bf16[256,256]{1,0:T(8,128)(2,1)S(1)}, u32[]{:S(2)}, u32[]{:S(2)}) collective-permute-start(bf16[256,256]{1,0:T(8,128)(2,1)S(1)} %get-tuple-element.37), channel_id=1, source_target_pairs={{1,3},{3,2},{2,0},{0,1},{5,7},{7,6},{6,4},{4,5},{9,11},{11,10},{10... | collective-permute-start | bytes 393224 | tf_op jit(solution)/shard_map/ppermute | solution.py:363
  24.5 10.9 %collective-permute-start.5 = (bf16[256,256]{1,0:T(8,128)(2,1)S(1)}, bf16[256,256]{1,0:T(8,128)(2,1)S(1)}, u32[]{:S(2)}, u32[]{:S(2)}) collective-permute-start(bf16[256,256]{1,0:T(8,128)(2,1)S(1)} %split.8), channel_id=1, source_target_pairs={{1,3},{3,2},{2,0},{0,1},{5,7},{7,6},{6,4},{4,5},{9,11},{11,10},{10... | collective-permute-start | bytes 393224 | tf_op jit(solution)/shard_map/ppermute | solution.py:363
  25.8 11.2 %collective-permute-start.8 = (bf16[256,256]{1,0:T(8,128)(2,1)S(1)}, bf16[256,256]{1,0:T(8,128)(2,1)S(1)}, u32[]{:S(2)}, u32[]{:S(2)}) collective-permute-start(bf16[256,256]{1,0:T(8,128)(2,1)S(1)} %split.10), channel_id=1, source_target_pairs={{1,3},{3,2},{2,0},{0,1},{5,7},{7,6},{6,4},{4,5},{9,11},{11,10},{10... | collective-permute-start | bytes 393224 | tf_op jit(solution)/shard_map/ppermute | solution.py:363
  28.6 11.2 %collective-permute-start.11 = (bf16[256,256]{1,0:T(8,128)(2,1)S(1)}, bf16[256,256]{1,0:T(8,128)(2,1)S(1)}, u32[]{:S(2)}, u32[]{:S(2)}) collective-permute-start(bf16[256,256]{1,0:T(8,128)(2,1)S(1)} %split.12), channel_id=1, source_target_pairs={{1,3},{3,2},{2,0},{0,1},{5,7},{7,6},{6,4},{4,5},{9,11},{11,10},{10... | collective-permute-start | bytes 393224 | tf_op jit(solution)/shard_map/ppermute | solution.py:363
  31.4 10.5 %collective-permute-start.14 = (bf16[256,256]{1,0:T(8,128)(2,1)S(1)}, bf16[256,256]{1,0:T(8,128)(2,1)S(1)}, u32[]{:S(2)}, u32[]{:S(2)}) collective-permute-start(bf16[256,256]{1,0:T(8,128)(2,1)S(1)} %split.13), channel_id=1, source_target_pairs={{1,3},{3,2},{2,0},{0,1},{5,7},{7,6},{6,4},{4,5},{9,11},{11,10},{10... | collective-permute-start | bytes 393224 | tf_op jit(solution)/shard_map/ppermute | solution.py:363
  42.5 1.5 %collective-permute-start.15 = (f32[64,640]{1,0:T(8,128)S(1)}, f32[64,640]{1,0:T(8,128)S(1)}, u32[]{:S(2)}, u32[]{:S(2)}) collective-permute-start(f32[64,640]{1,0:T(8,128)S(1)} %get-tuple-element.42), channel_id=1, source_target_pairs={{4,0},{0,4},{5,1},{1,5},{6,2},{2,6},{7,3},{3,7},{12,8},{8,12},{13,... | collective-permute-start | bytes 491528 | tf_op jit(solution)/shard_map/ppermute | solution.py:380

commit v21 on v18

--- a/solution.py
+++ b/solution.py
@@ -193,28 +193,37 @@
     return call(split_kernel, "split", [((rows, width // parts), chunk.dtype)] * parts, [chunk], flops=SPLIT_FLOPS)
 
 
-def project_kernel(chunks, shards, map_rows, has_acc, place, *refs):
-    e_refs, maps, out_ref = refs[:chunks], refs[chunks : chunks + shards], refs[-1]
+def project_kernel(sizes, shards, map_rows, has_acc, places, *refs):
+    count, out_ref = sum(sizes), refs[-1]
+    maps = refs[count : count + shards]
     half = out_ref.shape[1] // 2
-    depth = e_refs[0].shape[1]
-    shard, row = place()
-    row = pl.multiple_of(row, depth)
-    chunk = jnp.concatenate([r[...] for r in e_refs], axis=1)
-
-    def add(map_ref):
-        for side in range(2):
-            columns = slice(side * half, (side + 1) * half)
-            product = dot(chunk, map_ref[pl.ds(side * map_rows + row, chunk.shape[1]), :])
-            out_ref[:, columns] = refs[-2][:, columns] + product if has_acc else product
-
-    in_shard(maps, shard, add)
-
-
-def project(acc, chunks, place, shards, map_rows):
+    before = refs[-2] if has_acc else None
+    start = 0
+    for size, place in zip(sizes, places):
+        e_refs = refs[start : start + size]
+        start += size
+        shard, row = place()
+        row = pl.multiple_of(row, e_refs[0].shape[1])
+        chunk = jnp.concatenate([r[...] for r in e_refs], axis=1)
+
+        def add(map_ref, chunk=chunk, row=row, before=before):
+            for side in range(2):
+                columns = slice(side * half, (side + 1) * half)
+                product = dot(chunk, map_ref[pl.ds(side * map_rows + row, chunk.shape[1]), :])
+                out_ref[:, columns] = product if before is None else before[:, columns] + product
+
+        in_shard(maps, shard, add)
+        before = out_ref
+
+
+def project(acc, groups, shards, map_rows):
+    chunks = [x for group, _ in groups for x in group]
     rows, width = chunks[0].shape[0], shards[0].shape[1]
     operands = [*chunks, *shards] + ([] if acc is None else [acc])
-    return call(
-        functools.partial(project_kernel, len(chunks), len(shards), map_rows, acc is not None, place),
+    sizes = [len(group) for group, _ in groups]
+    places = [place for _, place in groups]
+    return call(
+        functools.partial(project_kernel, sizes, len(shards), map_rows, acc is not None, places),
         "project",
         [((rows, 2 * width), F32)],
         operands,
@@ -341,11 +350,11 @@
     map_rows = (shards[0].shape[0] - tgt_rows) // 2
 
     order = ring_order(n_head)
-    ring = [(order[i], order[(i + 1) % n_head]) for i in range(n_head)]
-    before = {target: source for source, target in ring}
-
-    def place(turn, first):
+    rings = [[(o[i], o[(i + 1) % n_head]) for i in range(n_head)] for o in (order, order[::-1])]
+
+    def place(way, turn, first):
         head, ctx = lax.axis_index("head"), lax.axis_index("ctx")
+        before = {target: source for source, target in rings[way]}
         owner = 0
         for i in range(n_head):
             source = i
@@ -357,16 +366,26 @@
             return None, row
         return jnp.where(lax.div(row, map_rows) == ctx, 0, 1), lax.rem(row, map_rows)
 
+    def grouped(turn, pieces):
+        first = heads * HEAD_DIM
+        at = [0 if p < first else 1 for p in offsets(pieces)]
+        groups = [[x for x, w in zip(pieces, at) if w == way] for way in range(2)]
+        return [(g, functools.partial(place, way, turn, way * first)) for way, g in enumerate(groups) if g]
+
+    def offsets(pieces):
+        return [sum(x.shape[1] for x in pieces[:i]) for i in range(len(pieces))]
+
     acc, last = None, n_head - 1
     for turn in range(last):
         pieces = [p for h in held for p in split(h, h.shape[1] // HEAD_DIM)] if turn else held
-        later = [lax.ppermute(p, "head", ring) for p in pieces]
-        acc = project(acc, held, functools.partial(place, turn, 0), shards, map_rows)
+        ways = [0 if p < heads * HEAD_DIM else 1 for p in offsets(pieces)]
+        later = [lax.ppermute(p, "head", rings[way]) for p, way in zip(pieces, ways)]
+        acc = project(acc, grouped(turn, held), shards, map_rows)
         held = later
-    acc = project(acc, held[:-1], functools.partial(place, last, 0), shards, map_rows)
+    acc = project(acc, grouped(last, held[:-1]), shards, map_rows)
     depth = held[-1].shape[1]
     last_maps, targets, mask = prepare(
-        functools.partial(place, last, features - depth),
+        functools.partial(place, 1, last, features - depth),
         depth,
         shards,
         map_rows,

time: 44.2 us -> 46.1 us (1.043)
  waiting for transfers between devices: 7.51 us -> 15.9 us
  starting transfers between devices: 26.3 us -> 19.1 us
  Pallas kernels: 10.1 us -> 10.8 us
    ppermute x11, waiting for transfers between devices: 6.11 us -> 14.5 us  [on_device(): lax.ppermute(p, 'head', rings[way])]
    ppermute x11, starting transfers between devices: 25.2 us -> 18 us  [on_device(): lax.ppermute(p, 'head', rings[way])]
    pallas_call x21, Pallas kernels: 10.1 us -> 10.8 us  [call(): pl.pallas_call(kernel, in_specs=specs or [VMEM] * len(operands), out_spec...]
  transfers between devices with their start and end apart: 16 -> 16, of which waited for: 4 -> 7; matrix products, arithmetic and copies ran while one was open for 0% -> 0% of each run, Pallas kernels for 19% -> 20%
where the time goes in v21:
time: 46.1 us; the launch traced here: 46 us
  starting transfers between devices  19.1 us (41%)
  waiting for transfers between devices  15.9 us (34%)
  Pallas kernels  10.8 us (23%)
    ppermute x11, starting transfers between devices, on_device(): lax.ppermute(p, 'head', rings[way])  18 us
    ppermute x11, waiting for transfers between devices, on_device(): lax.ppermute(p, 'head', rings[way])  14.5 us
    pallas_call x21, Pallas kernels, call(): pl.pallas_call(kernel, in_specs=specs or [VMEM] * len(operands), out_spec...  10.8 us
    ppermute x1, waiting for transfers between devices, on_device(): lax.ppermute(piece, 'ctx', [(target, source) for source, target in pairs])  1.38 us
    ppermute x4, starting transfers between devices, on_device(): bring = lambda x: [lax.ppermute(x, 'ctx', pairs) for pairs in links]  1.03 us
  transfers between devices with their start and end apart: 16, of which 7 were waited for; matrix products, arithmetic and copies ran while one was open for 0% of the time, Pallas kernels for 20%

profile of v21, /device:TPU:0, one launch (start us, length us, event | category | flops | bytes accessed | tf_op | source)
XLA Modules:
  0.0 46.0 jit_solution(12928924754668472629)
XLA Ops:
  1.0 1.4 %fetch.1 = (bf16[256,1024]{1,0:T(8,128)(2,1)S(1)}, bf16[256,1024]{1,0:T(8,128)(2,1)S(1)}, bf16[256,1024]{1,0:T(8,128)(2,1)S(1)}, s32[1,256]{1,0:T(1,128)S(1)}) custom-call(bf16[256,1024]{1,0:T(8,128)(2,1)} %refs_0_.1, bf16[256,1024]{1,0:T(8,128)(2,1)} %refs_1_.1, bf16[256,1024]{1,0:T(8,128)(2,1)} %refs_2_.1, s32[1,256]{1,0:T(1,128)} %bitcast.2), custom_call_target="tpu_custom_call" | custom-call | bytes 3147776 | tf_op jit(solution)/shard_map/fetch/pallas_call | solution.py:62
  2.4 0.6 %weigh.2 = (bf16[256,1024]{1,0:T(8,128)(2,1)S(1)}, f32[256,128]{1,0:T(8,128)S(1)}) custom-call(s32[1,256]{1,0:T(1,128)S(1)} %get-tuple-element.24.refs_0_.refs_2_, s32[1,256]{1,0:T(1,128)S(1)} %collective-permute-done.refs_1_.refs_3_, bf16[256,1024]{1,0:T(8,128)(2,1)S(1)} %get-tuple-element.25.refs_2_, bf16[256,1024]{1,0:T(8,128)(2,1)S(1)} %get-tuple-element.26.refs_3_, ...), custom_call_target="tpu_custom_call" | custom-call | flops 6000000000 | bytes 2230272 | tf_op jit(solution)/shard_map/weigh/pallas_call | solution.py:62
  3.2 4.0 %collective-permute-start.3 = (bf16[256,256]{1,0:T(8,128)(2,1)S(1)}, bf16[256,256]{1,0:T(8,128)(2,1)S(1)}, u32[]{:S(2)}, u32[]{:S(2)}) collective-permute-start(bf16[256,256]{1,0:T(8,128)(2,1)S(1)} %mix.3.refs_0_), channel_id=1, source_target_pairs={{0,2},{2,3},{3,1},{1,0},{4,6},{6,7},{7,5},{5,4},{8,10},{10,11},{11... | collective-permute-start | bytes 393224 | tf_op jit(solution)/shard_map/ppermute | solution.py:382
  7.4 1.6 %collective-permute-start.6 = (bf16[256,256]{1,0:T(8,128)(2,1)S(1)}, bf16[256,256]{1,0:T(8,128)(2,1)S(1)}, u32[]{:S(2)}, u32[]{:S(2)}) collective-permute-start(bf16[256,256]{1,0:T(8,128)(2,1)S(1)} %mix.4.refs_1_), channel_id=1, source_target_pairs={{0,2},{2,3},{3,1},{1,0},{4,6},{6,7},{7,5},{5,4},{8,10},{10,11},{11... | collective-permute-start | bytes 393224 | tf_op jit(solution)/shard_map/ppermute | solution.py:382
  10.5 2.2 %pack.1.refs_3_.refs_4_.refs_0_ = bf16[4160,512]{1,0:T(8,128)(2,1)S(1)} custom-call(bf16[2048,512]{1,0:T(8,128)(2,1)} %refs_0_.2, bf16[2048,512]{1,0:T(8,128)(2,1)} %refs_1_.2, bf16[64,512]{1,0:T(8,128)(2,1)} %refs_2_.2), custom_call_target="tpu_custom_call" | custom-call | bytes 8519680 | tf_op jit(solution)/shard_map/pack/pallas_call | solution.py:62
  12.8 2.5 %collective-permute-start.4 = (bf16[256,256]{1,0:T(8,128)(2,1)S(1)}, bf16[256,256]{1,0:T(8,128)(2,1)S(1)}, u32[]{:S(2)}, u32[]{:S(2)}) collective-permute-start(bf16[256,256]{1,0:T(8,128)(2,1)S(1)} %split.7), channel_id=1, source_target_pairs={{0,2},{2,3},{3,1},{1,0},{4,6},{6,7},{7,5},{5,4},{8,10},{10,11},{11... | collective-permute-start | bytes 393224 | tf_op jit(solution)/shard_map/ppermute | solution.py:382
  15.4 2.0 %collective-permute-start.7 = (bf16[256,256]{1,0:T(8,128)(2,1)S(1)}, bf16[256,256]{1,0:T(8,128)(2,1)S(1)}, u32[]{:S(2)}, u32[]{:S(2)}) collective-permute-start(bf16[256,256]{1,0:T(8,128)(2,1)S(1)} %split.9), channel_id=1, source_target_pairs={{0,2},{2,3},{3,1},{1,0},{4,6},{6,7},{7,5},{5,4},{8,10},{10,11},{11... | collective-permute-start | bytes 393224 | tf_op jit(solution)/shard_map/ppermute | solution.py:382
  17.4 4.0 %collective-permute-done.9.source.refs_2_ = bf16[256,512]{1,0:T(8,128)(2,1)S(1)} collective-permute-done((bf16[256,512]{1,0:T(8,128)(2,1)S(1)}, bf16[256,512]{1,0:T(8,128)(2,1)S(1)}, u32[]{:S(2)}, u32[]{:S(2)}) %collective-permute-start.9) | collective-permute-done | bytes 262176 | tf_op jit(solution)/shard_map/ppermute | solution.py:382
  21.4 0.7 %collective-permute-start.10 = (bf16[256,256]{1,0:T(8,128)(2,1)S(1)}, bf16[256,256]{1,0:T(8,128)(2,1)S(1)}, u32[]{:S(2)}, u32[]{:S(2)}) collective-permute-start(bf16[256,256]{1,0:T(8,128)(2,1)S(1)} %get-tuple-element.33), channel_id=1, source_target_pairs={{1,3},{3,2},{2,0},{0,1},{5,7},{7,6},{6,4},{4,5},{9,11},{11,10},{10... | collective-permute-start | bytes 393224 | tf_op jit(solution)/shard_map/ppermute | solution.py:382
  22.1 2.4 %collective-permute-start.13 = (bf16[256,256]{1,0:T(8,128)(2,1)S(1)}, bf16[256,256]{1,0:T(8,128)(2,1)S(1)}, u32[]{:S(2)}, u32[]{:S(2)}) collective-permute-start(bf16[256,256]{1,0:T(8,128)(2,1)S(1)} %get-tuple-element.37), channel_id=1, source_target_pairs={{1,3},{3,2},{2,0},{0,1},{5,7},{7,6},{6,4},{4,5},{9,11},{11,10},{10... | collective-permute-start | bytes 393224 | tf_op jit(solution)/shard_map/ppermute | solution.py:382
  24.5 1.3 %collective-permute-start.5 = (bf16[256,256]{1,0:T(8,128)(2,1)S(1)}, bf16[256,256]{1,0:T(8,128)(2,1)S(1)}, u32[]{:S(2)}, u32[]{:S(2)}) collective-permute-start(bf16[256,256]{1,0:T(8,128)(2,1)S(1)} %split.8), channel_id=1, source_target_pairs={{0,2},{2,3},{3,1},{1,0},{4,6},{6,7},{7,5},{5,4},{8,10},{10,11},{11... | collective-permute-start | bytes 393224 | tf_op jit(solution)/shard_map/ppermute | solution.py:382
  25.8 1.1 %collective-permute-done.7.source.refs_1_ = bf16[256,256]{1,0:T(8,128)(2,1)S(1)} collective-permute-done((bf16[256,256]{1,0:T(8,128)(2,1)S(1)}, bf16[256,256]{1,0:T(8,128)(2,1)S(1)}, u32[]{:S(2)}, u32[]{:S(2)}) %collective-permute-start.7) | collective-permute-done | bytes 131104 | tf_op jit(solution)/shard_map/ppermute | solution.py:382
  26.9 1.7 %collective-permute-start.8 = (bf16[256,256]{1,0:T(8,128)(2,1)S(1)}, bf16[256,256]{1,0:T(8,128)(2,1)S(1)}, u32[]{:S(2)}, u32[]{:S(2)}) collective-permute-start(bf16[256,256]{1,0:T(8,128)(2,1)S(1)} %split.10), channel_id=1, source_target_pairs={{0,2},{2,3},{3,1},{1,0},{4,6},{6,7},{7,5},{5,4},{8,10},{10,11},{11... | collective-permute-start | bytes 393224 | tf_op jit(solution)/shard_map/ppermute | solution.py:382
  28.6 0.7 %collective-permute-done.10.source.refs_2_ = bf16[256,256]{1,0:T(8,128)(2,1)S(1)} collective-permute-done((bf16[256,256]{1,0:T(8,128)(2,1)S(1)}, bf16[256,256]{1,0:T(8,128)(2,1)S(1)}, u32[]{:S(2)}, u32[]{:S(2)}) %collective-permute-start.10) | collective-permute-done | bytes 131104 | tf_op jit(solution)/shard_map/ppermute | solution.py:382
  29.3 1.2 %collective-permute-start.11 = (bf16[256,256]{1,0:T(8,128)(2,1)S(1)}, bf16[256,256]{1,0:T(8,128)(2,1)S(1)}, u32[]{:S(2)}, u32[]{:S(2)}) collective-permute-start(bf16[256,256]{1,0:T(8,128)(2,1)S(1)} %split.12), channel_id=1, source_target_pairs={{1,3},{3,2},{2,0},{0,1},{5,7},{7,6},{6,4},{4,5},{9,11},{11,10},{10... | collective-permute-start | bytes 393224 | tf_op jit(solution)/shard_map/ppermute | solution.py:382
  30.5 6.3 %collective-permute-done.13.refs_3_.source = bf16[256,256]{1,0:T(8,128)(2,1)S(1)} collective-permute-done((bf16[256,256]{1,0:T(8,128)(2,1)S(1)}, bf16[256,256]{1,0:T(8,128)(2,1)S(1)}, u32[]{:S(2)}, u32[]{:S(2)}) %collective-permute-start.13) | collective-permute-done | bytes 131104 | tf_op jit(solution)/shard_map/ppermute | solution.py:382
  37.1 0.9 %project.4.refs_5_ = f32[256,1024]{1,0:T(8,128)S(1)} custom-call(bf16[256,256]{1,0:T(8,128)(2,1)S(1)} %mix.3.refs_0_, bf16[256,256]{1,0:T(8,128)(2,1)S(1)} %mix.4.refs_1_, bf16[256,512]{1,0:T(8,128)(2,1)S(1)} %mix.5.refs_2_, bf16[4160,512]{1,0:T(8,128)(2,1)S(1)} %pack.1.refs_3_.refs_4_.refs_0_, ...), custom_call_target="tpu_custom_call" | custom-call | flops 536870912 | bytes 10092544 | tf_op jit(solution)/shard_map/project/pallas_call | solution.py:62
  38.0 0.9 %project.5.refs_6_ = f32[256,1024]{1,0:T(8,128)S(1)} custom-call(bf16[256,256]{1,0:T(8,128)(2,1)S(1)} %collective-permute-done.3.source.refs_0_, bf16[256,256]{1,0:T(8,128)(2,1)S(1)} %collective-permute-done.6.source.refs_1_, bf16[256,512]{1,0:T(8,128)(2,1)S(1)} %collective-permute-done.9.source.refs_2_, bf16[4160,512]{1,0:T(8,128)(2,1)S(1)} %pack.1.refs_3_.refs_4_.refs_0_, ...), custom_call_target="tpu_custom_call" | custom-call | flops 536870912 | bytes 11141120 | tf_op jit(solution)/shard_map/project/pallas_call | solution.py:62
  39.0 0.9 %project.6.refs_5_ = f32[256,1024]{1,0:T(8,128)S(1)} custom-call(bf16[256,256]{1,0:T(8,128)(2,1)S(1)} %collective-permute-done.4.source.refs_0_, bf16[256,256]{1,0:T(8,128)(2,1)S(1)} %collective-permute-done.7.source.refs_1_, bf16[256,256]{1,0:T(8,128)(2,1)S(1)} %collective-permute-done.10.source.refs_2_, ...), custom_call_target="tpu_custom_call" | custom-call | flops 536870912 | bytes 11141120 | tf_op jit(solution)/shard_map/project/pallas_call | solution.py:62
  40.3 0.8 %project.7.acc_ref = f32[256,1024]{1,0:T(8,128)S(1)} custom-call(bf16[256,256]{1,0:T(8,128)(2,1)S(1)} %collective-permute-done.5.refs_0_, bf16[256,256]{1,0:T(8,128)(2,1)S(1)} %collective-permute-done.8.refs_1_, bf16[256,256]{1,0:T(8,128)(2,1)S(1)} %collective-permute-done.11.refs_2_, bf16[4160,512]{1,0:T(8,128)(2,1)S(1)} %pack.1.refs_3_.refs_4_.refs_0_, ...), custom_call_target="tpu_custom_call" | custom-call | flops 402653184 | bytes 11010048 | tf_op jit(solution)/shard_map/project/pallas_call | solution.py:62
  41.1 2.0 %collective-permute-done.14.e_ref = bf16[256,256]{1,0:T(8,128)(2,1)S(1)} collective-permute-done((bf16[256,256]{1,0:T(8,128)(2,1)S(1)}, bf16[256,256]{1,0:T(8,128)(2,1)S(1)}, u32[]{:S(2)}, u32[]{:S(2)}) %collective-permute-start.14) | collective-permute-done | bytes 131104 | tf_op jit(solution)/shard_map/ppermute | solution.py:382
  43.1 0.6 %cross_attend.1 = (f32[64,640]{1,0:T(8,128)S(1)}, f32[64,640]{1,0:T(8,128)S(1)}) custom-call(f32[256,1024]{1,0:T(8,128)S(1)} %project.7.acc_ref, bf16[256,256]{1,0:T(8,128)(2,1)S(1)} %collective-permute-done.14.e_ref, bf16[256,1024]{1,0:T(8,128)(2,1)S(1)} %get-tuple-element.38.map_ref, bf16[128,512]{1,0:T(8,128)(2,1)S(1)} %get-tuple-element.39.tgt_ref, ...), custom_call_target="tpu_custom_call" | custom-call | flops 134217728 | bytes 2293760 | tf_op jit(solution)/shard_map/cross_attend/pallas_call | solution.py:62
  43.8 1.4 %collective-permute-done.15.refs_1_ = f32[64,640]{1,0:T(8,128)S(1)} collective-permute-done((f32[64,640]{1,0:T(8,128)S(1)}, f32[64,640]{1,0:T(8,128)S(1)}, u32[]{:S(2)}, u32[]{:S(2)}) %collective-permute-start.15) | collective-permute-done | bytes 163872 | tf_op jit(solution)/shard_map/ppermute | solution.py:399
  45.1 0.8 %combine.1 = bf16[64,512]{1,0:T(8,128)(2,1)} custom-call(f32[64,640]{1,0:T(8,128)S(1)} %get-tuple-element.41.refs_0_, f32[64,640]{1,0:T(8,128)S(1)} %collective-permute-done.15.refs_1_), custom_call_target="tpu_custom_call" | custom-call | bytes 393216 | tf_op jit(solution)/shard_map/combine/pallas_call | solution.py:62
  (29 shorter events, 3.7 us)
Async XLA Ops:
  0.0 2.4 %collective-permute-start.1 = (bf16[256,1024]{1,0:T(8,128)(2,1)}, bf16[256,1024]{1,0:T(8,128)(2,1)S(1)}, u32[]{:S(2)}, u32[]{:S(2)}) collective-permute-start(bf16[256,1024]{1,0:T(8,128)(2,1)} %refs_1_.1), channel_id=1, source_target_pairs={{0,4},{4,0},{1,5},{5,1},{2,6},{6,2},{3,7},{7,3},{8,12},{12,8},{9,1... | collective-permute-start | bytes 1572872 | tf_op jit(solution)/shard_map/ppermute | solution.py:328
  0.5 1.9 %collective-permute-start = (s32[1,256]{1,0:T(1,128)}, s32[1,256]{1,0:T(1,128)S(1)}, u32[]{:S(2)}, u32[]{:S(2)}) collective-permute-start(s32[1,256]{1,0:T(1,128)} %bitcast.1), channel_id=1, source_target_pairs={{0,4},{4,0},{1,5},{5,1},{2,6},{6,2},{3,7},{7,3},{8,12},{12,8},{9,1... | collective-permute-start | bytes 3080 | tf_op jit(solution)/shard_map/ppermute | solution.py:328
  0.5 2.4 %collective-permute-start.2 = (bf16[256,1024]{1,0:T(8,128)(2,1)}, bf16[256,1024]{1,0:T(8,128)(2,1)S(1)}, u32[]{:S(2)}, u32[]{:S(2)}) collective-permute-start(bf16[256,1024]{1,0:T(8,128)(2,1)} %refs_2_.1), channel_id=1, source_target_pairs={{0,4},{4,0},{1,5},{5,1},{2,6},{6,2},{3,7},{7,3},{8,12},{12,8},{9,1... | collective-permute-start | bytes 1572872 | tf_op jit(solution)/shard_map/ppermute | solution.py:328
  3.2 9.6 %collective-permute-start.3 = (bf16[256,256]{1,0:T(8,128)(2,1)S(1)}, bf16[256,256]{1,0:T(8,128)(2,1)S(1)}, u32[]{:S(2)}, u32[]{:S(2)}) collective-permute-start(bf16[256,256]{1,0:T(8,128)(2,1)S(1)} %mix.3.refs_0_), channel_id=1, source_target_pairs={{0,2},{2,3},{3,1},{1,0},{4,6},{6,7},{7,5},{5,4},{8,10},{10,11},{11... | collective-permute-start | bytes 393224 | tf_op jit(solution)/shard_map/ppermute | solution.py:382
  7.4 7.9 %collective-permute-start.6 = (bf16[256,256]{1,0:T(8,128)(2,1)S(1)}, bf16[256,256]{1,0:T(8,128)(2,1)S(1)}, u32[]{:S(2)}, u32[]{:S(2)}) collective-permute-start(bf16[256,256]{1,0:T(8,128)(2,1)S(1)} %mix.4.refs_1_), channel_id=1, source_target_pairs={{0,2},{2,3},{3,1},{1,0},{4,6},{6,7},{7,5},{5,4},{8,10},{10,11},{11... | collective-permute-start | bytes 393224 | tf_op jit(solution)/shard_map/ppermute | solution.py:382
  10.0 11.4 %collective-permute-start.9 = (bf16[256,512]{1,0:T(8,128)(2,1)S(1)}, bf16[256,512]{1,0:T(8,128)(2,1)S(1)}, u32[]{:S(2)}, u32[]{:S(2)}) collective-permute-start(bf16[256,512]{1,0:T(8,128)(2,1)S(1)} %mix.5.refs_2_), channel_id=1, source_target_pairs={{1,3},{3,2},{2,0},{0,1},{5,7},{7,6},{6,4},{4,5},{9,11},{11,10},{10... | collective-permute-start | bytes 786440 | tf_op jit(solution)/shard_map/ppermute | solution.py:382
  12.7 24.2 %collective-permute-start.12 = (bf16[4160,512]{1,0:T(8,128)(2,1)S(1)}, bf16[4160,512]{1,0:T(8,128)(2,1)S(1)}, u32[]{:S(2)}, u32[]{:S(2)}) collective-permute-start(bf16[4160,512]{1,0:T(8,128)(2,1)S(1)} %pack.1.refs_3_.refs_4_.refs_0_), channel_id=1, source_target_pairs={{0,4},{4,0},{1,5},{5,1},{2,6},{6,2},{3,7},{7,3},{8,12},{12,8},{9,1... | collective-permute-start | bytes 12779528 | tf_op jit(solution)/shard_map/ppermute | solution.py:328
  12.8 11.6 %collective-permute-start.4 = (bf16[256,256]{1,0:T(8,128)(2,1)S(1)}, bf16[256,256]{1,0:T(8,128)(2,1)S(1)}, u32[]{:S(2)}, u32[]{:S(2)}) collective-permute-start(bf16[256,256]{1,0:T(8,128)(2,1)S(1)} %split.7), channel_id=1, source_target_pairs={{0,2},{2,3},{3,1},{1,0},{4,6},{6,7},{7,5},{5,4},{8,10},{10,11},{11... | collective-permute-start | bytes 393224 | tf_op jit(solution)/shard_map/ppermute | solution.py:382
  15.4 11.5 %collective-permute-start.7 = (bf16[256,256]{1,0:T(8,128)(2,1)S(1)}, bf16[256,256]{1,0:T(8,128)(2,1)S(1)}, u32[]{:S(2)}, u32[]{:S(2)}) collective-permute-start(bf16[256,256]{1,0:T(8,128)(2,1)S(1)} %split.9), channel_id=1, source_target_pairs={{0,2},{2,3},{3,1},{1,0},{4,6},{6,7},{7,5},{5,4},{8,10},{10,11},{11... | collective-permute-start | bytes 393224 | tf_op jit(solution)/shard_map/ppermute | solution.py:382
  21.4 7.9 %collective-permute-start.10 = (bf16[256,256]{1,0:T(8,128)(2,1)S(1)}, bf16[256,256]{1,0:T(8,128)(2,1)S(1)}, u32[]{:S(2)}, u32[]{:S(2)}) collective-permute-start(bf16[256,256]{1,0:T(8,128)(2,1)S(1)} %get-tuple-element.33), channel_id=1, source_target_pairs={{1,3},{3,2},{2,0},{0,1},{5,7},{7,6},{6,4},{4,5},{9,11},{11,10},{10... | collective-permute-start | bytes 393224 | tf_op jit(solution)/shard_map/ppermute | solution.py:382
  22.1 14.7 %collective-permute-start.13 = (bf16[256,256]{1,0:T(8,128)(2,1)S(1)}, bf16[256,256]{1,0:T(8,128)(2,1)S(1)}, u32[]{:S(2)}, u32[]{:S(2)}) collective-permute-start(bf16[256,256]{1,0:T(8,128)(2,1)S(1)} %get-tuple-element.37), channel_id=1, source_target_pairs={{1,3},{3,2},{2,0},{0,1},{5,7},{7,6},{6,4},{4,5},{9,11},{11,10},{10... | collective-permute-start | bytes 393224 | tf_op jit(solution)/shard_map/ppermute | solution.py:382
  24.5 15.4 %collective-permute-start.5 = (bf16[256,256]{1,0:T(8,128)(2,1)S(1)}, bf16[256,256]{1,0:T(8,128)(2,1)S(1)}, u32[]{:S(2)}, u32[]{:S(2)}) collective-permute-start(bf16[256,256]{1,0:T(8,128)(2,1)S(1)} %split.8), channel_id=1, source_target_pairs={{0,2},{2,3},{3,1},{1,0},{4,6},{6,7},{7,5},{5,4},{8,10},{10,11},{11... | collective-permute-start | bytes 393224 | tf_op jit(solution)/shard_map/ppermute | solution.py:382
  26.9 13.0 %collective-permute-start.8 = (bf16[256,256]{1,0:T(8,128)(2,1)S(1)}, bf16[256,256]{1,0:T(8,128)(2,1)S(1)}, u32[]{:S(2)}, u32[]{:S(2)}) collective-permute-start(bf16[256,256]{1,0:T(8,128)(2,1)S(1)} %split.10), channel_id=1, source_target_pairs={{0,2},{2,3},{3,1},{1,0},{4,6},{6,7},{7,5},{5,4},{8,10},{10,11},{11... | collective-permute-start | bytes 393224 | tf_op jit(solution)/shard_map/ppermute | solution.py:382
  29.3 11.0 %collective-permute-start.11 = (bf16[256,256]{1,0:T(8,128)(2,1)S(1)}, bf16[256,256]{1,0:T(8,128)(2,1)S(1)}, u32[]{:S(2)}, u32[]{:S(2)}) collective-permute-start(bf16[256,256]{1,0:T(8,128)(2,1)S(1)} %split.12), channel_id=1, source_target_pairs={{1,3},{3,2},{2,0},{0,1},{5,7},{7,6},{6,4},{4,5},{9,11},{11,10},{10... | collective-permute-start | bytes 393224 | tf_op jit(solution)/shard_map/ppermute | solution.py:382
  36.8 6.2 %collective-permute-start.14 = (bf16[256,256]{1,0:T(8,128)(2,1)S(1)}, bf16[256,256]{1,0:T(8,128)(2,1)S(1)}, u32[]{:S(2)}, u32[]{:S(2)}) collective-permute-start(bf16[256,256]{1,0:T(8,128)(2,1)S(1)} %split.13), channel_id=1, source_target_pairs={{1,3},{3,2},{2,0},{0,1},{5,7},{7,6},{6,4},{4,5},{9,11},{11,10},{10... | collective-permute-start | bytes 393224 | tf_op jit(solution)/shard_map/ppermute | solution.py:382
  43.7 1.5 %collective-permute-start.15 = (f32[64,640]{1,0:T(8,128)S(1)}, f32[64,640]{1,0:T(8,128)S(1)}, u32[]{:S(2)}, u32[]{:S(2)}) collective-permute-start(f32[64,640]{1,0:T(8,128)S(1)} %get-tuple-element.42), channel_id=1, source_target_pairs={{4,0},{0,4},{5,1},{1,5},{6,2},{2,6},{7,3},{3,7},{12,8},{8,12},{13,... | collective-permute-start | bytes 491528 | tf_op jit(solution)/shard_map/ppermute | solution.py:399

commit v22 on v20

--- a/solution.py
+++ b/solution.py
@@ -326,11 +326,16 @@
     held = []
     for j in range(chunks):
         weights, totals = weigh(query, [own_key, *keys], [marks, *near_marks], j * heads, heads)
-        size = heads if j else 1
+        size = 1
         for skip in range(0, heads, size):
             held.append(mix(weights, totals, [own_value, *values], skip, j * heads + skip, size))
 
-    key_map, value_map, tgt_query, held[-1] = lax.optimization_barrier((key_map, value_map, tgt_query, held[-1]))
+    order = ring_order(n_head)
+    ring = [(order[i], order[(i + 1) % n_head]) for i in range(n_head)]
+    before = {target: source for source, target in ring}
+
+    sent, held = held, [lax.ppermute(h, "head", ring) for h in held]
+    key_map, value_map, tgt_query, arrived = lax.optimization_barrier((key_map, value_map, tgt_query, held[0]))
     near_targets = []
     if n_ctx == 2:
         own_maps = pack(key_map, value_map, tgt_query)
@@ -339,10 +344,6 @@
         whole = [lax.all_gather(x, "ctx", axis=0, tiled=True) for x in (key_map, value_map)]
         shards, near_targets = [pack(*whole, tgt_query)], bring(tgt_query)
     map_rows = (shards[0].shape[0] - tgt_rows) // 2
-
-    order = ring_order(n_head)[::-1]
-    ring = [(order[i], order[(i + 1) % n_head]) for i in range(n_head)]
-    before = {target: source for source, target in ring}
 
     def place(turn, first):
         head, ctx = lax.axis_index("head"), lax.axis_index("ctx")
@@ -357,12 +358,14 @@
             return None, row
         return jnp.where(lax.div(row, map_rows) == ctx, 0, 1), lax.rem(row, map_rows)
 
-    acc, last = None, n_head - 1
-    for turn in range(last):
-        pieces = [p for h in held for p in split(h, h.shape[1] // HEAD_DIM)] if turn else held
+    last = n_head - 1
+    acc = project(None, sent, functools.partial(place, 0, 0), shards, map_rows)
+    arrived = [arrived, *held[1:]]
+    for turn in range(1, last):
+        pieces = [p for h in held for p in split(h, h.shape[1] // HEAD_DIM)]
         later = [lax.ppermute(p, "head", ring) for p in pieces]
-        acc = project(acc, held, functools.partial(place, turn, 0), shards, map_rows)
-        held = later
+        acc = project(acc, arrived, functools.partial(place, turn, 0), shards, map_rows)
+        held = arrived = later
     acc = project(acc, held[:-1], functools.partial(place, last, 0), shards, map_rows)
     depth = held[-1].shape[1]
     last_maps, targets, mask = prepare(

time: 45 us -> 44.2 us (0.982)
  waiting for transfers between devices: 16.1 us -> 5.8 us
  starting transfers between devices: 18.4 us -> 27.8 us
    ppermute x11 -> x8, waiting for transfers between devices: 14.7 us -> 3.94 us  [on_device(): later = [lax.ppermute(p, 'head', ring) for p in pieces]]
    ppermute x0 -> x4, starting transfers between devices: none -> 6.07 us  [on_device(): sent, held = (held, [lax.ppermute(h, 'head', ring) for h in held])]
    ppermute x11 -> x8, starting transfers between devices: 17.3 us -> 20.6 us  [on_device(): later = [lax.ppermute(p, 'head', ring) for p in pieces]]
    ppermute x0 -> x4, waiting for transfers between devices: none -> 0.47 us  [on_device(): sent, held = (held, [lax.ppermute(h, 'head', ring) for h in held])]
    pallas_call x21 -> x23, Pallas kernels: 10.1 us -> 10.3 us  [call(): pl.pallas_call(kernel, in_specs=specs or [VMEM] * len(operands), out_spec...]
  transfers between devices with their start and end apart: 16 -> 17, of which waited for: 9 -> 4; matrix products, arithmetic and copies ran while one was open for 0% -> 0% of each run, Pallas kernels for 19% -> 19%
where the time goes in v22:
time: 44.2 us; the launch traced here: 44.1 us
  starting transfers between devices  27.8 us (63%)
  Pallas kernels  10.3 us (23%)
  waiting for transfers between devices  5.8 us (13%)
    ppermute x8, starting transfers between devices, on_device(): later = [lax.ppermute(p, 'head', ring) for p in pieces]  20.6 us
    pallas_call x23, Pallas kernels, call(): pl.pallas_call(kernel, in_specs=specs or [VMEM] * len(operands), out_spec...  10.3 us
    ppermute x4, starting transfers between devices, on_device(): sent, held = (held, [lax.ppermute(h, 'head', ring) for h in held])  6.07 us
    ppermute x8, waiting for transfers between devices, on_device(): later = [lax.ppermute(p, 'head', ring) for p in pieces]  3.94 us
    ppermute x1, waiting for transfers between devices, on_device(): lax.ppermute(piece, 'ctx', [(target, source) for source, target in pairs])  1.38 us
    ppermute x4, starting transfers between devices, on_device(): bring = lambda x: [lax.ppermute(x, 'ctx', pairs) for pairs in links]  1.03 us
  transfers between devices with their start and end apart: 17, of which 4 were waited for; matrix products, arithmetic and copies ran while one was open for 0% of the time, Pallas kernels for 19%

profile of v22, /device:TPU:0, one launch (start us, length us, event | category | flops | bytes accessed | tf_op | source)
XLA Modules:
  0.0 44.1 jit_solution(14298702579800836495)
XLA Ops:
  1.0 1.4 %fetch.1 = (bf16[256,1024]{1,0:T(8,128)(2,1)S(1)}, bf16[256,1024]{1,0:T(8,128)(2,1)S(1)}, bf16[256,1024]{1,0:T(8,128)(2,1)S(1)}, s32[1,256]{1,0:T(1,128)S(1)}) custom-call(bf16[256,1024]{1,0:T(8,128)(2,1)} %refs_0_.1, bf16[256,1024]{1,0:T(8,128)(2,1)} %refs_1_.1, bf16[256,1024]{1,0:T(8,128)(2,1)} %refs_2_.1, s32[1,256]{1,0:T(1,128)} %bitcast.2), custom_call_target="tpu_custom_call" | custom-call | bytes 3147776 | tf_op jit(solution)/shard_map/fetch/pallas_call | solution.py:62
  2.4 0.6 %weigh.2 = (bf16[256,1024]{1,0:T(8,128)(2,1)S(1)}, f32[256,128]{1,0:T(8,128)S(1)}) custom-call(s32[1,256]{1,0:T(1,128)S(1)} %get-tuple-element.22.refs_0_.refs_2_, s32[1,256]{1,0:T(1,128)S(1)} %collective-permute-done.refs_1_.refs_3_, bf16[256,1024]{1,0:T(8,128)(2,1)S(1)} %get-tuple-element.23.refs_2_, bf16[256,1024]{1,0:T(8,128)(2,1)S(1)} %get-tuple-element.24.refs_3_, ...), custom_call_target="tpu_custom_call" | custom-call | flops 6000000000 | bytes 2230272 | tf_op jit(solution)/shard_map/weigh/pallas_call | solution.py:62
  3.2 4.0 %collective-permute-start.3 = (bf16[256,256]{1,0:T(8,128)(2,1)S(1)}, bf16[256,256]{1,0:T(8,128)(2,1)S(1)}, u32[]{:S(2)}, u32[]{:S(2)}) collective-permute-start(bf16[256,256]{1,0:T(8,128)(2,1)S(1)} %mix.4.refs_0_), channel_id=1, source_target_pairs={{0,2},{2,3},{3,1},{1,0},{4,6},{6,7},{7,5},{5,4},{8,10},{10,11},{11... | collective-permute-start | bytes 393224 | tf_op jit(solution)/shard_map/ppermute | solution.py:337
  7.5 1.6 %collective-permute-start.6 = (bf16[256,256]{1,0:T(8,128)(2,1)S(1)}, bf16[256,256]{1,0:T(8,128)(2,1)S(1)}, u32[]{:S(2)}, u32[]{:S(2)}) collective-permute-start(bf16[256,256]{1,0:T(8,128)(2,1)S(1)} %mix.5.refs_1_), channel_id=1, source_target_pairs={{0,2},{2,3},{3,1},{1,0},{4,6},{6,7},{7,5},{5,4},{8,10},{10,11},{11... | collective-permute-start | bytes 393224 | tf_op jit(solution)/shard_map/ppermute | solution.py:337
  9.1 0.6 %weigh.3 = (bf16[256,1024]{1,0:T(8,128)(2,1)S(1)}, f32[256,128]{1,0:T(8,128)S(1)}) custom-call(s32[1,256]{1,0:T(1,128)S(1)} %get-tuple-element.22.refs_0_.refs_2_, s32[1,256]{1,0:T(1,128)S(1)} %collective-permute-done.refs_1_.refs_3_, bf16[256,1024]{1,0:T(8,128)(2,1)S(1)} %get-tuple-element.23.refs_2_, bf16[256,1024]{1,0:T(8,128)(2,1)S(1)} %get-tuple-element.24.refs_3_, ...), custom_call_target="tpu_custom_call" | custom-call | flops 6000000000 | bytes 2230272 | tf_op jit(solution)/shard_map/weigh/pallas_call | solution.py:62
  10.6 0.5 %collective-permute-done.3.source.refs_0_ = bf16[256,256]{1,0:T(8,128)(2,1)S(1)} collective-permute-done((bf16[256,256]{1,0:T(8,128)(2,1)S(1)}, bf16[256,256]{1,0:T(8,128)(2,1)S(1)}, u32[]{:S(2)}, u32[]{:S(2)}) %collective-permute-start.3) | collective-permute-done | bytes 131104 | tf_op jit(solution)/shard_map/ppermute | solution.py:337
  11.1 3.4 %collective-permute-start.4 = (bf16[256,256]{1,0:T(8,128)(2,1)S(1)}, bf16[256,256]{1,0:T(8,128)(2,1)S(1)}, u32[]{:S(2)}, u32[]{:S(2)}) collective-permute-start(bf16[256,256]{1,0:T(8,128)(2,1)S(1)} %split.8), channel_id=1, source_target_pairs={{0,2},{2,3},{3,1},{1,0},{4,6},{6,7},{7,5},{5,4},{8,10},{10,11},{11... | collective-permute-start | bytes 393224 | tf_op jit(solution)/shard_map/ppermute | solution.py:366
  14.5 2.8 %collective-permute-start.7 = (bf16[256,256]{1,0:T(8,128)(2,1)S(1)}, bf16[256,256]{1,0:T(8,128)(2,1)S(1)}, u32[]{:S(2)}, u32[]{:S(2)}) collective-permute-start(bf16[256,256]{1,0:T(8,128)(2,1)S(1)} %split.10), channel_id=1, source_target_pairs={{0,2},{2,3},{3,1},{1,0},{4,6},{6,7},{7,5},{5,4},{8,10},{10,11},{11... | collective-permute-start | bytes 393224 | tf_op jit(solution)/shard_map/ppermute | solution.py:366
  17.3 2.8 %collective-permute-start.10 = (bf16[256,256]{1,0:T(8,128)(2,1)S(1)}, bf16[256,256]{1,0:T(8,128)(2,1)S(1)}, u32[]{:S(2)}, u32[]{:S(2)}) collective-permute-start(bf16[256,256]{1,0:T(8,128)(2,1)S(1)} %split.12), channel_id=1, source_target_pairs={{0,2},{2,3},{3,1},{1,0},{4,6},{6,7},{7,5},{5,4},{8,10},{10,11},{11... | collective-permute-start | bytes 393224 | tf_op jit(solution)/shard_map/ppermute | solution.py:366
  20.1 2.2 %pack.1.refs_4_.refs_3_.refs_0_ = bf16[4160,512]{1,0:T(8,128)(2,1)S(1)} custom-call(bf16[2048,512]{1,0:T(8,128)(2,1)} %refs_0_.2, bf16[2048,512]{1,0:T(8,128)(2,1)} %refs_1_.2, bf16[64,512]{1,0:T(8,128)(2,1)} %refs_2_.2), custom_call_target="tpu_custom_call" | custom-call | bytes 8519680 | tf_op jit(solution)/shard_map/pack/pallas_call | solution.py:62
  22.5 0.7 %collective-permute-start.14 = (bf16[256,256]{1,0:T(8,128)(2,1)S(1)}, bf16[256,256]{1,0:T(8,128)(2,1)S(1)}, u32[]{:S(2)}, u32[]{:S(2)}) collective-permute-start(bf16[256,256]{1,0:T(8,128)(2,1)S(1)} %split.14), channel_id=1, source_target_pairs={{0,2},{2,3},{3,1},{1,0},{4,6},{6,7},{7,5},{5,4},{8,10},{10,11},{11... | collective-permute-start | bytes 393224 | tf_op jit(solution)/shard_map/ppermute | solution.py:366
  23.2 2.5 %collective-permute-start.5 = (bf16[256,256]{1,0:T(8,128)(2,1)S(1)}, bf16[256,256]{1,0:T(8,128)(2,1)S(1)}, u32[]{:S(2)}, u32[]{:S(2)}) collective-permute-start(bf16[256,256]{1,0:T(8,128)(2,1)S(1)} %split.9), channel_id=1, source_target_pairs={{0,2},{2,3},{3,1},{1,0},{4,6},{6,7},{7,5},{5,4},{8,10},{10,11},{11... | collective-permute-start | bytes 393224 | tf_op jit(solution)/shard_map/ppermute | solution.py:366
  25.8 2.8 %collective-permute-start.8 = (bf16[256,256]{1,0:T(8,128)(2,1)S(1)}, bf16[256,256]{1,0:T(8,128)(2,1)S(1)}, u32[]{:S(2)}, u32[]{:S(2)}) collective-permute-start(bf16[256,256]{1,0:T(8,128)(2,1)S(1)} %split.11), channel_id=1, source_target_pairs={{0,2},{2,3},{3,1},{1,0},{4,6},{6,7},{7,5},{5,4},{8,10},{10,11},{11... | collective-permute-start | bytes 393224 | tf_op jit(solution)/shard_map/ppermute | solution.py:366
  28.6 2.8 %collective-permute-start.11 = (bf16[256,256]{1,0:T(8,128)(2,1)S(1)}, bf16[256,256]{1,0:T(8,128)(2,1)S(1)}, u32[]{:S(2)}, u32[]{:S(2)}) collective-permute-start(bf16[256,256]{1,0:T(8,128)(2,1)S(1)} %split.13), channel_id=1, source_target_pairs={{0,2},{2,3},{3,1},{1,0},{4,6},{6,7},{7,5},{5,4},{8,10},{10,11},{11... | collective-permute-start | bytes 393224 | tf_op jit(solution)/shard_map/ppermute | solution.py:366
  31.4 2.8 %collective-permute-start.15 = (bf16[256,256]{1,0:T(8,128)(2,1)S(1)}, bf16[256,256]{1,0:T(8,128)(2,1)S(1)}, u32[]{:S(2)}, u32[]{:S(2)}) collective-permute-start(bf16[256,256]{1,0:T(8,128)(2,1)S(1)} %split.15), channel_id=1, source_target_pairs={{0,2},{2,3},{3,1},{1,0},{4,6},{6,7},{7,5},{5,4},{8,10},{10,11},{11... | collective-permute-start | bytes 393224 | tf_op jit(solution)/shard_map/ppermute | solution.py:366
  34.4 0.7 %project.4.refs_6_ = f32[256,1024]{1,0:T(8,128)S(1)} custom-call(bf16[256,256]{1,0:T(8,128)(2,1)S(1)} %mix.4.refs_0_, bf16[256,256]{1,0:T(8,128)(2,1)S(1)} %mix.5.refs_1_, bf16[256,256]{1,0:T(8,128)(2,1)S(1)} %mix.6.refs_2_, bf16[256,256]{1,0:T(8,128)(2,1)S(1)} %mix.7.refs_3_, bf16[4160,512]{1,0:T(8,128)(2,1)S(1)} %pack.1.refs_4_.refs_3_.refs_0_, ...), custom_call_target="tpu_custom_call" | custom-call | flops 536870912 | bytes 10092544 | tf_op jit(solution)/shard_map/project/pallas_call | solution.py:62
  35.1 0.7 %project.5.refs_6_ = f32[256,1024]{1,0:T(8,128)S(1)} custom-call(bf16[256,256]{1,0:T(8,128)(2,1)S(1)} %collective-permute-done.3.source.refs_0_, bf16[256,256]{1,0:T(8,128)(2,1)S(1)} %collective-permute-done.6.source.refs_1_, bf16[256,256]{1,0:T(8,128)(2,1)S(1)} %collective-permute-done.9.source.refs_2_, ...), custom_call_target="tpu_custom_call" | custom-call | flops 536870912 | bytes 11141120 | tf_op jit(solution)/shard_map/project/pallas_call | solution.py:62
  35.9 0.7 %project.6.refs_5_ = f32[256,1024]{1,0:T(8,128)S(1)} custom-call(bf16[256,256]{1,0:T(8,128)(2,1)S(1)} %collective-permute-done.4.source.refs_0_, bf16[256,256]{1,0:T(8,128)(2,1)S(1)} %collective-permute-done.7.source.refs_1_, bf16[256,256]{1,0:T(8,128)(2,1)S(1)} %collective-permute-done.10.source.refs_2_, ...), custom_call_target="tpu_custom_call" | custom-call | flops 536870912 | bytes 11141120 | tf_op jit(solution)/shard_map/project/pallas_call | solution.py:62
  36.7 2.5 %collective-permute-done.11.refs_2_ = bf16[256,256]{1,0:T(8,128)(2,1)S(1)} collective-permute-done((bf16[256,256]{1,0:T(8,128)(2,1)S(1)}, bf16[256,256]{1,0:T(8,128)(2,1)S(1)}, u32[]{:S(2)}, u32[]{:S(2)}) %collective-permute-start.11) | collective-permute-done | bytes 131104 | tf_op jit(solution)/shard_map/ppermute | solution.py:366
  39.2 0.6 %project.7.acc_ref = f32[256,1024]{1,0:T(8,128)S(1)} custom-call(bf16[256,256]{1,0:T(8,128)(2,1)S(1)} %collective-permute-done.5.refs_0_, bf16[256,256]{1,0:T(8,128)(2,1)S(1)} %collective-permute-done.8.refs_1_, bf16[256,256]{1,0:T(8,128)(2,1)S(1)} %collective-permute-done.11.refs_2_, bf16[4160,512]{1,0:T(8,128)(2,1)S(1)} %pack.1.refs_4_.refs_3_.refs_0_, ...), custom_call_target="tpu_custom_call" | custom-call | flops 402653184 | bytes 11010048 | tf_op jit(solution)/shard_map/project/pallas_call | solution.py:62
  39.8 1.4 %collective-permute-done.15.e_ref = bf16[256,256]{1,0:T(8,128)(2,1)S(1)} collective-permute-done((bf16[256,256]{1,0:T(8,128)(2,1)S(1)}, bf16[256,256]{1,0:T(8,128)(2,1)S(1)}, u32[]{:S(2)}, u32[]{:S(2)}) %collective-permute-start.15) | collective-permute-done | bytes 131104 | tf_op jit(solution)/shard_map/ppermute | solution.py:366
  41.2 0.6 %cross_attend.1 = (f32[64,640]{1,0:T(8,128)S(1)}, f32[64,640]{1,0:T(8,128)S(1)}) custom-call(f32[256,1024]{1,0:T(8,128)S(1)} %project.7.acc_ref, bf16[256,256]{1,0:T(8,128)(2,1)S(1)} %collective-permute-done.15.e_ref, bf16[256,1024]{1,0:T(8,128)(2,1)S(1)} %get-tuple-element.34.map_ref, bf16[128,512]{1,0:T(8,128)(2,1)S(1)} %get-tuple-element.35.tgt_ref, ...), custom_call_target="tpu_custom_call" | custom-call | flops 134217728 | bytes 2293760 | tf_op jit(solution)/shard_map/cross_attend/pallas_call | solution.py:62
  41.9 1.4 %collective-permute-done.16.refs_1_ = f32[64,640]{1,0:T(8,128)S(1)} collective-permute-done((f32[64,640]{1,0:T(8,128)S(1)}, f32[64,640]{1,0:T(8,128)S(1)}, u32[]{:S(2)}, u32[]{:S(2)}) %collective-permute-start.16) | collective-permute-done | bytes 163872 | tf_op jit(solution)/shard_map/ppermute | solution.py:383
  43.3 0.8 %combine.1 = bf16[64,512]{1,0:T(8,128)(2,1)} custom-call(f32[64,640]{1,0:T(8,128)S(1)} %get-tuple-element.37.refs_0_, f32[64,640]{1,0:T(8,128)S(1)} %collective-permute-done.16.refs_1_), custom_call_target="tpu_custom_call" | custom-call | bytes 393216 | tf_op jit(solution)/shard_map/combine/pallas_call | solution.py:62
  (33 shorter events, 2.8 us)
Async XLA Ops:
  0.0 2.4 %collective-permute-start.1 = (bf16[256,1024]{1,0:T(8,128)(2,1)}, bf16[256,1024]{1,0:T(8,128)(2,1)S(1)}, u32[]{:S(2)}, u32[]{:S(2)}) collective-permute-start(bf16[256,1024]{1,0:T(8,128)(2,1)} %refs_1_.1), channel_id=1, source_target_pairs={{0,4},{4,0},{1,5},{5,1},{2,6},{6,2},{3,7},{7,3},{8,12},{12,8},{9,1... | collective-permute-start | bytes 1572872 | tf_op jit(solution)/shard_map/ppermute | solution.py:319
  0.5 1.9 %collective-permute-start = (s32[1,256]{1,0:T(1,128)}, s32[1,256]{1,0:T(1,128)S(1)}, u32[]{:S(2)}, u32[]{:S(2)}) collective-permute-start(s32[1,256]{1,0:T(1,128)} %bitcast.1), channel_id=1, source_target_pairs={{0,4},{4,0},{1,5},{5,1},{2,6},{6,2},{3,7},{7,3},{8,12},{12,8},{9,1... | collective-permute-start | bytes 3080 | tf_op jit(solution)/shard_map/ppermute | solution.py:319
  0.5 2.4 %collective-permute-start.2 = (bf16[256,1024]{1,0:T(8,128)(2,1)}, bf16[256,1024]{1,0:T(8,128)(2,1)S(1)}, u32[]{:S(2)}, u32[]{:S(2)}) collective-permute-start(bf16[256,1024]{1,0:T(8,128)(2,1)} %refs_2_.1), channel_id=1, source_target_pairs={{0,4},{4,0},{1,5},{5,1},{2,6},{6,2},{3,7},{7,3},{8,12},{12,8},{9,1... | collective-permute-start | bytes 1572872 | tf_op jit(solution)/shard_map/ppermute | solution.py:319
  3.2 7.9 %collective-permute-start.3 = (bf16[256,256]{1,0:T(8,128)(2,1)S(1)}, bf16[256,256]{1,0:T(8,128)(2,1)S(1)}, u32[]{:S(2)}, u32[]{:S(2)}) collective-permute-start(bf16[256,256]{1,0:T(8,128)(2,1)S(1)} %mix.4.refs_0_), channel_id=1, source_target_pairs={{0,2},{2,3},{3,1},{1,0},{4,6},{6,7},{7,5},{5,4},{8,10},{10,11},{11... | collective-permute-start | bytes 393224 | tf_op jit(solution)/shard_map/ppermute | solution.py:337
  7.5 7.1 %collective-permute-start.6 = (bf16[256,256]{1,0:T(8,128)(2,1)S(1)}, bf16[256,256]{1,0:T(8,128)(2,1)S(1)}, u32[]{:S(2)}, u32[]{:S(2)}) collective-permute-start(bf16[256,256]{1,0:T(8,128)(2,1)S(1)} %mix.5.refs_1_), channel_id=1, source_target_pairs={{0,2},{2,3},{3,1},{1,0},{4,6},{6,7},{7,5},{5,4},{8,10},{10,11},{11... | collective-permute-start | bytes 393224 | tf_op jit(solution)/shard_map/ppermute | solution.py:337
  9.9 7.4 %collective-permute-start.9 = (bf16[256,256]{1,0:T(8,128)(2,1)S(1)}, bf16[256,256]{1,0:T(8,128)(2,1)S(1)}, u32[]{:S(2)}, u32[]{:S(2)}) collective-permute-start(bf16[256,256]{1,0:T(8,128)(2,1)S(1)} %mix.6.refs_2_), channel_id=1, source_target_pairs={{0,2},{2,3},{3,1},{1,0},{4,6},{6,7},{7,5},{5,4},{8,10},{10,11},{11... | collective-permute-start | bytes 393224 | tf_op jit(solution)/shard_map/ppermute | solution.py:337
  10.5 11.9 %collective-permute-start.13 = (bf16[256,256]{1,0:T(8,128)(2,1)S(1)}, bf16[256,256]{1,0:T(8,128)(2,1)S(1)}, u32[]{:S(2)}, u32[]{:S(2)}) collective-permute-start(bf16[256,256]{1,0:T(8,128)(2,1)S(1)} %mix.7.refs_3_), channel_id=1, source_target_pairs={{0,2},{2,3},{3,1},{1,0},{4,6},{6,7},{7,5},{5,4},{8,10},{10,11},{11... | collective-permute-start | bytes 393224 | tf_op jit(solution)/shard_map/ppermute | solution.py:337
  11.1 12.1 %collective-permute-start.4 = (bf16[256,256]{1,0:T(8,128)(2,1)S(1)}, bf16[256,256]{1,0:T(8,128)(2,1)S(1)}, u32[]{:S(2)}, u32[]{:S(2)}) collective-permute-start(bf16[256,256]{1,0:T(8,128)(2,1)S(1)} %split.8), channel_id=1, source_target_pairs={{0,2},{2,3},{3,1},{1,0},{4,6},{6,7},{7,5},{5,4},{8,10},{10,11},{11... | collective-permute-start | bytes 393224 | tf_op jit(solution)/shard_map/ppermute | solution.py:366
  14.5 11.2 %collective-permute-start.7 = (bf16[256,256]{1,0:T(8,128)(2,1)S(1)}, bf16[256,256]{1,0:T(8,128)(2,1)S(1)}, u32[]{:S(2)}, u32[]{:S(2)}) collective-permute-start(bf16[256,256]{1,0:T(8,128)(2,1)S(1)} %split.10), channel_id=1, source_target_pairs={{0,2},{2,3},{3,1},{1,0},{4,6},{6,7},{7,5},{5,4},{8,10},{10,11},{11... | collective-permute-start | bytes 393224 | tf_op jit(solution)/shard_map/ppermute | solution.py:366
  17.3 11.2 %collective-permute-start.10 = (bf16[256,256]{1,0:T(8,128)(2,1)S(1)}, bf16[256,256]{1,0:T(8,128)(2,1)S(1)}, u32[]{:S(2)}, u32[]{:S(2)}) collective-permute-start(bf16[256,256]{1,0:T(8,128)(2,1)S(1)} %split.12), channel_id=1, source_target_pairs={{0,2},{2,3},{3,1},{1,0},{4,6},{6,7},{7,5},{5,4},{8,10},{10,11},{11... | collective-permute-start | bytes 393224 | tf_op jit(solution)/shard_map/ppermute | solution.py:366
  22.4 11.8 %collective-permute-start.12 = (bf16[4160,512]{1,0:T(8,128)(2,1)S(1)}, bf16[4160,512]{1,0:T(8,128)(2,1)S(1)}, u32[]{:S(2)}, u32[]{:S(2)}) collective-permute-start(bf16[4160,512]{1,0:T(8,128)(2,1)S(1)} %pack.1.refs_4_.refs_3_.refs_0_), channel_id=1, source_target_pairs={{0,4},{4,0},{1,5},{5,1},{2,6},{6,2},{3,7},{7,3},{8,12},{12,8},{9,1... | collective-permute-start | bytes 12779528 | tf_op jit(solution)/shard_map/ppermute | solution.py:319
  22.5 8.9 %collective-permute-start.14 = (bf16[256,256]{1,0:T(8,128)(2,1)S(1)}, bf16[256,256]{1,0:T(8,128)(2,1)S(1)}, u32[]{:S(2)}, u32[]{:S(2)}) collective-permute-start(bf16[256,256]{1,0:T(8,128)(2,1)S(1)} %split.14), channel_id=1, source_target_pairs={{0,2},{2,3},{3,1},{1,0},{4,6},{6,7},{7,5},{5,4},{8,10},{10,11},{11... | collective-permute-start | bytes 393224 | tf_op jit(solution)/shard_map/ppermute | solution.py:366
  23.2 13.4 %collective-permute-start.5 = (bf16[256,256]{1,0:T(8,128)(2,1)S(1)}, bf16[256,256]{1,0:T(8,128)(2,1)S(1)}, u32[]{:S(2)}, u32[]{:S(2)}) collective-permute-start(bf16[256,256]{1,0:T(8,128)(2,1)S(1)} %split.9), channel_id=1, source_target_pairs={{0,2},{2,3},{3,1},{1,0},{4,6},{6,7},{7,5},{5,4},{8,10},{10,11},{11... | collective-permute-start | bytes 393224 | tf_op jit(solution)/shard_map/ppermute | solution.py:366
  25.8 10.9 %collective-permute-start.8 = (bf16[256,256]{1,0:T(8,128)(2,1)S(1)}, bf16[256,256]{1,0:T(8,128)(2,1)S(1)}, u32[]{:S(2)}, u32[]{:S(2)}) collective-permute-start(bf16[256,256]{1,0:T(8,128)(2,1)S(1)} %split.11), channel_id=1, source_target_pairs={{0,2},{2,3},{3,1},{1,0},{4,6},{6,7},{7,5},{5,4},{8,10},{10,11},{11... | collective-permute-start | bytes 393224 | tf_op jit(solution)/shard_map/ppermute | solution.py:366
  28.6 10.6 %collective-permute-start.11 = (bf16[256,256]{1,0:T(8,128)(2,1)S(1)}, bf16[256,256]{1,0:T(8,128)(2,1)S(1)}, u32[]{:S(2)}, u32[]{:S(2)}) collective-permute-start(bf16[256,256]{1,0:T(8,128)(2,1)S(1)} %split.13), channel_id=1, source_target_pairs={{0,2},{2,3},{3,1},{1,0},{4,6},{6,7},{7,5},{5,4},{8,10},{10,11},{11... | collective-permute-start | bytes 393224 | tf_op jit(solution)/shard_map/ppermute | solution.py:366
  31.4 9.8 %collective-permute-start.15 = (bf16[256,256]{1,0:T(8,128)(2,1)S(1)}, bf16[256,256]{1,0:T(8,128)(2,1)S(1)}, u32[]{:S(2)}, u32[]{:S(2)}) collective-permute-start(bf16[256,256]{1,0:T(8,128)(2,1)S(1)} %split.15), channel_id=1, source_target_pairs={{0,2},{2,3},{3,1},{1,0},{4,6},{6,7},{7,5},{5,4},{8,10},{10,11},{11... | collective-permute-start | bytes 393224 | tf_op jit(solution)/shard_map/ppermute | solution.py:366
  41.8 1.5 %collective-permute-start.16 = (f32[64,640]{1,0:T(8,128)S(1)}, f32[64,640]{1,0:T(8,128)S(1)}, u32[]{:S(2)}, u32[]{:S(2)}) collective-permute-start(f32[64,640]{1,0:T(8,128)S(1)} %get-tuple-element.38), channel_id=1, source_target_pairs={{4,0},{0,4},{5,1},{1,5},{6,2},{2,6},{7,3},{3,7},{12,8},{8,12},{13,... | collective-permute-start | bytes 491528 | tf_op jit(solution)/shard_map/ppermute | solution.py:383

commit v23 on v22

--- a/solution.py
+++ b/solution.py
@@ -258,41 +258,65 @@
     )
 
 
-def cross_kernel(acc_ref, e_ref, map_ref, tgt_ref, mask_ref, *outs):
+def attend_memory(queries, memory, same):
+    heads = len(queries)
+    scores = [dot_t(q, k) for q, k in zip(queries, memory[:heads])]
+    tops, weights, totals = zip(*[softmax_block(x, same) for x in scores])
+    summed = [dot(w.astype(BF16), v) for w, v in zip(weights, memory[heads:])]
+    lane = lax.broadcasted_iota(jnp.int32, (same.shape[0], LANES), 1)
+    stats = jnp.zeros(lane.shape, F32)
+    for h in range(heads):
+        stats = jnp.where(lane == h, tops[h], jnp.where(lane == heads + h, totals[h], stats))
+    return jnp.concatenate([*summed, stats], axis=1)
+
+
+def cross_near_kernel(acc_ref, e_ref, map_ref, tgt_ref, mask_ref, mem_ref, *outs):
     heads = map_ref.shape[1] // 2 // HEAD_DIM
+    count = outs[0].shape[0]
     chunk = e_ref[...]
-    queries = [tgt_ref[:, head_columns(h)] for h in range(heads)]
+    parts = [slice((i + 1) * count, (i + 2) * count) for i in range(len(outs))]
+    queries = [[tgt_ref[part, head_columns(h)] for h in range(heads)] for part in parts]
+    same = [mask_ref[part, :] > 0 for part in parts]
     memory = []
     for h in range(2 * heads):
         at = head_columns(h)
         memory.append((acc_ref[:, at] + dot(chunk, map_ref[:, at])).astype(BF16))
-    keys, values = memory[:heads], memory[heads:]
-    count = outs[0].shape[0]
-    same = mask_ref[...] > 0
-    scores = [dot_t(queries[h], keys[h]) for h in range(heads)]
-    tops, weights, totals = zip(*[softmax_block(x, same) for x in scores])
-    summed = [dot(w.astype(BF16), v) for w, v in zip(weights, values)]
-    lane = lax.broadcasted_iota(jnp.int32, (same.shape[0], LANES), 1)
-    stats = jnp.zeros(lane.shape, F32)
-    for h in range(heads):
-        stats = jnp.where(lane == h, tops[h], jnp.where(lane == heads + h, totals[h], stats))
-    for i, out_ref in enumerate(outs):
-        part = slice(i * count, (i + 1) * count)
-        for h in range(heads):
-            out_ref[:, head_columns(h)] = summed[h][part]
-        out_ref[:, heads * HEAD_DIM :] = stats[part]
-
-
-def cross_attend(acc, chunk, maps, targets, mask, parts):
+    shares = [attend_memory(q, memory, m) for q, m in zip(queries, same)]
+    for out_ref, share in zip(outs, shares):
+        out_ref[...] = share
+    for h in range(2 * heads):
+        mem_ref[:, head_columns(h)] = memory[h]
+
+
+def cross_near(acc, chunk, maps, targets, mask, parts):
     width = targets.shape[1]
-    count = targets.shape[0] // parts
-    return call(
-        cross_kernel,
-        "cross_attend",
-        [((count, width + LANES), F32)] * parts,
+    share = ((targets.shape[0] // parts, width + LANES), F32)
+    return call(
+        cross_near_kernel,
+        "cross_near",
+        [((acc.shape[0], 2 * width), BF16)] + [share] * (parts - 1),
         [acc, chunk, maps, targets, mask],
         flops=2 * chunk.size * 2 * width,
     )
+
+
+def cross_own_kernel(mem_ref, tgt_ref, mask_ref, out_ref):
+    heads = mem_ref.shape[1] // 2 // HEAD_DIM
+    count = out_ref.shape[0]
+    memory = [mem_ref[:, head_columns(h)] for h in range(2 * heads)]
+    queries = [tgt_ref[:count, head_columns(h)] for h in range(heads)]
+    out_ref[...] = attend_memory(queries, memory, mask_ref[:count, :] > 0)
+
+
+def cross_own(memory, targets, mask, parts):
+    count, width = targets.shape[0] // parts, targets.shape[1]
+    return call(
+        cross_own_kernel,
+        "cross_own",
+        [((count, width + LANES), F32)],
+        [memory, targets, mask],
+        flops=4 * count * width * memory.shape[0],
+    )[0]
 
 
 def combine_kernel(*refs):
@@ -377,8 +401,8 @@
         near_targets,
         [marks, *near_marks],
     )
-    own, *shares = cross_attend(acc, held[-1], last_maps, targets, mask, 1 + len(links))
-    combined = [own]
+    memory, *shares = cross_near(acc, held[-1], last_maps, targets, mask, 1 + len(links))
+    combined = [cross_own(memory, targets, mask, 1 + len(links))]
     for i, (pairs, piece) in enumerate(zip(links, shares)):
         other = lax.ppermute(piece, "ctx", [(target, source) for source, target in pairs])
         if n_ctx > 2:

time: 44.2 us -> 44.2 us (level)
    pallas_call x23 -> x24, Pallas kernels: 10.3 us -> 10.7 us  [call(): pl.pallas_call(kernel, in_specs=specs or [VMEM] * len(operands), out_spec...]
  transfers between devices with their start and end apart: 17 -> 17, of which waited for: 4 -> 4; matrix products, arithmetic and copies ran while one was open for 0% -> 0% of each run, Pallas kernels for 19% -> 20%
where the time goes in v23:
time: 44.2 us; the launch traced here: 44.1 us
  starting transfers between devices  27.8 us (63%)
  Pallas kernels  10.7 us (24%)
  waiting for transfers between devices  5.38 us (12%)
    ppermute x8, starting transfers between devices, on_device(): later = [lax.ppermute(p, 'head', ring) for p in pieces]  20.6 us
    pallas_call x24, Pallas kernels, call(): pl.pallas_call(kernel, in_specs=specs or [VMEM] * len(operands), out_spec...  10.7 us
    ppermute x4, starting transfers between devices, on_device(): sent, held = (held, [lax.ppermute(h, 'head', ring) for h in held])  6.07 us
    ppermute x8, waiting for transfers between devices, on_device(): later = [lax.ppermute(p, 'head', ring) for p in pieces]  3.94 us
    ppermute x4, starting transfers between devices, on_device(): bring = lambda x: [lax.ppermute(x, 'ctx', pairs) for pairs in links]  1.03 us
    ppermute x1, waiting for transfers between devices, on_device(): lax.ppermute(piece, 'ctx', [(target, source) for source, target in pairs])  0.96 us
  transfers between devices with their start and end apart: 17, of which 4 were waited for; matrix products, arithmetic and copies ran while one was open for 0% of the time, Pallas kernels for 20%

profile of v23, /device:TPU:0, one launch (start us, length us, event | category | flops | bytes accessed | tf_op | source)
XLA Modules:
  0.0 44.1 jit_solution(12969251537118617423)
XLA Ops:
  1.0 1.4 %fetch.1 = (bf16[256,1024]{1,0:T(8,128)(2,1)S(1)}, bf16[256,1024]{1,0:T(8,128)(2,1)S(1)}, bf16[256,1024]{1,0:T(8,128)(2,1)S(1)}, s32[1,256]{1,0:T(1,128)S(1)}) custom-call(bf16[256,1024]{1,0:T(8,128)(2,1)} %refs_0_.1, bf16[256,1024]{1,0:T(8,128)(2,1)} %refs_1_.1, bf16[256,1024]{1,0:T(8,128)(2,1)} %refs_2_.1, s32[1,256]{1,0:T(1,128)} %bitcast.2), custom_call_target="tpu_custom_call" | custom-call | bytes 3147776 | tf_op jit(solution)/shard_map/fetch/pallas_call | solution.py:62
  2.4 0.6 %weigh.2 = (bf16[256,1024]{1,0:T(8,128)(2,1)S(1)}, f32[256,128]{1,0:T(8,128)S(1)}) custom-call(s32[1,256]{1,0:T(1,128)S(1)} %get-tuple-element.22.refs_0_.refs_2_, s32[1,256]{1,0:T(1,128)S(1)} %collective-permute-done.refs_1_.refs_3_, bf16[256,1024]{1,0:T(8,128)(2,1)S(1)} %get-tuple-element.23.refs_2_, bf16[256,1024]{1,0:T(8,128)(2,1)S(1)} %get-tuple-element.24.refs_3_, ...), custom_call_target="tpu_custom_call" | custom-call | flops 6000000000 | bytes 2230272 | tf_op jit(solution)/shard_map/weigh/pallas_call | solution.py:62
  3.2 4.0 %collective-permute-start.3 = (bf16[256,256]{1,0:T(8,128)(2,1)S(1)}, bf16[256,256]{1,0:T(8,128)(2,1)S(1)}, u32[]{:S(2)}, u32[]{:S(2)}) collective-permute-start(bf16[256,256]{1,0:T(8,128)(2,1)S(1)} %mix.4.refs_0_), channel_id=1, source_target_pairs={{0,2},{2,3},{3,1},{1,0},{4,6},{6,7},{7,5},{5,4},{8,10},{10,11},{11... | collective-permute-start | bytes 393224 | tf_op jit(solution)/shard_map/ppermute | solution.py:361
  7.5 1.6 %collective-permute-start.6 = (bf16[256,256]{1,0:T(8,128)(2,1)S(1)}, bf16[256,256]{1,0:T(8,128)(2,1)S(1)}, u32[]{:S(2)}, u32[]{:S(2)}) collective-permute-start(bf16[256,256]{1,0:T(8,128)(2,1)S(1)} %mix.5.refs_1_), channel_id=1, source_target_pairs={{0,2},{2,3},{3,1},{1,0},{4,6},{6,7},{7,5},{5,4},{8,10},{10,11},{11... | collective-permute-start | bytes 393224 | tf_op jit(solution)/shard_map/ppermute | solution.py:361
  9.1 0.6 %weigh.3 = (bf16[256,1024]{1,0:T(8,128)(2,1)S(1)}, f32[256,128]{1,0:T(8,128)S(1)}) custom-call(s32[1,256]{1,0:T(1,128)S(1)} %get-tuple-element.22.refs_0_.refs_2_, s32[1,256]{1,0:T(1,128)S(1)} %collective-permute-done.refs_1_.refs_3_, bf16[256,1024]{1,0:T(8,128)(2,1)S(1)} %get-tuple-element.23.refs_2_, bf16[256,1024]{1,0:T(8,128)(2,1)S(1)} %get-tuple-element.24.refs_3_, ...), custom_call_target="tpu_custom_call" | custom-call | flops 6000000000 | bytes 2230272 | tf_op jit(solution)/shard_map/weigh/pallas_call | solution.py:62
  10.6 0.5 %collective-permute-done.3.source.refs_0_ = bf16[256,256]{1,0:T(8,128)(2,1)S(1)} collective-permute-done((bf16[256,256]{1,0:T(8,128)(2,1)S(1)}, bf16[256,256]{1,0:T(8,128)(2,1)S(1)}, u32[]{:S(2)}, u32[]{:S(2)}) %collective-permute-start.3) | collective-permute-done | bytes 131104 | tf_op jit(solution)/shard_map/ppermute | solution.py:361
  11.1 3.4 %collective-permute-start.4 = (bf16[256,256]{1,0:T(8,128)(2,1)S(1)}, bf16[256,256]{1,0:T(8,128)(2,1)S(1)}, u32[]{:S(2)}, u32[]{:S(2)}) collective-permute-start(bf16[256,256]{1,0:T(8,128)(2,1)S(1)} %split.8), channel_id=1, source_target_pairs={{0,2},{2,3},{3,1},{1,0},{4,6},{6,7},{7,5},{5,4},{8,10},{10,11},{11... | collective-permute-start | bytes 393224 | tf_op jit(solution)/shard_map/ppermute | solution.py:390
  14.5 2.8 %collective-permute-start.7 = (bf16[256,256]{1,0:T(8,128)(2,1)S(1)}, bf16[256,256]{1,0:T(8,128)(2,1)S(1)}, u32[]{:S(2)}, u32[]{:S(2)}) collective-permute-start(bf16[256,256]{1,0:T(8,128)(2,1)S(1)} %split.10), channel_id=1, source_target_pairs={{0,2},{2,3},{3,1},{1,0},{4,6},{6,7},{7,5},{5,4},{8,10},{10,11},{11... | collective-permute-start | bytes 393224 | tf_op jit(solution)/shard_map/ppermute | solution.py:390
  17.3 2.8 %collective-permute-start.10 = (bf16[256,256]{1,0:T(8,128)(2,1)S(1)}, bf16[256,256]{1,0:T(8,128)(2,1)S(1)}, u32[]{:S(2)}, u32[]{:S(2)}) collective-permute-start(bf16[256,256]{1,0:T(8,128)(2,1)S(1)} %split.12), channel_id=1, source_target_pairs={{0,2},{2,3},{3,1},{1,0},{4,6},{6,7},{7,5},{5,4},{8,10},{10,11},{11... | collective-permute-start | bytes 393224 | tf_op jit(solution)/shard_map/ppermute | solution.py:390
  20.1 2.2 %pack.1.refs_4_.refs_3_.refs_0_ = bf16[4160,512]{1,0:T(8,128)(2,1)S(1)} custom-call(bf16[2048,512]{1,0:T(8,128)(2,1)} %refs_0_.2, bf16[2048,512]{1,0:T(8,128)(2,1)} %refs_1_.2, bf16[64,512]{1,0:T(8,128)(2,1)} %refs_2_.2), custom_call_target="tpu_custom_call" | custom-call | bytes 8519680 | tf_op jit(solution)/shard_map/pack/pallas_call | solution.py:62
  22.5 0.7 %collective-permute-start.14 = (bf16[256,256]{1,0:T(8,128)(2,1)S(1)}, bf16[256,256]{1,0:T(8,128)(2,1)S(1)}, u32[]{:S(2)}, u32[]{:S(2)}) collective-permute-start(bf16[256,256]{1,0:T(8,128)(2,1)S(1)} %split.14), channel_id=1, source_target_pairs={{0,2},{2,3},{3,1},{1,0},{4,6},{6,7},{7,5},{5,4},{8,10},{10,11},{11... | collective-permute-start | bytes 393224 | tf_op jit(solution)/shard_map/ppermute | solution.py:390
  23.2 2.5 %collective-permute-start.5 = (bf16[256,256]{1,0:T(8,128)(2,1)S(1)}, bf16[256,256]{1,0:T(8,128)(2,1)S(1)}, u32[]{:S(2)}, u32[]{:S(2)}) collective-permute-start(bf16[256,256]{1,0:T(8,128)(2,1)S(1)} %split.9), channel_id=1, source_target_pairs={{0,2},{2,3},{3,1},{1,0},{4,6},{6,7},{7,5},{5,4},{8,10},{10,11},{11... | collective-permute-start | bytes 393224 | tf_op jit(solution)/shard_map/ppermute | solution.py:390
  25.8 2.8 %collective-permute-start.8 = (bf16[256,256]{1,0:T(8,128)(2,1)S(1)}, bf16[256,256]{1,0:T(8,128)(2,1)S(1)}, u32[]{:S(2)}, u32[]{:S(2)}) collective-permute-start(bf16[256,256]{1,0:T(8,128)(2,1)S(1)} %split.11), channel_id=1, source_target_pairs={{0,2},{2,3},{3,1},{1,0},{4,6},{6,7},{7,5},{5,4},{8,10},{10,11},{11... | collective-permute-start | bytes 393224 | tf_op jit(solution)/shard_map/ppermute | solution.py:390
  28.6 2.8 %collective-permute-start.11 = (bf16[256,256]{1,0:T(8,128)(2,1)S(1)}, bf16[256,256]{1,0:T(8,128)(2,1)S(1)}, u32[]{:S(2)}, u32[]{:S(2)}) collective-permute-start(bf16[256,256]{1,0:T(8,128)(2,1)S(1)} %split.13), channel_id=1, source_target_pairs={{0,2},{2,3},{3,1},{1,0},{4,6},{6,7},{7,5},{5,4},{8,10},{10,11},{11... | collective-permute-start | bytes 393224 | tf_op jit(solution)/shard_map/ppermute | solution.py:390
  31.4 2.8 %collective-permute-start.15 = (bf16[256,256]{1,0:T(8,128)(2,1)S(1)}, bf16[256,256]{1,0:T(8,128)(2,1)S(1)}, u32[]{:S(2)}, u32[]{:S(2)}) collective-permute-start(bf16[256,256]{1,0:T(8,128)(2,1)S(1)} %split.15), channel_id=1, source_target_pairs={{0,2},{2,3},{3,1},{1,0},{4,6},{6,7},{7,5},{5,4},{8,10},{10,11},{11... | collective-permute-start | bytes 393224 | tf_op jit(solution)/shard_map/ppermute | solution.py:390
  34.4 0.7 %project.4.refs_6_ = f32[256,1024]{1,0:T(8,128)S(1)} custom-call(bf16[256,256]{1,0:T(8,128)(2,1)S(1)} %mix.4.refs_0_, bf16[256,256]{1,0:T(8,128)(2,1)S(1)} %mix.5.refs_1_, bf16[256,256]{1,0:T(8,128)(2,1)S(1)} %mix.6.refs_2_, bf16[256,256]{1,0:T(8,128)(2,1)S(1)} %mix.7.refs_3_, bf16[4160,512]{1,0:T(8,128)(2,1)S(1)} %pack.1.refs_4_.refs_3_.refs_0_, ...), custom_call_target="tpu_custom_call" | custom-call | flops 536870912 | bytes 10092544 | tf_op jit(solution)/shard_map/project/pallas_call | solution.py:62
  35.1 0.7 %project.5.refs_6_ = f32[256,1024]{1,0:T(8,128)S(1)} custom-call(bf16[256,256]{1,0:T(8,128)(2,1)S(1)} %collective-permute-done.3.source.refs_0_, bf16[256,256]{1,0:T(8,128)(2,1)S(1)} %collective-permute-done.6.source.refs_1_, bf16[256,256]{1,0:T(8,128)(2,1)S(1)} %collective-permute-done.9.source.refs_2_, ...), custom_call_target="tpu_custom_call" | custom-call | flops 536870912 | bytes 11141120 | tf_op jit(solution)/shard_map/project/pallas_call | solution.py:62
  35.9 0.7 %project.6.refs_5_ = f32[256,1024]{1,0:T(8,128)S(1)} custom-call(bf16[256,256]{1,0:T(8,128)(2,1)S(1)} %collective-permute-done.4.source.refs_0_, bf16[256,256]{1,0:T(8,128)(2,1)S(1)} %collective-permute-done.7.source.refs_1_, bf16[256,256]{1,0:T(8,128)(2,1)S(1)} %collective-permute-done.10.source.refs_2_, ...), custom_call_target="tpu_custom_call" | custom-call | flops 536870912 | bytes 11141120 | tf_op jit(solution)/shard_map/project/pallas_call | solution.py:62
  36.7 2.5 %collective-permute-done.11.refs_2_ = bf16[256,256]{1,0:T(8,128)(2,1)S(1)} collective-permute-done((bf16[256,256]{1,0:T(8,128)(2,1)S(1)}, bf16[256,256]{1,0:T(8,128)(2,1)S(1)}, u32[]{:S(2)}, u32[]{:S(2)}) %collective-permute-start.11) | collective-permute-done | bytes 131104 | tf_op jit(solution)/shard_map/ppermute | solution.py:390
  39.2 0.6 %project.7.acc_ref = f32[256,1024]{1,0:T(8,128)S(1)} custom-call(bf16[256,256]{1,0:T(8,128)(2,1)S(1)} %collective-permute-done.5.refs_0_, bf16[256,256]{1,0:T(8,128)(2,1)S(1)} %collective-permute-done.8.refs_1_, bf16[256,256]{1,0:T(8,128)(2,1)S(1)} %collective-permute-done.11.refs_2_, bf16[4160,512]{1,0:T(8,128)(2,1)S(1)} %pack.1.refs_4_.refs_3_.refs_0_, ...), custom_call_target="tpu_custom_call" | custom-call | flops 402653184 | bytes 11010048 | tf_op jit(solution)/shard_map/project/pallas_call | solution.py:62
  39.8 1.4 %collective-permute-done.15.e_ref = bf16[256,256]{1,0:T(8,128)(2,1)S(1)} collective-permute-done((bf16[256,256]{1,0:T(8,128)(2,1)S(1)}, bf16[256,256]{1,0:T(8,128)(2,1)S(1)}, u32[]{:S(2)}, u32[]{:S(2)}) %collective-permute-start.15) | collective-permute-done | bytes 131104 | tf_op jit(solution)/shard_map/ppermute | solution.py:390
  41.2 0.6 %cross_near.1 = (bf16[256,1024]{1,0:T(8,128)(2,1)S(1)}, f32[64,640]{1,0:T(8,128)S(1)}) custom-call(f32[256,1024]{1,0:T(8,128)S(1)} %project.7.acc_ref, bf16[256,256]{1,0:T(8,128)(2,1)S(1)} %collective-permute-done.15.e_ref, bf16[256,1024]{1,0:T(8,128)(2,1)S(1)} %get-tuple-element.34.map_ref, bf16[128,512]{1,0:T(8,128)(2,1)S(1)} %get-tuple-element.35.tgt_ref, ...), custom_call_target="tpu_custom_call" | custom-call | flops 134217728 | bytes 2654208 | tf_op jit(solution)/shard_map/cross_near/pallas_call | solution.py:62
  42.3 1.0 %collective-permute-done.16.refs_1_ = f32[64,640]{1,0:T(8,128)S(1)} collective-permute-done((f32[64,640]{1,0:T(8,128)S(1)}, f32[64,640]{1,0:T(8,128)S(1)}, u32[]{:S(2)}, u32[]{:S(2)}) %collective-permute-start.16) | collective-permute-done | bytes 163872 | tf_op jit(solution)/shard_map/ppermute | solution.py:407
  43.2 0.8 %combine.1 = bf16[64,512]{1,0:T(8,128)(2,1)} custom-call(f32[64,640]{1,0:T(8,128)S(1)} %cross_own.1.refs_0_, f32[64,640]{1,0:T(8,128)S(1)} %collective-permute-done.16.refs_1_), custom_call_target="tpu_custom_call" | custom-call | bytes 393216 | tf_op jit(solution)/shard_map/combine/pallas_call | solution.py:62
  (34 shorter events, 3.2 us)
Async XLA Ops:
  0.0 2.4 %collective-permute-start.1 = (bf16[256,1024]{1,0:T(8,128)(2,1)}, bf16[256,1024]{1,0:T(8,128)(2,1)S(1)}, u32[]{:S(2)}, u32[]{:S(2)}) collective-permute-start(bf16[256,1024]{1,0:T(8,128)(2,1)} %refs_1_.1), channel_id=1, source_target_pairs={{0,4},{4,0},{1,5},{5,1},{2,6},{6,2},{3,7},{7,3},{8,12},{12,8},{9,1... | collective-permute-start | bytes 1572872 | tf_op jit(solution)/shard_map/ppermute | solution.py:343
  0.5 1.9 %collective-permute-start = (s32[1,256]{1,0:T(1,128)}, s32[1,256]{1,0:T(1,128)S(1)}, u32[]{:S(2)}, u32[]{:S(2)}) collective-permute-start(s32[1,256]{1,0:T(1,128)} %bitcast.1), channel_id=1, source_target_pairs={{0,4},{4,0},{1,5},{5,1},{2,6},{6,2},{3,7},{7,3},{8,12},{12,8},{9,1... | collective-permute-start | bytes 3080 | tf_op jit(solution)/shard_map/ppermute | solution.py:343
  0.5 2.4 %collective-permute-start.2 = (bf16[256,1024]{1,0:T(8,128)(2,1)}, bf16[256,1024]{1,0:T(8,128)(2,1)S(1)}, u32[]{:S(2)}, u32[]{:S(2)}) collective-permute-start(bf16[256,1024]{1,0:T(8,128)(2,1)} %refs_2_.1), channel_id=1, source_target_pairs={{0,4},{4,0},{1,5},{5,1},{2,6},{6,2},{3,7},{7,3},{8,12},{12,8},{9,1... | collective-permute-start | bytes 1572872 | tf_op jit(solution)/shard_map/ppermute | solution.py:343
  3.2 7.9 %collective-permute-start.3 = (bf16[256,256]{1,0:T(8,128)(2,1)S(1)}, bf16[256,256]{1,0:T(8,128)(2,1)S(1)}, u32[]{:S(2)}, u32[]{:S(2)}) collective-permute-start(bf16[256,256]{1,0:T(8,128)(2,1)S(1)} %mix.4.refs_0_), channel_id=1, source_target_pairs={{0,2},{2,3},{3,1},{1,0},{4,6},{6,7},{7,5},{5,4},{8,10},{10,11},{11... | collective-permute-start | bytes 393224 | tf_op jit(solution)/shard_map/ppermute | solution.py:361
  7.5 7.1 %collective-permute-start.6 = (bf16[256,256]{1,0:T(8,128)(2,1)S(1)}, bf16[256,256]{1,0:T(8,128)(2,1)S(1)}, u32[]{:S(2)}, u32[]{:S(2)}) collective-permute-start(bf16[256,256]{1,0:T(8,128)(2,1)S(1)} %mix.5.refs_1_), channel_id=1, source_target_pairs={{0,2},{2,3},{3,1},{1,0},{4,6},{6,7},{7,5},{5,4},{8,10},{10,11},{11... | collective-permute-start | bytes 393224 | tf_op jit(solution)/shard_map/ppermute | solution.py:361
  9.9 7.4 %collective-permute-start.9 = (bf16[256,256]{1,0:T(8,128)(2,1)S(1)}, bf16[256,256]{1,0:T(8,128)(2,1)S(1)}, u32[]{:S(2)}, u32[]{:S(2)}) collective-permute-start(bf16[256,256]{1,0:T(8,128)(2,1)S(1)} %mix.6.refs_2_), channel_id=1, source_target_pairs={{0,2},{2,3},{3,1},{1,0},{4,6},{6,7},{7,5},{5,4},{8,10},{10,11},{11... | collective-permute-start | bytes 393224 | tf_op jit(solution)/shard_map/ppermute | solution.py:361
  10.5 11.9 %collective-permute-start.13 = (bf16[256,256]{1,0:T(8,128)(2,1)S(1)}, bf16[256,256]{1,0:T(8,128)(2,1)S(1)}, u32[]{:S(2)}, u32[]{:S(2)}) collective-permute-start(bf16[256,256]{1,0:T(8,128)(2,1)S(1)} %mix.7.refs_3_), channel_id=1, source_target_pairs={{0,2},{2,3},{3,1},{1,0},{4,6},{6,7},{7,5},{5,4},{8,10},{10,11},{11... | collective-permute-start | bytes 393224 | tf_op jit(solution)/shard_map/ppermute | solution.py:361
  11.1 12.1 %collective-permute-start.4 = (bf16[256,256]{1,0:T(8,128)(2,1)S(1)}, bf16[256,256]{1,0:T(8,128)(2,1)S(1)}, u32[]{:S(2)}, u32[]{:S(2)}) collective-permute-start(bf16[256,256]{1,0:T(8,128)(2,1)S(1)} %split.8), channel_id=1, source_target_pairs={{0,2},{2,3},{3,1},{1,0},{4,6},{6,7},{7,5},{5,4},{8,10},{10,11},{11... | collective-permute-start | bytes 393224 | tf_op jit(solution)/shard_map/ppermute | solution.py:390
  14.5 11.2 %collective-permute-start.7 = (bf16[256,256]{1,0:T(8,128)(2,1)S(1)}, bf16[256,256]{1,0:T(8,128)(2,1)S(1)}, u32[]{:S(2)}, u32[]{:S(2)}) collective-permute-start(bf16[256,256]{1,0:T(8,128)(2,1)S(1)} %split.10), channel_id=1, source_target_pairs={{0,2},{2,3},{3,1},{1,0},{4,6},{6,7},{7,5},{5,4},{8,10},{10,11},{11... | collective-permute-start | bytes 393224 | tf_op jit(solution)/shard_map/ppermute | solution.py:390
  17.3 11.2 %collective-permute-start.10 = (bf16[256,256]{1,0:T(8,128)(2,1)S(1)}, bf16[256,256]{1,0:T(8,128)(2,1)S(1)}, u32[]{:S(2)}, u32[]{:S(2)}) collective-permute-start(bf16[256,256]{1,0:T(8,128)(2,1)S(1)} %split.12), channel_id=1, source_target_pairs={{0,2},{2,3},{3,1},{1,0},{4,6},{6,7},{7,5},{5,4},{8,10},{10,11},{11... | collective-permute-start | bytes 393224 | tf_op jit(solution)/shard_map/ppermute | solution.py:390
  22.4 11.8 %collective-permute-start.12 = (bf16[4160,512]{1,0:T(8,128)(2,1)S(1)}, bf16[4160,512]{1,0:T(8,128)(2,1)S(1)}, u32[]{:S(2)}, u32[]{:S(2)}) collective-permute-start(bf16[4160,512]{1,0:T(8,128)(2,1)S(1)} %pack.1.refs_4_.refs_3_.refs_0_), channel_id=1, source_target_pairs={{0,4},{4,0},{1,5},{5,1},{2,6},{6,2},{3,7},{7,3},{8,12},{12,8},{9,1... | collective-permute-start | bytes 12779528 | tf_op jit(solution)/shard_map/ppermute | solution.py:343
  22.5 8.9 %collective-permute-start.14 = (bf16[256,256]{1,0:T(8,128)(2,1)S(1)}, bf16[256,256]{1,0:T(8,128)(2,1)S(1)}, u32[]{:S(2)}, u32[]{:S(2)}) collective-permute-start(bf16[256,256]{1,0:T(8,128)(2,1)S(1)} %split.14), channel_id=1, source_target_pairs={{0,2},{2,3},{3,1},{1,0},{4,6},{6,7},{7,5},{5,4},{8,10},{10,11},{11... | collective-permute-start | bytes 393224 | tf_op jit(solution)/shard_map/ppermute | solution.py:390
  23.2 13.4 %collective-permute-start.5 = (bf16[256,256]{1,0:T(8,128)(2,1)S(1)}, bf16[256,256]{1,0:T(8,128)(2,1)S(1)}, u32[]{:S(2)}, u32[]{:S(2)}) collective-permute-start(bf16[256,256]{1,0:T(8,128)(2,1)S(1)} %split.9), channel_id=1, source_target_pairs={{0,2},{2,3},{3,1},{1,0},{4,6},{6,7},{7,5},{5,4},{8,10},{10,11},{11... | collective-permute-start | bytes 393224 | tf_op jit(solution)/shard_map/ppermute | solution.py:390
  25.8 10.9 %collective-permute-start.8 = (bf16[256,256]{1,0:T(8,128)(2,1)S(1)}, bf16[256,256]{1,0:T(8,128)(2,1)S(1)}, u32[]{:S(2)}, u32[]{:S(2)}) collective-permute-start(bf16[256,256]{1,0:T(8,128)(2,1)S(1)} %split.11), channel_id=1, source_target_pairs={{0,2},{2,3},{3,1},{1,0},{4,6},{6,7},{7,5},{5,4},{8,10},{10,11},{11... | collective-permute-start | bytes 393224 | tf_op jit(solution)/shard_map/ppermute | solution.py:390
  28.6 10.6 %collective-permute-start.11 = (bf16[256,256]{1,0:T(8,128)(2,1)S(1)}, bf16[256,256]{1,0:T(8,128)(2,1)S(1)}, u32[]{:S(2)}, u32[]{:S(2)}) collective-permute-start(bf16[256,256]{1,0:T(8,128)(2,1)S(1)} %split.13), channel_id=1, source_target_pairs={{0,2},{2,3},{3,1},{1,0},{4,6},{6,7},{7,5},{5,4},{8,10},{10,11},{11... | collective-permute-start | bytes 393224 | tf_op jit(solution)/shard_map/ppermute | solution.py:390
  31.4 9.8 %collective-permute-start.15 = (bf16[256,256]{1,0:T(8,128)(2,1)S(1)}, bf16[256,256]{1,0:T(8,128)(2,1)S(1)}, u32[]{:S(2)}, u32[]{:S(2)}) collective-permute-start(bf16[256,256]{1,0:T(8,128)(2,1)S(1)} %split.15), channel_id=1, source_target_pairs={{0,2},{2,3},{3,1},{1,0},{4,6},{6,7},{7,5},{5,4},{8,10},{10,11},{11... | collective-permute-start | bytes 393224 | tf_op jit(solution)/shard_map/ppermute | solution.py:390
  41.8 1.5 %collective-permute-start.16 = (f32[64,640]{1,0:T(8,128)S(1)}, f32[64,640]{1,0:T(8,128)S(1)}, u32[]{:S(2)}, u32[]{:S(2)}) collective-permute-start(f32[64,640]{1,0:T(8,128)S(1)} %get-tuple-element.38), channel_id=1, source_target_pairs={{4,0},{0,4},{5,1},{1,5},{6,2},{2,6},{7,3},{3,7},{12,8},{8,12},{13,... | collective-permute-start | bytes 491528 | tf_op jit(solution)/shard_map/ppermute | solution.py:407

commit v24 on v23

--- a/solution.py
+++ b/solution.py
@@ -386,7 +386,7 @@
     acc = project(None, sent, functools.partial(place, 0, 0), shards, map_rows)
     arrived = [arrived, *held[1:]]
     for turn in range(1, last):
-        pieces = [p for h in held for p in split(h, h.shape[1] // HEAD_DIM)]
+        pieces = [p for h in held[:-1] for p in split(h, 1)] + list(split(held[-1], 2 if turn == last - 1 else 1))
         later = [lax.ppermute(p, "head", ring) for p in pieces]
         acc = project(acc, arrived, functools.partial(place, turn, 0), shards, map_rows)
         held = arrived = later

time: 44.2 us -> 44.2 us (level)
  waiting for transfers between devices: 5.38 us -> 4.62 us
  starting transfers between devices: 27.8 us -> 28.5 us
    ppermute x8 -> x9, waiting for transfers between devices: 3.94 us -> 3.18 us  [on_device(): later = [lax.ppermute(p, 'head', ring) for p in pieces]]
    ppermute x8 -> x9, starting transfers between devices: 20.6 us -> 21.3 us  [on_device(): later = [lax.ppermute(p, 'head', ring) for p in pieces]]
  transfers between devices with their start and end apart: 17 -> 18, of which waited for: 4 -> 3; matrix products, arithmetic and copies ran while one was open for 0% -> 0% of each run, Pallas kernels for 20% -> 21%
where the time goes in v24:
time: 44.2 us; the launch traced here: 44.1 us
  starting transfers between devices  28.5 us (64%)
  Pallas kernels  10.8 us (24%)
  waiting for transfers between devices  4.62 us (10%)
    ppermute x9, starting transfers between devices, on_device(): later = [lax.ppermute(p, 'head', ring) for p in pieces]  21.3 us
    pallas_call x24, Pallas kernels, call(): pl.pallas_call(kernel, in_specs=specs or [VMEM] * len(operands), out_spec...  10.8 us
    ppermute x4, starting transfers between devices, on_device(): sent, held = (held, [lax.ppermute(h, 'head', ring) for h in held])  6.07 us
    ppermute x9, waiting for transfers between devices, on_device(): later = [lax.ppermute(p, 'head', ring) for p in pieces]  3.18 us
    ppermute x4, starting transfers between devices, on_device(): bring = lambda x: [lax.ppermute(x, 'ctx', pairs) for pairs in links]  1.03 us
    ppermute x1, waiting for transfers between devices, on_device(): lax.ppermute(piece, 'ctx', [(target, source) for source, target in pairs])  0.96 us
  transfers between devices with their start and end apart: 18, of which 3 were waited for; matrix products, arithmetic and copies ran while one was open for 0% of the time, Pallas kernels for 21%

profile of v24, /device:TPU:0, one launch (start us, length us, event | category | flops | bytes accessed | tf_op | source)
XLA Modules:
  0.0 44.1 jit_solution(16754916901437204773)
XLA Ops:
  1.0 1.4 %fetch.1 = (bf16[256,1024]{1,0:T(8,128)(2,1)S(1)}, bf16[256,1024]{1,0:T(8,128)(2,1)S(1)}, bf16[256,1024]{1,0:T(8,128)(2,1)S(1)}, s32[1,256]{1,0:T(1,128)S(1)}) custom-call(bf16[256,1024]{1,0:T(8,128)(2,1)} %refs_0_.1, bf16[256,1024]{1,0:T(8,128)(2,1)} %refs_1_.1, bf16[256,1024]{1,0:T(8,128)(2,1)} %refs_2_.1, s32[1,256]{1,0:T(1,128)} %bitcast.2), custom_call_target="tpu_custom_call" | custom-call | bytes 3147776 | tf_op jit(solution)/shard_map/fetch/pallas_call | solution.py:62
  2.4 0.6 %weigh.2 = (bf16[256,1024]{1,0:T(8,128)(2,1)S(1)}, f32[256,128]{1,0:T(8,128)S(1)}) custom-call(s32[1,256]{1,0:T(1,128)S(1)} %get-tuple-element.24.refs_0_.refs_2_, s32[1,256]{1,0:T(1,128)S(1)} %collective-permute-done.refs_1_.refs_3_, bf16[256,1024]{1,0:T(8,128)(2,1)S(1)} %get-tuple-element.25.refs_2_, bf16[256,1024]{1,0:T(8,128)(2,1)S(1)} %get-tuple-element.26.refs_3_, ...), custom_call_target="tpu_custom_call" | custom-call | flops 6000000000 | bytes 2230272 | tf_op jit(solution)/shard_map/weigh/pallas_call | solution.py:62
  3.2 4.0 %collective-permute-start.3 = (bf16[256,256]{1,0:T(8,128)(2,1)S(1)}, bf16[256,256]{1,0:T(8,128)(2,1)S(1)}, u32[]{:S(2)}, u32[]{:S(2)}) collective-permute-start(bf16[256,256]{1,0:T(8,128)(2,1)S(1)} %mix.4.refs_0_), channel_id=1, source_target_pairs={{0,2},{2,3},{3,1},{1,0},{4,6},{6,7},{7,5},{5,4},{8,10},{10,11},{11... | collective-permute-start | bytes 393224 | tf_op jit(solution)/shard_map/ppermute | solution.py:361
  7.5 1.6 %collective-permute-start.6 = (bf16[256,256]{1,0:T(8,128)(2,1)S(1)}, bf16[256,256]{1,0:T(8,128)(2,1)S(1)}, u32[]{:S(2)}, u32[]{:S(2)}) collective-permute-start(bf16[256,256]{1,0:T(8,128)(2,1)S(1)} %mix.5.refs_1_), channel_id=1, source_target_pairs={{0,2},{2,3},{3,1},{1,0},{4,6},{6,7},{7,5},{5,4},{8,10},{10,11},{11... | collective-permute-start | bytes 393224 | tf_op jit(solution)/shard_map/ppermute | solution.py:361
  9.1 0.6 %weigh.3 = (bf16[256,1024]{1,0:T(8,128)(2,1)S(1)}, f32[256,128]{1,0:T(8,128)S(1)}) custom-call(s32[1,256]{1,0:T(1,128)S(1)} %get-tuple-element.24.refs_0_.refs_2_, s32[1,256]{1,0:T(1,128)S(1)} %collective-permute-done.refs_1_.refs_3_, bf16[256,1024]{1,0:T(8,128)(2,1)S(1)} %get-tuple-element.25.refs_2_, bf16[256,1024]{1,0:T(8,128)(2,1)S(1)} %get-tuple-element.26.refs_3_, ...), custom_call_target="tpu_custom_call" | custom-call | flops 6000000000 | bytes 2230272 | tf_op jit(solution)/shard_map/weigh/pallas_call | solution.py:62
  10.6 0.5 %collective-permute-done.3.source.refs_0_ = bf16[256,256]{1,0:T(8,128)(2,1)S(1)} collective-permute-done((bf16[256,256]{1,0:T(8,128)(2,1)S(1)}, bf16[256,256]{1,0:T(8,128)(2,1)S(1)}, u32[]{:S(2)}, u32[]{:S(2)}) %collective-permute-start.3) | collective-permute-done | bytes 131104 | tf_op jit(solution)/shard_map/ppermute | solution.py:361
  11.1 3.4 %collective-permute-start.4 = (bf16[256,256]{1,0:T(8,128)(2,1)S(1)}, bf16[256,256]{1,0:T(8,128)(2,1)S(1)}, u32[]{:S(2)}, u32[]{:S(2)}) collective-permute-start(bf16[256,256]{1,0:T(8,128)(2,1)S(1)} %split.8), channel_id=1, source_target_pairs={{0,2},{2,3},{3,1},{1,0},{4,6},{6,7},{7,5},{5,4},{8,10},{10,11},{11... | collective-permute-start | bytes 393224 | tf_op jit(solution)/shard_map/ppermute | solution.py:390
  14.5 2.8 %collective-permute-start.7 = (bf16[256,256]{1,0:T(8,128)(2,1)S(1)}, bf16[256,256]{1,0:T(8,128)(2,1)S(1)}, u32[]{:S(2)}, u32[]{:S(2)}) collective-permute-start(bf16[256,256]{1,0:T(8,128)(2,1)S(1)} %split.10), channel_id=1, source_target_pairs={{0,2},{2,3},{3,1},{1,0},{4,6},{6,7},{7,5},{5,4},{8,10},{10,11},{11... | collective-permute-start | bytes 393224 | tf_op jit(solution)/shard_map/ppermute | solution.py:390
  17.3 2.8 %collective-permute-start.10 = (bf16[256,256]{1,0:T(8,128)(2,1)S(1)}, bf16[256,256]{1,0:T(8,128)(2,1)S(1)}, u32[]{:S(2)}, u32[]{:S(2)}) collective-permute-start(bf16[256,256]{1,0:T(8,128)(2,1)S(1)} %split.12), channel_id=1, source_target_pairs={{0,2},{2,3},{3,1},{1,0},{4,6},{6,7},{7,5},{5,4},{8,10},{10,11},{11... | collective-permute-start | bytes 393224 | tf_op jit(solution)/shard_map/ppermute | solution.py:390
  20.2 2.8 %collective-permute-start.13 = (bf16[256,256]{1,0:T(8,128)(2,1)S(1)}, bf16[256,256]{1,0:T(8,128)(2,1)S(1)}, u32[]{:S(2)}, u32[]{:S(2)}) collective-permute-start(bf16[256,256]{1,0:T(8,128)(2,1)S(1)} %split.14), channel_id=1, source_target_pairs={{0,2},{2,3},{3,1},{1,0},{4,6},{6,7},{7,5},{5,4},{8,10},{10,11},{11... | collective-permute-start | bytes 393224 | tf_op jit(solution)/shard_map/ppermute | solution.py:390
  22.9 2.2 %pack.1.refs_4_.refs_0_ = bf16[4160,512]{1,0:T(8,128)(2,1)S(1)} custom-call(bf16[2048,512]{1,0:T(8,128)(2,1)} %refs_0_.2, bf16[2048,512]{1,0:T(8,128)(2,1)} %refs_1_.2, bf16[64,512]{1,0:T(8,128)(2,1)} %refs_2_.2), custom_call_target="tpu_custom_call" | custom-call | bytes 8519680 | tf_op jit(solution)/shard_map/pack/pallas_call | solution.py:62
  25.3 0.7 %collective-permute-start.5 = (bf16[256,256]{1,0:T(8,128)(2,1)S(1)}, bf16[256,256]{1,0:T(8,128)(2,1)S(1)}, u32[]{:S(2)}, u32[]{:S(2)}) collective-permute-start(bf16[256,256]{1,0:T(8,128)(2,1)S(1)} %split.9), channel_id=1, source_target_pairs={{0,2},{2,3},{3,1},{1,0},{4,6},{6,7},{7,5},{5,4},{8,10},{10,11},{11... | collective-permute-start | bytes 393224 | tf_op jit(solution)/shard_map/ppermute | solution.py:390
  26.1 2.5 %collective-permute-start.8 = (bf16[256,256]{1,0:T(8,128)(2,1)S(1)}, bf16[256,256]{1,0:T(8,128)(2,1)S(1)}, u32[]{:S(2)}, u32[]{:S(2)}) collective-permute-start(bf16[256,256]{1,0:T(8,128)(2,1)S(1)} %split.11), channel_id=1, source_target_pairs={{0,2},{2,3},{3,1},{1,0},{4,6},{6,7},{7,5},{5,4},{8,10},{10,11},{11... | collective-permute-start | bytes 393224 | tf_op jit(solution)/shard_map/ppermute | solution.py:390
  28.6 2.8 %collective-permute-start.11 = (bf16[256,256]{1,0:T(8,128)(2,1)S(1)}, bf16[256,256]{1,0:T(8,128)(2,1)S(1)}, u32[]{:S(2)}, u32[]{:S(2)}) collective-permute-start(bf16[256,256]{1,0:T(8,128)(2,1)S(1)} %split.13), channel_id=1, source_target_pairs={{0,2},{2,3},{3,1},{1,0},{4,6},{6,7},{7,5},{5,4},{8,10},{10,11},{11... | collective-permute-start | bytes 393224 | tf_op jit(solution)/shard_map/ppermute | solution.py:390
  31.4 2.8 %collective-permute-start.14 = (bf16[256,128]{1,0:T(8,128)(2,1)S(1)}, bf16[256,128]{1,0:T(8,128)(2,1)S(1)}, u32[]{:S(2)}, u32[]{:S(2)}) collective-permute-start(bf16[256,128]{1,0:T(8,128)(2,1)S(1)} %get-tuple-element.32), channel_id=1, source_target_pairs={{0,2},{2,3},{3,1},{1,0},{4,6},{6,7},{7,5},{5,4},{8,10},{10,11},{11... | collective-permute-start | bytes 196616 | tf_op jit(solution)/shard_map/ppermute | solution.py:390
  34.2 0.7 %collective-permute-start.16 = (bf16[256,128]{1,0:T(8,128)(2,1)S(1)}, bf16[256,128]{1,0:T(8,128)(2,1)S(1)}, u32[]{:S(2)}, u32[]{:S(2)}) collective-permute-start(bf16[256,128]{1,0:T(8,128)(2,1)S(1)} %get-tuple-element.37), channel_id=1, source_target_pairs={{0,2},{2,3},{3,1},{1,0},{4,6},{6,7},{7,5},{5,4},{8,10},{10,11},{11... | collective-permute-start | bytes 196616 | tf_op jit(solution)/shard_map/ppermute | solution.py:390
  34.9 0.7 %project.4.refs_6_ = f32[256,1024]{1,0:T(8,128)S(1)} custom-call(bf16[256,256]{1,0:T(8,128)(2,1)S(1)} %mix.4.refs_0_, bf16[256,256]{1,0:T(8,128)(2,1)S(1)} %mix.5.refs_1_, bf16[256,256]{1,0:T(8,128)(2,1)S(1)} %mix.6.refs_2_, bf16[256,256]{1,0:T(8,128)(2,1)S(1)} %mix.7.refs_3_, bf16[4160,512]{1,0:T(8,128)(2,1)S(1)} %pack.1.refs_4_.refs_0_, ...), custom_call_target="tpu_custom_call" | custom-call | flops 536870912 | bytes 10092544 | tf_op jit(solution)/shard_map/project/pallas_call | solution.py:62
  35.6 0.7 %project.5.refs_6_ = f32[256,1024]{1,0:T(8,128)S(1)} custom-call(bf16[256,256]{1,0:T(8,128)(2,1)S(1)} %collective-permute-done.3.source.refs_0_, bf16[256,256]{1,0:T(8,128)(2,1)S(1)} %collective-permute-done.6.source.refs_1_, bf16[256,256]{1,0:T(8,128)(2,1)S(1)} %collective-permute-done.9.source.refs_2_, ...), custom_call_target="tpu_custom_call" | custom-call | flops 536870912 | bytes 11141120 | tf_op jit(solution)/shard_map/project/pallas_call | solution.py:62
  36.4 0.7 %project.6.refs_6_ = f32[256,1024]{1,0:T(8,128)S(1)} custom-call(bf16[256,256]{1,0:T(8,128)(2,1)S(1)} %collective-permute-done.4.source.refs_0_, bf16[256,256]{1,0:T(8,128)(2,1)S(1)} %collective-permute-done.7.source.refs_1_, bf16[256,256]{1,0:T(8,128)(2,1)S(1)} %collective-permute-done.10.source.refs_2_, ...), custom_call_target="tpu_custom_call" | custom-call | flops 536870912 | bytes 11141120 | tf_op jit(solution)/shard_map/project/pallas_call | solution.py:62
  37.3 3.2 %collective-permute-done.14.refs_3_ = bf16[256,128]{1,0:T(8,128)(2,1)S(1)} collective-permute-done((bf16[256,128]{1,0:T(8,128)(2,1)S(1)}, bf16[256,128]{1,0:T(8,128)(2,1)S(1)}, u32[]{:S(2)}, u32[]{:S(2)}) %collective-permute-start.14) | collective-permute-done | bytes 65568 | tf_op jit(solution)/shard_map/ppermute | solution.py:390
  40.5 0.7 %project.7.acc_ref = f32[256,1024]{1,0:T(8,128)S(1)} custom-call(bf16[256,256]{1,0:T(8,128)(2,1)S(1)} %collective-permute-done.5.refs_0_, bf16[256,256]{1,0:T(8,128)(2,1)S(1)} %collective-permute-done.8.refs_1_, bf16[256,256]{1,0:T(8,128)(2,1)S(1)} %collective-permute-done.11.refs_2_, bf16[256,128]{1,0:T(8,128)(2,1)S(1)} %collective-permute-done.14.refs_3_, ...), custom_call_target="tpu_custom_call" | custom-call | flops 469762048 | bytes 11075584 | tf_op jit(solution)/shard_map/project/pallas_call | solution.py:62
  41.2 0.6 %cross_near.1 = (bf16[256,1024]{1,0:T(8,128)(2,1)S(1)}, f32[64,640]{1,0:T(8,128)S(1)}) custom-call(f32[256,1024]{1,0:T(8,128)S(1)} %project.7.acc_ref, bf16[256,128]{1,0:T(8,128)(2,1)S(1)} %collective-permute-done.16.e_ref, bf16[128,1024]{1,0:T(8,128)(2,1)S(1)} %get-tuple-element.38.map_ref, bf16[128,512]{1,0:T(8,128)(2,1)S(1)} %get-tuple-element.39.tgt_ref, ...), custom_call_target="tpu_custom_call" | custom-call | flops 67108864 | bytes 2326528 | tf_op jit(solution)/shard_map/cross_near/pallas_call | solution.py:62
  42.3 1.0 %collective-permute-done.17.refs_1_ = f32[64,640]{1,0:T(8,128)S(1)} collective-permute-done((f32[64,640]{1,0:T(8,128)S(1)}, f32[64,640]{1,0:T(8,128)S(1)}, u32[]{:S(2)}, u32[]{:S(2)}) %collective-permute-start.17) | collective-permute-done | bytes 163872 | tf_op jit(solution)/shard_map/ppermute | solution.py:407
  43.3 0.8 %combine.1 = bf16[64,512]{1,0:T(8,128)(2,1)} custom-call(f32[64,640]{1,0:T(8,128)S(1)} %cross_own.1.refs_0_, f32[64,640]{1,0:T(8,128)S(1)} %collective-permute-done.17.refs_1_), custom_call_target="tpu_custom_call" | custom-call | bytes 393216 | tf_op jit(solution)/shard_map/combine/pallas_call | solution.py:62
  (36 shorter events, 3.3 us)
Async XLA Ops:
  0.0 2.4 %collective-permute-start.1 = (bf16[256,1024]{1,0:T(8,128)(2,1)}, bf16[256,1024]{1,0:T(8,128)(2,1)S(1)}, u32[]{:S(2)}, u32[]{:S(2)}) collective-permute-start(bf16[256,1024]{1,0:T(8,128)(2,1)} %refs_1_.1), channel_id=1, source_target_pairs={{0,4},{4,0},{1,5},{5,1},{2,6},{6,2},{3,7},{7,3},{8,12},{12,8},{9,1... | collective-permute-start | bytes 1572872 | tf_op jit(solution)/shard_map/ppermute | solution.py:343
  0.5 1.9 %collective-permute-start = (s32[1,256]{1,0:T(1,128)}, s32[1,256]{1,0:T(1,128)S(1)}, u32[]{:S(2)}, u32[]{:S(2)}) collective-permute-start(s32[1,256]{1,0:T(1,128)} %bitcast.1), channel_id=1, source_target_pairs={{0,4},{4,0},{1,5},{5,1},{2,6},{6,2},{3,7},{7,3},{8,12},{12,8},{9,1... | collective-permute-start | bytes 3080 | tf_op jit(solution)/shard_map/ppermute | solution.py:343
  0.5 2.4 %collective-permute-start.2 = (bf16[256,1024]{1,0:T(8,128)(2,1)}, bf16[256,1024]{1,0:T(8,128)(2,1)S(1)}, u32[]{:S(2)}, u32[]{:S(2)}) collective-permute-start(bf16[256,1024]{1,0:T(8,128)(2,1)} %refs_2_.1), channel_id=1, source_target_pairs={{0,4},{4,0},{1,5},{5,1},{2,6},{6,2},{3,7},{7,3},{8,12},{12,8},{9,1... | collective-permute-start | bytes 1572872 | tf_op jit(solution)/shard_map/ppermute | solution.py:343
  3.2 7.9 %collective-permute-start.3 = (bf16[256,256]{1,0:T(8,128)(2,1)S(1)}, bf16[256,256]{1,0:T(8,128)(2,1)S(1)}, u32[]{:S(2)}, u32[]{:S(2)}) collective-permute-start(bf16[256,256]{1,0:T(8,128)(2,1)S(1)} %mix.4.refs_0_), channel_id=1, source_target_pairs={{0,2},{2,3},{3,1},{1,0},{4,6},{6,7},{7,5},{5,4},{8,10},{10,11},{11... | collective-permute-start | bytes 393224 | tf_op jit(solution)/shard_map/ppermute | solution.py:361
  7.5 7.1 %collective-permute-start.6 = (bf16[256,256]{1,0:T(8,128)(2,1)S(1)}, bf16[256,256]{1,0:T(8,128)(2,1)S(1)}, u32[]{:S(2)}, u32[]{:S(2)}) collective-permute-start(bf16[256,256]{1,0:T(8,128)(2,1)S(1)} %mix.5.refs_1_), channel_id=1, source_target_pairs={{0,2},{2,3},{3,1},{1,0},{4,6},{6,7},{7,5},{5,4},{8,10},{10,11},{11... | collective-permute-start | bytes 393224 | tf_op jit(solution)/shard_map/ppermute | solution.py:361
  9.9 7.4 %collective-permute-start.9 = (bf16[256,256]{1,0:T(8,128)(2,1)S(1)}, bf16[256,256]{1,0:T(8,128)(2,1)S(1)}, u32[]{:S(2)}, u32[]{:S(2)}) collective-permute-start(bf16[256,256]{1,0:T(8,128)(2,1)S(1)} %mix.6.refs_2_), channel_id=1, source_target_pairs={{0,2},{2,3},{3,1},{1,0},{4,6},{6,7},{7,5},{5,4},{8,10},{10,11},{11... | collective-permute-start | bytes 393224 | tf_op jit(solution)/shard_map/ppermute | solution.py:361
  10.5 9.6 %collective-permute-start.12 = (bf16[256,256]{1,0:T(8,128)(2,1)S(1)}, bf16[256,256]{1,0:T(8,128)(2,1)S(1)}, u32[]{:S(2)}, u32[]{:S(2)}) collective-permute-start(bf16[256,256]{1,0:T(8,128)(2,1)S(1)} %mix.7.refs_3_), channel_id=1, source_target_pairs={{0,2},{2,3},{3,1},{1,0},{4,6},{6,7},{7,5},{5,4},{8,10},{10,11},{11... | collective-permute-start | bytes 393224 | tf_op jit(solution)/shard_map/ppermute | solution.py:361
  11.1 14.2 %collective-permute-start.4 = (bf16[256,256]{1,0:T(8,128)(2,1)S(1)}, bf16[256,256]{1,0:T(8,128)(2,1)S(1)}, u32[]{:S(2)}, u32[]{:S(2)}) collective-permute-start(bf16[256,256]{1,0:T(8,128)(2,1)S(1)} %split.8), channel_id=1, source_target_pairs={{0,2},{2,3},{3,1},{1,0},{4,6},{6,7},{7,5},{5,4},{8,10},{10,11},{11... | collective-permute-start | bytes 393224 | tf_op jit(solution)/shard_map/ppermute | solution.py:390
  14.5 11.5 %collective-permute-start.7 = (bf16[256,256]{1,0:T(8,128)(2,1)S(1)}, bf16[256,256]{1,0:T(8,128)(2,1)S(1)}, u32[]{:S(2)}, u32[]{:S(2)}) collective-permute-start(bf16[256,256]{1,0:T(8,128)(2,1)S(1)} %split.10), channel_id=1, source_target_pairs={{0,2},{2,3},{3,1},{1,0},{4,6},{6,7},{7,5},{5,4},{8,10},{10,11},{11... | collective-permute-start | bytes 393224 | tf_op jit(solution)/shard_map/ppermute | solution.py:390
  17.3 11.2 %collective-permute-start.10 = (bf16[256,256]{1,0:T(8,128)(2,1)S(1)}, bf16[256,256]{1,0:T(8,128)(2,1)S(1)}, u32[]{:S(2)}, u32[]{:S(2)}) collective-permute-start(bf16[256,256]{1,0:T(8,128)(2,1)S(1)} %split.12), channel_id=1, source_target_pairs={{0,2},{2,3},{3,1},{1,0},{4,6},{6,7},{7,5},{5,4},{8,10},{10,11},{11... | collective-permute-start | bytes 393224 | tf_op jit(solution)/shard_map/ppermute | solution.py:390
  20.2 11.2 %collective-permute-start.13 = (bf16[256,256]{1,0:T(8,128)(2,1)S(1)}, bf16[256,256]{1,0:T(8,128)(2,1)S(1)}, u32[]{:S(2)}, u32[]{:S(2)}) collective-permute-start(bf16[256,256]{1,0:T(8,128)(2,1)S(1)} %split.14), channel_id=1, source_target_pairs={{0,2},{2,3},{3,1},{1,0},{4,6},{6,7},{7,5},{5,4},{8,10},{10,11},{11... | collective-permute-start | bytes 393224 | tf_op jit(solution)/shard_map/ppermute | solution.py:390
  25.2 9.0 %collective-permute-start.15 = (bf16[4160,512]{1,0:T(8,128)(2,1)S(1)}, bf16[4160,512]{1,0:T(8,128)(2,1)S(1)}, u32[]{:S(2)}, u32[]{:S(2)}) collective-permute-start(bf16[4160,512]{1,0:T(8,128)(2,1)S(1)} %pack.1.refs_4_.refs_0_), channel_id=1, source_target_pairs={{0,4},{4,0},{1,5},{5,1},{2,6},{6,2},{3,7},{7,3},{8,12},{12,8},{9,1... | collective-permute-start | bytes 12779528 | tf_op jit(solution)/shard_map/ppermute | solution.py:343
  25.3 15.2 %collective-permute-start.5 = (bf16[256,256]{1,0:T(8,128)(2,1)S(1)}, bf16[256,256]{1,0:T(8,128)(2,1)S(1)}, u32[]{:S(2)}, u32[]{:S(2)}) collective-permute-start(bf16[256,256]{1,0:T(8,128)(2,1)S(1)} %split.9), channel_id=1, source_target_pairs={{0,2},{2,3},{3,1},{1,0},{4,6},{6,7},{7,5},{5,4},{8,10},{10,11},{11... | collective-permute-start | bytes 393224 | tf_op jit(solution)/shard_map/ppermute | solution.py:390
  26.1 14.4 %collective-permute-start.8 = (bf16[256,256]{1,0:T(8,128)(2,1)S(1)}, bf16[256,256]{1,0:T(8,128)(2,1)S(1)}, u32[]{:S(2)}, u32[]{:S(2)}) collective-permute-start(bf16[256,256]{1,0:T(8,128)(2,1)S(1)} %split.11), channel_id=1, source_target_pairs={{0,2},{2,3},{3,1},{1,0},{4,6},{6,7},{7,5},{5,4},{8,10},{10,11},{11... | collective-permute-start | bytes 393224 | tf_op jit(solution)/shard_map/ppermute | solution.py:390
  28.6 11.9 %collective-permute-start.11 = (bf16[256,256]{1,0:T(8,128)(2,1)S(1)}, bf16[256,256]{1,0:T(8,128)(2,1)S(1)}, u32[]{:S(2)}, u32[]{:S(2)}) collective-permute-start(bf16[256,256]{1,0:T(8,128)(2,1)S(1)} %split.13), channel_id=1, source_target_pairs={{0,2},{2,3},{3,1},{1,0},{4,6},{6,7},{7,5},{5,4},{8,10},{10,11},{11... | collective-permute-start | bytes 393224 | tf_op jit(solution)/shard_map/ppermute | solution.py:390
  31.4 9.1 %collective-permute-start.14 = (bf16[256,128]{1,0:T(8,128)(2,1)S(1)}, bf16[256,128]{1,0:T(8,128)(2,1)S(1)}, u32[]{:S(2)}, u32[]{:S(2)}) collective-permute-start(bf16[256,128]{1,0:T(8,128)(2,1)S(1)} %get-tuple-element.32), channel_id=1, source_target_pairs={{0,2},{2,3},{3,1},{1,0},{4,6},{6,7},{7,5},{5,4},{8,10},{10,11},{11... | collective-permute-start | bytes 196616 | tf_op jit(solution)/shard_map/ppermute | solution.py:390
  34.2 7.0 %collective-permute-start.16 = (bf16[256,128]{1,0:T(8,128)(2,1)S(1)}, bf16[256,128]{1,0:T(8,128)(2,1)S(1)}, u32[]{:S(2)}, u32[]{:S(2)}) collective-permute-start(bf16[256,128]{1,0:T(8,128)(2,1)S(1)} %get-tuple-element.37), channel_id=1, source_target_pairs={{0,2},{2,3},{3,1},{1,0},{4,6},{6,7},{7,5},{5,4},{8,10},{10,11},{11... | collective-permute-start | bytes 196616 | tf_op jit(solution)/shard_map/ppermute | solution.py:390
  41.8 1.5 %collective-permute-start.17 = (f32[64,640]{1,0:T(8,128)S(1)}, f32[64,640]{1,0:T(8,128)S(1)}, u32[]{:S(2)}, u32[]{:S(2)}) collective-permute-start(f32[64,640]{1,0:T(8,128)S(1)} %get-tuple-element.42), channel_id=1, source_target_pairs={{4,0},{0,4},{5,1},{1,5},{6,2},{2,6},{7,3},{3,7},{12,8},{8,12},{13,... | collective-permute-start | bytes 491528 | tf_op jit(solution)/shard_map/ppermute | solution.py:407

commit v25 on v24

--- a/solution.py
+++ b/solution.py
@@ -390,8 +390,10 @@
         later = [lax.ppermute(p, "head", ring) for p in pieces]
         acc = project(acc, arrived, functools.partial(place, turn, 0), shards, map_rows)
         held = arrived = later
-    acc = project(acc, held[:-1], functools.partial(place, last, 0), shards, map_rows)
     depth = held[-1].shape[1]
+    acc = project(acc, held[:-2], functools.partial(place, last, 0), shards, map_rows)
+    near_last = functools.partial(place, last, features - depth - held[-2].shape[1])
+    acc = project(acc, held[-2:-1], near_last, shards, map_rows)
     last_maps, targets, mask = prepare(
         functools.partial(place, last, features - depth),
         depth,

time: 44.2 us -> 44.7 us (1.011)
  waiting for transfers between devices: 4.62 us -> 5.3 us
    ppermute x9, waiting for transfers between devices: 3.18 us -> 3.92 us  [on_device(): later = [lax.ppermute(p, 'head', ring) for p in pieces]]
    pallas_call x24 -> x25, Pallas kernels: 10.8 us -> 10.9 us  [call(): pl.pallas_call(kernel, in_specs=specs or [VMEM] * len(operands), out_spec...]
  transfers between devices with their start and end apart: 18 -> 18, of which waited for: 3 -> 9; matrix products, arithmetic and copies ran while one was open for 0% -> 0% of each run, Pallas kernels for 21% -> 21%
where the time goes in v25:
time: 44.7 us; the launch traced here: 44.5 us
  starting transfers between devices  28.1 us (63%)
  Pallas kernels  10.9 us (24%)
  waiting for transfers between devices  5.3 us (12%)
    ppermute x9, starting transfers between devices, on_device(): later = [lax.ppermute(p, 'head', ring) for p in pieces]  20.9 us
    pallas_call x25, Pallas kernels, call(): pl.pallas_call(kernel, in_specs=specs or [VMEM] * len(operands), out_spec...  10.9 us
    ppermute x4, starting transfers between devices, on_device(): sent, held = (held, [lax.ppermute(h, 'head', ring) for h in held])  6.09 us
    ppermute x9, waiting for transfers between devices, on_device(): later = [lax.ppermute(p, 'head', ring) for p in pieces]  3.92 us
    ppermute x4, starting transfers between devices, on_device(): bring = lambda x: [lax.ppermute(x, 'ctx', pairs) for pairs in links]  1.03 us
    ppermute x1, waiting for transfers between devices, on_device(): lax.ppermute(piece, 'ctx', [(target, source) for source, target in pairs])  0.96 us
  transfers between devices with their start and end apart: 18, of which 9 were waited for; matrix products, arithmetic and copies ran while one was open for 0% of the time, Pallas kernels for 21%

profile of v25, /device:TPU:0, one launch (start us, length us, event | category | flops | bytes accessed | tf_op | source)
XLA Modules:
  0.0 44.5 jit_solution(2610614537984609591)
XLA Ops:
  1.0 1.4 %fetch.1 = (bf16[256,1024]{1,0:T(8,128)(2,1)S(1)}, bf16[256,1024]{1,0:T(8,128)(2,1)S(1)}, bf16[256,1024]{1,0:T(8,128)(2,1)S(1)}, s32[1,256]{1,0:T(1,128)S(1)}) custom-call(bf16[256,1024]{1,0:T(8,128)(2,1)} %refs_0_.1, bf16[256,1024]{1,0:T(8,128)(2,1)} %refs_1_.1, bf16[256,1024]{1,0:T(8,128)(2,1)} %refs_2_.1, s32[1,256]{1,0:T(1,128)} %bitcast.2), custom_call_target="tpu_custom_call" | custom-call | bytes 3147776 | tf_op jit(solution)/shard_map/fetch/pallas_call | solution.py:62
  2.4 0.6 %weigh.2 = (bf16[256,1024]{1,0:T(8,128)(2,1)S(1)}, f32[256,128]{1,0:T(8,128)S(1)}) custom-call(s32[1,256]{1,0:T(1,128)S(1)} %get-tuple-element.24.refs_0_.refs_2_, s32[1,256]{1,0:T(1,128)S(1)} %collective-permute-done.refs_1_.refs_3_, bf16[256,1024]{1,0:T(8,128)(2,1)S(1)} %get-tuple-element.25.refs_2_, bf16[256,1024]{1,0:T(8,128)(2,1)S(1)} %get-tuple-element.26.refs_3_, ...), custom_call_target="tpu_custom_call" | custom-call | flops 6000000000 | bytes 2230272 | tf_op jit(solution)/shard_map/weigh/pallas_call | solution.py:62
  3.2 4.0 %collective-permute-start.3 = (bf16[256,256]{1,0:T(8,128)(2,1)S(1)}, bf16[256,256]{1,0:T(8,128)(2,1)S(1)}, u32[]{:S(2)}, u32[]{:S(2)}) collective-permute-start(bf16[256,256]{1,0:T(8,128)(2,1)S(1)} %mix.4.refs_3_), channel_id=1, source_target_pairs={{0,2},{2,3},{3,1},{1,0},{4,6},{6,7},{7,5},{5,4},{8,10},{10,11},{11... | collective-permute-start | bytes 393224 | tf_op jit(solution)/shard_map/ppermute | solution.py:361
  7.2 0.6 %weigh.3 = (bf16[256,1024]{1,0:T(8,128)(2,1)S(1)}, f32[256,128]{1,0:T(8,128)S(1)}) custom-call(s32[1,256]{1,0:T(1,128)S(1)} %get-tuple-element.24.refs_0_.refs_2_, s32[1,256]{1,0:T(1,128)S(1)} %collective-permute-done.refs_1_.refs_3_, bf16[256,1024]{1,0:T(8,128)(2,1)S(1)} %get-tuple-element.25.refs_2_, bf16[256,1024]{1,0:T(8,128)(2,1)S(1)} %get-tuple-element.26.refs_3_, ...), custom_call_target="tpu_custom_call" | custom-call | flops 6000000000 | bytes 2230272 | tf_op jit(solution)/shard_map/weigh/pallas_call | solution.py:62
  8.0 1.6 %collective-permute-start.6 = (bf16[256,256]{1,0:T(8,128)(2,1)S(1)}, bf16[256,256]{1,0:T(8,128)(2,1)S(1)}, u32[]{:S(2)}, u32[]{:S(2)}) collective-permute-start(bf16[256,256]{1,0:T(8,128)(2,1)S(1)} %mix.5.refs_0_), channel_id=1, source_target_pairs={{0,2},{2,3},{3,1},{1,0},{4,6},{6,7},{7,5},{5,4},{8,10},{10,11},{11... | collective-permute-start | bytes 393224 | tf_op jit(solution)/shard_map/ppermute | solution.py:361
  10.9 3.4 %collective-permute-start.4 = (bf16[256,256]{1,0:T(8,128)(2,1)S(1)}, bf16[256,256]{1,0:T(8,128)(2,1)S(1)}, u32[]{:S(2)}, u32[]{:S(2)}) collective-permute-start(bf16[256,256]{1,0:T(8,128)(2,1)S(1)} %split.8), channel_id=1, source_target_pairs={{0,2},{2,3},{3,1},{1,0},{4,6},{6,7},{7,5},{5,4},{8,10},{10,11},{11... | collective-permute-start | bytes 393224 | tf_op jit(solution)/shard_map/ppermute | solution.py:390
  14.5 2.2 %pack.1.refs_4_.refs_3_.refs_1_.refs_0_ = bf16[4160,512]{1,0:T(8,128)(2,1)S(1)} custom-call(bf16[2048,512]{1,0:T(8,128)(2,1)} %refs_0_.2, bf16[2048,512]{1,0:T(8,128)(2,1)} %refs_1_.2, bf16[64,512]{1,0:T(8,128)(2,1)} %refs_2_.2), custom_call_target="tpu_custom_call" | custom-call | bytes 8519680 | tf_op jit(solution)/shard_map/pack/pallas_call | solution.py:62
  16.8 2.7 %collective-permute-start.8 = (bf16[256,256]{1,0:T(8,128)(2,1)S(1)}, bf16[256,256]{1,0:T(8,128)(2,1)S(1)}, u32[]{:S(2)}, u32[]{:S(2)}) collective-permute-start(bf16[256,256]{1,0:T(8,128)(2,1)S(1)} %split.10), channel_id=1, source_target_pairs={{0,2},{2,3},{3,1},{1,0},{4,6},{6,7},{7,5},{5,4},{8,10},{10,11},{11... | collective-permute-start | bytes 393224 | tf_op jit(solution)/shard_map/ppermute | solution.py:390
  19.5 0.9 %collective-permute-start.11 = (bf16[256,256]{1,0:T(8,128)(2,1)S(1)}, bf16[256,256]{1,0:T(8,128)(2,1)S(1)}, u32[]{:S(2)}, u32[]{:S(2)}) collective-permute-start(bf16[256,256]{1,0:T(8,128)(2,1)S(1)} %split.12), channel_id=1, source_target_pairs={{0,2},{2,3},{3,1},{1,0},{4,6},{6,7},{7,5},{5,4},{8,10},{10,11},{11... | collective-permute-start | bytes 393224 | tf_op jit(solution)/shard_map/ppermute | solution.py:390
  20.4 2.3 %collective-permute-start.14 = (bf16[256,256]{1,0:T(8,128)(2,1)S(1)}, bf16[256,256]{1,0:T(8,128)(2,1)S(1)}, u32[]{:S(2)}, u32[]{:S(2)}) collective-permute-start(bf16[256,256]{1,0:T(8,128)(2,1)S(1)} %split.14), channel_id=1, source_target_pairs={{0,2},{2,3},{3,1},{1,0},{4,6},{6,7},{7,5},{5,4},{8,10},{10,11},{11... | collective-permute-start | bytes 393224 | tf_op jit(solution)/shard_map/ppermute | solution.py:390
  22.9 2.7 %collective-permute-start.5 = (bf16[256,128]{1,0:T(8,128)(2,1)S(1)}, bf16[256,128]{1,0:T(8,128)(2,1)S(1)}, u32[]{:S(2)}, u32[]{:S(2)}) collective-permute-start(bf16[256,128]{1,0:T(8,128)(2,1)S(1)} %get-tuple-element.30), channel_id=1, source_target_pairs={{0,2},{2,3},{3,1},{1,0},{4,6},{6,7},{7,5},{5,4},{8,10},{10,11},{11... | collective-permute-start | bytes 196616 | tf_op jit(solution)/shard_map/ppermute | solution.py:390
  25.7 2.7 %collective-permute-start.9 = (bf16[256,256]{1,0:T(8,128)(2,1)S(1)}, bf16[256,256]{1,0:T(8,128)(2,1)S(1)}, u32[]{:S(2)}, u32[]{:S(2)}) collective-permute-start(bf16[256,256]{1,0:T(8,128)(2,1)S(1)} %split.11), channel_id=1, source_target_pairs={{0,2},{2,3},{3,1},{1,0},{4,6},{6,7},{7,5},{5,4},{8,10},{10,11},{11... | collective-permute-start | bytes 393224 | tf_op jit(solution)/shard_map/ppermute | solution.py:390
  28.5 2.7 %collective-permute-start.12 = (bf16[256,256]{1,0:T(8,128)(2,1)S(1)}, bf16[256,256]{1,0:T(8,128)(2,1)S(1)}, u32[]{:S(2)}, u32[]{:S(2)}) collective-permute-start(bf16[256,256]{1,0:T(8,128)(2,1)S(1)} %split.13), channel_id=1, source_target_pairs={{0,2},{2,3},{3,1},{1,0},{4,6},{6,7},{7,5},{5,4},{8,10},{10,11},{11... | collective-permute-start | bytes 393224 | tf_op jit(solution)/shard_map/ppermute | solution.py:390
  31.3 2.7 %collective-permute-start.15 = (bf16[256,256]{1,0:T(8,128)(2,1)S(1)}, bf16[256,256]{1,0:T(8,128)(2,1)S(1)}, u32[]{:S(2)}, u32[]{:S(2)}) collective-permute-start(bf16[256,256]{1,0:T(8,128)(2,1)S(1)} %split.15), channel_id=1, source_target_pairs={{0,2},{2,3},{3,1},{1,0},{4,6},{6,7},{7,5},{5,4},{8,10},{10,11},{11... | collective-permute-start | bytes 393224 | tf_op jit(solution)/shard_map/ppermute | solution.py:390
  34.0 0.9 %collective-permute-start.16 = (bf16[256,128]{1,0:T(8,128)(2,1)S(1)}, bf16[256,128]{1,0:T(8,128)(2,1)S(1)}, u32[]{:S(2)}, u32[]{:S(2)}) collective-permute-start(bf16[256,128]{1,0:T(8,128)(2,1)S(1)} %get-tuple-element.37), channel_id=1, source_target_pairs={{0,2},{2,3},{3,1},{1,0},{4,6},{6,7},{7,5},{5,4},{8,10},{10,11},{11... | collective-permute-start | bytes 196616 | tf_op jit(solution)/shard_map/ppermute | solution.py:390
  34.9 0.7 %project.5.refs_6_ = f32[256,1024]{1,0:T(8,128)S(1)} custom-call(bf16[256,256]{1,0:T(8,128)(2,1)S(1)} %mix.5.refs_0_, bf16[256,256]{1,0:T(8,128)(2,1)S(1)} %mix.6.refs_1_, bf16[256,256]{1,0:T(8,128)(2,1)S(1)} %mix.7.refs_2_, bf16[256,256]{1,0:T(8,128)(2,1)S(1)} %mix.4.refs_3_, bf16[4160,512]{1,0:T(8,128)(2,1)S(1)} %pack.1.refs_4_.refs_3_.refs_1_.refs_0_, ...), custom_call_target="tpu_custom_call" | custom-call | flops 536870912 | bytes 10092544 | tf_op jit(solution)/shard_map/project/pallas_call | solution.py:62
  35.6 0.7 %project.6.refs_6_ = f32[256,1024]{1,0:T(8,128)S(1)} custom-call(bf16[256,256]{1,0:T(8,128)(2,1)S(1)} %collective-permute-done.6.source.refs_0_, bf16[256,256]{1,0:T(8,128)(2,1)S(1)} %collective-permute-done.10.source.refs_1_, bf16[256,256]{1,0:T(8,128)(2,1)S(1)} %collective-permute-done.13.source.refs_2_, ...), custom_call_target="tpu_custom_call" | custom-call | flops 536870912 | bytes 11141120 | tf_op jit(solution)/shard_map/project/pallas_call | solution.py:62
  36.4 0.7 %project.7.refs_5_ = f32[256,1024]{1,0:T(8,128)S(1)} custom-call(bf16[256,256]{1,0:T(8,128)(2,1)S(1)} %collective-permute-done.8.source.refs_0_, bf16[256,256]{1,0:T(8,128)(2,1)S(1)} %collective-permute-done.11.source.refs_1_, bf16[256,256]{1,0:T(8,128)(2,1)S(1)} %collective-permute-done.14.source.refs_2_, ...), custom_call_target="tpu_custom_call" | custom-call | flops 536870912 | bytes 11141120 | tf_op jit(solution)/shard_map/project/pallas_call | solution.py:62
  37.3 1.0 %collective-permute-done.12.refs_1_ = bf16[256,256]{1,0:T(8,128)(2,1)S(1)} collective-permute-done((bf16[256,256]{1,0:T(8,128)(2,1)S(1)}, bf16[256,256]{1,0:T(8,128)(2,1)S(1)}, u32[]{:S(2)}, u32[]{:S(2)}) %collective-permute-start.12) | collective-permute-done | bytes 131104 | tf_op jit(solution)/shard_map/ppermute | solution.py:390
  38.3 2.4 %collective-permute-done.15.refs_2_ = bf16[256,256]{1,0:T(8,128)(2,1)S(1)} collective-permute-done((bf16[256,256]{1,0:T(8,128)(2,1)S(1)}, bf16[256,256]{1,0:T(8,128)(2,1)S(1)}, u32[]{:S(2)}, u32[]{:S(2)}) %collective-permute-start.15) | collective-permute-done | bytes 131104 | tf_op jit(solution)/shard_map/ppermute | solution.py:390
  40.7 0.6 %project.8.refs_3_ = f32[256,1024]{1,0:T(8,128)S(1)} custom-call(bf16[256,256]{1,0:T(8,128)(2,1)S(1)} %collective-permute-done.9.refs_0_, bf16[256,256]{1,0:T(8,128)(2,1)S(1)} %collective-permute-done.12.refs_1_, bf16[256,256]{1,0:T(8,128)(2,1)S(1)} %collective-permute-done.15.refs_2_, bf16[4160,512]{1,0:T(8,128)(2,1)S(1)} %pack.1.refs_4_.refs_3_.refs_1_.refs_0_, ...), custom_call_target="tpu_custom_call" | custom-call | flops 402653184 | bytes 11010048 | tf_op jit(solution)/shard_map/project/pallas_call | solution.py:62
  41.7 0.6 %cross_near.1 = (bf16[256,1024]{1,0:T(8,128)(2,1)S(1)}, f32[64,640]{1,0:T(8,128)S(1)}) custom-call(f32[256,1024]{1,0:T(8,128)S(1)} %project.9.acc_ref, bf16[256,128]{1,0:T(8,128)(2,1)S(1)} %collective-permute-done.16.e_ref, bf16[128,1024]{1,0:T(8,128)(2,1)S(1)} %get-tuple-element.38.map_ref, bf16[128,512]{1,0:T(8,128)(2,1)S(1)} %get-tuple-element.39.tgt_ref, ...), custom_call_target="tpu_custom_call" | custom-call | flops 67108864 | bytes 2326528 | tf_op jit(solution)/shard_map/cross_near/pallas_call | solution.py:62
  42.7 1.0 %collective-permute-done.17.refs_1_ = f32[64,640]{1,0:T(8,128)S(1)} collective-permute-done((f32[64,640]{1,0:T(8,128)S(1)}, f32[64,640]{1,0:T(8,128)S(1)}, u32[]{:S(2)}, u32[]{:S(2)}) %collective-permute-start.17) | collective-permute-done | bytes 163872 | tf_op jit(solution)/shard_map/ppermute | solution.py:409
  43.7 0.8 %combine.1 = bf16[64,512]{1,0:T(8,128)(2,1)} custom-call(f32[64,640]{1,0:T(8,128)S(1)} %cross_own.1.refs_0_, f32[64,640]{1,0:T(8,128)S(1)} %collective-permute-done.17.refs_1_), custom_call_target="tpu_custom_call" | custom-call | bytes 393216 | tf_op jit(solution)/shard_map/combine/pallas_call | solution.py:62
  (37 shorter events, 4.4 us)
Async XLA Ops:
  0.0 2.4 %collective-permute-start.1 = (bf16[256,1024]{1,0:T(8,128)(2,1)}, bf16[256,1024]{1,0:T(8,128)(2,1)S(1)}, u32[]{:S(2)}, u32[]{:S(2)}) collective-permute-start(bf16[256,1024]{1,0:T(8,128)(2,1)} %refs_1_.1), channel_id=1, source_target_pairs={{0,4},{4,0},{1,5},{5,1},{2,6},{6,2},{3,7},{7,3},{8,12},{12,8},{9,1... | collective-permute-start | bytes 1572872 | tf_op jit(solution)/shard_map/ppermute | solution.py:343
  0.5 1.9 %collective-permute-start = (s32[1,256]{1,0:T(1,128)}, s32[1,256]{1,0:T(1,128)S(1)}, u32[]{:S(2)}, u32[]{:S(2)}) collective-permute-start(s32[1,256]{1,0:T(1,128)} %bitcast.1), channel_id=1, source_target_pairs={{0,4},{4,0},{1,5},{5,1},{2,6},{6,2},{3,7},{7,3},{8,12},{12,8},{9,1... | collective-permute-start | bytes 3080 | tf_op jit(solution)/shard_map/ppermute | solution.py:343
  0.5 2.4 %collective-permute-start.2 = (bf16[256,1024]{1,0:T(8,128)(2,1)}, bf16[256,1024]{1,0:T(8,128)(2,1)S(1)}, u32[]{:S(2)}, u32[]{:S(2)}) collective-permute-start(bf16[256,1024]{1,0:T(8,128)(2,1)} %refs_2_.1), channel_id=1, source_target_pairs={{0,4},{4,0},{1,5},{5,1},{2,6},{6,2},{3,7},{7,3},{8,12},{12,8},{9,1... | collective-permute-start | bytes 1572872 | tf_op jit(solution)/shard_map/ppermute | solution.py:343
  3.2 7.7 %collective-permute-start.3 = (bf16[256,256]{1,0:T(8,128)(2,1)S(1)}, bf16[256,256]{1,0:T(8,128)(2,1)S(1)}, u32[]{:S(2)}, u32[]{:S(2)}) collective-permute-start(bf16[256,256]{1,0:T(8,128)(2,1)S(1)} %mix.4.refs_3_), channel_id=1, source_target_pairs={{0,2},{2,3},{3,1},{1,0},{4,6},{6,7},{7,5},{5,4},{8,10},{10,11},{11... | collective-permute-start | bytes 393224 | tf_op jit(solution)/shard_map/ppermute | solution.py:361
  8.0 6.4 %collective-permute-start.6 = (bf16[256,256]{1,0:T(8,128)(2,1)S(1)}, bf16[256,256]{1,0:T(8,128)(2,1)S(1)}, u32[]{:S(2)}, u32[]{:S(2)}) collective-permute-start(bf16[256,256]{1,0:T(8,128)(2,1)S(1)} %mix.5.refs_0_), channel_id=1, source_target_pairs={{0,2},{2,3},{3,1},{1,0},{4,6},{6,7},{7,5},{5,4},{8,10},{10,11},{11... | collective-permute-start | bytes 393224 | tf_op jit(solution)/shard_map/ppermute | solution.py:361
  9.9 9.6 %collective-permute-start.10 = (bf16[256,256]{1,0:T(8,128)(2,1)S(1)}, bf16[256,256]{1,0:T(8,128)(2,1)S(1)}, u32[]{:S(2)}, u32[]{:S(2)}) collective-permute-start(bf16[256,256]{1,0:T(8,128)(2,1)S(1)} %mix.6.refs_1_), channel_id=1, source_target_pairs={{0,2},{2,3},{3,1},{1,0},{4,6},{6,7},{7,5},{5,4},{8,10},{10,11},{11... | collective-permute-start | bytes 393224 | tf_op jit(solution)/shard_map/ppermute | solution.py:361
  10.5 9.9 %collective-permute-start.13 = (bf16[256,256]{1,0:T(8,128)(2,1)S(1)}, bf16[256,256]{1,0:T(8,128)(2,1)S(1)}, u32[]{:S(2)}, u32[]{:S(2)}) collective-permute-start(bf16[256,256]{1,0:T(8,128)(2,1)S(1)} %mix.7.refs_2_), channel_id=1, source_target_pairs={{0,2},{2,3},{3,1},{1,0},{4,6},{6,7},{7,5},{5,4},{8,10},{10,11},{11... | collective-permute-start | bytes 393224 | tf_op jit(solution)/shard_map/ppermute | solution.py:361
  10.9 12.0 %collective-permute-start.4 = (bf16[256,256]{1,0:T(8,128)(2,1)S(1)}, bf16[256,256]{1,0:T(8,128)(2,1)S(1)}, u32[]{:S(2)}, u32[]{:S(2)}) collective-permute-start(bf16[256,256]{1,0:T(8,128)(2,1)S(1)} %split.8), channel_id=1, source_target_pairs={{0,2},{2,3},{3,1},{1,0},{4,6},{6,7},{7,5},{5,4},{8,10},{10,11},{11... | collective-permute-start | bytes 393224 | tf_op jit(solution)/shard_map/ppermute | solution.py:390
  16.7 17.3 %collective-permute-start.7 = (bf16[4160,512]{1,0:T(8,128)(2,1)S(1)}, bf16[4160,512]{1,0:T(8,128)(2,1)S(1)}, u32[]{:S(2)}, u32[]{:S(2)}) collective-permute-start(bf16[4160,512]{1,0:T(8,128)(2,1)S(1)} %pack.1.refs_4_.refs_3_.refs_1_.refs_0_), channel_id=1, source_target_pairs={{0,4},{4,0},{1,5},{5,1},{2,6},{6,2},{3,7},{7,3},{8,12},{12,8},{9,1... | collective-permute-start | bytes 12779528 | tf_op jit(solution)/shard_map/ppermute | solution.py:343
  16.8 8.9 %collective-permute-start.8 = (bf16[256,256]{1,0:T(8,128)(2,1)S(1)}, bf16[256,256]{1,0:T(8,128)(2,1)S(1)}, u32[]{:S(2)}, u32[]{:S(2)}) collective-permute-start(bf16[256,256]{1,0:T(8,128)(2,1)S(1)} %split.10), channel_id=1, source_target_pairs={{0,2},{2,3},{3,1},{1,0},{4,6},{6,7},{7,5},{5,4},{8,10},{10,11},{11... | collective-permute-start | bytes 393224 | tf_op jit(solution)/shard_map/ppermute | solution.py:390
  19.5 9.0 %collective-permute-start.11 = (bf16[256,256]{1,0:T(8,128)(2,1)S(1)}, bf16[256,256]{1,0:T(8,128)(2,1)S(1)}, u32[]{:S(2)}, u32[]{:S(2)}) collective-permute-start(bf16[256,256]{1,0:T(8,128)(2,1)S(1)} %split.12), channel_id=1, source_target_pairs={{0,2},{2,3},{3,1},{1,0},{4,6},{6,7},{7,5},{5,4},{8,10},{10,11},{11... | collective-permute-start | bytes 393224 | tf_op jit(solution)/shard_map/ppermute | solution.py:390
  20.4 10.9 %collective-permute-start.14 = (bf16[256,256]{1,0:T(8,128)(2,1)S(1)}, bf16[256,256]{1,0:T(8,128)(2,1)S(1)}, u32[]{:S(2)}, u32[]{:S(2)}) collective-permute-start(bf16[256,256]{1,0:T(8,128)(2,1)S(1)} %split.14), channel_id=1, source_target_pairs={{0,2},{2,3},{3,1},{1,0},{4,6},{6,7},{7,5},{5,4},{8,10},{10,11},{11... | collective-permute-start | bytes 393224 | tf_op jit(solution)/shard_map/ppermute | solution.py:390
  22.9 18.4 %collective-permute-start.5 = (bf16[256,128]{1,0:T(8,128)(2,1)S(1)}, bf16[256,128]{1,0:T(8,128)(2,1)S(1)}, u32[]{:S(2)}, u32[]{:S(2)}) collective-permute-start(bf16[256,128]{1,0:T(8,128)(2,1)S(1)} %get-tuple-element.30), channel_id=1, source_target_pairs={{0,2},{2,3},{3,1},{1,0},{4,6},{6,7},{7,5},{5,4},{8,10},{10,11},{11... | collective-permute-start | bytes 196616 | tf_op jit(solution)/shard_map/ppermute | solution.py:390
  25.7 11.6 %collective-permute-start.9 = (bf16[256,256]{1,0:T(8,128)(2,1)S(1)}, bf16[256,256]{1,0:T(8,128)(2,1)S(1)}, u32[]{:S(2)}, u32[]{:S(2)}) collective-permute-start(bf16[256,256]{1,0:T(8,128)(2,1)S(1)} %split.11), channel_id=1, source_target_pairs={{0,2},{2,3},{3,1},{1,0},{4,6},{6,7},{7,5},{5,4},{8,10},{10,11},{11... | collective-permute-start | bytes 393224 | tf_op jit(solution)/shard_map/ppermute | solution.py:390
  28.5 9.8 %collective-permute-start.12 = (bf16[256,256]{1,0:T(8,128)(2,1)S(1)}, bf16[256,256]{1,0:T(8,128)(2,1)S(1)}, u32[]{:S(2)}, u32[]{:S(2)}) collective-permute-start(bf16[256,256]{1,0:T(8,128)(2,1)S(1)} %split.13), channel_id=1, source_target_pairs={{0,2},{2,3},{3,1},{1,0},{4,6},{6,7},{7,5},{5,4},{8,10},{10,11},{11... | collective-permute-start | bytes 393224 | tf_op jit(solution)/shard_map/ppermute | solution.py:390
  31.3 9.4 %collective-permute-start.15 = (bf16[256,256]{1,0:T(8,128)(2,1)S(1)}, bf16[256,256]{1,0:T(8,128)(2,1)S(1)}, u32[]{:S(2)}, u32[]{:S(2)}) collective-permute-start(bf16[256,256]{1,0:T(8,128)(2,1)S(1)} %split.15), channel_id=1, source_target_pairs={{0,2},{2,3},{3,1},{1,0},{4,6},{6,7},{7,5},{5,4},{8,10},{10,11},{11... | collective-permute-start | bytes 393224 | tf_op jit(solution)/shard_map/ppermute | solution.py:390
  34.0 7.7 %collective-permute-start.16 = (bf16[256,128]{1,0:T(8,128)(2,1)S(1)}, bf16[256,128]{1,0:T(8,128)(2,1)S(1)}, u32[]{:S(2)}, u32[]{:S(2)}) collective-permute-start(bf16[256,128]{1,0:T(8,128)(2,1)S(1)} %get-tuple-element.37), channel_id=1, source_target_pairs={{0,2},{2,3},{3,1},{1,0},{4,6},{6,7},{7,5},{5,4},{8,10},{10,11},{11... | collective-permute-start | bytes 196616 | tf_op jit(solution)/shard_map/ppermute | solution.py:390
  42.2 1.5 %collective-permute-start.17 = (f32[64,640]{1,0:T(8,128)S(1)}, f32[64,640]{1,0:T(8,128)S(1)}, u32[]{:S(2)}, u32[]{:S(2)}) collective-permute-start(f32[64,640]{1,0:T(8,128)S(1)} %get-tuple-element.42), channel_id=1, source_target_pairs={{4,0},{0,4},{5,1},{1,5},{6,2},{2,6},{7,3},{3,7},{12,8},{8,12},{13,... | collective-permute-start | bytes 491528 | tf_op jit(solution)/shard_map/ppermute | solution.py:409

commit v26 on v23

--- a/solution.py
+++ b/solution.py
@@ -50,7 +50,7 @@
 
 
 def softmax_block(scores, same):
-    scores = jnp.where(same, scores * SCALE, NEG_FILL)
+    scores = jnp.where(same, scores, NEG_FILL)
     top = jnp.max(scores, axis=1, keepdims=True)
     weights = jnp.exp(scores - top)
     return top, weights, jnp.sum(weights, axis=1, keepdims=True)
@@ -128,7 +128,7 @@
     for h in range(heads):
         at = head_columns(first + h)
         scores = jnp.concatenate([dot_t(q_ref[:, at], k[:, at]) for k in keys], axis=1)
-        _, weights, total = softmax_block(scores, same)
+        _, weights, total = softmax_block(scores * SCALE, same)
         results.append(weights.astype(BF16))
         totals = jnp.where(lane == h, 1.0 / total, totals)
     for h in range(heads):
@@ -240,7 +240,7 @@
     targets = [maps[0][below, :]] + ([r[...] for r in near] if near else [m[below, :] for m in maps[1:]])
     for i, (target, mark_ref) in enumerate(zip(targets, marks)):
         part = slice(i * count, (i + 1) * count)
-        tgt_ref[part, :] = target
+        tgt_ref[part, :] = target * SCALE
         down_ref[...] = down_lanes(mark_ref[...])
         down = down_ref[pl.ds(0, count, stride=step), :]
         mask_ref[part, :] = same_mark(down, own).astype(F32)

time: 44.2 us -> 44.2 us (level)
  no operation moved by 1% of the time
where the time goes in v26:
time: 44.2 us; the launch traced here: 44.1 us
  starting transfers between devices  27.8 us (63%)
  Pallas kernels  10.7 us (24%)
  waiting for transfers between devices  5.38 us (12%)
    ppermute x8, starting transfers between devices, on_device(): later = [lax.ppermute(p, 'head', ring) for p in pieces]  20.6 us
    pallas_call x24, Pallas kernels, call(): pl.pallas_call(kernel, in_specs=specs or [VMEM] * len(operands), out_spec...  10.7 us
    ppermute x4, starting transfers between devices, on_device(): sent, held = (held, [lax.ppermute(h, 'head', ring) for h in held])  6.07 us
    ppermute x8, waiting for transfers between devices, on_device(): later = [lax.ppermute(p, 'head', ring) for p in pieces]  3.94 us
    ppermute x4, starting transfers between devices, on_device(): bring = lambda x: [lax.ppermute(x, 'ctx', pairs) for pairs in links]  1.03 us
    ppermute x1, waiting for transfers between devices, on_device(): lax.ppermute(piece, 'ctx', [(target, source) for source, target in pairs])  0.96 us
  transfers between devices with their start and end apart: 17, of which 4 were waited for; matrix products, arithmetic and copies ran while one was open for 0% of the time, Pallas kernels for 20%

profile of v26, /device:TPU:0, one launch (start us, length us, event | category | flops | bytes accessed | tf_op | source)
XLA Modules:
  0.0 44.1 jit_solution(8888671627831133593)
XLA Ops:
  1.0 1.4 %fetch.1 = (bf16[256,1024]{1,0:T(8,128)(2,1)S(1)}, bf16[256,1024]{1,0:T(8,128)(2,1)S(1)}, bf16[256,1024]{1,0:T(8,128)(2,1)S(1)}, s32[1,256]{1,0:T(1,128)S(1)}) custom-call(bf16[256,1024]{1,0:T(8,128)(2,1)} %refs_0_.1, bf16[256,1024]{1,0:T(8,128)(2,1)} %refs_1_.1, bf16[256,1024]{1,0:T(8,128)(2,1)} %refs_2_.1, s32[1,256]{1,0:T(1,128)} %bitcast.2), custom_call_target="tpu_custom_call" | custom-call | bytes 3147776 | tf_op jit(solution)/shard_map/fetch/pallas_call | solution.py:62
  2.4 0.6 %weigh.2 = (bf16[256,1024]{1,0:T(8,128)(2,1)S(1)}, f32[256,128]{1,0:T(8,128)S(1)}) custom-call(s32[1,256]{1,0:T(1,128)S(1)} %get-tuple-element.22.refs_0_.refs_2_, s32[1,256]{1,0:T(1,128)S(1)} %collective-permute-done.refs_1_.refs_3_, bf16[256,1024]{1,0:T(8,128)(2,1)S(1)} %get-tuple-element.23.refs_2_, bf16[256,1024]{1,0:T(8,128)(2,1)S(1)} %get-tuple-element.24.refs_3_, ...), custom_call_target="tpu_custom_call" | custom-call | flops 6000000000 | bytes 2230272 | tf_op jit(solution)/shard_map/weigh/pallas_call | solution.py:62
  3.2 4.0 %collective-permute-start.3 = (bf16[256,256]{1,0:T(8,128)(2,1)S(1)}, bf16[256,256]{1,0:T(8,128)(2,1)S(1)}, u32[]{:S(2)}, u32[]{:S(2)}) collective-permute-start(bf16[256,256]{1,0:T(8,128)(2,1)S(1)} %mix.4.refs_0_), channel_id=1, source_target_pairs={{0,2},{2,3},{3,1},{1,0},{4,6},{6,7},{7,5},{5,4},{8,10},{10,11},{11... | collective-permute-start | bytes 393224 | tf_op jit(solution)/shard_map/ppermute | solution.py:361
  7.5 1.6 %collective-permute-start.6 = (bf16[256,256]{1,0:T(8,128)(2,1)S(1)}, bf16[256,256]{1,0:T(8,128)(2,1)S(1)}, u32[]{:S(2)}, u32[]{:S(2)}) collective-permute-start(bf16[256,256]{1,0:T(8,128)(2,1)S(1)} %mix.5.refs_1_), channel_id=1, source_target_pairs={{0,2},{2,3},{3,1},{1,0},{4,6},{6,7},{7,5},{5,4},{8,10},{10,11},{11... | collective-permute-start | bytes 393224 | tf_op jit(solution)/shard_map/ppermute | solution.py:361
  9.1 0.6 %weigh.3 = (bf16[256,1024]{1,0:T(8,128)(2,1)S(1)}, f32[256,128]{1,0:T(8,128)S(1)}) custom-call(s32[1,256]{1,0:T(1,128)S(1)} %get-tuple-element.22.refs_0_.refs_2_, s32[1,256]{1,0:T(1,128)S(1)} %collective-permute-done.refs_1_.refs_3_, bf16[256,1024]{1,0:T(8,128)(2,1)S(1)} %get-tuple-element.23.refs_2_, bf16[256,1024]{1,0:T(8,128)(2,1)S(1)} %get-tuple-element.24.refs_3_, ...), custom_call_target="tpu_custom_call" | custom-call | flops 6000000000 | bytes 2230272 | tf_op jit(solution)/shard_map/weigh/pallas_call | solution.py:62
  10.6 0.5 %collective-permute-done.3.source.refs_0_ = bf16[256,256]{1,0:T(8,128)(2,1)S(1)} collective-permute-done((bf16[256,256]{1,0:T(8,128)(2,1)S(1)}, bf16[256,256]{1,0:T(8,128)(2,1)S(1)}, u32[]{:S(2)}, u32[]{:S(2)}) %collective-permute-start.3) | collective-permute-done | bytes 131104 | tf_op jit(solution)/shard_map/ppermute | solution.py:361
  11.1 3.4 %collective-permute-start.4 = (bf16[256,256]{1,0:T(8,128)(2,1)S(1)}, bf16[256,256]{1,0:T(8,128)(2,1)S(1)}, u32[]{:S(2)}, u32[]{:S(2)}) collective-permute-start(bf16[256,256]{1,0:T(8,128)(2,1)S(1)} %split.8), channel_id=1, source_target_pairs={{0,2},{2,3},{3,1},{1,0},{4,6},{6,7},{7,5},{5,4},{8,10},{10,11},{11... | collective-permute-start | bytes 393224 | tf_op jit(solution)/shard_map/ppermute | solution.py:390
  14.5 2.8 %collective-permute-start.7 = (bf16[256,256]{1,0:T(8,128)(2,1)S(1)}, bf16[256,256]{1,0:T(8,128)(2,1)S(1)}, u32[]{:S(2)}, u32[]{:S(2)}) collective-permute-start(bf16[256,256]{1,0:T(8,128)(2,1)S(1)} %split.10), channel_id=1, source_target_pairs={{0,2},{2,3},{3,1},{1,0},{4,6},{6,7},{7,5},{5,4},{8,10},{10,11},{11... | collective-permute-start | bytes 393224 | tf_op jit(solution)/shard_map/ppermute | solution.py:390
  17.3 2.8 %collective-permute-start.10 = (bf16[256,256]{1,0:T(8,128)(2,1)S(1)}, bf16[256,256]{1,0:T(8,128)(2,1)S(1)}, u32[]{:S(2)}, u32[]{:S(2)}) collective-permute-start(bf16[256,256]{1,0:T(8,128)(2,1)S(1)} %split.12), channel_id=1, source_target_pairs={{0,2},{2,3},{3,1},{1,0},{4,6},{6,7},{7,5},{5,4},{8,10},{10,11},{11... | collective-permute-start | bytes 393224 | tf_op jit(solution)/shard_map/ppermute | solution.py:390
  20.1 2.2 %pack.1.refs_4_.refs_3_.refs_0_ = bf16[4160,512]{1,0:T(8,128)(2,1)S(1)} custom-call(bf16[2048,512]{1,0:T(8,128)(2,1)} %refs_0_.2, bf16[2048,512]{1,0:T(8,128)(2,1)} %refs_1_.2, bf16[64,512]{1,0:T(8,128)(2,1)} %refs_2_.2), custom_call_target="tpu_custom_call" | custom-call | bytes 8519680 | tf_op jit(solution)/shard_map/pack/pallas_call | solution.py:62
  22.5 0.7 %collective-permute-start.14 = (bf16[256,256]{1,0:T(8,128)(2,1)S(1)}, bf16[256,256]{1,0:T(8,128)(2,1)S(1)}, u32[]{:S(2)}, u32[]{:S(2)}) collective-permute-start(bf16[256,256]{1,0:T(8,128)(2,1)S(1)} %split.14), channel_id=1, source_target_pairs={{0,2},{2,3},{3,1},{1,0},{4,6},{6,7},{7,5},{5,4},{8,10},{10,11},{11... | collective-permute-start | bytes 393224 | tf_op jit(solution)/shard_map/ppermute | solution.py:390
  23.2 2.5 %collective-permute-start.5 = (bf16[256,256]{1,0:T(8,128)(2,1)S(1)}, bf16[256,256]{1,0:T(8,128)(2,1)S(1)}, u32[]{:S(2)}, u32[]{:S(2)}) collective-permute-start(bf16[256,256]{1,0:T(8,128)(2,1)S(1)} %split.9), channel_id=1, source_target_pairs={{0,2},{2,3},{3,1},{1,0},{4,6},{6,7},{7,5},{5,4},{8,10},{10,11},{11... | collective-permute-start | bytes 393224 | tf_op jit(solution)/shard_map/ppermute | solution.py:390
  25.8 2.8 %collective-permute-start.8 = (bf16[256,256]{1,0:T(8,128)(2,1)S(1)}, bf16[256,256]{1,0:T(8,128)(2,1)S(1)}, u32[]{:S(2)}, u32[]{:S(2)}) collective-permute-start(bf16[256,256]{1,0:T(8,128)(2,1)S(1)} %split.11), channel_id=1, source_target_pairs={{0,2},{2,3},{3,1},{1,0},{4,6},{6,7},{7,5},{5,4},{8,10},{10,11},{11... | collective-permute-start | bytes 393224 | tf_op jit(solution)/shard_map/ppermute | solution.py:390
  28.6 2.8 %collective-permute-start.11 = (bf16[256,256]{1,0:T(8,128)(2,1)S(1)}, bf16[256,256]{1,0:T(8,128)(2,1)S(1)}, u32[]{:S(2)}, u32[]{:S(2)}) collective-permute-start(bf16[256,256]{1,0:T(8,128)(2,1)S(1)} %split.13), channel_id=1, source_target_pairs={{0,2},{2,3},{3,1},{1,0},{4,6},{6,7},{7,5},{5,4},{8,10},{10,11},{11... | collective-permute-start | bytes 393224 | tf_op jit(solution)/shard_map/ppermute | solution.py:390
  31.4 2.8 %collective-permute-start.15 = (bf16[256,256]{1,0:T(8,128)(2,1)S(1)}, bf16[256,256]{1,0:T(8,128)(2,1)S(1)}, u32[]{:S(2)}, u32[]{:S(2)}) collective-permute-start(bf16[256,256]{1,0:T(8,128)(2,1)S(1)} %split.15), channel_id=1, source_target_pairs={{0,2},{2,3},{3,1},{1,0},{4,6},{6,7},{7,5},{5,4},{8,10},{10,11},{11... | collective-permute-start | bytes 393224 | tf_op jit(solution)/shard_map/ppermute | solution.py:390
  34.4 0.7 %project.4.refs_6_ = f32[256,1024]{1,0:T(8,128)S(1)} custom-call(bf16[256,256]{1,0:T(8,128)(2,1)S(1)} %mix.4.refs_0_, bf16[256,256]{1,0:T(8,128)(2,1)S(1)} %mix.5.refs_1_, bf16[256,256]{1,0:T(8,128)(2,1)S(1)} %mix.6.refs_2_, bf16[256,256]{1,0:T(8,128)(2,1)S(1)} %mix.7.refs_3_, bf16[4160,512]{1,0:T(8,128)(2,1)S(1)} %pack.1.refs_4_.refs_3_.refs_0_, ...), custom_call_target="tpu_custom_call" | custom-call | flops 536870912 | bytes 10092544 | tf_op jit(solution)/shard_map/project/pallas_call | solution.py:62
  35.1 0.7 %project.5.refs_6_ = f32[256,1024]{1,0:T(8,128)S(1)} custom-call(bf16[256,256]{1,0:T(8,128)(2,1)S(1)} %collective-permute-done.3.source.refs_0_, bf16[256,256]{1,0:T(8,128)(2,1)S(1)} %collective-permute-done.6.source.refs_1_, bf16[256,256]{1,0:T(8,128)(2,1)S(1)} %collective-permute-done.9.source.refs_2_, ...), custom_call_target="tpu_custom_call" | custom-call | flops 536870912 | bytes 11141120 | tf_op jit(solution)/shard_map/project/pallas_call | solution.py:62
  35.9 0.7 %project.6.refs_5_ = f32[256,1024]{1,0:T(8,128)S(1)} custom-call(bf16[256,256]{1,0:T(8,128)(2,1)S(1)} %collective-permute-done.4.source.refs_0_, bf16[256,256]{1,0:T(8,128)(2,1)S(1)} %collective-permute-done.7.source.refs_1_, bf16[256,256]{1,0:T(8,128)(2,1)S(1)} %collective-permute-done.10.source.refs_2_, ...), custom_call_target="tpu_custom_call" | custom-call | flops 536870912 | bytes 11141120 | tf_op jit(solution)/shard_map/project/pallas_call | solution.py:62
  36.7 2.5 %collective-permute-done.11.refs_2_ = bf16[256,256]{1,0:T(8,128)(2,1)S(1)} collective-permute-done((bf16[256,256]{1,0:T(8,128)(2,1)S(1)}, bf16[256,256]{1,0:T(8,128)(2,1)S(1)}, u32[]{:S(2)}, u32[]{:S(2)}) %collective-permute-start.11) | collective-permute-done | bytes 131104 | tf_op jit(solution)/shard_map/ppermute | solution.py:390
  39.2 0.6 %project.7.acc_ref = f32[256,1024]{1,0:T(8,128)S(1)} custom-call(bf16[256,256]{1,0:T(8,128)(2,1)S(1)} %collective-permute-done.5.refs_0_, bf16[256,256]{1,0:T(8,128)(2,1)S(1)} %collective-permute-done.8.refs_1_, bf16[256,256]{1,0:T(8,128)(2,1)S(1)} %collective-permute-done.11.refs_2_, bf16[4160,512]{1,0:T(8,128)(2,1)S(1)} %pack.1.refs_4_.refs_3_.refs_0_, ...), custom_call_target="tpu_custom_call" | custom-call | flops 402653184 | bytes 11010048 | tf_op jit(solution)/shard_map/project/pallas_call | solution.py:62
  39.8 1.4 %collective-permute-done.15.e_ref = bf16[256,256]{1,0:T(8,128)(2,1)S(1)} collective-permute-done((bf16[256,256]{1,0:T(8,128)(2,1)S(1)}, bf16[256,256]{1,0:T(8,128)(2,1)S(1)}, u32[]{:S(2)}, u32[]{:S(2)}) %collective-permute-start.15) | collective-permute-done | bytes 131104 | tf_op jit(solution)/shard_map/ppermute | solution.py:390
  41.2 0.6 %cross_near.1 = (bf16[256,1024]{1,0:T(8,128)(2,1)S(1)}, f32[64,640]{1,0:T(8,128)S(1)}) custom-call(f32[256,1024]{1,0:T(8,128)S(1)} %project.7.acc_ref, bf16[256,256]{1,0:T(8,128)(2,1)S(1)} %collective-permute-done.15.e_ref, bf16[256,1024]{1,0:T(8,128)(2,1)S(1)} %get-tuple-element.34.map_ref, bf16[128,512]{1,0:T(8,128)(2,1)S(1)} %get-tuple-element.35.tgt_ref, ...), custom_call_target="tpu_custom_call" | custom-call | flops 134217728 | bytes 2654208 | tf_op jit(solution)/shard_map/cross_near/pallas_call | solution.py:62
  42.3 1.0 %collective-permute-done.16.refs_1_ = f32[64,640]{1,0:T(8,128)S(1)} collective-permute-done((f32[64,640]{1,0:T(8,128)S(1)}, f32[64,640]{1,0:T(8,128)S(1)}, u32[]{:S(2)}, u32[]{:S(2)}) %collective-permute-start.16) | collective-permute-done | bytes 163872 | tf_op jit(solution)/shard_map/ppermute | solution.py:407
  43.2 0.8 %combine.1 = bf16[64,512]{1,0:T(8,128)(2,1)} custom-call(f32[64,640]{1,0:T(8,128)S(1)} %cross_own.1.refs_0_, f32[64,640]{1,0:T(8,128)S(1)} %collective-permute-done.16.refs_1_), custom_call_target="tpu_custom_call" | custom-call | bytes 393216 | tf_op jit(solution)/shard_map/combine/pallas_call | solution.py:62
  (34 shorter events, 3.2 us)
Async XLA Ops:
  0.0 2.4 %collective-permute-start.1 = (bf16[256,1024]{1,0:T(8,128)(2,1)}, bf16[256,1024]{1,0:T(8,128)(2,1)S(1)}, u32[]{:S(2)}, u32[]{:S(2)}) collective-permute-start(bf16[256,1024]{1,0:T(8,128)(2,1)} %refs_1_.1), channel_id=1, source_target_pairs={{0,4},{4,0},{1,5},{5,1},{2,6},{6,2},{3,7},{7,3},{8,12},{12,8},{9,1... | collective-permute-start | bytes 1572872 | tf_op jit(solution)/shard_map/ppermute | solution.py:343
  0.5 1.9 %collective-permute-start = (s32[1,256]{1,0:T(1,128)}, s32[1,256]{1,0:T(1,128)S(1)}, u32[]{:S(2)}, u32[]{:S(2)}) collective-permute-start(s32[1,256]{1,0:T(1,128)} %bitcast.1), channel_id=1, source_target_pairs={{0,4},{4,0},{1,5},{5,1},{2,6},{6,2},{3,7},{7,3},{8,12},{12,8},{9,1... | collective-permute-start | bytes 3080 | tf_op jit(solution)/shard_map/ppermute | solution.py:343
  0.5 2.4 %collective-permute-start.2 = (bf16[256,1024]{1,0:T(8,128)(2,1)}, bf16[256,1024]{1,0:T(8,128)(2,1)S(1)}, u32[]{:S(2)}, u32[]{:S(2)}) collective-permute-start(bf16[256,1024]{1,0:T(8,128)(2,1)} %refs_2_.1), channel_id=1, source_target_pairs={{0,4},{4,0},{1,5},{5,1},{2,6},{6,2},{3,7},{7,3},{8,12},{12,8},{9,1... | collective-permute-start | bytes 1572872 | tf_op jit(solution)/shard_map/ppermute | solution.py:343
  3.2 7.9 %collective-permute-start.3 = (bf16[256,256]{1,0:T(8,128)(2,1)S(1)}, bf16[256,256]{1,0:T(8,128)(2,1)S(1)}, u32[]{:S(2)}, u32[]{:S(2)}) collective-permute-start(bf16[256,256]{1,0:T(8,128)(2,1)S(1)} %mix.4.refs_0_), channel_id=1, source_target_pairs={{0,2},{2,3},{3,1},{1,0},{4,6},{6,7},{7,5},{5,4},{8,10},{10,11},{11... | collective-permute-start | bytes 393224 | tf_op jit(solution)/shard_map/ppermute | solution.py:361
  7.5 7.1 %collective-permute-start.6 = (bf16[256,256]{1,0:T(8,128)(2,1)S(1)}, bf16[256,256]{1,0:T(8,128)(2,1)S(1)}, u32[]{:S(2)}, u32[]{:S(2)}) collective-permute-start(bf16[256,256]{1,0:T(8,128)(2,1)S(1)} %mix.5.refs_1_), channel_id=1, source_target_pairs={{0,2},{2,3},{3,1},{1,0},{4,6},{6,7},{7,5},{5,4},{8,10},{10,11},{11... | collective-permute-start | bytes 393224 | tf_op jit(solution)/shard_map/ppermute | solution.py:361
  9.9 7.4 %collective-permute-start.9 = (bf16[256,256]{1,0:T(8,128)(2,1)S(1)}, bf16[256,256]{1,0:T(8,128)(2,1)S(1)}, u32[]{:S(2)}, u32[]{:S(2)}) collective-permute-start(bf16[256,256]{1,0:T(8,128)(2,1)S(1)} %mix.6.refs_2_), channel_id=1, source_target_pairs={{0,2},{2,3},{3,1},{1,0},{4,6},{6,7},{7,5},{5,4},{8,10},{10,11},{11... | collective-permute-start | bytes 393224 | tf_op jit(solution)/shard_map/ppermute | solution.py:361
  10.5 11.9 %collective-permute-start.13 = (bf16[256,256]{1,0:T(8,128)(2,1)S(1)}, bf16[256,256]{1,0:T(8,128)(2,1)S(1)}, u32[]{:S(2)}, u32[]{:S(2)}) collective-permute-start(bf16[256,256]{1,0:T(8,128)(2,1)S(1)} %mix.7.refs_3_), channel_id=1, source_target_pairs={{0,2},{2,3},{3,1},{1,0},{4,6},{6,7},{7,5},{5,4},{8,10},{10,11},{11... | collective-permute-start | bytes 393224 | tf_op jit(solution)/shard_map/ppermute | solution.py:361
  11.1 12.1 %collective-permute-start.4 = (bf16[256,256]{1,0:T(8,128)(2,1)S(1)}, bf16[256,256]{1,0:T(8,128)(2,1)S(1)}, u32[]{:S(2)}, u32[]{:S(2)}) collective-permute-start(bf16[256,256]{1,0:T(8,128)(2,1)S(1)} %split.8), channel_id=1, source_target_pairs={{0,2},{2,3},{3,1},{1,0},{4,6},{6,7},{7,5},{5,4},{8,10},{10,11},{11... | collective-permute-start | bytes 393224 | tf_op jit(solution)/shard_map/ppermute | solution.py:390
  14.5 11.2 %collective-permute-start.7 = (bf16[256,256]{1,0:T(8,128)(2,1)S(1)}, bf16[256,256]{1,0:T(8,128)(2,1)S(1)}, u32[]{:S(2)}, u32[]{:S(2)}) collective-permute-start(bf16[256,256]{1,0:T(8,128)(2,1)S(1)} %split.10), channel_id=1, source_target_pairs={{0,2},{2,3},{3,1},{1,0},{4,6},{6,7},{7,5},{5,4},{8,10},{10,11},{11... | collective-permute-start | bytes 393224 | tf_op jit(solution)/shard_map/ppermute | solution.py:390
  17.3 11.2 %collective-permute-start.10 = (bf16[256,256]{1,0:T(8,128)(2,1)S(1)}, bf16[256,256]{1,0:T(8,128)(2,1)S(1)}, u32[]{:S(2)}, u32[]{:S(2)}) collective-permute-start(bf16[256,256]{1,0:T(8,128)(2,1)S(1)} %split.12), channel_id=1, source_target_pairs={{0,2},{2,3},{3,1},{1,0},{4,6},{6,7},{7,5},{5,4},{8,10},{10,11},{11... | collective-permute-start | bytes 393224 | tf_op jit(solution)/shard_map/ppermute | solution.py:390
  22.4 11.8 %collective-permute-start.12 = (bf16[4160,512]{1,0:T(8,128)(2,1)S(1)}, bf16[4160,512]{1,0:T(8,128)(2,1)S(1)}, u32[]{:S(2)}, u32[]{:S(2)}) collective-permute-start(bf16[4160,512]{1,0:T(8,128)(2,1)S(1)} %pack.1.refs_4_.refs_3_.refs_0_), channel_id=1, source_target_pairs={{0,4},{4,0},{1,5},{5,1},{2,6},{6,2},{3,7},{7,3},{8,12},{12,8},{9,1... | collective-permute-start | bytes 12779528 | tf_op jit(solution)/shard_map/ppermute | solution.py:343
  22.5 8.9 %collective-permute-start.14 = (bf16[256,256]{1,0:T(8,128)(2,1)S(1)}, bf16[256,256]{1,0:T(8,128)(2,1)S(1)}, u32[]{:S(2)}, u32[]{:S(2)}) collective-permute-start(bf16[256,256]{1,0:T(8,128)(2,1)S(1)} %split.14), channel_id=1, source_target_pairs={{0,2},{2,3},{3,1},{1,0},{4,6},{6,7},{7,5},{5,4},{8,10},{10,11},{11... | collective-permute-start | bytes 393224 | tf_op jit(solution)/shard_map/ppermute | solution.py:390
  23.2 13.4 %collective-permute-start.5 = (bf16[256,256]{1,0:T(8,128)(2,1)S(1)}, bf16[256,256]{1,0:T(8,128)(2,1)S(1)}, u32[]{:S(2)}, u32[]{:S(2)}) collective-permute-start(bf16[256,256]{1,0:T(8,128)(2,1)S(1)} %split.9), channel_id=1, source_target_pairs={{0,2},{2,3},{3,1},{1,0},{4,6},{6,7},{7,5},{5,4},{8,10},{10,11},{11... | collective-permute-start | bytes 393224 | tf_op jit(solution)/shard_map/ppermute | solution.py:390
  25.8 10.9 %collective-permute-start.8 = (bf16[256,256]{1,0:T(8,128)(2,1)S(1)}, bf16[256,256]{1,0:T(8,128)(2,1)S(1)}, u32[]{:S(2)}, u32[]{:S(2)}) collective-permute-start(bf16[256,256]{1,0:T(8,128)(2,1)S(1)} %split.11), channel_id=1, source_target_pairs={{0,2},{2,3},{3,1},{1,0},{4,6},{6,7},{7,5},{5,4},{8,10},{10,11},{11... | collective-permute-start | bytes 393224 | tf_op jit(solution)/shard_map/ppermute | solution.py:390
  28.6 10.6 %collective-permute-start.11 = (bf16[256,256]{1,0:T(8,128)(2,1)S(1)}, bf16[256,256]{1,0:T(8,128)(2,1)S(1)}, u32[]{:S(2)}, u32[]{:S(2)}) collective-permute-start(bf16[256,256]{1,0:T(8,128)(2,1)S(1)} %split.13), channel_id=1, source_target_pairs={{0,2},{2,3},{3,1},{1,0},{4,6},{6,7},{7,5},{5,4},{8,10},{10,11},{11... | collective-permute-start | bytes 393224 | tf_op jit(solution)/shard_map/ppermute | solution.py:390
  31.4 9.8 %collective-permute-start.15 = (bf16[256,256]{1,0:T(8,128)(2,1)S(1)}, bf16[256,256]{1,0:T(8,128)(2,1)S(1)}, u32[]{:S(2)}, u32[]{:S(2)}) collective-permute-start(bf16[256,256]{1,0:T(8,128)(2,1)S(1)} %split.15), channel_id=1, source_target_pairs={{0,2},{2,3},{3,1},{1,0},{4,6},{6,7},{7,5},{5,4},{8,10},{10,11},{11... | collective-permute-start | bytes 393224 | tf_op jit(solution)/shard_map/ppermute | solution.py:390
  41.8 1.5 %collective-permute-start.16 = (f32[64,640]{1,0:T(8,128)S(1)}, f32[64,640]{1,0:T(8,128)S(1)}, u32[]{:S(2)}, u32[]{:S(2)}) collective-permute-start(f32[64,640]{1,0:T(8,128)S(1)} %get-tuple-element.38), channel_id=1, source_target_pairs={{4,0},{0,4},{5,1},{1,5},{6,2},{2,6},{7,3},{3,7},{12,8},{8,12},{13,... | collective-permute-start | bytes 491528 | tf_op jit(solution)/shard_map/ppermute | solution.py:407
